TPU v7x, 32 devices: a whole 2x2x4 slice. The times are simulated.
32 devices in a mesh: row: 8 (over y, x, core), col: 4 (over z).
Axes of the slice: x: 2, y: 2, z: 4, core: 2. Of those that a mesh axis runs over, the one named last changes fastest.
Arguments:
- grad_out: float32 [16384, 256], P(('row', 'col')), may hold values from -6 to 6
- relu_mask: int32 [16384, 256], P(('row', 'col')), may hold values 0 or 1
- basis_zero: float32 [16384, 256], P(('row', 'col')), may hold values from -6 to 6
- basis_one: float32 [16384, 256], P(('row', 'col')), may hold values from -6 to 6
- basis_two: float32 [16384, 256], P(('row', 'col')), may hold values from -6 to 6
- cheb_weight: float32 [3, 256, 256], replicated, may hold values from -0.375 to 0.375
- tile_values: float32 [32, 128, 128, 128], P(('row', 'col')), may hold values from -0.125 to 0.125
- tile_rows: int32 [32, 128], P(('row', 'col')), may hold values from 0 to 15
- tile_slots: int32 [32, 128], P(('row', 'col')), may hold values from 0 to 7, as said below
- send_blocks: int32 [32, 8, 1], P(('row', 'col')), may hold values from 0 to 3
- live_tiles: int32 [32], P(('row', 'col')), may hold values from 8 to 128, as said below
Outputs:
- grad_features: float32 [16384, 256], P(('row', 'col'))
- weight_grad: float32 [3, 256, 256], replicated
Inputs may be any that keep to these rules, and one draw needn't show every extreme that they name: `tile_slots`: slot q of device (r, c) is the node block send_blocks[q * 4 + c, r, 0] of device q * 4 + c. On every device each of the 8 slots is the column of at least one used operator block. `send_blocks`: indices of the device's own node blocks. `live_tiles`: some device uses all 128 slots.
All inputs are finite; a program needn't handle non-finite values. No bound on the sum of `relu_mask` on one device may be relied on, other than what follows from the above.
Results may differ from a plain program's by a relative error of at most 0.0001.
Values sent between devices are 32-bit elements; how exact they have to be, the bound alone decides.
No kernel may reach another device: no remote copies, remote signals or barrier semaphores. Data moves between devices by JAX's collectives and lax.ppermute only.
A program may use at most 128 MiB of HBM per device.

v0:
```python
import jax
import jax.numpy as jnp
from jax import lax
from jax.sharding import PartitionSpec as P

F = 256
TB = 128
CAP = 1
CHB = 4
TILES_DEV = 128


def reduce_weights(local_grad):
    return lax.psum(local_grad, ("row", "col"))


def per_device(
    grad_out,
    relu_mask,
    basis_zero,
    basis_one,
    basis_two,
    cheb_weight,
    tile_values,
    tile_rows,
    tile_slots,
    send_blocks,
    live_tiles,
):
    highest = lax.Precision.HIGHEST
    masked = jnp.where(relu_mask > 0, grad_out, jnp.zeros_like(grad_out))
    bases = jnp.stack([basis_zero, basis_one, basis_two])
    local_grad = jnp.einsum("knf,ng->kfg", bases, masked, precision=highest)
    weight_grad = reduce_weights(local_grad)
    terms = jnp.einsum("ng,kfg->knf", masked, cheb_weight, precision=highest)
    slot_count = lax.axis_size("row") * CAP
    values = tile_values[0]
    rows = tile_rows[0]
    slots = tile_slots[0]
    used = (jnp.arange(TILES_DEV, dtype=jnp.int32) < live_tiles[0]).astype(values.dtype)
    owners = send_blocks[0].reshape(slot_count)
    selector = (owners[:, None] == jnp.arange(CHB, dtype=jnp.int32)[None, :]).astype(values.dtype)

    def collect(received):
        return jnp.einsum("qb,qtf->btf", selector, received, precision=highest)

    def transposed(field):
        own_blocks = field.reshape(CHB, TB, F)
        slab = lax.all_gather(own_blocks, "col", axis=0, tiled=True)
        gathered = slab[rows]
        contrib = (
            jnp.einsum("tab,taf->tbf", values, gathered, precision=highest) * used[:, None, None]
        )
        partial_sums = jax.ops.segment_sum(contrib, slots, num_segments=slot_count)
        received = lax.all_to_all(partial_sums, "row", split_axis=0, concat_axis=0, tiled=True)
        summed = collect(received)
        return summed.reshape(CHB * TB, F)

    carried = terms[1] + 2.0 * transposed(terms[2])
    grad_features = terms[0] - terms[2] + transposed(carried)
    return (grad_features, weight_grad)


def solution(mesh):
    placed = (
        P(("row", "col"), None),
        P(("row", "col"), None),
        P(("row", "col"), None),
        P(("row", "col"), None),
        P(("row", "col"), None),
        P(),
        P(("row", "col"), None, None, None),
        P(("row", "col"), None),
        P(("row", "col"), None),
        P(("row", "col"), None, None),
        P(("row", "col")),
    )
    return jax.shard_map(
        per_device,
        mesh=mesh,
        in_specs=placed,
        out_specs=(P(("row", "col"), None), P()),
        check_vma=False,
    )
```

profile of v0, /device:TPU:0, one launch (start us, length us, event | category | flops | bytes accessed | tf_op | source)
XLA Modules:
  0.0 412.3 jit_solution(2922234468886981791)
XLA Ops:
  8.0 0.0 copy-start
  8.0 0.0 all-gather.3.cloned.1.call-start
  8.1 1.1 copy-done
  9.1 2.6 convolution_bitcast_fusion
  11.8 1.0 fusion.28
  12.8 0.0 all-gather.3.cloned.1.call-update
  12.8 0.0 all-gather.5.cloned.1.call-start
  13.6 0.7 fusion.22
  14.2 47.4 %all-gather.3.cloned.1.call-done = f32[16,128,256]{2,1,0:T(8,128)} async-done(((f32[4,128,256]{2,1,0:T(8,128)}), f32[16,128,256]{2,1,0:T(8,128)}) %all-gather.3.cloned.1.call-update) | async-done | bytes 2097168 | tf_op jit(solution)/shard_map/all_gather | solution.py:49
  61.6 11.4 %gather_fusion = f32[128,128,256]{2,1,0:T(8,128)} fusion(f32[16,128,256]{2,1,0:T(8,128)} %all-gather.3.cloned.1.call-done, s32[1024]{0:T(1024)S(1)} %pad_clamp_fusion), kind=kCustom, calls=%fused_computation | custom fusion | bytes 33554944 | tf_op jit(solution)/shard_map/gather | solution.py:50
  73.0 0.0 copy-start.2
  73.0 24.8 %multiply_bitcast_fusion.1 = f32[128,128,256]{2,1,0:T(8,128)} fusion(f32[128,128,256]{2,1,0:T(8,128)} %gather_fusion, f32[1,128,128,128]{3,2,1,0:T(8,128)} %param.17, f32[128]{0:T(128)S(1)} %compare_convert_fusion), kind=kOutput, calls=%fused_computation.5 | convolution fusion | flops 6446645248 | bytes 41943552 | tf_op jit(solution)/shard_map/tab,taf->tbf/dot_general | solution.py:52
  97.8 0.1 broadcast.30.clone
  97.9 0.0 copy-done.2
  97.9 0.0 copy-start.3
  97.9 24.4 %scatter_fusion = f32[8,128,256]{2,1,0:T(8,128)S(1)} fusion(f32[8,128,256]{2,1,0:T(8,128)S(1)} %broadcast.30.clone, s32[128]{0:T(128)S(1)} %bitcast.47, f32[128,128,256]{2,1,0:T(8,128)} %multiply_bitcast_fusion.1), kind=kCustom, calls=%fused_computation.2 | custom fusion | flops 4194304 | bytes 50332160 | tf_op jit(solution)/shard_map/scatter-add | solution.py:54
  122.3 18.8 %all_to_all.10 = f32[8,128,256]{2,1,0:T(8,128)S(1)} all-to-all(f32[8,128,256]{2,1,0:T(8,128)S(1)} %scatter_fusion), channel_id=1, replica_groups=mesh['row'=8,'col'=4] {'row'}, dimensions={0} | all-to-all | bytes 2097152 | tf_op jit(solution)/shard_map/all_to_all | solution.py:55
  141.1 0.0 copy-done.3
  141.1 1.2 fusion.8
  142.3 2.0 fusion.16
  144.3 0.0 all-gather.5.cloned.1.call-update
  144.3 43.0 %all-gather.5.cloned.1.call-done = f32[16,128,256]{2,1,0:T(8,128)} async-done(((f32[4,128,256]{2,1,0:T(8,128)}), f32[16,128,256]{2,1,0:T(8,128)}) %all-gather.5.cloned.1.call-update) | async-done | bytes 2097168 | tf_op jit(solution)/shard_map/all_gather | solution.py:49
  187.3 11.4 %gather_fusion.1 = f32[128,128,256]{2,1,0:T(8,128)} fusion(f32[16,128,256]{2,1,0:T(8,128)} %all-gather.5.cloned.1.call-done, s32[1024]{0:T(1024)S(1)} %pad_clamp_fusion), kind=kCustom, calls=%fused_computation.1 | custom fusion | bytes 33554944 | tf_op jit(solution)/shard_map/gather | solution.py:50
  198.7 24.7 %multiply_bitcast_fusion = f32[128,128,256]{2,1,0:T(8,128)} fusion(f32[128,128,256]{2,1,0:T(8,128)} %gather_fusion.1, f32[1,128,128,128]{3,2,1,0:T(8,128)} %param.17, f32[128]{0:T(128)S(1)} %compare_convert_fusion), kind=kOutput, calls=%fused_computation.4 | convolution fusion | flops 6446645248 | bytes 41943552 | tf_op jit(solution)/shard_map/tab,taf->tbf/dot_general | solution.py:52
  223.5 1.1 broadcast.30
  224.5 0.0 copy-start.1
  224.5 36.3 %scatter_fusion.1 = f32[8,128,256]{2,1,0:T(8,128)} fusion(f32[8,128,256]{2,1,0:T(8,128)} %broadcast.30, s32[128]{0:T(128)S(1)} %bitcast.48, f32[128,128,256]{2,1,0:T(8,128)} %multiply_bitcast_fusion), kind=kCustom, calls=%fused_computation.3 | custom fusion | flops 4194304 | bytes 50332160 | tf_op jit(solution)/shard_map/scatter-add | solution.py:54
  260.8 3.6 all-to-all-start.1
  264.4 0.3 all-reduce.2.cloned.1.call-start
  264.7 2.0 copy.20
  266.7 2.0 copy.21
  268.8 2.0 copy.22
  270.8 4.0 fusion.2
  274.8 0.0 all-reduce.2.cloned.1.call-update
  274.8 5.1 %all-to-all-done.1 = f32[8,128,256]{2,1,0:T(8,128)S(1)} async-done(((f32[8,128,256]{2,1,0:T(8,128)}), f32[8,128,256]{2,1,0:T(8,128)S(1)}, u32[]{:S(2)}, u32[]{:S(2)}) %all-to-all-start.1) | async-done | bytes 1048608 | tf_op jit(solution)/shard_map/all_to_all | solution.py:55
  279.8 1.2 fusion.10
  281.0 0.1 copy.19
  281.1 0.9 fusion.13
  282.0 120.7 %all-reduce.2.cloned.1.call-done = f32[3,256,256]{2,1,0:T(8,128)} async-done(((f32[3,256,256]{2,1,0:T(8,128)}), f32[3,256,256]{2,1,0:T(8,128)}) %all-reduce.2.cloned.1.call-update) | async-done | bytes 786448 | tf_op jit(solution)/shard_map/psum | solution.py:14
  402.8 2.1 copy.36
  404.8 0.0 copy-done.1
  (2 shorter events, 0.0 us)
Async XLA Ops:
  8.0 1.1 copy-start
  8.0 53.6 %all-gather.3.cloned.1.call-start = ((), (), s32[]{:S(2)}) async-start(), calls=%async_computation.2 | async-start | bytes 2621440 | tf_op jit(solution)/shard_map/all_gather | solution.py:49
  12.8 174.5 %all-gather.5.cloned.1.call-start = ((), (), s32[]{:S(2)}) async-start(), calls=%async_computation.3 | async-start | bytes 2621440 | tf_op jit(solution)/shard_map/all_gather | solution.py:49
  73.0 24.9 %copy-start.2 = (s32[1,128]{1,0:T(1,128)S(1)}, s32[1,128]{1,0:T(1,128)}, u32[]{:S(2)}) copy-start(s32[1,128]{1,0:T(1,128)} %param.19) | copy-start | bytes 1540
  97.9 43.2 %copy-start.3 = (s32[1,8,1]{1,2,0:T(1,128)S(1)}, s32[1,8,1]{1,2,0:T(1,128)}, u32[]{:S(2)}) copy-start(s32[1,8,1]{1,2,0:T(1,128)} %param.20) | copy-start | bytes 100
  224.5 180.3 %copy-start.1 = (f32[3,256,256]{2,1,0:T(8,128)S(1)}, f32[3,256,256]{2,1,0:T(8,128)}, u32[]{:S(2)}) copy-start(f32[3,256,256]{2,1,0:T(8,128)} %param.16) | copy-start | bytes 2359300
  260.8 19.0 %all-to-all-start.1 = ((f32[8,128,256]{2,1,0:T(8,128)}), f32[8,128,256]{2,1,0:T(8,128)S(1)}, u32[]{:S(2)}, u32[]{:S(2)}) async-start(f32[8,128,256]{2,1,0:T(8,128)} %scatter_fusion.1), calls=%async_computation.1 | async-start | bytes 2097152 | tf_op jit(solution)/shard_map/all_to_all | solution.py:55
  264.4 138.3 %all-reduce.2.cloned.1.call-start = ((), (), s32[]{:S(2)}) async-start(), calls=%async_computation.4 | async-start | bytes 1572864 | tf_op jit(solution)/shard_map/psum | solution.py:14
Sparse Core Ops, SparseCore 0:
  13.0 48.6 all-gather.2
  144.4 42.8 all-gather.4
Sparse Core Ops, SparseCore 1:
  274.9 127.8 all-reduce.1
where the time goes:
time: 413 us; the launch traced here: 412 us
  waiting for transfers between devices  216 us (52%)
  other arithmetic  64.2 us (16%)
  matrix products  58.4 us (14%)
  local copies, waits for them, and re-layouts  34.3 us (8%)
  blocking collectives  18.8 us (5%)
  between operations  16.2 us (4%)
    psum x1, waiting for transfers between devices, reduce_weights(): return lax.psum(local_grad, ('row', 'col'))  121 us
    all_gather x2, waiting for transfers between devices, transposed(): slab = lax.all_gather(own_blocks, 'col', axis=0, tiled=True)  90.4 us
    scatter-add x2, other arithmetic, transposed(): partial_sums = jax.ops.segment_sum(contrib, slots, num_segments=slot_count)  60.6 us
    dot_general x2, matrix products, transposed(): jnp.einsum('tab,taf->tbf', values, gathered, precision=highest)  49.5 us
    gather x2, local copies, waits for them, and re-layouts, transposed(): gathered = slab[rows]  22.8 us
    all_to_all x1, blocking collectives, transposed(): lax.all_to_all(partial_sums, 'row', split_axis=0, concat_axis=0, tiled=True)  18.8 us
    unnamed x12, local copies, waits for them, and re-layouts  9.27 us
  transfers between devices with their start and end apart: 4, of which 4 were waited for; matrix products, arithmetic and copies ran while one was open for 3% of the time, Pallas kernels for 0%

commit v1 on v0

v1 whole, which is shorter than its diff:
```python
import functools

import jax
import jax.numpy as jnp
from jax import lax
from jax.experimental import pallas as pl
from jax.experimental.pallas import tpu as pltpu
from jax.sharding import PartitionSpec as P

F = 256
H = 128
TB = 128
CHB = 4
NODES_DEV = CHB * TB
TILES_DEV = 128
GROUPS = 8
MIB = 1 << 20
BF16 = jnp.bfloat16
F32 = jnp.float32

SMEM = pl.BlockSpec(memory_space=pltpu.SMEM)
VMEM = pl.BlockSpec(memory_space=pltpu.VMEM)
ANY = pl.BlockSpec(memory_space=pl.ANY)


def params(mib):
    return pltpu.CompilerParams(vmem_limit_bytes=mib * MIB)


def cost(flops, bytes_accessed):
    return pl.CostEstimate(flops=flops, bytes_accessed=bytes_accessed, transcendentals=0)


def split(x):
    high = x.astype(BF16)
    low = (x - high.astype(F32)).astype(BF16)
    return high, low


def dot3(a, b, dims):
    ah, al = a
    bh, bl = b

    def one(x, y):
        return lax.dot_general(x, y, (dims, ((), ())), preferred_element_type=F32)

    return one(ah, bh) + (one(ah, bl) + one(al, bh))


def masked_of(grad_ref, mask_ref):
    grad = grad_ref[...]
    return jnp.where(mask_ref[...] > 0, grad, jnp.zeros_like(grad))


def term_two_kernel(grad_ref, mask_ref, weight_ref, left_ref, right_ref):
    term = dot3(split(masked_of(grad_ref, mask_ref)), split(weight_ref[0]), ((1,), (1,)))
    left_ref[...] = term[:, :H]
    right_ref[...] = term[:, H:]


def term_two(grad_out, relu_mask, cheb_weight):
    full = pl.BlockSpec((NODES_DEV, F), lambda i: (0, 0))
    half = pl.BlockSpec((NODES_DEV, H), lambda i: (0, 0))
    out = jax.ShapeDtypeStruct((NODES_DEV, H), F32)
    return pl.pallas_call(
        term_two_kernel,
        grid=(1,),
        in_specs=[full, full, pl.BlockSpec((1, F, F), lambda i: (2, 0, 0))],
        out_specs=[half, half],
        out_shape=[out, out],
        compiler_params=params(16),
        cost_estimate=cost(6 * NODES_DEV * F * F, 4 * NODES_DEV * F * 3 + 4 * F * F),
        name="term_two",
    )(grad_out, relu_mask, cheb_weight)


def local_kernel(n_row, ids_ref, grad_ref, mask_ref, b0, b1, b2, weight_ref, *rest):
    left_ref, right_ref, diff_ref = rest[:3]
    pieces = rest[3 : 3 + n_row]
    total = rest[3 + n_row]
    masked = split(masked_of(grad_ref, mask_ref))
    term = dot3(masked, split(weight_ref[1]), ((1,), (1,)))
    left_ref[...] = term[:, :H]
    right_ref[...] = term[:, H:]
    diff_ref[...] = dot3(masked, split(weight_ref[0] - weight_ref[2]), ((1,), (1,)))
    for k, basis in enumerate((b0, b1, b2)):
        total[k * F : (k + 1) * F, :] = dot3(split(basis[...]), masked, ((0,), (0,)))
    rows = 3 * F // n_row
    for j, piece in enumerate(pieces):
        begin = pl.multiple_of((ids_ref[0] ^ j) * rows, 8)
        piece[...] = total[pl.ds(begin, rows), :]


def local_terms(n_row, ids, grad_out, relu_mask, b0, b1, b2, cheb_weight):
    half = jax.ShapeDtypeStruct((NODES_DEV, H), F32)
    piece = jax.ShapeDtypeStruct((3 * F // n_row, F), F32)
    outs = pl.pallas_call(
        functools.partial(local_kernel, n_row),
        in_specs=[SMEM] + [VMEM] * 6,
        out_specs=[VMEM] * (3 + n_row),
        out_shape=[half, half, jax.ShapeDtypeStruct((NODES_DEV, F), F32)] + [piece] * n_row,
        scratch_shapes=[pltpu.VMEM((3 * F, F), F32)],
        compiler_params=params(32),
        cost_estimate=cost(30 * NODES_DEV * F * F, 4 * NODES_DEV * F * 8),
        name="local_terms",
    )(ids, grad_out, relu_mask, b0, b1, b2, cheb_weight)
    return outs[0], outs[1], outs[2], outs[3:]


def operator_kernel(n_row, n_col, ids_ref, live_ref, rows_ref, slots_ref, values_ref, out_ref, tiles, acc, lists, counts, sems):
    origin = pl.program_id(0)
    size = TILES_DEV // GROUPS

    def copy(g):
        part = pl.ds(g * size, size)
        return pltpu.make_async_copy(values_ref.at[part], tiles.at[part], sems.at[g])

    @pl.when(origin == 0)
    def _():
        for g in range(GROUPS):
            copy(g).start()
        for s in range(n_col):
            counts[s] = 0

        def place(t, carry):
            row = rows_ref[t]
            s = lax.rem(row // CHB - ids_ref[1] + n_col, n_col)
            position = (slots_ref[t] ^ ids_ref[0]) * CHB + lax.rem(row, CHB)
            n = counts[s]
            lists[s, n] = position * TILES_DEV + t
            counts[s] = n + 1
            return carry

        lax.fori_loop(0, live_ref[0], place, 0)
        for g in range(GROUPS):
            copy(g).wait()

    acc[...] = jnp.zeros_like(acc)

    def add(n, carry):
        entry = lists[origin, n]
        position = entry // TILES_DEV
        acc[position] += tiles[lax.rem(entry, TILES_DEV)]
        return carry

    lax.fori_loop(0, counts[origin], add, 0)

    def store(slot, carry):
        here = pl.ds(pl.multiple_of(slot * TB, TB), TB)
        for i in range(CHB):
            high, low = split(acc[slot * CHB + i].T)
            out_ref[0, here, i * TB : (i + 1) * TB] = high
            out_ref[0, here, NODES_DEV + i * TB : NODES_DEV + (i + 1) * TB] = low
        return carry

    lax.fori_loop(0, n_row, store, 0)


def build_operator(n_row, n_col, ids, live, rows, slots, values):
    wide = (n_row * TB, 2 * NODES_DEV)
    return pl.pallas_call(
        functools.partial(operator_kernel, n_row, n_col),
        grid=(n_col,),
        in_specs=[SMEM] * 4 + [ANY],
        out_specs=pl.BlockSpec((1,) + wide, lambda s: (s, 0, 0)),
        out_shape=jax.ShapeDtypeStruct((n_col,) + wide, BF16),
        scratch_shapes=[
            pltpu.VMEM((TILES_DEV, TB, TB), F32),
            pltpu.VMEM((n_row * CHB, TB, TB), F32),
            pltpu.SMEM((n_col, TILES_DEV), jnp.int32),
            pltpu.SMEM((n_col,), jnp.int32),
            pltpu.SemaphoreType.DMA((GROUPS,)),
        ],
        compiler_params=params(48),
        cost_estimate=cost(0, 4 * TILES_DEV * TB * TB * 5),
        name="operator",
    )(ids, live, rows, slots, values)


def product_kernel(n_row, origins, has_prev, last, *refs):
    n = len(origins)
    op_ref, fields = refs[0], refs[1 : 1 + n]
    prev = refs[1 + n] if has_prev else None
    outs = refs[1 + n + has_prev : -2]
    buf, sems = refs[-2:]
    pairs = n_row // 2
    wide = 2 * TB

    def copy(k, p):
        source = op_ref.at[origins[k], pl.ds(p * wide, wide)]
        return pltpu.make_async_copy(source, buf.at[k, pl.ds(p * wide, wide)], sems.at[k, p])

    for p in range(pairs):
        for k in range(n):
            copy(k, p).start()
    right = []
    for field in fields:
        high, low = split(field[...])
        both = jnp.concatenate([high, low], axis=1)
        right.append(jnp.concatenate([both, both], axis=0))
    for p in range(pairs):
        total = None
        for k in range(n):
            copy(k, p).wait()
            here = jnp.dot(buf[k, p * wide : (p + 1) * wide, :], right[k], preferred_element_type=F32)
            total = here if total is None else total + here
        summed = total[:, :H] + total[:, H:]
        if has_prev:
            summed = summed + prev[p * wide : (p + 1) * wide, :]
        if last:
            outs[2 * p][...] = summed[:TB]
            outs[2 * p + 1][...] = summed[TB:]
        else:
            outs[0][p * wide : (p + 1) * wide, :] = summed


def product(n_row, origins, operator, fields, prev, last):
    rows = n_row * TB
    n = len(origins)
    has_prev = prev is not None
    if last:
        out_shape = [jax.ShapeDtypeStruct((TB, H), F32)] * n_row
    else:
        out_shape = [jax.ShapeDtypeStruct((rows, H), F32)]
    out = pl.pallas_call(
        functools.partial(product_kernel, n_row, origins, has_prev, last),
        in_specs=[ANY] + [VMEM] * (n + has_prev),
        out_specs=[VMEM] * len(out_shape),
        out_shape=out_shape,
        scratch_shapes=[
            pltpu.VMEM((n, rows, 2 * NODES_DEV), BF16),
            pltpu.SemaphoreType.DMA((n, n_row // 2)),
        ],
        compiler_params=params(40),
        cost_estimate=cost(
            2 * n * rows * 2 * NODES_DEV * F, n * rows * NODES_DEV * 4 + 4 * n * NODES_DEV * H + 8 * rows * H
        ),
        name="product",
    )(operator, *fields, *((prev,) if has_prev else ()))
    return out if last else out[0]


def collect_kernel(n_row, scale, halves, ids_ref, owners_ref, base_ref, *refs):
    out_ref = refs[-1]
    out_ref[...] = base_ref[...]
    for h in range(halves):
        for j in range(n_row):
            owner = owners_ref[ids_ref[0] ^ j]
            here = pl.ds(pl.multiple_of(owner * TB, TB), TB)
            came = refs[h * n_row + j][...]
            out_ref[here, h * H : (h + 1) * H] += came if scale == 1.0 else scale * came


def collect(n_row, scale, ids, owners, base, received):
    halves = len(received) // n_row
    return pl.pallas_call(
        functools.partial(collect_kernel, n_row, scale, halves),
        in_specs=[SMEM, SMEM] + [VMEM] * (1 + len(received)),
        out_specs=VMEM,
        out_shape=jax.ShapeDtypeStruct(base.shape, F32),
        compiler_params=params(24),
        cost_estimate=cost(0, 4 * (2 * base.size + len(received) * TB * H)),
        name="collect",
    )(ids, owners, base, *received)


def assemble_kernel(n_row, ids_ref, *refs):
    out_ref = refs[-1]
    rows = 3 * F // n_row
    for j in range(n_row):
        begin = pl.multiple_of((ids_ref[0] ^ j) * rows, 8)
        out_ref[pl.ds(begin, rows), :] = refs[j][...]


def assemble(n_row, ids, pieces):
    return pl.pallas_call(
        functools.partial(assemble_kernel, n_row),
        in_specs=[SMEM] + [VMEM] * n_row,
        out_specs=VMEM,
        out_shape=jax.ShapeDtypeStruct((3 * F, F), F32),
        compiler_params=params(16),
        cost_estimate=cost(0, 8 * 3 * F * F),
        name="assemble",
    )(ids, *pieces)


def exchange(n_row, pieces):
    moved = [pieces[0]]
    for j in range(1, n_row):
        moved.append(lax.ppermute(pieces[j], "row", [(r, r ^ j) for r in range(n_row)]))
    return moved


def shift(n_col, x, step):
    return lax.ppermute(x, "col", [(c, (c + step) % n_col) for c in range(n_col)])


def reduce_weights(n_row, n_col, ids, pieces):
    mine = functools.reduce(jnp.add, exchange(n_row, pieces))
    step = 1
    while step < n_col:
        mine = mine + lax.ppermute(mine, "col", [(c, c ^ step) for c in range(n_col)])
        step *= 2
    return assemble(n_row, ids, exchange(n_row, [mine] * n_row)).reshape(3, F, F)


def transposed(n_row, n_col, operator, field, side):
    long = n_col // 2
    short = n_col - 1 - long
    total = product(n_row, (0,), operator, [field], None, n_col == 1)
    ahead, behind = field, field
    for s in range(1, long + 1):
        fields, origins = [], []
        ahead = shift(n_col, ahead, side)
        fields.append(ahead)
        origins.append((-side * s) % n_col)
        if s <= short:
            behind = shift(n_col, behind, -side)
            fields.append(behind)
            origins.append((side * s) % n_col)
        total = product(n_row, tuple(origins), operator, fields, total, s == long)
    return exchange(n_row, total)


def per_device(
    grad_out,
    relu_mask,
    basis_zero,
    basis_one,
    basis_two,
    cheb_weight,
    tile_values,
    tile_rows,
    tile_slots,
    send_blocks,
    live_tiles,
):
    n_row = lax.axis_size("row")
    n_col = lax.axis_size("col")
    ids = jnp.stack([lax.axis_index("row"), lax.axis_index("col")]).astype(jnp.int32)
    owners = send_blocks.reshape(n_row)
    two = term_two(grad_out, relu_mask, cheb_weight)
    operator = build_operator(
        n_row, n_col, ids, live_tiles, tile_rows.reshape(TILES_DEV), tile_slots.reshape(TILES_DEV), tile_values[0]
    )
    one_left, one_right, diff, pieces = local_terms(
        n_row, ids, grad_out, relu_mask, basis_zero, basis_one, basis_two, cheb_weight
    )
    received = []
    for side, field, one in ((1, two[0], one_left), (-1, two[1], one_right)):
        first = transposed(n_row, n_col, operator, field, side)
        carried = collect(n_row, 2.0, ids, owners, one, first)
        received += transposed(n_row, n_col, operator, carried, side)
    weight_grad = reduce_weights(n_row, n_col, ids, pieces)
    grad_features = collect(n_row, 1.0, ids, owners, diff, received)
    return grad_features, weight_grad


def solution(mesh):
    placed = (
        P(("row", "col"), None),
        P(("row", "col"), None),
        P(("row", "col"), None),
        P(("row", "col"), None),
        P(("row", "col"), None),
        P(),
        P(("row", "col"), None, None, None),
        P(("row", "col"), None),
        P(("row", "col"), None),
        P(("row", "col"), None, None),
        P(("row", "col")),
    )
    return jax.shard_map(
        per_device,
        mesh=mesh,
        in_specs=placed,
        out_specs=(P(("row", "col"), None), P()),
        check_vma=False,
    )
```

time: 413 us -> 156 us (0.38)
  waiting for transfers between devices: 216 us -> 33 us
  other arithmetic: 64.2 us -> 0.15 us
  matrix products: 58.4 us -> 0 us
  starting transfers between devices: 3.98 us -> 59.1 us
  Pallas kernels: 0 us -> 46.8 us
  local copies, waits for them, and re-layouts: 34.3 us -> 14.2 us
  blocking collectives: 18.8 us -> 0 us
  between operations: 16.2 us -> 1.66 us
    psum x1 -> x0, waiting for transfers between devices: 121 us -> none  [reduce_weights(): return lax.psum(local_grad, ('row', 'col'))]
    all_gather x2 -> x0, waiting for transfers between devices: 90.4 us -> none  [transposed(): slab = lax.all_gather(own_blocks, 'col', axis=0, tiled=True)]
    scatter-add x2 -> x0, other arithmetic: 60.6 us -> none  [transposed(): partial_sums = jax.ops.segment_sum(contrib, slots, num_segments=slot_count)]
    ppermute x0 -> x56, starting transfers between devices: none -> 59.1 us  [the longest x42 38.1 us: exchange(): lax.ppermute(pieces[j], 'row', [(r, r ^ j) for r in range(n_row)])]
    dot_general x6 -> x0, matrix products: 58.4 us -> none  [the longest x2 49.5 us: transposed(): jnp.einsum('tab,taf->tbf', values, gathered, precision=highest)]
    pallas_call x0 -> x19, Pallas kernels: none -> 46.8 us  [the longest x12 28.7 us: product(): pl.pallas_call(functools.partial(product_kernel, n_row, origins, has_prev...]
    ppermute x0 -> x56, waiting for transfers between devices: none -> 33 us  [the longest x2 16.8 us: reduce_weights(): lax.ppermute(mine, 'col', [(c, c ^ step) for c in range(n_col)])]
    gather x2 -> x0, local copies, waits for them, and re-layouts: 22.8 us -> none  [transposed(): gathered = slab[rows]]
  transfers between devices with their start and end apart: 4 -> 56, of which waited for: 4 -> 12; matrix products, arithmetic and copies ran while one was open for 3% -> 0% of each run, Pallas kernels for 0% -> 29%
where the time goes in v1:
time: 156 us; the launch traced here: 155 us
  starting transfers between devices  59.1 us (38%)
  Pallas kernels  46.8 us (30%)
  waiting for transfers between devices  33 us (21%)
  local copies, waits for them, and re-layouts  14.2 us (9%)
  between operations  1.66 us (1%)
    ppermute x42, starting transfers between devices, exchange(): lax.ppermute(pieces[j], 'row', [(r, r ^ j) for r in range(n_row)])  38.1 us
    pallas_call x12, Pallas kernels, product(): pl.pallas_call(functools.partial(product_kernel, n_row, origins, has_prev...  28.7 us
    ppermute x12, starting transfers between devices, shift(): lax.ppermute(x, 'col', [(c, (c + step) % n_col) for c in range(n_col)])  19.8 us
    ppermute x2, waiting for transfers between devices, reduce_weights(): lax.ppermute(mine, 'col', [(c, c ^ step) for c in range(n_col)])  16.8 us
    unnamed x26, local copies, waits for them, and re-layouts  14.2 us
    pallas_call x1, Pallas kernels, build_operator(): pl.pallas_call(functools.partial(operator_kernel, n_row, n_col), grid=(n_...  11.6 us
    ppermute x42, waiting for transfers between devices, exchange(): lax.ppermute(pieces[j], 'row', [(r, r ^ j) for r in range(n_row)])  9.55 us
    ppermute x12, waiting for transfers between devices, shift(): lax.ppermute(x, 'col', [(c, (c + step) % n_col) for c in range(n_col)])  6.66 us
  transfers between devices with their start and end apart: 56, of which 12 were waited for; matrix products, arithmetic and copies ran while one was open for 0% of the time, Pallas kernels for 29%

profile of v1, /device:TPU:0, one launch (start us, length us, event | category | flops | bytes accessed | tf_op | source)
XLA Modules:
  0.0 155.0 jit_solution(14681469312159015129)
XLA Ops:
  0.6 1.1 copy-done.1
  1.8 1.0 copy-done.3
  2.8 1.0 copy-done.5
  4.3 5.1 %collective-permute-start.20 = (f32[512,128]{1,0:T(8,128)S(1)}, f32[512,128]{1,0:T(8,128)S(1)}, u32[]{:S(2)}, u32[]{:S(2)}) collective-permute-start(f32[512,128]{1,0:T(8,128)S(1)} %get-tuple-element.67.refs_1_), channel_id=1, source_target_pairs={{0,3},{1,0},{2,1},{3,2},{4,7},{5,4},{6,5},{7,6},{8,11},{9,8},{10,9... | collective-permute-start | bytes 786440 | tf_op jit(solution)/shard_map/ppermute | solution.py:295
  9.4 6.6 %collective-permute-done.20.refs_1_ = f32[512,128]{1,0:T(8,128)S(1)} collective-permute-done((f32[512,128]{1,0:T(8,128)S(1)}, f32[512,128]{1,0:T(8,128)S(1)}, u32[]{:S(2)}, u32[]{:S(2)}) %collective-permute-start.20) | collective-permute-done | bytes 262176 | tf_op jit(solution)/shard_map/ppermute | solution.py:295
  16.1 4.3 %collective-permute-start.21 = (f32[512,128]{1,0:T(8,128)S(1)}, f32[512,128]{1,0:T(8,128)S(1)}, u32[]{:S(2)}, u32[]{:S(2)}) collective-permute-start(f32[512,128]{1,0:T(8,128)S(1)} %collective-permute-done.20.refs_1_), channel_id=1, source_target_pairs={{0,3},{1,0},{2,1},{3,2},{4,7},{5,4},{6,5},{7,6},{8,11},{9,8},{10,9... | collective-permute-start | bytes 786440 | tf_op jit(solution)/shard_map/ppermute | solution.py:295
  20.4 1.1 copy-done.2
  21.5 1.0 copy-done.4
  22.5 1.0 copy-done.6
  23.6 1.0 copy-done.10
  24.6 1.0 copy-done.11
  25.7 1.0 copy-done.12
  26.7 1.9 %local_terms.1 = (f32[512,128]{1,0:T(8,128)S(1)}, f32[512,128]{1,0:T(8,128)S(1)}, f32[512,256]{1,0:T(8,128)S(1)}, f32[96,256]{1,0:T(8,128)S(1)}, f32[96,256]{1,0...) custom-call(s32[2]{0:T(128)S(1)} %pad_add_fusion.ids_ref, ...), custom_call_target="tpu_custom_call" | custom-call | flops 1006632960 | bytes 4194304 | tf_op jit(solution)/shard_map/local_terms/pallas_call | solution.py:97
  28.7 1.6 %collective-permute-start.41 = (f32[96,256]{1,0:T(8,128)S(1)}, f32[96,256]{1,0:T(8,128)S(1)}, u32[]{:S(2)}, u32[]{:S(2)}) collective-permute-start(f32[96,256]{1,0:T(8,128)S(1)} %get-tuple-element.86), channel_id=1, source_target_pairs={{0,8},{4,12},{8,0},{12,4},{16,24},{20,28},{24,16},{28,20},{1,9},{5... | collective-permute-start | bytes 294920 | tf_op jit(solution)/shard_map/ppermute | solution.py:290
  32.2 11.6 %operator.1.refs_0_ = bf16[4,1024,1024]{2,1,0:T(8,128)(2,1)} custom-call(s32[2]{0:T(128)S(1)} %pad_add_fusion.ids_ref, s32[1]{0:T(128)S(6)} %copy.13.live_ref, s32[128]{0:T(128)S(1)} %bitcast.10, s32[128]{0:T(128)S(1)} %bitcast.11, f32[128,128,128]{2,1,0:T(8,128)} %bitcast.12), custom_call_target="tpu_custom_call" | custom-call | bytes 41943040 | tf_op jit(solution)/shard_map/operator/pallas_call | solution.py:161
  43.8 2.0 %collective-permute-start.1 = (f32[512,128]{1,0:T(8,128)S(1)}, f32[512,128]{1,0:T(8,128)S(1)}, u32[]{:S(2)}, u32[]{:S(2)}) collective-permute-start(f32[512,128]{1,0:T(8,128)S(1)} %collective-permute-done.refs_1_), channel_id=1, source_target_pairs={{0,1},{1,2},{2,3},{3,0},{4,5},{5,6},{6,7},{7,4},{8,9},{9,10},{10,1... | collective-permute-start | bytes 786440 | tf_op jit(solution)/shard_map/ppermute | solution.py:295
  45.9 3.4 %copy-done = bf16[4,1024,1024]{2,1,0:T(8,128)(2,1)S(1)} copy-done((bf16[4,1024,1024]{2,1,0:T(8,128)(2,1)S(1)}, bf16[4,1024,1024]{2,1,0:T(8,128)(2,1)}, u32[]{:S(2)}) %copy-start) | copy-done | bytes 8388632
  49.2 1.9 %product.18.refs_3_ = f32[1024,128]{1,0:T(8,128)S(1)} custom-call(bf16[4,1024,1024]{2,1,0:T(8,128)(2,1)S(1)} %copy-done, f32[512,128]{1,0:T(8,128)S(1)} %get-tuple-element.67.refs_1_), custom_call_target="tpu_custom_call" | custom-call | flops 536870912 | bytes 3407872 | tf_op jit(solution)/shard_map/product/pallas_call | solution.py:225
  51.2 2.6 %collective-permute-start.43 = (f32[96,256]{1,0:T(8,128)S(1)}, f32[96,256]{1,0:T(8,128)S(1)}, u32[]{:S(2)}, u32[]{:S(2)}) collective-permute-start(f32[96,256]{1,0:T(8,128)S(1)} %get-tuple-element.88), channel_id=1, source_target_pairs={{0,16},{4,20},{8,24},{12,28},{16,0},{20,4},{24,8},{28,12},{1,17},{... | collective-permute-start | bytes 294920 | tf_op jit(solution)/shard_map/ppermute | solution.py:290
  53.8 3.4 %product.19.refs_2_ = f32[1024,128]{1,0:T(8,128)S(1)} custom-call(bf16[4,1024,1024]{2,1,0:T(8,128)(2,1)S(1)} %copy-done, f32[512,128]{1,0:T(8,128)S(1)} %collective-permute-done.20.refs_1_, f32[512,128]{1,0:T(8,128)S(1)} %collective-permute-done.22.refs_2_, f32[1024,128]{1,0:T(8,128)S(1)} %product.18.refs_3_), custom_call_target="tpu_custom_call" | custom-call | flops 1073741824 | bytes 5767168 | tf_op jit(solution)/shard_map/product/pallas_call | solution.py:225
  57.3 1.9 %product.20 = (f32[128,128]{1,0:T(8,128)S(1)}, f32[128,128]{1,0:T(8,128)S(1)}, f32[128,128]{1,0:T(8,128)S(1)}, f32[128,128]{1,0:T(8,128)S(1)}, f32[128,128]{1,0:...) custom-call(bf16[4,1024,1024]{2,1,0:T(8,128)(2,1)S(1)} %copy-done, ...), custom_call_target="tpu_custom_call" | custom-call | flops 536870912 | bytes 3407872 | tf_op jit(solution)/shard_map/product/pallas_call | solution.py:225
  60.3 1.9 %product.12.refs_3_ = f32[1024,128]{1,0:T(8,128)S(1)} custom-call(bf16[4,1024,1024]{2,1,0:T(8,128)(2,1)S(1)} %copy-done, f32[512,128]{1,0:T(8,128)S(1)} %get-tuple-element.49.refs_1_), custom_call_target="tpu_custom_call" | custom-call | flops 536870912 | bytes 3407872 | tf_op jit(solution)/shard_map/product/pallas_call | solution.py:225
  62.2 1.0 collective-permute-start.25
  63.1 1.7 %collective-permute-start.26 = (f32[128,128]{1,0:T(8,128)S(1)}, f32[128,128]{1,0:T(8,128)S(1)}, u32[]{:S(2)}, u32[]{:S(2)}) collective-permute-start(f32[128,128]{1,0:T(8,128)S(1)} %get-tuple-element.72), channel_id=1, source_target_pairs={{0,16},{4,20},{8,24},{12,28},{16,0},{20,4},{24,8},{28,12},{1,17},{... | collective-permute-start | bytes 196616 | tf_op jit(solution)/shard_map/ppermute | solution.py:290
  65.2 1.1 collective-permute-start.28
  66.3 1.2 collective-permute-start.29
  67.6 3.4 %product.13.refs_2_ = f32[1024,128]{1,0:T(8,128)S(1)} custom-call(bf16[4,1024,1024]{2,1,0:T(8,128)(2,1)S(1)} %copy-done, f32[512,128]{1,0:T(8,128)S(1)} %collective-permute-done.refs_1_, f32[512,128]{1,0:T(8,128)S(1)} %collective-permute-done.2.refs_2_, f32[1024,128]{1,0:T(8,128)S(1)} %product.12.refs_3_), custom_call_target="tpu_custom_call" | custom-call | flops 1073741824 | bytes 5767168 | tf_op jit(solution)/shard_map/product/pallas_call | solution.py:225
  71.0 1.8 %collective-permute-start.45 = (f32[96,256]{1,0:T(8,128)S(1)}, f32[96,256]{1,0:T(8,128)S(1)}, u32[]{:S(2)}, u32[]{:S(2)}) collective-permute-start(f32[96,256]{1,0:T(8,128)S(1)} %get-tuple-element.90), channel_id=1, source_target_pairs={{0,24},{4,28},{8,16},{12,20},{16,8},{20,12},{24,0},{28,4},{1,25},{... | collective-permute-start | bytes 294920 | tf_op jit(solution)/shard_map/ppermute | solution.py:290
  72.8 1.2 collective-permute-start.46
  74.0 1.9 %product.14 = (f32[128,128]{1,0:T(8,128)S(1)}, f32[128,128]{1,0:T(8,128)S(1)}, f32[128,128]{1,0:T(8,128)S(1)}, f32[128,128]{1,0:T(8,128)S(1)}, f32[128,128]{1,0:...) custom-call(bf16[4,1024,1024]{2,1,0:T(8,128)(2,1)S(1)} %copy-done, ...), custom_call_target="tpu_custom_call" | custom-call | flops 536870912 | bytes 3407872 | tf_op jit(solution)/shard_map/product/pallas_call | solution.py:225
  78.5 1.7 %collective-permute-start.6 = (f32[128,128]{1,0:T(8,128)S(1)}, f32[128,128]{1,0:T(8,128)S(1)}, u32[]{:S(2)}, u32[]{:S(2)}) collective-permute-start(f32[128,128]{1,0:T(8,128)S(1)} %get-tuple-element.54), channel_id=1, source_target_pairs={{0,16},{4,20},{8,24},{12,28},{16,0},{20,4},{24,8},{28,12},{1,17},{... | collective-permute-start | bytes 196616 | tf_op jit(solution)/shard_map/ppermute | solution.py:290
  80.8 1.3 collective-permute-start.8
  82.1 1.1 collective-permute-start.9
  83.2 2.2 %collective-permute-start.30 = (f32[512,128]{1,0:T(8,128)S(1)}, f32[512,128]{1,0:T(8,128)S(1)}, u32[]{:S(2)}, u32[]{:S(2)}) collective-permute-start(f32[512,128]{1,0:T(8,128)S(1)} %collect.4.refs_1_), channel_id=1, source_target_pairs={{0,3},{1,0},{2,1},{3,2},{4,7},{5,4},{6,5},{7,6},{8,11},{9,8},{10,9... | collective-permute-start | bytes 786440 | tf_op jit(solution)/shard_map/ppermute | solution.py:295
  86.0 1.4 collective-permute-done.9.refs_7_
  88.4 5.8 %collective-permute-done.47 = f32[96,256]{1,0:T(8,128)S(1)} collective-permute-done((f32[96,256]{1,0:T(8,128)S(1)}, f32[96,256]{1,0:T(8,128)S(1)}, u32[]{:S(2)}, u32[]{:S(2)}) %collective-permute-start.47) | collective-permute-done | bytes 98336 | tf_op jit(solution)/shard_map/ppermute | solution.py:302
  94.2 1.1 collective-permute-start.48
  95.3 2.0 %collective-permute-start.32 = (f32[512,128]{1,0:T(8,128)S(1)}, f32[512,128]{1,0:T(8,128)S(1)}, u32[]{:S(2)}, u32[]{:S(2)}) collective-permute-start(f32[512,128]{1,0:T(8,128)S(1)} %collect.4.refs_1_), channel_id=1, source_target_pairs={{0,1},{1,2},{2,3},{3,0},{4,5},{5,6},{6,7},{7,4},{8,9},{9,10},{10,1... | collective-permute-start | bytes 786440 | tf_op jit(solution)/shard_map/ppermute | solution.py:295
  97.3 1.9 %collective-permute-start.31 = (f32[512,128]{1,0:T(8,128)S(1)}, f32[512,128]{1,0:T(8,128)S(1)}, u32[]{:S(2)}, u32[]{:S(2)}) collective-permute-start(f32[512,128]{1,0:T(8,128)S(1)} %collective-permute-done.30.refs_1_), channel_id=1, source_target_pairs={{0,3},{1,0},{2,1},{3,2},{4,7},{5,4},{6,5},{7,6},{8,11},{9,8},{10,9... | collective-permute-start | bytes 786440 | tf_op jit(solution)/shard_map/ppermute | solution.py:295
  99.1 11.0 %collective-permute-done.48 = f32[96,256]{1,0:T(8,128)S(1)} collective-permute-done((f32[96,256]{1,0:T(8,128)S(1)}, f32[96,256]{1,0:T(8,128)S(1)}, u32[]{:S(2)}, u32[]{:S(2)}) %collective-permute-start.48) | collective-permute-done | bytes 98336 | tf_op jit(solution)/shard_map/ppermute | solution.py:302
  111.5 2.0 %collective-permute-start.11 = (f32[512,128]{1,0:T(8,128)S(1)}, f32[512,128]{1,0:T(8,128)S(1)}, u32[]{:S(2)}, u32[]{:S(2)}) collective-permute-start(f32[512,128]{1,0:T(8,128)S(1)} %collective-permute-done.10.refs_1_), channel_id=1, source_target_pairs={{0,1},{1,2},{2,3},{3,0},{4,5},{5,6},{6,7},{7,4},{8,9},{9,10},{10,1... | collective-permute-start | bytes 786440 | tf_op jit(solution)/shard_map/ppermute | solution.py:295
  113.6 1.9 %collective-permute-done.50.refs_2_ = f32[96,256]{1,0:T(8,128)S(1)} collective-permute-done((f32[96,256]{1,0:T(8,128)S(1)}, f32[96,256]{1,0:T(8,128)S(1)}, u32[]{:S(2)}, u32[]{:S(2)}) %collective-permute-start.50) | collective-permute-done | bytes 98336 | tf_op jit(solution)/shard_map/ppermute | solution.py:290
  115.5 1.9 %product.21.refs_3_ = f32[1024,128]{1,0:T(8,128)S(1)} custom-call(bf16[4,1024,1024]{2,1,0:T(8,128)(2,1)S(1)} %copy-done, f32[512,128]{1,0:T(8,128)S(1)} %collect.4.refs_1_), custom_call_target="tpu_custom_call" | custom-call | flops 536870912 | bytes 3407872 | tf_op jit(solution)/shard_map/product/pallas_call | solution.py:225
  117.4 1.9 %product.15.refs_3_ = f32[1024,128]{1,0:T(8,128)S(1)} custom-call(bf16[4,1024,1024]{2,1,0:T(8,128)(2,1)S(1)} %copy-done, f32[512,128]{1,0:T(8,128)S(1)} %collect.3.refs_1_), custom_call_target="tpu_custom_call" | custom-call | flops 536870912 | bytes 3407872 | tf_op jit(solution)/shard_map/product/pallas_call | solution.py:225
  119.3 1.1 collective-permute-done.51.refs_3_
  120.4 1.2 collective-permute-start.52
  121.7 1.8 %collective-permute-start.54 = (f32[96,256]{1,0:T(8,128)S(1)}, f32[96,256]{1,0:T(8,128)S(1)}, u32[]{:S(2)}, u32[]{:S(2)}) collective-permute-start(f32[96,256]{1,0:T(8,128)S(1)} %add.35.refs_0_), channel_id=1, source_target_pairs={{0,24},{4,28},{8,16},{12,20},{16,8},{20,12},{24,0},{28,4},{1,25},{... | collective-permute-start | bytes 294920 | tf_op jit(solution)/shard_map/ppermute | solution.py:290
  123.5 3.4 %product.22.refs_2_ = f32[1024,128]{1,0:T(8,128)S(1)} custom-call(bf16[4,1024,1024]{2,1,0:T(8,128)(2,1)S(1)} %copy-done, f32[512,128]{1,0:T(8,128)S(1)} %collective-permute-done.30.refs_1_, f32[512,128]{1,0:T(8,128)S(1)} %collective-permute-done.32.refs_2_, f32[1024,128]{1,0:T(8,128)S(1)} %product.21.refs_3_), custom_call_target="tpu_custom_call" | custom-call | flops 1073741824 | bytes 5767168 | tf_op jit(solution)/shard_map/product/pallas_call | solution.py:225
  126.8 1.9 %product.23 = (f32[128,128]{1,0:T(8,128)S(1)}, f32[128,128]{1,0:T(8,128)S(1)}, f32[128,128]{1,0:T(8,128)S(1)}, f32[128,128]{1,0:T(8,128)S(1)}, f32[128,128]{1,0:...) custom-call(bf16[4,1024,1024]{2,1,0:T(8,128)(2,1)S(1)} %copy-done, ...), custom_call_target="tpu_custom_call" | custom-call | flops 536870912 | bytes 3407872 | tf_op jit(solution)/shard_map/product/pallas_call | solution.py:225
  128.8 1.4 collective-permute-start.55
  130.2 1.1 collective-permute-start.34
  132.0 1.2 collective-permute-start.36
  133.2 3.4 %product.16.refs_2_ = f32[1024,128]{1,0:T(8,128)S(1)} custom-call(bf16[4,1024,1024]{2,1,0:T(8,128)(2,1)S(1)} %copy-done, f32[512,128]{1,0:T(8,128)S(1)} %collective-permute-done.10.refs_1_, f32[512,128]{1,0:T(8,128)S(1)} %collective-permute-done.12.refs_2_, f32[1024,128]{1,0:T(8,128)S(1)} %product.15.refs_3_), custom_call_target="tpu_custom_call" | custom-call | flops 1073741824 | bytes 5767168 | tf_op jit(solution)/shard_map/product/pallas_call | solution.py:225
  136.6 1.9 %product.17 = (f32[128,128]{1,0:T(8,128)S(1)}, f32[128,128]{1,0:T(8,128)S(1)}, f32[128,128]{1,0:T(8,128)S(1)}, f32[128,128]{1,0:T(8,128)S(1)}, f32[128,128]{1,0:...) custom-call(bf16[4,1024,1024]{2,1,0:T(8,128)(2,1)S(1)} %copy-done, ...), custom_call_target="tpu_custom_call" | custom-call | flops 536870912 | bytes 3407872 | tf_op jit(solution)/shard_map/product/pallas_call | solution.py:225
  139.1 1.6 %collective-permute-start.38 = (f32[128,128]{1,0:T(8,128)S(1)}, f32[128,128]{1,0:T(8,128)S(1)}, u32[]{:S(2)}, u32[]{:S(2)}) collective-permute-start(f32[128,128]{1,0:T(8,128)S(1)} %get-tuple-element.82), channel_id=1, source_target_pairs={{0,24},{4,28},{8,16},{12,20},{16,8},{20,12},{24,0},{28,4},{1,25},{... | collective-permute-start | bytes 196616 | tf_op jit(solution)/shard_map/ppermute | solution.py:290
  140.8 1.0 collective-permute-start.39
  142.2 1.0 collective-permute-start.14
  144.5 1.3 collective-permute-start.16
  146.6 1.7 %collective-permute-start.18 = (f32[128,128]{1,0:T(8,128)S(1)}, f32[128,128]{1,0:T(8,128)S(1)}, u32[]{:S(2)}, u32[]{:S(2)}) collective-permute-start(f32[128,128]{1,0:T(8,128)S(1)} %get-tuple-element.64), channel_id=1, source_target_pairs={{0,24},{4,28},{8,16},{12,20},{16,8},{20,12},{24,0},{28,4},{1,25},{... | collective-permute-start | bytes 196616 | tf_op jit(solution)/shard_map/ppermute | solution.py:290
  148.3 1.0 collective-permute-start.19
  149.3 1.5 assemble.1
  150.7 1.2 collective-permute-done.18.refs_6_
  151.9 1.6 %collective-permute-done.19.refs_7_ = f32[128,128]{1,0:T(8,128)S(1)} collective-permute-done((f32[128,128]{1,0:T(8,128)S(1)}, f32[128,128]{1,0:T(8,128)S(1)}, u32[]{:S(2)}, u32[]{:S(2)}) %collective-permute-start.19) | collective-permute-done | bytes 65568 | tf_op jit(solution)/shard_map/ppermute | solution.py:290
  153.5 1.5 collect.5
  (97 shorter events, 13.6 us)
Async XLA Ops:
  0.6 1.1 copy-start.1
  1.8 1.0 copy-start.3
  2.8 1.0 copy-start.5
  4.3 11.8 %collective-permute-start.20 = (f32[512,128]{1,0:T(8,128)S(1)}, f32[512,128]{1,0:T(8,128)S(1)}, u32[]{:S(2)}, u32[]{:S(2)}) collective-permute-start(f32[512,128]{1,0:T(8,128)S(1)} %get-tuple-element.67.refs_1_), channel_id=1, source_target_pairs={{0,3},{1,0},{2,1},{3,2},{4,7},{5,4},{6,5},{7,6},{8,11},{9,8},{10,9... | collective-permute-start | bytes 786440 | tf_op jit(solution)/shard_map/ppermute | solution.py:295
  9.4 41.9 %collective-permute-start.22 = (f32[512,128]{1,0:T(8,128)S(1)}, f32[512,128]{1,0:T(8,128)S(1)}, u32[]{:S(2)}, u32[]{:S(2)}) collective-permute-start(f32[512,128]{1,0:T(8,128)S(1)} %get-tuple-element.67.refs_1_), channel_id=1, source_target_pairs={{0,1},{1,2},{2,3},{3,0},{4,5},{5,6},{6,7},{7,4},{8,9},{9,10},{10,1... | collective-permute-start | bytes 786440 | tf_op jit(solution)/shard_map/ppermute | solution.py:295
  9.4 34.5 %collective-permute-start = (f32[512,128]{1,0:T(8,128)S(1)}, f32[512,128]{1,0:T(8,128)S(1)}, u32[]{:S(2)}, u32[]{:S(2)}) collective-permute-start(f32[512,128]{1,0:T(8,128)S(1)} %get-tuple-element.49.refs_1_), channel_id=1, source_target_pairs={{0,1},{1,2},{2,3},{3,0},{4,5},{5,6},{6,7},{7,4},{8,9},{9,10},{10,1... | collective-permute-start | bytes 786440 | tf_op jit(solution)/shard_map/ppermute | solution.py:295
  16.1 41.1 %collective-permute-start.21 = (f32[512,128]{1,0:T(8,128)S(1)}, f32[512,128]{1,0:T(8,128)S(1)}, u32[]{:S(2)}, u32[]{:S(2)}) collective-permute-start(f32[512,128]{1,0:T(8,128)S(1)} %collective-permute-done.20.refs_1_), channel_id=1, source_target_pairs={{0,3},{1,0},{2,1},{3,2},{4,7},{5,4},{6,5},{7,6},{8,11},{9,8},{10,9... | collective-permute-start | bytes 786440 | tf_op jit(solution)/shard_map/ppermute | solution.py:295
  20.4 1.1 copy-start.2
  21.5 1.0 copy-start.4
  22.5 1.0 copy-start.6
  28.6 15.2 %collective-permute-start.40 = (f32[96,256]{1,0:T(8,128)S(1)}, f32[96,256]{1,0:T(8,128)S(1)}, u32[]{:S(2)}, u32[]{:S(2)}) collective-permute-start(f32[96,256]{1,0:T(8,128)S(1)} %get-tuple-element.85), channel_id=1, source_target_pairs={{0,4},{4,0},{8,12},{12,8},{16,20},{20,16},{24,28},{28,24},{1,5},{5... | collective-permute-start | bytes 294920 | tf_op jit(solution)/shard_map/ppermute | solution.py:290
  28.7 22.5 %collective-permute-start.41 = (f32[96,256]{1,0:T(8,128)S(1)}, f32[96,256]{1,0:T(8,128)S(1)}, u32[]{:S(2)}, u32[]{:S(2)}) collective-permute-start(f32[96,256]{1,0:T(8,128)S(1)} %get-tuple-element.86), channel_id=1, source_target_pairs={{0,8},{4,12},{8,0},{12,4},{16,24},{20,28},{24,16},{28,20},{1,9},{5... | collective-permute-start | bytes 294920 | tf_op jit(solution)/shard_map/ppermute | solution.py:290
  43.8 19.4 %collective-permute-start.2 = (f32[512,128]{1,0:T(8,128)S(1)}, f32[512,128]{1,0:T(8,128)S(1)}, u32[]{:S(2)}, u32[]{:S(2)}) collective-permute-start(f32[512,128]{1,0:T(8,128)S(1)} %get-tuple-element.49.refs_1_), channel_id=1, source_target_pairs={{0,3},{1,0},{2,1},{3,2},{4,7},{5,4},{6,5},{7,6},{8,11},{9,8},{10,9... | collective-permute-start | bytes 786440 | tf_op jit(solution)/shard_map/ppermute | solution.py:295
  43.8 21.0 %collective-permute-start.1 = (f32[512,128]{1,0:T(8,128)S(1)}, f32[512,128]{1,0:T(8,128)S(1)}, u32[]{:S(2)}, u32[]{:S(2)}) collective-permute-start(f32[512,128]{1,0:T(8,128)S(1)} %collective-permute-done.refs_1_), channel_id=1, source_target_pairs={{0,1},{1,2},{2,3},{3,0},{4,5},{5,6},{6,7},{7,4},{8,9},{9,10},{10,1... | collective-permute-start | bytes 786440 | tf_op jit(solution)/shard_map/ppermute | solution.py:295
  45.9 3.4 %copy-start = (bf16[4,1024,1024]{2,1,0:T(8,128)(2,1)S(1)}, bf16[4,1024,1024]{2,1,0:T(8,128)(2,1)}, u32[]{:S(2)}) copy-start(bf16[4,1024,1024]{2,1,0:T(8,128)(2,1)} %operator.1.refs_0_) | copy-start | bytes 25165828
  51.2 8.0 %collective-permute-start.42 = (f32[96,256]{1,0:T(8,128)S(1)}, f32[96,256]{1,0:T(8,128)S(1)}, u32[]{:S(2)}, u32[]{:S(2)}) collective-permute-start(f32[96,256]{1,0:T(8,128)S(1)} %get-tuple-element.87), channel_id=1, source_target_pairs={{0,12},{4,8},{8,4},{12,0},{16,28},{20,24},{24,20},{28,16},{1,13},{... | collective-permute-start | bytes 294920 | tf_op jit(solution)/shard_map/ppermute | solution.py:290
  51.2 8.1 %collective-permute-start.43 = (f32[96,256]{1,0:T(8,128)S(1)}, f32[96,256]{1,0:T(8,128)S(1)}, u32[]{:S(2)}, u32[]{:S(2)}) collective-permute-start(f32[96,256]{1,0:T(8,128)S(1)} %get-tuple-element.88), channel_id=1, source_target_pairs={{0,16},{4,20},{8,24},{12,28},{16,0},{20,4},{24,8},{28,12},{1,17},{... | collective-permute-start | bytes 294920 | tf_op jit(solution)/shard_map/ppermute | solution.py:290
  57.2 5.0 %collective-permute-start.44 = (f32[96,256]{1,0:T(8,128)S(1)}, f32[96,256]{1,0:T(8,128)S(1)}, u32[]{:S(2)}, u32[]{:S(2)}) collective-permute-start(f32[96,256]{1,0:T(8,128)S(1)} %get-tuple-element.89), channel_id=1, source_target_pairs={{0,20},{4,16},{8,28},{12,24},{16,4},{20,0},{24,12},{28,8},{1,21},{... | collective-permute-start | bytes 294920 | tf_op jit(solution)/shard_map/ppermute | solution.py:290
  59.2 6.0 %collective-permute-start.23 = (f32[128,128]{1,0:T(8,128)S(1)}, f32[128,128]{1,0:T(8,128)S(1)}, u32[]{:S(2)}, u32[]{:S(2)}) collective-permute-start(f32[128,128]{1,0:T(8,128)S(1)} %get-tuple-element.69), channel_id=1, source_target_pairs={{0,4},{4,0},{8,12},{12,8},{16,20},{20,16},{24,28},{28,24},{1,5},{5... | collective-permute-start | bytes 196616 | tf_op jit(solution)/shard_map/ppermute | solution.py:290
  59.4 7.0 %collective-permute-start.24 = (f32[128,128]{1,0:T(8,128)S(1)}, f32[128,128]{1,0:T(8,128)S(1)}, u32[]{:S(2)}, u32[]{:S(2)}) collective-permute-start(f32[128,128]{1,0:T(8,128)S(1)} %get-tuple-element.70), channel_id=1, source_target_pairs={{0,8},{4,12},{8,0},{12,4},{16,24},{20,28},{24,16},{28,20},{1,9},{5... | collective-permute-start | bytes 196616 | tf_op jit(solution)/shard_map/ppermute | solution.py:290
  62.2 8.8 %collective-permute-start.25 = (f32[128,128]{1,0:T(8,128)S(1)}, f32[128,128]{1,0:T(8,128)S(1)}, u32[]{:S(2)}, u32[]{:S(2)}) collective-permute-start(f32[128,128]{1,0:T(8,128)S(1)} %get-tuple-element.71), channel_id=1, source_target_pairs={{0,12},{4,8},{8,4},{12,0},{16,28},{20,24},{24,20},{28,16},{1,13},{... | collective-permute-start | bytes 196616 | tf_op jit(solution)/shard_map/ppermute | solution.py:290
  63.1 9.7 %collective-permute-start.26 = (f32[128,128]{1,0:T(8,128)S(1)}, f32[128,128]{1,0:T(8,128)S(1)}, u32[]{:S(2)}, u32[]{:S(2)}) collective-permute-start(f32[128,128]{1,0:T(8,128)S(1)} %get-tuple-element.72), channel_id=1, source_target_pairs={{0,16},{4,20},{8,24},{12,28},{16,0},{20,4},{24,8},{28,12},{1,17},{... | collective-permute-start | bytes 196616 | tf_op jit(solution)/shard_map/ppermute | solution.py:290
  64.8 11.1 %collective-permute-start.27 = (f32[128,128]{1,0:T(8,128)S(1)}, f32[128,128]{1,0:T(8,128)S(1)}, u32[]{:S(2)}, u32[]{:S(2)}) collective-permute-start(f32[128,128]{1,0:T(8,128)S(1)} %get-tuple-element.73), channel_id=1, source_target_pairs={{0,20},{4,16},{8,28},{12,24},{16,4},{20,0},{24,12},{28,8},{1,21},{... | collective-permute-start | bytes 196616 | tf_op jit(solution)/shard_map/ppermute | solution.py:290
  65.2 10.8 %collective-permute-start.28 = (f32[128,128]{1,0:T(8,128)S(1)}, f32[128,128]{1,0:T(8,128)S(1)}, u32[]{:S(2)}, u32[]{:S(2)}) collective-permute-start(f32[128,128]{1,0:T(8,128)S(1)} %get-tuple-element.74), channel_id=1, source_target_pairs={{0,24},{4,28},{8,16},{12,20},{16,8},{20,12},{24,0},{28,4},{1,25},{... | collective-permute-start | bytes 196616 | tf_op jit(solution)/shard_map/ppermute | solution.py:290
  66.3 11.5 %copy-start.7 = (s32[1,8,1]{1,2,0:T(1,128)S(1)}, s32[1,8,1]{1,2,0:T(1,128)}, u32[]{:S(2)}) copy-start(s32[1,8,1]{1,2,0:T(1,128)} %param.20) | copy-start | bytes 100
  66.3 10.6 %collective-permute-start.29 = (f32[128,128]{1,0:T(8,128)S(1)}, f32[128,128]{1,0:T(8,128)S(1)}, u32[]{:S(2)}, u32[]{:S(2)}) collective-permute-start(f32[128,128]{1,0:T(8,128)S(1)} %get-tuple-element.75), channel_id=1, source_target_pairs={{0,28},{4,24},{8,20},{12,16},{16,12},{20,8},{24,4},{28,0},{1,29},{... | collective-permute-start | bytes 196616 | tf_op jit(solution)/shard_map/ppermute | solution.py:290
  71.0 7.5 %collective-permute-start.45 = (f32[96,256]{1,0:T(8,128)S(1)}, f32[96,256]{1,0:T(8,128)S(1)}, u32[]{:S(2)}, u32[]{:S(2)}) collective-permute-start(f32[96,256]{1,0:T(8,128)S(1)} %get-tuple-element.90), channel_id=1, source_target_pairs={{0,24},{4,28},{8,16},{12,20},{16,8},{20,12},{24,0},{28,4},{1,25},{... | collective-permute-start | bytes 294920 | tf_op jit(solution)/shard_map/ppermute | solution.py:290
  72.8 7.4 %collective-permute-start.46 = (f32[96,256]{1,0:T(8,128)S(1)}, f32[96,256]{1,0:T(8,128)S(1)}, u32[]{:S(2)}, u32[]{:S(2)}) collective-permute-start(f32[96,256]{1,0:T(8,128)S(1)} %get-tuple-element.91), channel_id=1, source_target_pairs={{0,28},{4,24},{8,20},{12,16},{16,12},{20,8},{24,4},{28,0},{1,29},{... | collective-permute-start | bytes 294920 | tf_op jit(solution)/shard_map/ppermute | solution.py:290
  75.9 4.9 %collective-permute-start.3 = (f32[128,128]{1,0:T(8,128)S(1)}, f32[128,128]{1,0:T(8,128)S(1)}, u32[]{:S(2)}, u32[]{:S(2)}) collective-permute-start(f32[128,128]{1,0:T(8,128)S(1)} %get-tuple-element.51), channel_id=1, source_target_pairs={{0,4},{4,0},{8,12},{12,8},{16,20},{20,16},{24,28},{28,24},{1,5},{5... | collective-permute-start | bytes 196616 | tf_op jit(solution)/shard_map/ppermute | solution.py:290
  76.1 6.0 %collective-permute-start.4 = (f32[128,128]{1,0:T(8,128)S(1)}, f32[128,128]{1,0:T(8,128)S(1)}, u32[]{:S(2)}, u32[]{:S(2)}) collective-permute-start(f32[128,128]{1,0:T(8,128)S(1)} %get-tuple-element.52), channel_id=1, source_target_pairs={{0,8},{4,12},{8,0},{12,4},{16,24},{20,28},{24,16},{28,20},{1,9},{5... | collective-permute-start | bytes 196616 | tf_op jit(solution)/shard_map/ppermute | solution.py:290
  76.9 6.3 %collective-permute-start.5 = (f32[128,128]{1,0:T(8,128)S(1)}, f32[128,128]{1,0:T(8,128)S(1)}, u32[]{:S(2)}, u32[]{:S(2)}) collective-permute-start(f32[128,128]{1,0:T(8,128)S(1)} %get-tuple-element.53), channel_id=1, source_target_pairs={{0,12},{4,8},{8,4},{12,0},{16,28},{20,24},{24,20},{28,16},{1,13},{... | collective-permute-start | bytes 196616 | tf_op jit(solution)/shard_map/ppermute | solution.py:290
  78.5 6.9 %collective-permute-start.6 = (f32[128,128]{1,0:T(8,128)S(1)}, f32[128,128]{1,0:T(8,128)S(1)}, u32[]{:S(2)}, u32[]{:S(2)}) collective-permute-start(f32[128,128]{1,0:T(8,128)S(1)} %get-tuple-element.54), channel_id=1, source_target_pairs={{0,16},{4,20},{8,24},{12,28},{16,0},{20,4},{24,8},{28,12},{1,17},{... | collective-permute-start | bytes 196616 | tf_op jit(solution)/shard_map/ppermute | solution.py:290
  80.2 5.3 %collective-permute-start.7 = (f32[128,128]{1,0:T(8,128)S(1)}, f32[128,128]{1,0:T(8,128)S(1)}, u32[]{:S(2)}, u32[]{:S(2)}) collective-permute-start(f32[128,128]{1,0:T(8,128)S(1)} %get-tuple-element.55), channel_id=1, source_target_pairs={{0,20},{4,16},{8,28},{12,24},{16,4},{20,0},{24,12},{28,8},{1,21},{... | collective-permute-start | bytes 196616 | tf_op jit(solution)/shard_map/ppermute | solution.py:290
  80.8 5.2 %collective-permute-start.8 = (f32[128,128]{1,0:T(8,128)S(1)}, f32[128,128]{1,0:T(8,128)S(1)}, u32[]{:S(2)}, u32[]{:S(2)}) collective-permute-start(f32[128,128]{1,0:T(8,128)S(1)} %get-tuple-element.56), channel_id=1, source_target_pairs={{0,24},{4,28},{8,16},{12,20},{16,8},{20,12},{24,0},{28,4},{1,25},{... | collective-permute-start | bytes 196616 | tf_op jit(solution)/shard_map/ppermute | solution.py:290
  82.1 5.3 %collective-permute-start.9 = (f32[128,128]{1,0:T(8,128)S(1)}, f32[128,128]{1,0:T(8,128)S(1)}, u32[]{:S(2)}, u32[]{:S(2)}) collective-permute-start(f32[128,128]{1,0:T(8,128)S(1)} %get-tuple-element.57), channel_id=1, source_target_pairs={{0,28},{4,24},{8,20},{12,16},{16,12},{20,8},{24,4},{28,0},{1,29},{... | collective-permute-start | bytes 196616 | tf_op jit(solution)/shard_map/ppermute | solution.py:290
  83.2 14.0 %collective-permute-start.30 = (f32[512,128]{1,0:T(8,128)S(1)}, f32[512,128]{1,0:T(8,128)S(1)}, u32[]{:S(2)}, u32[]{:S(2)}) collective-permute-start(f32[512,128]{1,0:T(8,128)S(1)} %collect.4.refs_1_), channel_id=1, source_target_pairs={{0,3},{1,0},{2,1},{3,2},{4,7},{5,4},{6,5},{7,6},{8,11},{9,8},{10,9... | collective-permute-start | bytes 786440 | tf_op jit(solution)/shard_map/ppermute | solution.py:295
  85.4 8.7 %collective-permute-start.47 = (f32[96,256]{1,0:T(8,128)S(1)}, f32[96,256]{1,0:T(8,128)S(1)}, u32[]{:S(2)}, u32[]{:S(2)}) collective-permute-start(f32[96,256]{1,0:T(8,128)S(1)} %add_add_fusion), channel_id=1, source_target_pairs={{0,1},{1,0},{2,3},{3,2},{4,5},{5,4},{6,7},{7,6},{8,9},{9,8},{10,11... | collective-permute-start | bytes 294920 | tf_op jit(solution)/shard_map/ppermute | solution.py:302
  88.1 23.5 %collective-permute-start.10 = (f32[512,128]{1,0:T(8,128)S(1)}, f32[512,128]{1,0:T(8,128)S(1)}, u32[]{:S(2)}, u32[]{:S(2)}) collective-permute-start(f32[512,128]{1,0:T(8,128)S(1)} %collect.3.refs_1_), channel_id=1, source_target_pairs={{0,1},{1,2},{2,3},{3,0},{4,5},{5,6},{6,7},{7,4},{8,9},{9,10},{10,1... | collective-permute-start | bytes 786440 | tf_op jit(solution)/shard_map/ppermute | solution.py:295
  94.2 15.9 %collective-permute-start.48 = (f32[96,256]{1,0:T(8,128)S(1)}, f32[96,256]{1,0:T(8,128)S(1)}, u32[]{:S(2)}, u32[]{:S(2)}) collective-permute-start(f32[96,256]{1,0:T(8,128)S(1)} %add.34), channel_id=1, source_target_pairs={{0,2},{1,3},{2,0},{3,1},{4,6},{5,7},{6,4},{7,5},{8,10},{9,11},{10,... | collective-permute-start | bytes 294920 | tf_op jit(solution)/shard_map/ppermute | solution.py:302
  95.3 26.3 %collective-permute-start.32 = (f32[512,128]{1,0:T(8,128)S(1)}, f32[512,128]{1,0:T(8,128)S(1)}, u32[]{:S(2)}, u32[]{:S(2)}) collective-permute-start(f32[512,128]{1,0:T(8,128)S(1)} %collect.4.refs_1_), channel_id=1, source_target_pairs={{0,1},{1,2},{2,3},{3,0},{4,5},{5,6},{6,7},{7,4},{8,9},{9,10},{10,1... | collective-permute-start | bytes 786440 | tf_op jit(solution)/shard_map/ppermute | solution.py:295
  97.3 24.4 %collective-permute-start.31 = (f32[512,128]{1,0:T(8,128)S(1)}, f32[512,128]{1,0:T(8,128)S(1)}, u32[]{:S(2)}, u32[]{:S(2)}) collective-permute-start(f32[512,128]{1,0:T(8,128)S(1)} %collective-permute-done.30.refs_1_), channel_id=1, source_target_pairs={{0,3},{1,0},{2,1},{3,2},{4,7},{5,4},{6,5},{7,6},{8,11},{9,8},{10,9... | collective-permute-start | bytes 786440 | tf_op jit(solution)/shard_map/ppermute | solution.py:295
  110.2 1.4 collective-permute-start.49
  110.2 5.2 %collective-permute-start.50 = (f32[96,256]{1,0:T(8,128)S(1)}, f32[96,256]{1,0:T(8,128)S(1)}, u32[]{:S(2)}, u32[]{:S(2)}) collective-permute-start(f32[96,256]{1,0:T(8,128)S(1)} %add.35.refs_0_), channel_id=1, source_target_pairs={{0,8},{4,12},{8,0},{12,4},{16,24},{20,28},{24,16},{28,20},{1,9},{5... | collective-permute-start | bytes 294920 | tf_op jit(solution)/shard_map/ppermute | solution.py:290
  111.5 19.8 %collective-permute-start.12 = (f32[512,128]{1,0:T(8,128)S(1)}, f32[512,128]{1,0:T(8,128)S(1)}, u32[]{:S(2)}, u32[]{:S(2)}) collective-permute-start(f32[512,128]{1,0:T(8,128)S(1)} %collect.3.refs_1_), channel_id=1, source_target_pairs={{0,3},{1,0},{2,1},{3,2},{4,7},{5,4},{6,5},{7,6},{8,11},{9,8},{10,9... | collective-permute-start | bytes 786440 | tf_op jit(solution)/shard_map/ppermute | solution.py:295
  111.5 20.5 %collective-permute-start.11 = (f32[512,128]{1,0:T(8,128)S(1)}, f32[512,128]{1,0:T(8,128)S(1)}, u32[]{:S(2)}, u32[]{:S(2)}) collective-permute-start(f32[512,128]{1,0:T(8,128)S(1)} %collective-permute-done.10.refs_1_), channel_id=1, source_target_pairs={{0,1},{1,2},{2,3},{3,0},{4,5},{5,6},{6,7},{7,4},{8,9},{9,10},{10,1... | collective-permute-start | bytes 786440 | tf_op jit(solution)/shard_map/ppermute | solution.py:295
  115.4 4.9 %collective-permute-start.51 = (f32[96,256]{1,0:T(8,128)S(1)}, f32[96,256]{1,0:T(8,128)S(1)}, u32[]{:S(2)}, u32[]{:S(2)}) collective-permute-start(f32[96,256]{1,0:T(8,128)S(1)} %add.35.refs_0_), channel_id=1, source_target_pairs={{0,12},{4,8},{8,4},{12,0},{16,28},{20,24},{24,20},{28,16},{1,13},{... | collective-permute-start | bytes 294920 | tf_op jit(solution)/shard_map/ppermute | solution.py:290
  120.4 8.4 %collective-permute-start.52 = (f32[96,256]{1,0:T(8,128)S(1)}, f32[96,256]{1,0:T(8,128)S(1)}, u32[]{:S(2)}, u32[]{:S(2)}) collective-permute-start(f32[96,256]{1,0:T(8,128)S(1)} %add.35.refs_0_), channel_id=1, source_target_pairs={{0,16},{4,20},{8,24},{12,28},{16,0},{20,4},{24,8},{28,12},{1,17},{... | collective-permute-start | bytes 294920 | tf_op jit(solution)/shard_map/ppermute | solution.py:290
  121.6 8.6 %collective-permute-start.53 = (f32[96,256]{1,0:T(8,128)S(1)}, f32[96,256]{1,0:T(8,128)S(1)}, u32[]{:S(2)}, u32[]{:S(2)}) collective-permute-start(f32[96,256]{1,0:T(8,128)S(1)} %add.35.refs_0_), channel_id=1, source_target_pairs={{0,20},{4,16},{8,28},{12,24},{16,4},{20,0},{24,12},{28,8},{1,21},{... | collective-permute-start | bytes 294920 | tf_op jit(solution)/shard_map/ppermute | solution.py:290
  121.7 8.5 %collective-permute-start.54 = (f32[96,256]{1,0:T(8,128)S(1)}, f32[96,256]{1,0:T(8,128)S(1)}, u32[]{:S(2)}, u32[]{:S(2)}) collective-permute-start(f32[96,256]{1,0:T(8,128)S(1)} %add.35.refs_0_), channel_id=1, source_target_pairs={{0,24},{4,28},{8,16},{12,20},{16,8},{20,12},{24,0},{28,4},{1,25},{... | collective-permute-start | bytes 294920 | tf_op jit(solution)/shard_map/ppermute | solution.py:290
  128.8 9.7 %collective-permute-start.55 = (f32[96,256]{1,0:T(8,128)S(1)}, f32[96,256]{1,0:T(8,128)S(1)}, u32[]{:S(2)}, u32[]{:S(2)}) collective-permute-start(f32[96,256]{1,0:T(8,128)S(1)} %add.35.refs_0_), channel_id=1, source_target_pairs={{0,28},{4,24},{8,20},{12,16},{16,12},{20,8},{24,4},{28,0},{1,29},{... | collective-permute-start | bytes 294920 | tf_op jit(solution)/shard_map/ppermute | solution.py:290
  130.2 9.0 %collective-permute-start.33 = (f32[128,128]{1,0:T(8,128)S(1)}, f32[128,128]{1,0:T(8,128)S(1)}, u32[]{:S(2)}, u32[]{:S(2)}) collective-permute-start(f32[128,128]{1,0:T(8,128)S(1)} %get-tuple-element.77), channel_id=1, source_target_pairs={{0,4},{4,0},{8,12},{12,8},{16,20},{20,16},{24,28},{28,24},{1,5},{5... | collective-permute-start | bytes 196616 | tf_op jit(solution)/shard_map/ppermute | solution.py:290
  130.2 10.6 %collective-permute-start.34 = (f32[128,128]{1,0:T(8,128)S(1)}, f32[128,128]{1,0:T(8,128)S(1)}, u32[]{:S(2)}, u32[]{:S(2)}) collective-permute-start(f32[128,128]{1,0:T(8,128)S(1)} %get-tuple-element.78), channel_id=1, source_target_pairs={{0,8},{4,12},{8,0},{12,4},{16,24},{20,28},{24,16},{28,20},{1,9},{5... | collective-permute-start | bytes 196616 | tf_op jit(solution)/shard_map/ppermute | solution.py:290
  131.3 10.5 %collective-permute-start.35 = (f32[128,128]{1,0:T(8,128)S(1)}, f32[128,128]{1,0:T(8,128)S(1)}, u32[]{:S(2)}, u32[]{:S(2)}) collective-permute-start(f32[128,128]{1,0:T(8,128)S(1)} %get-tuple-element.79), channel_id=1, source_target_pairs={{0,12},{4,8},{8,4},{12,0},{16,28},{20,24},{24,20},{28,16},{1,13},{... | collective-permute-start | bytes 196616 | tf_op jit(solution)/shard_map/ppermute | solution.py:290
  132.0 10.1 %collective-permute-start.36 = (f32[128,128]{1,0:T(8,128)S(1)}, f32[128,128]{1,0:T(8,128)S(1)}, u32[]{:S(2)}, u32[]{:S(2)}) collective-permute-start(f32[128,128]{1,0:T(8,128)S(1)} %get-tuple-element.80), channel_id=1, source_target_pairs={{0,16},{4,20},{8,24},{12,28},{16,0},{20,4},{24,8},{28,12},{1,17},{... | collective-permute-start | bytes 196616 | tf_op jit(solution)/shard_map/ppermute | solution.py:290
  138.5 4.7 %collective-permute-start.37 = (f32[128,128]{1,0:T(8,128)S(1)}, f32[128,128]{1,0:T(8,128)S(1)}, u32[]{:S(2)}, u32[]{:S(2)}) collective-permute-start(f32[128,128]{1,0:T(8,128)S(1)} %get-tuple-element.81), channel_id=1, source_target_pairs={{0,20},{4,16},{8,28},{12,24},{16,4},{20,0},{24,12},{28,8},{1,21},{... | collective-permute-start | bytes 196616 | tf_op jit(solution)/shard_map/ppermute | solution.py:290
  139.1 5.3 %collective-permute-start.38 = (f32[128,128]{1,0:T(8,128)S(1)}, f32[128,128]{1,0:T(8,128)S(1)}, u32[]{:S(2)}, u32[]{:S(2)}) collective-permute-start(f32[128,128]{1,0:T(8,128)S(1)} %get-tuple-element.82), channel_id=1, source_target_pairs={{0,24},{4,28},{8,16},{12,20},{16,8},{20,12},{24,0},{28,4},{1,25},{... | collective-permute-start | bytes 196616 | tf_op jit(solution)/shard_map/ppermute | solution.py:290
  140.8 5.2 %collective-permute-start.39 = (f32[128,128]{1,0:T(8,128)S(1)}, f32[128,128]{1,0:T(8,128)S(1)}, u32[]{:S(2)}, u32[]{:S(2)}) collective-permute-start(f32[128,128]{1,0:T(8,128)S(1)} %get-tuple-element.83), channel_id=1, source_target_pairs={{0,28},{4,24},{8,20},{12,16},{16,12},{20,8},{24,4},{28,0},{1,29},{... | collective-permute-start | bytes 196616 | tf_op jit(solution)/shard_map/ppermute | solution.py:290
  141.8 4.8 %collective-permute-start.13 = (f32[128,128]{1,0:T(8,128)S(1)}, f32[128,128]{1,0:T(8,128)S(1)}, u32[]{:S(2)}, u32[]{:S(2)}) collective-permute-start(f32[128,128]{1,0:T(8,128)S(1)} %get-tuple-element.59), channel_id=1, source_target_pairs={{0,4},{4,0},{8,12},{12,8},{16,20},{20,16},{24,28},{28,24},{1,5},{5... | collective-permute-start | bytes 196616 | tf_op jit(solution)/shard_map/ppermute | solution.py:290
  142.2 6.1 %collective-permute-start.14 = (f32[128,128]{1,0:T(8,128)S(1)}, f32[128,128]{1,0:T(8,128)S(1)}, u32[]{:S(2)}, u32[]{:S(2)}) collective-permute-start(f32[128,128]{1,0:T(8,128)S(1)} %get-tuple-element.60), channel_id=1, source_target_pairs={{0,8},{4,12},{8,0},{12,4},{16,24},{20,28},{24,16},{28,20},{1,9},{5... | collective-permute-start | bytes 196616 | tf_op jit(solution)/shard_map/ppermute | solution.py:290
  143.2 7.5 %collective-permute-start.15 = (f32[128,128]{1,0:T(8,128)S(1)}, f32[128,128]{1,0:T(8,128)S(1)}, u32[]{:S(2)}, u32[]{:S(2)}) collective-permute-start(f32[128,128]{1,0:T(8,128)S(1)} %get-tuple-element.61), channel_id=1, source_target_pairs={{0,12},{4,8},{8,4},{12,0},{16,28},{20,24},{24,20},{28,16},{1,13},{... | collective-permute-start | bytes 196616 | tf_op jit(solution)/shard_map/ppermute | solution.py:290
  144.5 6.3 %collective-permute-start.16 = (f32[128,128]{1,0:T(8,128)S(1)}, f32[128,128]{1,0:T(8,128)S(1)}, u32[]{:S(2)}, u32[]{:S(2)}) collective-permute-start(f32[128,128]{1,0:T(8,128)S(1)} %get-tuple-element.62), channel_id=1, source_target_pairs={{0,16},{4,20},{8,24},{12,28},{16,0},{20,4},{24,8},{28,12},{1,17},{... | collective-permute-start | bytes 196616 | tf_op jit(solution)/shard_map/ppermute | solution.py:290
  146.0 4.7 %collective-permute-start.17 = (f32[128,128]{1,0:T(8,128)S(1)}, f32[128,128]{1,0:T(8,128)S(1)}, u32[]{:S(2)}, u32[]{:S(2)}) collective-permute-start(f32[128,128]{1,0:T(8,128)S(1)} %get-tuple-element.63), channel_id=1, source_target_pairs={{0,20},{4,16},{8,28},{12,24},{16,4},{20,0},{24,12},{28,8},{1,21},{... | collective-permute-start | bytes 196616 | tf_op jit(solution)/shard_map/ppermute | solution.py:290
  146.6 5.3 %collective-permute-start.18 = (f32[128,128]{1,0:T(8,128)S(1)}, f32[128,128]{1,0:T(8,128)S(1)}, u32[]{:S(2)}, u32[]{:S(2)}) collective-permute-start(f32[128,128]{1,0:T(8,128)S(1)} %get-tuple-element.64), channel_id=1, source_target_pairs={{0,24},{4,28},{8,16},{12,20},{16,8},{20,12},{24,0},{28,4},{1,25},{... | collective-permute-start | bytes 196616 | tf_op jit(solution)/shard_map/ppermute | solution.py:290
  148.3 5.2 %collective-permute-start.19 = (f32[128,128]{1,0:T(8,128)S(1)}, f32[128,128]{1,0:T(8,128)S(1)}, u32[]{:S(2)}, u32[]{:S(2)}) collective-permute-start(f32[128,128]{1,0:T(8,128)S(1)} %get-tuple-element.65), channel_id=1, source_target_pairs={{0,28},{4,24},{8,20},{12,16},{16,12},{20,8},{24,4},{28,0},{1,29},{... | collective-permute-start | bytes 196616 | tf_op jit(solution)/shard_map/ppermute | solution.py:290
  (5 other events, 4.4 us)

commit v2 on v1

v2 whole, which is shorter than its diff:
```python
import functools

import jax
import jax.numpy as jnp
from jax import lax
from jax.experimental import pallas as pl
from jax.experimental.pallas import tpu as pltpu
from jax.sharding import PartitionSpec as P

F = 256
H = 128
TB = 128
CHB = 4
NODES_DEV = CHB * TB
TILES_DEV = 128
GROUPS = 8
MIB = 1 << 20
BF16 = jnp.bfloat16
F32 = jnp.float32

SMEM = pl.BlockSpec(memory_space=pltpu.SMEM)
VMEM = pl.BlockSpec(memory_space=pltpu.VMEM)
HBM = pl.BlockSpec(memory_space=pltpu.HBM)
RESIDENT_BYTES = 16 * MIB


def params(mib):
    return pltpu.CompilerParams(vmem_limit_bytes=mib * MIB)


def in_hbm(*arrays):
    return [pltpu.with_memory_space_constraint(x, pltpu.HBM) for x in arrays]


def cost(flops, bytes_accessed):
    return pl.CostEstimate(flops=flops, bytes_accessed=bytes_accessed, transcendentals=0)


def split(x):
    high = x.astype(BF16)
    low = (x - high.astype(F32)).astype(BF16)
    return high, low


def dot3(a, b, dims):
    ah, al = a
    bh, bl = b

    def one(x, y):
        return lax.dot_general(x, y, (dims, ((), ())), preferred_element_type=F32)

    return one(ah, bh) + (one(ah, bl) + one(al, bh))


def fetch(sources, targets, sems):
    copies = [pltpu.make_async_copy(a, b, sems.at[i]) for i, (a, b) in enumerate(zip(sources, targets))]
    for copy in copies:
        copy.start()
    return copies


def masked_of(grad, mask):
    return jnp.where(mask > 0, grad, jnp.zeros_like(grad))


def term_two_kernel(grad_hbm, mask_hbm, weight_hbm, left_ref, right_ref, grad, mask, weight, sems):
    for copy in fetch((grad_hbm, mask_hbm, weight_hbm.at[2]), (grad, mask, weight), sems):
        copy.wait()
    term = dot3(split(masked_of(grad[...], mask[...])), split(weight[...]), ((1,), (1,)))
    left_ref[...] = term[:, :H]
    right_ref[...] = term[:, H:]


def term_two(grad_out, relu_mask, cheb_weight):
    out = jax.ShapeDtypeStruct((NODES_DEV, H), F32)
    return pl.pallas_call(
        term_two_kernel,
        in_specs=[HBM] * 3,
        out_specs=[VMEM, VMEM],
        out_shape=[out, out],
        scratch_shapes=[
            pltpu.VMEM((NODES_DEV, F), F32),
            pltpu.VMEM((NODES_DEV, F), jnp.int32),
            pltpu.VMEM((F, F), F32),
            pltpu.SemaphoreType.DMA((3,)),
        ],
        compiler_params=params(16),
        cost_estimate=cost(6 * NODES_DEV * F * F, 4 * NODES_DEV * F * 3 + 4 * F * F),
        name="term_two",
    )(*in_hbm(grad_out, relu_mask, cheb_weight))


def local_kernel(
    grad_hbm, mask_hbm, weight_hbm, h0, h1, h2, left_ref, right_ref, diff_ref, total_ref, grad, mask, weight, bases, sems
):
    sources = (grad_hbm, mask_hbm, weight_hbm, h0, h1, h2)
    copies = fetch(sources, (grad, mask, weight, bases.at[0], bases.at[1], bases.at[2]), sems)
    for copy in copies[:3]:
        copy.wait()
    masked = split(masked_of(grad[...], mask[...]))
    term = dot3(masked, split(weight[1]), ((1,), (1,)))
    left_ref[...] = term[:, :H]
    right_ref[...] = term[:, H:]
    diff_ref[...] = dot3(masked, split(weight[0] - weight[2]), ((1,), (1,)))
    for k in range(3):
        copies[3 + k].wait()
        total_ref[k] = dot3(split(bases[k]), masked, ((0,), (0,)))


def local_terms(grad_out, relu_mask, cheb_weight, b0, b1, b2):
    half = jax.ShapeDtypeStruct((NODES_DEV, H), F32)
    return pl.pallas_call(
        local_kernel,
        in_specs=[HBM] * 6,
        out_specs=[VMEM] * 4,
        out_shape=[half, half, jax.ShapeDtypeStruct((NODES_DEV, F), F32), jax.ShapeDtypeStruct((3, F, F), F32)],
        scratch_shapes=[
            pltpu.VMEM((NODES_DEV, F), F32),
            pltpu.VMEM((NODES_DEV, F), jnp.int32),
            pltpu.VMEM((3, F, F), F32),
            pltpu.VMEM((3, NODES_DEV, F), F32),
            pltpu.SemaphoreType.DMA((6,)),
        ],
        compiler_params=params(32),
        cost_estimate=cost(30 * NODES_DEV * F * F, 4 * NODES_DEV * F * 8),
        name="local_terms",
    )(*in_hbm(grad_out, relu_mask, cheb_weight, b0, b1, b2))


def operator_kernel(
    n_row, n_col, resident, ids_ref, live_ref, rows_hbm, slots_hbm, values_ref, out_ref,
    tiles, acc, lists, counts, rows, slots, sems, small_sems,
):
    size = TILES_DEV // GROUPS

    def copy(g):
        part = pl.ds(g * size, size)
        return pltpu.make_async_copy(values_ref.at[0, part], tiles.at[part], sems.at[g])

    def begin():
        small = fetch((rows_hbm, slots_hbm), (rows, slots), small_sems)
        for g in range(GROUPS):
            copy(g).start()
        for s in range(n_col):
            counts[s] = 0
        for item in small:
            item.wait()

        def place(t, carry):
            row = rows[0, t]
            s = lax.rem(row // CHB - ids_ref[0] + n_col, n_col)
            position = slots[0, t] * CHB + lax.rem(row, CHB)
            n = counts[s]
            lists[s, n] = position * TILES_DEV + t
            counts[s] = n + 1
            return carry

        lax.fori_loop(0, live_ref[0], place, 0)
        for g in range(GROUPS):
            copy(g).wait()

    def one(origin, to):
        acc[...] = jnp.zeros_like(acc)

        def add(n, carry):
            entry = lists[origin, n]
            position = entry // TILES_DEV
            acc[position] += tiles[lax.rem(entry, TILES_DEV)]
            return carry

        lax.fori_loop(0, counts[origin], add, 0)

        def store(slot, carry):
            here = pl.ds(pl.multiple_of(slot * TB, TB), TB)
            for i in range(CHB):
                high, low = split(acc[slot * CHB + i].T)
                out_ref[to, here, i * TB : (i + 1) * TB] = high
                out_ref[to, here, NODES_DEV + i * TB : NODES_DEV + (i + 1) * TB] = low
            return carry

        lax.fori_loop(0, n_row, store, 0)

    if resident:
        begin()

        def each(origin, carry):
            one(origin, origin)
            return carry

        lax.fori_loop(0, n_col, each, 0)
    else:
        pl.when(pl.program_id(0) == 0)(begin)
        one(pl.program_id(0), 0)


def fits(n_row, n_col):
    return 4 * n_col * n_row * TB * NODES_DEV <= RESIDENT_BYTES


def build_operator(n_row, n_col, ids, live, rows, slots, values):
    wide = (n_row * TB, 2 * NODES_DEV)
    resident = fits(n_row, n_col)
    grid = {} if resident else {"grid": (n_col,)}
    return pl.pallas_call(
        functools.partial(operator_kernel, n_row, n_col, resident),
        in_specs=[SMEM] * 2 + [HBM] * 3,
        out_specs=VMEM if resident else pl.BlockSpec((1,) + wide, lambda s: (s, 0, 0)),
        out_shape=jax.ShapeDtypeStruct((n_col,) + wide, BF16),
        scratch_shapes=[
            pltpu.VMEM((TILES_DEV, TB, TB), F32),
            pltpu.VMEM((n_row * CHB, TB, TB), F32),
            pltpu.SMEM((n_col, TILES_DEV), jnp.int32),
            pltpu.SMEM((n_col,), jnp.int32),
            pltpu.SMEM((1, TILES_DEV), jnp.int32),
            pltpu.SMEM((1, TILES_DEV), jnp.int32),
            pltpu.SemaphoreType.DMA((GROUPS,)),
            pltpu.SemaphoreType.DMA((2,)),
        ],
        compiler_params=params(40),
        cost_estimate=cost(0, 4 * TILES_DEV * TB * TB * 5),
        name="operator",
        **grid,
    )(ids, live, *in_hbm(rows, slots, values))


def product_kernel(n_row, origins, has_prev, resident, *refs):
    n = len(origins)
    op_ref, fields = refs[0], refs[1 : 1 + n]
    prev = refs[1 + n] if has_prev else None
    out_ref = refs[1 + n + has_prev]
    pairs = n_row // 2
    wide = 2 * TB
    if not resident:
        buf, sems = refs[-2:]

        def copy(k, p):
            source = op_ref.at[origins[k], pl.ds(p * wide, wide)]
            return pltpu.make_async_copy(source, buf.at[k, pl.ds(p * wide, wide)], sems.at[k, p])

        for p in range(pairs):
            for k in range(n):
                copy(k, p).start()
    right = []
    for field in fields:
        high, low = split(field[...])
        both = jnp.concatenate([high, low], axis=1)
        right.append(jnp.concatenate([both, both], axis=0))
    for p in range(pairs):
        here = slice(p * wide, (p + 1) * wide)
        total = None
        for k in range(n):
            if resident:
                left = op_ref[origins[k], here, :]
            else:
                copy(k, p).wait()
                left = buf[k, here, :]
            part = jnp.dot(left, right[k], preferred_element_type=F32)
            total = part if total is None else total + part
        summed = total[:, :H] + total[:, H:]
        out_ref[here, :] = summed + prev[here, :] if has_prev else summed


def product(n_row, n_col, origins, operator, fields, prev):
    rows = n_row * TB
    n = len(origins)
    has_prev = prev is not None
    resident = fits(n_row, n_col)
    scratch = [
        pltpu.VMEM((n, rows, 2 * NODES_DEV), BF16),
        pltpu.SemaphoreType.DMA((n, n_row // 2)),
    ]
    return pl.pallas_call(
        functools.partial(product_kernel, n_row, origins, has_prev, resident),
        in_specs=[VMEM if resident else HBM] + [VMEM] * (n + has_prev),
        out_specs=VMEM,
        out_shape=jax.ShapeDtypeStruct((rows, H), F32),
        scratch_shapes=[] if resident else scratch,
        compiler_params=params(24 if resident else 40),
        cost_estimate=cost(
            2 * n * rows * 2 * NODES_DEV * F, n * rows * NODES_DEV * 4 + 4 * n * NODES_DEV * H + 8 * rows * H
        ),
        name="product",
    )(operator, *fields, *((prev,) if has_prev else ()))


def collect_kernel(n_row, scale, owners_ref, base_ref, *refs):
    out_ref = refs[-1]
    out_ref[...] = base_ref[...]
    for h, came in enumerate(refs[:-1]):
        for q in range(n_row):
            here = pl.ds(pl.multiple_of(owners_ref[q] * TB, TB), TB)
            out_ref[here, h * H : (h + 1) * H] += came[q] if scale == 1.0 else scale * came[q]


def collect(n_row, scale, owners, base, received):
    return pl.pallas_call(
        functools.partial(collect_kernel, n_row, scale),
        in_specs=[SMEM] + [VMEM] * (1 + len(received)),
        out_specs=VMEM,
        out_shape=jax.ShapeDtypeStruct(base.shape, F32),
        compiler_params=params(24),
        cost_estimate=cost(0, 4 * (2 * base.size + len(received) * n_row * TB * H)),
        name="collect",
    )(owners, base, *received)


def shift(n_col, x, step):
    return lax.ppermute(x, "col", [(c, (c + step) % n_col) for c in range(n_col)])


def exchange(pieces):
    return lax.all_to_all(pieces, "row", split_axis=0, concat_axis=0, tiled=True)


def reduce_weights(n_row, local):
    mine = jnp.sum(exchange(local.reshape(n_row, 3 * F // n_row, F)), axis=0)
    mine = jnp.sum(lax.all_gather(mine, "col", axis=0), axis=0)
    return lax.all_gather(mine, "row", axis=0, tiled=True).reshape(3, F, F)


def transposed(n_row, n_col, operator, field, side):
    long = n_col // 2
    short = n_col - 1 - long
    total = product(n_row, n_col, (0,), operator, [field], None)
    ahead, behind = field, field
    for s in range(1, long + 1):
        fields, origins = [], []
        ahead = shift(n_col, ahead, side)
        fields.append(ahead)
        origins.append((-side * s) % n_col)
        if s <= short:
            behind = shift(n_col, behind, -side)
            fields.append(behind)
            origins.append((side * s) % n_col)
        total = product(n_row, n_col, tuple(origins), operator, fields, total)
    return exchange(total.reshape(n_row, TB, H))


def per_device(
    grad_out,
    relu_mask,
    basis_zero,
    basis_one,
    basis_two,
    cheb_weight,
    tile_values,
    tile_rows,
    tile_slots,
    send_blocks,
    live_tiles,
):
    n_row = lax.axis_size("row")
    n_col = lax.axis_size("col")
    ids = lax.axis_index("col").astype(jnp.int32).reshape(1)
    owners = send_blocks.reshape(n_row)
    two = term_two(grad_out, relu_mask, cheb_weight)
    operator = build_operator(n_row, n_col, ids, live_tiles, tile_rows, tile_slots, tile_values)
    one_left, one_right, diff, local = local_terms(
        grad_out, relu_mask, cheb_weight, basis_zero, basis_one, basis_two
    )
    received = []
    for side, field, one in ((1, two[0], one_left), (-1, two[1], one_right)):
        first = transposed(n_row, n_col, operator, field, side)
        carried = collect(n_row, 2.0, owners, one, [first])
        received.append(transposed(n_row, n_col, operator, carried, side))
    weight_grad = reduce_weights(n_row, local)
    grad_features = collect(n_row, 1.0, owners, diff, received)
    return grad_features, weight_grad


def solution(mesh):
    placed = (
        P(("row", "col"), None),
        P(("row", "col"), None),
        P(("row", "col"), None),
        P(("row", "col"), None),
        P(("row", "col"), None),
        P(),
        P(("row", "col"), None, None, None),
        P(("row", "col"), None),
        P(("row", "col"), None),
        P(("row", "col"), None, None),
        P(("row", "col")),
    )
    return jax.shard_map(
        per_device,
        mesh=mesh,
        in_specs=placed,
        out_specs=(P(("row", "col"), None), P()),
        check_vma=False,
    )
```

time: 156 us -> 154 us (0.987)
  blocking collectives: 0 us -> 25.4 us
  Pallas kernels: 46.8 us -> 32.8 us
  starting transfers between devices: 59.1 us -> 48 us
  local copies, waits for them, and re-layouts: 14.2 us -> 12.3 us
    ppermute x44 -> x0, starting transfers between devices: 39.3 us -> none  [the longest x42 38.1 us: exchange(): lax.ppermute(pieces[j], 'row', [(r, r ^ j) for r in range(n_row)])]
    ppermute x44 -> x0, waiting for transfers between devices: 26.4 us -> none  [the longest x2 16.8 us: reduce_weights(): lax.ppermute(mine, 'col', [(c, c ^ step) for c in range(n_col)])]
    all_gather x0 -> x2, blocking collectives: none -> 25.4 us  [the longest x1 14.8 us: reduce_weights(): mine = jnp.sum(lax.all_gather(mine, 'col', axis=0), axis=0)]
    ppermute x12, waiting for transfers between devices: 6.66 us -> 29.5 us  [shift(): lax.ppermute(x, 'col', [(c, (c + step) % n_col) for c in range(n_col)])]
    all_to_all x0 -> x5, starting transfers between devices: none -> 22.5 us  [exchange(): lax.all_to_all(pieces, 'row', split_axis=0, concat_axis=0, tiled=True)]
    pallas_call x12, Pallas kernels: 28.7 us -> 14 us  [product(): pl.pallas_call(functools.partial(product_kernel, n_row, origins, has_prev...]
    ppermute x12, starting transfers between devices: 19.8 us -> 25.5 us  [shift(): lax.ppermute(x, 'col', [(c, (c + step) % n_col) for c in range(n_col)])]
    all_to_all x0 -> x5, waiting for transfers between devices: none -> 4.8 us  [exchange(): lax.all_to_all(pieces, 'row', split_axis=0, concat_axis=0, tiled=True)]
  transfers between devices with their start and end apart: 56 -> 17, of which waited for: 12 -> 8; matrix products, arithmetic and copies ran while one was open for 0% -> 0% of each run, Pallas kernels for 29% -> 19%
where the time goes in v2:
time: 154 us
  starting transfers between devices  48 us (31%)
  waiting for transfers between devices  34.3 us (22%)
  Pallas kernels  32.8 us (21%)
  blocking collectives  25.4 us (16%)
  local copies, waits for them, and re-layouts  12.3 us (8%)
    ppermute x12, waiting for transfers between devices, shift(): lax.ppermute(x, 'col', [(c, (c + step) % n_col) for c in range(n_col)])  29.5 us
    ppermute x12, starting transfers between devices, shift(): lax.ppermute(x, 'col', [(c, (c + step) % n_col) for c in range(n_col)])  25.5 us
    all_to_all x5, starting transfers between devices, exchange(): lax.all_to_all(pieces, 'row', split_axis=0, concat_axis=0, tiled=True)  22.5 us
    all_gather x1, blocking collectives, reduce_weights(): mine = jnp.sum(lax.all_gather(mine, 'col', axis=0), axis=0)  14.8 us
    pallas_call x12, Pallas kernels, product(): pl.pallas_call(functools.partial(product_kernel, n_row, origins, has_prev...  14 us
    unnamed x11, local copies, waits for them, and re-layouts  12.3 us
    all_gather x1, blocking collectives, reduce_weights(): return lax.all_gather(mine, 'row', axis=0, tiled=True).reshape(3, F, F)  10.6 us
    pallas_call x1, Pallas kernels, build_operator(): pl.pallas_call(functools.partial(operator_kernel, n_row, n_col, resident)...  9.42 us
  transfers between devices with their start and end apart: 17, of which 8 were waited for; matrix products, arithmetic and copies ran while one was open for 0% of the time, Pallas kernels for 19%

profile of v2, /device:TPU:0, one launch (start us, length us, event | category | flops | bytes accessed | tf_op | source)
XLA Modules:
  0.0 154.3 jit_solution(7770349113430254721)
XLA Ops:
  0.6 1.7 %term_two.1 = (f32[512,128]{1,0:T(8,128)S(1)}, f32[512,128]{1,0:T(8,128)S(1)}) custom-call(f32[512,256]{1,0:T(8,128)} %grad_hbm.3, s32[512,256]{1,0:T(8,128)} %mask_hbm.3, f32[3,256,256]{2,1,0:T(8,128)} %weight_hbm.3), custom_call_target="tpu_custom_call" | custom-call | flops 201326592 | bytes 1835008 | tf_op jit(solution)/shard_map/term_two/pallas_call | solution.py:76
  2.3 5.1 %collective-permute-start.6 = (f32[512,128]{1,0:T(8,128)S(1)}, f32[512,128]{1,0:T(8,128)S(1)}, u32[]{:S(2)}, u32[]{:S(2)}) collective-permute-start(f32[512,128]{1,0:T(8,128)S(1)} %get-tuple-element.12.refs_1_), channel_id=1, source_target_pairs={{0,3},{1,0},{2,1},{3,2},{4,7},{5,4},{6,5},{7,6},{8,11},{9,8},{10,9... | collective-permute-start | bytes 786440 | tf_op jit(solution)/shard_map/ppermute | solution.py:308
  7.5 0.0 collective-permute-start.8
  7.5 6.7 %collective-permute-done.6.refs_1_ = f32[512,128]{1,0:T(8,128)S(1)} collective-permute-done((f32[512,128]{1,0:T(8,128)S(1)}, f32[512,128]{1,0:T(8,128)S(1)}, u32[]{:S(2)}, u32[]{:S(2)}) %collective-permute-start.6) | collective-permute-done | bytes 262176 | tf_op jit(solution)/shard_map/ppermute | solution.py:308
  14.2 4.3 %collective-permute-start.7 = (f32[512,128]{1,0:T(8,128)S(1)}, f32[512,128]{1,0:T(8,128)S(1)}, u32[]{:S(2)}, u32[]{:S(2)}) collective-permute-start(f32[512,128]{1,0:T(8,128)S(1)} %collective-permute-done.6.refs_1_), channel_id=1, source_target_pairs={{0,3},{1,0},{2,1},{3,2},{4,7},{5,4},{6,5},{7,6},{8,11},{9,8},{10,9... | collective-permute-start | bytes 786440 | tf_op jit(solution)/shard_map/ppermute | solution.py:308
  18.5 0.0 collective-permute-start
  19.1 9.4 %operator.1.refs_0_ = bf16[4,1024,1024]{2,1,0:T(8,128)(2,1)S(1)} custom-call(s32[1]{0:T(128)} %bitcast.1.ids_ref, s32[1]{0:T(128)S(6)} %copy.14.live_ref, s32[1,128]{1,0:T(1,128)} %rows_hbm.1, s32[1,128]{1,0:T(1,128)} %slots_hbm.1, f32[1,128,128,128]{3,2,1,0:T(8,128)} %values_ref.1), custom_call_target="tpu_custom_call" | custom-call | bytes 41943040 | tf_op jit(solution)/shard_map/operator/pallas_call | solution.py:204
  28.5 0.0 copy-start
  28.5 0.7 product.18.refs_3_
  29.3 0.0 collective-permute-done.8.refs_2_
  29.3 1.3 product.19.refs_2_
  30.5 0.0 collective-permute-done.7.refs_1_
  30.6 1.2 copy-done
  31.8 1.5 product.20
  33.3 3.7 %all-to-all-start.2 = ((f32[8,128,128]{2,1,0:T(8,128)}), f32[8,128,128]{2,1,0:T(8,128)S(1)}, u32[]{:S(2)}, u32[]{:S(2)}) async-start(f32[8,128,128]{2,1,0:T(8,128)} %bitcast.4), calls=%async_computation.2 | async-start | bytes 1048576 | tf_op jit(solution)/shard_map/all_to_all | solution.py:312
  37.0 4.8 %collective-permute-start.2 = (f32[512,128]{1,0:T(8,128)S(1)}, f32[512,128]{1,0:T(8,128)S(1)}, u32[]{:S(2)}, u32[]{:S(2)}) collective-permute-start(f32[512,128]{1,0:T(8,128)S(1)} %get-tuple-element.10.refs_1_), channel_id=1, source_target_pairs={{0,3},{1,0},{2,1},{3,2},{4,7},{5,4},{6,5},{7,6},{8,11},{9,8},{10,9... | collective-permute-start | bytes 786440 | tf_op jit(solution)/shard_map/ppermute | solution.py:308
  41.9 0.0 collective-permute-done.refs_1_
  41.9 0.0 collective-permute-start.1
  41.9 0.0 copy-start.1
  41.9 3.4 %copy-done.1 = bf16[4,1024,1024]{2,1,0:T(8,128)(2,1)S(1)} copy-done((bf16[4,1024,1024]{2,1,0:T(8,128)(2,1)S(1)}, bf16[4,1024,1024]{2,1,0:T(8,128)(2,1)}, u32[]{:S(2)}) %copy-start.1) | copy-done | bytes 8388632
  45.2 0.7 product.12.refs_3_
  46.0 2.6 %collective-permute-done.2.refs_2_ = f32[512,128]{1,0:T(8,128)S(1)} collective-permute-done((f32[512,128]{1,0:T(8,128)S(1)}, f32[512,128]{1,0:T(8,128)S(1)}, u32[]{:S(2)}, u32[]{:S(2)}) %collective-permute-start.2) | collective-permute-done | bytes 262176 | tf_op jit(solution)/shard_map/ppermute | solution.py:308
  48.5 1.2 product.13.refs_2_
  49.8 0.0 copy-start.4
  49.8 4.5 %collective-permute-done.1.refs_1_ = f32[512,128]{1,0:T(8,128)S(1)} collective-permute-done((f32[512,128]{1,0:T(8,128)S(1)}, f32[512,128]{1,0:T(8,128)S(1)}, u32[]{:S(2)}, u32[]{:S(2)}) %collective-permute-start.1) | collective-permute-done | bytes 262176 | tf_op jit(solution)/shard_map/ppermute | solution.py:308
  54.3 1.5 product.14
  55.8 0.0 all-to-all-done.2.refs_0_
  55.8 3.9 %all-to-all-start = ((f32[8,128,128]{2,1,0:T(8,128)}), f32[8,128,128]{2,1,0:T(8,128)S(1)}, u32[]{:S(2)}, u32[]{:S(2)}) async-start(f32[8,128,128]{2,1,0:T(8,128)} %bitcast.2), calls=%async_computation | async-start | bytes 1048576 | tf_op jit(solution)/shard_map/all_to_all | solution.py:312
  59.7 4.9 %local_terms.1 = (f32[512,128]{1,0:T(8,128)S(1)}, f32[512,128]{1,0:T(8,128)S(1)}, f32[512,256]{1,0:T(8,128)S(1)}, f32[3,256,256]{2,1,0:T(8,128)}) custom-call(f32[512,256]{1,0:T(8,128)} %grad_hbm.3, s32[512,256]{1,0:T(8,128)} %mask_hbm.3, f32[3,256,256]{2,1,0:T(8,128)} %weight_hbm.3, f32[512,256]{1,0:T(8,128)} %h0.1, f32[512,256]{1,0:T(8,128)} %h1.1, ...), custom_call_target="tpu_custom_call" | custom-call | flops 1006632960 | bytes 4194304 | tf_op jit(solution)/shard_map/local_terms/pallas_call | solution.py:112
  64.6 4.8 %all-to-all-done.refs_0_ = f32[8,128,128]{2,1,0:T(8,128)S(1)} async-done(((f32[8,128,128]{2,1,0:T(8,128)}), f32[8,128,128]{2,1,0:T(8,128)S(1)}, u32[]{:S(2)}, u32[]{:S(2)}) %all-to-all-start) | async-done | bytes 524320 | tf_op jit(solution)/shard_map/all_to_all | solution.py:312
  69.4 3.5 %all-to-all-start.4 = ((f32[8,96,256]{2,1,0:T(8,128)}), f32[8,96,256]{2,1,0:T(8,128)S(1)}, u32[]{:S(2)}, u32[]{:S(2)}) async-start(f32[8,96,256]{2,1,0:T(8,128)} %bitcast.6), calls=%async_computation.4 | async-start | bytes 1572864 | tf_op jit(solution)/shard_map/all_to_all | solution.py:312
  73.0 0.0 copy-done.4
  73.0 0.6 collect.4.refs_1_
  73.6 1.9 %collective-permute-start.9 = (f32[512,128]{1,0:T(8,128)S(1)}, f32[512,128]{1,0:T(8,128)S(1)}, u32[]{:S(2)}, u32[]{:S(2)}) collective-permute-start(f32[512,128]{1,0:T(8,128)S(1)} %collect.4.refs_1_), channel_id=1, source_target_pairs={{0,3},{1,0},{2,1},{3,2},{4,7},{5,4},{6,5},{7,6},{8,11},{9,8},{10,9... | collective-permute-start | bytes 786440 | tf_op jit(solution)/shard_map/ppermute | solution.py:308
  75.5 0.2 collective-permute-start.11
  75.7 6.9 %collective-permute-done.9.refs_1_ = f32[512,128]{1,0:T(8,128)S(1)} collective-permute-done((f32[512,128]{1,0:T(8,128)S(1)}, f32[512,128]{1,0:T(8,128)S(1)}, u32[]{:S(2)}, u32[]{:S(2)}) %collective-permute-start.9) | collective-permute-done | bytes 262176 | tf_op jit(solution)/shard_map/ppermute | solution.py:308
  82.6 3.8 %collective-permute-start.10 = (f32[512,128]{1,0:T(8,128)S(1)}, f32[512,128]{1,0:T(8,128)S(1)}, u32[]{:S(2)}, u32[]{:S(2)}) collective-permute-start(f32[512,128]{1,0:T(8,128)S(1)} %collective-permute-done.9.refs_1_), channel_id=1, source_target_pairs={{0,3},{1,0},{2,1},{3,2},{4,7},{5,4},{6,5},{7,6},{8,11},{9,8},{10,9... | collective-permute-start | bytes 786440 | tf_op jit(solution)/shard_map/ppermute | solution.py:308
  86.4 0.6 collect.3.refs_1_
  87.1 3.3 %collective-permute-start.3 = (f32[512,128]{1,0:T(8,128)S(1)}, f32[512,128]{1,0:T(8,128)S(1)}, u32[]{:S(2)}, u32[]{:S(2)}) collective-permute-start(f32[512,128]{1,0:T(8,128)S(1)} %collect.3.refs_1_), channel_id=1, source_target_pairs={{0,1},{1,2},{2,3},{3,0},{4,5},{5,6},{6,7},{7,4},{8,9},{9,10},{10,1... | collective-permute-start | bytes 786440 | tf_op jit(solution)/shard_map/ppermute | solution.py:308
  90.4 3.4 %copy-done.2 = bf16[4,1024,1024]{2,1,0:T(8,128)(2,1)S(1)} copy-done((bf16[4,1024,1024]{2,1,0:T(8,128)(2,1)S(1)}, bf16[4,1024,1024]{2,1,0:T(8,128)(2,1)}, u32[]{:S(2)}) %copy-start.2) | copy-done | bytes 8388632
  93.8 0.7 product.21.refs_3_
  94.5 0.0 collective-permute-done.11.refs_2_
  94.5 1.3 product.22.refs_2_
  95.8 1.6 %collective-permute-done.10.refs_1_ = f32[512,128]{1,0:T(8,128)S(1)} collective-permute-done((f32[512,128]{1,0:T(8,128)S(1)}, f32[512,128]{1,0:T(8,128)S(1)}, u32[]{:S(2)}, u32[]{:S(2)}) %collective-permute-start.10) | collective-permute-done | bytes 262176 | tf_op jit(solution)/shard_map/ppermute | solution.py:308
  97.3 1.6 %product.23 = f32[1024,128]{1,0:T(8,128)} custom-call(bf16[4,1024,1024]{2,1,0:T(8,128)(2,1)S(1)} %copy-done.2, f32[512,128]{1,0:T(8,128)S(1)} %collective-permute-done.10.refs_1_, f32[1024,128]{1,0:T(8,128)S(1)} %product.22.refs_2_), custom_call_target="tpu_custom_call" | custom-call | flops 536870912 | bytes 3407872 | tf_op jit(solution)/shard_map/product/pallas_call | solution.py:272
  98.9 0.0 all-to-all-done.4
  98.9 7.5 %all-to-all-start.3 = ((f32[8,128,128]{2,1,0:T(8,128)}), f32[8,128,128]{2,1,0:T(8,128)S(1)}, u32[]{:S(2)}, u32[]{:S(2)}) async-start(f32[8,128,128]{2,1,0:T(8,128)} %bitcast.5), calls=%async_computation.3 | async-start | bytes 1048576 | tf_op jit(solution)/shard_map/all_to_all | solution.py:312
  106.4 0.0 collective-permute-start.5
  106.4 0.0 collective-permute-done.3.refs_1_
  106.4 2.0 %collective-permute-start.4 = (f32[512,128]{1,0:T(8,128)S(1)}, f32[512,128]{1,0:T(8,128)S(1)}, u32[]{:S(2)}, u32[]{:S(2)}) collective-permute-start(f32[512,128]{1,0:T(8,128)S(1)} %collective-permute-done.3.refs_1_), channel_id=1, source_target_pairs={{0,1},{1,2},{2,3},{3,0},{4,5},{5,6},{6,7},{7,4},{8,9},{9,10},{10,1... | collective-permute-start | bytes 786440 | tf_op jit(solution)/shard_map/ppermute | solution.py:308
  108.4 3.4 %copy-done.3 = bf16[4,1024,1024]{2,1,0:T(8,128)(2,1)S(1)} copy-done((bf16[4,1024,1024]{2,1,0:T(8,128)(2,1)S(1)}, bf16[4,1024,1024]{2,1,0:T(8,128)(2,1)}, u32[]{:S(2)}) %copy-start.3) | copy-done | bytes 8388632
  111.8 0.7 product.15.refs_3_
  112.5 3.0 %collective-permute-done.5.refs_2_ = f32[512,128]{1,0:T(8,128)S(1)} collective-permute-done((f32[512,128]{1,0:T(8,128)S(1)}, f32[512,128]{1,0:T(8,128)S(1)}, u32[]{:S(2)}, u32[]{:S(2)}) %collective-permute-start.5) | collective-permute-done | bytes 262176 | tf_op jit(solution)/shard_map/ppermute | solution.py:308
  115.5 1.2 product.16.refs_2_
  116.8 4.2 %collective-permute-done.4.refs_1_ = f32[512,128]{1,0:T(8,128)S(1)} collective-permute-done((f32[512,128]{1,0:T(8,128)S(1)}, f32[512,128]{1,0:T(8,128)S(1)}, u32[]{:S(2)}, u32[]{:S(2)}) %collective-permute-start.4) | collective-permute-done | bytes 262176 | tf_op jit(solution)/shard_map/ppermute | solution.py:308
  121.0 1.5 product.17
  122.5 0.0 all-to-all-done.3.refs_1_
  122.5 3.9 %all-to-all-start.1 = ((f32[8,128,128]{2,1,0:T(8,128)}), f32[8,128,128]{2,1,0:T(8,128)S(1)}, u32[]{:S(2)}, u32[]{:S(2)}) async-start(f32[8,128,128]{2,1,0:T(8,128)} %bitcast.3), calls=%async_computation.1 | async-start | bytes 1048576 | tf_op jit(solution)/shard_map/all_to_all | solution.py:312
  126.4 0.1 reduce_sum.18
  126.5 14.8 %all-gather = f32[384,256]{1,0:T(8,128)S(1)} all-gather(f32[96,256]{1,0:T(8,128)S(1)} %reduce_sum.18), channel_id=2, replica_groups=mesh['row'=8,'col'=4] {'col'}, dimensions={0}, use_global_device_ids=true | all-gather | bytes 491520 | tf_op jit(solution)/shard_map/all_gather | solution.py:317
  141.3 10.6 %all_gather.11 = f32[768,256]{1,0:T(8,128)S(1)} all-gather(f32[96,256]{1,0:T(8,128)S(1)} %reduce_sum.19), channel_id=1, replica_groups=mesh['row'=8,'col'=4] {'row'}, dimensions={0}, use_global_device_ids=true | all-gather | bytes 884736 | tf_op jit(solution)/shard_map/all_gather | solution.py:318
  151.9 0.0 all-to-all-done.1.refs_0_
  151.9 1.5 collect.5
  153.4 0.9 copy.15
  (3 shorter events, 0.0 us)
Async XLA Ops:
  2.3 11.8 %collective-permute-start.6 = (f32[512,128]{1,0:T(8,128)S(1)}, f32[512,128]{1,0:T(8,128)S(1)}, u32[]{:S(2)}, u32[]{:S(2)}) collective-permute-start(f32[512,128]{1,0:T(8,128)S(1)} %get-tuple-element.12.refs_1_), channel_id=1, source_target_pairs={{0,3},{1,0},{2,1},{3,2},{4,7},{5,4},{6,5},{7,6},{8,11},{9,8},{10,9... | collective-permute-start | bytes 786440 | tf_op jit(solution)/shard_map/ppermute | solution.py:308
  7.5 21.8 %collective-permute-start.8 = (f32[512,128]{1,0:T(8,128)S(1)}, f32[512,128]{1,0:T(8,128)S(1)}, u32[]{:S(2)}, u32[]{:S(2)}) collective-permute-start(f32[512,128]{1,0:T(8,128)S(1)} %get-tuple-element.12.refs_1_), channel_id=1, source_target_pairs={{0,1},{1,2},{2,3},{3,0},{4,5},{5,6},{6,7},{7,4},{8,9},{9,10},{10,1... | collective-permute-start | bytes 786440 | tf_op jit(solution)/shard_map/ppermute | solution.py:308
  14.2 16.4 %collective-permute-start.7 = (f32[512,128]{1,0:T(8,128)S(1)}, f32[512,128]{1,0:T(8,128)S(1)}, u32[]{:S(2)}, u32[]{:S(2)}) collective-permute-start(f32[512,128]{1,0:T(8,128)S(1)} %collective-permute-done.6.refs_1_), channel_id=1, source_target_pairs={{0,3},{1,0},{2,1},{3,2},{4,7},{5,4},{6,5},{7,6},{8,11},{9,8},{10,9... | collective-permute-start | bytes 786440 | tf_op jit(solution)/shard_map/ppermute | solution.py:308
  18.5 23.4 %collective-permute-start = (f32[512,128]{1,0:T(8,128)S(1)}, f32[512,128]{1,0:T(8,128)S(1)}, u32[]{:S(2)}, u32[]{:S(2)}) collective-permute-start(f32[512,128]{1,0:T(8,128)S(1)} %get-tuple-element.10.refs_1_), channel_id=1, source_target_pairs={{0,1},{1,2},{2,3},{3,0},{4,5},{5,6},{6,7},{7,4},{8,9},{9,10},{10,1... | collective-permute-start | bytes 786440 | tf_op jit(solution)/shard_map/ppermute | solution.py:308
  28.5 3.3 %copy-start = (bf16[4,1024,1024]{2,1,0:T(8,128)(2,1)}, bf16[4,1024,1024]{2,1,0:T(8,128)(2,1)S(1)}, u32[]{:S(2)}) copy-start(bf16[4,1024,1024]{2,1,0:T(8,128)(2,1)S(1)} %operator.1.refs_0_) | copy-start | bytes 25165828
  33.3 22.5 %all-to-all-start.2 = ((f32[8,128,128]{2,1,0:T(8,128)}), f32[8,128,128]{2,1,0:T(8,128)S(1)}, u32[]{:S(2)}, u32[]{:S(2)}) async-start(f32[8,128,128]{2,1,0:T(8,128)} %bitcast.4), calls=%async_computation.2 | async-start | bytes 1048576 | tf_op jit(solution)/shard_map/all_to_all | solution.py:312
  37.0 11.5 %collective-permute-start.2 = (f32[512,128]{1,0:T(8,128)S(1)}, f32[512,128]{1,0:T(8,128)S(1)}, u32[]{:S(2)}, u32[]{:S(2)}) collective-permute-start(f32[512,128]{1,0:T(8,128)S(1)} %get-tuple-element.10.refs_1_), channel_id=1, source_target_pairs={{0,3},{1,0},{2,1},{3,2},{4,7},{5,4},{6,5},{7,6},{8,11},{9,8},{10,9... | collective-permute-start | bytes 786440 | tf_op jit(solution)/shard_map/ppermute | solution.py:308
  41.9 12.4 %collective-permute-start.1 = (f32[512,128]{1,0:T(8,128)S(1)}, f32[512,128]{1,0:T(8,128)S(1)}, u32[]{:S(2)}, u32[]{:S(2)}) collective-permute-start(f32[512,128]{1,0:T(8,128)S(1)} %collective-permute-done.refs_1_), channel_id=1, source_target_pairs={{0,1},{1,2},{2,3},{3,0},{4,5},{5,6},{6,7},{7,4},{8,9},{9,10},{10,1... | collective-permute-start | bytes 786440 | tf_op jit(solution)/shard_map/ppermute | solution.py:308
  41.9 3.4 %copy-start.1 = (bf16[4,1024,1024]{2,1,0:T(8,128)(2,1)S(1)}, bf16[4,1024,1024]{2,1,0:T(8,128)(2,1)}, u32[]{:S(2)}) copy-start(bf16[4,1024,1024]{2,1,0:T(8,128)(2,1)} %copy-done) | copy-start | bytes 25165828
  49.8 23.2 %copy-start.4 = (s32[1,8,1]{1,2,0:T(1,128)S(1)}, s32[1,8,1]{1,2,0:T(1,128)}, u32[]{:S(2)}) copy-start(s32[1,8,1]{1,2,0:T(1,128)} %param.20) | copy-start | bytes 100
  55.8 13.6 %all-to-all-start = ((f32[8,128,128]{2,1,0:T(8,128)}), f32[8,128,128]{2,1,0:T(8,128)S(1)}, u32[]{:S(2)}, u32[]{:S(2)}) async-start(f32[8,128,128]{2,1,0:T(8,128)} %bitcast.2), calls=%async_computation | async-start | bytes 1048576 | tf_op jit(solution)/shard_map/all_to_all | solution.py:312
  69.4 29.5 %all-to-all-start.4 = ((f32[8,96,256]{2,1,0:T(8,128)}), f32[8,96,256]{2,1,0:T(8,128)S(1)}, u32[]{:S(2)}, u32[]{:S(2)}) async-start(f32[8,96,256]{2,1,0:T(8,128)} %bitcast.6), calls=%async_computation.4 | async-start | bytes 1572864 | tf_op jit(solution)/shard_map/all_to_all | solution.py:312
  73.6 9.0 %collective-permute-start.9 = (f32[512,128]{1,0:T(8,128)S(1)}, f32[512,128]{1,0:T(8,128)S(1)}, u32[]{:S(2)}, u32[]{:S(2)}) collective-permute-start(f32[512,128]{1,0:T(8,128)S(1)} %collect.4.refs_1_), channel_id=1, source_target_pairs={{0,3},{1,0},{2,1},{3,2},{4,7},{5,4},{6,5},{7,6},{8,11},{9,8},{10,9... | collective-permute-start | bytes 786440 | tf_op jit(solution)/shard_map/ppermute | solution.py:308
  75.5 19.0 %collective-permute-start.11 = (f32[512,128]{1,0:T(8,128)S(1)}, f32[512,128]{1,0:T(8,128)S(1)}, u32[]{:S(2)}, u32[]{:S(2)}) collective-permute-start(f32[512,128]{1,0:T(8,128)S(1)} %collect.4.refs_1_), channel_id=1, source_target_pairs={{0,1},{1,2},{2,3},{3,0},{4,5},{5,6},{6,7},{7,4},{8,9},{9,10},{10,1... | collective-permute-start | bytes 786440 | tf_op jit(solution)/shard_map/ppermute | solution.py:308
  82.6 14.7 %collective-permute-start.10 = (f32[512,128]{1,0:T(8,128)S(1)}, f32[512,128]{1,0:T(8,128)S(1)}, u32[]{:S(2)}, u32[]{:S(2)}) collective-permute-start(f32[512,128]{1,0:T(8,128)S(1)} %collective-permute-done.9.refs_1_), channel_id=1, source_target_pairs={{0,3},{1,0},{2,1},{3,2},{4,7},{5,4},{6,5},{7,6},{8,11},{9,8},{10,9... | collective-permute-start | bytes 786440 | tf_op jit(solution)/shard_map/ppermute | solution.py:308
  87.1 19.3 %collective-permute-start.3 = (f32[512,128]{1,0:T(8,128)S(1)}, f32[512,128]{1,0:T(8,128)S(1)}, u32[]{:S(2)}, u32[]{:S(2)}) collective-permute-start(f32[512,128]{1,0:T(8,128)S(1)} %collect.3.refs_1_), channel_id=1, source_target_pairs={{0,1},{1,2},{2,3},{3,0},{4,5},{5,6},{6,7},{7,4},{8,9},{9,10},{10,1... | collective-permute-start | bytes 786440 | tf_op jit(solution)/shard_map/ppermute | solution.py:308
  90.4 3.4 %copy-start.2 = (bf16[4,1024,1024]{2,1,0:T(8,128)(2,1)S(1)}, bf16[4,1024,1024]{2,1,0:T(8,128)(2,1)}, u32[]{:S(2)}) copy-start(bf16[4,1024,1024]{2,1,0:T(8,128)(2,1)} %copy-done) | copy-start | bytes 25165828
  98.9 23.6 %all-to-all-start.3 = ((f32[8,128,128]{2,1,0:T(8,128)}), f32[8,128,128]{2,1,0:T(8,128)S(1)}, u32[]{:S(2)}, u32[]{:S(2)}) async-start(f32[8,128,128]{2,1,0:T(8,128)} %bitcast.5), calls=%async_computation.3 | async-start | bytes 1048576 | tf_op jit(solution)/shard_map/all_to_all | solution.py:312
  106.4 9.2 %collective-permute-start.5 = (f32[512,128]{1,0:T(8,128)S(1)}, f32[512,128]{1,0:T(8,128)S(1)}, u32[]{:S(2)}, u32[]{:S(2)}) collective-permute-start(f32[512,128]{1,0:T(8,128)S(1)} %collect.3.refs_1_), channel_id=1, source_target_pairs={{0,3},{1,0},{2,1},{3,2},{4,7},{5,4},{6,5},{7,6},{8,11},{9,8},{10,9... | collective-permute-start | bytes 786440 | tf_op jit(solution)/shard_map/ppermute | solution.py:308
  106.4 14.6 %collective-permute-start.4 = (f32[512,128]{1,0:T(8,128)S(1)}, f32[512,128]{1,0:T(8,128)S(1)}, u32[]{:S(2)}, u32[]{:S(2)}) collective-permute-start(f32[512,128]{1,0:T(8,128)S(1)} %collective-permute-done.3.refs_1_), channel_id=1, source_target_pairs={{0,1},{1,2},{2,3},{3,0},{4,5},{5,6},{6,7},{7,4},{8,9},{9,10},{10,1... | collective-permute-start | bytes 786440 | tf_op jit(solution)/shard_map/ppermute | solution.py:308
  108.4 3.4 %copy-start.3 = (bf16[4,1024,1024]{2,1,0:T(8,128)(2,1)S(1)}, bf16[4,1024,1024]{2,1,0:T(8,128)(2,1)}, u32[]{:S(2)}) copy-start(bf16[4,1024,1024]{2,1,0:T(8,128)(2,1)} %copy-done) | copy-start | bytes 25165828
  122.5 29.4 %all-to-all-start.1 = ((f32[8,128,128]{2,1,0:T(8,128)}), f32[8,128,128]{2,1,0:T(8,128)S(1)}, u32[]{:S(2)}, u32[]{:S(2)}) async-start(f32[8,128,128]{2,1,0:T(8,128)} %bitcast.3), calls=%async_computation.1 | async-start | bytes 1048576 | tf_op jit(solution)/shard_map/all_to_all | solution.py:312

commit v3 on v2

--- a/solution.py
+++ b/solution.py
@@ -205,7 +205,7 @@
         functools.partial(operator_kernel, n_row, n_col, resident),
         in_specs=[SMEM] * 2 + [HBM] * 3,
         out_specs=VMEM if resident else pl.BlockSpec((1,) + wide, lambda s: (s, 0, 0)),
-        out_shape=jax.ShapeDtypeStruct((n_col,) + wide, BF16),
+        out_shape=(pltpu.VMEM if resident else jax.ShapeDtypeStruct)((n_col,) + wide, BF16),
         scratch_shapes=[
             pltpu.VMEM((TILES_DEV, TB, TB), F32),
             pltpu.VMEM((n_row * CHB, TB, TB), F32),
@@ -280,7 +280,11 @@
             2 * n * rows * 2 * NODES_DEV * F, n * rows * NODES_DEV * 4 + 4 * n * NODES_DEV * H + 8 * rows * H
         ),
         name="product",
-    )(operator, *fields, *((prev,) if has_prev else ()))
+    )(
+        pltpu.with_memory_space_constraint(operator, pltpu.VMEM) if resident else operator,
+        *fields,
+        *((prev,) if has_prev else ()),
+    )
 
 
 def collect_kernel(n_row, scale, owners_ref, base_ref, *refs):
@@ -312,27 +316,29 @@
     return lax.all_to_all(pieces, "row", split_axis=0, concat_axis=0, tiled=True)
 
 
-def reduce_weights(n_row, local):
-    mine = jnp.sum(exchange(local.reshape(n_row, 3 * F // n_row, F)), axis=0)
-    mine = jnp.sum(lax.all_gather(mine, "col", axis=0), axis=0)
-    return lax.all_gather(mine, "row", axis=0, tiled=True).reshape(3, F, F)
-
-
-def transposed(n_row, n_col, operator, field, side):
+def after(x, *others):
+    return lax.optimization_barrier((x, *others))[0]
+
+
+def gather(n_col, field, side):
     long = n_col // 2
     short = n_col - 1 - long
-    total = product(n_row, n_col, (0,), operator, [field], None)
     ahead, behind = field, field
+    steps = []
     for s in range(1, long + 1):
-        fields, origins = [], []
         ahead = shift(n_col, ahead, side)
-        fields.append(ahead)
-        origins.append((-side * s) % n_col)
+        step = [((-side * s) % n_col, ahead)]
         if s <= short:
             behind = shift(n_col, behind, -side)
-            fields.append(behind)
-            origins.append((side * s) % n_col)
-        total = product(n_row, n_col, tuple(origins), operator, fields, total)
+            step.append(((side * s) % n_col, behind))
+        steps.append(step)
+    return steps
+
+
+def transposed(n_row, n_col, operator, field, steps):
+    total = product(n_row, n_col, (0,), operator, [field], None)
+    for step in steps:
+        total = product(n_row, n_col, tuple(o for o, _ in step), operator, [x for _, x in step], total)
     return exchange(total.reshape(n_row, TB, H))
 
 
@@ -353,19 +359,28 @@
     n_col = lax.axis_size("col")
     ids = lax.axis_index("col").astype(jnp.int32).reshape(1)
     owners = send_blocks.reshape(n_row)
-    two = term_two(grad_out, relu_mask, cheb_weight)
-    operator = build_operator(n_row, n_col, ids, live_tiles, tile_rows, tile_slots, tile_values)
+    left, right = term_two(grad_out, relu_mask, cheb_weight)
+    left_steps = gather(n_col, left, 1)
     one_left, one_right, diff, local = local_terms(
         grad_out, relu_mask, cheb_weight, basis_zero, basis_one, basis_two
     )
-    received = []
-    for side, field, one in ((1, two[0], one_left), (-1, two[1], one_right)):
-        first = transposed(n_row, n_col, operator, field, side)
-        carried = collect(n_row, 2.0, owners, one, [first])
-        received.append(transposed(n_row, n_col, operator, carried, side))
-    weight_grad = reduce_weights(n_row, local)
-    grad_features = collect(n_row, 1.0, owners, diff, received)
-    return grad_features, weight_grad
+    pieces = exchange(local.reshape(n_row, 3 * F // n_row, F))
+    ids = after(ids, local)
+    operator = build_operator(n_row, n_col, ids, live_tiles, tile_rows, tile_slots, tile_values)
+    right_steps = gather(n_col, after(right, left_steps[0][0][1]), -1)
+    left_first = transposed(n_row, n_col, operator, after(left, pieces), left_steps)
+    shares = lax.all_gather(jnp.sum(pieces, axis=0), "col", axis=0)
+
+    left_carried = collect(n_row, 2.0, owners, one_left, [left_first])
+    left_steps = gather(n_col, left_carried, 1)
+    right_first = transposed(n_row, n_col, operator, right, right_steps)
+    right_carried = collect(n_row, 2.0, owners, one_right, [after(right_first, shares)])
+    weight_grad = lax.all_gather(jnp.sum(shares, axis=0), "row", axis=0, tiled=True)
+    right_steps = gather(n_col, right_carried, -1)
+    left_second = transposed(n_row, n_col, operator, left_carried, left_steps)
+    right_second = transposed(n_row, n_col, operator, right_carried, right_steps)
+    grad_features = collect(n_row, 1.0, owners, diff, [left_second, right_second])
+    return grad_features, weight_grad.reshape(3, F, F)
 
 
 def solution(mesh):

time: 154 us -> 161 us (1.045)
  waiting for transfers between devices: 34.3 us -> 16.9 us
  local copies, waits for them, and re-layouts: 12.3 us -> 24.4 us
  blocking collectives: 25.4 us -> 36.7 us
    ppermute x12, waiting for transfers between devices: 29.5 us -> 16.9 us  [shift(): lax.ppermute(x, 'col', [(c, (c + step) % n_col) for c in range(n_col)])]
    unnamed x11 -> x17, local copies, waits for them, and re-layouts: 12.3 us -> 24.4 us
    all_gather x2, blocking collectives: 25.4 us -> 36.7 us  [the longest x1 21.4 us: per_device(): shares = lax.all_gather(jnp.sum(pieces, axis=0), 'col', axis=0)]
    all_to_all x5, waiting for transfers between devices: 4.8 us -> 0.01 us  [exchange(): lax.all_to_all(pieces, 'row', split_axis=0, concat_axis=0, tiled=True)]
    all_to_all x5, starting transfers between devices: 22.5 us -> 20.7 us  [exchange(): lax.all_to_all(pieces, 'row', split_axis=0, concat_axis=0, tiled=True)]
  transfers between devices with their start and end apart: 17 -> 17, of which waited for: 8 -> 5; matrix products, arithmetic and copies ran while one was open for 0% -> 1% of each run, Pallas kernels for 19% -> 16%
where the time goes in v3:
time: 161 us; the launch traced here: 160 us
  starting transfers between devices  47.3 us (29%)
  blocking collectives  36.7 us (23%)
  Pallas kernels  32.4 us (20%)
  local copies, waits for them, and re-layouts  24.4 us (15%)
  waiting for transfers between devices  16.9 us (10%)
    ppermute x12, starting transfers between devices, shift(): lax.ppermute(x, 'col', [(c, (c + step) % n_col) for c in range(n_col)])  26.6 us
    unnamed x17, local copies, waits for them, and re-layouts  24.4 us
    all_gather x1, blocking collectives, per_device(): shares = lax.all_gather(jnp.sum(pieces, axis=0), 'col', axis=0)  21.4 us
    all_to_all x5, starting transfers between devices, exchange(): lax.all_to_all(pieces, 'row', split_axis=0, concat_axis=0, tiled=True)  20.7 us
    ppermute x12, waiting for transfers between devices, shift(): lax.ppermute(x, 'col', [(c, (c + step) % n_col) for c in range(n_col)])  16.9 us
    all_gather x1, blocking collectives, per_device(): lax.all_gather(jnp.sum(shares, axis=0), 'row', axis=0, tiled=True)  15.2 us
    pallas_call x12, Pallas kernels, product(): pl.pallas_call(functools.partial(product_kernel, n_row, origins, has_prev...  13.9 us
    pallas_call x1, Pallas kernels, build_operator(): pl.pallas_call(functools.partial(operator_kernel, n_row, n_col, resident)...  9.14 us
  transfers between devices with their start and end apart: 17, of which 5 were waited for; matrix products, arithmetic and copies ran while one was open for 1% of the time, Pallas kernels for 16%

profile of v3, /device:TPU:0, one launch (start us, length us, event | category | flops | bytes accessed | tf_op | source)
XLA Modules:
  0.0 160.4 jit_solution(9796071175159171680)
XLA Ops:
  0.6 5.0 %local_terms.1 = (f32[512,128]{1,0:T(8,128)S(1)}, f32[512,128]{1,0:T(8,128)S(1)}, f32[512,256]{1,0:T(8,128)S(1)}, f32[3,256,256]{2,1,0:T(8,128)}) custom-call(f32[512,256]{1,0:T(8,128)} %grad_hbm.3, s32[512,256]{1,0:T(8,128)} %mask_hbm.3, f32[3,256,256]{2,1,0:T(8,128)} %weight_hbm.3, f32[512,256]{1,0:T(8,128)} %h0.1, f32[512,256]{1,0:T(8,128)} %h1.1, ...), custom_call_target="tpu_custom_call" | custom-call | flops 1006632960 | bytes 4194304 | tf_op jit(solution)/shard_map/local_terms/pallas_call | solution.py:112
  5.6 5.2 %all-to-all-start = ((f32[8,96,256]{2,1,0:T(8,128)}), f32[8,96,256]{2,1,0:T(8,128)}, u32[]{:S(2)}, u32[]{:S(2)}) async-start(f32[8,96,256]{2,1,0:T(8,128)} %bitcast.2), calls=%async_computation | async-start | bytes 1572864 | tf_op jit(solution)/shard_map/all_to_all | solution.py:316
  10.8 1.7 %term_two.1 = (f32[512,128]{1,0:T(8,128)S(1)}, f32[512,128]{1,0:T(8,128)S(1)}) custom-call(f32[512,256]{1,0:T(8,128)} %grad_hbm.3, s32[512,256]{1,0:T(8,128)} %mask_hbm.3, f32[3,256,256]{2,1,0:T(8,128)} %weight_hbm.3), custom_call_target="tpu_custom_call" | custom-call | flops 201326592 | bytes 1835008 | tf_op jit(solution)/shard_map/term_two/pallas_call | solution.py:76
  12.5 2.2 %collective-permute-start = (f32[512,128]{1,0:T(8,128)S(1)}, f32[512,128]{1,0:T(8,128)S(1)}, u32[]{:S(2)}, u32[]{:S(2)}) collective-permute-start(f32[512,128]{1,0:T(8,128)S(1)} %get-tuple-element.17.refs_1_), channel_id=1, source_target_pairs={{0,1},{1,2},{2,3},{3,0},{4,5},{5,6},{6,7},{7,4},{8,9},{9,10},{10,1... | collective-permute-start | bytes 786440 | tf_op jit(solution)/shard_map/ppermute | solution.py:312
  14.6 2.1 %collective-permute-start.2 = (f32[512,128]{1,0:T(8,128)S(1)}, f32[512,128]{1,0:T(8,128)S(1)}, u32[]{:S(2)}, u32[]{:S(2)}) collective-permute-start(f32[512,128]{1,0:T(8,128)S(1)} %get-tuple-element.17.refs_1_), channel_id=1, source_target_pairs={{0,3},{1,0},{2,1},{3,2},{4,7},{5,4},{6,5},{7,6},{8,11},{9,8},{10,9... | collective-permute-start | bytes 786440 | tf_op jit(solution)/shard_map/ppermute | solution.py:312
  16.7 7.1 %collective-permute-done.refs_1_ = f32[512,128]{1,0:T(8,128)S(1)} collective-permute-done((f32[512,128]{1,0:T(8,128)S(1)}, f32[512,128]{1,0:T(8,128)S(1)}, u32[]{:S(2)}, u32[]{:S(2)}) %collective-permute-start) | collective-permute-done | bytes 262176 | tf_op jit(solution)/shard_map/ppermute | solution.py:312
  23.8 0.0 collective-permute-start.1
  24.5 9.1 %operator.1.refs_0_ = bf16[4,1024,1024]{2,1,0:T(8,128)(2,1)S(1)} custom-call(s32[1]{0:T(128)} %bitcast.1.ids_ref, s32[1]{0:T(128)S(6)} %copy.14.live_ref, s32[1,128]{1,0:T(1,128)} %rows_hbm.1, s32[1,128]{1,0:T(1,128)} %slots_hbm.1, f32[1,128,128,128]{3,2,1,0:T(8,128)} %values_ref.1), custom_call_target="tpu_custom_call" | custom-call | bytes 41943040 | tf_op jit(solution)/shard_map/operator/pallas_call | solution.py:204
  33.7 0.0 copy-start
  33.7 3.3 %copy-done = bf16[4,1024,1024]{2,1,0:T(8,128)(2,1)} copy-done((bf16[4,1024,1024]{2,1,0:T(8,128)(2,1)}, bf16[4,1024,1024]{2,1,0:T(8,128)(2,1)S(1)}, u32[]{:S(2)}) %copy-start) | copy-done | bytes 8388632
  36.9 8.3 %collective-permute-start.6 = (f32[512,128]{1,0:T(8,128)S(1)}, f32[512,128]{1,0:T(8,128)S(1)}, u32[]{:S(2)}, u32[]{:S(2)}) collective-permute-start(f32[512,128]{1,0:T(8,128)S(1)} %get-tuple-element.20.refs_1_), channel_id=1, source_target_pairs={{0,3},{1,0},{2,1},{3,2},{4,7},{5,4},{6,5},{7,6},{8,11},{9,8},{10,9... | collective-permute-start | bytes 786440 | tf_op jit(solution)/shard_map/ppermute | solution.py:312
  45.3 0.0 all-to-all-done
  45.3 3.4 %copy-done.1 = bf16[4,1024,1024]{2,1,0:T(8,128)(2,1)S(1)} copy-done((bf16[4,1024,1024]{2,1,0:T(8,128)(2,1)S(1)}, bf16[4,1024,1024]{2,1,0:T(8,128)(2,1)}, u32[]{:S(2)}) %copy-start.1) | copy-done | bytes 8388632
  48.6 0.7 product.12.refs_3_
  49.4 0.0 collective-permute-done.2.refs_2_
  49.4 1.3 product.13.refs_2_
  50.6 0.0 collective-permute-done.1.refs_1_
  50.6 1.5 product.14
  52.2 3.6 %all-to-all-start.1 = ((f32[8,128,128]{2,1,0:T(8,128)}), f32[8,128,128]{2,1,0:T(8,128)S(1)}, u32[]{:S(2)}, u32[]{:S(2)}) async-start(f32[8,128,128]{2,1,0:T(8,128)} %bitcast.3), calls=%async_computation.1 | async-start | bytes 1048576 | tf_op jit(solution)/shard_map/all_to_all | solution.py:316
  55.8 0.1 collective-permute-start.8
  55.9 0.0 collective-permute-done.6.refs_1_
  55.9 3.8 %collective-permute-start.7 = (f32[512,128]{1,0:T(8,128)S(1)}, f32[512,128]{1,0:T(8,128)S(1)}, u32[]{:S(2)}, u32[]{:S(2)}) collective-permute-start(f32[512,128]{1,0:T(8,128)S(1)} %collective-permute-done.6.refs_1_), channel_id=1, source_target_pairs={{0,3},{1,0},{2,1},{3,2},{4,7},{5,4},{6,5},{7,6},{8,11},{9,8},{10,9... | collective-permute-start | bytes 786440 | tf_op jit(solution)/shard_map/ppermute | solution.py:312
  59.7 3.4 %copy-done.2 = bf16[4,1024,1024]{2,1,0:T(8,128)(2,1)S(1)} copy-done((bf16[4,1024,1024]{2,1,0:T(8,128)(2,1)S(1)}, bf16[4,1024,1024]{2,1,0:T(8,128)(2,1)}, u32[]{:S(2)}) %copy-start.2) | copy-done | bytes 8388632
  63.1 0.7 product.18.refs_3_
  63.8 3.0 %collective-permute-done.8.refs_2_ = f32[512,128]{1,0:T(8,128)S(1)} collective-permute-done((f32[512,128]{1,0:T(8,128)S(1)}, f32[512,128]{1,0:T(8,128)S(1)}, u32[]{:S(2)}, u32[]{:S(2)}) %collective-permute-start.8) | collective-permute-done | bytes 262176 | tf_op jit(solution)/shard_map/ppermute | solution.py:312
  66.8 1.2 product.19.refs_2_
  68.1 0.0 all-to-all-done.1.refs_0_
  68.1 0.6 collect.3.refs_1_
  68.7 0.1 collective-permute-start.3
  68.8 1.3 collective-permute-done.7.refs_1_
  70.1 3.4 %copy-done.3 = bf16[4,1024,1024]{2,1,0:T(8,128)(2,1)S(1)} copy-done((bf16[4,1024,1024]{2,1,0:T(8,128)(2,1)S(1)}, bf16[4,1024,1024]{2,1,0:T(8,128)(2,1)}, u32[]{:S(2)}) %copy-start.3) | copy-done | bytes 8388632
  73.5 1.5 product.20
  75.0 3.9 %all-to-all-start.3 = ((f32[8,128,128]{2,1,0:T(8,128)}), f32[8,128,128]{2,1,0:T(8,128)S(1)}, u32[]{:S(2)}, u32[]{:S(2)}) async-start(f32[8,128,128]{2,1,0:T(8,128)} %bitcast.5), calls=%async_computation.3 | async-start | bytes 1048576 | tf_op jit(solution)/shard_map/all_to_all | solution.py:316
  78.9 2.8 %collective-permute-start.5 = (f32[512,128]{1,0:T(8,128)S(1)}, f32[512,128]{1,0:T(8,128)S(1)}, u32[]{:S(2)}, u32[]{:S(2)}) collective-permute-start(f32[512,128]{1,0:T(8,128)S(1)} %collect.3.refs_1_), channel_id=1, source_target_pairs={{0,3},{1,0},{2,1},{3,2},{4,7},{5,4},{6,5},{7,6},{8,11},{9,8},{10,9... | collective-permute-start | bytes 786440 | tf_op jit(solution)/shard_map/ppermute | solution.py:312
  81.6 1.2 reduce_sum.18
  82.8 0.0 collective-permute-done.3.refs_1_
  82.8 0.1 collective-permute-start.4
  82.9 21.4 %all-gather = f32[384,256]{1,0:T(8,128)S(1)} all-gather(f32[96,256]{1,0:T(8,128)S(1)} %reduce_sum.18), channel_id=2, replica_groups=mesh['row'=8,'col'=4] {'col'}, dimensions={0}, use_global_device_ids=true | all-gather | bytes 491520 | tf_op jit(solution)/shard_map/all_gather | solution.py:372
  104.3 3.4 %copy-done.4 = bf16[4,1024,1024]{2,1,0:T(8,128)(2,1)S(1)} copy-done((bf16[4,1024,1024]{2,1,0:T(8,128)(2,1)S(1)}, bf16[4,1024,1024]{2,1,0:T(8,128)(2,1)}, u32[]{:S(2)}) %copy-start.4) | copy-done | bytes 8388632
  107.7 0.7 product.15.refs_3_
  108.4 0.0 all-to-all-done.3.refs_0_
  108.4 0.6 collect.4.refs_1_
  109.0 3.5 %collective-permute-start.9 = (f32[512,128]{1,0:T(8,128)S(1)}, f32[512,128]{1,0:T(8,128)S(1)}, u32[]{:S(2)}, u32[]{:S(2)}) collective-permute-start(f32[512,128]{1,0:T(8,128)S(1)} %collect.4.refs_1_), channel_id=1, source_target_pairs={{0,3},{1,0},{2,1},{3,2},{4,7},{5,4},{6,5},{7,6},{8,11},{9,8},{10,9... | collective-permute-start | bytes 786440 | tf_op jit(solution)/shard_map/ppermute | solution.py:312
  112.5 0.0 collective-permute-done.5.refs_2_
  112.5 3.4 %copy-done.5 = bf16[4,1024,1024]{2,1,0:T(8,128)(2,1)S(1)} copy-done((bf16[4,1024,1024]{2,1,0:T(8,128)(2,1)S(1)}, bf16[4,1024,1024]{2,1,0:T(8,128)(2,1)}, u32[]{:S(2)}) %copy-start.5) | copy-done | bytes 8388632
  115.9 1.3 product.16.refs_2_
  117.2 0.0 collective-permute-done.4.refs_1_
  117.2 1.5 product.17
  118.7 4.1 %all-to-all-start.2 = ((f32[8,128,128]{2,1,0:T(8,128)}), f32[8,128,128]{2,1,0:T(8,128)S(1)}, u32[]{:S(2)}, u32[]{:S(2)}) async-start(f32[8,128,128]{2,1,0:T(8,128)} %bitcast.4), calls=%async_computation.2 | async-start | bytes 1048576 | tf_op jit(solution)/shard_map/all_to_all | solution.py:316
  122.9 0.0 collective-permute-start.11
  122.9 0.0 collective-permute-done.9.refs_1_
  122.9 3.8 %collective-permute-start.10 = (f32[512,128]{1,0:T(8,128)S(1)}, f32[512,128]{1,0:T(8,128)S(1)}, u32[]{:S(2)}, u32[]{:S(2)}) collective-permute-start(f32[512,128]{1,0:T(8,128)S(1)} %collective-permute-done.9.refs_1_), channel_id=1, source_target_pairs={{0,3},{1,0},{2,1},{3,2},{4,7},{5,4},{6,5},{7,6},{8,11},{9,8},{10,9... | collective-permute-start | bytes 786440 | tf_op jit(solution)/shard_map/ppermute | solution.py:312
  126.7 3.4 %copy-done.6 = bf16[4,1024,1024]{2,1,0:T(8,128)(2,1)S(1)} copy-done((bf16[4,1024,1024]{2,1,0:T(8,128)(2,1)S(1)}, bf16[4,1024,1024]{2,1,0:T(8,128)(2,1)}, u32[]{:S(2)}) %copy-start.6) | copy-done | bytes 8388632
  130.1 0.7 product.21.refs_3_
  130.8 3.0 %collective-permute-done.11.refs_2_ = f32[512,128]{1,0:T(8,128)S(1)} collective-permute-done((f32[512,128]{1,0:T(8,128)S(1)}, f32[512,128]{1,0:T(8,128)S(1)}, u32[]{:S(2)}, u32[]{:S(2)}) %collective-permute-start.11) | collective-permute-done | bytes 262176 | tf_op jit(solution)/shard_map/ppermute | solution.py:312
  133.8 1.2 product.22.refs_2_
  135.1 2.4 %collective-permute-done.10.refs_1_ = f32[512,128]{1,0:T(8,128)S(1)} collective-permute-done((f32[512,128]{1,0:T(8,128)S(1)}, f32[512,128]{1,0:T(8,128)S(1)}, u32[]{:S(2)}, u32[]{:S(2)}) %collective-permute-start.10) | collective-permute-done | bytes 262176 | tf_op jit(solution)/shard_map/ppermute | solution.py:312
  137.4 1.5 product.23
  138.9 0.0 all-to-all-done.2.refs_0_
  138.9 3.9 %all-to-all-start.4 = ((f32[8,128,128]{2,1,0:T(8,128)}), f32[8,128,128]{2,1,0:T(8,128)S(1)}, u32[]{:S(2)}, u32[]{:S(2)}) async-start(f32[8,128,128]{2,1,0:T(8,128)} %bitcast.7), calls=%async_computation.4 | async-start | bytes 1048576 | tf_op jit(solution)/shard_map/all_to_all | solution.py:316
  142.8 15.2 %all_gather.11 = f32[768,256]{1,0:T(8,128)S(1)} all-gather(f32[96,256]{1,0:T(8,128)S(1)} %reduce_sum.19), channel_id=1, replica_groups=mesh['row'=8,'col'=4] {'row'}, dimensions={0}, use_global_device_ids=true | all-gather | bytes 884736 | tf_op jit(solution)/shard_map/all_gather | solution.py:378
  158.1 0.0 all-to-all-done.4.refs_1_
  158.1 1.5 collect.5
  159.6 0.9 copy.15
  (9 shorter events, 0.0 us)
Async XLA Ops:
  5.6 39.7 %all-to-all-start = ((f32[8,96,256]{2,1,0:T(8,128)}), f32[8,96,256]{2,1,0:T(8,128)}, u32[]{:S(2)}, u32[]{:S(2)}) async-start(f32[8,96,256]{2,1,0:T(8,128)} %bitcast.2), calls=%async_computation | async-start | bytes 1572864 | tf_op jit(solution)/shard_map/all_to_all | solution.py:316
  12.5 11.4 %collective-permute-start = (f32[512,128]{1,0:T(8,128)S(1)}, f32[512,128]{1,0:T(8,128)S(1)}, u32[]{:S(2)}, u32[]{:S(2)}) collective-permute-start(f32[512,128]{1,0:T(8,128)S(1)} %get-tuple-element.17.refs_1_), channel_id=1, source_target_pairs={{0,1},{1,2},{2,3},{3,0},{4,5},{5,6},{6,7},{7,4},{8,9},{9,10},{10,1... | collective-permute-start | bytes 786440 | tf_op jit(solution)/shard_map/ppermute | solution.py:312
  14.6 34.7 %collective-permute-start.2 = (f32[512,128]{1,0:T(8,128)S(1)}, f32[512,128]{1,0:T(8,128)S(1)}, u32[]{:S(2)}, u32[]{:S(2)}) collective-permute-start(f32[512,128]{1,0:T(8,128)S(1)} %get-tuple-element.17.refs_1_), channel_id=1, source_target_pairs={{0,3},{1,0},{2,1},{3,2},{4,7},{5,4},{6,5},{7,6},{8,11},{9,8},{10,9... | collective-permute-start | bytes 786440 | tf_op jit(solution)/shard_map/ppermute | solution.py:312
  23.8 26.8 %collective-permute-start.1 = (f32[512,128]{1,0:T(8,128)S(1)}, f32[512,128]{1,0:T(8,128)S(1)}, u32[]{:S(2)}, u32[]{:S(2)}) collective-permute-start(f32[512,128]{1,0:T(8,128)S(1)} %collective-permute-done.refs_1_), channel_id=1, source_target_pairs={{0,1},{1,2},{2,3},{3,0},{4,5},{5,6},{6,7},{7,4},{8,9},{9,10},{10,1... | collective-permute-start | bytes 786440 | tf_op jit(solution)/shard_map/ppermute | solution.py:312
  33.7 3.3 %copy-start = (bf16[4,1024,1024]{2,1,0:T(8,128)(2,1)}, bf16[4,1024,1024]{2,1,0:T(8,128)(2,1)S(1)}, u32[]{:S(2)}) copy-start(bf16[4,1024,1024]{2,1,0:T(8,128)(2,1)S(1)} %operator.1.refs_0_) | copy-start | bytes 25165828
  36.9 18.9 %collective-permute-start.6 = (f32[512,128]{1,0:T(8,128)S(1)}, f32[512,128]{1,0:T(8,128)S(1)}, u32[]{:S(2)}, u32[]{:S(2)}) collective-permute-start(f32[512,128]{1,0:T(8,128)S(1)} %get-tuple-element.20.refs_1_), channel_id=1, source_target_pairs={{0,3},{1,0},{2,1},{3,2},{4,7},{5,4},{6,5},{7,6},{8,11},{9,8},{10,9... | collective-permute-start | bytes 786440 | tf_op jit(solution)/shard_map/ppermute | solution.py:312
  45.3 3.4 %copy-start.1 = (bf16[4,1024,1024]{2,1,0:T(8,128)(2,1)S(1)}, bf16[4,1024,1024]{2,1,0:T(8,128)(2,1)}, u32[]{:S(2)}) copy-start(bf16[4,1024,1024]{2,1,0:T(8,128)(2,1)} %copy-done) | copy-start | bytes 25165828
  52.2 15.9 %copy-start.7 = (s32[1,8,1]{1,2,0:T(1,128)S(1)}, s32[1,8,1]{1,2,0:T(1,128)}, u32[]{:S(2)}) copy-start(s32[1,8,1]{1,2,0:T(1,128)} %param.20) | copy-start | bytes 100
  52.2 15.9 %all-to-all-start.1 = ((f32[8,128,128]{2,1,0:T(8,128)}), f32[8,128,128]{2,1,0:T(8,128)S(1)}, u32[]{:S(2)}, u32[]{:S(2)}) async-start(f32[8,128,128]{2,1,0:T(8,128)} %bitcast.3), calls=%async_computation.1 | async-start | bytes 1048576 | tf_op jit(solution)/shard_map/all_to_all | solution.py:316
  55.8 11.0 %collective-permute-start.8 = (f32[512,128]{1,0:T(8,128)S(1)}, f32[512,128]{1,0:T(8,128)S(1)}, u32[]{:S(2)}, u32[]{:S(2)}) collective-permute-start(f32[512,128]{1,0:T(8,128)S(1)} %get-tuple-element.20.refs_1_), channel_id=1, source_target_pairs={{0,1},{1,2},{2,3},{3,0},{4,5},{5,6},{6,7},{7,4},{8,9},{9,10},{10,1... | collective-permute-start | bytes 786440 | tf_op jit(solution)/shard_map/ppermute | solution.py:312
  55.9 14.2 %collective-permute-start.7 = (f32[512,128]{1,0:T(8,128)S(1)}, f32[512,128]{1,0:T(8,128)S(1)}, u32[]{:S(2)}, u32[]{:S(2)}) collective-permute-start(f32[512,128]{1,0:T(8,128)S(1)} %collective-permute-done.6.refs_1_), channel_id=1, source_target_pairs={{0,3},{1,0},{2,1},{3,2},{4,7},{5,4},{6,5},{7,6},{8,11},{9,8},{10,9... | collective-permute-start | bytes 786440 | tf_op jit(solution)/shard_map/ppermute | solution.py:312
  59.7 3.4 %copy-start.2 = (bf16[4,1024,1024]{2,1,0:T(8,128)(2,1)S(1)}, bf16[4,1024,1024]{2,1,0:T(8,128)(2,1)}, u32[]{:S(2)}) copy-start(bf16[4,1024,1024]{2,1,0:T(8,128)(2,1)} %copy-done) | copy-start | bytes 25165828
  68.7 14.1 %collective-permute-start.3 = (f32[512,128]{1,0:T(8,128)S(1)}, f32[512,128]{1,0:T(8,128)S(1)}, u32[]{:S(2)}, u32[]{:S(2)}) collective-permute-start(f32[512,128]{1,0:T(8,128)S(1)} %collect.3.refs_1_), channel_id=1, source_target_pairs={{0,1},{1,2},{2,3},{3,0},{4,5},{5,6},{6,7},{7,4},{8,9},{9,10},{10,1... | collective-permute-start | bytes 786440 | tf_op jit(solution)/shard_map/ppermute | solution.py:312
  70.1 3.4 %copy-start.3 = (bf16[4,1024,1024]{2,1,0:T(8,128)(2,1)S(1)}, bf16[4,1024,1024]{2,1,0:T(8,128)(2,1)}, u32[]{:S(2)}) copy-start(bf16[4,1024,1024]{2,1,0:T(8,128)(2,1)} %copy-done) | copy-start | bytes 25165828
  75.0 33.4 %all-to-all-start.3 = ((f32[8,128,128]{2,1,0:T(8,128)}), f32[8,128,128]{2,1,0:T(8,128)S(1)}, u32[]{:S(2)}, u32[]{:S(2)}) async-start(f32[8,128,128]{2,1,0:T(8,128)} %bitcast.5), calls=%async_computation.3 | async-start | bytes 1048576 | tf_op jit(solution)/shard_map/all_to_all | solution.py:316
  78.9 33.7 %collective-permute-start.5 = (f32[512,128]{1,0:T(8,128)S(1)}, f32[512,128]{1,0:T(8,128)S(1)}, u32[]{:S(2)}, u32[]{:S(2)}) collective-permute-start(f32[512,128]{1,0:T(8,128)S(1)} %collect.3.refs_1_), channel_id=1, source_target_pairs={{0,3},{1,0},{2,1},{3,2},{4,7},{5,4},{6,5},{7,6},{8,11},{9,8},{10,9... | collective-permute-start | bytes 786440 | tf_op jit(solution)/shard_map/ppermute | solution.py:312
  82.8 34.4 %collective-permute-start.4 = (f32[512,128]{1,0:T(8,128)S(1)}, f32[512,128]{1,0:T(8,128)S(1)}, u32[]{:S(2)}, u32[]{:S(2)}) collective-permute-start(f32[512,128]{1,0:T(8,128)S(1)} %collective-permute-done.3.refs_1_), channel_id=1, source_target_pairs={{0,1},{1,2},{2,3},{3,0},{4,5},{5,6},{6,7},{7,4},{8,9},{9,10},{10,1... | collective-permute-start | bytes 786440 | tf_op jit(solution)/shard_map/ppermute | solution.py:312
  104.3 3.4 %copy-start.4 = (bf16[4,1024,1024]{2,1,0:T(8,128)(2,1)S(1)}, bf16[4,1024,1024]{2,1,0:T(8,128)(2,1)}, u32[]{:S(2)}) copy-start(bf16[4,1024,1024]{2,1,0:T(8,128)(2,1)} %copy-done) | copy-start | bytes 25165828
  109.0 13.8 %collective-permute-start.9 = (f32[512,128]{1,0:T(8,128)S(1)}, f32[512,128]{1,0:T(8,128)S(1)}, u32[]{:S(2)}, u32[]{:S(2)}) collective-permute-start(f32[512,128]{1,0:T(8,128)S(1)} %collect.4.refs_1_), channel_id=1, source_target_pairs={{0,3},{1,0},{2,1},{3,2},{4,7},{5,4},{6,5},{7,6},{8,11},{9,8},{10,9... | collective-permute-start | bytes 786440 | tf_op jit(solution)/shard_map/ppermute | solution.py:312
  112.5 3.4 %copy-start.5 = (bf16[4,1024,1024]{2,1,0:T(8,128)(2,1)S(1)}, bf16[4,1024,1024]{2,1,0:T(8,128)(2,1)}, u32[]{:S(2)}) copy-start(bf16[4,1024,1024]{2,1,0:T(8,128)(2,1)} %copy-done) | copy-start | bytes 25165828
  118.7 20.2 %all-to-all-start.2 = ((f32[8,128,128]{2,1,0:T(8,128)}), f32[8,128,128]{2,1,0:T(8,128)S(1)}, u32[]{:S(2)}, u32[]{:S(2)}) async-start(f32[8,128,128]{2,1,0:T(8,128)} %bitcast.4), calls=%async_computation.2 | async-start | bytes 1048576 | tf_op jit(solution)/shard_map/all_to_all | solution.py:316
  122.9 10.9 %collective-permute-start.11 = (f32[512,128]{1,0:T(8,128)S(1)}, f32[512,128]{1,0:T(8,128)S(1)}, u32[]{:S(2)}, u32[]{:S(2)}) collective-permute-start(f32[512,128]{1,0:T(8,128)S(1)} %collect.4.refs_1_), channel_id=1, source_target_pairs={{0,1},{1,2},{2,3},{3,0},{4,5},{5,6},{6,7},{7,4},{8,9},{9,10},{10,1... | collective-permute-start | bytes 786440 | tf_op jit(solution)/shard_map/ppermute | solution.py:312
  122.9 14.6 %collective-permute-start.10 = (f32[512,128]{1,0:T(8,128)S(1)}, f32[512,128]{1,0:T(8,128)S(1)}, u32[]{:S(2)}, u32[]{:S(2)}) collective-permute-start(f32[512,128]{1,0:T(8,128)S(1)} %collective-permute-done.9.refs_1_), channel_id=1, source_target_pairs={{0,3},{1,0},{2,1},{3,2},{4,7},{5,4},{6,5},{7,6},{8,11},{9,8},{10,9... | collective-permute-start | bytes 786440 | tf_op jit(solution)/shard_map/ppermute | solution.py:312
  126.7 3.4 %copy-start.6 = (bf16[4,1024,1024]{2,1,0:T(8,128)(2,1)S(1)}, bf16[4,1024,1024]{2,1,0:T(8,128)(2,1)}, u32[]{:S(2)}) copy-start(bf16[4,1024,1024]{2,1,0:T(8,128)(2,1)} %copy-done) | copy-start | bytes 25165828
  138.9 19.1 %all-to-all-start.4 = ((f32[8,128,128]{2,1,0:T(8,128)}), f32[8,128,128]{2,1,0:T(8,128)S(1)}, u32[]{:S(2)}, u32[]{:S(2)}) async-start(f32[8,128,128]{2,1,0:T(8,128)} %bitcast.7), calls=%async_computation.4 | async-start | bytes 1048576 | tf_op jit(solution)/shard_map/all_to_all | solution.py:316

commit v4 on v3

v4 whole, which is shorter than its diff:
```python
import functools

import jax
import jax.numpy as jnp
from jax import lax
from jax.experimental import pallas as pl
from jax.experimental.pallas import tpu as pltpu
from jax.sharding import PartitionSpec as P

F = 256
H = 128
TB = 128
CHB = 4
NODES_DEV = CHB * TB
TILES_DEV = 128
GROUPS = 8
MIB = 1 << 20
LIGHT = pl.CostEstimate(flops=1024, bytes_accessed=1024, transcendentals=0)
BF16 = jnp.bfloat16
F32 = jnp.float32

SMEM = pl.BlockSpec(memory_space=pltpu.SMEM)
VMEM = pl.BlockSpec(memory_space=pltpu.VMEM)
HBM = pl.BlockSpec(memory_space=pltpu.HBM)


def params(mib):
    return pltpu.CompilerParams(vmem_limit_bytes=mib * MIB)


def in_hbm(*arrays):
    return [pltpu.with_memory_space_constraint(x, pltpu.HBM) for x in arrays]


def split(x):
    high = x.astype(BF16)
    low = (x - high.astype(F32)).astype(BF16)
    return high, low


def dot3(a, b, dims):
    ah, al = a
    bh, bl = b

    def one(x, y):
        return lax.dot_general(x, y, (dims, ((), ())), preferred_element_type=F32)

    return one(ah, bh) + (one(ah, bl) + one(al, bh))


def fetch(sources, targets, sems):
    copies = [pltpu.make_async_copy(a, b, sems.at[i]) for i, (a, b) in enumerate(zip(sources, targets))]
    for copy in copies:
        copy.start()
    return copies


def masked_of(grad, mask):
    return jnp.where(mask > 0, grad, jnp.zeros_like(grad))


def term_two_kernel(grad_hbm, mask_hbm, weight_hbm, left_ref, right_ref, grad, mask, weight, sems):
    for copy in fetch((grad_hbm, mask_hbm, weight_hbm.at[2]), (grad, mask, weight), sems):
        copy.wait()
    term = dot3(split(masked_of(grad[...], mask[...])), split(weight[...]), ((1,), (1,)))
    left_ref[...] = term[:, :H]
    right_ref[...] = term[:, H:]


def term_two(grad_out, relu_mask, cheb_weight):
    out = jax.ShapeDtypeStruct((NODES_DEV, H), F32)
    return pl.pallas_call(
        term_two_kernel,
        in_specs=[HBM] * 3,
        out_specs=[VMEM, VMEM],
        out_shape=[out, out],
        scratch_shapes=[
            pltpu.VMEM((NODES_DEV, F), F32),
            pltpu.VMEM((NODES_DEV, F), jnp.int32),
            pltpu.VMEM((F, F), F32),
            pltpu.SemaphoreType.DMA((3,)),
        ],
        compiler_params=params(16),
        cost_estimate=LIGHT,
        name="term_two",
    )(*in_hbm(grad_out, relu_mask, cheb_weight))


def local_kernel(
    first_ref, grad_hbm, mask_hbm, weight_hbm, h0, h1, h2, left_ref, right_ref, diff_ref, total_ref, grad, mask, weight, bases, sems
):
    sources = (grad_hbm, mask_hbm, weight_hbm, h0, h1, h2)
    copies = fetch(sources, (grad, mask, weight, bases.at[0], bases.at[1], bases.at[2]), sems)
    for copy in copies[:3]:
        copy.wait()
    masked = split(masked_of(grad[...], mask[...]))
    term = dot3(masked, split(weight[1]), ((1,), (1,)))
    left_ref[...] = term[:, :H]
    right_ref[...] = term[:, H:]
    diff_ref[...] = dot3(masked, split(weight[0] - weight[2]), ((1,), (1,)))
    for k in range(3):
        copies[3 + k].wait()
        total_ref[k] = dot3(split(bases[k]), masked, ((0,), (0,)))


def local_terms(first, grad_out, relu_mask, cheb_weight, b0, b1, b2):
    half = jax.ShapeDtypeStruct((NODES_DEV, H), F32)
    return pl.pallas_call(
        local_kernel,
        in_specs=[pl.BlockSpec(memory_space=pl.ANY)] + [HBM] * 6,
        out_specs=[VMEM] * 4,
        out_shape=[half, half, jax.ShapeDtypeStruct((NODES_DEV, F), F32), jax.ShapeDtypeStruct((3, F, F), F32)],
        scratch_shapes=[
            pltpu.VMEM((NODES_DEV, F), F32),
            pltpu.VMEM((NODES_DEV, F), jnp.int32),
            pltpu.VMEM((3, F, F), F32),
            pltpu.VMEM((3, NODES_DEV, F), F32),
            pltpu.SemaphoreType.DMA((6,)),
        ],
        compiler_params=params(32),
        cost_estimate=LIGHT,
        name="local_terms",
    )(first, *in_hbm(grad_out, relu_mask, cheb_weight, b0, b1, b2))


def operator_kernel(
    n_row, n_col, ids_ref, live_ref, rows_hbm, slots_hbm, values_ref, out_ref,
    tiles, acc, lists, counts, rows, slots, sems, small_sems,
):
    origin = pl.program_id(0)
    size = TILES_DEV // GROUPS

    def copy(g):
        part = pl.ds(g * size, size)
        return pltpu.make_async_copy(values_ref.at[0, part], tiles.at[part], sems.at[g])

    @pl.when(origin == 0)
    def _():
        small = fetch((rows_hbm, slots_hbm), (rows, slots), small_sems)
        for g in range(GROUPS):
            copy(g).start()
        for s in range(n_col):
            counts[s] = 0
        for item in small:
            item.wait()

        def place(t, carry):
            row = rows[0, t]
            s = lax.rem(row // CHB - ids_ref[0] + n_col, n_col)
            position = slots[0, t] * CHB + lax.rem(row, CHB)
            n = counts[s]
            lists[s, n] = position * TILES_DEV + t
            counts[s] = n + 1
            return carry

        lax.fori_loop(0, live_ref[0], place, 0)
        for g in range(GROUPS):
            copy(g).wait()

    acc[...] = jnp.zeros_like(acc)

    def add(n, carry):
        entry = lists[origin, n]
        acc[entry // TILES_DEV] += tiles[lax.rem(entry, TILES_DEV)]
        return carry

    lax.fori_loop(0, counts[origin], add, 0)

    def store(slot, carry):
        here = pl.ds(pl.multiple_of(slot * TB, TB), TB)
        for i in range(CHB):
            high, low = split(acc[slot * CHB + i].T)
            out_ref[0, here, i * TB : (i + 1) * TB] = high
            out_ref[0, here, NODES_DEV + i * TB : NODES_DEV + (i + 1) * TB] = low
        return carry

    lax.fori_loop(0, n_row, store, 0)


def build_operator(n_row, n_col, ids, live, rows, slots, values):
    wide = (n_row * TB, 2 * NODES_DEV)
    return pl.pallas_call(
        functools.partial(operator_kernel, n_row, n_col),
        grid=(n_col,),
        in_specs=[SMEM] * 2 + [HBM] * 3,
        out_specs=pl.BlockSpec((1,) + wide, lambda s: (s, 0, 0)),
        out_shape=pltpu.HBM((n_col,) + wide, BF16),
        scratch_shapes=[
            pltpu.VMEM((TILES_DEV, TB, TB), F32),
            pltpu.VMEM((n_row * CHB, TB, TB), F32),
            pltpu.SMEM((n_col, TILES_DEV), jnp.int32),
            pltpu.SMEM((n_col,), jnp.int32),
            pltpu.SMEM((1, TILES_DEV), jnp.int32),
            pltpu.SMEM((1, TILES_DEV), jnp.int32),
            pltpu.SemaphoreType.DMA((GROUPS,)),
            pltpu.SemaphoreType.DMA((2,)),
        ],
        compiler_params=params(40),
        cost_estimate=LIGHT,
        name="operator",
    )(ids, live, *in_hbm(rows, slots, values))


def product_kernel(n_row, n_col, origins, has_prev, extra, *refs):
    n = len(origins)
    ids_ref, op_ref, refs = refs[0], refs[1], refs[2:]
    fields, refs = refs[:n], refs[n:]
    if has_prev:
        prev, refs = refs[0], refs[1:]
    if extra:
        carriers, refs = refs[:n_col], refs[n_col:]
        out_ref, buf, sems, ordered = refs
    else:
        out_ref, buf, sems = refs
    pairs = n_row // 2
    wide = 2 * TB

    def copy(k, p):
        source = op_ref.at[origins[k], pl.ds(p * wide, wide)]
        return pltpu.make_async_copy(source, buf.at[k, pl.ds(p * wide, wide)], sems.at[k, p])

    for p in range(pairs):
        for k in range(n):
            copy(k, p).start()
    right = []
    for field in fields:
        high, low = split(field[:NODES_DEV, :])
        both = jnp.concatenate([high, low], axis=1)
        right.append(jnp.concatenate([both, both], axis=0))
    if extra:
        for k in range(n_col):
            ordered[lax.rem(ids_ref[0] + k, n_col)] = carriers[k][NODES_DEV:, :]
        share = ordered[0]
        for k in range(1, n_col):
            share = share + ordered[k]
        for q in range(n_row):
            out_ref[q, TB:, :] = share
    for p in range(pairs):
        here = slice(p * wide, (p + 1) * wide)
        total = None
        for k in range(n):
            copy(k, p).wait()
            part = jnp.dot(buf[k, here, :], right[k], preferred_element_type=F32)
            total = part if total is None else total + part
        summed = total[:, :H] + total[:, H:]
        if has_prev:
            summed = summed + prev[here, :]
        if extra:
            out_ref[2 * p, :TB, :] = summed[:TB]
            out_ref[2 * p + 1, :TB, :] = summed[TB:]
        else:
            out_ref[here, :] = summed


def product(n_row, n_col, ids, origins, operator, fields, prev, carriers=()):
    rows = n_row * TB
    n = len(origins)
    has_prev = prev is not None
    extra = carriers[0].shape[0] - NODES_DEV if carriers else 0
    shape = (n_row, TB + extra, H) if extra else (rows, H)
    scratch = [
        pltpu.VMEM((n, rows, 2 * NODES_DEV), BF16),
        pltpu.SemaphoreType.DMA((n, n_row // 2)),
    ]
    if extra:
        scratch.append(pltpu.VMEM((n_col, extra, H), F32))
    return pl.pallas_call(
        functools.partial(product_kernel, n_row, n_col, origins, has_prev, extra),
        in_specs=[SMEM, HBM] + [VMEM] * (n + has_prev + len(carriers)),
        out_specs=VMEM,
        out_shape=jax.ShapeDtypeStruct(shape, F32),
        scratch_shapes=scratch,
        compiler_params=params(40),
        cost_estimate=LIGHT,
        name="product",
    )(ids, *in_hbm(operator), *fields, *((prev,) if has_prev else ()), *carriers)


def collect_kernel(n_row, scale, halves, owners_ref, base_ref, *refs):
    came, refs = refs[:halves], refs[halves:]
    out_ref = refs[-1]
    out_ref[:NODES_DEV, :] = base_ref[...]
    for h in range(halves):
        for q in range(n_row):
            here = pl.ds(pl.multiple_of(owners_ref[q] * TB, TB), TB)
            block = came[h][q, :TB, :]
            out_ref[here, h * H : (h + 1) * H] += block if scale == 1.0 else scale * block
    if len(refs) > 1:
        half = refs[0].shape[0]
        out_ref[NODES_DEV : NODES_DEV + half, :] = refs[0][:, :H]
        out_ref[NODES_DEV + half :, :] = refs[0][:, H:]


def collect(n_row, scale, owners, base, received, share=None):
    shares = () if share is None else (share,)
    under = 2 * share.shape[0] if shares else 0
    return pl.pallas_call(
        functools.partial(collect_kernel, n_row, scale, len(received)),
        in_specs=[SMEM] + [VMEM] * (1 + len(received) + len(shares)),
        out_specs=VMEM,
        out_shape=jax.ShapeDtypeStruct((NODES_DEV + under, base.shape[1]), F32),
        compiler_params=params(24),
        cost_estimate=LIGHT,
        name="collect",
    )(owners, base, *received, *shares)


def assemble_kernel(n_row, came_ref, out_ref):
    rows = 3 * F // n_row
    for q in range(n_row):
        out_ref[q * rows : (q + 1) * rows, :H] = came_ref[q, TB : TB + rows, :]
        out_ref[q * rows : (q + 1) * rows, H:] = came_ref[q, TB + rows :, :]


def assemble(n_row, came):
    return pl.pallas_call(
        functools.partial(assemble_kernel, n_row),
        in_specs=[VMEM],
        out_specs=VMEM,
        out_shape=jax.ShapeDtypeStruct((3 * F, F), F32),
        compiler_params=params(16),
        cost_estimate=LIGHT,
        name="assemble",
    )(came).reshape(3, F, F)


def shift(n_col, x, step):
    return lax.ppermute(x, "col", [(c, (c + step) % n_col) for c in range(n_col)])


def exchange(pieces):
    return lax.all_to_all(pieces, "row", split_axis=0, concat_axis=0, tiled=True)


def after(x, *others):
    return lax.optimization_barrier((x, *others))[0]


def gather(n_col, field, side):
    long = n_col // 2
    short = n_col - 1 - long
    ahead, behind = field, field
    steps = []
    for s in range(1, long + 1):
        ahead = shift(n_col, ahead, side)
        step = [((-side * s) % n_col, ahead)]
        if s <= short:
            behind = shift(n_col, behind, -side)
            step.append(((side * s) % n_col, behind))
        steps.append(step)
    return steps


def transposed(n_row, n_col, ids, operator, field, steps, carrying=False):
    total = product(n_row, n_col, ids, (0,), operator, [field], None)
    carriers = [None] * n_col
    carriers[0] = field
    for step in steps:
        for origin, x in step:
            carriers[origin] = x
        last = carrying and step is steps[-1]
        origins, fields = zip(*step)
        total = product(n_row, n_col, ids, origins, operator, fields, total, carriers if last else ())
    return exchange(total.reshape(n_row, -1, H))


def per_device(
    grad_out,
    relu_mask,
    basis_zero,
    basis_one,
    basis_two,
    cheb_weight,
    tile_values,
    tile_rows,
    tile_slots,
    send_blocks,
    live_tiles,
):
    n_row = lax.axis_size("row")
    n_col = lax.axis_size("col")
    ids = lax.axis_index("col").astype(jnp.int32).reshape(1)
    owners = send_blocks.reshape(n_row)
    left, right = term_two(grad_out, relu_mask, cheb_weight)
    left_steps = gather(n_col, left, 1)
    one_left, one_right, diff, local = local_terms(
        left, grad_out, relu_mask, cheb_weight, basis_zero, basis_one, basis_two
    )
    pieces = exchange(local.reshape(n_row, 3 * F // n_row, F))
    operator = build_operator(n_row, n_col, after(ids, local), live_tiles, tile_rows, tile_slots, tile_values)
    right_steps = gather(n_col, after(right, left_steps[0][0][1]), -1)
    left_first = transposed(n_row, n_col, ids, operator, left, left_steps)
    share = jnp.sum(pieces, axis=0)

    left_carried = collect(n_row, 2.0, owners, one_left, [left_first], share)
    left_steps = gather(n_col, left_carried, 1)
    right_first = transposed(n_row, n_col, ids, operator, right, right_steps)
    right_carried = collect(n_row, 2.0, owners, one_right, [right_first])
    right_steps = gather(n_col, right_carried, -1)
    left_second = transposed(n_row, n_col, ids, operator, left_carried, left_steps, True)
    weight_grad = assemble(n_row, left_second)
    right_second = transposed(n_row, n_col, ids, operator, right_carried, right_steps)
    grad_features = collect(n_row, 1.0, owners, diff, [left_second, right_second])
    return grad_features, weight_grad


def solution(mesh):
    placed = (
        P(("row", "col"), None),
        P(("row", "col"), None),
        P(("row", "col"), None),
        P(("row", "col"), None),
        P(("row", "col"), None),
        P(),
        P(("row", "col"), None, None, None),
        P(("row", "col"), None),
        P(("row", "col"), None),
        P(("row", "col"), None, None),
        P(("row", "col")),
    )
    return jax.shard_map(
        per_device,
        mesh=mesh,
        in_specs=placed,
        out_specs=(P(("row", "col"), None), P()),
        check_vma=False,
    )
```

time: 161 us -> 154 us (0.957)
  blocking collectives: 36.7 us -> 0 us
  Pallas kernels: 32.4 us -> 62.7 us
  waiting for transfers between devices: 16.9 us -> 41.9 us
  local copies, waits for them, and re-layouts: 24.4 us -> 0.01 us
    all_gather x2 -> x0, blocking collectives: 36.7 us -> none  [the longest x1 21.4 us: per_device(): shares = lax.all_gather(jnp.sum(pieces, axis=0), 'col', axis=0)]
    pallas_call x17 -> x18, Pallas kernels: 30.7 us -> 61 us  [the longest x12 42.2 us: product(): pl.pallas_call(functools.partial(product_kernel, n_row, n_col, origins, h...]
    unnamed x17 -> x2, local copies, waits for them, and re-layouts: 24.4 us -> 0.01 us
    ppermute x12, waiting for transfers between devices: 16.9 us -> 33.1 us  [shift(): lax.ppermute(x, 'col', [(c, (c + step) % n_col) for c in range(n_col)])]
    all_to_all x5, waiting for transfers between devices: 0.01 us -> 8.75 us  [exchange(): lax.all_to_all(pieces, 'row', split_axis=0, concat_axis=0, tiled=True)]
    ppermute x12, starting transfers between devices: 26.6 us -> 24.1 us  [shift(): lax.ppermute(x, 'col', [(c, (c + step) % n_col) for c in range(n_col)])]
  transfers between devices with their start and end apart: 17 -> 17, of which waited for: 5 -> 8; matrix products, arithmetic and copies ran while one was open for 1% -> 1% of each run, Pallas kernels for 16% -> 36%
where the time goes in v4:
time: 154 us; the launch traced here: 153 us
  Pallas kernels  62.7 us (41%)
  starting transfers between devices  45.9 us (30%)
  waiting for transfers between devices  41.9 us (27%)
    pallas_call x12, Pallas kernels, product(): pl.pallas_call(functools.partial(product_kernel, n_row, n_col, origins, h...  42.2 us
    ppermute x12, waiting for transfers between devices, shift(): lax.ppermute(x, 'col', [(c, (c + step) % n_col) for c in range(n_col)])  33.1 us
    ppermute x12, starting transfers between devices, shift(): lax.ppermute(x, 'col', [(c, (c + step) % n_col) for c in range(n_col)])  24.1 us
    all_to_all x5, starting transfers between devices, exchange(): lax.all_to_all(pieces, 'row', split_axis=0, concat_axis=0, tiled=True)  21.8 us
    pallas_call x1, Pallas kernels, build_operator(): pl.pallas_call(functools.partial(operator_kernel, n_row, n_col), grid=(n_...  10.1 us
    all_to_all x5, waiting for transfers between devices, exchange(): lax.all_to_all(pieces, 'row', split_axis=0, concat_axis=0, tiled=True)  8.75 us
    pallas_call x1, Pallas kernels, local_terms(): pl.pallas_call(local_kernel, in_specs=[pl.BlockSpec(memory_space=pl.ANY)]...  4.96 us
  transfers between devices with their start and end apart: 17, of which 8 were waited for; matrix products, arithmetic and copies ran while one was open for 1% of the time, Pallas kernels for 36%

profile of v4, /device:TPU:0, one launch (start us, length us, event | category | flops | bytes accessed | tf_op | source)
XLA Modules:
  0.0 153.2 jit_solution(11648304384857422722)
XLA Ops:
  0.6 1.7 %term_two.1 = (f32[512,128]{1,0:T(8,128)S(1)}, f32[512,128]{1,0:T(8,128)S(1)}) custom-call(f32[512,256]{1,0:T(8,128)} %grad_hbm.3, s32[512,256]{1,0:T(8,128)} %mask_hbm.3, f32[3,256,256]{2,1,0:T(8,128)} %weight_hbm.3), custom_call_target="tpu_custom_call" | custom-call | flops 1024 | bytes 1024 | tf_op jit(solution)/shard_map/term_two/pallas_call | solution.py:72
  2.4 5.0 %local_terms.1 = (f32[512,128]{1,0:T(8,128)S(1)}, f32[512,128]{1,0:T(8,128)S(1)}, f32[512,256]{1,0:T(8,128)S(1)}, f32[3,256,256]{2,1,0:T(8,128)}) custom-call(f32[512,128]{1,0:T(8,128)S(1)} %get-tuple-element.10.first_ref.refs_2_, f32[512,256]{1,0:T(8,128)} %grad_hbm.3, s32[512,256]{1,0:T(8,128)} %mask_hbm.3, f32[3,256,256]{2,1,0:T(8,128)} %weight_hbm.3, ...), custom_call_target="tpu_custom_call" | custom-call | flops 1024 | bytes 1024 | tf_op jit(solution)/shard_map/local_terms/pallas_call | solution.py:108
  7.3 5.2 %all-to-all-start.1 = ((f32[8,96,256]{2,1,0:T(8,128)}), f32[8,96,256]{2,1,0:T(8,128)}, u32[]{:S(2)}, u32[]{:S(2)}) async-start(f32[8,96,256]{2,1,0:T(8,128)} %bitcast.3), calls=%async_computation.1 | async-start | bytes 1572864 | tf_op jit(solution)/shard_map/all_to_all | solution.py:332
  12.5 2.1 %collective-permute-start = (f32[512,128]{1,0:T(8,128)S(1)}, f32[512,128]{1,0:T(8,128)S(1)}, u32[]{:S(2)}, u32[]{:S(2)}) collective-permute-start(f32[512,128]{1,0:T(8,128)S(1)} %get-tuple-element.10.first_ref.refs_2_), channel_id=1, source_target_pairs={{0,1},{1,2},{2,3},{3,0},{4,5},{5,6},{6,7},{7,4},{8,9},{9,10},{10,1... | collective-permute-start | bytes 786440 | tf_op jit(solution)/shard_map/ppermute | solution.py:328
  14.6 2.1 %collective-permute-start.2 = (f32[512,128]{1,0:T(8,128)S(1)}, f32[512,128]{1,0:T(8,128)S(1)}, u32[]{:S(2)}, u32[]{:S(2)}) collective-permute-start(f32[512,128]{1,0:T(8,128)S(1)} %get-tuple-element.10.first_ref.refs_2_), channel_id=1, source_target_pairs={{0,3},{1,0},{2,1},{3,2},{4,7},{5,4},{6,5},{7,6},{8,11},{9,8},{10,9... | collective-permute-start | bytes 786440 | tf_op jit(solution)/shard_map/ppermute | solution.py:328
  16.7 7.0 %collective-permute-done.refs_2_ = f32[512,128]{1,0:T(8,128)S(1)} collective-permute-done((f32[512,128]{1,0:T(8,128)S(1)}, f32[512,128]{1,0:T(8,128)S(1)}, u32[]{:S(2)}, u32[]{:S(2)}) %collective-permute-start) | collective-permute-done | bytes 262176 | tf_op jit(solution)/shard_map/ppermute | solution.py:328
  23.8 0.0 collective-permute-start.1
  24.4 10.1 %operator.1.refs_1_ = bf16[4,1024,1024]{2,1,0:T(8,128)(2,1)} custom-call(s32[1]{0:T(128)} %bitcast.1.ids_ref.refs_0_, s32[1]{0:T(128)S(6)} %copy.13.live_ref, s32[1,128]{1,0:T(1,128)} %rows_hbm.1, s32[1,128]{1,0:T(1,128)} %slots_hbm.1, f32[1,128,128,128]{3,2,1,0:T(8,128)} %values_ref.1), custom_call_target="tpu_custom_call" | custom-call | flops 1024 | bytes 1024 | tf_op jit(solution)/shard_map/operator/pallas_call | solution.py:182
  34.5 2.8 %product.12.refs_4_ = f32[1024,128]{1,0:T(8,128)S(1)} custom-call(s32[1]{0:T(128)} %bitcast.1.ids_ref.refs_0_, bf16[4,1024,1024]{2,1,0:T(8,128)(2,1)} %operator.1.refs_1_, f32[512,128]{1,0:T(8,128)S(1)} %get-tuple-element.10.first_ref.refs_2_), custom_call_target="tpu_custom_call" | custom-call | flops 1024 | bytes 1024 | tf_op jit(solution)/shard_map/product/pallas_call | solution.py:267
  37.3 0.0 copy-start
  37.3 0.0 collective-permute-done.2.refs_3_
  37.3 4.2 %product.13.refs_3_ = f32[1024,128]{1,0:T(8,128)S(1)} custom-call(s32[1]{0:T(128)} %bitcast.1.ids_ref.refs_0_, bf16[4,1024,1024]{2,1,0:T(8,128)(2,1)} %operator.1.refs_1_, f32[512,128]{1,0:T(8,128)S(1)} %collective-permute-done.refs_2_, f32[512,128]{1,0:T(8,128)S(1)} %collective-permute-done.2.refs_3_, f32[1024,128]{1,0:T(8,128)S(1)} %product.12.refs_4_), custom_call_target="tpu_custom_call" | custom-call | flops 1024 | bytes 1024 | tf_op jit(solution)/shard_map/product/pallas_call | solution.py:267
  41.5 0.0 collective-permute-done.1.refs_2_
  41.5 3.5 %product.14 = f32[1024,128]{1,0:T(8,128)} custom-call(s32[1]{0:T(128)} %bitcast.1.ids_ref.refs_0_, bf16[4,1024,1024]{2,1,0:T(8,128)(2,1)} %operator.1.refs_1_, f32[512,128]{1,0:T(8,128)S(1)} %collective-permute-done.1.refs_2_, f32[1024,128]{1,0:T(8,128)S(1)} %product.13.refs_3_), custom_call_target="tpu_custom_call" | custom-call | flops 1024 | bytes 1024 | tf_op jit(solution)/shard_map/product/pallas_call | solution.py:267
  45.1 0.0 all-to-all-done.1
  45.1 5.3 %all-to-all-start = ((f32[8,128,128]{2,1,0:T(8,128)}), f32[8,128,128]{2,1,0:T(8,128)S(1)}, u32[]{:S(2)}, u32[]{:S(2)}) async-start(f32[8,128,128]{2,1,0:T(8,128)} %bitcast.2), calls=%async_computation | async-start | bytes 1048576 | tf_op jit(solution)/shard_map/all_to_all | solution.py:332
  50.4 5.5 %collective-permute-start.6 = (f32[512,128]{1,0:T(8,128)S(1)}, f32[512,128]{1,0:T(8,128)S(1)}, u32[]{:S(2)}, u32[]{:S(2)}) collective-permute-start(f32[512,128]{1,0:T(8,128)S(1)} %get-tuple-element.17.refs_2_), channel_id=1, source_target_pairs={{0,3},{1,0},{2,1},{3,2},{4,7},{5,4},{6,5},{7,6},{8,11},{9,8},{10,9... | collective-permute-start | bytes 786440 | tf_op jit(solution)/shard_map/ppermute | solution.py:328
  55.9 0.0 collective-permute-start.8
  55.9 6.7 %collective-permute-done.6.refs_2_ = f32[512,128]{1,0:T(8,128)S(1)} collective-permute-done((f32[512,128]{1,0:T(8,128)S(1)}, f32[512,128]{1,0:T(8,128)S(1)}, u32[]{:S(2)}, u32[]{:S(2)}) %collective-permute-start.6) | collective-permute-done | bytes 262176 | tf_op jit(solution)/shard_map/ppermute | solution.py:328
  62.6 4.3 %collective-permute-start.7 = (f32[512,128]{1,0:T(8,128)S(1)}, f32[512,128]{1,0:T(8,128)S(1)}, u32[]{:S(2)}, u32[]{:S(2)}) collective-permute-start(f32[512,128]{1,0:T(8,128)S(1)} %collective-permute-done.6.refs_2_), channel_id=1, source_target_pairs={{0,3},{1,0},{2,1},{3,2},{4,7},{5,4},{6,5},{7,6},{8,11},{9,8},{10,9... | collective-permute-start | bytes 786440 | tf_op jit(solution)/shard_map/ppermute | solution.py:328
  66.9 1.2 reduce_sum.9.refs_1_
  68.0 0.0 all-to-all-done.refs_0_
  68.1 0.0 copy-done
  68.1 0.6 collect.3.refs_2_.refs_4_
  68.7 0.1 collective-permute-start.3
  68.8 2.8 %product.18.refs_4_ = f32[1024,128]{1,0:T(8,128)S(1)} custom-call(s32[1]{0:T(128)} %bitcast.1.ids_ref.refs_0_, bf16[4,1024,1024]{2,1,0:T(8,128)(2,1)} %operator.1.refs_1_, f32[512,128]{1,0:T(8,128)S(1)} %get-tuple-element.17.refs_2_), custom_call_target="tpu_custom_call" | custom-call | flops 1024 | bytes 1024 | tf_op jit(solution)/shard_map/product/pallas_call | solution.py:267
  71.5 0.0 collective-permute-done.8.refs_3_
  71.5 4.2 %product.19.refs_3_ = f32[1024,128]{1,0:T(8,128)S(1)} custom-call(s32[1]{0:T(128)} %bitcast.1.ids_ref.refs_0_, bf16[4,1024,1024]{2,1,0:T(8,128)(2,1)} %operator.1.refs_1_, f32[512,128]{1,0:T(8,128)S(1)} %collective-permute-done.6.refs_2_, f32[512,128]{1,0:T(8,128)S(1)} %collective-permute-done.8.refs_3_, f32[1024,128]{1,0:T(8,128)S(1)} %product.18.refs_4_), custom_call_target="tpu_custom_call" | custom-call | flops 1024 | bytes 1024 | tf_op jit(solution)/shard_map/product/pallas_call | solution.py:267
  75.7 0.4 collective-permute-done.7.refs_2_
  76.1 3.5 %product.20 = f32[1024,128]{1,0:T(8,128)} custom-call(s32[1]{0:T(128)} %bitcast.1.ids_ref.refs_0_, bf16[4,1024,1024]{2,1,0:T(8,128)(2,1)} %operator.1.refs_1_, f32[512,128]{1,0:T(8,128)S(1)} %collective-permute-done.7.refs_2_, f32[1024,128]{1,0:T(8,128)S(1)} %product.19.refs_3_), custom_call_target="tpu_custom_call" | custom-call | flops 1024 | bytes 1024 | tf_op jit(solution)/shard_map/product/pallas_call | solution.py:267
  79.6 3.9 %all-to-all-start.3 = ((f32[8,128,128]{2,1,0:T(8,128)}), f32[8,128,128]{2,1,0:T(8,128)S(1)}, u32[]{:S(2)}, u32[]{:S(2)}) async-start(f32[8,128,128]{2,1,0:T(8,128)} %bitcast.4), calls=%async_computation.3 | async-start | bytes 1048576 | tf_op jit(solution)/shard_map/all_to_all | solution.py:332
  83.5 3.8 %collective-permute-start.5 = (f32[704,128]{1,0:T(8,128)S(1)}, f32[704,128]{1,0:T(8,128)S(1)}, u32[]{:S(2)}, u32[]{:S(2)}) collective-permute-start(f32[704,128]{1,0:T(8,128)S(1)} %collect.3.refs_2_.refs_4_), channel_id=1, source_target_pairs={{0,3},{1,0},{2,1},{3,2},{4,7},{5,4},{6,5},{7,6},{8,11},{9,8},{10,9... | collective-permute-start | bytes 1081352 | tf_op jit(solution)/shard_map/ppermute | solution.py:328
  87.4 0.0 collective-permute-done.3.refs_2_.refs_7_
  87.4 0.0 collective-permute-start.4
  87.4 2.8 %product.15.refs_4_ = f32[1024,128]{1,0:T(8,128)S(1)} custom-call(s32[1]{0:T(128)} %bitcast.1.ids_ref.refs_0_, bf16[4,1024,1024]{2,1,0:T(8,128)(2,1)} %operator.1.refs_1_, f32[704,128]{1,0:T(8,128)S(1)} %collect.3.refs_2_.refs_4_), custom_call_target="tpu_custom_call" | custom-call | flops 1024 | bytes 1024 | tf_op jit(solution)/shard_map/product/pallas_call | solution.py:267
  90.1 6.0 %collective-permute-done.5.refs_3_.refs_5_ = f32[704,128]{1,0:T(8,128)S(1)} collective-permute-done((f32[704,128]{1,0:T(8,128)S(1)}, f32[704,128]{1,0:T(8,128)S(1)}, u32[]{:S(2)}, u32[]{:S(2)}) %collective-permute-start.5) | collective-permute-done | bytes 360480 | tf_op jit(solution)/shard_map/ppermute | solution.py:328
  96.1 4.2 %product.16.refs_3_ = f32[1024,128]{1,0:T(8,128)S(1)} custom-call(s32[1]{0:T(128)} %bitcast.1.ids_ref.refs_0_, bf16[4,1024,1024]{2,1,0:T(8,128)(2,1)} %operator.1.refs_1_, f32[704,128]{1,0:T(8,128)S(1)} %collective-permute-done.3.refs_2_.refs_7_, f32[704,128]{1,0:T(8,128)S(1)} %collective-permute-done.5.refs_3_.refs_5_, f32[1024,128]{1,0:T(8,128)S(1)} %product.15.refs_4_), custom_call_target="tpu_custom_call" | custom-call | flops 1024 | bytes 1024 | tf_op jit(solution)/shard_map/product/pallas_call | solution.py:267
  100.3 3.9 %collective-permute-done.4.refs_2_.refs_6_ = f32[704,128]{1,0:T(8,128)S(1)} collective-permute-done((f32[704,128]{1,0:T(8,128)S(1)}, f32[704,128]{1,0:T(8,128)S(1)}, u32[]{:S(2)}, u32[]{:S(2)}) %collective-permute-start.4) | collective-permute-done | bytes 360480 | tf_op jit(solution)/shard_map/ppermute | solution.py:328
  104.2 3.9 %product.17 = f32[8,320,128]{2,1,0:T(8,128)} custom-call(s32[1]{0:T(128)} %bitcast.1.ids_ref.refs_0_, bf16[4,1024,1024]{2,1,0:T(8,128)(2,1)} %operator.1.refs_1_, f32[704,128]{1,0:T(8,128)S(1)} %collective-permute-done.4.refs_2_.refs_6_, f32[1024,128]{1,0:T(8,128)S(1)} %product.16.refs_3_, f32[704,128]{1,0:T(8,128)S(1)} %collect.3.refs_2_.refs_4_, ...), custom_call_target="tpu_custom_call" | custom-call | flops 1024 | bytes 1024 | tf_op jit(solution)/shard_map/product/pallas_call | solution.py:267
  108.1 0.0 all-to-all-done.3.refs_0_
  108.1 3.9 %all-to-all-start.2 = ((f32[8,320,128]{2,1,0:T(8,128)}), f32[8,320,128]{2,1,0:T(8,128)S(1)}, u32[]{:S(2)}, u32[]{:S(2)}) async-start(f32[8,320,128]{2,1,0:T(8,128)} %product.17), calls=%async_computation.2 | async-start | bytes 2621440 | tf_op jit(solution)/shard_map/all_to_all | solution.py:332
  111.9 0.6 collect.4.refs_2_
  112.6 2.0 %collective-permute-start.9 = (f32[512,128]{1,0:T(8,128)S(1)}, f32[512,128]{1,0:T(8,128)S(1)}, u32[]{:S(2)}, u32[]{:S(2)}) collective-permute-start(f32[512,128]{1,0:T(8,128)S(1)} %collect.4.refs_2_), channel_id=1, source_target_pairs={{0,3},{1,0},{2,1},{3,2},{4,7},{5,4},{6,5},{7,6},{8,11},{9,8},{10,9... | collective-permute-start | bytes 786440 | tf_op jit(solution)/shard_map/ppermute | solution.py:328
  114.6 0.0 collective-permute-start.11
  114.6 6.7 %collective-permute-done.9.refs_2_ = f32[512,128]{1,0:T(8,128)S(1)} collective-permute-done((f32[512,128]{1,0:T(8,128)S(1)}, f32[512,128]{1,0:T(8,128)S(1)}, u32[]{:S(2)}, u32[]{:S(2)}) %collective-permute-start.9) | collective-permute-done | bytes 262176 | tf_op jit(solution)/shard_map/ppermute | solution.py:328
  121.4 4.2 %collective-permute-start.10 = (f32[512,128]{1,0:T(8,128)S(1)}, f32[512,128]{1,0:T(8,128)S(1)}, u32[]{:S(2)}, u32[]{:S(2)}) collective-permute-start(f32[512,128]{1,0:T(8,128)S(1)} %collective-permute-done.9.refs_2_), channel_id=1, source_target_pairs={{0,3},{1,0},{2,1},{3,2},{4,7},{5,4},{6,5},{7,6},{8,11},{9,8},{10,9... | collective-permute-start | bytes 786440 | tf_op jit(solution)/shard_map/ppermute | solution.py:328
  125.5 2.8 %product.21.refs_4_ = f32[1024,128]{1,0:T(8,128)S(1)} custom-call(s32[1]{0:T(128)} %bitcast.1.ids_ref.refs_0_, bf16[4,1024,1024]{2,1,0:T(8,128)(2,1)} %operator.1.refs_1_, f32[512,128]{1,0:T(8,128)S(1)} %collect.4.refs_2_), custom_call_target="tpu_custom_call" | custom-call | flops 1024 | bytes 1024 | tf_op jit(solution)/shard_map/product/pallas_call | solution.py:267
  128.3 0.0 collective-permute-done.11.refs_3_
  128.3 4.2 %product.22.refs_3_ = f32[1024,128]{1,0:T(8,128)S(1)} custom-call(s32[1]{0:T(128)} %bitcast.1.ids_ref.refs_0_, bf16[4,1024,1024]{2,1,0:T(8,128)(2,1)} %operator.1.refs_1_, f32[512,128]{1,0:T(8,128)S(1)} %collective-permute-done.9.refs_2_, f32[512,128]{1,0:T(8,128)S(1)} %collective-permute-done.11.refs_3_, f32[1024,128]{1,0:T(8,128)S(1)} %product.21.refs_4_), custom_call_target="tpu_custom_call" | custom-call | flops 1024 | bytes 1024 | tf_op jit(solution)/shard_map/product/pallas_call | solution.py:267
  132.5 2.4 %collective-permute-done.10.refs_2_ = f32[512,128]{1,0:T(8,128)S(1)} collective-permute-done((f32[512,128]{1,0:T(8,128)S(1)}, f32[512,128]{1,0:T(8,128)S(1)}, u32[]{:S(2)}, u32[]{:S(2)}) %collective-permute-start.10) | collective-permute-done | bytes 262176 | tf_op jit(solution)/shard_map/ppermute | solution.py:328
  134.9 3.6 %product.23 = f32[1024,128]{1,0:T(8,128)} custom-call(s32[1]{0:T(128)} %bitcast.1.ids_ref.refs_0_, bf16[4,1024,1024]{2,1,0:T(8,128)(2,1)} %operator.1.refs_1_, f32[512,128]{1,0:T(8,128)S(1)} %collective-permute-done.10.refs_2_, f32[1024,128]{1,0:T(8,128)S(1)} %product.22.refs_3_), custom_call_target="tpu_custom_call" | custom-call | flops 1024 | bytes 1024 | tf_op jit(solution)/shard_map/product/pallas_call | solution.py:267
  138.5 0.0 all-to-all-done.2.refs_0_.came_ref
  138.5 3.5 %all-to-all-start.4 = ((f32[8,128,128]{2,1,0:T(8,128)}), f32[8,128,128]{2,1,0:T(8,128)S(1)}, u32[]{:S(2)}, u32[]{:S(2)}) async-start(f32[8,128,128]{2,1,0:T(8,128)} %bitcast.5), calls=%async_computation.4 | async-start | bytes 1048576 | tf_op jit(solution)/shard_map/all_to_all | solution.py:332
  142.0 0.9 assemble.1
  142.9 8.7 %all-to-all-done.4.refs_1_ = f32[8,128,128]{2,1,0:T(8,128)S(1)} async-done(((f32[8,128,128]{2,1,0:T(8,128)}), f32[8,128,128]{2,1,0:T(8,128)S(1)}, u32[]{:S(2)}, u32[]{:S(2)}) %all-to-all-start.4) | async-done | bytes 524320 | tf_op jit(solution)/shard_map/all_to_all | solution.py:332
  151.7 1.5 collect.5
Async XLA Ops:
  7.3 37.7 %all-to-all-start.1 = ((f32[8,96,256]{2,1,0:T(8,128)}), f32[8,96,256]{2,1,0:T(8,128)}, u32[]{:S(2)}, u32[]{:S(2)}) async-start(f32[8,96,256]{2,1,0:T(8,128)} %bitcast.3), calls=%async_computation.1 | async-start | bytes 1572864 | tf_op jit(solution)/shard_map/all_to_all | solution.py:332
  12.5 11.3 %collective-permute-start = (f32[512,128]{1,0:T(8,128)S(1)}, f32[512,128]{1,0:T(8,128)S(1)}, u32[]{:S(2)}, u32[]{:S(2)}) collective-permute-start(f32[512,128]{1,0:T(8,128)S(1)} %get-tuple-element.10.first_ref.refs_2_), channel_id=1, source_target_pairs={{0,1},{1,2},{2,3},{3,0},{4,5},{5,6},{6,7},{7,4},{8,9},{9,10},{10,1... | collective-permute-start | bytes 786440 | tf_op jit(solution)/shard_map/ppermute | solution.py:328
  14.6 22.7 %collective-permute-start.2 = (f32[512,128]{1,0:T(8,128)S(1)}, f32[512,128]{1,0:T(8,128)S(1)}, u32[]{:S(2)}, u32[]{:S(2)}) collective-permute-start(f32[512,128]{1,0:T(8,128)S(1)} %get-tuple-element.10.first_ref.refs_2_), channel_id=1, source_target_pairs={{0,3},{1,0},{2,1},{3,2},{4,7},{5,4},{6,5},{7,6},{8,11},{9,8},{10,9... | collective-permute-start | bytes 786440 | tf_op jit(solution)/shard_map/ppermute | solution.py:328
  23.8 17.7 %collective-permute-start.1 = (f32[512,128]{1,0:T(8,128)S(1)}, f32[512,128]{1,0:T(8,128)S(1)}, u32[]{:S(2)}, u32[]{:S(2)}) collective-permute-start(f32[512,128]{1,0:T(8,128)S(1)} %collective-permute-done.refs_2_), channel_id=1, source_target_pairs={{0,1},{1,2},{2,3},{3,0},{4,5},{5,6},{6,7},{7,4},{8,9},{9,10},{10,1... | collective-permute-start | bytes 786440 | tf_op jit(solution)/shard_map/ppermute | solution.py:328
  37.3 30.8 %copy-start = (s32[1,8,1]{1,2,0:T(1,128)S(1)}, s32[1,8,1]{1,2,0:T(1,128)}, u32[]{:S(2)}) copy-start(s32[1,8,1]{1,2,0:T(1,128)} %param.20) | copy-start | bytes 100
  45.1 23.0 %all-to-all-start = ((f32[8,128,128]{2,1,0:T(8,128)}), f32[8,128,128]{2,1,0:T(8,128)S(1)}, u32[]{:S(2)}, u32[]{:S(2)}) async-start(f32[8,128,128]{2,1,0:T(8,128)} %bitcast.2), calls=%async_computation | async-start | bytes 1048576 | tf_op jit(solution)/shard_map/all_to_all | solution.py:332
  50.4 12.2 %collective-permute-start.6 = (f32[512,128]{1,0:T(8,128)S(1)}, f32[512,128]{1,0:T(8,128)S(1)}, u32[]{:S(2)}, u32[]{:S(2)}) collective-permute-start(f32[512,128]{1,0:T(8,128)S(1)} %get-tuple-element.17.refs_2_), channel_id=1, source_target_pairs={{0,3},{1,0},{2,1},{3,2},{4,7},{5,4},{6,5},{7,6},{8,11},{9,8},{10,9... | collective-permute-start | bytes 786440 | tf_op jit(solution)/shard_map/ppermute | solution.py:328
  55.9 15.6 %collective-permute-start.8 = (f32[512,128]{1,0:T(8,128)S(1)}, f32[512,128]{1,0:T(8,128)S(1)}, u32[]{:S(2)}, u32[]{:S(2)}) collective-permute-start(f32[512,128]{1,0:T(8,128)S(1)} %get-tuple-element.17.refs_2_), channel_id=1, source_target_pairs={{0,1},{1,2},{2,3},{3,0},{4,5},{5,6},{6,7},{7,4},{8,9},{9,10},{10,1... | collective-permute-start | bytes 786440 | tf_op jit(solution)/shard_map/ppermute | solution.py:328
  62.6 13.5 %collective-permute-start.7 = (f32[512,128]{1,0:T(8,128)S(1)}, f32[512,128]{1,0:T(8,128)S(1)}, u32[]{:S(2)}, u32[]{:S(2)}) collective-permute-start(f32[512,128]{1,0:T(8,128)S(1)} %collective-permute-done.6.refs_2_), channel_id=1, source_target_pairs={{0,3},{1,0},{2,1},{3,2},{4,7},{5,4},{6,5},{7,6},{8,11},{9,8},{10,9... | collective-permute-start | bytes 786440 | tf_op jit(solution)/shard_map/ppermute | solution.py:328
  68.7 18.7 %collective-permute-start.3 = (f32[704,128]{1,0:T(8,128)S(1)}, f32[704,128]{1,0:T(8,128)S(1)}, u32[]{:S(2)}, u32[]{:S(2)}) collective-permute-start(f32[704,128]{1,0:T(8,128)S(1)} %collect.3.refs_2_.refs_4_), channel_id=1, source_target_pairs={{0,1},{1,2},{2,3},{3,0},{4,5},{5,6},{6,7},{7,4},{8,9},{9,10},{10,1... | collective-permute-start | bytes 1081352 | tf_op jit(solution)/shard_map/ppermute | solution.py:328
  79.6 28.4 %all-to-all-start.3 = ((f32[8,128,128]{2,1,0:T(8,128)}), f32[8,128,128]{2,1,0:T(8,128)S(1)}, u32[]{:S(2)}, u32[]{:S(2)}) async-start(f32[8,128,128]{2,1,0:T(8,128)} %bitcast.4), calls=%async_computation.3 | async-start | bytes 1048576 | tf_op jit(solution)/shard_map/all_to_all | solution.py:332
  83.5 12.6 %collective-permute-start.5 = (f32[704,128]{1,0:T(8,128)S(1)}, f32[704,128]{1,0:T(8,128)S(1)}, u32[]{:S(2)}, u32[]{:S(2)}) collective-permute-start(f32[704,128]{1,0:T(8,128)S(1)} %collect.3.refs_2_.refs_4_), channel_id=1, source_target_pairs={{0,3},{1,0},{2,1},{3,2},{4,7},{5,4},{6,5},{7,6},{8,11},{9,8},{10,9... | collective-permute-start | bytes 1081352 | tf_op jit(solution)/shard_map/ppermute | solution.py:328
  87.4 16.8 %collective-permute-start.4 = (f32[704,128]{1,0:T(8,128)S(1)}, f32[704,128]{1,0:T(8,128)S(1)}, u32[]{:S(2)}, u32[]{:S(2)}) collective-permute-start(f32[704,128]{1,0:T(8,128)S(1)} %collective-permute-done.3.refs_2_.refs_7_), channel_id=1, source_target_pairs={{0,1},{1,2},{2,3},{3,0},{4,5},{5,6},{6,7},{7,4},{8,9},{9,10},{10,1... | collective-permute-start | bytes 1081352 | tf_op jit(solution)/shard_map/ppermute | solution.py:328
  108.1 30.4 %all-to-all-start.2 = ((f32[8,320,128]{2,1,0:T(8,128)}), f32[8,320,128]{2,1,0:T(8,128)S(1)}, u32[]{:S(2)}, u32[]{:S(2)}) async-start(f32[8,320,128]{2,1,0:T(8,128)} %product.17), calls=%async_computation.2 | async-start | bytes 2621440 | tf_op jit(solution)/shard_map/all_to_all | solution.py:332
  112.6 8.8 %collective-permute-start.9 = (f32[512,128]{1,0:T(8,128)S(1)}, f32[512,128]{1,0:T(8,128)S(1)}, u32[]{:S(2)}, u32[]{:S(2)}) collective-permute-start(f32[512,128]{1,0:T(8,128)S(1)} %collect.4.refs_2_), channel_id=1, source_target_pairs={{0,3},{1,0},{2,1},{3,2},{4,7},{5,4},{6,5},{7,6},{8,11},{9,8},{10,9... | collective-permute-start | bytes 786440 | tf_op jit(solution)/shard_map/ppermute | solution.py:328
  114.6 13.7 %collective-permute-start.11 = (f32[512,128]{1,0:T(8,128)S(1)}, f32[512,128]{1,0:T(8,128)S(1)}, u32[]{:S(2)}, u32[]{:S(2)}) collective-permute-start(f32[512,128]{1,0:T(8,128)S(1)} %collect.4.refs_2_), channel_id=1, source_target_pairs={{0,1},{1,2},{2,3},{3,0},{4,5},{5,6},{6,7},{7,4},{8,9},{9,10},{10,1... | collective-permute-start | bytes 786440 | tf_op jit(solution)/shard_map/ppermute | solution.py:328
  121.4 13.6 %collective-permute-start.10 = (f32[512,128]{1,0:T(8,128)S(1)}, f32[512,128]{1,0:T(8,128)S(1)}, u32[]{:S(2)}, u32[]{:S(2)}) collective-permute-start(f32[512,128]{1,0:T(8,128)S(1)} %collective-permute-done.9.refs_2_), channel_id=1, source_target_pairs={{0,3},{1,0},{2,1},{3,2},{4,7},{5,4},{6,5},{7,6},{8,11},{9,8},{10,9... | collective-permute-start | bytes 786440 | tf_op jit(solution)/shard_map/ppermute | solution.py:328
  138.5 13.2 %all-to-all-start.4 = ((f32[8,128,128]{2,1,0:T(8,128)}), f32[8,128,128]{2,1,0:T(8,128)S(1)}, u32[]{:S(2)}, u32[]{:S(2)}) async-start(f32[8,128,128]{2,1,0:T(8,128)} %bitcast.5), calls=%async_computation.4 | async-start | bytes 1048576 | tf_op jit(solution)/shard_map/all_to_all | solution.py:332

commit v5 on v4

v5 whole, which is shorter than its diff:
```python
import functools

import jax
import jax.numpy as jnp
from jax import lax
from jax.experimental import pallas as pl
from jax.experimental.pallas import tpu as pltpu
from jax.sharding import PartitionSpec as P

F = 256
H = 128
TB = 128
CHB = 4
WIDE = 2 * TB
LANES = 128
NODES_DEV = CHB * TB
TILES_DEV = 128
GROUPS = 8
MIB = 1 << 20
LIGHT = pl.CostEstimate(flops=1024, bytes_accessed=1024, transcendentals=0)
BF16 = jnp.bfloat16
F32 = jnp.float32

SMEM = pl.BlockSpec(memory_space=pltpu.SMEM)
VMEM = pl.BlockSpec(memory_space=pltpu.VMEM)
HBM = pl.BlockSpec(memory_space=pltpu.HBM)


def params(mib):
    return pltpu.CompilerParams(vmem_limit_bytes=mib * MIB)


def in_hbm(*arrays):
    return [pltpu.with_memory_space_constraint(x, pltpu.HBM) for x in arrays]


def split(x):
    high = x.astype(BF16)
    low = (x - high.astype(F32)).astype(BF16)
    return high, low


def dot3(a, b, dims):
    ah, al = a
    bh, bl = b

    def one(x, y):
        return lax.dot_general(x, y, (dims, ((), ())), preferred_element_type=F32)

    return one(ah, bh) + (one(ah, bl) + one(al, bh))


def fetch(sources, targets, sems):
    copies = [pltpu.make_async_copy(a, b, sems.at[i]) for i, (a, b) in enumerate(zip(sources, targets))]
    for copy in copies:
        copy.start()
    return copies


def masked_of(grad, mask):
    return jnp.where(mask > 0, grad, jnp.zeros_like(grad))


def term_two_kernel(grad_hbm, mask_hbm, weight_hbm, left_ref, right_ref, grad, mask, weight, sems):
    for copy in fetch((grad_hbm, mask_hbm, weight_hbm.at[2]), (grad, mask, weight), sems):
        copy.wait()
    term = dot3(split(weight[...]), split(masked_of(grad[...], mask[...])), ((1,), (1,)))
    left_ref[...] = term[:H]
    right_ref[...] = term[H:]


def term_two(grad_out, relu_mask, cheb_weight):
    out = jax.ShapeDtypeStruct((H, NODES_DEV), F32)
    return pl.pallas_call(
        term_two_kernel,
        in_specs=[HBM] * 3,
        out_specs=[VMEM, VMEM],
        out_shape=[out, out],
        scratch_shapes=[
            pltpu.VMEM((NODES_DEV, F), F32),
            pltpu.VMEM((NODES_DEV, F), jnp.int32),
            pltpu.VMEM((F, F), F32),
            pltpu.SemaphoreType.DMA((3,)),
        ],
        compiler_params=params(16),
        cost_estimate=LIGHT,
        name="term_two",
    )(*in_hbm(grad_out, relu_mask, cheb_weight))


def local_kernel(
    n_row, first_ref, grad_hbm, mask_hbm, weight_hbm, h0, h1, h2, left_ref, right_ref, diff_ref, pieces_ref,
    grad, mask, weight, bases, sems,
):
    sources = (grad_hbm, mask_hbm, weight_hbm, h0, h1, h2)
    copies = fetch(sources, (grad, mask, weight, bases.at[0], bases.at[1], bases.at[2]), sems)
    for copy in copies[:3]:
        copy.wait()
    values = masked_of(grad[...], mask[...])
    masked = split(values)
    term = dot3(split(weight[1]), masked, ((1,), (1,)))
    left_ref[...] = term[:H]
    right_ref[...] = term[H:]
    diff_ref[...] = dot3(split(weight[0] - weight[2]), masked, ((1,), (1,)))
    turned = split(values.T)
    rows = F // n_row
    for k in range(3):
        copies[3 + k].wait()
        part = dot3(turned, split(bases[k]), ((1,), (0,)))
        for j in range(F // LANES):
            here = (k * (F // LANES) + j) * rows
            for q in range(n_row):
                pieces_ref[q, here : here + rows, :] = part[q * rows : (q + 1) * rows, j * LANES : (j + 1) * LANES]


def local_terms(n_row, first, grad_out, relu_mask, cheb_weight, b0, b1, b2):
    half = jax.ShapeDtypeStruct((H, NODES_DEV), F32)
    share = 3 * F * F // n_row // LANES
    return pl.pallas_call(
        functools.partial(local_kernel, n_row),
        in_specs=[pl.BlockSpec(memory_space=pl.ANY)] + [HBM] * 6,
        out_specs=[VMEM] * 4,
        out_shape=[
            half,
            half,
            jax.ShapeDtypeStruct((F, NODES_DEV), F32),
            jax.ShapeDtypeStruct((n_row, share, LANES), F32),
        ],
        scratch_shapes=[
            pltpu.VMEM((NODES_DEV, F), F32),
            pltpu.VMEM((NODES_DEV, F), jnp.int32),
            pltpu.VMEM((3, F, F), F32),
            pltpu.VMEM((3, NODES_DEV, F), F32),
            pltpu.SemaphoreType.DMA((6,)),
        ],
        compiler_params=params(32),
        cost_estimate=LIGHT,
        name="local_terms",
    )(first, *in_hbm(grad_out, relu_mask, cheb_weight, b0, b1, b2))


def operator_kernel(
    n_col, ids_ref, live_ref, rows_hbm, slots_hbm, values_ref, out_ref,
    tiles, acc, lists, counts, rows, slots, sems, small_sems,
):
    origin = pl.program_id(0)
    size = TILES_DEV // GROUPS

    def copy(g):
        part = pl.ds(g * size, size)
        return pltpu.make_async_copy(values_ref.at[0, part], tiles.at[part], sems.at[g])

    @pl.when(origin == 0)
    def _():
        small = fetch((rows_hbm, slots_hbm), (rows, slots), small_sems)
        for g in range(GROUPS):
            copy(g).start()
        for s in range(n_col):
            counts[s] = 0
        for item in small:
            item.wait()

        def place(t, carry):
            row = rows[0, t]
            s = lax.rem(row // CHB - ids_ref[0] + n_col, n_col)
            position = slots[0, t] * CHB + lax.rem(row, CHB)
            n = counts[s]
            lists[s, n] = position * TILES_DEV + t
            counts[s] = n + 1
            return carry

        lax.fori_loop(0, live_ref[0], place, 0)

    acc[...] = jnp.zeros_like(acc)

    @pl.when(origin == 0)
    def _():
        for g in range(GROUPS):
            copy(g).wait()

    def add(n, carry):
        entry = lists[origin, n]
        position = entry // TILES_DEV
        slot = position // CHB
        at_row = pl.ds(pl.multiple_of(lax.rem(position, CHB) * TB, TB), TB)
        at_lane = pl.ds(pl.multiple_of(lax.rem(slot, 2) * TB, TB), TB)
        acc[slot // 2, at_row, at_lane] += tiles[lax.rem(entry, TILES_DEV)]
        return carry

    lax.fori_loop(0, counts[origin], add, 0)
    for p in range(acc.shape[0]):
        high, low = split(acc[p])
        out_ref[0, p, :NODES_DEV, :] = high
        out_ref[0, p, NODES_DEV:, :] = low


def build_operator(n_row, n_col, ids, live, rows, slots, values):
    part = (n_row // 2, 2 * NODES_DEV, WIDE)
    return pl.pallas_call(
        functools.partial(operator_kernel, n_col),
        grid=(n_col,),
        in_specs=[SMEM] * 2 + [HBM] * 3,
        out_specs=pl.BlockSpec((1,) + part, lambda s: (s, 0, 0, 0)),
        out_shape=pltpu.HBM((n_col,) + part, BF16),
        scratch_shapes=[
            pltpu.VMEM((TILES_DEV, TB, TB), F32),
            pltpu.VMEM((n_row // 2, NODES_DEV, WIDE), F32),
            pltpu.SMEM((n_col, TILES_DEV), jnp.int32),
            pltpu.SMEM((n_col,), jnp.int32),
            pltpu.SMEM((1, TILES_DEV), jnp.int32),
            pltpu.SMEM((1, TILES_DEV), jnp.int32),
            pltpu.SemaphoreType.DMA((GROUPS,)),
            pltpu.SemaphoreType.DMA((2,)),
        ],
        compiler_params=params(40),
        cost_estimate=LIGHT,
        name="operator",
    )(ids, live, *in_hbm(rows, slots, values))


def product_kernel(n_row, n_col, origins, has_prev, last, has_under, n_carriers, *refs):
    n = len(origins)
    ids_ref, op_ref, refs = refs[0], refs[1], refs[2:]
    fields, refs = refs[:n], refs[n:]
    if has_prev:
        prev, refs = refs[0], refs[1:]
    if has_under:
        under, refs = refs[0], refs[1:]
    carriers, refs = refs[:n_carriers], refs[n_carriers:]
    out_ref, buf, sems = refs[:3]

    def copy(k, p):
        return pltpu.make_async_copy(op_ref.at[origins[k], p], buf.at[k, p], sems.at[k, p])

    for p in range(n_row // 2):
        for k in range(n):
            copy(k, p).start()
    left = []
    for field in fields:
        high, low = split(field[:H, :])
        left.append(jnp.concatenate([jnp.concatenate([x, x], axis=1) for x in (high, low)], axis=0))
    if has_under:
        out_ref[:, H:, :] = under[...]
    if n_carriers:
        ordered = refs[3]
        for k in range(n_col):
            ordered[lax.rem(ids_ref[0] + k, n_col)] = carriers[k][H:, :]
        share = ordered[0]
        for k in range(1, n_col):
            share = share + ordered[k]
        rows = share.shape[0]
        for j in range(NODES_DEV // LANES):
            for q in range(n_row):
                out_ref[q, H + j * rows : H + (j + 1) * rows, :] = share[:, j * LANES : (j + 1) * LANES]
    for p in range(n_row // 2):
        here = slice(p * WIDE, (p + 1) * WIDE)
        total = None
        for k in range(n):
            copy(k, p).wait()
            part = jnp.dot(left[k], buf[k, p], preferred_element_type=F32)
            total = part if total is None else total + part
        summed = total[:H] + total[H:]
        if has_prev:
            summed = summed + prev[:, here]
        if last:
            out_ref[2 * p, :H, :] = summed[:, :TB]
            out_ref[2 * p + 1, :H, :] = summed[:, TB:]
        else:
            out_ref[:, here] = summed


def product(n_row, n_col, ids, origins, operator, fields, prev, last, under=None, carriers=()):
    n = len(origins)
    has_prev = prev is not None
    has_under = under is not None
    share = under.shape[1] if has_under else 0
    scratch = [
        pltpu.VMEM((n, n_row // 2, 2 * NODES_DEV, WIDE), BF16),
        pltpu.SemaphoreType.DMA((n, n_row // 2)),
    ]
    if carriers:
        rows = carriers[0].shape[0] - H
        share = rows * NODES_DEV // LANES
        scratch.append(pltpu.VMEM((n_col, rows, NODES_DEV), F32))
    shape = (n_row, H + share, TB) if last else (H, n_row * TB)
    count = n + has_prev + has_under + len(carriers)
    return pl.pallas_call(
        functools.partial(product_kernel, n_row, n_col, origins, has_prev, last, has_under, len(carriers)),
        in_specs=[SMEM, HBM] + [VMEM] * count,
        out_specs=VMEM,
        out_shape=jax.ShapeDtypeStruct(shape, F32),
        scratch_shapes=scratch,
        compiler_params=params(48),
        cost_estimate=LIGHT,
        name="product",
    )(
        ids,
        *in_hbm(operator),
        *fields,
        *((prev,) if has_prev else ()),
        *((under,) if has_under else ()),
        *carriers,
    )


def carry_kernel(n_row, rows, owners_ref, base_ref, came_ref, out_ref):
    out_ref[:H, :] = base_ref[...]
    for q in range(n_row):
        here = pl.ds(pl.multiple_of(owners_ref[q] * TB, TB), TB)
        out_ref[:H, here] += 2.0 * came_ref[q, :H, :]
    if rows:
        share = came_ref[0, H:, :]
        for q in range(1, n_row):
            share = share + came_ref[q, H:, :]
        for j in range(NODES_DEV // LANES):
            out_ref[H:, j * LANES : (j + 1) * LANES] = share[j * rows : (j + 1) * rows, :]


def carry(n_row, owners, base, came):
    rows = (came.shape[1] - H) * LANES // NODES_DEV
    return pl.pallas_call(
        functools.partial(carry_kernel, n_row, rows),
        in_specs=[SMEM, VMEM, VMEM],
        out_specs=VMEM,
        out_shape=jax.ShapeDtypeStruct((H + rows, NODES_DEV), F32),
        compiler_params=params(24),
        cost_estimate=LIGHT,
        name="carry",
    )(owners, base, came)


def finish_kernel(n_row, owners_ref, base_ref, left_ref, right_ref, out_ref, total):
    total[...] = base_ref[...]
    for h, came in enumerate((left_ref, right_ref)):
        for q in range(n_row):
            here = pl.ds(pl.multiple_of(owners_ref[q] * TB, TB), TB)
            total[h * H : (h + 1) * H, here] += came[q, :H, :]
    out_ref[...] = total[...].T


def finish(n_row, owners, base, left, right):
    return pl.pallas_call(
        functools.partial(finish_kernel, n_row),
        in_specs=[SMEM] + [VMEM] * 3,
        out_specs=VMEM,
        out_shape=jax.ShapeDtypeStruct((NODES_DEV, F), F32),
        scratch_shapes=[pltpu.VMEM((F, NODES_DEV), F32)],
        compiler_params=params(24),
        cost_estimate=LIGHT,
        name="finish",
    )(owners, base, left, right)


def assemble_kernel(n_row, came_ref, out_ref, turned):
    rows = F // n_row
    per = F // LANES
    for q in range(n_row):
        for j in range(3 * per):
            here = slice(H + j * rows, H + (j + 1) * rows)
            turned[q * rows : (q + 1) * rows, j * LANES : (j + 1) * LANES] = came_ref[q, here, :]
    for k in range(3):
        out_ref[k] = turned[:, k * F : (k + 1) * F].T


def assemble(n_row, came):
    return pl.pallas_call(
        functools.partial(assemble_kernel, n_row),
        in_specs=[VMEM],
        out_specs=VMEM,
        out_shape=jax.ShapeDtypeStruct((3, F, F), F32),
        scratch_shapes=[pltpu.VMEM((F, 3 * F), F32)],
        compiler_params=params(16),
        cost_estimate=LIGHT,
        name="assemble",
    )(came)


def shift(n_col, x, step):
    return lax.ppermute(x, "col", [(c, (c + step) % n_col) for c in range(n_col)])


def exchange(pieces):
    return lax.all_to_all(pieces, "row", split_axis=0, concat_axis=0, tiled=True)


def after(x, *others):
    return lax.optimization_barrier((x, *others))[0]


def gather(n_col, field, side, *done):
    long = n_col // 2
    short = n_col - 1 - long
    ahead, behind = field, field
    steps = [[(0, field)]]
    for s in range(1, long + 1):
        if s == 2:
            ahead = after(ahead, behind, *done)
        ahead = shift(n_col, ahead, side)
        step = [((-side * s) % n_col, ahead)]
        if s <= short:
            behind = shift(n_col, behind, -side)
            step.append(((side * s) % n_col, behind))
        steps.append(step)
    return steps


def early(n_row, n_col, ids, operator, steps):
    pairs = [pair for step in steps[:-1] for pair in step]
    total = None
    for begin in range(0, len(pairs), 3):
        origins, fields = zip(*pairs[begin : begin + 3])
        total = product(n_row, n_col, ids, origins, operator, fields, total, False)
    return total


def final(n_row, n_col, ids, operator, steps, total, under=None, carrying=False):
    origins, fields = zip(*steps[-1])
    carriers = [x for _, x in sorted((p for step in steps for p in step), key=lambda p: p[0])] if carrying else ()
    return product(n_row, n_col, ids, origins, operator, fields, total, True, under, carriers)


def per_device(
    grad_out,
    relu_mask,
    basis_zero,
    basis_one,
    basis_two,
    cheb_weight,
    tile_values,
    tile_rows,
    tile_slots,
    send_blocks,
    live_tiles,
):
    n_row = lax.axis_size("row")
    n_col = lax.axis_size("col")
    ids = lax.axis_index("col").astype(jnp.int32).reshape(1)
    owners = send_blocks.reshape(n_row)
    left, right = term_two(grad_out, relu_mask, cheb_weight)
    one_left, one_right, diff, pieces = local_terms(
        n_row, left, grad_out, relu_mask, cheb_weight, basis_zero, basis_one, basis_two
    )
    operator = build_operator(n_row, n_col, ids, live_tiles, tile_rows, tile_slots, tile_values)
    common = (n_row, n_col, ids, operator)

    steps = gather(n_col, left, 1, operator, pieces)
    left_early = early(*common, steps)
    right_steps = gather(n_col, after(right, left_early, steps[-1][0][1]), -1)
    left_came = exchange(final(*common, steps, left_early, under=pieces))
    right_early = early(*common, right_steps)

    left_carried = carry(n_row, owners, after(one_left, right_early, right_steps[-1][0][1]), left_came)
    steps = gather(n_col, left_carried, 1)
    right_came = exchange(final(*common, right_steps, right_early))
    left_early = early(*common, steps)

    right_carried = carry(n_row, owners, after(one_right, left_early, steps[-1][0][1]), right_came)
    right_steps = gather(n_col, right_carried, -1)
    left_came = exchange(final(*common, steps, left_early, carrying=True))
    right_early = early(*common, right_steps)

    right_came = exchange(final(*common, right_steps, right_early))
    weight_grad = assemble(n_row, left_came)
    return finish(n_row, owners, diff, left_came, right_came), weight_grad


def solution(mesh):
    placed = (
        P(("row", "col"), None),
        P(("row", "col"), None),
        P(("row", "col"), None),
        P(("row", "col"), None),
        P(("row", "col"), None),
        P(),
        P(("row", "col"), None, None, None),
        P(("row", "col"), None),
        P(("row", "col"), None),
        P(("row", "col"), None, None),
        P(("row", "col")),
    )
    return jax.shard_map(
        per_device,
        mesh=mesh,
        in_specs=placed,
        out_specs=(P(("row", "col"), None), P()),
        check_vma=False,
    )
```

time: 154 us -> 140 us (0.909)
  starting transfers between devices: 45.9 us -> 37.4 us
  Pallas kernels: 62.7 us -> 56.2 us
  waiting for transfers between devices: 41.9 us -> 44.7 us
    all_to_all x5 -> x4, starting transfers between devices: 21.8 us -> 14.6 us  [exchange(): lax.all_to_all(pieces, 'row', split_axis=0, concat_axis=0, tiled=True)]
    pallas_call x12 -> x8, Pallas kernels: 42.2 us -> 36.4 us  [product(): pl.pallas_call(functools.partial(product_kernel, n_row, n_col, origins, h...]
    ppermute x12, waiting for transfers between devices: 33.1 us -> 36.1 us  [shift(): lax.ppermute(x, 'col', [(c, (c + step) % n_col) for c in range(n_col)])]
    all_to_all x5 -> x4, waiting for transfers between devices: 8.75 us -> 8.6 us  [exchange(): lax.all_to_all(pieces, 'row', split_axis=0, concat_axis=0, tiled=True)]
  transfers between devices with their start and end apart: 17 -> 16, of which waited for: 8 -> 11; matrix products, arithmetic and copies ran while one was open for 1% -> 0% of each run, Pallas kernels for 36% -> 34%
where the time goes in v5:
time: 140 us
  Pallas kernels  56.2 us (40%)
  waiting for transfers between devices  44.7 us (32%)
  starting transfers between devices  37.4 us (27%)
  between operations  1.46 us (1%)
    pallas_call x8, Pallas kernels, product(): pl.pallas_call(functools.partial(product_kernel, n_row, n_col, origins, h...  36.4 us
    ppermute x12, waiting for transfers between devices, shift(): lax.ppermute(x, 'col', [(c, (c + step) % n_col) for c in range(n_col)])  36.1 us
    ppermute x12, starting transfers between devices, shift(): lax.ppermute(x, 'col', [(c, (c + step) % n_col) for c in range(n_col)])  22.8 us
    all_to_all x4, starting transfers between devices, exchange(): lax.all_to_all(pieces, 'row', split_axis=0, concat_axis=0, tiled=True)  14.6 us
    pallas_call x1, Pallas kernels, build_operator(): pl.pallas_call(functools.partial(operator_kernel, n_col), grid=(n_col,),...  9.83 us
    all_to_all x4, waiting for transfers between devices, exchange(): lax.all_to_all(pieces, 'row', split_axis=0, concat_axis=0, tiled=True)  8.6 us
    pallas_call x1, Pallas kernels, local_terms(): pl.pallas_call(functools.partial(local_kernel, n_row), in_specs=[pl.Block...  3.98 us
  transfers between devices with their start and end apart: 16, of which 11 were waited for; matrix products, arithmetic and copies ran while one was open for 0% of the time, Pallas kernels for 34%

profile of v5, /device:TPU:0, one launch (start us, length us, event | category | flops | bytes accessed | tf_op | source)
XLA Modules:
  0.0 139.8 jit_solution(7755070181111177713)
XLA Ops:
  0.6 1.7 %term_two.1 = (f32[128,512]{1,0:T(8,128)S(1)}, f32[128,512]{1,0:T(8,128)S(1)}) custom-call(f32[512,256]{1,0:T(8,128)} %grad_hbm.3, s32[512,256]{1,0:T(8,128)} %mask_hbm.3, f32[3,256,256]{2,1,0:T(8,128)} %weight_hbm.3), custom_call_target="tpu_custom_call" | custom-call | flops 1024 | bytes 1024 | tf_op jit(solution)/shard_map/term_two/pallas_call | solution.py:74
  2.4 5.1 %collective-permute-start.1 = (f32[128,512]{1,0:T(8,128)S(1)}, f32[128,512]{1,0:T(8,128)S(1)}, u32[]{:S(2)}, u32[]{:S(2)}) collective-permute-start(f32[128,512]{1,0:T(8,128)S(1)} %get-tuple-element.15.first_ref.refs_2_), channel_id=1, source_target_pairs={{0,3},{1,0},{2,1},{3,2},{4,7},{5,4},{6,5},{7,6},{8,11},{9,8},{10,9... | collective-permute-start | bytes 786440 | tf_op jit(solution)/shard_map/ppermute | solution.py:379
  7.5 0.0 collective-permute-start
  7.5 4.0 %local_terms.1 = (f32[128,512]{1,0:T(8,128)S(1)}, f32[128,512]{1,0:T(8,128)S(1)}, f32[256,512]{1,0:T(8,128)S(1)}, f32[8,192,128]{2,1,0:T(8,128)S(1)}) custom-call(f32[128,512]{1,0:T(8,128)S(1)} %get-tuple-element.15.first_ref.refs_2_, f32[512,256]{1,0:T(8,128)} %grad_hbm.3, s32[512,256]{1,0:T(8,128)} %mask_hbm.3, f32[3,256,256]{2,1,0:T(8,128)} %weight_hbm.3, ...), custom_call_target="tpu_custom_call" | custom-call | flops 1024 | bytes 1024 | tf_op jit(solution)/shard_map/local_terms/pallas_call | solution.py:119
  12.1 9.8 %operator.1.refs_1_ = bf16[4,4,1024,256]{3,2,1,0:T(8,128)(2,1)} custom-call(s32[1]{0:T(128)} %bitcast.1.ids_ref.refs_0_, s32[1]{0:T(128)S(6)} %copy.13.live_ref, s32[1,128]{1,0:T(1,128)} %rows_hbm.1, s32[1,128]{1,0:T(1,128)} %slots_hbm.1, f32[1,128,128,128]{3,2,1,0:T(8,128)} %values_ref.1), custom_call_target="tpu_custom_call" | custom-call | flops 1024 | bytes 1024 | tf_op jit(solution)/shard_map/operator/pallas_call | solution.py:199
  22.0 0.0 collective-permute-done.1.refs_4_
  22.0 0.0 collective-permute-done.refs_3_
  22.0 0.1 collective-permute-start.2
  22.1 5.4 %product.8.refs_3_ = f32[128,1024]{1,0:T(8,128)S(1)} custom-call(s32[1]{0:T(128)} %bitcast.1.ids_ref.refs_0_, bf16[4,4,1024,256]{3,2,1,0:T(8,128)(2,1)} %operator.1.refs_1_, f32[128,512]{1,0:T(8,128)S(1)} %get-tuple-element.15.first_ref.refs_2_, f32[128,512]{1,0:T(8,128)S(1)} %collective-permute-done.refs_3_, f32[128,512]{1,0:T(8,128)S(1)} %collective-permute-done.1.refs_4_), custom_call_target="tpu_custom_call" | custom-call | flops 1024 | bytes 1024 | tf_op jit(solution)/shard_map/product/pallas_call | solution.py:287
  27.4 2.8 %collective-permute-done.2.refs_2_ = f32[128,512]{1,0:T(8,128)S(1)} collective-permute-done((f32[128,512]{1,0:T(8,128)S(1)}, f32[128,512]{1,0:T(8,128)S(1)}, u32[]{:S(2)}, u32[]{:S(2)}) %collective-permute-start.2) | collective-permute-done | bytes 262176 | tf_op jit(solution)/shard_map/ppermute | solution.py:379
  30.2 3.9 %product.10 = f32[8,320,128]{2,1,0:T(8,128)} custom-call(s32[1]{0:T(128)} %bitcast.1.ids_ref.refs_0_, bf16[4,4,1024,256]{3,2,1,0:T(8,128)(2,1)} %operator.1.refs_1_, f32[128,512]{1,0:T(8,128)S(1)} %collective-permute-done.2.refs_2_, f32[128,1024]{1,0:T(8,128)S(1)} %product.8.refs_3_, f32[8,192,128]{2,1,0:T(8,128)S(1)} %get-tuple-element.19.refs_4_), custom_call_target="tpu_custom_call" | custom-call | flops 1024 | bytes 1024 | tf_op jit(solution)/shard_map/product/pallas_call | solution.py:287
  34.1 3.9 %all-to-all-start = ((f32[8,320,128]{2,1,0:T(8,128)}), f32[8,320,128]{2,1,0:T(8,128)S(1)}, u32[]{:S(2)}, u32[]{:S(2)}) async-start(f32[8,320,128]{2,1,0:T(8,128)} %product.10), calls=%async_computation | async-start | bytes 2621440 | tf_op jit(solution)/shard_map/all_to_all | solution.py:383
  38.0 0.0 copy-start
  38.0 0.1 collective-permute-start.4
  38.0 3.8 %collective-permute-start.3 = (f32[128,512]{1,0:T(8,128)S(1)}, f32[128,512]{1,0:T(8,128)S(1)}, u32[]{:S(2)}, u32[]{:S(2)}) collective-permute-start(f32[128,512]{1,0:T(8,128)S(1)} %get-tuple-element.21.refs_2_), channel_id=1, source_target_pairs={{0,3},{1,0},{2,1},{3,2},{4,7},{5,4},{6,5},{7,6},{8,11},{9,8},{10,9... | collective-permute-start | bytes 786440 | tf_op jit(solution)/shard_map/ppermute | solution.py:379
  41.9 7.1 %collective-permute-done.4.refs_4_ = f32[128,512]{1,0:T(8,128)S(1)} collective-permute-done((f32[128,512]{1,0:T(8,128)S(1)}, f32[128,512]{1,0:T(8,128)S(1)}, u32[]{:S(2)}, u32[]{:S(2)}) %collective-permute-start.4) | collective-permute-done | bytes 262176 | tf_op jit(solution)/shard_map/ppermute | solution.py:379
  49.0 3.4 %collective-permute-done.3.refs_3_ = f32[128,512]{1,0:T(8,128)S(1)} collective-permute-done((f32[128,512]{1,0:T(8,128)S(1)}, f32[128,512]{1,0:T(8,128)S(1)}, u32[]{:S(2)}, u32[]{:S(2)}) %collective-permute-start.3) | collective-permute-done | bytes 262176 | tf_op jit(solution)/shard_map/ppermute | solution.py:379
  52.4 2.0 %collective-permute-start.5 = (f32[128,512]{1,0:T(8,128)S(1)}, f32[128,512]{1,0:T(8,128)S(1)}, u32[]{:S(2)}, u32[]{:S(2)}) collective-permute-start(f32[128,512]{1,0:T(8,128)S(1)} %collective-permute-done.3.refs_3_), channel_id=1, source_target_pairs={{0,3},{1,0},{2,1},{3,2},{4,7},{5,4},{6,5},{7,6},{8,11},{9,8},{10,9... | collective-permute-start | bytes 786440 | tf_op jit(solution)/shard_map/ppermute | solution.py:379
  54.4 5.4 %product.9.refs_3_ = f32[128,1024]{1,0:T(8,128)S(1)} custom-call(s32[1]{0:T(128)} %bitcast.1.ids_ref.refs_0_, bf16[4,4,1024,256]{3,2,1,0:T(8,128)(2,1)} %operator.1.refs_1_, f32[128,512]{1,0:T(8,128)S(1)} %get-tuple-element.21.refs_2_, f32[128,512]{1,0:T(8,128)S(1)} %collective-permute-done.3.refs_3_, f32[128,512]{1,0:T(8,128)S(1)} %collective-permute-done.4.refs_4_), custom_call_target="tpu_custom_call" | custom-call | flops 1024 | bytes 1024 | tf_op jit(solution)/shard_map/product/pallas_call | solution.py:287
  59.8 0.5 collective-permute-done.5.refs_2_
  60.2 0.0 all-to-all-done.came_ref
  60.2 0.0 copy-done
  60.2 0.7 carry.2.refs_2_.refs_4_
  60.9 4.1 %collective-permute-start.7 = (f32[176,512]{1,0:T(8,128)S(1)}, f32[176,512]{1,0:T(8,128)S(1)}, u32[]{:S(2)}, u32[]{:S(2)}) collective-permute-start(f32[176,512]{1,0:T(8,128)S(1)} %carry.2.refs_2_.refs_4_), channel_id=1, source_target_pairs={{0,3},{1,0},{2,1},{3,2},{4,7},{5,4},{6,5},{7,6},{8,11},{9,8},{10,9... | collective-permute-start | bytes 1081352 | tf_op jit(solution)/shard_map/ppermute | solution.py:379
  65.0 0.0 collective-permute-start.6
  65.0 3.6 %product.13 = f32[8,128,128]{2,1,0:T(8,128)} custom-call(s32[1]{0:T(128)} %bitcast.1.ids_ref.refs_0_, bf16[4,4,1024,256]{3,2,1,0:T(8,128)(2,1)} %operator.1.refs_1_, f32[128,512]{1,0:T(8,128)S(1)} %collective-permute-done.5.refs_2_, f32[128,1024]{1,0:T(8,128)S(1)} %product.9.refs_3_), custom_call_target="tpu_custom_call" | custom-call | flops 1024 | bytes 1024 | tf_op jit(solution)/shard_map/product/pallas_call | solution.py:287
  68.6 3.6 %all-to-all-start.2 = ((f32[8,128,128]{2,1,0:T(8,128)}), f32[8,128,128]{2,1,0:T(8,128)S(1)}, u32[]{:S(2)}, u32[]{:S(2)}) async-start(f32[8,128,128]{2,1,0:T(8,128)} %product.13), calls=%async_computation.2 | async-start | bytes 1048576 | tf_op jit(solution)/shard_map/all_to_all | solution.py:383
  72.2 1.7 %collective-permute-done.7.refs_4_.refs_5_ = f32[176,512]{1,0:T(8,128)S(1)} collective-permute-done((f32[176,512]{1,0:T(8,128)S(1)}, f32[176,512]{1,0:T(8,128)S(1)}, u32[]{:S(2)}, u32[]{:S(2)}) %collective-permute-start.7) | collective-permute-done | bytes 360480 | tf_op jit(solution)/shard_map/ppermute | solution.py:379
  73.9 6.4 %collective-permute-done.6.refs_3_.refs_7_ = f32[176,512]{1,0:T(8,128)S(1)} collective-permute-done((f32[176,512]{1,0:T(8,128)S(1)}, f32[176,512]{1,0:T(8,128)S(1)}, u32[]{:S(2)}, u32[]{:S(2)}) %collective-permute-start.6) | collective-permute-done | bytes 360480 | tf_op jit(solution)/shard_map/ppermute | solution.py:379
  80.3 1.8 %collective-permute-start.8 = (f32[176,512]{1,0:T(8,128)S(1)}, f32[176,512]{1,0:T(8,128)S(1)}, u32[]{:S(2)}, u32[]{:S(2)}) collective-permute-start(f32[176,512]{1,0:T(8,128)S(1)} %collective-permute-done.6.refs_3_.refs_7_), channel_id=1, source_target_pairs={{0,1},{1,2},{2,3},{3,0},{4,5},{5,6},{6,7},{7,4},{8,9},{9,10},{10,1... | collective-permute-start | bytes 1081352 | tf_op jit(solution)/shard_map/ppermute | solution.py:379
  82.1 5.4 %product.11.refs_3_ = f32[128,1024]{1,0:T(8,128)S(1)} custom-call(s32[1]{0:T(128)} %bitcast.1.ids_ref.refs_0_, bf16[4,4,1024,256]{3,2,1,0:T(8,128)(2,1)} %operator.1.refs_1_, f32[176,512]{1,0:T(8,128)S(1)} %carry.2.refs_2_.refs_4_, f32[176,512]{1,0:T(8,128)S(1)} %collective-permute-done.6.refs_3_.refs_7_, f32[176,512]{1,0:T(8,128)S(1)} %collective-permute-done.7.refs_4_.refs_5_), custom_call_target="tpu_custom_call" | custom-call | flops 1024 | bytes 1024 | tf_op jit(solution)/shard_map/product/pallas_call | solution.py:287
  87.5 3.3 %collective-permute-done.8.refs_2_.refs_6_ = f32[176,512]{1,0:T(8,128)S(1)} collective-permute-done((f32[176,512]{1,0:T(8,128)S(1)}, f32[176,512]{1,0:T(8,128)S(1)}, u32[]{:S(2)}, u32[]{:S(2)}) %collective-permute-start.8) | collective-permute-done | bytes 360480 | tf_op jit(solution)/shard_map/ppermute | solution.py:379
  90.8 3.9 %product.12 = f32[8,320,128]{2,1,0:T(8,128)} custom-call(s32[1]{0:T(128)} %bitcast.1.ids_ref.refs_0_, bf16[4,4,1024,256]{3,2,1,0:T(8,128)(2,1)} %operator.1.refs_1_, f32[176,512]{1,0:T(8,128)S(1)} %collective-permute-done.8.refs_2_.refs_6_, f32[128,1024]{1,0:T(8,128)S(1)} %product.11.refs_3_, f32[176,512]{1,0:T(8,128)S(1)} %carry.2.refs_2_.refs_4_, ...), custom_call_target="tpu_custom_call" | custom-call | flops 1024 | bytes 1024 | tf_op jit(solution)/shard_map/product/pallas_call | solution.py:287
  94.7 0.0 all-to-all-done.2.came_ref
  94.7 3.6 %all-to-all-start.1 = ((f32[8,320,128]{2,1,0:T(8,128)}), f32[8,320,128]{2,1,0:T(8,128)S(1)}, u32[]{:S(2)}, u32[]{:S(2)}) async-start(f32[8,320,128]{2,1,0:T(8,128)} %product.12), calls=%async_computation.1 | async-start | bytes 2621440 | tf_op jit(solution)/shard_map/all_to_all | solution.py:383
  98.3 0.7 carry.3.refs_2_
  99.0 0.1 collective-permute-start.10
  99.0 3.8 %collective-permute-start.9 = (f32[128,512]{1,0:T(8,128)S(1)}, f32[128,512]{1,0:T(8,128)S(1)}, u32[]{:S(2)}, u32[]{:S(2)}) collective-permute-start(f32[128,512]{1,0:T(8,128)S(1)} %carry.3.refs_2_), channel_id=1, source_target_pairs={{0,3},{1,0},{2,1},{3,2},{4,7},{5,4},{6,5},{7,6},{8,11},{9,8},{10,9... | collective-permute-start | bytes 786440 | tf_op jit(solution)/shard_map/ppermute | solution.py:379
  102.8 7.1 %collective-permute-done.10.refs_4_ = f32[128,512]{1,0:T(8,128)S(1)} collective-permute-done((f32[128,512]{1,0:T(8,128)S(1)}, f32[128,512]{1,0:T(8,128)S(1)}, u32[]{:S(2)}, u32[]{:S(2)}) %collective-permute-start.10) | collective-permute-done | bytes 262176 | tf_op jit(solution)/shard_map/ppermute | solution.py:379
  110.0 3.4 %collective-permute-done.9.refs_3_ = f32[128,512]{1,0:T(8,128)S(1)} collective-permute-done((f32[128,512]{1,0:T(8,128)S(1)}, f32[128,512]{1,0:T(8,128)S(1)}, u32[]{:S(2)}, u32[]{:S(2)}) %collective-permute-start.9) | collective-permute-done | bytes 262176 | tf_op jit(solution)/shard_map/ppermute | solution.py:379
  113.3 2.0 %collective-permute-start.11 = (f32[128,512]{1,0:T(8,128)S(1)}, f32[128,512]{1,0:T(8,128)S(1)}, u32[]{:S(2)}, u32[]{:S(2)}) collective-permute-start(f32[128,512]{1,0:T(8,128)S(1)} %collective-permute-done.9.refs_3_), channel_id=1, source_target_pairs={{0,3},{1,0},{2,1},{3,2},{4,7},{5,4},{6,5},{7,6},{8,11},{9,8},{10,9... | collective-permute-start | bytes 786440 | tf_op jit(solution)/shard_map/ppermute | solution.py:379
  115.3 5.4 %product.14.refs_3_ = f32[128,1024]{1,0:T(8,128)S(1)} custom-call(s32[1]{0:T(128)} %bitcast.1.ids_ref.refs_0_, bf16[4,4,1024,256]{3,2,1,0:T(8,128)(2,1)} %operator.1.refs_1_, f32[128,512]{1,0:T(8,128)S(1)} %carry.3.refs_2_, f32[128,512]{1,0:T(8,128)S(1)} %collective-permute-done.9.refs_3_, f32[128,512]{1,0:T(8,128)S(1)} %collective-permute-done.10.refs_4_), custom_call_target="tpu_custom_call" | custom-call | flops 1024 | bytes 1024 | tf_op jit(solution)/shard_map/product/pallas_call | solution.py:287
  120.7 0.5 collective-permute-done.11.refs_2_
  121.2 3.6 %product.15 = f32[8,128,128]{2,1,0:T(8,128)} custom-call(s32[1]{0:T(128)} %bitcast.1.ids_ref.refs_0_, bf16[4,4,1024,256]{3,2,1,0:T(8,128)(2,1)} %operator.1.refs_1_, f32[128,512]{1,0:T(8,128)S(1)} %collective-permute-done.11.refs_2_, f32[128,1024]{1,0:T(8,128)S(1)} %product.14.refs_3_), custom_call_target="tpu_custom_call" | custom-call | flops 1024 | bytes 1024 | tf_op jit(solution)/shard_map/product/pallas_call | solution.py:287
  124.7 0.0 all-to-all-done.1.left_ref.came_ref
  124.7 3.5 %all-to-all-start.3 = ((f32[8,128,128]{2,1,0:T(8,128)}), f32[8,128,128]{2,1,0:T(8,128)S(1)}, u32[]{:S(2)}, u32[]{:S(2)}) async-start(f32[8,128,128]{2,1,0:T(8,128)} %product.15), calls=%async_computation.3 | async-start | bytes 1048576 | tf_op jit(solution)/shard_map/all_to_all | solution.py:383
  128.3 1.1 assemble.1
  129.4 8.6 %all-to-all-done.3.right_ref = f32[8,128,128]{2,1,0:T(8,128)S(1)} async-done(((f32[8,128,128]{2,1,0:T(8,128)}), f32[8,128,128]{2,1,0:T(8,128)S(1)}, u32[]{:S(2)}, u32[]{:S(2)}) %all-to-all-start.3) | async-done | bytes 524320 | tf_op jit(solution)/shard_map/all_to_all | solution.py:383
  138.0 1.8 %finish.1 = f32[512,256]{1,0:T(8,128)} custom-call(s32[8]{0:T(128)S(1)} %bitcast.4, f32[256,512]{1,0:T(8,128)S(1)} %get-tuple-element.16.base_ref, f32[8,320,128]{2,1,0:T(8,128)S(1)} %all-to-all-done.1.left_ref.came_ref, f32[8,128,128]{2,1,0:T(8,128)S(1)} %all-to-all-done.3.right_ref), custom_call_target="tpu_custom_call" | custom-call | flops 1024 | bytes 1024 | tf_op jit(solution)/shard_map/finish/pallas_call | solution.py:342
Async XLA Ops:
  2.4 19.6 %collective-permute-start.1 = (f32[128,512]{1,0:T(8,128)S(1)}, f32[128,512]{1,0:T(8,128)S(1)}, u32[]{:S(2)}, u32[]{:S(2)}) collective-permute-start(f32[128,512]{1,0:T(8,128)S(1)} %get-tuple-element.15.first_ref.refs_2_), channel_id=1, source_target_pairs={{0,3},{1,0},{2,1},{3,2},{4,7},{5,4},{6,5},{7,6},{8,11},{9,8},{10,9... | collective-permute-start | bytes 786440 | tf_op jit(solution)/shard_map/ppermute | solution.py:379
  7.5 14.5 %collective-permute-start = (f32[128,512]{1,0:T(8,128)S(1)}, f32[128,512]{1,0:T(8,128)S(1)}, u32[]{:S(2)}, u32[]{:S(2)}) collective-permute-start(f32[128,512]{1,0:T(8,128)S(1)} %get-tuple-element.15.first_ref.refs_2_), channel_id=1, source_target_pairs={{0,1},{1,2},{2,3},{3,0},{4,5},{5,6},{6,7},{7,4},{8,9},{9,10},{10,1... | collective-permute-start | bytes 786440 | tf_op jit(solution)/shard_map/ppermute | solution.py:379
  22.0 8.2 %collective-permute-start.2 = (f32[128,512]{1,0:T(8,128)S(1)}, f32[128,512]{1,0:T(8,128)S(1)}, u32[]{:S(2)}, u32[]{:S(2)}) collective-permute-start(f32[128,512]{1,0:T(8,128)S(1)} %collective-permute-done.refs_3_), channel_id=1, source_target_pairs={{0,1},{1,2},{2,3},{3,0},{4,5},{5,6},{6,7},{7,4},{8,9},{9,10},{10,1... | collective-permute-start | bytes 786440 | tf_op jit(solution)/shard_map/ppermute | solution.py:379
  34.1 26.1 %all-to-all-start = ((f32[8,320,128]{2,1,0:T(8,128)}), f32[8,320,128]{2,1,0:T(8,128)S(1)}, u32[]{:S(2)}, u32[]{:S(2)}) async-start(f32[8,320,128]{2,1,0:T(8,128)} %product.10), calls=%async_computation | async-start | bytes 2621440 | tf_op jit(solution)/shard_map/all_to_all | solution.py:383
  38.0 22.3 %copy-start = (s32[1,8,1]{1,2,0:T(1,128)S(1)}, s32[1,8,1]{1,2,0:T(1,128)}, u32[]{:S(2)}) copy-start(s32[1,8,1]{1,2,0:T(1,128)} %param.20) | copy-start | bytes 100
  38.0 11.0 %collective-permute-start.4 = (f32[128,512]{1,0:T(8,128)S(1)}, f32[128,512]{1,0:T(8,128)S(1)}, u32[]{:S(2)}, u32[]{:S(2)}) collective-permute-start(f32[128,512]{1,0:T(8,128)S(1)} %get-tuple-element.21.refs_2_), channel_id=1, source_target_pairs={{0,1},{1,2},{2,3},{3,0},{4,5},{5,6},{6,7},{7,4},{8,9},{9,10},{10,1... | collective-permute-start | bytes 786440 | tf_op jit(solution)/shard_map/ppermute | solution.py:379
  38.0 14.3 %collective-permute-start.3 = (f32[128,512]{1,0:T(8,128)S(1)}, f32[128,512]{1,0:T(8,128)S(1)}, u32[]{:S(2)}, u32[]{:S(2)}) collective-permute-start(f32[128,512]{1,0:T(8,128)S(1)} %get-tuple-element.21.refs_2_), channel_id=1, source_target_pairs={{0,3},{1,0},{2,1},{3,2},{4,7},{5,4},{6,5},{7,6},{8,11},{9,8},{10,9... | collective-permute-start | bytes 786440 | tf_op jit(solution)/shard_map/ppermute | solution.py:379
  52.4 7.9 %collective-permute-start.5 = (f32[128,512]{1,0:T(8,128)S(1)}, f32[128,512]{1,0:T(8,128)S(1)}, u32[]{:S(2)}, u32[]{:S(2)}) collective-permute-start(f32[128,512]{1,0:T(8,128)S(1)} %collective-permute-done.3.refs_3_), channel_id=1, source_target_pairs={{0,3},{1,0},{2,1},{3,2},{4,7},{5,4},{6,5},{7,6},{8,11},{9,8},{10,9... | collective-permute-start | bytes 786440 | tf_op jit(solution)/shard_map/ppermute | solution.py:379
  60.9 13.0 %collective-permute-start.7 = (f32[176,512]{1,0:T(8,128)S(1)}, f32[176,512]{1,0:T(8,128)S(1)}, u32[]{:S(2)}, u32[]{:S(2)}) collective-permute-start(f32[176,512]{1,0:T(8,128)S(1)} %carry.2.refs_2_.refs_4_), channel_id=1, source_target_pairs={{0,3},{1,0},{2,1},{3,2},{4,7},{5,4},{6,5},{7,6},{8,11},{9,8},{10,9... | collective-permute-start | bytes 1081352 | tf_op jit(solution)/shard_map/ppermute | solution.py:379
  65.0 15.3 %collective-permute-start.6 = (f32[176,512]{1,0:T(8,128)S(1)}, f32[176,512]{1,0:T(8,128)S(1)}, u32[]{:S(2)}, u32[]{:S(2)}) collective-permute-start(f32[176,512]{1,0:T(8,128)S(1)} %carry.2.refs_2_.refs_4_), channel_id=1, source_target_pairs={{0,1},{1,2},{2,3},{3,0},{4,5},{5,6},{6,7},{7,4},{8,9},{9,10},{10,1... | collective-permute-start | bytes 1081352 | tf_op jit(solution)/shard_map/ppermute | solution.py:379
  68.6 26.1 %all-to-all-start.2 = ((f32[8,128,128]{2,1,0:T(8,128)}), f32[8,128,128]{2,1,0:T(8,128)S(1)}, u32[]{:S(2)}, u32[]{:S(2)}) async-start(f32[8,128,128]{2,1,0:T(8,128)} %product.13), calls=%async_computation.2 | async-start | bytes 1048576 | tf_op jit(solution)/shard_map/all_to_all | solution.py:383
  80.3 10.5 %collective-permute-start.8 = (f32[176,512]{1,0:T(8,128)S(1)}, f32[176,512]{1,0:T(8,128)S(1)}, u32[]{:S(2)}, u32[]{:S(2)}) collective-permute-start(f32[176,512]{1,0:T(8,128)S(1)} %collective-permute-done.6.refs_3_.refs_7_), channel_id=1, source_target_pairs={{0,1},{1,2},{2,3},{3,0},{4,5},{5,6},{6,7},{7,4},{8,9},{9,10},{10,1... | collective-permute-start | bytes 1081352 | tf_op jit(solution)/shard_map/ppermute | solution.py:379
  94.7 30.0 %all-to-all-start.1 = ((f32[8,320,128]{2,1,0:T(8,128)}), f32[8,320,128]{2,1,0:T(8,128)S(1)}, u32[]{:S(2)}, u32[]{:S(2)}) async-start(f32[8,320,128]{2,1,0:T(8,128)} %product.12), calls=%async_computation.1 | async-start | bytes 2621440 | tf_op jit(solution)/shard_map/all_to_all | solution.py:383
  99.0 11.0 %collective-permute-start.10 = (f32[128,512]{1,0:T(8,128)S(1)}, f32[128,512]{1,0:T(8,128)S(1)}, u32[]{:S(2)}, u32[]{:S(2)}) collective-permute-start(f32[128,512]{1,0:T(8,128)S(1)} %carry.3.refs_2_), channel_id=1, source_target_pairs={{0,1},{1,2},{2,3},{3,0},{4,5},{5,6},{6,7},{7,4},{8,9},{9,10},{10,1... | collective-permute-start | bytes 786440 | tf_op jit(solution)/shard_map/ppermute | solution.py:379
  99.0 14.3 %collective-permute-start.9 = (f32[128,512]{1,0:T(8,128)S(1)}, f32[128,512]{1,0:T(8,128)S(1)}, u32[]{:S(2)}, u32[]{:S(2)}) collective-permute-start(f32[128,512]{1,0:T(8,128)S(1)} %carry.3.refs_2_), channel_id=1, source_target_pairs={{0,3},{1,0},{2,1},{3,2},{4,7},{5,4},{6,5},{7,6},{8,11},{9,8},{10,9... | collective-permute-start | bytes 786440 | tf_op jit(solution)/shard_map/ppermute | solution.py:379
  113.3 7.8 %collective-permute-start.11 = (f32[128,512]{1,0:T(8,128)S(1)}, f32[128,512]{1,0:T(8,128)S(1)}, u32[]{:S(2)}, u32[]{:S(2)}) collective-permute-start(f32[128,512]{1,0:T(8,128)S(1)} %collective-permute-done.9.refs_3_), channel_id=1, source_target_pairs={{0,3},{1,0},{2,1},{3,2},{4,7},{5,4},{6,5},{7,6},{8,11},{9,8},{10,9... | collective-permute-start | bytes 786440 | tf_op jit(solution)/shard_map/ppermute | solution.py:379
  124.7 13.3 %all-to-all-start.3 = ((f32[8,128,128]{2,1,0:T(8,128)}), f32[8,128,128]{2,1,0:T(8,128)S(1)}, u32[]{:S(2)}, u32[]{:S(2)}) async-start(f32[8,128,128]{2,1,0:T(8,128)} %product.15), calls=%async_computation.3 | async-start | bytes 1048576 | tf_op jit(solution)/shard_map/all_to_all | solution.py:383

commit v6 on v5

--- a/solution.py
+++ b/solution.py
@@ -17,6 +17,7 @@
 TILES_DEV = 128
 GROUPS = 8
 MIB = 1 << 20
+HEAVY = pl.CostEstimate(flops=1 << 34, bytes_accessed=64 * MIB, transcendentals=0)
 LIGHT = pl.CostEstimate(flops=1024, bytes_accessed=1024, transcendentals=0)
 BF16 = jnp.bfloat16
 F32 = jnp.float32
@@ -291,7 +292,7 @@
         out_shape=jax.ShapeDtypeStruct(shape, F32),
         scratch_shapes=scratch,
         compiler_params=params(48),
-        cost_estimate=LIGHT,
+        cost_estimate=LIGHT if last else HEAVY,
         name="product",
     )(
         ids,

time: 140 us -> 136 us (0.971)
  starting transfers between devices: 37.4 us -> 33 us
  local copies, waits for them, and re-layouts: 0.01 us -> 2.35 us
  waiting for transfers between devices: 44.7 us -> 42.5 us
    ppermute x12, waiting for transfers between devices: 36.1 us -> 19.7 us  [shift(): lax.ppermute(x, 'col', [(c, (c + step) % n_col) for c in range(n_col)])]
    all_to_all x4, waiting for transfers between devices: 8.6 us -> 22.8 us  [exchange(): lax.all_to_all(pieces, 'row', split_axis=0, concat_axis=0, tiled=True)]
    ppermute x12, starting transfers between devices: 22.8 us -> 17.5 us  [shift(): lax.ppermute(x, 'col', [(c, (c + step) % n_col) for c in range(n_col)])]
    unnamed x2 -> x10, local copies, waits for them, and re-layouts: 0.01 us -> 2.35 us
    pallas_call x1, Pallas kernels: 9.83 us -> 7.63 us  [build_operator(): pl.pallas_call(functools.partial(operator_kernel, n_col), grid=(n_col,),...]
    pallas_call x8, Pallas kernels: 36.4 us -> 38.3 us  [product(): pl.pallas_call(functools.partial(product_kernel, n_row, n_col, origins, h...]
  transfers between devices with their start and end apart: 16 -> 16, of which waited for: 11 -> 8; matrix products, arithmetic and copies ran while one was open for 0% -> 0% of each run, Pallas kernels for 34% -> 38%
where the time goes in v6:
time: 136 us
  Pallas kernels  56.7 us (42%)
  waiting for transfers between devices  42.5 us (31%)
  starting transfers between devices  33 us (24%)
  local copies, waits for them, and re-layouts  2.35 us (2%)
  between operations  1.49 us (1%)
    pallas_call x8, Pallas kernels, product(): pl.pallas_call(functools.partial(product_kernel, n_row, n_col, origins, h...  38.3 us
    all_to_all x4, waiting for transfers between devices, exchange(): lax.all_to_all(pieces, 'row', split_axis=0, concat_axis=0, tiled=True)  22.8 us
    ppermute x12, waiting for transfers between devices, shift(): lax.ppermute(x, 'col', [(c, (c + step) % n_col) for c in range(n_col)])  19.7 us
    ppermute x12, starting transfers between devices, shift(): lax.ppermute(x, 'col', [(c, (c + step) % n_col) for c in range(n_col)])  17.5 us
    all_to_all x4, starting transfers between devices, exchange(): lax.all_to_all(pieces, 'row', split_axis=0, concat_axis=0, tiled=True)  15.6 us
    pallas_call x1, Pallas kernels, build_operator(): pl.pallas_call(functools.partial(operator_kernel, n_col), grid=(n_col,),...  7.63 us
    pallas_call x1, Pallas kernels, local_terms(): pl.pallas_call(functools.partial(local_kernel, n_row), in_specs=[pl.Block...  3.98 us
  transfers between devices with their start and end apart: 16, of which 8 were waited for; matrix products, arithmetic and copies ran while one was open for 0% of the time, Pallas kernels for 38%

profile of v6, /device:TPU:0, one launch (start us, length us, event | category | flops | bytes accessed | tf_op | source)
XLA Modules:
  0.0 136.0 jit_solution(1007703520380435496)
XLA Ops:
  0.6 1.7 %term_two.1 = (f32[128,512]{1,0:T(8,128)S(1)}, f32[128,512]{1,0:T(8,128)S(1)}) custom-call(f32[512,256]{1,0:T(8,128)} %grad_hbm.3, s32[512,256]{1,0:T(8,128)} %mask_hbm.3, f32[3,256,256]{2,1,0:T(8,128)} %weight_hbm.3), custom_call_target="tpu_custom_call" | custom-call | flops 1024 | bytes 1024 | tf_op jit(solution)/shard_map/term_two/pallas_call | solution.py:75
  2.4 5.1 %collective-permute-start.1 = (f32[128,512]{1,0:T(8,128)S(1)}, f32[128,512]{1,0:T(8,128)S(1)}, u32[]{:S(2)}, u32[]{:S(2)}) collective-permute-start(f32[128,512]{1,0:T(8,128)S(1)} %get-tuple-element.15.first_ref.refs_2_), channel_id=1, source_target_pairs={{0,3},{1,0},{2,1},{3,2},{4,7},{5,4},{6,5},{7,6},{8,11},{9,8},{10,9... | collective-permute-start | bytes 786440 | tf_op jit(solution)/shard_map/ppermute | solution.py:380
  7.5 0.0 collective-permute-start
  7.5 4.0 %local_terms.1 = (f32[128,512]{1,0:T(8,128)S(1)}, f32[128,512]{1,0:T(8,128)S(1)}, f32[256,512]{1,0:T(8,128)S(1)}, f32[8,192,128]{2,1,0:T(8,128)S(1)}) custom-call(f32[128,512]{1,0:T(8,128)S(1)} %get-tuple-element.15.first_ref.refs_2_, f32[512,256]{1,0:T(8,128)} %grad_hbm.3, s32[512,256]{1,0:T(8,128)} %mask_hbm.3, f32[3,256,256]{2,1,0:T(8,128)} %weight_hbm.3, ...), custom_call_target="tpu_custom_call" | custom-call | flops 1024 | bytes 1024 | tf_op jit(solution)/shard_map/local_terms/pallas_call | solution.py:120
  11.5 0.0 copy-start
  11.5 0.7 copy-done
  12.8 7.6 %operator.1.refs_1_ = bf16[4,4,1024,256]{3,2,1,0:T(8,128)(2,1)} custom-call(s32[1]{0:T(128)} %bitcast.1.ids_ref.refs_0_, s32[1]{0:T(128)S(6)} %copy.13.live_ref, s32[1,128]{1,0:T(1,128)} %rows_hbm.1, s32[1,128]{1,0:T(1,128)} %slots_hbm.1, f32[1,128,128,128]{3,2,1,0:T(8,128)} %values_ref.1), custom_call_target="tpu_custom_call" | custom-call | flops 1024 | bytes 1024 | tf_op jit(solution)/shard_map/operator/pallas_call | solution.py:200
  20.5 0.0 collective-permute-done.1.refs_4_
  20.5 0.0 collective-permute-done.refs_3_
  20.5 0.7 collective-permute-start.2
  21.2 5.4 %product.8.refs_3_ = f32[128,1024]{1,0:T(8,128)S(1)} custom-call(s32[1]{0:T(128)} %bitcast.1.ids_ref.refs_0_, bf16[4,4,1024,256]{3,2,1,0:T(8,128)(2,1)} %operator.1.refs_1_, f32[128,512]{1,0:T(8,128)S(1)} %get-tuple-element.15.first_ref.refs_2_, f32[128,512]{1,0:T(8,128)S(1)} %collective-permute-done.refs_3_, f32[128,512]{1,0:T(8,128)S(1)} %collective-permute-done.1.refs_4_), custom_call_target="tpu_custom_call" | custom-call | flops 17179869184 | bytes 67108864 | tf_op jit(solution)/shard_map/product/pallas_call | solution.py:288
  26.6 3.8 %collective-permute-done.2.refs_2_ = f32[128,512]{1,0:T(8,128)S(1)} collective-permute-done((f32[128,512]{1,0:T(8,128)S(1)}, f32[128,512]{1,0:T(8,128)S(1)}, u32[]{:S(2)}, u32[]{:S(2)}) %collective-permute-start.2) | collective-permute-done | bytes 262176 | tf_op jit(solution)/shard_map/ppermute | solution.py:380
  30.3 0.0 collective-permute-start.4
  30.3 3.8 %collective-permute-start.3 = (f32[128,512]{1,0:T(8,128)S(1)}, f32[128,512]{1,0:T(8,128)}, u32[]{:S(2)}, u32[]{:S(2)}) collective-permute-start(f32[128,512]{1,0:T(8,128)S(1)} %get-tuple-element.21.refs_2_), channel_id=1, source_target_pairs={{0,3},{1,0},{2,1},{3,2},{4,7},{5,4},{6,5},{7,6},{8,11},{9,8},{10,9... | collective-permute-start | bytes 786440 | tf_op jit(solution)/shard_map/ppermute | solution.py:380
  34.2 3.9 %product.10 = f32[8,320,128]{2,1,0:T(8,128)} custom-call(s32[1]{0:T(128)} %bitcast.1.ids_ref.refs_0_, bf16[4,4,1024,256]{3,2,1,0:T(8,128)(2,1)} %operator.1.refs_1_, f32[128,512]{1,0:T(8,128)S(1)} %collective-permute-done.2.refs_2_, f32[128,1024]{1,0:T(8,128)S(1)} %product.8.refs_3_, f32[8,192,128]{2,1,0:T(8,128)S(1)} %get-tuple-element.19.refs_4_), custom_call_target="tpu_custom_call" | custom-call | flops 1024 | bytes 1024 | tf_op jit(solution)/shard_map/product/pallas_call | solution.py:288
  38.0 5.0 %all-to-all-start = ((f32[8,320,128]{2,1,0:T(8,128)}), f32[8,320,128]{2,1,0:T(8,128)S(1)}, u32[]{:S(2)}, u32[]{:S(2)}) async-start(f32[8,320,128]{2,1,0:T(8,128)} %product.10), calls=%async_computation | async-start | bytes 2621440 | tf_op jit(solution)/shard_map/all_to_all | solution.py:384
  43.0 0.0 copy-start.2
  43.0 0.0 collective-permute-done.4.refs_4_
  43.0 0.0 copy-start.3
  43.1 0.7 copy-done.3
  43.7 0.0 collective-permute-done.3.refs_3_
  43.7 1.0 collective-permute-start.5
  44.7 0.0 copy-start.4
  44.7 0.9 copy-done.4
  45.6 6.3 %product.9.refs_3_ = f32[128,1024]{1,0:T(8,128)S(1)} custom-call(s32[1]{0:T(128)} %bitcast.1.ids_ref.refs_0_, bf16[4,4,1024,256]{3,2,1,0:T(8,128)(2,1)} %operator.1.refs_1_, f32[128,512]{1,0:T(8,128)S(1)} %get-tuple-element.21.refs_2_, f32[128,512]{1,0:T(8,128)} %collective-permute-done.3.refs_3_, f32[128,512]{1,0:T(8,128)S(1)} %copy-done.4), custom_call_target="tpu_custom_call" | custom-call | flops 17179869184 | bytes 67108864 | tf_op jit(solution)/shard_map/product/pallas_call | solution.py:288
  52.0 0.7 collective-permute-done.5.refs_2_
  52.7 8.6 %all-to-all-done.came_ref = f32[8,320,128]{2,1,0:T(8,128)S(1)} async-done(((f32[8,320,128]{2,1,0:T(8,128)}), f32[8,320,128]{2,1,0:T(8,128)S(1)}, u32[]{:S(2)}, u32[]{:S(2)}) %all-to-all-start) | async-done | bytes 1310752 | tf_op jit(solution)/shard_map/all_to_all | solution.py:384
  61.2 0.0 copy-done.2
  61.2 0.7 carry.2.refs_2_.refs_4_
  61.9 0.1 collective-permute-start.7
  62.0 2.0 %collective-permute-start.6 = (f32[176,512]{1,0:T(8,128)S(1)}, f32[176,512]{1,0:T(8,128)S(1)}, u32[]{:S(2)}, u32[]{:S(2)}) collective-permute-start(f32[176,512]{1,0:T(8,128)S(1)} %carry.2.refs_2_.refs_4_), channel_id=1, source_target_pairs={{0,1},{1,2},{2,3},{3,0},{4,5},{5,6},{6,7},{7,4},{8,9},{9,10},{10,1... | collective-permute-start | bytes 1081352 | tf_op jit(solution)/shard_map/ppermute | solution.py:380
  64.0 3.5 %product.13 = f32[8,128,128]{2,1,0:T(8,128)} custom-call(s32[1]{0:T(128)} %bitcast.1.ids_ref.refs_0_, bf16[4,4,1024,256]{3,2,1,0:T(8,128)(2,1)} %operator.1.refs_1_, f32[128,512]{1,0:T(8,128)S(1)} %collective-permute-done.5.refs_2_, f32[128,1024]{1,0:T(8,128)S(1)} %product.9.refs_3_), custom_call_target="tpu_custom_call" | custom-call | flops 1024 | bytes 1024 | tf_op jit(solution)/shard_map/product/pallas_call | solution.py:288
  67.6 3.5 %all-to-all-start.2 = ((f32[8,128,128]{2,1,0:T(8,128)}), f32[8,128,128]{2,1,0:T(8,128)S(1)}, u32[]{:S(2)}, u32[]{:S(2)}) async-start(f32[8,128,128]{2,1,0:T(8,128)} %product.13), calls=%async_computation.2 | async-start | bytes 1048576 | tf_op jit(solution)/shard_map/all_to_all | solution.py:384
  71.1 0.0 copy-start.1
  71.1 9.8 %collective-permute-done.7.refs_4_.refs_5_ = f32[176,512]{1,0:T(8,128)S(1)} collective-permute-done((f32[176,512]{1,0:T(8,128)S(1)}, f32[176,512]{1,0:T(8,128)S(1)}, u32[]{:S(2)}, u32[]{:S(2)}) %collective-permute-start.7) | collective-permute-done | bytes 360480 | tf_op jit(solution)/shard_map/ppermute | solution.py:380
  80.9 0.0 collective-permute-done.6.refs_3_.refs_7_
  81.0 0.0 collective-permute-start.8
  81.0 5.4 %product.11.refs_3_ = f32[128,1024]{1,0:T(8,128)S(1)} custom-call(s32[1]{0:T(128)} %bitcast.1.ids_ref.refs_0_, bf16[4,4,1024,256]{3,2,1,0:T(8,128)(2,1)} %operator.1.refs_1_, f32[176,512]{1,0:T(8,128)S(1)} %carry.2.refs_2_.refs_4_, f32[176,512]{1,0:T(8,128)S(1)} %collective-permute-done.6.refs_3_.refs_7_, f32[176,512]{1,0:T(8,128)S(1)} %collective-permute-done.7.refs_4_.refs_5_), custom_call_target="tpu_custom_call" | custom-call | flops 17179869184 | bytes 67108864 | tf_op jit(solution)/shard_map/product/pallas_call | solution.py:288
  86.3 3.9 %collective-permute-done.8.refs_2_.refs_6_ = f32[176,512]{1,0:T(8,128)S(1)} collective-permute-done((f32[176,512]{1,0:T(8,128)S(1)}, f32[176,512]{1,0:T(8,128)S(1)}, u32[]{:S(2)}, u32[]{:S(2)}) %collective-permute-start.8) | collective-permute-done | bytes 360480 | tf_op jit(solution)/shard_map/ppermute | solution.py:380
  90.3 0.0 all-to-all-done.2.came_ref
  90.3 0.0 copy-done.1
  90.3 1.4 %carry.3.refs_2_ = f32[128,512]{1,0:T(8,128)} custom-call(s32[8]{0:T(128)S(1)} %bitcast.3, f32[128,512]{1,0:T(8,128)S(1)} %copy-done.1, f32[8,128,128]{2,1,0:T(8,128)S(1)} %all-to-all-done.2.came_ref), custom_call_target="tpu_custom_call" | custom-call | flops 1024 | bytes 1024 | tf_op jit(solution)/shard_map/carry/pallas_call | solution.py:322
  91.6 0.0 collective-permute-start.10
  91.7 3.8 %collective-permute-start.9 = (f32[128,512]{1,0:T(8,128)}, f32[128,512]{1,0:T(8,128)}, u32[]{:S(2)}, u32[]{:S(2)}) collective-permute-start(f32[128,512]{1,0:T(8,128)} %carry.3.refs_2_), channel_id=1, source_target_pairs={{0,3},{1,0},{2,1},{3,2},{4,7},{5,4},{6,5},{7,6},{8,11},{9,8},{10,9... | collective-permute-start | bytes 786440 | tf_op jit(solution)/shard_map/ppermute | solution.py:380
  95.5 3.9 %product.12 = f32[8,320,128]{2,1,0:T(8,128)} custom-call(s32[1]{0:T(128)} %bitcast.1.ids_ref.refs_0_, bf16[4,4,1024,256]{3,2,1,0:T(8,128)(2,1)} %operator.1.refs_1_, f32[176,512]{1,0:T(8,128)S(1)} %collective-permute-done.8.refs_2_.refs_6_, f32[128,1024]{1,0:T(8,128)S(1)} %product.11.refs_3_, f32[176,512]{1,0:T(8,128)S(1)} %carry.2.refs_2_.refs_4_, ...), custom_call_target="tpu_custom_call" | custom-call | flops 1024 | bytes 1024 | tf_op jit(solution)/shard_map/product/pallas_call | solution.py:288
  99.3 3.6 %all-to-all-start.1 = ((f32[8,320,128]{2,1,0:T(8,128)}), f32[8,320,128]{2,1,0:T(8,128)S(1)}, u32[]{:S(2)}, u32[]{:S(2)}) async-start(f32[8,320,128]{2,1,0:T(8,128)} %product.12), calls=%async_computation.1 | async-start | bytes 2621440 | tf_op jit(solution)/shard_map/all_to_all | solution.py:384
  102.9 0.0 collective-permute-done.10.refs_4_
  102.9 0.0 collective-permute-done.9.refs_3_
  103.0 1.0 collective-permute-start.11
  104.0 6.4 %product.14.refs_3_ = f32[128,1024]{1,0:T(8,128)S(1)} custom-call(s32[1]{0:T(128)} %bitcast.1.ids_ref.refs_0_, bf16[4,4,1024,256]{3,2,1,0:T(8,128)(2,1)} %operator.1.refs_1_, f32[128,512]{1,0:T(8,128)} %carry.3.refs_2_, f32[128,512]{1,0:T(8,128)} %collective-permute-done.9.refs_3_, f32[128,512]{1,0:T(8,128)S(1)} %collective-permute-done.10.refs_4_), custom_call_target="tpu_custom_call" | custom-call | flops 17179869184 | bytes 67108864 | tf_op jit(solution)/shard_map/product/pallas_call | solution.py:288
  110.4 1.5 %collective-permute-done.11.refs_2_ = f32[128,512]{1,0:T(8,128)S(1)} collective-permute-done((f32[128,512]{1,0:T(8,128)}, f32[128,512]{1,0:T(8,128)S(1)}, u32[]{:S(2)}, u32[]{:S(2)}) %collective-permute-start.11) | collective-permute-done | bytes 262176 | tf_op jit(solution)/shard_map/ppermute | solution.py:380
  111.8 3.6 %product.15 = f32[8,128,128]{2,1,0:T(8,128)} custom-call(s32[1]{0:T(128)} %bitcast.1.ids_ref.refs_0_, bf16[4,4,1024,256]{3,2,1,0:T(8,128)(2,1)} %operator.1.refs_1_, f32[128,512]{1,0:T(8,128)S(1)} %collective-permute-done.11.refs_2_, f32[128,1024]{1,0:T(8,128)S(1)} %product.14.refs_3_), custom_call_target="tpu_custom_call" | custom-call | flops 1024 | bytes 1024 | tf_op jit(solution)/shard_map/product/pallas_call | solution.py:288
  115.4 5.7 %all-to-all-done.1.left_ref.came_ref = f32[8,320,128]{2,1,0:T(8,128)S(1)} async-done(((f32[8,320,128]{2,1,0:T(8,128)}), f32[8,320,128]{2,1,0:T(8,128)S(1)}, u32[]{:S(2)}, u32[]{:S(2)}) %all-to-all-start.1) | async-done | bytes 1310752 | tf_op jit(solution)/shard_map/all_to_all | solution.py:384
  121.1 3.5 %all-to-all-start.3 = ((f32[8,128,128]{2,1,0:T(8,128)}), f32[8,128,128]{2,1,0:T(8,128)S(1)}, u32[]{:S(2)}, u32[]{:S(2)}) async-start(f32[8,128,128]{2,1,0:T(8,128)} %product.15), calls=%async_computation.3 | async-start | bytes 1048576 | tf_op jit(solution)/shard_map/all_to_all | solution.py:384
  124.6 1.1 assemble.1
  125.7 8.5 %all-to-all-done.3.right_ref = f32[8,128,128]{2,1,0:T(8,128)S(1)} async-done(((f32[8,128,128]{2,1,0:T(8,128)}), f32[8,128,128]{2,1,0:T(8,128)S(1)}, u32[]{:S(2)}, u32[]{:S(2)}) %all-to-all-start.3) | async-done | bytes 524320 | tf_op jit(solution)/shard_map/all_to_all | solution.py:384
  134.3 1.8 %finish.1 = f32[512,256]{1,0:T(8,128)} custom-call(s32[8]{0:T(128)S(1)} %bitcast.4, f32[256,512]{1,0:T(8,128)S(1)} %get-tuple-element.16.base_ref, f32[8,320,128]{2,1,0:T(8,128)S(1)} %all-to-all-done.1.left_ref.came_ref, f32[8,128,128]{2,1,0:T(8,128)S(1)} %all-to-all-done.3.right_ref), custom_call_target="tpu_custom_call" | custom-call | flops 1024 | bytes 1024 | tf_op jit(solution)/shard_map/finish/pallas_call | solution.py:343
Async XLA Ops:
  2.4 18.1 %collective-permute-start.1 = (f32[128,512]{1,0:T(8,128)S(1)}, f32[128,512]{1,0:T(8,128)S(1)}, u32[]{:S(2)}, u32[]{:S(2)}) collective-permute-start(f32[128,512]{1,0:T(8,128)S(1)} %get-tuple-element.15.first_ref.refs_2_), channel_id=1, source_target_pairs={{0,3},{1,0},{2,1},{3,2},{4,7},{5,4},{6,5},{7,6},{8,11},{9,8},{10,9... | collective-permute-start | bytes 786440 | tf_op jit(solution)/shard_map/ppermute | solution.py:380
  7.5 13.0 %collective-permute-start = (f32[128,512]{1,0:T(8,128)S(1)}, f32[128,512]{1,0:T(8,128)S(1)}, u32[]{:S(2)}, u32[]{:S(2)}) collective-permute-start(f32[128,512]{1,0:T(8,128)S(1)} %get-tuple-element.15.first_ref.refs_2_), channel_id=1, source_target_pairs={{0,1},{1,2},{2,3},{3,0},{4,5},{5,6},{6,7},{7,4},{8,9},{9,10},{10,1... | collective-permute-start | bytes 786440 | tf_op jit(solution)/shard_map/ppermute | solution.py:380
  11.5 0.7 copy-start
  20.5 9.8 %collective-permute-start.2 = (f32[128,512]{1,0:T(8,128)S(1)}, f32[128,512]{1,0:T(8,128)S(1)}, u32[]{:S(2)}, u32[]{:S(2)}) collective-permute-start(f32[128,512]{1,0:T(8,128)S(1)} %collective-permute-done.refs_3_), channel_id=1, source_target_pairs={{0,1},{1,2},{2,3},{3,0},{4,5},{5,6},{6,7},{7,4},{8,9},{9,10},{10,1... | collective-permute-start | bytes 786440 | tf_op jit(solution)/shard_map/ppermute | solution.py:380
  30.3 12.7 %collective-permute-start.4 = (f32[128,512]{1,0:T(8,128)S(1)}, f32[128,512]{1,0:T(8,128)S(1)}, u32[]{:S(2)}, u32[]{:S(2)}) collective-permute-start(f32[128,512]{1,0:T(8,128)S(1)} %get-tuple-element.21.refs_2_), channel_id=1, source_target_pairs={{0,1},{1,2},{2,3},{3,0},{4,5},{5,6},{6,7},{7,4},{8,9},{9,10},{10,1... | collective-permute-start | bytes 786440 | tf_op jit(solution)/shard_map/ppermute | solution.py:380
  30.3 13.4 %collective-permute-start.3 = (f32[128,512]{1,0:T(8,128)S(1)}, f32[128,512]{1,0:T(8,128)}, u32[]{:S(2)}, u32[]{:S(2)}) collective-permute-start(f32[128,512]{1,0:T(8,128)S(1)} %get-tuple-element.21.refs_2_), channel_id=1, source_target_pairs={{0,3},{1,0},{2,1},{3,2},{4,7},{5,4},{6,5},{7,6},{8,11},{9,8},{10,9... | collective-permute-start | bytes 786440 | tf_op jit(solution)/shard_map/ppermute | solution.py:380
  38.0 23.2 %all-to-all-start = ((f32[8,320,128]{2,1,0:T(8,128)}), f32[8,320,128]{2,1,0:T(8,128)S(1)}, u32[]{:S(2)}, u32[]{:S(2)}) async-start(f32[8,320,128]{2,1,0:T(8,128)} %product.10), calls=%async_computation | async-start | bytes 2621440 | tf_op jit(solution)/shard_map/all_to_all | solution.py:384
  43.0 18.2 %copy-start.2 = (s32[1,8,1]{1,2,0:T(1,128)S(1)}, s32[1,8,1]{1,2,0:T(1,128)}, u32[]{:S(2)}) copy-start(s32[1,8,1]{1,2,0:T(1,128)} %param.20) | copy-start | bytes 100
  43.0 0.7 copy-start.3
  43.7 8.9 %collective-permute-start.5 = (f32[128,512]{1,0:T(8,128)}, f32[128,512]{1,0:T(8,128)S(1)}, u32[]{:S(2)}, u32[]{:S(2)}) collective-permute-start(f32[128,512]{1,0:T(8,128)} %collective-permute-done.3.refs_3_), channel_id=1, source_target_pairs={{0,3},{1,0},{2,1},{3,2},{4,7},{5,4},{6,5},{7,6},{8,11},{9,8},{10,9... | collective-permute-start | bytes 786440 | tf_op jit(solution)/shard_map/ppermute | solution.py:380
  44.7 0.9 copy-start.4
  61.9 19.0 %collective-permute-start.7 = (f32[176,512]{1,0:T(8,128)S(1)}, f32[176,512]{1,0:T(8,128)S(1)}, u32[]{:S(2)}, u32[]{:S(2)}) collective-permute-start(f32[176,512]{1,0:T(8,128)S(1)} %carry.2.refs_2_.refs_4_), channel_id=1, source_target_pairs={{0,3},{1,0},{2,1},{3,2},{4,7},{5,4},{6,5},{7,6},{8,11},{9,8},{10,9... | collective-permute-start | bytes 1081352 | tf_op jit(solution)/shard_map/ppermute | solution.py:380
  62.0 18.9 %collective-permute-start.6 = (f32[176,512]{1,0:T(8,128)S(1)}, f32[176,512]{1,0:T(8,128)S(1)}, u32[]{:S(2)}, u32[]{:S(2)}) collective-permute-start(f32[176,512]{1,0:T(8,128)S(1)} %carry.2.refs_2_.refs_4_), channel_id=1, source_target_pairs={{0,1},{1,2},{2,3},{3,0},{4,5},{5,6},{6,7},{7,4},{8,9},{9,10},{10,1... | collective-permute-start | bytes 1081352 | tf_op jit(solution)/shard_map/ppermute | solution.py:380
  67.6 22.7 %all-to-all-start.2 = ((f32[8,128,128]{2,1,0:T(8,128)}), f32[8,128,128]{2,1,0:T(8,128)S(1)}, u32[]{:S(2)}, u32[]{:S(2)}) async-start(f32[8,128,128]{2,1,0:T(8,128)} %product.13), calls=%async_computation.2 | async-start | bytes 1048576 | tf_op jit(solution)/shard_map/all_to_all | solution.py:384
  71.1 19.2 %copy-start.1 = (f32[128,512]{1,0:T(8,128)S(1)}, f32[128,512]{1,0:T(8,128)}, u32[]{:S(2)}) copy-start(f32[128,512]{1,0:T(8,128)} %copy-done) | copy-start | bytes 786436
  81.0 9.3 %collective-permute-start.8 = (f32[176,512]{1,0:T(8,128)S(1)}, f32[176,512]{1,0:T(8,128)S(1)}, u32[]{:S(2)}, u32[]{:S(2)}) collective-permute-start(f32[176,512]{1,0:T(8,128)S(1)} %collective-permute-done.6.refs_3_.refs_7_), channel_id=1, source_target_pairs={{0,1},{1,2},{2,3},{3,0},{4,5},{5,6},{6,7},{7,4},{8,9},{9,10},{10,1... | collective-permute-start | bytes 1081352 | tf_op jit(solution)/shard_map/ppermute | solution.py:380
  91.6 11.3 %collective-permute-start.10 = (f32[128,512]{1,0:T(8,128)}, f32[128,512]{1,0:T(8,128)S(1)}, u32[]{:S(2)}, u32[]{:S(2)}) collective-permute-start(f32[128,512]{1,0:T(8,128)} %carry.3.refs_2_), channel_id=1, source_target_pairs={{0,1},{1,2},{2,3},{3,0},{4,5},{5,6},{6,7},{7,4},{8,9},{9,10},{10,1... | collective-permute-start | bytes 786440 | tf_op jit(solution)/shard_map/ppermute | solution.py:380
  91.7 11.3 %collective-permute-start.9 = (f32[128,512]{1,0:T(8,128)}, f32[128,512]{1,0:T(8,128)}, u32[]{:S(2)}, u32[]{:S(2)}) collective-permute-start(f32[128,512]{1,0:T(8,128)} %carry.3.refs_2_), channel_id=1, source_target_pairs={{0,3},{1,0},{2,1},{3,2},{4,7},{5,4},{6,5},{7,6},{8,11},{9,8},{10,9... | collective-permute-start | bytes 786440 | tf_op jit(solution)/shard_map/ppermute | solution.py:380
  99.3 21.7 %all-to-all-start.1 = ((f32[8,320,128]{2,1,0:T(8,128)}), f32[8,320,128]{2,1,0:T(8,128)S(1)}, u32[]{:S(2)}, u32[]{:S(2)}) async-start(f32[8,320,128]{2,1,0:T(8,128)} %product.12), calls=%async_computation.1 | async-start | bytes 2621440 | tf_op jit(solution)/shard_map/all_to_all | solution.py:384
  103.0 8.9 %collective-permute-start.11 = (f32[128,512]{1,0:T(8,128)}, f32[128,512]{1,0:T(8,128)S(1)}, u32[]{:S(2)}, u32[]{:S(2)}) collective-permute-start(f32[128,512]{1,0:T(8,128)} %collective-permute-done.9.refs_3_), channel_id=1, source_target_pairs={{0,3},{1,0},{2,1},{3,2},{4,7},{5,4},{6,5},{7,6},{8,11},{9,8},{10,9... | collective-permute-start | bytes 786440 | tf_op jit(solution)/shard_map/ppermute | solution.py:380
  121.1 13.2 %all-to-all-start.3 = ((f32[8,128,128]{2,1,0:T(8,128)}), f32[8,128,128]{2,1,0:T(8,128)S(1)}, u32[]{:S(2)}, u32[]{:S(2)}) async-start(f32[8,128,128]{2,1,0:T(8,128)} %product.15), calls=%async_computation.3 | async-start | bytes 1048576 | tf_op jit(solution)/shard_map/all_to_all | solution.py:384

commit v7 on v6

--- a/solution.py
+++ b/solution.py
@@ -219,14 +219,12 @@
     )(ids, live, *in_hbm(rows, slots, values))
 
 
-def product_kernel(n_row, n_col, origins, has_prev, last, has_under, n_carriers, *refs):
+def product_kernel(n_row, n_col, origins, has_prev, last, n_carriers, *refs):
     n = len(origins)
     ids_ref, op_ref, refs = refs[0], refs[1], refs[2:]
     fields, refs = refs[:n], refs[n:]
     if has_prev:
         prev, refs = refs[0], refs[1:]
-    if has_under:
-        under, refs = refs[0], refs[1:]
     carriers, refs = refs[:n_carriers], refs[n_carriers:]
     out_ref, buf, sems = refs[:3]
 
@@ -240,8 +238,6 @@
     for field in fields:
         high, low = split(field[:H, :])
         left.append(jnp.concatenate([jnp.concatenate([x, x], axis=1) for x in (high, low)], axis=0))
-    if has_under:
-        out_ref[:, H:, :] = under[...]
     if n_carriers:
         ordered = refs[3]
         for k in range(n_col):
@@ -270,11 +266,10 @@
             out_ref[:, here] = summed
 
 
-def product(n_row, n_col, ids, origins, operator, fields, prev, last, under=None, carriers=()):
+def product(n_row, n_col, ids, origins, operator, fields, prev, last, carriers=()):
     n = len(origins)
     has_prev = prev is not None
-    has_under = under is not None
-    share = under.shape[1] if has_under else 0
+    share = 0
     scratch = [
         pltpu.VMEM((n, n_row // 2, 2 * NODES_DEV, WIDE), BF16),
         pltpu.SemaphoreType.DMA((n, n_row // 2)),
@@ -284,9 +279,9 @@
         share = rows * NODES_DEV // LANES
         scratch.append(pltpu.VMEM((n_col, rows, NODES_DEV), F32))
     shape = (n_row, H + share, TB) if last else (H, n_row * TB)
-    count = n + has_prev + has_under + len(carriers)
-    return pl.pallas_call(
-        functools.partial(product_kernel, n_row, n_col, origins, has_prev, last, has_under, len(carriers)),
+    count = n + has_prev + len(carriers)
+    return pl.pallas_call(
+        functools.partial(product_kernel, n_row, n_col, origins, has_prev, last, len(carriers)),
         in_specs=[SMEM, HBM] + [VMEM] * count,
         out_specs=VMEM,
         out_shape=jax.ShapeDtypeStruct(shape, F32),
@@ -299,35 +294,36 @@
         *in_hbm(operator),
         *fields,
         *((prev,) if has_prev else ()),
-        *((under,) if has_under else ()),
         *carriers,
     )
 
 
-def carry_kernel(n_row, rows, owners_ref, base_ref, came_ref, out_ref):
+def carry_kernel(n_row, rows, owners_ref, base_ref, came_ref, *refs):
+    out_ref = refs[-1]
     out_ref[:H, :] = base_ref[...]
     for q in range(n_row):
         here = pl.ds(pl.multiple_of(owners_ref[q] * TB, TB), TB)
-        out_ref[:H, here] += 2.0 * came_ref[q, :H, :]
+        out_ref[:H, here] += 2.0 * came_ref[q]
     if rows:
-        share = came_ref[0, H:, :]
+        pieces_ref = refs[0]
+        share = pieces_ref[0]
         for q in range(1, n_row):
-            share = share + came_ref[q, H:, :]
+            share = share + pieces_ref[q]
         for j in range(NODES_DEV // LANES):
             out_ref[H:, j * LANES : (j + 1) * LANES] = share[j * rows : (j + 1) * rows, :]
 
 
-def carry(n_row, owners, base, came):
-    rows = (came.shape[1] - H) * LANES // NODES_DEV
+def carry(n_row, owners, base, came, *pieces):
+    rows = pieces[0].shape[1] * LANES // NODES_DEV if pieces else 0
     return pl.pallas_call(
         functools.partial(carry_kernel, n_row, rows),
-        in_specs=[SMEM, VMEM, VMEM],
+        in_specs=[SMEM] + [VMEM] * (2 + len(pieces)),
         out_specs=VMEM,
         out_shape=jax.ShapeDtypeStruct((H + rows, NODES_DEV), F32),
         compiler_params=params(24),
         cost_estimate=LIGHT,
         name="carry",
-    )(owners, base, came)
+    )(owners, base, came, *pieces)
 
 
 def finish_kernel(n_row, owners_ref, base_ref, left_ref, right_ref, out_ref, total):
@@ -388,6 +384,12 @@
     return lax.optimization_barrier((x, *others))[0]
 
 
+def opposite(field, below, above):
+    col = lax.axis_index("col")
+    sent = jnp.where(col == 1, above, jnp.where(col == 2, below, field))
+    return lax.ppermute(sent, "col", [(1, 0), (2, 3), (3, 1), (0, 2)])
+
+
 def gather(n_col, field, side, *done):
     long = n_col // 2
     short = n_col - 1 - long
@@ -396,7 +398,10 @@
     for s in range(1, long + 1):
         if s == 2:
             ahead = after(ahead, behind, *done)
-        ahead = shift(n_col, ahead, side)
+        if s == 2 and n_col == 4:
+            ahead = opposite(field, ahead, behind) if side > 0 else opposite(field, behind, ahead)
+        else:
+            ahead = shift(n_col, ahead, side)
         step = [((-side * s) % n_col, ahead)]
         if s <= short:
             behind = shift(n_col, behind, -side)
@@ -414,10 +419,10 @@
     return total
 
 
-def final(n_row, n_col, ids, operator, steps, total, under=None, carrying=False):
+def final(n_row, n_col, ids, operator, steps, total, carrying=False):
     origins, fields = zip(*steps[-1])
     carriers = [x for _, x in sorted((p for step in steps for p in step), key=lambda p: p[0])] if carrying else ()
-    return product(n_row, n_col, ids, origins, operator, fields, total, True, under, carriers)
+    return product(n_row, n_col, ids, origins, operator, fields, total, True, carriers)
 
 
 def per_device(
@@ -445,12 +450,13 @@
     common = (n_row, n_col, ids, operator)
 
     steps = gather(n_col, left, 1, operator, pieces)
+    pieces = exchange(after(pieces, steps[1][0][1]))
     left_early = early(*common, steps)
     right_steps = gather(n_col, after(right, left_early, steps[-1][0][1]), -1)
-    left_came = exchange(final(*common, steps, left_early, under=pieces))
+    left_came = exchange(final(*common, steps, left_early))
     right_early = early(*common, right_steps)
 
-    left_carried = carry(n_row, owners, after(one_left, right_early, right_steps[-1][0][1]), left_came)
+    left_carried = carry(n_row, owners, after(one_left, right_early, right_steps[-1][0][1]), left_came, pieces)
     steps = gather(n_col, left_carried, 1)
     right_came = exchange(final(*common, right_steps, right_early))
     left_early = early(*common, steps)

time: 136 us -> 140 us (1.029)
  starting transfers between devices: 33 us -> 39.9 us
  waiting for transfers between devices: 42.5 us -> 38.7 us
    ppermute x0 -> x4, waiting for transfers between devices: none -> 5.92 us  [opposite(): return lax.ppermute(sent, 'col', [(1, 0), (2, 3), (3, 1), (0, 2)])]
    all_to_all x4 -> x5, waiting for transfers between devices: 22.8 us -> 17 us  [exchange(): lax.all_to_all(pieces, 'row', split_axis=0, concat_axis=0, tiled=True)]
    ppermute x0 -> x4, starting transfers between devices: none -> 4.5 us  [opposite(): return lax.ppermute(sent, 'col', [(1, 0), (2, 3), (3, 1), (0, 2)])]
    ppermute x12 -> x8, waiting for transfers between devices: 19.7 us -> 15.8 us  [shift(): lax.ppermute(x, 'col', [(c, (c + step) % n_col) for c in range(n_col)])]
    all_to_all x4 -> x5, starting transfers between devices: 15.6 us -> 18.6 us  [exchange(): lax.all_to_all(pieces, 'row', split_axis=0, concat_axis=0, tiled=True)]
    ppermute x12 -> x8, starting transfers between devices: 17.5 us -> 16.8 us  [shift(): lax.ppermute(x, 'col', [(c, (c + step) % n_col) for c in range(n_col)])]
  transfers between devices with their start and end apart: 16 -> 17, of which waited for: 8 -> 11; matrix products, arithmetic and copies ran while one was open for 0% -> 1% of each run, Pallas kernels for 38% -> 37%
where the time goes in v7:
time: 140 us; the launch traced here: 139 us
  Pallas kernels  56.5 us (40%)
  starting transfers between devices  39.9 us (28%)
  waiting for transfers between devices  38.7 us (28%)
  local copies, waits for them, and re-layouts  1.69 us (1%)
  between operations  1.49 us (1%)
    pallas_call x8, Pallas kernels, product(): pl.pallas_call(functools.partial(product_kernel, n_row, n_col, origins, h...  37 us
    all_to_all x5, starting transfers between devices, exchange(): lax.all_to_all(pieces, 'row', split_axis=0, concat_axis=0, tiled=True)  18.6 us
    all_to_all x5, waiting for transfers between devices, exchange(): lax.all_to_all(pieces, 'row', split_axis=0, concat_axis=0, tiled=True)  17 us
    ppermute x8, starting transfers between devices, shift(): lax.ppermute(x, 'col', [(c, (c + step) % n_col) for c in range(n_col)])  16.8 us
    ppermute x8, waiting for transfers between devices, shift(): lax.ppermute(x, 'col', [(c, (c + step) % n_col) for c in range(n_col)])  15.8 us
    pallas_call x1, Pallas kernels, build_operator(): pl.pallas_call(functools.partial(operator_kernel, n_col), grid=(n_col,),...  8.62 us
    ppermute x4, waiting for transfers between devices, opposite(): return lax.ppermute(sent, 'col', [(1, 0), (2, 3), (3, 1), (0, 2)])  5.92 us
    pallas_call x1, Pallas kernels, local_terms(): pl.pallas_call(functools.partial(local_kernel, n_row), in_specs=[pl.Block...  4.86 us
  transfers between devices with their start and end apart: 17, of which 11 were waited for; matrix products, arithmetic and copies ran while one was open for 1% of the time, Pallas kernels for 37%

profile of v7, /device:TPU:0, one launch (start us, length us, event | category | flops | bytes accessed | tf_op | source)
XLA Modules:
  0.0 139.2 jit_solution(12966629672848662742)
XLA Ops:
  0.6 1.7 %term_two.1 = (f32[128,512]{1,0:T(8,128)S(1)}, f32[128,512]{1,0:T(8,128)S(1)}) custom-call(f32[512,256]{1,0:T(8,128)} %grad_hbm.3, s32[512,256]{1,0:T(8,128)} %mask_hbm.3, f32[3,256,256]{2,1,0:T(8,128)} %weight_hbm.3), custom_call_target="tpu_custom_call" | custom-call | flops 1024 | bytes 1024 | tf_op jit(solution)/shard_map/term_two/pallas_call | solution.py:75
  2.4 3.1 %collective-permute-start = (f32[128,512]{1,0:T(8,128)S(1)}, f32[128,512]{1,0:T(8,128)S(1)}, u32[]{:S(2)}, u32[]{:S(2)}) collective-permute-start(f32[128,512]{1,0:T(8,128)S(1)} %get-tuple-element.16.first_ref.refs_2_), channel_id=1, source_target_pairs={{0,1},{1,2},{2,3},{3,0},{4,5},{5,6},{6,7},{7,4},{8,9},{9,10},{10,1... | collective-permute-start | bytes 786440 | tf_op jit(solution)/shard_map/ppermute | solution.py:376
  5.5 2.1 %collective-permute-start.1 = (f32[128,512]{1,0:T(8,128)S(1)}, f32[128,512]{1,0:T(8,128)S(1)}, u32[]{:S(2)}, u32[]{:S(2)}) collective-permute-start(f32[128,512]{1,0:T(8,128)S(1)} %get-tuple-element.16.first_ref.refs_2_), channel_id=1, source_target_pairs={{0,3},{1,0},{2,1},{3,2},{4,7},{5,4},{6,5},{7,6},{8,11},{9,8},{10,9... | collective-permute-start | bytes 786440 | tf_op jit(solution)/shard_map/ppermute | solution.py:376
  7.6 4.9 %local_terms.1 = (f32[128,512]{1,0:T(8,128)S(1)}, f32[128,512]{1,0:T(8,128)S(1)}, f32[256,512]{1,0:T(8,128)S(1)}, f32[8,192,128]{2,1,0:T(8,128)}) custom-call(f32[128,512]{1,0:T(8,128)S(1)} %get-tuple-element.16.first_ref.refs_2_, f32[512,256]{1,0:T(8,128)} %grad_hbm.3, s32[512,256]{1,0:T(8,128)} %mask_hbm.3, f32[3,256,256]{2,1,0:T(8,128)} %weight_hbm.3, ...), custom_call_target="tpu_custom_call" | custom-call | flops 1024 | bytes 1024 | tf_op jit(solution)/shard_map/local_terms/pallas_call | solution.py:120
  12.4 0.0 copy-start
  12.4 0.7 copy-done
  13.2 0.0 copy-start.2
  13.8 8.6 %operator.1.refs_1_ = bf16[4,4,1024,256]{3,2,1,0:T(8,128)(2,1)} custom-call(s32[1]{0:T(128)} %bitcast.1.ids_ref.refs_0_, s32[1]{0:T(128)S(6)} %copy.13.live_ref, s32[1,128]{1,0:T(1,128)} %rows_hbm.1, s32[1,128]{1,0:T(1,128)} %slots_hbm.1, f32[1,128,128,128]{3,2,1,0:T(8,128)} %values_ref.1), custom_call_target="tpu_custom_call" | custom-call | flops 1024 | bytes 1024 | tf_op jit(solution)/shard_map/operator/pallas_call | solution.py:200
  22.4 0.0 copy-done.2
  22.5 0.0 collective-permute-done.refs_3_
  22.5 3.6 %all-to-all-start.1 = ((f32[8,192,128]{2,1,0:T(8,128)}), f32[8,192,128]{2,1,0:T(8,128)S(1)}, u32[]{:S(2)}, u32[]{:S(2)}) async-start(f32[8,192,128]{2,1,0:T(8,128)} %get-tuple-element.25), calls=%async_computation.1 | async-start | bytes 1572864 | tf_op jit(solution)/shard_map/all_to_all | solution.py:380
  26.0 0.0 collective-permute-done.1.refs_4_
  26.1 0.1 select_select_fusion.3
  26.1 1.8 %collective-permute-start.2 = (f32[128,512]{1,0:T(8,128)S(1)}, f32[128,512]{1,0:T(8,128)S(1)}, u32[]{:S(2)}, u32[]{:S(2)}) collective-permute-start(f32[128,512]{1,0:T(8,128)S(1)} %select_select_fusion.3), channel_id=1, source_target_pairs={{1,0},{2,3},{3,1},{0,2},{5,4},{6,7},{7,5},{4,6},{9,8},{10,11},{11,... | collective-permute-start | bytes 786440 | tf_op jit(solution)/shard_map/ppermute | solution.py:390
  27.9 5.4 %product.8.refs_3_ = f32[128,1024]{1,0:T(8,128)S(1)} custom-call(s32[1]{0:T(128)} %bitcast.1.ids_ref.refs_0_, bf16[4,4,1024,256]{3,2,1,0:T(8,128)(2,1)} %operator.1.refs_1_, f32[128,512]{1,0:T(8,128)S(1)} %get-tuple-element.16.first_ref.refs_2_, f32[128,512]{1,0:T(8,128)S(1)} %collective-permute-done.refs_3_, f32[128,512]{1,0:T(8,128)S(1)} %collective-permute-done.1.refs_4_), custom_call_target="tpu_custom_call" | custom-call | flops 17179869184 | bytes 67108864 | tf_op jit(solution)/shard_map/product/pallas_call | solution.py:283
  33.3 1.5 %collective-permute-done.2.refs_2_ = f32[128,512]{1,0:T(8,128)S(1)} collective-permute-done((f32[128,512]{1,0:T(8,128)S(1)}, f32[128,512]{1,0:T(8,128)S(1)}, u32[]{:S(2)}, u32[]{:S(2)}) %collective-permute-start.2) | collective-permute-done | bytes 262176 | tf_op jit(solution)/shard_map/ppermute | solution.py:390
  34.8 2.1 %collective-permute-start.4 = (f32[128,512]{1,0:T(8,128)S(1)}, f32[128,512]{1,0:T(8,128)S(1)}, u32[]{:S(2)}, u32[]{:S(2)}) collective-permute-start(f32[128,512]{1,0:T(8,128)S(1)} %get-tuple-element.22.refs_2_), channel_id=1, source_target_pairs={{0,1},{1,2},{2,3},{3,0},{4,5},{5,6},{6,7},{7,4},{8,9},{9,10},{10,1... | collective-permute-start | bytes 786440 | tf_op jit(solution)/shard_map/ppermute | solution.py:376
  36.9 1.7 %collective-permute-start.3 = (f32[128,512]{1,0:T(8,128)S(1)}, f32[128,512]{1,0:T(8,128)S(1)}, u32[]{:S(2)}, u32[]{:S(2)}) collective-permute-start(f32[128,512]{1,0:T(8,128)S(1)} %get-tuple-element.22.refs_2_), channel_id=1, source_target_pairs={{0,3},{1,0},{2,1},{3,2},{4,7},{5,4},{6,5},{7,6},{8,11},{9,8},{10,9... | collective-permute-start | bytes 786440 | tf_op jit(solution)/shard_map/ppermute | solution.py:376
  38.6 3.6 %product.10 = f32[8,128,128]{2,1,0:T(8,128)} custom-call(s32[1]{0:T(128)} %bitcast.1.ids_ref.refs_0_, bf16[4,4,1024,256]{3,2,1,0:T(8,128)(2,1)} %operator.1.refs_1_, f32[128,512]{1,0:T(8,128)S(1)} %collective-permute-done.2.refs_2_, f32[128,1024]{1,0:T(8,128)S(1)} %product.8.refs_3_), custom_call_target="tpu_custom_call" | custom-call | flops 1024 | bytes 1024 | tf_op jit(solution)/shard_map/product/pallas_call | solution.py:283
  42.2 3.7 %collective-permute-done.4.refs_4_ = f32[128,512]{1,0:T(8,128)S(1)} collective-permute-done((f32[128,512]{1,0:T(8,128)S(1)}, f32[128,512]{1,0:T(8,128)S(1)}, u32[]{:S(2)}, u32[]{:S(2)}) %collective-permute-start.4) | collective-permute-done | bytes 262176 | tf_op jit(solution)/shard_map/ppermute | solution.py:376
  45.8 4.1 %collective-permute-done.3.refs_3_ = f32[128,512]{1,0:T(8,128)S(1)} collective-permute-done((f32[128,512]{1,0:T(8,128)S(1)}, f32[128,512]{1,0:T(8,128)S(1)}, u32[]{:S(2)}, u32[]{:S(2)}) %collective-permute-start.3) | collective-permute-done | bytes 262176 | tf_op jit(solution)/shard_map/ppermute | solution.py:376
  50.0 0.8 select_select_fusion.2
  50.7 0.6 collective-permute-start.5
  51.3 0.0 all-to-all-done.1.refs_0_
  51.3 3.6 %all-to-all-start = ((f32[8,128,128]{2,1,0:T(8,128)}), f32[8,128,128]{2,1,0:T(8,128)S(1)}, u32[]{:S(2)}, u32[]{:S(2)}) async-start(f32[8,128,128]{2,1,0:T(8,128)} %product.10), calls=%async_computation | async-start | bytes 1048576 | tf_op jit(solution)/shard_map/all_to_all | solution.py:380
  55.0 0.0 copy-start.4
  55.0 5.4 %product.9.refs_3_ = f32[128,1024]{1,0:T(8,128)S(1)} custom-call(s32[1]{0:T(128)} %bitcast.1.ids_ref.refs_0_, bf16[4,4,1024,256]{3,2,1,0:T(8,128)(2,1)} %operator.1.refs_1_, f32[128,512]{1,0:T(8,128)S(1)} %get-tuple-element.22.refs_2_, f32[128,512]{1,0:T(8,128)S(1)} %collective-permute-done.3.refs_3_, f32[128,512]{1,0:T(8,128)S(1)} %collective-permute-done.4.refs_4_), custom_call_target="tpu_custom_call" | custom-call | flops 17179869184 | bytes 67108864 | tf_op jit(solution)/shard_map/product/pallas_call | solution.py:283
  60.4 0.0 collective-permute-done.5.refs_2_
  60.4 4.3 %all-to-all-done.came_ref = f32[8,128,128]{2,1,0:T(8,128)S(1)} async-done(((f32[8,128,128]{2,1,0:T(8,128)}), f32[8,128,128]{2,1,0:T(8,128)S(1)}, u32[]{:S(2)}, u32[]{:S(2)}) %all-to-all-start) | async-done | bytes 524320 | tf_op jit(solution)/shard_map/all_to_all | solution.py:380
  64.7 0.0 copy-done.4
  64.7 0.0 copy-start.3
  64.7 0.9 copy-done.3
  65.7 0.7 carry.2.refs_2_.refs_4_
  66.4 1.5 %collective-permute-start.7 = (f32[176,512]{1,0:T(8,128)S(1)}, f32[176,512]{1,0:T(8,128)S(1)}, u32[]{:S(2)}, u32[]{:S(2)}) collective-permute-start(f32[176,512]{1,0:T(8,128)S(1)} %carry.2.refs_2_.refs_4_), channel_id=1, source_target_pairs={{0,1},{1,2},{2,3},{3,0},{4,5},{5,6},{6,7},{7,4},{8,9},{9,10},{10,1... | collective-permute-start | bytes 1081352 | tf_op jit(solution)/shard_map/ppermute | solution.py:376
  67.8 2.4 %collective-permute-start.6 = (f32[176,512]{1,0:T(8,128)S(1)}, f32[176,512]{1,0:T(8,128)S(1)}, u32[]{:S(2)}, u32[]{:S(2)}) collective-permute-start(f32[176,512]{1,0:T(8,128)S(1)} %carry.2.refs_2_.refs_4_), channel_id=1, source_target_pairs={{0,3},{1,0},{2,1},{3,2},{4,7},{5,4},{6,5},{7,6},{8,11},{9,8},{10,9... | collective-permute-start | bytes 1081352 | tf_op jit(solution)/shard_map/ppermute | solution.py:376
  70.3 3.5 %product.13 = f32[8,128,128]{2,1,0:T(8,128)} custom-call(s32[1]{0:T(128)} %bitcast.1.ids_ref.refs_0_, bf16[4,4,1024,256]{3,2,1,0:T(8,128)(2,1)} %operator.1.refs_1_, f32[128,512]{1,0:T(8,128)S(1)} %collective-permute-done.5.refs_2_, f32[128,1024]{1,0:T(8,128)S(1)} %product.9.refs_3_), custom_call_target="tpu_custom_call" | custom-call | flops 1024 | bytes 1024 | tf_op jit(solution)/shard_map/product/pallas_call | solution.py:283
  73.8 3.5 %all-to-all-start.3 = ((f32[8,128,128]{2,1,0:T(8,128)}), f32[8,128,128]{2,1,0:T(8,128)S(1)}, u32[]{:S(2)}, u32[]{:S(2)}) async-start(f32[8,128,128]{2,1,0:T(8,128)} %product.13), calls=%async_computation.3 | async-start | bytes 1048576 | tf_op jit(solution)/shard_map/all_to_all | solution.py:380
  77.3 2.3 %collective-permute-done.7.refs_3_.refs_7_ = f32[176,512]{1,0:T(8,128)S(1)} collective-permute-done((f32[176,512]{1,0:T(8,128)S(1)}, f32[176,512]{1,0:T(8,128)S(1)}, u32[]{:S(2)}, u32[]{:S(2)}) %collective-permute-start.7) | collective-permute-done | bytes 360480 | tf_op jit(solution)/shard_map/ppermute | solution.py:376
  79.6 3.5 %collective-permute-done.6.refs_4_.refs_5_ = f32[176,512]{1,0:T(8,128)S(1)} collective-permute-done((f32[176,512]{1,0:T(8,128)S(1)}, f32[176,512]{1,0:T(8,128)S(1)}, u32[]{:S(2)}, u32[]{:S(2)}) %collective-permute-start.6) | collective-permute-done | bytes 360480 | tf_op jit(solution)/shard_map/ppermute | solution.py:376
  83.1 0.1 select_select_fusion
  83.2 0.0 copy-start.1
  83.2 1.5 %collective-permute-start.8 = (f32[176,512]{1,0:T(8,128)S(1)}, f32[176,512]{1,0:T(8,128)S(1)}, u32[]{:S(2)}, u32[]{:S(2)}) collective-permute-start(f32[176,512]{1,0:T(8,128)S(1)} %select_select_fusion), channel_id=1, source_target_pairs={{1,0},{2,3},{3,1},{0,2},{5,4},{6,7},{7,5},{4,6},{9,8},{10,11},{11,... | collective-permute-start | bytes 1081352 | tf_op jit(solution)/shard_map/ppermute | solution.py:390
  84.7 5.4 %product.11.refs_3_ = f32[128,1024]{1,0:T(8,128)S(1)} custom-call(s32[1]{0:T(128)} %bitcast.1.ids_ref.refs_0_, bf16[4,4,1024,256]{3,2,1,0:T(8,128)(2,1)} %operator.1.refs_1_, f32[176,512]{1,0:T(8,128)S(1)} %carry.2.refs_2_.refs_4_, f32[176,512]{1,0:T(8,128)S(1)} %collective-permute-done.7.refs_3_.refs_7_, f32[176,512]{1,0:T(8,128)S(1)} %collective-permute-done.6.refs_4_.refs_5_), custom_call_target="tpu_custom_call" | custom-call | flops 17179869184 | bytes 67108864 | tf_op jit(solution)/shard_map/product/pallas_call | solution.py:283
  90.1 3.1 %collective-permute-done.8.refs_2_.refs_6_ = f32[176,512]{1,0:T(8,128)S(1)} collective-permute-done((f32[176,512]{1,0:T(8,128)S(1)}, f32[176,512]{1,0:T(8,128)S(1)}, u32[]{:S(2)}, u32[]{:S(2)}) %collective-permute-start.8) | collective-permute-done | bytes 360480 | tf_op jit(solution)/shard_map/ppermute | solution.py:390
  93.2 0.0 all-to-all-done.3.came_ref
  93.2 0.0 copy-done.1
  93.2 0.7 carry.3.refs_2_
  93.9 2.7 %collective-permute-start.10 = (f32[128,512]{1,0:T(8,128)S(1)}, f32[128,512]{1,0:T(8,128)S(1)}, u32[]{:S(2)}, u32[]{:S(2)}) collective-permute-start(f32[128,512]{1,0:T(8,128)S(1)} %carry.3.refs_2_), channel_id=1, source_target_pairs={{0,1},{1,2},{2,3},{3,0},{4,5},{5,6},{6,7},{7,4},{8,9},{9,10},{10,1... | collective-permute-start | bytes 786440 | tf_op jit(solution)/shard_map/ppermute | solution.py:376
  96.6 1.2 collective-permute-start.9
  97.8 3.9 %product.12 = f32[8,320,128]{2,1,0:T(8,128)} custom-call(s32[1]{0:T(128)} %bitcast.1.ids_ref.refs_0_, bf16[4,4,1024,256]{3,2,1,0:T(8,128)(2,1)} %operator.1.refs_1_, f32[176,512]{1,0:T(8,128)S(1)} %collective-permute-done.8.refs_2_.refs_6_, f32[128,1024]{1,0:T(8,128)S(1)} %product.11.refs_3_, f32[176,512]{1,0:T(8,128)S(1)} %carry.2.refs_2_.refs_4_, ...), custom_call_target="tpu_custom_call" | custom-call | flops 1024 | bytes 1024 | tf_op jit(solution)/shard_map/product/pallas_call | solution.py:283
  101.6 4.4 %all-to-all-start.2 = ((f32[8,320,128]{2,1,0:T(8,128)}), f32[8,320,128]{2,1,0:T(8,128)S(1)}, u32[]{:S(2)}, u32[]{:S(2)}) async-start(f32[8,320,128]{2,1,0:T(8,128)} %product.12), calls=%async_computation.2 | async-start | bytes 2621440 | tf_op jit(solution)/shard_map/all_to_all | solution.py:380
  106.1 0.0 collective-permute-done.10.refs_4_
  106.1 2.2 %collective-permute-done.9.refs_3_ = f32[128,512]{1,0:T(8,128)} collective-permute-done((f32[128,512]{1,0:T(8,128)S(1)}, f32[128,512]{1,0:T(8,128)}, u32[]{:S(2)}, u32[]{:S(2)}) %collective-permute-start.9) | collective-permute-done | bytes 262176 | tf_op jit(solution)/shard_map/ppermute | solution.py:376
  108.2 0.1 select_select_fusion.1
  108.3 0.6 collective-permute-start.11
  108.9 6.3 %product.14.refs_3_ = f32[128,1024]{1,0:T(8,128)S(1)} custom-call(s32[1]{0:T(128)} %bitcast.1.ids_ref.refs_0_, bf16[4,4,1024,256]{3,2,1,0:T(8,128)(2,1)} %operator.1.refs_1_, f32[128,512]{1,0:T(8,128)S(1)} %carry.3.refs_2_, f32[128,512]{1,0:T(8,128)} %collective-permute-done.9.refs_3_, f32[128,512]{1,0:T(8,128)S(1)} %collective-permute-done.10.refs_4_), custom_call_target="tpu_custom_call" | custom-call | flops 17179869184 | bytes 67108864 | tf_op jit(solution)/shard_map/product/pallas_call | solution.py:283
  115.3 1.3 collective-permute-done.11.refs_2_
  116.5 3.5 %product.15 = f32[8,128,128]{2,1,0:T(8,128)} custom-call(s32[1]{0:T(128)} %bitcast.1.ids_ref.refs_0_, bf16[4,4,1024,256]{3,2,1,0:T(8,128)(2,1)} %operator.1.refs_1_, f32[128,512]{1,0:T(8,128)S(1)} %collective-permute-done.11.refs_2_, f32[128,1024]{1,0:T(8,128)S(1)} %product.14.refs_3_), custom_call_target="tpu_custom_call" | custom-call | flops 1024 | bytes 1024 | tf_op jit(solution)/shard_map/product/pallas_call | solution.py:283
  120.1 4.2 %all-to-all-done.2.left_ref.came_ref = f32[8,320,128]{2,1,0:T(8,128)S(1)} async-done(((f32[8,320,128]{2,1,0:T(8,128)}), f32[8,320,128]{2,1,0:T(8,128)S(1)}, u32[]{:S(2)}, u32[]{:S(2)}) %all-to-all-start.2) | async-done | bytes 1310752 | tf_op jit(solution)/shard_map/all_to_all | solution.py:380
  124.3 3.5 %all-to-all-start.4 = ((f32[8,128,128]{2,1,0:T(8,128)}), f32[8,128,128]{2,1,0:T(8,128)S(1)}, u32[]{:S(2)}, u32[]{:S(2)}) async-start(f32[8,128,128]{2,1,0:T(8,128)} %product.15), calls=%async_computation.4 | async-start | bytes 1048576 | tf_op jit(solution)/shard_map/all_to_all | solution.py:380
  127.8 1.1 assemble.1
  128.9 8.5 %all-to-all-done.4.right_ref = f32[8,128,128]{2,1,0:T(8,128)S(1)} async-done(((f32[8,128,128]{2,1,0:T(8,128)}), f32[8,128,128]{2,1,0:T(8,128)S(1)}, u32[]{:S(2)}, u32[]{:S(2)}) %all-to-all-start.4) | async-done | bytes 524320 | tf_op jit(solution)/shard_map/all_to_all | solution.py:380
  137.5 1.8 %finish.1 = f32[512,256]{1,0:T(8,128)} custom-call(s32[8]{0:T(128)S(1)} %bitcast.4, f32[256,512]{1,0:T(8,128)S(1)} %get-tuple-element.17.base_ref, f32[8,320,128]{2,1,0:T(8,128)S(1)} %all-to-all-done.2.left_ref.came_ref, f32[8,128,128]{2,1,0:T(8,128)S(1)} %all-to-all-done.4.right_ref), custom_call_target="tpu_custom_call" | custom-call | flops 1024 | bytes 1024 | tf_op jit(solution)/shard_map/finish/pallas_call | solution.py:339
Async XLA Ops:
  2.4 20.1 %collective-permute-start = (f32[128,512]{1,0:T(8,128)S(1)}, f32[128,512]{1,0:T(8,128)S(1)}, u32[]{:S(2)}, u32[]{:S(2)}) collective-permute-start(f32[128,512]{1,0:T(8,128)S(1)} %get-tuple-element.16.first_ref.refs_2_), channel_id=1, source_target_pairs={{0,1},{1,2},{2,3},{3,0},{4,5},{5,6},{6,7},{7,4},{8,9},{9,10},{10,1... | collective-permute-start | bytes 786440 | tf_op jit(solution)/shard_map/ppermute | solution.py:376
  5.5 20.6 %collective-permute-start.1 = (f32[128,512]{1,0:T(8,128)S(1)}, f32[128,512]{1,0:T(8,128)S(1)}, u32[]{:S(2)}, u32[]{:S(2)}) collective-permute-start(f32[128,512]{1,0:T(8,128)S(1)} %get-tuple-element.16.first_ref.refs_2_), channel_id=1, source_target_pairs={{0,3},{1,0},{2,1},{3,2},{4,7},{5,4},{6,5},{7,6},{8,11},{9,8},{10,9... | collective-permute-start | bytes 786440 | tf_op jit(solution)/shard_map/ppermute | solution.py:376
  12.4 0.7 copy-start
  13.2 9.3 %copy-start.2 = (f32[128,512]{1,0:T(8,128)}, f32[128,512]{1,0:T(8,128)S(1)}, u32[]{:S(2)}) copy-start(f32[128,512]{1,0:T(8,128)S(1)} %get-tuple-element.24.base_ref) | copy-start | bytes 786436
  22.5 28.9 %all-to-all-start.1 = ((f32[8,192,128]{2,1,0:T(8,128)}), f32[8,192,128]{2,1,0:T(8,128)S(1)}, u32[]{:S(2)}, u32[]{:S(2)}) async-start(f32[8,192,128]{2,1,0:T(8,128)} %get-tuple-element.25), calls=%async_computation.1 | async-start | bytes 1572864 | tf_op jit(solution)/shard_map/all_to_all | solution.py:380
  26.1 8.7 %collective-permute-start.2 = (f32[128,512]{1,0:T(8,128)S(1)}, f32[128,512]{1,0:T(8,128)S(1)}, u32[]{:S(2)}, u32[]{:S(2)}) collective-permute-start(f32[128,512]{1,0:T(8,128)S(1)} %select_select_fusion.3), channel_id=1, source_target_pairs={{1,0},{2,3},{3,1},{0,2},{5,4},{6,7},{7,5},{4,6},{9,8},{10,11},{11,... | collective-permute-start | bytes 786440 | tf_op jit(solution)/shard_map/ppermute | solution.py:390
  34.8 11.1 %collective-permute-start.4 = (f32[128,512]{1,0:T(8,128)S(1)}, f32[128,512]{1,0:T(8,128)S(1)}, u32[]{:S(2)}, u32[]{:S(2)}) collective-permute-start(f32[128,512]{1,0:T(8,128)S(1)} %get-tuple-element.22.refs_2_), channel_id=1, source_target_pairs={{0,1},{1,2},{2,3},{3,0},{4,5},{5,6},{6,7},{7,4},{8,9},{9,10},{10,1... | collective-permute-start | bytes 786440 | tf_op jit(solution)/shard_map/ppermute | solution.py:376
  36.9 13.0 %collective-permute-start.3 = (f32[128,512]{1,0:T(8,128)S(1)}, f32[128,512]{1,0:T(8,128)S(1)}, u32[]{:S(2)}, u32[]{:S(2)}) collective-permute-start(f32[128,512]{1,0:T(8,128)S(1)} %get-tuple-element.22.refs_2_), channel_id=1, source_target_pairs={{0,3},{1,0},{2,1},{3,2},{4,7},{5,4},{6,5},{7,6},{8,11},{9,8},{10,9... | collective-permute-start | bytes 786440 | tf_op jit(solution)/shard_map/ppermute | solution.py:376
  50.7 9.6 %collective-permute-start.5 = (f32[128,512]{1,0:T(8,128)}, f32[128,512]{1,0:T(8,128)S(1)}, u32[]{:S(2)}, u32[]{:S(2)}) collective-permute-start(f32[128,512]{1,0:T(8,128)} %select_select_fusion.2), channel_id=1, source_target_pairs={{1,0},{2,3},{3,1},{0,2},{5,4},{6,7},{7,5},{4,6},{9,8},{10,11},{11,... | collective-permute-start | bytes 786440 | tf_op jit(solution)/shard_map/ppermute | solution.py:390
  51.3 13.4 %all-to-all-start = ((f32[8,128,128]{2,1,0:T(8,128)}), f32[8,128,128]{2,1,0:T(8,128)S(1)}, u32[]{:S(2)}, u32[]{:S(2)}) async-start(f32[8,128,128]{2,1,0:T(8,128)} %product.10), calls=%async_computation | async-start | bytes 1048576 | tf_op jit(solution)/shard_map/all_to_all | solution.py:380
  55.0 9.7 %copy-start.4 = (s32[1,8,1]{1,2,0:T(1,128)S(1)}, s32[1,8,1]{1,2,0:T(1,128)}, u32[]{:S(2)}) copy-start(s32[1,8,1]{1,2,0:T(1,128)} %param.20) | copy-start | bytes 100
  64.7 1.0 copy-start.3
  66.4 13.2 %collective-permute-start.7 = (f32[176,512]{1,0:T(8,128)S(1)}, f32[176,512]{1,0:T(8,128)S(1)}, u32[]{:S(2)}, u32[]{:S(2)}) collective-permute-start(f32[176,512]{1,0:T(8,128)S(1)} %carry.2.refs_2_.refs_4_), channel_id=1, source_target_pairs={{0,1},{1,2},{2,3},{3,0},{4,5},{5,6},{6,7},{7,4},{8,9},{9,10},{10,1... | collective-permute-start | bytes 1081352 | tf_op jit(solution)/shard_map/ppermute | solution.py:376
  67.8 15.3 %collective-permute-start.6 = (f32[176,512]{1,0:T(8,128)S(1)}, f32[176,512]{1,0:T(8,128)S(1)}, u32[]{:S(2)}, u32[]{:S(2)}) collective-permute-start(f32[176,512]{1,0:T(8,128)S(1)} %carry.2.refs_2_.refs_4_), channel_id=1, source_target_pairs={{0,3},{1,0},{2,1},{3,2},{4,7},{5,4},{6,5},{7,6},{8,11},{9,8},{10,9... | collective-permute-start | bytes 1081352 | tf_op jit(solution)/shard_map/ppermute | solution.py:376
  73.8 19.4 %all-to-all-start.3 = ((f32[8,128,128]{2,1,0:T(8,128)}), f32[8,128,128]{2,1,0:T(8,128)S(1)}, u32[]{:S(2)}, u32[]{:S(2)}) async-start(f32[8,128,128]{2,1,0:T(8,128)} %product.13), calls=%async_computation.3 | async-start | bytes 1048576 | tf_op jit(solution)/shard_map/all_to_all | solution.py:380
  83.2 10.0 %copy-start.1 = (f32[128,512]{1,0:T(8,128)S(1)}, f32[128,512]{1,0:T(8,128)}, u32[]{:S(2)}) copy-start(f32[128,512]{1,0:T(8,128)} %copy-done) | copy-start | bytes 786436
  83.2 10.0 %collective-permute-start.8 = (f32[176,512]{1,0:T(8,128)S(1)}, f32[176,512]{1,0:T(8,128)S(1)}, u32[]{:S(2)}, u32[]{:S(2)}) collective-permute-start(f32[176,512]{1,0:T(8,128)S(1)} %select_select_fusion), channel_id=1, source_target_pairs={{1,0},{2,3},{3,1},{0,2},{5,4},{6,7},{7,5},{4,6},{9,8},{10,11},{11,... | collective-permute-start | bytes 1081352 | tf_op jit(solution)/shard_map/ppermute | solution.py:390
  93.9 12.2 %collective-permute-start.10 = (f32[128,512]{1,0:T(8,128)S(1)}, f32[128,512]{1,0:T(8,128)S(1)}, u32[]{:S(2)}, u32[]{:S(2)}) collective-permute-start(f32[128,512]{1,0:T(8,128)S(1)} %carry.3.refs_2_), channel_id=1, source_target_pairs={{0,1},{1,2},{2,3},{3,0},{4,5},{5,6},{6,7},{7,4},{8,9},{9,10},{10,1... | collective-permute-start | bytes 786440 | tf_op jit(solution)/shard_map/ppermute | solution.py:376
  96.6 11.7 %collective-permute-start.9 = (f32[128,512]{1,0:T(8,128)S(1)}, f32[128,512]{1,0:T(8,128)}, u32[]{:S(2)}, u32[]{:S(2)}) collective-permute-start(f32[128,512]{1,0:T(8,128)S(1)} %carry.3.refs_2_), channel_id=1, source_target_pairs={{0,3},{1,0},{2,1},{3,2},{4,7},{5,4},{6,5},{7,6},{8,11},{9,8},{10,9... | collective-permute-start | bytes 786440 | tf_op jit(solution)/shard_map/ppermute | solution.py:376
  101.6 22.6 %all-to-all-start.2 = ((f32[8,320,128]{2,1,0:T(8,128)}), f32[8,320,128]{2,1,0:T(8,128)S(1)}, u32[]{:S(2)}, u32[]{:S(2)}) async-start(f32[8,320,128]{2,1,0:T(8,128)} %product.12), calls=%async_computation.2 | async-start | bytes 2621440 | tf_op jit(solution)/shard_map/all_to_all | solution.py:380
  108.3 8.2 %collective-permute-start.11 = (f32[128,512]{1,0:T(8,128)S(1)}, f32[128,512]{1,0:T(8,128)S(1)}, u32[]{:S(2)}, u32[]{:S(2)}) collective-permute-start(f32[128,512]{1,0:T(8,128)S(1)} %select_select_fusion.1), channel_id=1, source_target_pairs={{1,0},{2,3},{3,1},{0,2},{5,4},{6,7},{7,5},{4,6},{9,8},{10,11},{11,... | collective-permute-start | bytes 786440 | tf_op jit(solution)/shard_map/ppermute | solution.py:390
  124.3 13.2 %all-to-all-start.4 = ((f32[8,128,128]{2,1,0:T(8,128)}), f32[8,128,128]{2,1,0:T(8,128)S(1)}, u32[]{:S(2)}, u32[]{:S(2)}) async-start(f32[8,128,128]{2,1,0:T(8,128)} %product.15), calls=%async_computation.4 | async-start | bytes 1048576 | tf_op jit(solution)/shard_map/all_to_all | solution.py:380

commit v8 on v7

--- a/solution.py
+++ b/solution.py
@@ -140,10 +140,14 @@
     )(first, *in_hbm(grad_out, relu_mask, cheb_weight, b0, b1, b2))
 
 
-def operator_kernel(
-    n_col, ids_ref, live_ref, rows_hbm, slots_hbm, values_ref, out_ref,
-    tiles, acc, lists, counts, rows, slots, sems, small_sems,
-):
+def stacked(field):
+    high, low = split(field)
+    return jnp.concatenate([jnp.concatenate([x, x], axis=1) for x in (high, low)], axis=0)
+
+
+def operator_kernel(n_col, origins, ids_ref, live_ref, rows_hbm, slots_hbm, values_ref, *refs):
+    fields, refs = refs[: len(origins)], refs[len(origins) :]
+    out_ref, total_ref, tiles, acc, lists, counts, rows, slots, sems, small_sems = refs
     origin = pl.program_id(0)
     size = TILES_DEV // GROUPS
 
@@ -189,20 +193,36 @@
         return carry
 
     lax.fori_loop(0, counts[origin], add, 0)
-    for p in range(acc.shape[0]):
+    pairs = acc.shape[0]
+    for p in range(pairs):
         high, low = split(acc[p])
         out_ref[0, p, :NODES_DEV, :] = high
         out_ref[0, p, NODES_DEV:, :] = low
 
-
-def build_operator(n_row, n_col, ids, live, rows, slots, values):
+    for k, field in zip(origins, fields):
+
+        @pl.when(origin == k)
+        def _():
+            left = stacked(field[...])
+            for p in range(pairs):
+                part = jnp.dot(left, out_ref[0, p], preferred_element_type=F32)
+                summed = part[:H] + part[H:]
+                here = slice(p * WIDE, (p + 1) * WIDE)
+                total_ref[:, here] = summed if k == 0 else total_ref[:, here] + summed
+
+
+def build_operator(n_row, n_col, ids, live, rows, slots, values, pairs):
     part = (n_row // 2, 2 * NODES_DEV, WIDE)
-    return pl.pallas_call(
-        functools.partial(operator_kernel, n_col),
+    origins, fields = zip(*pairs)
+    return pl.pallas_call(
+        functools.partial(operator_kernel, n_col, origins),
         grid=(n_col,),
-        in_specs=[SMEM] * 2 + [HBM] * 3,
-        out_specs=pl.BlockSpec((1,) + part, lambda s: (s, 0, 0, 0)),
-        out_shape=pltpu.HBM((n_col,) + part, BF16),
+        in_specs=[SMEM] * 2 + [HBM] * 3 + [pl.BlockSpec((H, NODES_DEV), lambda s: (0, 0))] * len(fields),
+        out_specs=[
+            pl.BlockSpec((1,) + part, lambda s: (s, 0, 0, 0)),
+            pl.BlockSpec((H, n_row * TB), lambda s: (0, 0)),
+        ],
+        out_shape=[pltpu.HBM((n_col,) + part, BF16), jax.ShapeDtypeStruct((H, n_row * TB), F32)],
         scratch_shapes=[
             pltpu.VMEM((TILES_DEV, TB, TB), F32),
             pltpu.VMEM((n_row // 2, NODES_DEV, WIDE), F32),
@@ -214,9 +234,9 @@
             pltpu.SemaphoreType.DMA((2,)),
         ],
         compiler_params=params(40),
-        cost_estimate=LIGHT,
+        cost_estimate=HEAVY,
         name="operator",
-    )(ids, live, *in_hbm(rows, slots, values))
+    )(ids, live, *in_hbm(rows, slots, values), *fields)
 
 
 def product_kernel(n_row, n_col, origins, has_prev, last, n_carriers, *refs):
@@ -234,10 +254,7 @@
     for p in range(n_row // 2):
         for k in range(n):
             copy(k, p).start()
-    left = []
-    for field in fields:
-        high, low = split(field[:H, :])
-        left.append(jnp.concatenate([jnp.concatenate([x, x], axis=1) for x in (high, low)], axis=0))
+    left = [stacked(field[:H, :]) for field in fields]
     if n_carriers:
         ordered = refs[3]
         for k in range(n_col):
@@ -390,14 +407,14 @@
     return lax.ppermute(sent, "col", [(1, 0), (2, 3), (3, 1), (0, 2)])
 
 
-def gather(n_col, field, side, *done):
+def gather(n_col, field, side):
     long = n_col // 2
     short = n_col - 1 - long
     ahead, behind = field, field
     steps = [[(0, field)]]
     for s in range(1, long + 1):
         if s == 2:
-            ahead = after(ahead, behind, *done)
+            ahead = after(ahead, behind)
         if s == 2 and n_col == 4:
             ahead = opposite(field, ahead, behind) if side > 0 else opposite(field, behind, ahead)
         else:
@@ -410,9 +427,8 @@
     return steps
 
 
-def early(n_row, n_col, ids, operator, steps):
-    pairs = [pair for step in steps[:-1] for pair in step]
-    total = None
+def early(n_row, n_col, ids, operator, steps, total=None, done=0):
+    pairs = [pair for step in steps[:-1] for pair in step][done:]
     for begin in range(0, len(pairs), 3):
         origins, fields = zip(*pairs[begin : begin + 3])
         total = product(n_row, n_col, ids, origins, operator, fields, total, False)
@@ -446,14 +462,17 @@
     one_left, one_right, diff, pieces = local_terms(
         n_row, left, grad_out, relu_mask, cheb_weight, basis_zero, basis_one, basis_two
     )
-    operator = build_operator(n_row, n_col, ids, live_tiles, tile_rows, tile_slots, tile_values)
+    steps = gather(n_col, left, 1)
+    first = steps[0] + steps[1] if len(steps) > 2 else steps[0]
+    operator, left_early = build_operator(
+        n_row, n_col, ids, live_tiles, tile_rows, tile_slots, tile_values, first
+    )
+    pieces = exchange(pieces)
     common = (n_row, n_col, ids, operator)
 
-    steps = gather(n_col, left, 1, operator, pieces)
-    pieces = exchange(after(pieces, steps[1][0][1]))
-    left_early = early(*common, steps)
+    left_early = early(*common, steps, left_early, len(first))
     right_steps = gather(n_col, after(right, left_early, steps[-1][0][1]), -1)
-    left_came = exchange(final(*common, steps, left_early))
+    left_came = exchange(final(*common, steps, after(left_early, pieces)))
     right_early = early(*common, right_steps)
 
     left_carried = carry(n_row, owners, after(one_left, right_early, right_steps[-1][0][1]), left_came, pieces)

time: 140 us -> 132 us (0.943)
  waiting for transfers between devices: 38.7 us -> 30.7 us
  starting transfers between devices: 39.9 us -> 45 us
  Pallas kernels: 56.5 us -> 52.3 us
    ppermute x8, waiting for transfers between devices: 15.8 us -> 9.61 us  [shift(): lax.ppermute(x, 'col', [(c, (c + step) % n_col) for c in range(n_col)])]
    all_to_all x5, starting transfers between devices: 18.6 us -> 24.4 us  [exchange(): lax.all_to_all(pieces, 'row', split_axis=0, concat_axis=0, tiled=True)]
    pallas_call x8 -> x7, Pallas kernels: 37 us -> 31.6 us  [product(): pl.pallas_call(functools.partial(product_kernel, n_row, n_col, origins, h...]
    all_to_all x5, waiting for transfers between devices: 17 us -> 14.3 us  [exchange(): lax.all_to_all(pieces, 'row', split_axis=0, concat_axis=0, tiled=True)]
  transfers between devices with their start and end apart: 17 -> 17, of which waited for: 11 -> 8; matrix products, arithmetic and copies ran while one was open for 1% -> 0% of each run, Pallas kernels for 37% -> 36%
where the time goes in v8:
time: 132 us; the launch traced here: 131 us
  Pallas kernels  52.3 us (40%)
  starting transfers between devices  45 us (34%)
  waiting for transfers between devices  30.7 us (23%)
  local copies, waits for them, and re-layouts  1.68 us (1%)
  between operations  1.47 us (1%)
    pallas_call x7, Pallas kernels, product(): pl.pallas_call(functools.partial(product_kernel, n_row, n_col, origins, h...  31.6 us
    all_to_all x5, starting transfers between devices, exchange(): lax.all_to_all(pieces, 'row', split_axis=0, concat_axis=0, tiled=True)  24.4 us
    ppermute x8, starting transfers between devices, shift(): lax.ppermute(x, 'col', [(c, (c + step) % n_col) for c in range(n_col)])  16.7 us
    all_to_all x5, waiting for transfers between devices, exchange(): lax.all_to_all(pieces, 'row', split_axis=0, concat_axis=0, tiled=True)  14.3 us
    pallas_call x1, Pallas kernels, build_operator(): pl.pallas_call(functools.partial(operator_kernel, n_col, origins), grid=(...  9.89 us
    ppermute x8, waiting for transfers between devices, shift(): lax.ppermute(x, 'col', [(c, (c + step) % n_col) for c in range(n_col)])  9.61 us
    ppermute x4, waiting for transfers between devices, opposite(): return lax.ppermute(sent, 'col', [(1, 0), (2, 3), (3, 1), (0, 2)])  6.76 us
    pallas_call x1, Pallas kernels, local_terms(): pl.pallas_call(functools.partial(local_kernel, n_row), in_specs=[pl.Block...  4.86 us
  transfers between devices with their start and end apart: 17, of which 8 were waited for; matrix products, arithmetic and copies ran while one was open for 0% of the time, Pallas kernels for 36%

profile of v8, /device:TPU:0, one launch (start us, length us, event | category | flops | bytes accessed | tf_op | source)
XLA Modules:
  0.0 131.5 jit_solution(9984039468165630302)
XLA Ops:
  0.6 1.7 %term_two.1 = (f32[128,512]{1,0:T(8,128)S(1)}, f32[128,512]{1,0:T(8,128)S(1)}) custom-call(f32[512,256]{1,0:T(8,128)} %grad_hbm.3, s32[512,256]{1,0:T(8,128)} %mask_hbm.3, f32[3,256,256]{2,1,0:T(8,128)} %weight_hbm.3), custom_call_target="tpu_custom_call" | custom-call | flops 1024 | bytes 1024 | tf_op jit(solution)/shard_map/term_two/pallas_call | solution.py:75
  2.4 5.1 %collective-permute-start.1 = (f32[128,512]{1,0:T(8,128)S(1)}, f32[128,512]{1,0:T(8,128)S(1)}, u32[]{:S(2)}, u32[]{:S(2)}) collective-permute-start(f32[128,512]{1,0:T(8,128)S(1)} %get-tuple-element.18.first_ref.refs_0_), channel_id=1, source_target_pairs={{0,3},{1,0},{2,1},{3,2},{4,7},{5,4},{6,5},{7,6},{8,11},{9,8},{10,9... | collective-permute-start | bytes 786440 | tf_op jit(solution)/shard_map/ppermute | solution.py:393
  7.5 0.0 collective-permute-start
  7.5 4.9 %local_terms.1 = (f32[128,512]{1,0:T(8,128)S(1)}, f32[128,512]{1,0:T(8,128)S(1)}, f32[256,512]{1,0:T(8,128)S(1)}, f32[8,192,128]{2,1,0:T(8,128)}) custom-call(f32[128,512]{1,0:T(8,128)S(1)} %get-tuple-element.18.first_ref.refs_0_, f32[512,256]{1,0:T(8,128)} %grad_hbm.3, s32[512,256]{1,0:T(8,128)} %mask_hbm.3, f32[3,256,256]{2,1,0:T(8,128)} %weight_hbm.3, ...), custom_call_target="tpu_custom_call" | custom-call | flops 1024 | bytes 1024 | tf_op jit(solution)/shard_map/local_terms/pallas_call | solution.py:120
  12.4 0.0 copy-start
  12.4 0.7 copy-done
  13.1 0.0 copy-start.2
  13.1 3.7 %all-to-all-start = ((f32[8,192,128]{2,1,0:T(8,128)}), f32[8,192,128]{2,1,0:T(8,128)S(1)}, u32[]{:S(2)}, u32[]{:S(2)}) async-start(f32[8,192,128]{2,1,0:T(8,128)} %get-tuple-element.28), calls=%async_computation | async-start | bytes 1572864 | tf_op jit(solution)/shard_map/all_to_all | solution.py:397
  17.5 0.0 collective-permute-done.1.refs_2_
  17.5 2.1 %collective-permute-done.refs_1_ = f32[128,512]{1,0:T(8,128)S(1)} collective-permute-done((f32[128,512]{1,0:T(8,128)S(1)}, f32[128,512]{1,0:T(8,128)S(1)}, u32[]{:S(2)}, u32[]{:S(2)}) %collective-permute-start) | collective-permute-done | bytes 262176 | tf_op jit(solution)/shard_map/ppermute | solution.py:393
  19.6 0.0 copy-done.2
  19.6 0.1 select_select_fusion.3
  19.6 0.8 collective-permute-start.2
  20.4 9.9 %operator.1 = (bf16[4,4,1024,256]{3,2,1,0:T(8,128)(2,1)}, f32[128,1024]{1,0:T(8,128)S(1)}) custom-call(s32[1]{0:T(128)} %bitcast.1.ids_ref.refs_0_, s32[1]{0:T(128)S(6)} %copy.13.live_ref, s32[1,128]{1,0:T(1,128)} %rows_hbm.1, s32[1,128]{1,0:T(1,128)} %slots_hbm.1, f32[1,128,128,128]{3,2,1,0:T(8,128)} %values_ref.1, ...), custom_call_target="tpu_custom_call" | custom-call | flops 17179869184 | bytes 67108864 | tf_op jit(solution)/shard_map/operator/pallas_call | solution.py:217
  30.3 0.0 collective-permute-done.2.refs_2_
  30.3 3.3 %collective-permute-start.4 = (f32[128,512]{1,0:T(8,128)S(1)}, f32[128,512]{1,0:T(8,128)S(1)}, u32[]{:S(2)}, u32[]{:S(2)}) collective-permute-start(f32[128,512]{1,0:T(8,128)S(1)} %get-tuple-element.25.refs_2_), channel_id=1, source_target_pairs={{0,1},{1,2},{2,3},{3,0},{4,5},{5,6},{6,7},{7,4},{8,9},{9,10},{10,1... | collective-permute-start | bytes 786440 | tf_op jit(solution)/shard_map/ppermute | solution.py:393
  33.6 0.6 collective-permute-start.3
  34.2 0.0 all-to-all-done.refs_0_
  34.2 3.6 %product.8 = f32[8,128,128]{2,1,0:T(8,128)} custom-call(s32[1]{0:T(128)} %bitcast.1.ids_ref.refs_0_, bf16[4,4,1024,256]{3,2,1,0:T(8,128)(2,1)} %get-tuple-element.20.refs_1_, f32[128,512]{1,0:T(8,128)S(1)} %collective-permute-done.2.refs_2_, f32[128,1024]{1,0:T(8,128)S(1)} %get-tuple-element.29.refs_3_), custom_call_target="tpu_custom_call" | custom-call | flops 1024 | bytes 1024 | tf_op jit(solution)/shard_map/product/pallas_call | solution.py:300
  37.8 4.2 %all-to-all-start.1 = ((f32[8,128,128]{2,1,0:T(8,128)}), f32[8,128,128]{2,1,0:T(8,128)S(1)}, u32[]{:S(2)}, u32[]{:S(2)}) async-start(f32[8,128,128]{2,1,0:T(8,128)} %product.8), calls=%async_computation.1 | async-start | bytes 1048576 | tf_op jit(solution)/shard_map/all_to_all | solution.py:397
  42.0 0.0 collective-permute-done.4.refs_4_
  42.0 2.4 %collective-permute-done.3.refs_3_ = f32[128,512]{1,0:T(8,128)S(1)} collective-permute-done((f32[128,512]{1,0:T(8,128)S(1)}, f32[128,512]{1,0:T(8,128)S(1)}, u32[]{:S(2)}, u32[]{:S(2)}) %collective-permute-start.3) | collective-permute-done | bytes 262176 | tf_op jit(solution)/shard_map/ppermute | solution.py:393
  44.4 0.1 select_select_fusion.2
  44.5 0.0 copy-start.4
  44.5 1.5 %collective-permute-start.5 = (f32[128,512]{1,0:T(8,128)S(1)}, f32[128,512]{1,0:T(8,128)S(1)}, u32[]{:S(2)}, u32[]{:S(2)}) collective-permute-start(f32[128,512]{1,0:T(8,128)S(1)} %select_select_fusion.2), channel_id=1, source_target_pairs={{1,0},{2,3},{3,1},{0,2},{5,4},{6,7},{7,5},{4,6},{9,8},{10,11},{11,... | collective-permute-start | bytes 786440 | tf_op jit(solution)/shard_map/ppermute | solution.py:407
  46.0 5.4 %product.7.refs_3_ = f32[128,1024]{1,0:T(8,128)S(1)} custom-call(s32[1]{0:T(128)} %bitcast.1.ids_ref.refs_0_, bf16[4,4,1024,256]{3,2,1,0:T(8,128)(2,1)} %get-tuple-element.20.refs_1_, f32[128,512]{1,0:T(8,128)S(1)} %get-tuple-element.25.refs_2_, f32[128,512]{1,0:T(8,128)S(1)} %collective-permute-done.3.refs_3_, f32[128,512]{1,0:T(8,128)S(1)} %collective-permute-done.4.refs_4_), custom_call_target="tpu_custom_call" | custom-call | flops 17179869184 | bytes 67108864 | tf_op jit(solution)/shard_map/product/pallas_call | solution.py:300
  51.4 0.9 collective-permute-done.5.refs_2_
  52.3 0.0 all-to-all-done.1.came_ref
  52.3 0.0 copy-done.4
  52.3 0.0 copy-start.3
  52.3 0.9 copy-done.3
  53.2 0.7 carry.2.refs_2_.refs_4_
  53.9 1.9 %collective-permute-start.7 = (f32[176,512]{1,0:T(8,128)S(1)}, f32[176,512]{1,0:T(8,128)S(1)}, u32[]{:S(2)}, u32[]{:S(2)}) collective-permute-start(f32[176,512]{1,0:T(8,128)S(1)} %carry.2.refs_2_.refs_4_), channel_id=1, source_target_pairs={{0,1},{1,2},{2,3},{3,0},{4,5},{5,6},{6,7},{7,4},{8,9},{9,10},{10,1... | collective-permute-start | bytes 1081352 | tf_op jit(solution)/shard_map/ppermute | solution.py:393
  55.9 1.9 %collective-permute-start.6 = (f32[176,512]{1,0:T(8,128)S(1)}, f32[176,512]{1,0:T(8,128)S(1)}, u32[]{:S(2)}, u32[]{:S(2)}) collective-permute-start(f32[176,512]{1,0:T(8,128)S(1)} %carry.2.refs_2_.refs_4_), channel_id=1, source_target_pairs={{0,3},{1,0},{2,1},{3,2},{4,7},{5,4},{6,5},{7,6},{8,11},{9,8},{10,9... | collective-permute-start | bytes 1081352 | tf_op jit(solution)/shard_map/ppermute | solution.py:393
  57.8 3.5 %product.11 = f32[8,128,128]{2,1,0:T(8,128)} custom-call(s32[1]{0:T(128)} %bitcast.1.ids_ref.refs_0_, bf16[4,4,1024,256]{3,2,1,0:T(8,128)(2,1)} %get-tuple-element.20.refs_1_, f32[128,512]{1,0:T(8,128)S(1)} %collective-permute-done.5.refs_2_, f32[128,1024]{1,0:T(8,128)S(1)} %product.7.refs_3_), custom_call_target="tpu_custom_call" | custom-call | flops 1024 | bytes 1024 | tf_op jit(solution)/shard_map/product/pallas_call | solution.py:300
  61.4 6.1 %all-to-all-start.3 = ((f32[8,128,128]{2,1,0:T(8,128)}), f32[8,128,128]{2,1,0:T(8,128)S(1)}, u32[]{:S(2)}, u32[]{:S(2)}) async-start(f32[8,128,128]{2,1,0:T(8,128)} %product.11), calls=%async_computation.3 | async-start | bytes 1048576 | tf_op jit(solution)/shard_map/all_to_all | solution.py:397
  67.4 0.0 collective-permute-done.7.refs_3_.refs_7_
  67.4 5.1 %collective-permute-done.6.refs_4_.refs_5_ = f32[176,512]{1,0:T(8,128)S(1)} collective-permute-done((f32[176,512]{1,0:T(8,128)S(1)}, f32[176,512]{1,0:T(8,128)S(1)}, u32[]{:S(2)}, u32[]{:S(2)}) %collective-permute-start.6) | collective-permute-done | bytes 360480 | tf_op jit(solution)/shard_map/ppermute | solution.py:393
  72.5 0.1 select_select_fusion
  72.6 0.0 copy-start.1
  72.6 0.6 collective-permute-start.8
  73.2 5.4 %product.9.refs_3_ = f32[128,1024]{1,0:T(8,128)S(1)} custom-call(s32[1]{0:T(128)} %bitcast.1.ids_ref.refs_0_, bf16[4,4,1024,256]{3,2,1,0:T(8,128)(2,1)} %get-tuple-element.20.refs_1_, f32[176,512]{1,0:T(8,128)S(1)} %carry.2.refs_2_.refs_4_, f32[176,512]{1,0:T(8,128)S(1)} %collective-permute-done.7.refs_3_.refs_7_, ...), custom_call_target="tpu_custom_call" | custom-call | flops 17179869184 | bytes 67108864 | tf_op jit(solution)/shard_map/product/pallas_call | solution.py:300
  78.6 4.4 %collective-permute-done.8.refs_2_.refs_6_ = f32[176,512]{1,0:T(8,128)S(1)} collective-permute-done((f32[176,512]{1,0:T(8,128)S(1)}, f32[176,512]{1,0:T(8,128)S(1)}, u32[]{:S(2)}, u32[]{:S(2)}) %collective-permute-start.8) | collective-permute-done | bytes 360480 | tf_op jit(solution)/shard_map/ppermute | solution.py:407
  83.0 0.0 all-to-all-done.3.came_ref
  83.0 0.0 copy-done.1
  83.0 0.7 carry.3.refs_2_
  83.7 1.4 %collective-permute-start.10 = (f32[128,512]{1,0:T(8,128)S(1)}, f32[128,512]{1,0:T(8,128)S(1)}, u32[]{:S(2)}, u32[]{:S(2)}) collective-permute-start(f32[128,512]{1,0:T(8,128)S(1)} %carry.3.refs_2_), channel_id=1, source_target_pairs={{0,1},{1,2},{2,3},{3,0},{4,5},{5,6},{6,7},{7,4},{8,9},{9,10},{10,1... | collective-permute-start | bytes 786440 | tf_op jit(solution)/shard_map/ppermute | solution.py:393
  85.1 2.5 %collective-permute-start.9 = (f32[128,512]{1,0:T(8,128)S(1)}, f32[128,512]{1,0:T(8,128)}, u32[]{:S(2)}, u32[]{:S(2)}) collective-permute-start(f32[128,512]{1,0:T(8,128)S(1)} %carry.3.refs_2_), channel_id=1, source_target_pairs={{0,3},{1,0},{2,1},{3,2},{4,7},{5,4},{6,5},{7,6},{8,11},{9,8},{10,9... | collective-permute-start | bytes 786440 | tf_op jit(solution)/shard_map/ppermute | solution.py:393
  87.6 3.9 %product.10 = f32[8,320,128]{2,1,0:T(8,128)} custom-call(s32[1]{0:T(128)} %bitcast.1.ids_ref.refs_0_, bf16[4,4,1024,256]{3,2,1,0:T(8,128)(2,1)} %get-tuple-element.20.refs_1_, f32[176,512]{1,0:T(8,128)S(1)} %collective-permute-done.8.refs_2_.refs_6_, f32[128,1024]{1,0:T(8,128)S(1)} %product.9.refs_3_, f32[176,512]{1,0:T(8,128)S(1)} %carry.2.refs_2_.refs_4_, ...), custom_call_target="tpu_custom_call" | custom-call | flops 1024 | bytes 1024 | tf_op jit(solution)/shard_map/product/pallas_call | solution.py:300
  91.4 6.9 %all-to-all-start.2 = ((f32[8,320,128]{2,1,0:T(8,128)}), f32[8,320,128]{2,1,0:T(8,128)S(1)}, u32[]{:S(2)}, u32[]{:S(2)}) async-start(f32[8,320,128]{2,1,0:T(8,128)} %product.10), calls=%async_computation.2 | async-start | bytes 2621440 | tf_op jit(solution)/shard_map/all_to_all | solution.py:397
  98.3 0.0 collective-permute-done.10.refs_4_
  98.3 0.0 collective-permute-done.9.refs_3_
  98.3 0.1 select_select_fusion.1
  98.4 0.9 collective-permute-start.11
  99.4 6.3 %product.12.refs_3_ = f32[128,1024]{1,0:T(8,128)S(1)} custom-call(s32[1]{0:T(128)} %bitcast.1.ids_ref.refs_0_, bf16[4,4,1024,256]{3,2,1,0:T(8,128)(2,1)} %get-tuple-element.20.refs_1_, f32[128,512]{1,0:T(8,128)S(1)} %carry.3.refs_2_, f32[128,512]{1,0:T(8,128)} %collective-permute-done.9.refs_3_, f32[128,512]{1,0:T(8,128)S(1)} %collective-permute-done.10.refs_4_), custom_call_target="tpu_custom_call" | custom-call | flops 17179869184 | bytes 67108864 | tf_op jit(solution)/shard_map/product/pallas_call | solution.py:300
  105.7 1.5 %collective-permute-done.11.refs_2_ = f32[128,512]{1,0:T(8,128)S(1)} collective-permute-done((f32[128,512]{1,0:T(8,128)S(1)}, f32[128,512]{1,0:T(8,128)S(1)}, u32[]{:S(2)}, u32[]{:S(2)}) %collective-permute-start.11) | collective-permute-done | bytes 262176 | tf_op jit(solution)/shard_map/ppermute | solution.py:407
  107.2 3.5 %product.13 = f32[8,128,128]{2,1,0:T(8,128)} custom-call(s32[1]{0:T(128)} %bitcast.1.ids_ref.refs_0_, bf16[4,4,1024,256]{3,2,1,0:T(8,128)(2,1)} %get-tuple-element.20.refs_1_, f32[128,512]{1,0:T(8,128)S(1)} %collective-permute-done.11.refs_2_, f32[128,1024]{1,0:T(8,128)S(1)} %product.12.refs_3_), custom_call_target="tpu_custom_call" | custom-call | flops 1024 | bytes 1024 | tf_op jit(solution)/shard_map/product/pallas_call | solution.py:300
  110.7 5.8 %all-to-all-done.2.left_ref.came_ref = f32[8,320,128]{2,1,0:T(8,128)S(1)} async-done(((f32[8,320,128]{2,1,0:T(8,128)}), f32[8,320,128]{2,1,0:T(8,128)S(1)}, u32[]{:S(2)}, u32[]{:S(2)}) %all-to-all-start.2) | async-done | bytes 1310752 | tf_op jit(solution)/shard_map/all_to_all | solution.py:397
  116.5 3.5 %all-to-all-start.4 = ((f32[8,128,128]{2,1,0:T(8,128)}), f32[8,128,128]{2,1,0:T(8,128)S(1)}, u32[]{:S(2)}, u32[]{:S(2)}) async-start(f32[8,128,128]{2,1,0:T(8,128)} %product.13), calls=%async_computation.4 | async-start | bytes 1048576 | tf_op jit(solution)/shard_map/all_to_all | solution.py:397
  120.0 1.1 assemble.1
  121.2 8.5 %all-to-all-done.4.right_ref = f32[8,128,128]{2,1,0:T(8,128)S(1)} async-done(((f32[8,128,128]{2,1,0:T(8,128)}), f32[8,128,128]{2,1,0:T(8,128)S(1)}, u32[]{:S(2)}, u32[]{:S(2)}) %all-to-all-start.4) | async-done | bytes 524320 | tf_op jit(solution)/shard_map/all_to_all | solution.py:397
  129.7 1.8 %finish.1 = f32[512,256]{1,0:T(8,128)} custom-call(s32[8]{0:T(128)S(1)} %bitcast.4, f32[256,512]{1,0:T(8,128)S(1)} %get-tuple-element.19.base_ref, f32[8,320,128]{2,1,0:T(8,128)S(1)} %all-to-all-done.2.left_ref.came_ref, f32[8,128,128]{2,1,0:T(8,128)S(1)} %all-to-all-done.4.right_ref), custom_call_target="tpu_custom_call" | custom-call | flops 1024 | bytes 1024 | tf_op jit(solution)/shard_map/finish/pallas_call | solution.py:356
Async XLA Ops:
  2.4 15.1 %collective-permute-start.1 = (f32[128,512]{1,0:T(8,128)S(1)}, f32[128,512]{1,0:T(8,128)S(1)}, u32[]{:S(2)}, u32[]{:S(2)}) collective-permute-start(f32[128,512]{1,0:T(8,128)S(1)} %get-tuple-element.18.first_ref.refs_0_), channel_id=1, source_target_pairs={{0,3},{1,0},{2,1},{3,2},{4,7},{5,4},{6,5},{7,6},{8,11},{9,8},{10,9... | collective-permute-start | bytes 786440 | tf_op jit(solution)/shard_map/ppermute | solution.py:393
  7.5 12.1 %collective-permute-start = (f32[128,512]{1,0:T(8,128)S(1)}, f32[128,512]{1,0:T(8,128)S(1)}, u32[]{:S(2)}, u32[]{:S(2)}) collective-permute-start(f32[128,512]{1,0:T(8,128)S(1)} %get-tuple-element.18.first_ref.refs_0_), channel_id=1, source_target_pairs={{0,1},{1,2},{2,3},{3,0},{4,5},{5,6},{6,7},{7,4},{8,9},{9,10},{10,1... | collective-permute-start | bytes 786440 | tf_op jit(solution)/shard_map/ppermute | solution.py:393
  12.4 0.7 copy-start
  13.1 6.5 %copy-start.2 = (f32[128,512]{1,0:T(8,128)}, f32[128,512]{1,0:T(8,128)S(1)}, u32[]{:S(2)}) copy-start(f32[128,512]{1,0:T(8,128)S(1)} %get-tuple-element.27.base_ref) | copy-start | bytes 786436
  13.1 21.1 %all-to-all-start = ((f32[8,192,128]{2,1,0:T(8,128)}), f32[8,192,128]{2,1,0:T(8,128)S(1)}, u32[]{:S(2)}, u32[]{:S(2)}) async-start(f32[8,192,128]{2,1,0:T(8,128)} %get-tuple-element.28), calls=%async_computation | async-start | bytes 1572864 | tf_op jit(solution)/shard_map/all_to_all | solution.py:397
  19.6 10.7 %collective-permute-start.2 = (f32[128,512]{1,0:T(8,128)S(1)}, f32[128,512]{1,0:T(8,128)S(1)}, u32[]{:S(2)}, u32[]{:S(2)}) collective-permute-start(f32[128,512]{1,0:T(8,128)S(1)} %select_select_fusion.3), channel_id=1, source_target_pairs={{1,0},{2,3},{3,1},{0,2},{5,4},{6,7},{7,5},{4,6},{9,8},{10,11},{11,... | collective-permute-start | bytes 786440 | tf_op jit(solution)/shard_map/ppermute | solution.py:407
  30.3 11.7 %collective-permute-start.4 = (f32[128,512]{1,0:T(8,128)S(1)}, f32[128,512]{1,0:T(8,128)S(1)}, u32[]{:S(2)}, u32[]{:S(2)}) collective-permute-start(f32[128,512]{1,0:T(8,128)S(1)} %get-tuple-element.25.refs_2_), channel_id=1, source_target_pairs={{0,1},{1,2},{2,3},{3,0},{4,5},{5,6},{6,7},{7,4},{8,9},{9,10},{10,1... | collective-permute-start | bytes 786440 | tf_op jit(solution)/shard_map/ppermute | solution.py:393
  33.6 10.8 %collective-permute-start.3 = (f32[128,512]{1,0:T(8,128)S(1)}, f32[128,512]{1,0:T(8,128)S(1)}, u32[]{:S(2)}, u32[]{:S(2)}) collective-permute-start(f32[128,512]{1,0:T(8,128)S(1)} %get-tuple-element.25.refs_2_), channel_id=1, source_target_pairs={{0,3},{1,0},{2,1},{3,2},{4,7},{5,4},{6,5},{7,6},{8,11},{9,8},{10,9... | collective-permute-start | bytes 786440 | tf_op jit(solution)/shard_map/ppermute | solution.py:393
  37.8 14.5 %all-to-all-start.1 = ((f32[8,128,128]{2,1,0:T(8,128)}), f32[8,128,128]{2,1,0:T(8,128)S(1)}, u32[]{:S(2)}, u32[]{:S(2)}) async-start(f32[8,128,128]{2,1,0:T(8,128)} %product.8), calls=%async_computation.1 | async-start | bytes 1048576 | tf_op jit(solution)/shard_map/all_to_all | solution.py:397
  44.5 7.8 %copy-start.4 = (s32[1,8,1]{1,2,0:T(1,128)S(1)}, s32[1,8,1]{1,2,0:T(1,128)}, u32[]{:S(2)}) copy-start(s32[1,8,1]{1,2,0:T(1,128)} %param.20) | copy-start | bytes 100
  44.5 7.8 %collective-permute-start.5 = (f32[128,512]{1,0:T(8,128)S(1)}, f32[128,512]{1,0:T(8,128)S(1)}, u32[]{:S(2)}, u32[]{:S(2)}) collective-permute-start(f32[128,512]{1,0:T(8,128)S(1)} %select_select_fusion.2), channel_id=1, source_target_pairs={{1,0},{2,3},{3,1},{0,2},{5,4},{6,7},{7,5},{4,6},{9,8},{10,11},{11,... | collective-permute-start | bytes 786440 | tf_op jit(solution)/shard_map/ppermute | solution.py:407
  52.3 1.0 copy-start.3
  53.9 13.5 %collective-permute-start.7 = (f32[176,512]{1,0:T(8,128)S(1)}, f32[176,512]{1,0:T(8,128)S(1)}, u32[]{:S(2)}, u32[]{:S(2)}) collective-permute-start(f32[176,512]{1,0:T(8,128)S(1)} %carry.2.refs_2_.refs_4_), channel_id=1, source_target_pairs={{0,1},{1,2},{2,3},{3,0},{4,5},{5,6},{6,7},{7,4},{8,9},{9,10},{10,1... | collective-permute-start | bytes 1081352 | tf_op jit(solution)/shard_map/ppermute | solution.py:393
  55.9 16.7 %collective-permute-start.6 = (f32[176,512]{1,0:T(8,128)S(1)}, f32[176,512]{1,0:T(8,128)S(1)}, u32[]{:S(2)}, u32[]{:S(2)}) collective-permute-start(f32[176,512]{1,0:T(8,128)S(1)} %carry.2.refs_2_.refs_4_), channel_id=1, source_target_pairs={{0,3},{1,0},{2,1},{3,2},{4,7},{5,4},{6,5},{7,6},{8,11},{9,8},{10,9... | collective-permute-start | bytes 1081352 | tf_op jit(solution)/shard_map/ppermute | solution.py:393
  61.4 21.7 %all-to-all-start.3 = ((f32[8,128,128]{2,1,0:T(8,128)}), f32[8,128,128]{2,1,0:T(8,128)S(1)}, u32[]{:S(2)}, u32[]{:S(2)}) async-start(f32[8,128,128]{2,1,0:T(8,128)} %product.11), calls=%async_computation.3 | async-start | bytes 1048576 | tf_op jit(solution)/shard_map/all_to_all | solution.py:397
  72.6 10.4 %copy-start.1 = (f32[128,512]{1,0:T(8,128)S(1)}, f32[128,512]{1,0:T(8,128)}, u32[]{:S(2)}) copy-start(f32[128,512]{1,0:T(8,128)} %copy-done) | copy-start | bytes 786436
  72.6 10.4 %collective-permute-start.8 = (f32[176,512]{1,0:T(8,128)S(1)}, f32[176,512]{1,0:T(8,128)S(1)}, u32[]{:S(2)}, u32[]{:S(2)}) collective-permute-start(f32[176,512]{1,0:T(8,128)S(1)} %select_select_fusion), channel_id=1, source_target_pairs={{1,0},{2,3},{3,1},{0,2},{5,4},{6,7},{7,5},{4,6},{9,8},{10,11},{11,... | collective-permute-start | bytes 1081352 | tf_op jit(solution)/shard_map/ppermute | solution.py:407
  83.7 14.7 %collective-permute-start.10 = (f32[128,512]{1,0:T(8,128)S(1)}, f32[128,512]{1,0:T(8,128)S(1)}, u32[]{:S(2)}, u32[]{:S(2)}) collective-permute-start(f32[128,512]{1,0:T(8,128)S(1)} %carry.3.refs_2_), channel_id=1, source_target_pairs={{0,1},{1,2},{2,3},{3,0},{4,5},{5,6},{6,7},{7,4},{8,9},{9,10},{10,1... | collective-permute-start | bytes 786440 | tf_op jit(solution)/shard_map/ppermute | solution.py:393
  85.1 13.3 %collective-permute-start.9 = (f32[128,512]{1,0:T(8,128)S(1)}, f32[128,512]{1,0:T(8,128)}, u32[]{:S(2)}, u32[]{:S(2)}) collective-permute-start(f32[128,512]{1,0:T(8,128)S(1)} %carry.3.refs_2_), channel_id=1, source_target_pairs={{0,3},{1,0},{2,1},{3,2},{4,7},{5,4},{6,5},{7,6},{8,11},{9,8},{10,9... | collective-permute-start | bytes 786440 | tf_op jit(solution)/shard_map/ppermute | solution.py:393
  91.4 25.1 %all-to-all-start.2 = ((f32[8,320,128]{2,1,0:T(8,128)}), f32[8,320,128]{2,1,0:T(8,128)S(1)}, u32[]{:S(2)}, u32[]{:S(2)}) async-start(f32[8,320,128]{2,1,0:T(8,128)} %product.10), calls=%async_computation.2 | async-start | bytes 2621440 | tf_op jit(solution)/shard_map/all_to_all | solution.py:397
  98.4 8.8 %collective-permute-start.11 = (f32[128,512]{1,0:T(8,128)S(1)}, f32[128,512]{1,0:T(8,128)S(1)}, u32[]{:S(2)}, u32[]{:S(2)}) collective-permute-start(f32[128,512]{1,0:T(8,128)S(1)} %select_select_fusion.1), channel_id=1, source_target_pairs={{1,0},{2,3},{3,1},{0,2},{5,4},{6,7},{7,5},{4,6},{9,8},{10,11},{11,... | collective-permute-start | bytes 786440 | tf_op jit(solution)/shard_map/ppermute | solution.py:407
  116.5 13.2 %all-to-all-start.4 = ((f32[8,128,128]{2,1,0:T(8,128)}), f32[8,128,128]{2,1,0:T(8,128)S(1)}, u32[]{:S(2)}, u32[]{:S(2)}) async-start(f32[8,128,128]{2,1,0:T(8,128)} %product.13), calls=%async_computation.4 | async-start | bytes 1048576 | tf_op jit(solution)/shard_map/all_to_all | solution.py:397

commit v9 on v8

--- a/solution.py
+++ b/solution.py
@@ -283,7 +283,7 @@
             out_ref[:, here] = summed
 
 
-def product(n_row, n_col, ids, origins, operator, fields, prev, last, carriers=()):
+def product(n_row, n_col, ids, origins, operator, fields, prev, last, carriers=(), weight=LIGHT):
     n = len(origins)
     has_prev = prev is not None
     share = 0
@@ -304,7 +304,7 @@
         out_shape=jax.ShapeDtypeStruct(shape, F32),
         scratch_shapes=scratch,
         compiler_params=params(48),
-        cost_estimate=LIGHT if last else HEAVY,
+        cost_estimate=weight,
         name="product",
     )(
         ids,
@@ -330,7 +330,7 @@
             out_ref[H:, j * LANES : (j + 1) * LANES] = share[j * rows : (j + 1) * rows, :]
 
 
-def carry(n_row, owners, base, came, *pieces):
+def carry(n_row, owners, base, came, *pieces, weight=LIGHT):
     rows = pieces[0].shape[1] * LANES // NODES_DEV if pieces else 0
     return pl.pallas_call(
         functools.partial(carry_kernel, n_row, rows),
@@ -338,7 +338,7 @@
         out_specs=VMEM,
         out_shape=jax.ShapeDtypeStruct((H + rows, NODES_DEV), F32),
         compiler_params=params(24),
-        cost_estimate=LIGHT,
+        cost_estimate=weight,
         name="carry",
     )(owners, base, came, *pieces)
 
@@ -401,37 +401,50 @@
     return lax.optimization_barrier((x, *others))[0]
 
 
-def opposite(field, below, above):
+def for_opposite(field, below, above):
     col = lax.axis_index("col")
-    sent = jnp.where(col == 1, above, jnp.where(col == 2, below, field))
+    return jnp.where(col == 1, above, jnp.where(col == 2, below, field))
+
+
+def opposite(sent):
     return lax.ppermute(sent, "col", [(1, 0), (2, 3), (3, 1), (0, 2)])
 
 
-def gather(n_col, field, side):
+def begin(n_col, field, side):
+    return shift(n_col, field, side), shift(n_col, field, -side) if n_col > 2 else field
+
+
+def then_sent(n_col, field, side, begun, *done):
+    ahead, behind = begun
+    ahead = after(ahead, behind, *done)
+    if n_col != 4:
+        return ahead
+    return for_opposite(field, ahead, behind) if side > 0 else for_opposite(field, behind, ahead)
+
+
+def gather(n_col, field, side, begun, sent):
     long = n_col // 2
     short = n_col - 1 - long
-    ahead, behind = field, field
+    ahead, behind = begun
     steps = [[(0, field)]]
     for s in range(1, long + 1):
-        if s == 2:
-            ahead = after(ahead, behind)
         if s == 2 and n_col == 4:
-            ahead = opposite(field, ahead, behind) if side > 0 else opposite(field, behind, ahead)
-        else:
-            ahead = shift(n_col, ahead, side)
+            ahead = opposite(sent)
+        elif s > 1:
+            ahead = shift(n_col, sent if s == 2 else ahead, side)
         step = [((-side * s) % n_col, ahead)]
         if s <= short:
-            behind = shift(n_col, behind, -side)
+            behind = shift(n_col, behind, -side) if s > 1 else behind
             step.append(((side * s) % n_col, behind))
         steps.append(step)
     return steps
 
 
-def early(n_row, n_col, ids, operator, steps, total=None, done=0):
+def early(n_row, n_col, ids, operator, steps, total=None, done=0, weight=HEAVY):
     pairs = [pair for step in steps[:-1] for pair in step][done:]
     for begin in range(0, len(pairs), 3):
         origins, fields = zip(*pairs[begin : begin + 3])
-        total = product(n_row, n_col, ids, origins, operator, fields, total, False)
+        total = product(n_row, n_col, ids, origins, operator, fields, total, False, weight=weight)
     return total
 
 
@@ -462,7 +475,9 @@
     one_left, one_right, diff, pieces = local_terms(
         n_row, left, grad_out, relu_mask, cheb_weight, basis_zero, basis_one, basis_two
     )
-    steps = gather(n_col, left, 1)
+    begun = begin(n_col, left, 1)
+    sent = then_sent(n_col, left, 1, begun)
+    steps = gather(n_col, left, 1, begun, sent)
     first = steps[0] + steps[1] if len(steps) > 2 else steps[0]
     operator, left_early = build_operator(
         n_row, n_col, ids, live_tiles, tile_rows, tile_slots, tile_values, first
@@ -470,22 +485,28 @@
     pieces = exchange(pieces)
     common = (n_row, n_col, ids, operator)
 
+    right_begun = begin(n_col, after(right, sent), -1)
     left_early = early(*common, steps, left_early, len(first))
-    right_steps = gather(n_col, after(right, left_early, steps[-1][0][1]), -1)
-    left_came = exchange(final(*common, steps, after(left_early, pieces)))
-    right_early = early(*common, right_steps)
-
-    left_carried = carry(n_row, owners, after(one_left, right_early, right_steps[-1][0][1]), left_came, pieces)
-    steps = gather(n_col, left_carried, 1)
-    right_came = exchange(final(*common, right_steps, right_early))
-    left_early = early(*common, steps)
-
-    right_carried = carry(n_row, owners, after(one_right, left_early, steps[-1][0][1]), right_came)
-    right_steps = gather(n_col, right_carried, -1)
-    left_came = exchange(final(*common, steps, left_early, carrying=True))
-    right_early = early(*common, right_steps)
-
-    right_came = exchange(final(*common, right_steps, right_early))
+    left_last = final(*common, steps, after(left_early, pieces))
+    left_came = exchange(left_last)
+    sent = then_sent(n_col, right, -1, right_begun, left_last)
+    right_steps = gather(n_col, after(right, left_last), -1, right_begun, sent)
+    right_last = final(*common, right_steps, early(*common, right_steps))
+
+    left_carried = carry(n_row, owners, after(one_left, right_last), left_came, pieces)
+    begun = begin(n_col, left_carried, 1)
+    steps = gather(n_col, left_carried, 1, begun, then_sent(n_col, left_carried, 1, begun))
+    right_came = exchange(right_last)
+
+    right_carried = carry(n_row, owners, after(one_right, *begun), right_came, weight=HEAVY)
+    right_begun = begin(n_col, right_carried, -1)
+    steps[0] = [(0, after(left_carried, right_carried))]
+    left_last = final(*common, steps, early(*common, steps, weight=LIGHT), carrying=True)
+    left_came = exchange(left_last)
+    sent = then_sent(n_col, right_carried, -1, right_begun, left_last)
+    right_steps = gather(n_col, right_carried, -1, right_begun, sent)
+
+    right_came = exchange(final(*common, right_steps, early(*common, right_steps)))
     weight_grad = assemble(n_row, left_came)
     return finish(n_row, owners, diff, left_came, right_came), weight_grad
 

time: 132 us -> 134 us (1.015)
  waiting for transfers between devices: 30.7 us -> 41 us
  starting transfers between devices: 45 us -> 36.6 us
    ppermute x8, waiting for transfers between devices: 9.61 us -> 17.4 us  [shift(): lax.ppermute(x, 'col', [(c, (c + step) % n_col) for c in range(n_col)])]
    all_to_all x5, starting transfers between devices: 24.4 us -> 18.6 us  [exchange(): lax.all_to_all(pieces, 'row', split_axis=0, concat_axis=0, tiled=True)]
    ppermute x8, starting transfers between devices: 16.7 us -> 11.8 us  [shift(): lax.ppermute(x, 'col', [(c, (c + step) % n_col) for c in range(n_col)])]
    ppermute x4, waiting for transfers between devices: 6.76 us -> 10.4 us  [opposite(): return lax.ppermute(sent, 'col', [(1, 0), (2, 3), (3, 1), (0, 2)])]
    ppermute x4, starting transfers between devices: 3.85 us -> 6.14 us  [opposite(): return lax.ppermute(sent, 'col', [(1, 0), (2, 3), (3, 1), (0, 2)])]
  transfers between devices with their start and end apart: 17 -> 17, of which waited for: 8 -> 10; matrix products, arithmetic and copies ran while one was open for 0% -> 1% of each run, Pallas kernels for 36% -> 36%
where the time goes in v9:
time: 134 us
  Pallas kernels  52.2 us (39%)
  waiting for transfers between devices  41 us (31%)
  starting transfers between devices  36.6 us (27%)
  between operations  1.51 us (1%)
  local copies, waits for them, and re-layouts  1.45 us (1%)
    pallas_call x7, Pallas kernels, product(): pl.pallas_call(functools.partial(product_kernel, n_row, n_col, origins, h...  31.6 us
    all_to_all x5, starting transfers between devices, exchange(): lax.all_to_all(pieces, 'row', split_axis=0, concat_axis=0, tiled=True)  18.6 us
    ppermute x8, waiting for transfers between devices, shift(): lax.ppermute(x, 'col', [(c, (c + step) % n_col) for c in range(n_col)])  17.4 us
    all_to_all x5, waiting for transfers between devices, exchange(): lax.all_to_all(pieces, 'row', split_axis=0, concat_axis=0, tiled=True)  13.1 us
    ppermute x8, starting transfers between devices, shift(): lax.ppermute(x, 'col', [(c, (c + step) % n_col) for c in range(n_col)])  11.8 us
    ppermute x4, waiting for transfers between devices, opposite(): return lax.ppermute(sent, 'col', [(1, 0), (2, 3), (3, 1), (0, 2)])  10.4 us
    pallas_call x1, Pallas kernels, build_operator(): pl.pallas_call(functools.partial(operator_kernel, n_col, origins), grid=(...  9.74 us
    ppermute x4, starting transfers between devices, opposite(): return lax.ppermute(sent, 'col', [(1, 0), (2, 3), (3, 1), (0, 2)])  6.14 us
  transfers between devices with their start and end apart: 17, of which 10 were waited for; matrix products, arithmetic and copies ran while one was open for 1% of the time, Pallas kernels for 36%

profile of v9, /device:TPU:0, one launch (start us, length us, event | category | flops | bytes accessed | tf_op | source)
XLA Modules:
  0.0 133.7 jit_solution(15353017946988249578)
XLA Ops:
  0.6 1.7 %term_two.1 = (f32[128,512]{1,0:T(8,128)S(1)}, f32[128,512]{1,0:T(8,128)S(1)}) custom-call(f32[512,256]{1,0:T(8,128)} %grad_hbm.3, s32[512,256]{1,0:T(8,128)} %mask_hbm.3, f32[3,256,256]{2,1,0:T(8,128)} %weight_hbm.3), custom_call_target="tpu_custom_call" | custom-call | flops 1024 | bytes 1024 | tf_op jit(solution)/shard_map/term_two/pallas_call | solution.py:75
  2.4 3.1 %collective-permute-start = (f32[128,512]{1,0:T(8,128)S(1)}, f32[128,512]{1,0:T(8,128)S(1)}, u32[]{:S(2)}, u32[]{:S(2)}) collective-permute-start(f32[128,512]{1,0:T(8,128)S(1)} %get-tuple-element.20.first_ref.refs_0_), channel_id=1, source_target_pairs={{0,1},{1,2},{2,3},{3,0},{4,5},{5,6},{6,7},{7,4},{8,9},{9,10},{10,1... | collective-permute-start | bytes 786440 | tf_op jit(solution)/shard_map/ppermute | solution.py:393
  5.5 2.1 %collective-permute-start.1 = (f32[128,512]{1,0:T(8,128)S(1)}, f32[128,512]{1,0:T(8,128)S(1)}, u32[]{:S(2)}, u32[]{:S(2)}) collective-permute-start(f32[128,512]{1,0:T(8,128)S(1)} %get-tuple-element.20.first_ref.refs_0_), channel_id=1, source_target_pairs={{0,3},{1,0},{2,1},{3,2},{4,7},{5,4},{6,5},{7,6},{8,11},{9,8},{10,9... | collective-permute-start | bytes 786440 | tf_op jit(solution)/shard_map/ppermute | solution.py:393
  7.6 4.9 %local_terms.1 = (f32[128,512]{1,0:T(8,128)S(1)}, f32[128,512]{1,0:T(8,128)S(1)}, f32[256,512]{1,0:T(8,128)S(1)}, f32[8,192,128]{2,1,0:T(8,128)}) custom-call(f32[128,512]{1,0:T(8,128)S(1)} %get-tuple-element.20.first_ref.refs_0_, f32[512,256]{1,0:T(8,128)} %grad_hbm.3, s32[512,256]{1,0:T(8,128)} %mask_hbm.3, f32[3,256,256]{2,1,0:T(8,128)} %weight_hbm.3, ...), custom_call_target="tpu_custom_call" | custom-call | flops 1024 | bytes 1024 | tf_op jit(solution)/shard_map/local_terms/pallas_call | solution.py:120
  12.4 0.0 copy-start
  12.4 0.7 copy-done
  13.1 0.0 copy-start.3
  13.1 0.7 copy-done.3
  13.9 3.9 %all-to-all-start = ((f32[8,192,128]{2,1,0:T(8,128)}), f32[8,192,128]{2,1,0:T(8,128)S(1)}, u32[]{:S(2)}, u32[]{:S(2)}) async-start(f32[8,192,128]{2,1,0:T(8,128)} %get-tuple-element.28), calls=%async_computation | async-start | bytes 1572864 | tf_op jit(solution)/shard_map/all_to_all | solution.py:397
  18.4 0.0 collective-permute-done.refs_1_
  18.4 0.4 collective-permute-done.1.refs_2_
  18.8 0.8 select_select_fusion.3
  19.6 2.3 %collective-permute-start.2 = (f32[128,512]{1,0:T(8,128)S(1)}, f32[128,512]{1,0:T(8,128)S(1)}, u32[]{:S(2)}, u32[]{:S(2)}) collective-permute-start(f32[128,512]{1,0:T(8,128)S(1)} %get-tuple-element.31.refs_2_), channel_id=1, source_target_pairs={{0,3},{1,0},{2,1},{3,2},{4,7},{5,4},{6,5},{7,6},{8,11},{9,8},{10,9... | collective-permute-start | bytes 786440 | tf_op jit(solution)/shard_map/ppermute | solution.py:393
  21.9 0.0 collective-permute-start.3
  21.9 1.0 collective-permute-start.4
  22.9 9.7 %operator.1 = (bf16[4,4,1024,256]{3,2,1,0:T(8,128)(2,1)}, f32[128,1024]{1,0:T(8,128)S(1)}) custom-call(s32[1]{0:T(128)} %bitcast.1.ids_ref.refs_0_, s32[1]{0:T(128)S(6)} %copy.13.live_ref, s32[1,128]{1,0:T(1,128)} %rows_hbm.1, s32[1,128]{1,0:T(1,128)} %slots_hbm.1, f32[1,128,128,128]{3,2,1,0:T(8,128)} %values_ref.1, ...), custom_call_target="tpu_custom_call" | custom-call | flops 17179869184 | bytes 67108864 | tf_op jit(solution)/shard_map/operator/pallas_call | solution.py:217
  32.7 0.0 all-to-all-done.refs_0_
  32.7 6.6 %collective-permute-done.4.refs_2_ = f32[128,512]{1,0:T(8,128)} collective-permute-done((f32[128,512]{1,0:T(8,128)}, f32[128,512]{1,0:T(8,128)}, u32[]{:S(2)}, u32[]{:S(2)}) %collective-permute-start.4) | collective-permute-done | bytes 262176 | tf_op jit(solution)/shard_map/ppermute | solution.py:410
  39.2 4.5 %product.7 = f32[8,128,128]{2,1,0:T(8,128)} custom-call(s32[1]{0:T(128)} %bitcast.1.ids_ref.refs_0_, bf16[4,4,1024,256]{3,2,1,0:T(8,128)(2,1)} %get-tuple-element.22.refs_1_, f32[128,512]{1,0:T(8,128)} %collective-permute-done.4.refs_2_, f32[128,1024]{1,0:T(8,128)S(1)} %get-tuple-element.29.refs_3_), custom_call_target="tpu_custom_call" | custom-call | flops 1024 | bytes 1024 | tf_op jit(solution)/shard_map/product/pallas_call | solution.py:300
  43.7 3.9 %all-to-all-start.1 = ((f32[8,128,128]{2,1,0:T(8,128)}), f32[8,128,128]{2,1,0:T(8,128)S(1)}, u32[]{:S(2)}, u32[]{:S(2)}) async-start(f32[8,128,128]{2,1,0:T(8,128)} %product.7), calls=%async_computation.1 | async-start | bytes 1048576 | tf_op jit(solution)/shard_map/all_to_all | solution.py:397
  47.6 0.0 collective-permute-done.2.refs_3_
  47.6 0.0 collective-permute-done.3.refs_4_
  47.6 0.1 select_select_fusion.2
  47.7 2.8 %collective-permute-start.5 = (f32[128,512]{1,0:T(8,128)S(1)}, f32[128,512]{1,0:T(8,128)S(1)}, u32[]{:S(2)}, u32[]{:S(2)}) collective-permute-start(f32[128,512]{1,0:T(8,128)S(1)} %select_select_fusion.2), channel_id=1, source_target_pairs={{1,0},{2,3},{3,1},{0,2},{5,4},{6,7},{7,5},{4,6},{9,8},{10,11},{11,... | collective-permute-start | bytes 786440 | tf_op jit(solution)/shard_map/ppermute | solution.py:410
  50.5 5.4 %product.8.refs_3_ = f32[128,1024]{1,0:T(8,128)S(1)} custom-call(s32[1]{0:T(128)} %bitcast.1.ids_ref.refs_0_, bf16[4,4,1024,256]{3,2,1,0:T(8,128)(2,1)} %get-tuple-element.22.refs_1_, f32[128,512]{1,0:T(8,128)S(1)} %get-tuple-element.31.refs_2_, f32[128,512]{1,0:T(8,128)S(1)} %collective-permute-done.2.refs_3_, f32[128,512]{1,0:T(8,128)S(1)} %collective-permute-done.3.refs_4_), custom_call_target="tpu_custom_call" | custom-call | flops 17179869184 | bytes 67108864 | tf_op jit(solution)/shard_map/product/pallas_call | solution.py:300
  55.9 0.0 copy-start.1
  55.9 0.0 copy-start.2
  55.9 0.0 copy-start.4
  55.9 0.8 collective-permute-done.5.refs_2_
  56.7 3.6 %product.9 = f32[8,128,128]{2,1,0:T(8,128)} custom-call(s32[1]{0:T(128)} %bitcast.1.ids_ref.refs_0_, bf16[4,4,1024,256]{3,2,1,0:T(8,128)(2,1)} %get-tuple-element.22.refs_1_, f32[128,512]{1,0:T(8,128)S(1)} %collective-permute-done.5.refs_2_, f32[128,1024]{1,0:T(8,128)S(1)} %product.8.refs_3_), custom_call_target="tpu_custom_call" | custom-call | flops 1024 | bytes 1024 | tf_op jit(solution)/shard_map/product/pallas_call | solution.py:300
  60.3 0.0 all-to-all-done.1.came_ref
  60.3 0.0 copy-done.1
  60.3 0.0 copy-done.2
  60.3 0.7 carry.2.refs_2_.refs_4_
  61.0 2.2 %collective-permute-start.6 = (f32[176,512]{1,0:T(8,128)S(1)}, f32[176,512]{1,0:T(8,128)S(1)}, u32[]{:S(2)}, u32[]{:S(2)}) collective-permute-start(f32[176,512]{1,0:T(8,128)S(1)} %carry.2.refs_2_.refs_4_), channel_id=1, source_target_pairs={{0,3},{1,0},{2,1},{3,2},{4,7},{5,4},{6,5},{7,6},{8,11},{9,8},{10,9... | collective-permute-start | bytes 1081352 | tf_op jit(solution)/shard_map/ppermute | solution.py:393
  63.2 0.0 collective-permute-start.7
  63.2 3.8 %all-to-all-start.2 = ((f32[8,128,128]{2,1,0:T(8,128)}), f32[8,128,128]{2,1,0:T(8,128)S(1)}, u32[]{:S(2)}, u32[]{:S(2)}) async-start(f32[8,128,128]{2,1,0:T(8,128)} %product.9), calls=%async_computation.2 | async-start | bytes 1048576 | tf_op jit(solution)/shard_map/all_to_all | solution.py:397
  67.1 5.0 %collective-permute-done.6.refs_4_.refs_5_ = f32[176,512]{1,0:T(8,128)S(1)} collective-permute-done((f32[176,512]{1,0:T(8,128)S(1)}, f32[176,512]{1,0:T(8,128)S(1)}, u32[]{:S(2)}, u32[]{:S(2)}) %collective-permute-start.6) | collective-permute-done | bytes 360480 | tf_op jit(solution)/shard_map/ppermute | solution.py:393
  72.1 9.5 %collective-permute-done.7.refs_3_.refs_7_ = f32[176,512]{1,0:T(8,128)S(1)} collective-permute-done((f32[176,512]{1,0:T(8,128)S(1)}, f32[176,512]{1,0:T(8,128)S(1)}, u32[]{:S(2)}, u32[]{:S(2)}) %collective-permute-start.7) | collective-permute-done | bytes 360480 | tf_op jit(solution)/shard_map/ppermute | solution.py:393
  81.6 0.1 select_select_fusion
  81.7 0.6 collective-permute-start.8
  82.3 0.0 all-to-all-done.2.came_ref
  82.3 0.0 copy-done.4
  82.3 0.7 carry.3.refs_2_
  82.9 1.6 %collective-permute-start.9 = (f32[128,512]{1,0:T(8,128)S(1)}, f32[128,512]{1,0:T(8,128)S(1)}, u32[]{:S(2)}, u32[]{:S(2)}) collective-permute-start(f32[128,512]{1,0:T(8,128)S(1)} %carry.3.refs_2_), channel_id=1, source_target_pairs={{0,3},{1,0},{2,1},{3,2},{4,7},{5,4},{6,5},{7,6},{8,11},{9,8},{10,9... | collective-permute-start | bytes 786440 | tf_op jit(solution)/shard_map/ppermute | solution.py:393
  84.5 0.5 collective-permute-start.10
  85.0 5.4 %product.10.refs_3_ = f32[128,1024]{1,0:T(8,128)S(1)} custom-call(s32[1]{0:T(128)} %bitcast.1.ids_ref.refs_0_, bf16[4,4,1024,256]{3,2,1,0:T(8,128)(2,1)} %get-tuple-element.22.refs_1_, f32[176,512]{1,0:T(8,128)S(1)} %carry.2.refs_2_.refs_4_, f32[176,512]{1,0:T(8,128)S(1)} %collective-permute-done.7.refs_3_.refs_7_, ...), custom_call_target="tpu_custom_call" | custom-call | flops 1024 | bytes 1024 | tf_op jit(solution)/shard_map/product/pallas_call | solution.py:300
  90.4 2.7 %collective-permute-done.8.refs_2_.refs_6_ = f32[176,512]{1,0:T(8,128)S(1)} collective-permute-done((f32[176,512]{1,0:T(8,128)S(1)}, f32[176,512]{1,0:T(8,128)S(1)}, u32[]{:S(2)}, u32[]{:S(2)}) %collective-permute-start.8) | collective-permute-done | bytes 360480 | tf_op jit(solution)/shard_map/ppermute | solution.py:410
  93.1 3.9 %product.11 = f32[8,320,128]{2,1,0:T(8,128)} custom-call(s32[1]{0:T(128)} %bitcast.1.ids_ref.refs_0_, bf16[4,4,1024,256]{3,2,1,0:T(8,128)(2,1)} %get-tuple-element.22.refs_1_, f32[176,512]{1,0:T(8,128)S(1)} %collective-permute-done.8.refs_2_.refs_6_, f32[128,1024]{1,0:T(8,128)S(1)} %product.10.refs_3_, f32[176,512]{1,0:T(8,128)S(1)} %carry.2.refs_2_.refs_4_, ...), custom_call_target="tpu_custom_call" | custom-call | flops 1024 | bytes 1024 | tf_op jit(solution)/shard_map/product/pallas_call | solution.py:300
  97.0 3.6 %all-to-all-start.3 = ((f32[8,320,128]{2,1,0:T(8,128)}), f32[8,320,128]{2,1,0:T(8,128)S(1)}, u32[]{:S(2)}, u32[]{:S(2)}) async-start(f32[8,320,128]{2,1,0:T(8,128)} %product.11), calls=%async_computation.3 | async-start | bytes 2621440 | tf_op jit(solution)/shard_map/all_to_all | solution.py:397
  100.6 0.0 collective-permute-done.9.refs_3_
  100.6 2.4 %collective-permute-done.10.refs_4_ = f32[128,512]{1,0:T(8,128)S(1)} collective-permute-done((f32[128,512]{1,0:T(8,128)S(1)}, f32[128,512]{1,0:T(8,128)S(1)}, u32[]{:S(2)}, u32[]{:S(2)}) %collective-permute-start.10) | collective-permute-done | bytes 262176 | tf_op jit(solution)/shard_map/ppermute | solution.py:393
  103.0 0.1 select_select_fusion.1
  103.1 1.8 %collective-permute-start.11 = (f32[128,512]{1,0:T(8,128)S(1)}, f32[128,512]{1,0:T(8,128)S(1)}, u32[]{:S(2)}, u32[]{:S(2)}) collective-permute-start(f32[128,512]{1,0:T(8,128)S(1)} %select_select_fusion.1), channel_id=1, source_target_pairs={{1,0},{2,3},{3,1},{0,2},{5,4},{6,7},{7,5},{4,6},{9,8},{10,11},{11,... | collective-permute-start | bytes 786440 | tf_op jit(solution)/shard_map/ppermute | solution.py:410
  104.8 5.4 %product.12.refs_3_ = f32[128,1024]{1,0:T(8,128)S(1)} custom-call(s32[1]{0:T(128)} %bitcast.1.ids_ref.refs_0_, bf16[4,4,1024,256]{3,2,1,0:T(8,128)(2,1)} %get-tuple-element.22.refs_1_, f32[128,512]{1,0:T(8,128)S(1)} %carry.3.refs_2_, f32[128,512]{1,0:T(8,128)S(1)} %collective-permute-done.9.refs_3_, f32[128,512]{1,0:T(8,128)S(1)} %collective-permute-done.10.refs_4_), custom_call_target="tpu_custom_call" | custom-call | flops 17179869184 | bytes 67108864 | tf_op jit(solution)/shard_map/product/pallas_call | solution.py:300
  110.2 0.4 collective-permute-done.11.refs_2_
  110.6 3.6 %product.13 = f32[8,128,128]{2,1,0:T(8,128)} custom-call(s32[1]{0:T(128)} %bitcast.1.ids_ref.refs_0_, bf16[4,4,1024,256]{3,2,1,0:T(8,128)(2,1)} %get-tuple-element.22.refs_1_, f32[128,512]{1,0:T(8,128)S(1)} %collective-permute-done.11.refs_2_, f32[128,1024]{1,0:T(8,128)S(1)} %product.12.refs_3_), custom_call_target="tpu_custom_call" | custom-call | flops 1024 | bytes 1024 | tf_op jit(solution)/shard_map/product/pallas_call | solution.py:300
  114.1 4.6 %all-to-all-done.3.left_ref.came_ref = f32[8,320,128]{2,1,0:T(8,128)S(1)} async-done(((f32[8,320,128]{2,1,0:T(8,128)}), f32[8,320,128]{2,1,0:T(8,128)S(1)}, u32[]{:S(2)}, u32[]{:S(2)}) %all-to-all-start.3) | async-done | bytes 1310752 | tf_op jit(solution)/shard_map/all_to_all | solution.py:397
  118.7 3.5 %all-to-all-start.4 = ((f32[8,128,128]{2,1,0:T(8,128)}), f32[8,128,128]{2,1,0:T(8,128)S(1)}, u32[]{:S(2)}, u32[]{:S(2)}) async-start(f32[8,128,128]{2,1,0:T(8,128)} %product.13), calls=%async_computation.4 | async-start | bytes 1048576 | tf_op jit(solution)/shard_map/all_to_all | solution.py:397
  122.2 1.1 assemble.1
  123.4 8.5 %all-to-all-done.4.right_ref = f32[8,128,128]{2,1,0:T(8,128)S(1)} async-done(((f32[8,128,128]{2,1,0:T(8,128)}), f32[8,128,128]{2,1,0:T(8,128)S(1)}, u32[]{:S(2)}, u32[]{:S(2)}) %all-to-all-start.4) | async-done | bytes 524320 | tf_op jit(solution)/shard_map/all_to_all | solution.py:397
  131.9 1.8 %finish.1 = f32[512,256]{1,0:T(8,128)} custom-call(s32[8]{0:T(128)S(1)} %bitcast.4, f32[256,512]{1,0:T(8,128)S(1)} %get-tuple-element.21.base_ref, f32[8,320,128]{2,1,0:T(8,128)S(1)} %all-to-all-done.3.left_ref.came_ref, f32[8,128,128]{2,1,0:T(8,128)S(1)} %all-to-all-done.4.right_ref), custom_call_target="tpu_custom_call" | custom-call | flops 1024 | bytes 1024 | tf_op jit(solution)/shard_map/finish/pallas_call | solution.py:356
Async XLA Ops:
  2.4 16.0 %collective-permute-start = (f32[128,512]{1,0:T(8,128)S(1)}, f32[128,512]{1,0:T(8,128)S(1)}, u32[]{:S(2)}, u32[]{:S(2)}) collective-permute-start(f32[128,512]{1,0:T(8,128)S(1)} %get-tuple-element.20.first_ref.refs_0_), channel_id=1, source_target_pairs={{0,1},{1,2},{2,3},{3,0},{4,5},{5,6},{6,7},{7,4},{8,9},{9,10},{10,1... | collective-permute-start | bytes 786440 | tf_op jit(solution)/shard_map/ppermute | solution.py:393
  5.5 13.4 %collective-permute-start.1 = (f32[128,512]{1,0:T(8,128)S(1)}, f32[128,512]{1,0:T(8,128)S(1)}, u32[]{:S(2)}, u32[]{:S(2)}) collective-permute-start(f32[128,512]{1,0:T(8,128)S(1)} %get-tuple-element.20.first_ref.refs_0_), channel_id=1, source_target_pairs={{0,3},{1,0},{2,1},{3,2},{4,7},{5,4},{6,5},{7,6},{8,11},{9,8},{10,9... | collective-permute-start | bytes 786440 | tf_op jit(solution)/shard_map/ppermute | solution.py:393
  12.4 0.7 copy-start
  13.1 0.7 copy-start.3
  13.9 18.8 %all-to-all-start = ((f32[8,192,128]{2,1,0:T(8,128)}), f32[8,192,128]{2,1,0:T(8,128)S(1)}, u32[]{:S(2)}, u32[]{:S(2)}) async-start(f32[8,192,128]{2,1,0:T(8,128)} %get-tuple-element.28), calls=%async_computation | async-start | bytes 1572864 | tf_op jit(solution)/shard_map/all_to_all | solution.py:397
  19.6 28.0 %collective-permute-start.2 = (f32[128,512]{1,0:T(8,128)S(1)}, f32[128,512]{1,0:T(8,128)S(1)}, u32[]{:S(2)}, u32[]{:S(2)}) collective-permute-start(f32[128,512]{1,0:T(8,128)S(1)} %get-tuple-element.31.refs_2_), channel_id=1, source_target_pairs={{0,3},{1,0},{2,1},{3,2},{4,7},{5,4},{6,5},{7,6},{8,11},{9,8},{10,9... | collective-permute-start | bytes 786440 | tf_op jit(solution)/shard_map/ppermute | solution.py:393
  21.9 25.7 %collective-permute-start.3 = (f32[128,512]{1,0:T(8,128)S(1)}, f32[128,512]{1,0:T(8,128)S(1)}, u32[]{:S(2)}, u32[]{:S(2)}) collective-permute-start(f32[128,512]{1,0:T(8,128)S(1)} %get-tuple-element.31.refs_2_), channel_id=1, source_target_pairs={{0,1},{1,2},{2,3},{3,0},{4,5},{5,6},{6,7},{7,4},{8,9},{9,10},{10,1... | collective-permute-start | bytes 786440 | tf_op jit(solution)/shard_map/ppermute | solution.py:393
  21.9 17.3 %collective-permute-start.4 = (f32[128,512]{1,0:T(8,128)}, f32[128,512]{1,0:T(8,128)}, u32[]{:S(2)}, u32[]{:S(2)}) collective-permute-start(f32[128,512]{1,0:T(8,128)} %select_select_fusion.3), channel_id=1, source_target_pairs={{1,0},{2,3},{3,1},{0,2},{5,4},{6,7},{7,5},{4,6},{9,8},{10,11},{11,... | collective-permute-start | bytes 786440 | tf_op jit(solution)/shard_map/ppermute | solution.py:410
  43.7 16.5 %all-to-all-start.1 = ((f32[8,128,128]{2,1,0:T(8,128)}), f32[8,128,128]{2,1,0:T(8,128)S(1)}, u32[]{:S(2)}, u32[]{:S(2)}) async-start(f32[8,128,128]{2,1,0:T(8,128)} %product.7), calls=%async_computation.1 | async-start | bytes 1048576 | tf_op jit(solution)/shard_map/all_to_all | solution.py:397
  47.7 9.0 %collective-permute-start.5 = (f32[128,512]{1,0:T(8,128)S(1)}, f32[128,512]{1,0:T(8,128)S(1)}, u32[]{:S(2)}, u32[]{:S(2)}) collective-permute-start(f32[128,512]{1,0:T(8,128)S(1)} %select_select_fusion.2), channel_id=1, source_target_pairs={{1,0},{2,3},{3,1},{0,2},{5,4},{6,7},{7,5},{4,6},{9,8},{10,11},{11,... | collective-permute-start | bytes 786440 | tf_op jit(solution)/shard_map/ppermute | solution.py:410
  55.9 4.4 %copy-start.1 = (f32[128,512]{1,0:T(8,128)S(1)}, f32[128,512]{1,0:T(8,128)}, u32[]{:S(2)}) copy-start(f32[128,512]{1,0:T(8,128)} %copy-done) | copy-start | bytes 786436
  55.9 4.4 %copy-start.2 = (s32[1,8,1]{1,2,0:T(1,128)S(1)}, s32[1,8,1]{1,2,0:T(1,128)}, u32[]{:S(2)}) copy-start(s32[1,8,1]{1,2,0:T(1,128)} %param.20) | copy-start | bytes 100
  55.9 26.4 %copy-start.4 = (f32[128,512]{1,0:T(8,128)S(1)}, f32[128,512]{1,0:T(8,128)}, u32[]{:S(2)}) copy-start(f32[128,512]{1,0:T(8,128)} %copy-done.3) | copy-start | bytes 786436
  61.0 11.1 %collective-permute-start.6 = (f32[176,512]{1,0:T(8,128)S(1)}, f32[176,512]{1,0:T(8,128)S(1)}, u32[]{:S(2)}, u32[]{:S(2)}) collective-permute-start(f32[176,512]{1,0:T(8,128)S(1)} %carry.2.refs_2_.refs_4_), channel_id=1, source_target_pairs={{0,3},{1,0},{2,1},{3,2},{4,7},{5,4},{6,5},{7,6},{8,11},{9,8},{10,9... | collective-permute-start | bytes 1081352 | tf_op jit(solution)/shard_map/ppermute | solution.py:393
  63.2 18.4 %collective-permute-start.7 = (f32[176,512]{1,0:T(8,128)S(1)}, f32[176,512]{1,0:T(8,128)S(1)}, u32[]{:S(2)}, u32[]{:S(2)}) collective-permute-start(f32[176,512]{1,0:T(8,128)S(1)} %carry.2.refs_2_.refs_4_), channel_id=1, source_target_pairs={{0,1},{1,2},{2,3},{3,0},{4,5},{5,6},{6,7},{7,4},{8,9},{9,10},{10,1... | collective-permute-start | bytes 1081352 | tf_op jit(solution)/shard_map/ppermute | solution.py:393
  63.2 19.0 %all-to-all-start.2 = ((f32[8,128,128]{2,1,0:T(8,128)}), f32[8,128,128]{2,1,0:T(8,128)S(1)}, u32[]{:S(2)}, u32[]{:S(2)}) async-start(f32[8,128,128]{2,1,0:T(8,128)} %product.9), calls=%async_computation.2 | async-start | bytes 1048576 | tf_op jit(solution)/shard_map/all_to_all | solution.py:397
  81.7 11.4 %collective-permute-start.8 = (f32[176,512]{1,0:T(8,128)S(1)}, f32[176,512]{1,0:T(8,128)S(1)}, u32[]{:S(2)}, u32[]{:S(2)}) collective-permute-start(f32[176,512]{1,0:T(8,128)S(1)} %select_select_fusion), channel_id=1, source_target_pairs={{1,0},{2,3},{3,1},{0,2},{5,4},{6,7},{7,5},{4,6},{9,8},{10,11},{11,... | collective-permute-start | bytes 1081352 | tf_op jit(solution)/shard_map/ppermute | solution.py:410
  82.9 17.6 %collective-permute-start.9 = (f32[128,512]{1,0:T(8,128)S(1)}, f32[128,512]{1,0:T(8,128)S(1)}, u32[]{:S(2)}, u32[]{:S(2)}) collective-permute-start(f32[128,512]{1,0:T(8,128)S(1)} %carry.3.refs_2_), channel_id=1, source_target_pairs={{0,3},{1,0},{2,1},{3,2},{4,7},{5,4},{6,5},{7,6},{8,11},{9,8},{10,9... | collective-permute-start | bytes 786440 | tf_op jit(solution)/shard_map/ppermute | solution.py:393
  84.5 18.5 %collective-permute-start.10 = (f32[128,512]{1,0:T(8,128)S(1)}, f32[128,512]{1,0:T(8,128)S(1)}, u32[]{:S(2)}, u32[]{:S(2)}) collective-permute-start(f32[128,512]{1,0:T(8,128)S(1)} %carry.3.refs_2_), channel_id=1, source_target_pairs={{0,1},{1,2},{2,3},{3,0},{4,5},{5,6},{6,7},{7,4},{8,9},{9,10},{10,1... | collective-permute-start | bytes 786440 | tf_op jit(solution)/shard_map/ppermute | solution.py:393
  97.0 21.7 %all-to-all-start.3 = ((f32[8,320,128]{2,1,0:T(8,128)}), f32[8,320,128]{2,1,0:T(8,128)S(1)}, u32[]{:S(2)}, u32[]{:S(2)}) async-start(f32[8,320,128]{2,1,0:T(8,128)} %product.11), calls=%async_computation.3 | async-start | bytes 2621440 | tf_op jit(solution)/shard_map/all_to_all | solution.py:397
  103.1 7.5 %collective-permute-start.11 = (f32[128,512]{1,0:T(8,128)S(1)}, f32[128,512]{1,0:T(8,128)S(1)}, u32[]{:S(2)}, u32[]{:S(2)}) collective-permute-start(f32[128,512]{1,0:T(8,128)S(1)} %select_select_fusion.1), channel_id=1, source_target_pairs={{1,0},{2,3},{3,1},{0,2},{5,4},{6,7},{7,5},{4,6},{9,8},{10,11},{11,... | collective-permute-start | bytes 786440 | tf_op jit(solution)/shard_map/ppermute | solution.py:410
  118.7 13.2 %all-to-all-start.4 = ((f32[8,128,128]{2,1,0:T(8,128)}), f32[8,128,128]{2,1,0:T(8,128)S(1)}, u32[]{:S(2)}, u32[]{:S(2)}) async-start(f32[8,128,128]{2,1,0:T(8,128)} %product.13), calls=%async_computation.4 | async-start | bytes 1048576 | tf_op jit(solution)/shard_map/all_to_all | solution.py:397

commit v10 on v8

--- a/solution.py
+++ b/solution.py
@@ -90,43 +90,35 @@
 
 
 def local_kernel(
-    n_row, first_ref, grad_hbm, mask_hbm, weight_hbm, h0, h1, h2, left_ref, right_ref, diff_ref, pieces_ref,
+    first_ref, grad_hbm, mask_hbm, weight_hbm, h0, h1, h2, left_ref, right_ref, diff_ref, upper_ref, lower_ref,
     grad, mask, weight, bases, sems,
 ):
     sources = (grad_hbm, mask_hbm, weight_hbm, h0, h1, h2)
     copies = fetch(sources, (grad, mask, weight, bases.at[0], bases.at[1], bases.at[2]), sems)
     for copy in copies[:3]:
         copy.wait()
-    values = masked_of(grad[...], mask[...])
-    masked = split(values)
+    masked = split(masked_of(grad[...], mask[...]))
     term = dot3(split(weight[1]), masked, ((1,), (1,)))
     left_ref[...] = term[:H]
     right_ref[...] = term[H:]
     diff_ref[...] = dot3(split(weight[0] - weight[2]), masked, ((1,), (1,)))
-    turned = split(values.T)
-    rows = F // n_row
     for k in range(3):
         copies[3 + k].wait()
-        part = dot3(turned, split(bases[k]), ((1,), (0,)))
-        for j in range(F // LANES):
-            here = (k * (F // LANES) + j) * rows
-            for q in range(n_row):
-                pieces_ref[q, here : here + rows, :] = part[q * rows : (q + 1) * rows, j * LANES : (j + 1) * LANES]
-
-
-def local_terms(n_row, first, grad_out, relu_mask, cheb_weight, b0, b1, b2):
+        part = dot3(split(bases[k]), masked, ((0,), (0,)))
+        for j in range(2):
+            place = k * F + j * H
+            target = upper_ref if place < 3 * H else lower_ref
+            target[place % (3 * H) : place % (3 * H) + H, :] = part[j * H : (j + 1) * H]
+
+
+def local_terms(first, grad_out, relu_mask, cheb_weight, b0, b1, b2):
     half = jax.ShapeDtypeStruct((H, NODES_DEV), F32)
-    share = 3 * F * F // n_row // LANES
-    return pl.pallas_call(
-        functools.partial(local_kernel, n_row),
+    part = jax.ShapeDtypeStruct((3 * H, F), F32)
+    return pl.pallas_call(
+        local_kernel,
         in_specs=[pl.BlockSpec(memory_space=pl.ANY)] + [HBM] * 6,
-        out_specs=[VMEM] * 4,
-        out_shape=[
-            half,
-            half,
-            jax.ShapeDtypeStruct((F, NODES_DEV), F32),
-            jax.ShapeDtypeStruct((n_row, share, LANES), F32),
-        ],
+        out_specs=[VMEM] * 5,
+        out_shape=[half, half, jax.ShapeDtypeStruct((F, NODES_DEV), F32), part, part],
         scratch_shapes=[
             pltpu.VMEM((NODES_DEV, F), F32),
             pltpu.VMEM((NODES_DEV, F), jnp.int32),
@@ -239,14 +231,12 @@
     )(ids, live, *in_hbm(rows, slots, values), *fields)
 
 
-def product_kernel(n_row, n_col, origins, has_prev, last, n_carriers, *refs):
+def product_kernel(n_row, origins, has_prev, last, *refs):
     n = len(origins)
-    ids_ref, op_ref, refs = refs[0], refs[1], refs[2:]
-    fields, refs = refs[:n], refs[n:]
+    op_ref, fields, refs = refs[0], refs[1 : 1 + n], refs[1 + n :]
     if has_prev:
         prev, refs = refs[0], refs[1:]
-    carriers, refs = refs[:n_carriers], refs[n_carriers:]
-    out_ref, buf, sems = refs[:3]
+    out_ref, buf, sems = refs
 
     def copy(k, p):
         return pltpu.make_async_copy(op_ref.at[origins[k], p], buf.at[k, p], sems.at[k, p])
@@ -254,18 +244,7 @@
     for p in range(n_row // 2):
         for k in range(n):
             copy(k, p).start()
-    left = [stacked(field[:H, :]) for field in fields]
-    if n_carriers:
-        ordered = refs[3]
-        for k in range(n_col):
-            ordered[lax.rem(ids_ref[0] + k, n_col)] = carriers[k][H:, :]
-        share = ordered[0]
-        for k in range(1, n_col):
-            share = share + ordered[k]
-        rows = share.shape[0]
-        for j in range(NODES_DEV // LANES):
-            for q in range(n_row):
-                out_ref[q, H + j * rows : H + (j + 1) * rows, :] = share[:, j * LANES : (j + 1) * LANES]
+    left = [stacked(field[...]) for field in fields]
     for p in range(n_row // 2):
         here = slice(p * WIDE, (p + 1) * WIDE)
         total = None
@@ -277,70 +256,47 @@
         if has_prev:
             summed = summed + prev[:, here]
         if last:
-            out_ref[2 * p, :H, :] = summed[:, :TB]
-            out_ref[2 * p + 1, :H, :] = summed[:, TB:]
+            out_ref[2 * p] = summed[:, :TB]
+            out_ref[2 * p + 1] = summed[:, TB:]
         else:
             out_ref[:, here] = summed
 
 
-def product(n_row, n_col, ids, origins, operator, fields, prev, last, carriers=()):
+def product(n_row, origins, operator, fields, prev, last):
     n = len(origins)
     has_prev = prev is not None
-    share = 0
-    scratch = [
-        pltpu.VMEM((n, n_row // 2, 2 * NODES_DEV, WIDE), BF16),
-        pltpu.SemaphoreType.DMA((n, n_row // 2)),
-    ]
-    if carriers:
-        rows = carriers[0].shape[0] - H
-        share = rows * NODES_DEV // LANES
-        scratch.append(pltpu.VMEM((n_col, rows, NODES_DEV), F32))
-    shape = (n_row, H + share, TB) if last else (H, n_row * TB)
-    count = n + has_prev + len(carriers)
-    return pl.pallas_call(
-        functools.partial(product_kernel, n_row, n_col, origins, has_prev, last, len(carriers)),
-        in_specs=[SMEM, HBM] + [VMEM] * count,
+    return pl.pallas_call(
+        functools.partial(product_kernel, n_row, origins, has_prev, last),
+        in_specs=[HBM] + [VMEM] * (n + has_prev),
         out_specs=VMEM,
-        out_shape=jax.ShapeDtypeStruct(shape, F32),
-        scratch_shapes=scratch,
+        out_shape=jax.ShapeDtypeStruct((n_row, H, TB) if last else (H, n_row * TB), F32),
+        scratch_shapes=[
+            pltpu.VMEM((n, n_row // 2, 2 * NODES_DEV, WIDE), BF16),
+            pltpu.SemaphoreType.DMA((n, n_row // 2)),
+        ],
         compiler_params=params(48),
         cost_estimate=LIGHT if last else HEAVY,
         name="product",
-    )(
-        ids,
-        *in_hbm(operator),
-        *fields,
-        *((prev,) if has_prev else ()),
-        *carriers,
-    )
-
-
-def carry_kernel(n_row, rows, owners_ref, base_ref, came_ref, *refs):
-    out_ref = refs[-1]
-    out_ref[:H, :] = base_ref[...]
+    )(*in_hbm(operator), *fields, *((prev,) if has_prev else ()))
+
+
+def carry_kernel(n_row, owners_ref, base_ref, came_ref, out_ref):
+    out_ref[...] = base_ref[...]
     for q in range(n_row):
         here = pl.ds(pl.multiple_of(owners_ref[q] * TB, TB), TB)
-        out_ref[:H, here] += 2.0 * came_ref[q]
-    if rows:
-        pieces_ref = refs[0]
-        share = pieces_ref[0]
-        for q in range(1, n_row):
-            share = share + pieces_ref[q]
-        for j in range(NODES_DEV // LANES):
-            out_ref[H:, j * LANES : (j + 1) * LANES] = share[j * rows : (j + 1) * rows, :]
-
-
-def carry(n_row, owners, base, came, *pieces):
-    rows = pieces[0].shape[1] * LANES // NODES_DEV if pieces else 0
-    return pl.pallas_call(
-        functools.partial(carry_kernel, n_row, rows),
-        in_specs=[SMEM] + [VMEM] * (2 + len(pieces)),
+        out_ref[:, here] += 2.0 * came_ref[q]
+
+
+def carry(n_row, owners, base, came):
+    return pl.pallas_call(
+        functools.partial(carry_kernel, n_row),
+        in_specs=[SMEM, VMEM, VMEM],
         out_specs=VMEM,
-        out_shape=jax.ShapeDtypeStruct((H + rows, NODES_DEV), F32),
+        out_shape=jax.ShapeDtypeStruct((H, NODES_DEV), F32),
         compiler_params=params(24),
         cost_estimate=LIGHT,
         name="carry",
-    )(owners, base, came, *pieces)
+    )(owners, base, came)
 
 
 def finish_kernel(n_row, owners_ref, base_ref, left_ref, right_ref, out_ref, total):
@@ -348,7 +304,7 @@
     for h, came in enumerate((left_ref, right_ref)):
         for q in range(n_row):
             here = pl.ds(pl.multiple_of(owners_ref[q] * TB, TB), TB)
-            total[h * H : (h + 1) * H, here] += came[q, :H, :]
+            total[h * H : (h + 1) * H, here] += came[q]
     out_ref[...] = total[...].T
 
 
@@ -363,30 +319,6 @@
         cost_estimate=LIGHT,
         name="finish",
     )(owners, base, left, right)
-
-
-def assemble_kernel(n_row, came_ref, out_ref, turned):
-    rows = F // n_row
-    per = F // LANES
-    for q in range(n_row):
-        for j in range(3 * per):
-            here = slice(H + j * rows, H + (j + 1) * rows)
-            turned[q * rows : (q + 1) * rows, j * LANES : (j + 1) * LANES] = came_ref[q, here, :]
-    for k in range(3):
-        out_ref[k] = turned[:, k * F : (k + 1) * F].T
-
-
-def assemble(n_row, came):
-    return pl.pallas_call(
-        functools.partial(assemble_kernel, n_row),
-        in_specs=[VMEM],
-        out_specs=VMEM,
-        out_shape=jax.ShapeDtypeStruct((3, F, F), F32),
-        scratch_shapes=[pltpu.VMEM((F, 3 * F), F32)],
-        compiler_params=params(16),
-        cost_estimate=LIGHT,
-        name="assemble",
-    )(came)
 
 
 def shift(n_col, x, step):
@@ -427,18 +359,17 @@
     return steps
 
 
-def early(n_row, n_col, ids, operator, steps, total=None, done=0):
+def early(n_row, operator, steps, total=None, done=0):
     pairs = [pair for step in steps[:-1] for pair in step][done:]
     for begin in range(0, len(pairs), 3):
         origins, fields = zip(*pairs[begin : begin + 3])
-        total = product(n_row, n_col, ids, origins, operator, fields, total, False)
+        total = product(n_row, origins, operator, fields, total, False)
     return total
 
 
-def final(n_row, n_col, ids, operator, steps, total, carrying=False):
+def final(n_row, operator, steps, total):
     origins, fields = zip(*steps[-1])
-    carriers = [x for _, x in sorted((p for step in steps for p in step), key=lambda p: p[0])] if carrying else ()
-    return product(n_row, n_col, ids, origins, operator, fields, total, True, carriers)
+    return product(n_row, origins, operator, fields, total, True)
 
 
 def per_device(
@@ -459,35 +390,36 @@
     ids = lax.axis_index("col").astype(jnp.int32).reshape(1)
     owners = send_blocks.reshape(n_row)
     left, right = term_two(grad_out, relu_mask, cheb_weight)
-    one_left, one_right, diff, pieces = local_terms(
-        n_row, left, grad_out, relu_mask, cheb_weight, basis_zero, basis_one, basis_two
+    one_left, one_right, diff, upper, lower = local_terms(
+        left, grad_out, relu_mask, cheb_weight, basis_zero, basis_one, basis_two
     )
+    upper_sum, lower_sum = lax.psum(upper, ("row", "col")), lax.psum(lower, ("col", "row"))
     steps = gather(n_col, left, 1)
     first = steps[0] + steps[1] if len(steps) > 2 else steps[0]
     operator, left_early = build_operator(
-        n_row, n_col, ids, live_tiles, tile_rows, tile_slots, tile_values, first
+        n_row, n_col, after(ids, upper), live_tiles, tile_rows, tile_slots, tile_values, first
     )
-    pieces = exchange(pieces)
-    common = (n_row, n_col, ids, operator)
+    common = (n_row, operator)
 
     left_early = early(*common, steps, left_early, len(first))
     right_steps = gather(n_col, after(right, left_early, steps[-1][0][1]), -1)
-    left_came = exchange(final(*common, steps, after(left_early, pieces)))
+    left_came = exchange(final(*common, steps, left_early))
     right_early = early(*common, right_steps)
 
-    left_carried = carry(n_row, owners, after(one_left, right_early, right_steps[-1][0][1]), left_came, pieces)
+    left_carried = carry(n_row, owners, after(one_left, right_early, right_steps[-1][0][1]), left_came)
     steps = gather(n_col, left_carried, 1)
     right_came = exchange(final(*common, right_steps, right_early))
     left_early = early(*common, steps)
 
     right_carried = carry(n_row, owners, after(one_right, left_early, steps[-1][0][1]), right_came)
     right_steps = gather(n_col, right_carried, -1)
-    left_came = exchange(final(*common, steps, left_early, carrying=True))
+    left_came = exchange(final(*common, steps, left_early))
     right_early = early(*common, right_steps)
 
-    right_came = exchange(final(*common, right_steps, right_early))
-    weight_grad = assemble(n_row, left_came)
-    return finish(n_row, owners, diff, left_came, right_came), weight_grad
+    right_last = final(*common, right_steps, right_early)
+    right_came = exchange(right_last)
+    weight_grad = jnp.concatenate([after(upper_sum, right_last), after(lower_sum, right_last)])
+    return finish(n_row, owners, diff, left_came, right_came), weight_grad.reshape(3, F, F)
 
 
 def solution(mesh):

time: 132 us -> 358 us (2.71)
  waiting for transfers between devices: 30.7 us -> 254 us
  between operations: 1.47 us -> 14.9 us
  starting transfers between devices: 45 us -> 37.1 us
    psum x0 -> x2, waiting for transfers between devices: none -> 231 us  [the longest x1 133 us: per_device(): lax.psum(upper, ('row', 'col'))]
    all_to_all x5 -> x4, waiting for transfers between devices: 14.3 us -> 0.01 us  [exchange(): lax.all_to_all(pieces, 'row', split_axis=0, concat_axis=0, tiled=True)]
    all_to_all x5 -> x4, starting transfers between devices: 24.4 us -> 14.8 us  [exchange(): lax.all_to_all(pieces, 'row', split_axis=0, concat_axis=0, tiled=True)]
    ppermute x8, waiting for transfers between devices: 9.61 us -> 17.3 us  [shift(): lax.ppermute(x, 'col', [(c, (c + step) % n_col) for c in range(n_col)])]
    pallas_call x11 -> x10, Pallas kernels: 38.9 us -> 36.6 us  [the longest x7 30.4 us: product(): pl.pallas_call(functools.partial(product_kernel, n_row, origins, has_prev...]
  transfers between devices with their start and end apart: 17 -> 18, of which waited for: 8 -> 12; matrix products, arithmetic and copies ran while one was open for 0% -> 1% of each run, Pallas kernels for 36% -> 13%
where the time goes in v10:
time: 358 us
  waiting for transfers between devices  254 us (71%)
  Pallas kernels  49.7 us (14%)
  starting transfers between devices  37.1 us (10%)
  between operations  14.9 us (4%)
    psum x1, waiting for transfers between devices, per_device(): lax.psum(upper, ('row', 'col'))  133 us
    psum x1, waiting for transfers between devices, per_device(): lax.psum(lower, ('col', 'row'))  98.2 us
    pallas_call x7, Pallas kernels, product(): pl.pallas_call(functools.partial(product_kernel, n_row, origins, has_prev...  30.4 us
    ppermute x8, waiting for transfers between devices, shift(): lax.ppermute(x, 'col', [(c, (c + step) % n_col) for c in range(n_col)])  17.3 us
    ppermute x8, starting transfers between devices, shift(): lax.ppermute(x, 'col', [(c, (c + step) % n_col) for c in range(n_col)])  16.9 us
    all_to_all x4, starting transfers between devices, exchange(): lax.all_to_all(pieces, 'row', split_axis=0, concat_axis=0, tiled=True)  14.8 us
    pallas_call x1, Pallas kernels, build_operator(): pl.pallas_call(functools.partial(operator_kernel, n_col, origins), grid=(...  9.63 us
  transfers between devices with their start and end apart: 18, of which 12 were waited for; matrix products, arithmetic and copies ran while one was open for 1% of the time, Pallas kernels for 13%

profile of v10, /device:TPU:0, one launch (start us, length us, event | category | flops | bytes accessed | tf_op | source)
XLA Modules:
  0.0 358.2 jit_solution(10976791440663073384)
XLA Ops:
  7.2 1.7 term_two.1
  8.9 5.1 %collective-permute-start.1 = (f32[128,512]{1,0:T(8,128)S(1)}, f32[128,512]{1,0:T(8,128)S(1)}, u32[]{:S(2)}, u32[]{:S(2)}) collective-permute-start(f32[128,512]{1,0:T(8,128)S(1)} %get-tuple-element.21.first_ref.refs_0_), channel_id=1, source_target_pairs={{0,3},{1,0},{2,1},{3,2},{4,7},{5,4},{6,5},{7,6},{8,11},{9,8},{10,9... | collective-permute-start | bytes 786440 | tf_op jit(solution)/shard_map/ppermute | solution.py:325
  14.0 0.0 collective-permute-start
  14.0 4.8 %local_terms.1 = (f32[128,512]{1,0:T(8,128)S(1)}, f32[128,512]{1,0:T(8,128)S(1)}, f32[256,512]{1,0:T(8,128)S(1)}, f32[384,256]{1,0:T(8,128)}, f32[384,256]{1,0:T(8,128)}) custom-call(f32[128,512]{1,0:T(8,128)S(1)} %get-tuple-element.21.first_ref.refs_0_, f32[512,256]{1,0:T(8,128)} %grad_hbm.3, s32[512,256]{1,0:T(8,128)} %mask_hbm.3, ...), custom_call_target="tpu_custom_call" | custom-call | flops 1024 | bytes 1024 | tf_op jit(solution)/shard_map/local_terms/pallas_call | solution.py:117
  19.5 1.2 collective-permute-done.1.refs_2_
  20.7 5.4 %collective-permute-done.refs_1_ = f32[128,512]{1,0:T(8,128)S(1)} collective-permute-done((f32[128,512]{1,0:T(8,128)S(1)}, f32[128,512]{1,0:T(8,128)S(1)}, u32[]{:S(2)}, u32[]{:S(2)}) %collective-permute-start) | collective-permute-done | bytes 262176 | tf_op jit(solution)/shard_map/ppermute | solution.py:325
  26.1 0.1 select_select_fusion.3
  26.2 0.8 collective-permute-start.2
  27.0 9.6 %operator.1 = (bf16[4,4,1024,256]{3,2,1,0:T(8,128)(2,1)}, f32[128,1024]{1,0:T(8,128)S(1)}) custom-call(s32[1]{0:T(128)} %bitcast.1.ids_ref, s32[1]{0:T(128)S(6)} %copy.15.live_ref, s32[1,128]{1,0:T(1,128)} %rows_hbm.1, s32[1,128]{1,0:T(1,128)} %slots_hbm.1, f32[1,128,128,128]{3,2,1,0:T(8,128)} %values_ref.1, ...), custom_call_target="tpu_custom_call" | custom-call | flops 17179869184 | bytes 67108864 | tf_op jit(solution)/shard_map/operator/pallas_call | solution.py:209
  36.6 0.0 collective-permute-done.2.refs_1_
  36.6 3.1 collective-permute-start.4
  39.7 1.0 collective-permute-start.3
  40.7 3.6 product.8
  44.2 4.3 %all-to-all-start = ((f32[8,128,128]{2,1,0:T(8,128)}), f32[8,128,128]{2,1,0:T(8,128)S(1)}, u32[]{:S(2)}, u32[]{:S(2)}) async-start(f32[8,128,128]{2,1,0:T(8,128)} %product.8), calls=%async_computation | async-start | bytes 1048576 | tf_op jit(solution)/shard_map/all_to_all | solution.py:329
  48.5 0.0 collective-permute-done.4.refs_3_
  48.5 2.6 collective-permute-done.3.refs_2_
  51.1 0.1 select_select_fusion.2
  51.2 0.0 copy-start
  51.2 2.7 collective-permute-start.5
  53.9 5.4 %product.7.refs_2_ = f32[128,1024]{1,0:T(8,128)S(1)} custom-call(bf16[4,4,1024,256]{3,2,1,0:T(8,128)(2,1)} %get-tuple-element.25.refs_0_, f32[128,512]{1,0:T(8,128)S(1)} %get-tuple-element.30.refs_1_, f32[128,512]{1,0:T(8,128)S(1)} %collective-permute-done.3.refs_2_, f32[128,512]{1,0:T(8,128)S(1)} %collective-permute-done.4.refs_3_), custom_call_target="tpu_custom_call" | custom-call | flops 17179869184 | bytes 67108864 | tf_op jit(solution)/shard_map/product/pallas_call | solution.py:268
  59.3 1.1 collective-permute-done.5.refs_1_
  60.4 0.0 all-to-all-done.came_ref
  60.4 0.0 copy-done
  60.4 0.7 carry.2.refs_1_
  61.0 2.7 collective-permute-start.7
  63.7 1.2 collective-permute-start.6
  64.9 3.5 product.11
  68.5 3.5 all-to-all-start.2
  72.0 0.0 all-reduce.5.cloned.1.call-start
  72.0 0.1 collective-permute-done.7.refs_2_
  72.2 4.0 %collective-permute-done.6.refs_3_ = f32[128,512]{1,0:T(8,128)S(1)} collective-permute-done((f32[128,512]{1,0:T(8,128)S(1)}, f32[128,512]{1,0:T(8,128)S(1)}, u32[]{:S(2)}, u32[]{:S(2)}) %collective-permute-start.6) | collective-permute-done | bytes 262176 | tf_op jit(solution)/shard_map/ppermute | solution.py:325
  76.2 0.1 select_select_fusion.1
  76.3 0.7 collective-permute-start.8
  76.9 5.4 %product.9.refs_2_ = f32[128,1024]{1,0:T(8,128)S(1)} custom-call(bf16[4,4,1024,256]{3,2,1,0:T(8,128)(2,1)} %get-tuple-element.25.refs_0_, f32[128,512]{1,0:T(8,128)S(1)} %carry.2.refs_1_, f32[128,512]{1,0:T(8,128)S(1)} %collective-permute-done.7.refs_2_, f32[128,512]{1,0:T(8,128)S(1)} %collective-permute-done.6.refs_3_), custom_call_target="tpu_custom_call" | custom-call | flops 17179869184 | bytes 67108864 | tf_op jit(solution)/shard_map/product/pallas_call | solution.py:268
  82.3 2.2 collective-permute-done.8.refs_1_
  84.5 0.0 all-to-all-done.2.came_ref
  84.5 0.7 carry.3.refs_1_
  85.2 1.6 collective-permute-start.10
  86.7 2.3 collective-permute-start.9
  89.0 0.0 all-reduce.5.cloned.1.call-update
  89.1 3.6 product.10
  92.6 3.5 all-to-all-start.1
  96.1 0.4 collective-permute-done.10.refs_3_
  96.5 3.5 collective-permute-done.9.refs_2_
  100.1 0.1 select_select_fusion
  100.1 1.1 collective-permute-start.11
  101.3 5.4 %product.12.refs_2_ = f32[128,1024]{1,0:T(8,128)S(1)} custom-call(bf16[4,4,1024,256]{3,2,1,0:T(8,128)(2,1)} %get-tuple-element.25.refs_0_, f32[128,512]{1,0:T(8,128)S(1)} %carry.3.refs_1_, f32[128,512]{1,0:T(8,128)S(1)} %collective-permute-done.9.refs_2_, f32[128,512]{1,0:T(8,128)S(1)} %collective-permute-done.10.refs_3_), custom_call_target="tpu_custom_call" | custom-call | flops 17179869184 | bytes 67108864 | tf_op jit(solution)/shard_map/product/pallas_call | solution.py:268
  106.7 1.6 collective-permute-done.11.refs_1_
  108.3 3.6 %product.13 = f32[8,128,128]{2,1,0:T(8,128)} custom-call(bf16[4,4,1024,256]{3,2,1,0:T(8,128)(2,1)} %get-tuple-element.25.refs_0_, f32[128,512]{1,0:T(8,128)S(1)} %collective-permute-done.11.refs_1_, f32[128,1024]{1,0:T(8,128)S(1)} %product.12.refs_2_), custom_call_target="tpu_custom_call" | custom-call | flops 1024 | bytes 1024 | tf_op jit(solution)/shard_map/product/pallas_call | solution.py:268
  111.9 0.0 all-to-all-done.1.left_ref
  111.9 3.5 all-to-all-start.3
  115.4 0.0 all-reduce.3.cloned.1.call-start
  115.5 0.7 all-reduce.3.cloned.1.call-update
  116.2 98.2 %all-reduce.5.cloned.1.call-done = f32[384,256]{1,0:T(8,128)} async-done(((f32[384,256]{1,0:T(8,128)}), f32[384,256]{1,0:T(8,128)}) %all-reduce.5.cloned.1.call-update) | async-done | bytes 393232 | tf_op jit(solution)/shard_map/psum | solution.py:396
  214.4 133.2 %all-reduce.3.cloned.1.call-done = f32[384,256]{1,0:T(8,128)} async-done(((f32[384,256]{1,0:T(8,128)}), f32[384,256]{1,0:T(8,128)}) %all-reduce.3.cloned.1.call-update) | async-done | bytes 393232 | tf_op jit(solution)/shard_map/psum | solution.py:396
  347.6 2.0 pad_maximum_fusion
  349.6 0.0 all-to-all-done.3.right_ref
  349.6 1.8 finish.1
Async XLA Ops:
  8.9 11.8 %collective-permute-start.1 = (f32[128,512]{1,0:T(8,128)S(1)}, f32[128,512]{1,0:T(8,128)S(1)}, u32[]{:S(2)}, u32[]{:S(2)}) collective-permute-start(f32[128,512]{1,0:T(8,128)S(1)} %get-tuple-element.21.first_ref.refs_0_), channel_id=1, source_target_pairs={{0,3},{1,0},{2,1},{3,2},{4,7},{5,4},{6,5},{7,6},{8,11},{9,8},{10,9... | collective-permute-start | bytes 786440 | tf_op jit(solution)/shard_map/ppermute | solution.py:325
  14.0 12.1 %collective-permute-start = (f32[128,512]{1,0:T(8,128)S(1)}, f32[128,512]{1,0:T(8,128)S(1)}, u32[]{:S(2)}, u32[]{:S(2)}) collective-permute-start(f32[128,512]{1,0:T(8,128)S(1)} %get-tuple-element.21.first_ref.refs_0_), channel_id=1, source_target_pairs={{0,1},{1,2},{2,3},{3,0},{4,5},{5,6},{6,7},{7,4},{8,9},{9,10},{10,1... | collective-permute-start | bytes 786440 | tf_op jit(solution)/shard_map/ppermute | solution.py:325
  26.2 10.4 %collective-permute-start.2 = (f32[128,512]{1,0:T(8,128)S(1)}, f32[128,512]{1,0:T(8,128)S(1)}, u32[]{:S(2)}, u32[]{:S(2)}) collective-permute-start(f32[128,512]{1,0:T(8,128)S(1)} %select_select_fusion.3), channel_id=1, source_target_pairs={{1,0},{2,3},{3,1},{0,2},{5,4},{6,7},{7,5},{4,6},{9,8},{10,11},{11,... | collective-permute-start | bytes 786440 | tf_op jit(solution)/shard_map/ppermute | solution.py:339
  36.6 11.9 %collective-permute-start.4 = (f32[128,512]{1,0:T(8,128)S(1)}, f32[128,512]{1,0:T(8,128)S(1)}, u32[]{:S(2)}, u32[]{:S(2)}) collective-permute-start(f32[128,512]{1,0:T(8,128)S(1)} %get-tuple-element.30.refs_1_), channel_id=1, source_target_pairs={{0,1},{1,2},{2,3},{3,0},{4,5},{5,6},{6,7},{7,4},{8,9},{9,10},{10,1... | collective-permute-start | bytes 786440 | tf_op jit(solution)/shard_map/ppermute | solution.py:325
  39.7 11.5 %collective-permute-start.3 = (f32[128,512]{1,0:T(8,128)S(1)}, f32[128,512]{1,0:T(8,128)S(1)}, u32[]{:S(2)}, u32[]{:S(2)}) collective-permute-start(f32[128,512]{1,0:T(8,128)S(1)} %get-tuple-element.30.refs_1_), channel_id=1, source_target_pairs={{0,3},{1,0},{2,1},{3,2},{4,7},{5,4},{6,5},{7,6},{8,11},{9,8},{10,9... | collective-permute-start | bytes 786440 | tf_op jit(solution)/shard_map/ppermute | solution.py:325
  44.2 16.2 %all-to-all-start = ((f32[8,128,128]{2,1,0:T(8,128)}), f32[8,128,128]{2,1,0:T(8,128)S(1)}, u32[]{:S(2)}, u32[]{:S(2)}) async-start(f32[8,128,128]{2,1,0:T(8,128)} %product.8), calls=%async_computation | async-start | bytes 1048576 | tf_op jit(solution)/shard_map/all_to_all | solution.py:329
  51.2 9.2 %copy-start = (s32[1,8,1]{1,2,0:T(1,128)S(1)}, s32[1,8,1]{1,2,0:T(1,128)}, u32[]{:S(2)}) copy-start(s32[1,8,1]{1,2,0:T(1,128)} %param.20) | copy-start | bytes 100
  51.2 9.2 %collective-permute-start.5 = (f32[128,512]{1,0:T(8,128)S(1)}, f32[128,512]{1,0:T(8,128)S(1)}, u32[]{:S(2)}, u32[]{:S(2)}) collective-permute-start(f32[128,512]{1,0:T(8,128)S(1)} %select_select_fusion.2), channel_id=1, source_target_pairs={{1,0},{2,3},{3,1},{0,2},{5,4},{6,7},{7,5},{4,6},{9,8},{10,11},{11,... | collective-permute-start | bytes 786440 | tf_op jit(solution)/shard_map/ppermute | solution.py:339
  61.0 11.1 %collective-permute-start.7 = (f32[128,512]{1,0:T(8,128)S(1)}, f32[128,512]{1,0:T(8,128)S(1)}, u32[]{:S(2)}, u32[]{:S(2)}) collective-permute-start(f32[128,512]{1,0:T(8,128)S(1)} %carry.2.refs_1_), channel_id=1, source_target_pairs={{0,1},{1,2},{2,3},{3,0},{4,5},{5,6},{6,7},{7,4},{8,9},{9,10},{10,1... | collective-permute-start | bytes 786440 | tf_op jit(solution)/shard_map/ppermute | solution.py:325
  63.7 12.5 %collective-permute-start.6 = (f32[128,512]{1,0:T(8,128)S(1)}, f32[128,512]{1,0:T(8,128)S(1)}, u32[]{:S(2)}, u32[]{:S(2)}) collective-permute-start(f32[128,512]{1,0:T(8,128)S(1)} %carry.2.refs_1_), channel_id=1, source_target_pairs={{0,3},{1,0},{2,1},{3,2},{4,7},{5,4},{6,5},{7,6},{8,11},{9,8},{10,9... | collective-permute-start | bytes 786440 | tf_op jit(solution)/shard_map/ppermute | solution.py:325
  68.5 16.0 %all-to-all-start.2 = ((f32[8,128,128]{2,1,0:T(8,128)}), f32[8,128,128]{2,1,0:T(8,128)S(1)}, u32[]{:S(2)}, u32[]{:S(2)}) async-start(f32[8,128,128]{2,1,0:T(8,128)} %product.11), calls=%async_computation.2 | async-start | bytes 1048576 | tf_op jit(solution)/shard_map/all_to_all | solution.py:329
  72.0 142.4 %all-reduce.5.cloned.1.call-start = ((), (), s32[]{:S(2)}) async-start(), calls=%async_computation.5 | async-start | bytes 786432 | tf_op jit(solution)/shard_map/psum | solution.py:396
  76.3 8.2 %collective-permute-start.8 = (f32[128,512]{1,0:T(8,128)S(1)}, f32[128,512]{1,0:T(8,128)S(1)}, u32[]{:S(2)}, u32[]{:S(2)}) collective-permute-start(f32[128,512]{1,0:T(8,128)S(1)} %select_select_fusion.1), channel_id=1, source_target_pairs={{1,0},{2,3},{3,1},{0,2},{5,4},{6,7},{7,5},{4,6},{9,8},{10,11},{11,... | collective-permute-start | bytes 786440 | tf_op jit(solution)/shard_map/ppermute | solution.py:339
  85.2 11.4 %collective-permute-start.10 = (f32[128,512]{1,0:T(8,128)S(1)}, f32[128,512]{1,0:T(8,128)S(1)}, u32[]{:S(2)}, u32[]{:S(2)}) collective-permute-start(f32[128,512]{1,0:T(8,128)S(1)} %carry.3.refs_1_), channel_id=1, source_target_pairs={{0,1},{1,2},{2,3},{3,0},{4,5},{5,6},{6,7},{7,4},{8,9},{9,10},{10,1... | collective-permute-start | bytes 786440 | tf_op jit(solution)/shard_map/ppermute | solution.py:325
  86.7 13.3 %collective-permute-start.9 = (f32[128,512]{1,0:T(8,128)S(1)}, f32[128,512]{1,0:T(8,128)S(1)}, u32[]{:S(2)}, u32[]{:S(2)}) collective-permute-start(f32[128,512]{1,0:T(8,128)S(1)} %carry.3.refs_1_), channel_id=1, source_target_pairs={{0,3},{1,0},{2,1},{3,2},{4,7},{5,4},{6,5},{7,6},{8,11},{9,8},{10,9... | collective-permute-start | bytes 786440 | tf_op jit(solution)/shard_map/ppermute | solution.py:325
  92.6 19.3 %all-to-all-start.1 = ((f32[8,128,128]{2,1,0:T(8,128)}), f32[8,128,128]{2,1,0:T(8,128)S(1)}, u32[]{:S(2)}, u32[]{:S(2)}) async-start(f32[8,128,128]{2,1,0:T(8,128)} %product.10), calls=%async_computation.1 | async-start | bytes 1048576 | tf_op jit(solution)/shard_map/all_to_all | solution.py:329
  100.1 8.1 %collective-permute-start.11 = (f32[128,512]{1,0:T(8,128)S(1)}, f32[128,512]{1,0:T(8,128)S(1)}, u32[]{:S(2)}, u32[]{:S(2)}) collective-permute-start(f32[128,512]{1,0:T(8,128)S(1)} %select_select_fusion), channel_id=1, source_target_pairs={{1,0},{2,3},{3,1},{0,2},{5,4},{6,7},{7,5},{4,6},{9,8},{10,11},{11,... | collective-permute-start | bytes 786440 | tf_op jit(solution)/shard_map/ppermute | solution.py:339
  111.9 237.7 %all-to-all-start.3 = ((f32[8,128,128]{2,1,0:T(8,128)}), f32[8,128,128]{2,1,0:T(8,128)S(1)}, u32[]{:S(2)}, u32[]{:S(2)}) async-start(f32[8,128,128]{2,1,0:T(8,128)} %product.13), calls=%async_computation.3 | async-start | bytes 1048576 | tf_op jit(solution)/shard_map/all_to_all | solution.py:329
  115.4 232.2 %all-reduce.3.cloned.1.call-start = ((), (), s32[]{:S(2)}) async-start(), calls=%async_computation.4 | async-start | bytes 786432 | tf_op jit(solution)/shard_map/psum | solution.py:396
Sparse Core Ops, SparseCore 0:
  89.2 125.1 all-reduce.4
  221.1 126.4 all-reduce.2

commit v11 on v8

--- a/solution.py
+++ b/solution.py
@@ -263,9 +263,11 @@
         for k in range(1, n_col):
             share = share + ordered[k]
         rows = share.shape[0]
-        for j in range(NODES_DEV // LANES):
+        groups = NODES_DEV // LANES // 2
+        for j in range(groups):
             for q in range(n_row):
-                out_ref[q, H + j * rows : H + (j + 1) * rows, :] = share[:, j * LANES : (j + 1) * LANES]
+                from_lane = (q % 2 * groups + j) * LANES
+                out_ref[q, H + j * rows : H + (j + 1) * rows, :] = share[:, from_lane : from_lane + LANES]
     for p in range(n_row // 2):
         here = slice(p * WIDE, (p + 1) * WIDE)
         total = None
@@ -293,7 +295,7 @@
     ]
     if carriers:
         rows = carriers[0].shape[0] - H
-        share = rows * NODES_DEV // LANES
+        share = rows * NODES_DEV // LANES // 2
         scratch.append(pltpu.VMEM((n_col, rows, NODES_DEV), F32))
     shape = (n_row, H + share, TB) if last else (H, n_row * TB)
     count = n + has_prev + len(carriers)
@@ -365,28 +367,34 @@
     )(owners, base, left, right)
 
 
-def assemble_kernel(n_row, came_ref, out_ref, turned):
+def assemble_kernel(n_row, row_ref, own_ref, other_ref, out_ref, halves, turned):
     rows = F // n_row
-    per = F // LANES
+    half = lax.rem(row_ref[0], 2)
+    halves[half] = own_ref[:, H:, :]
+    halves[1 - half] = other_ref[:, H:, :]
+    groups = 3 * F // LANES // 2
     for q in range(n_row):
-        for j in range(3 * per):
-            here = slice(H + j * rows, H + (j + 1) * rows)
-            turned[q * rows : (q + 1) * rows, j * LANES : (j + 1) * LANES] = came_ref[q, here, :]
+        for j in range(2 * groups):
+            here = slice(j % groups * rows, (j % groups + 1) * rows)
+            turned[q * rows : (q + 1) * rows, j * LANES : (j + 1) * LANES] = halves[j // groups, q, here, :]
     for k in range(3):
         out_ref[k] = turned[:, k * F : (k + 1) * F].T
 
 
-def assemble(n_row, came):
+def assemble(n_row, row, own, other):
     return pl.pallas_call(
         functools.partial(assemble_kernel, n_row),
-        in_specs=[VMEM],
+        in_specs=[SMEM, VMEM, VMEM],
         out_specs=VMEM,
         out_shape=jax.ShapeDtypeStruct((3, F, F), F32),
-        scratch_shapes=[pltpu.VMEM((F, 3 * F), F32)],
+        scratch_shapes=[
+            pltpu.VMEM((2, n_row, own.shape[1] - H, LANES), F32),
+            pltpu.VMEM((F, 3 * F), F32),
+        ],
         compiler_params=params(16),
         cost_estimate=LIGHT,
         name="assemble",
-    )(came)
+    )(row, own, other)
 
 
 def shift(n_col, x, step):
@@ -486,8 +494,10 @@
     right_early = early(*common, right_steps)
 
     right_came = exchange(final(*common, right_steps, right_early))
-    weight_grad = assemble(n_row, left_came)
-    return finish(n_row, owners, diff, left_came, right_came), weight_grad
+    other = lax.ppermute(left_came, "row", [(r, r ^ 1) for r in range(n_row)])
+    row = lax.axis_index("row").astype(jnp.int32).reshape(1)
+    weight_grad = assemble(n_row, row, left_came, other)
+    return finish(n_row, owners, after(diff, weight_grad), left_came, right_came), weight_grad
 
 
 def solution(mesh):

time: 132 us -> 139 us (1.053)
  local copies, waits for them, and re-layouts: 1.68 us -> 6.65 us
  starting transfers between devices: 45 us -> 40.8 us
  waiting for transfers between devices: 30.7 us -> 34.9 us
    ppermute x8, waiting for transfers between devices: 9.61 us -> 20.8 us  [shift(): lax.ppermute(x, 'col', [(c, (c + step) % n_col) for c in range(n_col)])]
    all_to_all x5, waiting for transfers between devices: 14.3 us -> 8.51 us  [exchange(): lax.all_to_all(pieces, 'row', split_axis=0, concat_axis=0, tiled=True)]
    unnamed x10 -> x22, local copies, waits for them, and re-layouts: 1.68 us -> 6.65 us
    all_to_all x5, starting transfers between devices: 24.4 us -> 19.7 us  [exchange(): lax.all_to_all(pieces, 'row', split_axis=0, concat_axis=0, tiled=True)]
  transfers between devices with their start and end apart: 17 -> 18, of which waited for: 8 -> 10; matrix products, arithmetic and copies ran while one was open for 0% -> 1% of each run, Pallas kernels for 36% -> 36%
where the time goes in v11:
time: 139 us; the launch traced here: 138 us
  Pallas kernels  53.6 us (39%)
  starting transfers between devices  40.8 us (29%)
  waiting for transfers between devices  34.9 us (25%)
  local copies, waits for them, and re-layouts  6.65 us (5%)
  between operations  1.49 us (1%)
    pallas_call x7, Pallas kernels, product(): pl.pallas_call(functools.partial(product_kernel, n_row, n_col, origins, h...  31.5 us
    ppermute x8, waiting for transfers between devices, shift(): lax.ppermute(x, 'col', [(c, (c + step) % n_col) for c in range(n_col)])  20.8 us
    all_to_all x5, starting transfers between devices, exchange(): lax.all_to_all(pieces, 'row', split_axis=0, concat_axis=0, tiled=True)  19.7 us
    ppermute x8, starting transfers between devices, shift(): lax.ppermute(x, 'col', [(c, (c + step) % n_col) for c in range(n_col)])  16.7 us
    pallas_call x1, Pallas kernels, build_operator(): pl.pallas_call(functools.partial(operator_kernel, n_col, origins), grid=(...  11.2 us
    all_to_all x5, waiting for transfers between devices, exchange(): lax.all_to_all(pieces, 'row', split_axis=0, concat_axis=0, tiled=True)  8.51 us
    unnamed x22, local copies, waits for them, and re-layouts  6.65 us
    ppermute x4, waiting for transfers between devices, opposite(): return lax.ppermute(sent, 'col', [(1, 0), (2, 3), (3, 1), (0, 2)])  5.54 us
  transfers between devices with their start and end apart: 18, of which 10 were waited for; matrix products, arithmetic and copies ran while one was open for 1% of the time, Pallas kernels for 36%

profile of v11, /device:TPU:0, one launch (start us, length us, event | category | flops | bytes accessed | tf_op | source)
XLA Modules:
  0.0 138.4 jit_solution(913308681248230827)
XLA Ops:
  0.6 1.7 %term_two.1 = (f32[128,512]{1,0:T(8,128)S(1)}, f32[128,512]{1,0:T(8,128)S(1)}) custom-call(f32[512,256]{1,0:T(8,128)} %grad_hbm.3, s32[512,256]{1,0:T(8,128)} %mask_hbm.3, f32[3,256,256]{2,1,0:T(8,128)} %weight_hbm.3), custom_call_target="tpu_custom_call" | custom-call | flops 1024 | bytes 1024 | tf_op jit(solution)/shard_map/term_two/pallas_call | solution.py:75
  2.4 5.1 %collective-permute-start.1 = (f32[128,512]{1,0:T(8,128)S(1)}, f32[128,512]{1,0:T(8,128)S(1)}, u32[]{:S(2)}, u32[]{:S(2)}) collective-permute-start(f32[128,512]{1,0:T(8,128)S(1)} %get-tuple-element.19.first_ref.refs_0_), channel_id=1, source_target_pairs={{0,3},{1,0},{2,1},{3,2},{4,7},{5,4},{6,5},{7,6},{8,11},{9,8},{10,9... | collective-permute-start | bytes 786440 | tf_op jit(solution)/shard_map/ppermute | solution.py:401
  7.5 0.0 collective-permute-start
  7.5 4.9 %local_terms.1 = (f32[128,512]{1,0:T(8,128)S(1)}, f32[128,512]{1,0:T(8,128)S(1)}, f32[256,512]{1,0:T(8,128)S(1)}, f32[8,192,128]{2,1,0:T(8,128)}) custom-call(f32[128,512]{1,0:T(8,128)S(1)} %get-tuple-element.19.first_ref.refs_0_, f32[512,256]{1,0:T(8,128)} %grad_hbm.3, s32[512,256]{1,0:T(8,128)} %mask_hbm.3, f32[3,256,256]{2,1,0:T(8,128)} %weight_hbm.3, ...), custom_call_target="tpu_custom_call" | custom-call | flops 1024 | bytes 1024 | tf_op jit(solution)/shard_map/local_terms/pallas_call | solution.py:120
  12.4 0.7 copy-done.6
  13.1 0.7 copy-done.8
  13.8 3.7 %all-to-all-start = ((f32[8,192,128]{2,1,0:T(8,128)}), f32[8,192,128]{2,1,0:T(8,128)S(1)}, u32[]{:S(2)}, u32[]{:S(2)}) async-start(f32[8,192,128]{2,1,0:T(8,128)} %get-tuple-element.29), calls=%async_computation | async-start | bytes 1572864 | tf_op jit(solution)/shard_map/all_to_all | solution.py:405
  18.2 0.0 collective-permute-done.1.refs_2_
  18.2 1.4 %collective-permute-done.refs_1_ = f32[128,512]{1,0:T(8,128)S(1)} collective-permute-done((f32[128,512]{1,0:T(8,128)S(1)}, f32[128,512]{1,0:T(8,128)S(1)}, u32[]{:S(2)}, u32[]{:S(2)}) %collective-permute-start) | collective-permute-done | bytes 262176 | tf_op jit(solution)/shard_map/ppermute | solution.py:401
  19.6 0.1 select_select_fusion.3
  19.6 0.8 collective-permute-start.2
  20.4 11.2 %operator.1 = (bf16[4,4,1024,256]{3,2,1,0:T(8,128)(2,1)}, f32[128,1024]{1,0:T(8,128)S(1)}) custom-call(s32[1]{0:T(128)} %bitcast.2.ids_ref.refs_0_, s32[1]{0:T(128)S(6)} %copy.13.live_ref, s32[1,128]{1,0:T(1,128)} %rows_hbm.1, s32[1,128]{1,0:T(1,128)} %slots_hbm.1, f32[1,128,128,128]{3,2,1,0:T(8,128)} %values_ref.1, ...), custom_call_target="tpu_custom_call" | custom-call | flops 17179869184 | bytes 67108864 | tf_op jit(solution)/shard_map/operator/pallas_call | solution.py:217
  31.6 0.0 collective-permute-done.2.refs_2_
  31.6 0.0 copy-start
  31.6 0.7 copy-done
  32.3 2.9 %collective-permute-start.4 = (f32[128,512]{1,0:T(8,128)S(1)}, f32[128,512]{1,0:T(8,128)S(1)}, u32[]{:S(2)}, u32[]{:S(2)}) collective-permute-start(f32[128,512]{1,0:T(8,128)S(1)} %get-tuple-element.26.refs_2_), channel_id=1, source_target_pairs={{0,1},{1,2},{2,3},{3,0},{4,5},{5,6},{6,7},{7,4},{8,9},{9,10},{10,1... | collective-permute-start | bytes 786440 | tf_op jit(solution)/shard_map/ppermute | solution.py:401
  35.2 0.9 collective-permute-start.3
  36.1 0.0 all-to-all-done.refs_0_
  36.2 0.9 copy-done.1
  37.1 3.5 %product.8 = f32[8,128,128]{2,1,0:T(8,128)} custom-call(s32[1]{0:T(128)} %bitcast.2.ids_ref.refs_0_, bf16[4,4,1024,256]{3,2,1,0:T(8,128)(2,1)} %get-tuple-element.21.refs_1_, f32[128,512]{1,0:T(8,128)S(1)} %copy-done.1, f32[128,1024]{1,0:T(8,128)S(1)} %get-tuple-element.30.refs_3_), custom_call_target="tpu_custom_call" | custom-call | flops 1024 | bytes 1024 | tf_op jit(solution)/shard_map/product/pallas_call | solution.py:302
  40.7 3.5 %all-to-all-start.1 = ((f32[8,128,128]{2,1,0:T(8,128)}), f32[8,128,128]{2,1,0:T(8,128)S(1)}, u32[]{:S(2)}, u32[]{:S(2)}) async-start(f32[8,128,128]{2,1,0:T(8,128)} %product.8), calls=%async_computation.1 | async-start | bytes 1048576 | tf_op jit(solution)/shard_map/all_to_all | solution.py:405
  44.2 0.0 collective-permute-done.4.refs_4_
  44.2 1.9 %collective-permute-done.3.refs_3_ = f32[128,512]{1,0:T(8,128)S(1)} collective-permute-done((f32[128,512]{1,0:T(8,128)S(1)}, f32[128,512]{1,0:T(8,128)S(1)}, u32[]{:S(2)}, u32[]{:S(2)}) %collective-permute-start.3) | collective-permute-done | bytes 262176 | tf_op jit(solution)/shard_map/ppermute | solution.py:401
  46.1 0.1 select_select_fusion.2
  46.1 0.0 copy-start.10
  46.2 1.6 %collective-permute-start.5 = (f32[128,512]{1,0:T(8,128)S(1)}, f32[128,512]{1,0:T(8,128)S(1)}, u32[]{:S(2)}, u32[]{:S(2)}) collective-permute-start(f32[128,512]{1,0:T(8,128)S(1)} %select_select_fusion.2), channel_id=1, source_target_pairs={{1,0},{2,3},{3,1},{0,2},{5,4},{6,7},{7,5},{4,6},{9,8},{10,11},{11,... | collective-permute-start | bytes 786440 | tf_op jit(solution)/shard_map/ppermute | solution.py:415
  47.7 5.4 %product.7.refs_3_ = f32[128,1024]{1,0:T(8,128)S(1)} custom-call(s32[1]{0:T(128)} %bitcast.2.ids_ref.refs_0_, bf16[4,4,1024,256]{3,2,1,0:T(8,128)(2,1)} %get-tuple-element.21.refs_1_, f32[128,512]{1,0:T(8,128)S(1)} %get-tuple-element.26.refs_2_, f32[128,512]{1,0:T(8,128)S(1)} %collective-permute-done.3.refs_3_, f32[128,512]{1,0:T(8,128)S(1)} %collective-permute-done.4.refs_4_), custom_call_target="tpu_custom_call" | custom-call | flops 17179869184 | bytes 67108864 | tf_op jit(solution)/shard_map/product/pallas_call | solution.py:302
  53.1 0.7 collective-permute-done.5.refs_2_
  53.9 0.7 copy-done.2
  54.6 0.0 all-to-all-done.1.came_ref
  54.6 0.9 copy-done.9
  55.5 0.7 carry.2.refs_2_.refs_4_
  56.2 1.9 %collective-permute-start.7 = (f32[176,512]{1,0:T(8,128)S(1)}, f32[176,512]{1,0:T(8,128)S(1)}, u32[]{:S(2)}, u32[]{:S(2)}) collective-permute-start(f32[176,512]{1,0:T(8,128)S(1)} %carry.2.refs_2_.refs_4_), channel_id=1, source_target_pairs={{0,1},{1,2},{2,3},{3,0},{4,5},{5,6},{6,7},{7,4},{8,9},{9,10},{10,1... | collective-permute-start | bytes 1081352 | tf_op jit(solution)/shard_map/ppermute | solution.py:401
  58.1 2.0 %collective-permute-start.6 = (f32[176,512]{1,0:T(8,128)S(1)}, f32[176,512]{1,0:T(8,128)S(1)}, u32[]{:S(2)}, u32[]{:S(2)}) collective-permute-start(f32[176,512]{1,0:T(8,128)S(1)} %carry.2.refs_2_.refs_4_), channel_id=1, source_target_pairs={{0,3},{1,0},{2,1},{3,2},{4,7},{5,4},{6,5},{7,6},{8,11},{9,8},{10,9... | collective-permute-start | bytes 1081352 | tf_op jit(solution)/shard_map/ppermute | solution.py:401
  60.1 0.9 copy-done.3
  61.0 3.6 %product.11 = f32[8,128,128]{2,1,0:T(8,128)} custom-call(s32[1]{0:T(128)} %bitcast.2.ids_ref.refs_0_, bf16[4,4,1024,256]{3,2,1,0:T(8,128)(2,1)} %get-tuple-element.21.refs_1_, f32[128,512]{1,0:T(8,128)S(1)} %copy-done.3, f32[128,1024]{1,0:T(8,128)S(1)} %product.7.refs_3_), custom_call_target="tpu_custom_call" | custom-call | flops 1024 | bytes 1024 | tf_op jit(solution)/shard_map/product/pallas_call | solution.py:302
  64.6 4.3 %all-to-all-start.3 = ((f32[8,128,128]{2,1,0:T(8,128)}), f32[8,128,128]{2,1,0:T(8,128)S(1)}, u32[]{:S(2)}, u32[]{:S(2)}) async-start(f32[8,128,128]{2,1,0:T(8,128)} %product.11), calls=%async_computation.3 | async-start | bytes 1048576 | tf_op jit(solution)/shard_map/all_to_all | solution.py:405
  68.9 0.6 collective-permute-done.7.refs_3_.refs_7_
  69.5 5.3 %collective-permute-done.6.refs_4_.refs_5_ = f32[176,512]{1,0:T(8,128)S(1)} collective-permute-done((f32[176,512]{1,0:T(8,128)S(1)}, f32[176,512]{1,0:T(8,128)S(1)}, u32[]{:S(2)}, u32[]{:S(2)}) %collective-permute-start.6) | collective-permute-done | bytes 360480 | tf_op jit(solution)/shard_map/ppermute | solution.py:401
  74.7 0.1 select_select_fusion
  74.8 0.8 collective-permute-start.8
  75.6 5.4 %product.9.refs_3_ = f32[128,1024]{1,0:T(8,128)S(1)} custom-call(s32[1]{0:T(128)} %bitcast.2.ids_ref.refs_0_, bf16[4,4,1024,256]{3,2,1,0:T(8,128)(2,1)} %get-tuple-element.21.refs_1_, f32[176,512]{1,0:T(8,128)S(1)} %carry.2.refs_2_.refs_4_, f32[176,512]{1,0:T(8,128)S(1)} %collective-permute-done.7.refs_3_.refs_7_, ...), custom_call_target="tpu_custom_call" | custom-call | flops 17179869184 | bytes 67108864 | tf_op jit(solution)/shard_map/product/pallas_call | solution.py:302
  81.0 4.4 %collective-permute-done.8.refs_2_.refs_6_ = f32[176,512]{1,0:T(8,128)S(1)} collective-permute-done((f32[176,512]{1,0:T(8,128)S(1)}, f32[176,512]{1,0:T(8,128)S(1)}, u32[]{:S(2)}, u32[]{:S(2)}) %collective-permute-start.8) | collective-permute-done | bytes 360480 | tf_op jit(solution)/shard_map/ppermute | solution.py:415
  85.4 3.7 %product.10 = f32[8,224,128]{2,1,0:T(8,128)} custom-call(s32[1]{0:T(128)} %bitcast.2.ids_ref.refs_0_, bf16[4,4,1024,256]{3,2,1,0:T(8,128)(2,1)} %get-tuple-element.21.refs_1_, f32[176,512]{1,0:T(8,128)S(1)} %collective-permute-done.8.refs_2_.refs_6_, f32[128,1024]{1,0:T(8,128)S(1)} %product.9.refs_3_, f32[176,512]{1,0:T(8,128)S(1)} %carry.2.refs_2_.refs_4_, ...), custom_call_target="tpu_custom_call" | custom-call | flops 1024 | bytes 1024 | tf_op jit(solution)/shard_map/product/pallas_call | solution.py:302
  89.1 0.0 all-to-all-done.3.came_ref
  89.1 4.4 %all-to-all-start.2 = ((f32[8,224,128]{2,1,0:T(8,128)}), f32[8,224,128]{2,1,0:T(8,128)S(1)}, u32[]{:S(2)}, u32[]{:S(2)}) async-start(f32[8,224,128]{2,1,0:T(8,128)} %product.10), calls=%async_computation.2 | async-start | bytes 1835008 | tf_op jit(solution)/shard_map/all_to_all | solution.py:405
  93.6 0.7 carry.3.refs_2_
  94.2 1.5 %collective-permute-start.11 = (f32[128,512]{1,0:T(8,128)S(1)}, f32[128,512]{1,0:T(8,128)S(1)}, u32[]{:S(2)}, u32[]{:S(2)}) collective-permute-start(f32[128,512]{1,0:T(8,128)S(1)} %carry.3.refs_2_), channel_id=1, source_target_pairs={{0,1},{1,2},{2,3},{3,0},{4,5},{5,6},{6,7},{7,4},{8,9},{9,10},{10,1... | collective-permute-start | bytes 786440 | tf_op jit(solution)/shard_map/ppermute | solution.py:401
  95.8 2.3 %collective-permute-start.10 = (f32[128,512]{1,0:T(8,128)S(1)}, f32[128,512]{1,0:T(8,128)S(1)}, u32[]{:S(2)}, u32[]{:S(2)}) collective-permute-start(f32[128,512]{1,0:T(8,128)S(1)} %carry.3.refs_2_), channel_id=1, source_target_pairs={{0,3},{1,0},{2,1},{3,2},{4,7},{5,4},{6,5},{7,6},{8,11},{9,8},{10,9... | collective-permute-start | bytes 786440 | tf_op jit(solution)/shard_map/ppermute | solution.py:401
  98.1 7.1 %collective-permute-done.11.refs_4_ = f32[128,512]{1,0:T(8,128)S(1)} collective-permute-done((f32[128,512]{1,0:T(8,128)S(1)}, f32[128,512]{1,0:T(8,128)S(1)}, u32[]{:S(2)}, u32[]{:S(2)}) %collective-permute-start.11) | collective-permute-done | bytes 262176 | tf_op jit(solution)/shard_map/ppermute | solution.py:401
  105.2 4.6 %collective-permute-done.10.refs_3_ = f32[128,512]{1,0:T(8,128)S(1)} collective-permute-done((f32[128,512]{1,0:T(8,128)S(1)}, f32[128,512]{1,0:T(8,128)S(1)}, u32[]{:S(2)}, u32[]{:S(2)}) %collective-permute-start.10) | collective-permute-done | bytes 262176 | tf_op jit(solution)/shard_map/ppermute | solution.py:401
  109.8 0.8 select_select_fusion.1
  110.6 1.2 collective-permute-start.12
  111.8 0.0 all-to-all-done.2.own_ref.left_ref
  111.8 0.0 collective-permute-start.9
  111.8 0.0 copy-start.5
  111.8 0.9 copy-done.5
  112.8 5.4 %product.12.refs_3_ = f32[128,1024]{1,0:T(8,128)S(1)} custom-call(s32[1]{0:T(128)} %bitcast.2.ids_ref.refs_0_, bf16[4,4,1024,256]{3,2,1,0:T(8,128)(2,1)} %get-tuple-element.21.refs_1_, f32[128,512]{1,0:T(8,128)S(1)} %carry.3.refs_2_, f32[128,512]{1,0:T(8,128)S(1)} %copy-done.5, f32[128,512]{1,0:T(8,128)S(1)} %collective-permute-done.11.refs_4_), custom_call_target="tpu_custom_call" | custom-call | flops 17179869184 | bytes 67108864 | tf_op jit(solution)/shard_map/product/pallas_call | solution.py:302
  118.2 0.4 collective-permute-done.12.refs_2_
  118.6 4.5 %product.13 = f32[8,128,128]{2,1,0:T(8,128)} custom-call(s32[1]{0:T(128)} %bitcast.2.ids_ref.refs_0_, bf16[4,4,1024,256]{3,2,1,0:T(8,128)(2,1)} %get-tuple-element.21.refs_1_, f32[128,512]{1,0:T(8,128)} %collective-permute-done.12.refs_2_, f32[128,1024]{1,0:T(8,128)S(1)} %product.12.refs_3_), custom_call_target="tpu_custom_call" | custom-call | flops 1024 | bytes 1024 | tf_op jit(solution)/shard_map/product/pallas_call | solution.py:302
  123.1 3.8 %all-to-all-start.4 = ((f32[8,128,128]{2,1,0:T(8,128)}), f32[8,128,128]{2,1,0:T(8,128)S(1)}, u32[]{:S(2)}, u32[]{:S(2)}) async-start(f32[8,128,128]{2,1,0:T(8,128)} %product.13), calls=%async_computation.4 | async-start | bytes 1048576 | tf_op jit(solution)/shard_map/all_to_all | solution.py:405
  126.9 1.2 assemble.1
  128.1 8.5 %all-to-all-done.4.right_ref = f32[8,128,128]{2,1,0:T(8,128)S(1)} async-done(((f32[8,128,128]{2,1,0:T(8,128)}), f32[8,128,128]{2,1,0:T(8,128)S(1)}, u32[]{:S(2)}, u32[]{:S(2)}) %all-to-all-start.4) | async-done | bytes 524320 | tf_op jit(solution)/shard_map/all_to_all | solution.py:405
  136.6 1.8 %finish.1 = f32[512,256]{1,0:T(8,128)} custom-call(s32[8]{0:T(128)S(1)} %bitcast.5, f32[256,512]{1,0:T(8,128)S(1)} %get-tuple-element.32.base_ref, f32[8,224,128]{2,1,0:T(8,128)S(1)} %all-to-all-done.2.own_ref.left_ref, f32[8,128,128]{2,1,0:T(8,128)S(1)} %all-to-all-done.4.right_ref), custom_call_target="tpu_custom_call" | custom-call | flops 1024 | bytes 1024 | tf_op jit(solution)/shard_map/finish/pallas_call | solution.py:358
  (12 shorter events, 0.0 us)
Async XLA Ops:
  2.4 15.8 %collective-permute-start.1 = (f32[128,512]{1,0:T(8,128)S(1)}, f32[128,512]{1,0:T(8,128)S(1)}, u32[]{:S(2)}, u32[]{:S(2)}) collective-permute-start(f32[128,512]{1,0:T(8,128)S(1)} %get-tuple-element.19.first_ref.refs_0_), channel_id=1, source_target_pairs={{0,3},{1,0},{2,1},{3,2},{4,7},{5,4},{6,5},{7,6},{8,11},{9,8},{10,9... | collective-permute-start | bytes 786440 | tf_op jit(solution)/shard_map/ppermute | solution.py:401
  7.5 12.1 %collective-permute-start = (f32[128,512]{1,0:T(8,128)S(1)}, f32[128,512]{1,0:T(8,128)S(1)}, u32[]{:S(2)}, u32[]{:S(2)}) collective-permute-start(f32[128,512]{1,0:T(8,128)S(1)} %get-tuple-element.19.first_ref.refs_0_), channel_id=1, source_target_pairs={{0,1},{1,2},{2,3},{3,0},{4,5},{5,6},{6,7},{7,4},{8,9},{9,10},{10,1... | collective-permute-start | bytes 786440 | tf_op jit(solution)/shard_map/ppermute | solution.py:401
  12.4 0.7 copy-start.6
  13.1 0.7 copy-start.8
  13.8 22.3 %all-to-all-start = ((f32[8,192,128]{2,1,0:T(8,128)}), f32[8,192,128]{2,1,0:T(8,128)S(1)}, u32[]{:S(2)}, u32[]{:S(2)}) async-start(f32[8,192,128]{2,1,0:T(8,128)} %get-tuple-element.29), calls=%async_computation | async-start | bytes 1572864 | tf_op jit(solution)/shard_map/all_to_all | solution.py:405
  19.6 12.0 %collective-permute-start.2 = (f32[128,512]{1,0:T(8,128)S(1)}, f32[128,512]{1,0:T(8,128)S(1)}, u32[]{:S(2)}, u32[]{:S(2)}) collective-permute-start(f32[128,512]{1,0:T(8,128)S(1)} %select_select_fusion.3), channel_id=1, source_target_pairs={{1,0},{2,3},{3,1},{0,2},{5,4},{6,7},{7,5},{4,6},{9,8},{10,11},{11,... | collective-permute-start | bytes 786440 | tf_op jit(solution)/shard_map/ppermute | solution.py:415
  31.6 0.7 copy-start
  32.3 11.9 %collective-permute-start.4 = (f32[128,512]{1,0:T(8,128)S(1)}, f32[128,512]{1,0:T(8,128)S(1)}, u32[]{:S(2)}, u32[]{:S(2)}) collective-permute-start(f32[128,512]{1,0:T(8,128)S(1)} %get-tuple-element.26.refs_2_), channel_id=1, source_target_pairs={{0,1},{1,2},{2,3},{3,0},{4,5},{5,6},{6,7},{7,4},{8,9},{9,10},{10,1... | collective-permute-start | bytes 786440 | tf_op jit(solution)/shard_map/ppermute | solution.py:401
  35.2 10.9 %collective-permute-start.3 = (f32[128,512]{1,0:T(8,128)S(1)}, f32[128,512]{1,0:T(8,128)S(1)}, u32[]{:S(2)}, u32[]{:S(2)}) collective-permute-start(f32[128,512]{1,0:T(8,128)S(1)} %get-tuple-element.26.refs_2_), channel_id=1, source_target_pairs={{0,3},{1,0},{2,1},{3,2},{4,7},{5,4},{6,5},{7,6},{8,11},{9,8},{10,9... | collective-permute-start | bytes 786440 | tf_op jit(solution)/shard_map/ppermute | solution.py:401
  36.1 1.0 copy-start.1
  40.7 13.9 %all-to-all-start.1 = ((f32[8,128,128]{2,1,0:T(8,128)}), f32[8,128,128]{2,1,0:T(8,128)S(1)}, u32[]{:S(2)}, u32[]{:S(2)}) async-start(f32[8,128,128]{2,1,0:T(8,128)} %product.8), calls=%async_computation.1 | async-start | bytes 1048576 | tf_op jit(solution)/shard_map/all_to_all | solution.py:405
  46.1 8.4 %copy-start.10 = (s32[1,8,1]{1,2,0:T(1,128)S(1)}, s32[1,8,1]{1,2,0:T(1,128)}, u32[]{:S(2)}) copy-start(s32[1,8,1]{1,2,0:T(1,128)} %param.20) | copy-start | bytes 100
  46.2 7.7 %collective-permute-start.5 = (f32[128,512]{1,0:T(8,128)S(1)}, f32[128,512]{1,0:T(8,128)S(1)}, u32[]{:S(2)}, u32[]{:S(2)}) collective-permute-start(f32[128,512]{1,0:T(8,128)S(1)} %select_select_fusion.2), channel_id=1, source_target_pairs={{1,0},{2,3},{3,1},{0,2},{5,4},{6,7},{7,5},{4,6},{9,8},{10,11},{11,... | collective-permute-start | bytes 786440 | tf_op jit(solution)/shard_map/ppermute | solution.py:415
  53.9 0.7 copy-start.2
  54.6 1.0 copy-start.9
  56.2 13.2 %collective-permute-start.7 = (f32[176,512]{1,0:T(8,128)S(1)}, f32[176,512]{1,0:T(8,128)S(1)}, u32[]{:S(2)}, u32[]{:S(2)}) collective-permute-start(f32[176,512]{1,0:T(8,128)S(1)} %carry.2.refs_2_.refs_4_), channel_id=1, source_target_pairs={{0,1},{1,2},{2,3},{3,0},{4,5},{5,6},{6,7},{7,4},{8,9},{9,10},{10,1... | collective-permute-start | bytes 1081352 | tf_op jit(solution)/shard_map/ppermute | solution.py:401
  58.1 16.6 %collective-permute-start.6 = (f32[176,512]{1,0:T(8,128)S(1)}, f32[176,512]{1,0:T(8,128)S(1)}, u32[]{:S(2)}, u32[]{:S(2)}) collective-permute-start(f32[176,512]{1,0:T(8,128)S(1)} %carry.2.refs_2_.refs_4_), channel_id=1, source_target_pairs={{0,3},{1,0},{2,1},{3,2},{4,7},{5,4},{6,5},{7,6},{8,11},{9,8},{10,9... | collective-permute-start | bytes 1081352 | tf_op jit(solution)/shard_map/ppermute | solution.py:401
  60.1 0.9 copy-start.3
  64.6 24.5 %all-to-all-start.3 = ((f32[8,128,128]{2,1,0:T(8,128)}), f32[8,128,128]{2,1,0:T(8,128)S(1)}, u32[]{:S(2)}, u32[]{:S(2)}) async-start(f32[8,128,128]{2,1,0:T(8,128)} %product.11), calls=%async_computation.3 | async-start | bytes 1048576 | tf_op jit(solution)/shard_map/all_to_all | solution.py:405
  74.8 10.6 %collective-permute-start.8 = (f32[176,512]{1,0:T(8,128)S(1)}, f32[176,512]{1,0:T(8,128)S(1)}, u32[]{:S(2)}, u32[]{:S(2)}) collective-permute-start(f32[176,512]{1,0:T(8,128)S(1)} %select_select_fusion), channel_id=1, source_target_pairs={{1,0},{2,3},{3,1},{0,2},{5,4},{6,7},{7,5},{4,6},{9,8},{10,11},{11,... | collective-permute-start | bytes 1081352 | tf_op jit(solution)/shard_map/ppermute | solution.py:415
  81.0 12.6 %copy-start.7 = (f32[128,512]{1,0:T(8,128)S(1)}, f32[128,512]{1,0:T(8,128)}, u32[]{:S(2)}) copy-start(f32[128,512]{1,0:T(8,128)} %copy-done.6) | copy-start | bytes 786436
  89.1 22.7 %all-to-all-start.2 = ((f32[8,224,128]{2,1,0:T(8,128)}), f32[8,224,128]{2,1,0:T(8,128)S(1)}, u32[]{:S(2)}, u32[]{:S(2)}) async-start(f32[8,224,128]{2,1,0:T(8,128)} %product.10), calls=%async_computation.2 | async-start | bytes 1835008 | tf_op jit(solution)/shard_map/all_to_all | solution.py:405
  94.2 11.0 %collective-permute-start.11 = (f32[128,512]{1,0:T(8,128)S(1)}, f32[128,512]{1,0:T(8,128)S(1)}, u32[]{:S(2)}, u32[]{:S(2)}) collective-permute-start(f32[128,512]{1,0:T(8,128)S(1)} %carry.3.refs_2_), channel_id=1, source_target_pairs={{0,1},{1,2},{2,3},{3,0},{4,5},{5,6},{6,7},{7,4},{8,9},{9,10},{10,1... | collective-permute-start | bytes 786440 | tf_op jit(solution)/shard_map/ppermute | solution.py:401
  95.8 14.0 %collective-permute-start.10 = (f32[128,512]{1,0:T(8,128)S(1)}, f32[128,512]{1,0:T(8,128)S(1)}, u32[]{:S(2)}, u32[]{:S(2)}) collective-permute-start(f32[128,512]{1,0:T(8,128)S(1)} %carry.3.refs_2_), channel_id=1, source_target_pairs={{0,3},{1,0},{2,1},{3,2},{4,7},{5,4},{6,5},{7,6},{8,11},{9,8},{10,9... | collective-permute-start | bytes 786440 | tf_op jit(solution)/shard_map/ppermute | solution.py:401
  109.8 2.0 %copy-start.4 = (f32[128,512]{1,0:T(8,128)}, f32[128,512]{1,0:T(8,128)S(1)}, u32[]{:S(2)}) copy-start(f32[128,512]{1,0:T(8,128)S(1)} %collective-permute-done.10.refs_3_) | copy-start | bytes 786436
  110.6 8.0 %collective-permute-start.12 = (f32[128,512]{1,0:T(8,128)}, f32[128,512]{1,0:T(8,128)}, u32[]{:S(2)}, u32[]{:S(2)}) collective-permute-start(f32[128,512]{1,0:T(8,128)} %select_select_fusion.1), channel_id=1, source_target_pairs={{1,0},{2,3},{3,1},{0,2},{5,4},{6,7},{7,5},{4,6},{9,8},{10,11},{11,... | collective-permute-start | bytes 786440 | tf_op jit(solution)/shard_map/ppermute | solution.py:415
  111.8 15.0 %collective-permute-start.9 = (f32[8,224,128]{2,1,0:T(8,128)S(1)}, f32[8,224,128]{2,1,0:T(8,128)S(1)}, u32[]{:S(2)}, u32[]{:S(2)}) collective-permute-start(f32[8,224,128]{2,1,0:T(8,128)S(1)} %all-to-all-done.2.own_ref.left_ref), channel_id=1, source_target_pairs={{0,4},{4,0},{8,12},{12,8},{16,20},{20,16},{24,28},{28,24},{1,5},{5... | collective-permute-start | bytes 2752520 | tf_op jit(solution)/shard_map/ppermute | solution.py:497
  111.8 1.0 copy-start.5
  123.1 13.5 %all-to-all-start.4 = ((f32[8,128,128]{2,1,0:T(8,128)}), f32[8,128,128]{2,1,0:T(8,128)S(1)}, u32[]{:S(2)}, u32[]{:S(2)}) async-start(f32[8,128,128]{2,1,0:T(8,128)} %product.13), calls=%async_computation.4 | async-start | bytes 1048576 | tf_op jit(solution)/shard_map/all_to_all | solution.py:405

commit v12 on v11

--- a/solution.py
+++ b/solution.py
@@ -25,6 +25,7 @@
 SMEM = pl.BlockSpec(memory_space=pltpu.SMEM)
 VMEM = pl.BlockSpec(memory_space=pltpu.VMEM)
 HBM = pl.BlockSpec(memory_space=pltpu.HBM)
+ANY = pl.BlockSpec(memory_space=pl.ANY)
 
 
 def params(mib):
@@ -90,8 +91,8 @@
 
 
 def local_kernel(
-    n_row, first_ref, grad_hbm, mask_hbm, weight_hbm, h0, h1, h2, left_ref, right_ref, diff_ref, pieces_ref,
-    grad, mask, weight, bases, sems,
+    n_row, first_ref, grad_hbm, mask_hbm, weight_hbm, h0, h1, h2, left_hbm, right_hbm, diff_ref, pieces_ref,
+    grad, mask, weight, bases, one, sems, one_sems,
 ):
     sources = (grad_hbm, mask_hbm, weight_hbm, h0, h1, h2)
     copies = fetch(sources, (grad, mask, weight, bases.at[0], bases.at[1], bases.at[2]), sems)
@@ -100,8 +101,8 @@
     values = masked_of(grad[...], mask[...])
     masked = split(values)
     term = dot3(split(weight[1]), masked, ((1,), (1,)))
-    left_ref[...] = term[:H]
-    right_ref[...] = term[H:]
+    one[...] = term
+    one_copies = fetch((one.at[pl.ds(0, H)], one.at[pl.ds(H, H)]), (left_hbm, right_hbm), one_sems)
     diff_ref[...] = dot3(split(weight[0] - weight[2]), masked, ((1,), (1,)))
     turned = split(values.T)
     rows = F // n_row
@@ -112,15 +113,17 @@
             here = (k * (F // LANES) + j) * rows
             for q in range(n_row):
                 pieces_ref[q, here : here + rows, :] = part[q * rows : (q + 1) * rows, j * LANES : (j + 1) * LANES]
+    for copy in one_copies:
+        copy.wait()
 
 
 def local_terms(n_row, first, grad_out, relu_mask, cheb_weight, b0, b1, b2):
-    half = jax.ShapeDtypeStruct((H, NODES_DEV), F32)
+    half = pltpu.HBM((H, NODES_DEV), F32)
     share = 3 * F * F // n_row // LANES
     return pl.pallas_call(
         functools.partial(local_kernel, n_row),
-        in_specs=[pl.BlockSpec(memory_space=pl.ANY)] + [HBM] * 6,
-        out_specs=[VMEM] * 4,
+        in_specs=[ANY] + [HBM] * 6,
+        out_specs=[HBM, HBM, VMEM, VMEM],
         out_shape=[
             half,
             half,
@@ -132,7 +135,9 @@
             pltpu.VMEM((NODES_DEV, F), jnp.int32),
             pltpu.VMEM((3, F, F), F32),
             pltpu.VMEM((3, NODES_DEV, F), F32),
+            pltpu.VMEM((F, NODES_DEV), F32),
             pltpu.SemaphoreType.DMA((6,)),
+            pltpu.SemaphoreType.DMA((2,)),
         ],
         compiler_params=params(32),
         cost_estimate=LIGHT,
@@ -246,17 +251,21 @@
     if has_prev:
         prev, refs = refs[0], refs[1:]
     carriers, refs = refs[:n_carriers], refs[n_carriers:]
-    out_ref, buf, sems = refs[:3]
+    out_ref, held, buf, field_sems, sems = refs[:5]
 
     def copy(k, p):
         return pltpu.make_async_copy(op_ref.at[origins[k], p], buf.at[k, p], sems.at[k, p])
 
+    field_copies = fetch([x.at[pl.ds(0, H)] for x in fields], [held.at[k] for k in range(n)], field_sems)
     for p in range(n_row // 2):
         for k in range(n):
             copy(k, p).start()
-    left = [stacked(field[:H, :]) for field in fields]
+    left = []
+    for k in range(n):
+        field_copies[k].wait()
+        left.append(stacked(held[k]))
     if n_carriers:
-        ordered = refs[3]
+        ordered = refs[5]
         for k in range(n_col):
             ordered[lax.rem(ids_ref[0] + k, n_col)] = carriers[k][H:, :]
         share = ordered[0]
@@ -290,7 +299,9 @@
     has_prev = prev is not None
     share = 0
     scratch = [
+        pltpu.VMEM((n, H, NODES_DEV), F32),
         pltpu.VMEM((n, n_row // 2, 2 * NODES_DEV, WIDE), BF16),
+        pltpu.SemaphoreType.DMA((n,)),
         pltpu.SemaphoreType.DMA((n, n_row // 2)),
     ]
     if carriers:
@@ -298,10 +309,10 @@
         share = rows * NODES_DEV // LANES // 2
         scratch.append(pltpu.VMEM((n_col, rows, NODES_DEV), F32))
     shape = (n_row, H + share, TB) if last else (H, n_row * TB)
-    count = n + has_prev + len(carriers)
+    count = has_prev + len(carriers)
     return pl.pallas_call(
         functools.partial(product_kernel, n_row, n_col, origins, has_prev, last, len(carriers)),
-        in_specs=[SMEM, HBM] + [VMEM] * count,
+        in_specs=[SMEM, HBM] + [ANY] * n + [VMEM] * count,
         out_specs=VMEM,
         out_shape=jax.ShapeDtypeStruct(shape, F32),
         scratch_shapes=scratch,
@@ -317,12 +328,13 @@
     )
 
 
-def carry_kernel(n_row, rows, owners_ref, base_ref, came_ref, *refs):
-    out_ref = refs[-1]
-    out_ref[:H, :] = base_ref[...]
+def carry_kernel(n_row, rows, owners_ref, base_hbm, came_ref, *refs):
+    out_ref, base, sems = refs[-3:]
+    (base_copy,) = fetch([base_hbm], [base], sems)
+    out_ref[:H, :] = jnp.zeros((H, NODES_DEV), F32)
     for q in range(n_row):
         here = pl.ds(pl.multiple_of(owners_ref[q] * TB, TB), TB)
-        out_ref[:H, here] += 2.0 * came_ref[q]
+        out_ref[:H, here] += came_ref[q]
     if rows:
         pieces_ref = refs[0]
         share = pieces_ref[0]
@@ -330,19 +342,22 @@
             share = share + pieces_ref[q]
         for j in range(NODES_DEV // LANES):
             out_ref[H:, j * LANES : (j + 1) * LANES] = share[j * rows : (j + 1) * rows, :]
+    base_copy.wait()
+    out_ref[:H, :] = base[...] + 2.0 * out_ref[:H, :]
 
 
 def carry(n_row, owners, base, came, *pieces):
     rows = pieces[0].shape[1] * LANES // NODES_DEV if pieces else 0
     return pl.pallas_call(
         functools.partial(carry_kernel, n_row, rows),
-        in_specs=[SMEM] + [VMEM] * (2 + len(pieces)),
+        in_specs=[SMEM, HBM] + [VMEM] * (1 + len(pieces)),
         out_specs=VMEM,
         out_shape=jax.ShapeDtypeStruct((H + rows, NODES_DEV), F32),
+        scratch_shapes=[pltpu.VMEM((H, NODES_DEV), F32), pltpu.SemaphoreType.DMA((1,))],
         compiler_params=params(24),
         cost_estimate=LIGHT,
         name="carry",
-    )(owners, base, came, *pieces)
+    )(owners, *in_hbm(base), came, *pieces)
 
 
 def finish_kernel(n_row, owners_ref, base_ref, left_ref, right_ref, out_ref, total):
@@ -493,8 +508,9 @@
     left_came = exchange(final(*common, steps, left_early, carrying=True))
     right_early = early(*common, right_steps)
 
-    right_came = exchange(final(*common, right_steps, right_early))
-    other = lax.ppermute(left_came, "row", [(r, r ^ 1) for r in range(n_row)])
+    right_last = final(*common, right_steps, right_early)
+    right_came = exchange(right_last)
+    other = lax.ppermute(after(left_came, right_last), "row", [(r, r ^ 1) for r in range(n_row)])
     row = lax.axis_index("row").astype(jnp.int32).reshape(1)
     weight_grad = assemble(n_row, row, left_came, other)
     return finish(n_row, owners, after(diff, weight_grad), left_came, right_came), weight_grad

time: 139 us -> 127 us (0.914)
  waiting for transfers between devices: 34.9 us -> 27.6 us
  local copies, waits for them, and re-layouts: 6.65 us -> 0.01 us
  starting transfers between devices: 40.8 us -> 42.4 us
    ppermute x8, waiting for transfers between devices: 20.8 us -> 13.1 us  [shift(): lax.ppermute(x, 'col', [(c, (c + step) % n_col) for c in range(n_col)])]
    unnamed x22 -> x2, local copies, waits for them, and re-layouts: 6.65 us -> 0.01 us
    pallas_call x2, Pallas kernels: 1.35 us -> 3.06 us  [carry(): pl.pallas_call(functools.partial(carry_kernel, n_row, rows), in_specs=[SM...]
    pallas_call x1, Pallas kernels: 11.2 us -> 9.73 us  [build_operator(): pl.pallas_call(functools.partial(operator_kernel, n_col, origins), grid=(...]
  transfers between devices with their start and end apart: 18 -> 18, of which waited for: 10 -> 10; matrix products, arithmetic and copies ran while one was open for 1% -> 0% of each run, Pallas kernels for 36% -> 37%
where the time goes in v12:
time: 127 us; the launch traced here: 125 us
  Pallas kernels  53.4 us (42%)
  starting transfers between devices  42.4 us (33%)
  waiting for transfers between devices  27.6 us (22%)
  between operations  1.49 us (1%)
    pallas_call x7, Pallas kernels, product(): pl.pallas_call(functools.partial(product_kernel, n_row, n_col, origins, h...  30.9 us
    all_to_all x5, starting transfers between devices, exchange(): lax.all_to_all(pieces, 'row', split_axis=0, concat_axis=0, tiled=True)  20.1 us
    ppermute x8, starting transfers between devices, shift(): lax.ppermute(x, 'col', [(c, (c + step) % n_col) for c in range(n_col)])  16.7 us
    ppermute x8, waiting for transfers between devices, shift(): lax.ppermute(x, 'col', [(c, (c + step) % n_col) for c in range(n_col)])  13.1 us
    pallas_call x1, Pallas kernels, build_operator(): pl.pallas_call(functools.partial(operator_kernel, n_col, origins), grid=(...  9.73 us
    all_to_all x5, waiting for transfers between devices, exchange(): lax.all_to_all(pieces, 'row', split_axis=0, concat_axis=0, tiled=True)  9.32 us
    ppermute x4, starting transfers between devices, opposite(): return lax.ppermute(sent, 'col', [(1, 0), (2, 3), (3, 1), (0, 2)])  5.49 us
    ppermute x4, waiting for transfers between devices, opposite(): return lax.ppermute(sent, 'col', [(1, 0), (2, 3), (3, 1), (0, 2)])  5.22 us
  transfers between devices with their start and end apart: 18, of which 10 were waited for; matrix products, arithmetic and copies ran while one was open for 0% of the time, Pallas kernels for 37%

profile of v12, /device:TPU:0, one launch (start us, length us, event | category | flops | bytes accessed | tf_op | source)
XLA Modules:
  0.0 125.1 jit_solution(12663563691224623439)
XLA Ops:
  0.6 1.7 %term_two.1 = (f32[128,512]{1,0:T(8,128)S(1)}, f32[128,512]{1,0:T(8,128)S(1)}) custom-call(f32[512,256]{1,0:T(8,128)} %grad_hbm.3, s32[512,256]{1,0:T(8,128)} %mask_hbm.3, f32[3,256,256]{2,1,0:T(8,128)} %weight_hbm.3), custom_call_target="tpu_custom_call" | custom-call | flops 1024 | bytes 1024 | tf_op jit(solution)/shard_map/term_two/pallas_call | solution.py:76
  2.4 5.1 %collective-permute-start.1 = (f32[128,512]{1,0:T(8,128)S(1)}, f32[128,512]{1,0:T(8,128)S(1)}, u32[]{:S(2)}, u32[]{:S(2)}) collective-permute-start(f32[128,512]{1,0:T(8,128)S(1)} %get-tuple-element.20.first_ref.refs_0_), channel_id=1, source_target_pairs={{0,3},{1,0},{2,1},{3,2},{4,7},{5,4},{6,5},{7,6},{8,11},{9,8},{10,9... | collective-permute-start | bytes 786440 | tf_op jit(solution)/shard_map/ppermute | solution.py:416
  7.5 0.0 collective-permute-start
  7.5 4.9 %local_terms.1 = (f32[128,512]{1,0:T(8,128)}, f32[128,512]{1,0:T(8,128)}, f32[256,512]{1,0:T(8,128)S(1)}, f32[8,192,128]{2,1,0:T(8,128)}) custom-call(f32[128,512]{1,0:T(8,128)S(1)} %get-tuple-element.20.first_ref.refs_0_, f32[512,256]{1,0:T(8,128)} %grad_hbm.3, s32[512,256]{1,0:T(8,128)} %mask_hbm.3, f32[3,256,256]{2,1,0:T(8,128)} %weight_hbm.3, ...), custom_call_target="tpu_custom_call" | custom-call | flops 1024 | bytes 1024 | tf_op jit(solution)/shard_map/local_terms/pallas_call | solution.py:123
  12.4 3.7 %all-to-all-start = ((f32[8,192,128]{2,1,0:T(8,128)}), f32[8,192,128]{2,1,0:T(8,128)S(1)}, u32[]{:S(2)}, u32[]{:S(2)}) async-start(f32[8,192,128]{2,1,0:T(8,128)} %get-tuple-element.30), calls=%async_computation | async-start | bytes 1572864 | tf_op jit(solution)/shard_map/all_to_all | solution.py:420
  16.8 0.0 collective-permute-done.1.refs_2_
  16.8 2.8 %collective-permute-done.refs_1_ = f32[128,512]{1,0:T(8,128)S(1)} collective-permute-done((f32[128,512]{1,0:T(8,128)S(1)}, f32[128,512]{1,0:T(8,128)S(1)}, u32[]{:S(2)}, u32[]{:S(2)}) %collective-permute-start) | collective-permute-done | bytes 262176 | tf_op jit(solution)/shard_map/ppermute | solution.py:416
  19.6 0.1 select_select_fusion.3
  19.6 0.8 collective-permute-start.2
  20.4 9.7 %operator.1 = (bf16[4,4,1024,256]{3,2,1,0:T(8,128)(2,1)}, f32[128,1024]{1,0:T(8,128)S(1)}) custom-call(s32[1]{0:T(128)} %bitcast.2.ids_ref.refs_0_, s32[1]{0:T(128)S(6)} %copy.13.live_ref, s32[1,128]{1,0:T(1,128)} %rows_hbm.1, s32[1,128]{1,0:T(1,128)} %slots_hbm.1, f32[1,128,128,128]{3,2,1,0:T(8,128)} %values_ref.1, ...), custom_call_target="tpu_custom_call" | custom-call | flops 17179869184 | bytes 67108864 | tf_op jit(solution)/shard_map/operator/pallas_call | solution.py:222
  30.2 0.0 collective-permute-done.2.refs_2_
  30.2 1.4 %collective-permute-start.4 = (f32[128,512]{1,0:T(8,128)S(1)}, f32[128,512]{1,0:T(8,128)S(1)}, u32[]{:S(2)}, u32[]{:S(2)}) collective-permute-start(f32[128,512]{1,0:T(8,128)S(1)} %get-tuple-element.27.refs_2_), channel_id=1, source_target_pairs={{0,1},{1,2},{2,3},{3,0},{4,5},{5,6},{6,7},{7,4},{8,9},{9,10},{10,1... | collective-permute-start | bytes 786440 | tf_op jit(solution)/shard_map/ppermute | solution.py:416
  31.6 2.5 %collective-permute-start.3 = (f32[128,512]{1,0:T(8,128)S(1)}, f32[128,512]{1,0:T(8,128)S(1)}, u32[]{:S(2)}, u32[]{:S(2)}) collective-permute-start(f32[128,512]{1,0:T(8,128)S(1)} %get-tuple-element.27.refs_2_), channel_id=1, source_target_pairs={{0,3},{1,0},{2,1},{3,2},{4,7},{5,4},{6,5},{7,6},{8,11},{9,8},{10,9... | collective-permute-start | bytes 786440 | tf_op jit(solution)/shard_map/ppermute | solution.py:416
  34.0 0.0 all-to-all-done.refs_0_
  34.0 3.6 %product.8 = f32[8,128,128]{2,1,0:T(8,128)} custom-call(s32[1]{0:T(128)} %bitcast.2.ids_ref.refs_0_, bf16[4,4,1024,256]{3,2,1,0:T(8,128)(2,1)} %get-tuple-element.22.refs_1_, f32[128,512]{1,0:T(8,128)S(1)} %collective-permute-done.2.refs_2_, f32[128,1024]{1,0:T(8,128)S(1)} %get-tuple-element.31.refs_3_), custom_call_target="tpu_custom_call" | custom-call | flops 1024 | bytes 1024 | tf_op jit(solution)/shard_map/product/pallas_call | solution.py:313
  37.6 5.8 %all-to-all-start.1 = ((f32[8,128,128]{2,1,0:T(8,128)}), f32[8,128,128]{2,1,0:T(8,128)S(1)}, u32[]{:S(2)}, u32[]{:S(2)}) async-start(f32[8,128,128]{2,1,0:T(8,128)} %product.8), calls=%async_computation.1 | async-start | bytes 1048576 | tf_op jit(solution)/shard_map/all_to_all | solution.py:420
  43.4 0.0 collective-permute-done.4.refs_4_
  43.4 0.8 collective-permute-done.3.refs_3_
  44.2 0.1 select_select_fusion.2
  44.3 0.0 copy-start
  44.3 2.4 %collective-permute-start.5 = (f32[128,512]{1,0:T(8,128)S(1)}, f32[128,512]{1,0:T(8,128)S(1)}, u32[]{:S(2)}, u32[]{:S(2)}) collective-permute-start(f32[128,512]{1,0:T(8,128)S(1)} %select_select_fusion.2), channel_id=1, source_target_pairs={{1,0},{2,3},{3,1},{0,2},{5,4},{6,7},{7,5},{4,6},{9,8},{10,11},{11,... | collective-permute-start | bytes 786440 | tf_op jit(solution)/shard_map/ppermute | solution.py:430
  46.7 5.5 %product.7.refs_3_ = f32[128,1024]{1,0:T(8,128)S(1)} custom-call(s32[1]{0:T(128)} %bitcast.2.ids_ref.refs_0_, bf16[4,4,1024,256]{3,2,1,0:T(8,128)(2,1)} %get-tuple-element.22.refs_1_, f32[128,512]{1,0:T(8,128)S(1)} %get-tuple-element.27.refs_2_, f32[128,512]{1,0:T(8,128)S(1)} %collective-permute-done.3.refs_3_, f32[128,512]{1,0:T(8,128)S(1)} %collective-permute-done.4.refs_4_), custom_call_target="tpu_custom_call" | custom-call | flops 17179869184 | bytes 67108864 | tf_op jit(solution)/shard_map/product/pallas_call | solution.py:313
  52.2 0.1 collective-permute-done.5.refs_2_
  52.3 0.9 all-to-all-done.1.came_ref
  53.2 0.0 copy-done
  53.2 1.5 %carry.2.refs_2_.refs_4_ = f32[176,512]{1,0:T(8,128)S(1)} custom-call(s32[8]{0:T(128)S(1)} %bitcast.3, f32[128,512]{1,0:T(8,128)} %get-tuple-element.29.base_hbm, f32[8,128,128]{2,1,0:T(8,128)S(1)} %all-to-all-done.1.came_ref, f32[8,192,128]{2,1,0:T(8,128)S(1)} %all-to-all-done.refs_0_), custom_call_target="tpu_custom_call" | custom-call | flops 1024 | bytes 1024 | tf_op jit(solution)/shard_map/carry/pallas_call | solution.py:351
  54.7 0.9 collective-permute-start.7
  55.6 3.0 %collective-permute-start.6 = (f32[176,512]{1,0:T(8,128)S(1)}, f32[176,512]{1,0:T(8,128)S(1)}, u32[]{:S(2)}, u32[]{:S(2)}) collective-permute-start(f32[176,512]{1,0:T(8,128)S(1)} %carry.2.refs_2_.refs_4_), channel_id=1, source_target_pairs={{0,3},{1,0},{2,1},{3,2},{4,7},{5,4},{6,5},{7,6},{8,11},{9,8},{10,9... | collective-permute-start | bytes 1081352 | tf_op jit(solution)/shard_map/ppermute | solution.py:416
  58.6 3.6 %product.11 = f32[8,128,128]{2,1,0:T(8,128)} custom-call(s32[1]{0:T(128)} %bitcast.2.ids_ref.refs_0_, bf16[4,4,1024,256]{3,2,1,0:T(8,128)(2,1)} %get-tuple-element.22.refs_1_, f32[128,512]{1,0:T(8,128)S(1)} %collective-permute-done.5.refs_2_, f32[128,1024]{1,0:T(8,128)S(1)} %product.7.refs_3_), custom_call_target="tpu_custom_call" | custom-call | flops 1024 | bytes 1024 | tf_op jit(solution)/shard_map/product/pallas_call | solution.py:313
  62.2 3.5 %all-to-all-start.3 = ((f32[8,128,128]{2,1,0:T(8,128)}), f32[8,128,128]{2,1,0:T(8,128)S(1)}, u32[]{:S(2)}, u32[]{:S(2)}) async-start(f32[8,128,128]{2,1,0:T(8,128)} %product.11), calls=%async_computation.3 | async-start | bytes 1048576 | tf_op jit(solution)/shard_map/all_to_all | solution.py:420
  65.7 2.2 %collective-permute-done.7.refs_3_.refs_7_ = f32[176,512]{1,0:T(8,128)S(1)} collective-permute-done((f32[176,512]{1,0:T(8,128)S(1)}, f32[176,512]{1,0:T(8,128)S(1)}, u32[]{:S(2)}, u32[]{:S(2)}) %collective-permute-start.7) | collective-permute-done | bytes 360480 | tf_op jit(solution)/shard_map/ppermute | solution.py:416
  67.9 3.8 %collective-permute-done.6.refs_4_.refs_5_ = f32[176,512]{1,0:T(8,128)S(1)} collective-permute-done((f32[176,512]{1,0:T(8,128)S(1)}, f32[176,512]{1,0:T(8,128)S(1)}, u32[]{:S(2)}, u32[]{:S(2)}) %collective-permute-start.6) | collective-permute-done | bytes 360480 | tf_op jit(solution)/shard_map/ppermute | solution.py:416
  71.7 0.1 select_select_fusion
  71.8 1.6 %collective-permute-start.8 = (f32[176,512]{1,0:T(8,128)S(1)}, f32[176,512]{1,0:T(8,128)S(1)}, u32[]{:S(2)}, u32[]{:S(2)}) collective-permute-start(f32[176,512]{1,0:T(8,128)S(1)} %select_select_fusion), channel_id=1, source_target_pairs={{1,0},{2,3},{3,1},{0,2},{5,4},{6,7},{7,5},{4,6},{9,8},{10,11},{11,... | collective-permute-start | bytes 1081352 | tf_op jit(solution)/shard_map/ppermute | solution.py:430
  73.4 5.5 %product.9.refs_3_ = f32[128,1024]{1,0:T(8,128)S(1)} custom-call(s32[1]{0:T(128)} %bitcast.2.ids_ref.refs_0_, bf16[4,4,1024,256]{3,2,1,0:T(8,128)(2,1)} %get-tuple-element.22.refs_1_, f32[176,512]{1,0:T(8,128)S(1)} %carry.2.refs_2_.refs_4_, f32[176,512]{1,0:T(8,128)S(1)} %collective-permute-done.7.refs_3_.refs_7_, ...), custom_call_target="tpu_custom_call" | custom-call | flops 17179869184 | bytes 67108864 | tf_op jit(solution)/shard_map/product/pallas_call | solution.py:313
  78.9 3.1 %collective-permute-done.8.refs_2_.refs_6_ = f32[176,512]{1,0:T(8,128)S(1)} collective-permute-done((f32[176,512]{1,0:T(8,128)S(1)}, f32[176,512]{1,0:T(8,128)S(1)}, u32[]{:S(2)}, u32[]{:S(2)}) %collective-permute-start.8) | collective-permute-done | bytes 360480 | tf_op jit(solution)/shard_map/ppermute | solution.py:430
  82.0 0.0 all-to-all-done.3.came_ref
  82.0 1.5 %carry.3.refs_2_ = f32[128,512]{1,0:T(8,128)S(1)} custom-call(s32[8]{0:T(128)S(1)} %bitcast.4, f32[128,512]{1,0:T(8,128)} %get-tuple-element.34.base_hbm, f32[8,128,128]{2,1,0:T(8,128)S(1)} %all-to-all-done.3.came_ref), custom_call_target="tpu_custom_call" | custom-call | flops 1024 | bytes 1024 | tf_op jit(solution)/shard_map/carry/pallas_call | solution.py:351
  83.5 2.7 %collective-permute-start.10 = (f32[128,512]{1,0:T(8,128)S(1)}, f32[128,512]{1,0:T(8,128)S(1)}, u32[]{:S(2)}, u32[]{:S(2)}) collective-permute-start(f32[128,512]{1,0:T(8,128)S(1)} %carry.3.refs_2_), channel_id=1, source_target_pairs={{0,1},{1,2},{2,3},{3,0},{4,5},{5,6},{6,7},{7,4},{8,9},{9,10},{10,1... | collective-permute-start | bytes 786440 | tf_op jit(solution)/shard_map/ppermute | solution.py:416
  86.2 1.2 collective-permute-start.9
  87.4 3.8 %product.10 = f32[8,224,128]{2,1,0:T(8,128)} custom-call(s32[1]{0:T(128)} %bitcast.2.ids_ref.refs_0_, bf16[4,4,1024,256]{3,2,1,0:T(8,128)(2,1)} %get-tuple-element.22.refs_1_, f32[176,512]{1,0:T(8,128)S(1)} %collective-permute-done.8.refs_2_.refs_6_, f32[128,1024]{1,0:T(8,128)S(1)} %product.9.refs_3_, f32[176,512]{1,0:T(8,128)S(1)} %carry.2.refs_2_.refs_4_, ...), custom_call_target="tpu_custom_call" | custom-call | flops 1024 | bytes 1024 | tf_op jit(solution)/shard_map/product/pallas_call | solution.py:313
  91.2 3.6 %all-to-all-start.2 = ((f32[8,224,128]{2,1,0:T(8,128)}), f32[8,224,128]{2,1,0:T(8,128)S(1)}, u32[]{:S(2)}, u32[]{:S(2)}) async-start(f32[8,224,128]{2,1,0:T(8,128)} %product.10), calls=%async_computation.2 | async-start | bytes 1835008 | tf_op jit(solution)/shard_map/all_to_all | solution.py:420
  94.7 0.0 collective-permute-done.10.refs_4_
  94.8 3.5 %collective-permute-done.9.refs_3_ = f32[128,512]{1,0:T(8,128)} collective-permute-done((f32[128,512]{1,0:T(8,128)S(1)}, f32[128,512]{1,0:T(8,128)}, u32[]{:S(2)}, u32[]{:S(2)}) %collective-permute-start.9) | collective-permute-done | bytes 262176 | tf_op jit(solution)/shard_map/ppermute | solution.py:416
  98.2 0.1 select_select_fusion.1
  98.3 0.7 collective-permute-start.11
  99.0 5.5 %product.12.refs_3_ = f32[128,1024]{1,0:T(8,128)S(1)} custom-call(s32[1]{0:T(128)} %bitcast.2.ids_ref.refs_0_, bf16[4,4,1024,256]{3,2,1,0:T(8,128)(2,1)} %get-tuple-element.22.refs_1_, f32[128,512]{1,0:T(8,128)S(1)} %carry.3.refs_2_, f32[128,512]{1,0:T(8,128)} %collective-permute-done.9.refs_3_, f32[128,512]{1,0:T(8,128)S(1)} %collective-permute-done.10.refs_4_), custom_call_target="tpu_custom_call" | custom-call | flops 17179869184 | bytes 67108864 | tf_op jit(solution)/shard_map/product/pallas_call | solution.py:313
  104.5 2.0 %collective-permute-done.11.refs_2_ = f32[128,512]{1,0:T(8,128)S(1)} collective-permute-done((f32[128,512]{1,0:T(8,128)S(1)}, f32[128,512]{1,0:T(8,128)S(1)}, u32[]{:S(2)}, u32[]{:S(2)}) %collective-permute-start.11) | collective-permute-done | bytes 262176 | tf_op jit(solution)/shard_map/ppermute | solution.py:430
  106.5 3.6 %product.13 = f32[8,128,128]{2,1,0:T(8,128)} custom-call(s32[1]{0:T(128)} %bitcast.2.ids_ref.refs_0_, bf16[4,4,1024,256]{3,2,1,0:T(8,128)(2,1)} %get-tuple-element.22.refs_1_, f32[128,512]{1,0:T(8,128)S(1)} %collective-permute-done.11.refs_2_, f32[128,1024]{1,0:T(8,128)S(1)} %product.12.refs_3_), custom_call_target="tpu_custom_call" | custom-call | flops 1024 | bytes 1024 | tf_op jit(solution)/shard_map/product/pallas_call | solution.py:313
  110.1 0.0 all-to-all-done.2.own_ref.left_ref
  110.1 0.1 collective-permute-start.12
  110.2 3.5 %all-to-all-start.4 = ((f32[8,128,128]{2,1,0:T(8,128)}), f32[8,128,128]{2,1,0:T(8,128)S(1)}, u32[]{:S(2)}, u32[]{:S(2)}) async-start(f32[8,128,128]{2,1,0:T(8,128)} %product.13), calls=%async_computation.4 | async-start | bytes 1048576 | tf_op jit(solution)/shard_map/all_to_all | solution.py:420
  113.7 0.0 collective-permute-done.12.other_ref
  113.7 1.2 assemble.1
  115.0 8.4 %all-to-all-done.4.right_ref = f32[8,128,128]{2,1,0:T(8,128)S(1)} async-done(((f32[8,128,128]{2,1,0:T(8,128)}), f32[8,128,128]{2,1,0:T(8,128)S(1)}, u32[]{:S(2)}, u32[]{:S(2)}) %all-to-all-start.4) | async-done | bytes 524320 | tf_op jit(solution)/shard_map/all_to_all | solution.py:420
  123.4 1.8 %finish.1 = f32[512,256]{1,0:T(8,128)} custom-call(s32[8]{0:T(128)S(1)} %bitcast.5, f32[256,512]{1,0:T(8,128)S(1)} %get-tuple-element.37.base_ref, f32[8,224,128]{2,1,0:T(8,128)S(1)} %all-to-all-done.2.own_ref.left_ref, f32[8,128,128]{2,1,0:T(8,128)S(1)} %all-to-all-done.4.right_ref), custom_call_target="tpu_custom_call" | custom-call | flops 1024 | bytes 1024 | tf_op jit(solution)/shard_map/finish/pallas_call | solution.py:373
Async XLA Ops:
  2.4 14.4 %collective-permute-start.1 = (f32[128,512]{1,0:T(8,128)S(1)}, f32[128,512]{1,0:T(8,128)S(1)}, u32[]{:S(2)}, u32[]{:S(2)}) collective-permute-start(f32[128,512]{1,0:T(8,128)S(1)} %get-tuple-element.20.first_ref.refs_0_), channel_id=1, source_target_pairs={{0,3},{1,0},{2,1},{3,2},{4,7},{5,4},{6,5},{7,6},{8,11},{9,8},{10,9... | collective-permute-start | bytes 786440 | tf_op jit(solution)/shard_map/ppermute | solution.py:416
  7.5 12.1 %collective-permute-start = (f32[128,512]{1,0:T(8,128)S(1)}, f32[128,512]{1,0:T(8,128)S(1)}, u32[]{:S(2)}, u32[]{:S(2)}) collective-permute-start(f32[128,512]{1,0:T(8,128)S(1)} %get-tuple-element.20.first_ref.refs_0_), channel_id=1, source_target_pairs={{0,1},{1,2},{2,3},{3,0},{4,5},{5,6},{6,7},{7,4},{8,9},{9,10},{10,1... | collective-permute-start | bytes 786440 | tf_op jit(solution)/shard_map/ppermute | solution.py:416
  12.4 21.7 %all-to-all-start = ((f32[8,192,128]{2,1,0:T(8,128)}), f32[8,192,128]{2,1,0:T(8,128)S(1)}, u32[]{:S(2)}, u32[]{:S(2)}) async-start(f32[8,192,128]{2,1,0:T(8,128)} %get-tuple-element.30), calls=%async_computation | async-start | bytes 1572864 | tf_op jit(solution)/shard_map/all_to_all | solution.py:420
  19.6 10.5 %collective-permute-start.2 = (f32[128,512]{1,0:T(8,128)S(1)}, f32[128,512]{1,0:T(8,128)S(1)}, u32[]{:S(2)}, u32[]{:S(2)}) collective-permute-start(f32[128,512]{1,0:T(8,128)S(1)} %select_select_fusion.3), channel_id=1, source_target_pairs={{1,0},{2,3},{3,1},{0,2},{5,4},{6,7},{7,5},{4,6},{9,8},{10,11},{11,... | collective-permute-start | bytes 786440 | tf_op jit(solution)/shard_map/ppermute | solution.py:430
  30.2 13.3 %collective-permute-start.4 = (f32[128,512]{1,0:T(8,128)S(1)}, f32[128,512]{1,0:T(8,128)S(1)}, u32[]{:S(2)}, u32[]{:S(2)}) collective-permute-start(f32[128,512]{1,0:T(8,128)S(1)} %get-tuple-element.27.refs_2_), channel_id=1, source_target_pairs={{0,1},{1,2},{2,3},{3,0},{4,5},{5,6},{6,7},{7,4},{8,9},{9,10},{10,1... | collective-permute-start | bytes 786440 | tf_op jit(solution)/shard_map/ppermute | solution.py:416
  31.6 12.7 %collective-permute-start.3 = (f32[128,512]{1,0:T(8,128)S(1)}, f32[128,512]{1,0:T(8,128)S(1)}, u32[]{:S(2)}, u32[]{:S(2)}) collective-permute-start(f32[128,512]{1,0:T(8,128)S(1)} %get-tuple-element.27.refs_2_), channel_id=1, source_target_pairs={{0,3},{1,0},{2,1},{3,2},{4,7},{5,4},{6,5},{7,6},{8,11},{9,8},{10,9... | collective-permute-start | bytes 786440 | tf_op jit(solution)/shard_map/ppermute | solution.py:416
  37.6 15.5 %all-to-all-start.1 = ((f32[8,128,128]{2,1,0:T(8,128)}), f32[8,128,128]{2,1,0:T(8,128)S(1)}, u32[]{:S(2)}, u32[]{:S(2)}) async-start(f32[8,128,128]{2,1,0:T(8,128)} %product.8), calls=%async_computation.1 | async-start | bytes 1048576 | tf_op jit(solution)/shard_map/all_to_all | solution.py:420
  44.3 8.9 %copy-start = (s32[1,8,1]{1,2,0:T(1,128)S(1)}, s32[1,8,1]{1,2,0:T(1,128)}, u32[]{:S(2)}) copy-start(s32[1,8,1]{1,2,0:T(1,128)} %param.20) | copy-start | bytes 100
  44.3 8.0 %collective-permute-start.5 = (f32[128,512]{1,0:T(8,128)S(1)}, f32[128,512]{1,0:T(8,128)S(1)}, u32[]{:S(2)}, u32[]{:S(2)}) collective-permute-start(f32[128,512]{1,0:T(8,128)S(1)} %select_select_fusion.2), channel_id=1, source_target_pairs={{1,0},{2,3},{3,1},{0,2},{5,4},{6,7},{7,5},{4,6},{9,8},{10,11},{11,... | collective-permute-start | bytes 786440 | tf_op jit(solution)/shard_map/ppermute | solution.py:430
  54.7 13.2 %collective-permute-start.7 = (f32[176,512]{1,0:T(8,128)S(1)}, f32[176,512]{1,0:T(8,128)S(1)}, u32[]{:S(2)}, u32[]{:S(2)}) collective-permute-start(f32[176,512]{1,0:T(8,128)S(1)} %carry.2.refs_2_.refs_4_), channel_id=1, source_target_pairs={{0,1},{1,2},{2,3},{3,0},{4,5},{5,6},{6,7},{7,4},{8,9},{9,10},{10,1... | collective-permute-start | bytes 1081352 | tf_op jit(solution)/shard_map/ppermute | solution.py:416
  55.6 16.1 %collective-permute-start.6 = (f32[176,512]{1,0:T(8,128)S(1)}, f32[176,512]{1,0:T(8,128)S(1)}, u32[]{:S(2)}, u32[]{:S(2)}) collective-permute-start(f32[176,512]{1,0:T(8,128)S(1)} %carry.2.refs_2_.refs_4_), channel_id=1, source_target_pairs={{0,3},{1,0},{2,1},{3,2},{4,7},{5,4},{6,5},{7,6},{8,11},{9,8},{10,9... | collective-permute-start | bytes 1081352 | tf_op jit(solution)/shard_map/ppermute | solution.py:416
  62.2 19.8 %all-to-all-start.3 = ((f32[8,128,128]{2,1,0:T(8,128)}), f32[8,128,128]{2,1,0:T(8,128)S(1)}, u32[]{:S(2)}, u32[]{:S(2)}) async-start(f32[8,128,128]{2,1,0:T(8,128)} %product.11), calls=%async_computation.3 | async-start | bytes 1048576 | tf_op jit(solution)/shard_map/all_to_all | solution.py:420
  71.8 10.2 %collective-permute-start.8 = (f32[176,512]{1,0:T(8,128)S(1)}, f32[176,512]{1,0:T(8,128)S(1)}, u32[]{:S(2)}, u32[]{:S(2)}) collective-permute-start(f32[176,512]{1,0:T(8,128)S(1)} %select_select_fusion), channel_id=1, source_target_pairs={{1,0},{2,3},{3,1},{0,2},{5,4},{6,7},{7,5},{4,6},{9,8},{10,11},{11,... | collective-permute-start | bytes 1081352 | tf_op jit(solution)/shard_map/ppermute | solution.py:430
  83.5 11.2 %collective-permute-start.10 = (f32[128,512]{1,0:T(8,128)S(1)}, f32[128,512]{1,0:T(8,128)S(1)}, u32[]{:S(2)}, u32[]{:S(2)}) collective-permute-start(f32[128,512]{1,0:T(8,128)S(1)} %carry.3.refs_2_), channel_id=1, source_target_pairs={{0,1},{1,2},{2,3},{3,0},{4,5},{5,6},{6,7},{7,4},{8,9},{9,10},{10,1... | collective-permute-start | bytes 786440 | tf_op jit(solution)/shard_map/ppermute | solution.py:416
  86.2 12.0 %collective-permute-start.9 = (f32[128,512]{1,0:T(8,128)S(1)}, f32[128,512]{1,0:T(8,128)}, u32[]{:S(2)}, u32[]{:S(2)}) collective-permute-start(f32[128,512]{1,0:T(8,128)S(1)} %carry.3.refs_2_), channel_id=1, source_target_pairs={{0,3},{1,0},{2,1},{3,2},{4,7},{5,4},{6,5},{7,6},{8,11},{9,8},{10,9... | collective-permute-start | bytes 786440 | tf_op jit(solution)/shard_map/ppermute | solution.py:416
  91.2 18.9 %all-to-all-start.2 = ((f32[8,224,128]{2,1,0:T(8,128)}), f32[8,224,128]{2,1,0:T(8,128)S(1)}, u32[]{:S(2)}, u32[]{:S(2)}) async-start(f32[8,224,128]{2,1,0:T(8,128)} %product.10), calls=%async_computation.2 | async-start | bytes 1835008 | tf_op jit(solution)/shard_map/all_to_all | solution.py:420
  98.3 8.2 %collective-permute-start.11 = (f32[128,512]{1,0:T(8,128)S(1)}, f32[128,512]{1,0:T(8,128)S(1)}, u32[]{:S(2)}, u32[]{:S(2)}) collective-permute-start(f32[128,512]{1,0:T(8,128)S(1)} %select_select_fusion.1), channel_id=1, source_target_pairs={{1,0},{2,3},{3,1},{0,2},{5,4},{6,7},{7,5},{4,6},{9,8},{10,11},{11,... | collective-permute-start | bytes 786440 | tf_op jit(solution)/shard_map/ppermute | solution.py:430
  110.1 3.6 %collective-permute-start.12 = (f32[8,224,128]{2,1,0:T(8,128)S(1)}, f32[8,224,128]{2,1,0:T(8,128)S(1)}, u32[]{:S(2)}, u32[]{:S(2)}) collective-permute-start(f32[8,224,128]{2,1,0:T(8,128)S(1)} %all-to-all-done.2.own_ref.left_ref), channel_id=1, source_target_pairs={{0,4},{4,0},{8,12},{12,8},{16,20},{20,16},{24,28},{28,24},{1,5},{5... | collective-permute-start | bytes 2752520 | tf_op jit(solution)/shard_map/ppermute | solution.py:513
  110.2 13.2 %all-to-all-start.4 = ((f32[8,128,128]{2,1,0:T(8,128)}), f32[8,128,128]{2,1,0:T(8,128)S(1)}, u32[]{:S(2)}, u32[]{:S(2)}) async-start(f32[8,128,128]{2,1,0:T(8,128)} %product.13), calls=%async_computation.4 | async-start | bytes 1048576 | tf_op jit(solution)/shard_map/all_to_all | solution.py:420

commit v13 on v12

--- a/solution.py
+++ b/solution.py
@@ -150,17 +150,26 @@
     return jnp.concatenate([jnp.concatenate([x, x], axis=1) for x in (high, low)], axis=0)
 
 
+def add_block(acc, entry, block):
+    position = entry // TILES_DEV
+    slot = position // CHB
+    at_row = pl.ds(pl.multiple_of(lax.rem(position, CHB) * TB, TB), TB)
+    at_lane = pl.ds(pl.multiple_of(lax.rem(slot, 2) * TB, TB), TB)
+    acc[slot // 2, at_row, at_lane] += block
+
+
 def operator_kernel(n_col, origins, ids_ref, live_ref, rows_hbm, slots_hbm, values_ref, *refs):
     fields, refs = refs[: len(origins)], refs[len(origins) :]
-    out_ref, total_ref, tiles, acc, lists, counts, rows, slots, sems, small_sems = refs
-    origin = pl.program_id(0)
+    out_ref, total_ref, lists, counts, tiles, acc, rows, slots, sems, small_sems = refs
+    step = pl.program_id(0)
+    origin = jnp.where(step < n_col // 2, step, step + 1)
     size = TILES_DEV // GROUPS
 
     def copy(g):
         part = pl.ds(g * size, size)
         return pltpu.make_async_copy(values_ref.at[0, part], tiles.at[part], sems.at[g])
 
-    @pl.when(origin == 0)
+    @pl.when(step == 0)
     def _():
         small = fetch((rows_hbm, slots_hbm), (rows, slots), small_sems)
         for g in range(GROUPS):
@@ -183,18 +192,14 @@
 
     acc[...] = jnp.zeros_like(acc)
 
-    @pl.when(origin == 0)
+    @pl.when(step == 0)
     def _():
         for g in range(GROUPS):
             copy(g).wait()
 
     def add(n, carry):
         entry = lists[origin, n]
-        position = entry // TILES_DEV
-        slot = position // CHB
-        at_row = pl.ds(pl.multiple_of(lax.rem(position, CHB) * TB, TB), TB)
-        at_lane = pl.ds(pl.multiple_of(lax.rem(slot, 2) * TB, TB), TB)
-        acc[slot // 2, at_row, at_lane] += tiles[lax.rem(entry, TILES_DEV)]
+        add_block(acc, entry, tiles[lax.rem(entry, TILES_DEV)])
         return carry
 
     lax.fori_loop(0, counts[origin], add, 0)
@@ -221,18 +226,23 @@
     origins, fields = zip(*pairs)
     return pl.pallas_call(
         functools.partial(operator_kernel, n_col, origins),
-        grid=(n_col,),
+        grid=(n_col - 1,),
         in_specs=[SMEM] * 2 + [HBM] * 3 + [pl.BlockSpec((H, NODES_DEV), lambda s: (0, 0))] * len(fields),
         out_specs=[
             pl.BlockSpec((1,) + part, lambda s: (s, 0, 0, 0)),
             pl.BlockSpec((H, n_row * TB), lambda s: (0, 0)),
-        ],
-        out_shape=[pltpu.HBM((n_col,) + part, BF16), jax.ShapeDtypeStruct((H, n_row * TB), F32)],
+            SMEM,
+            SMEM,
+        ],
+        out_shape=[
+            pltpu.HBM((n_col - 1,) + part, BF16),
+            jax.ShapeDtypeStruct((H, n_row * TB), F32),
+            jax.ShapeDtypeStruct((n_col, TILES_DEV), jnp.int32),
+            jax.ShapeDtypeStruct((n_col,), jnp.int32),
+        ],
         scratch_shapes=[
             pltpu.VMEM((TILES_DEV, TB, TB), F32),
             pltpu.VMEM((n_row // 2, NODES_DEV, WIDE), F32),
-            pltpu.SMEM((n_col, TILES_DEV), jnp.int32),
-            pltpu.SMEM((n_col,), jnp.int32),
             pltpu.SMEM((1, TILES_DEV), jnp.int32),
             pltpu.SMEM((1, TILES_DEV), jnp.int32),
             pltpu.SemaphoreType.DMA((GROUPS,)),
@@ -244,14 +254,79 @@
     )(ids, live, *in_hbm(rows, slots, values), *fields)
 
 
-def product_kernel(n_row, n_col, origins, has_prev, last, n_carriers, *refs):
+def opposite_kernel(n_row, origin, lists, counts, values_ref, field_ref, prev, op_ref, out_ref, tiles, acc, held, buf, *sems):
+    tile_sems, field_sems, out_sems = sems
+
+    def copy(n):
+        t = lax.rem(lists[origin, n], TILES_DEV)
+        return pltpu.make_async_copy(values_ref.at[0, t], tiles.at[n], tile_sems.at[n])
+
+    def begin(n, carry):
+        copy(n).start()
+        return carry
+
+    (field_copy,) = fetch([field_ref], [held], field_sems)
+    lax.fori_loop(0, counts[origin], begin, 0)
+    acc[...] = jnp.zeros_like(acc)
+    field_copy.wait()
+    left = stacked(held[...])
+
+    def add(n, carry):
+        copy(n).wait()
+        add_block(acc, lists[origin, n], tiles[n])
+        return carry
+
+    lax.fori_loop(0, counts[origin], add, 0)
+    copies = []
+    for p in range(n_row // 2):
+        here = slice(p * WIDE, (p + 1) * WIDE)
+        high, low = split(acc[p])
+        buf[p, :NODES_DEV, :] = high
+        buf[p, NODES_DEV:, :] = low
+        copies.append(pltpu.make_async_copy(buf.at[p], op_ref.at[0, p], out_sems.at[p]))
+        copies[-1].start()
+        part = jnp.dot(left, buf[p], preferred_element_type=F32)
+        summed = part[:H] + part[H:] + prev[:, here]
+        out_ref[2 * p] = summed[:, :TB]
+        out_ref[2 * p + 1] = summed[:, TB:]
+    for item in copies:
+        item.wait()
+
+
+def build_opposite(n_row, n_col, lists, counts, values, field, prev):
+    part = (n_row // 2, 2 * NODES_DEV, WIDE)
+    return pl.pallas_call(
+        functools.partial(opposite_kernel, n_row, n_col // 2),
+        in_specs=[SMEM, SMEM, HBM, ANY, VMEM],
+        out_specs=[HBM, VMEM],
+        out_shape=[pltpu.HBM((1,) + part, BF16), jax.ShapeDtypeStruct((n_row, H, TB), F32)],
+        scratch_shapes=[
+            pltpu.VMEM((TILES_DEV, TB, TB), F32),
+            pltpu.VMEM((n_row // 2, NODES_DEV, WIDE), F32),
+            pltpu.VMEM((H, NODES_DEV), F32),
+            pltpu.VMEM(part, BF16),
+            pltpu.SemaphoreType.DMA((TILES_DEV,)),
+            pltpu.SemaphoreType.DMA((1,)),
+            pltpu.SemaphoreType.DMA((n_row // 2,)),
+        ],
+        compiler_params=params(48),
+        cost_estimate=LIGHT,
+        name="opposite",
+    )(lists, counts, *in_hbm(values), field, prev)
+
+
+def product_kernel(n_row, n_col, origins, has_prev, last, n_carriers, has_base, *refs):
     n = len(origins)
     ids_ref, op_ref, refs = refs[0], refs[1], refs[2:]
     fields, refs = refs[:n], refs[n:]
     if has_prev:
         prev, refs = refs[0], refs[1:]
     carriers, refs = refs[:n_carriers], refs[n_carriers:]
-    out_ref, held, buf, field_sems, sems = refs[:5]
+    if has_base:
+        base_hbm, out_ref, base_ref, refs = refs[0], refs[1], refs[2], refs[3:]
+    else:
+        out_ref, refs = refs[0], refs[1:]
+    held, buf, field_sems, sems = refs[:4]
 
     def copy(k, p):
         return pltpu.make_async_copy(op_ref.at[origins[k], p], buf.at[k, p], sems.at[k, p])
@@ -260,12 +335,14 @@
     for p in range(n_row // 2):
         for k in range(n):
             copy(k, p).start()
+    if has_base:
+        (base_copy,) = fetch([base_hbm], [base_ref], refs[4])
     left = []
     for k in range(n):
         field_copies[k].wait()
         left.append(stacked(held[k]))
     if n_carriers:
-        ordered = refs[5]
+        ordered = refs[4]
         for k in range(n_col):
             ordered[lax.rem(ids_ref[0] + k, n_col)] = carriers[k][H:, :]
         share = ordered[0]
@@ -292,11 +369,14 @@
             out_ref[2 * p + 1, :H, :] = summed[:, TB:]
         else:
             out_ref[:, here] = summed
-
-
-def product(n_row, n_col, ids, origins, operator, fields, prev, last, carriers=()):
+    if has_base:
+        base_copy.wait()
+
+
+def product(n_row, n_col, ids, origins, operator, fields, prev, last, carriers=(), base=None):
     n = len(origins)
     has_prev = prev is not None
+    has_base = base is not None
     share = 0
     scratch = [
         pltpu.VMEM((n, H, NODES_DEV), F32),
@@ -308,13 +388,15 @@
         rows = carriers[0].shape[0] - H
         share = rows * NODES_DEV // LANES // 2
         scratch.append(pltpu.VMEM((n_col, rows, NODES_DEV), F32))
-    shape = (n_row, H + share, TB) if last else (H, n_row * TB)
+    if has_base:
+        scratch.append(pltpu.SemaphoreType.DMA((1,)))
+    out = jax.ShapeDtypeStruct((n_row, H + share, TB) if last else (H, n_row * TB), F32)
     count = has_prev + len(carriers)
     return pl.pallas_call(
-        functools.partial(product_kernel, n_row, n_col, origins, has_prev, last, len(carriers)),
-        in_specs=[SMEM, HBM] + [ANY] * n + [VMEM] * count,
-        out_specs=VMEM,
-        out_shape=jax.ShapeDtypeStruct(shape, F32),
+        functools.partial(product_kernel, n_row, n_col, origins, has_prev, last, len(carriers), has_base),
+        in_specs=[SMEM, HBM] + [ANY] * n + [VMEM] * count + [HBM] * has_base,
+        out_specs=[VMEM, VMEM] if has_base else VMEM,
+        out_shape=[out, jax.ShapeDtypeStruct(base.shape, F32)] if has_base else out,
         scratch_shapes=scratch,
         compiler_params=params(48),
         cost_estimate=LIGHT if last else HEAVY,
@@ -325,16 +407,16 @@
         *fields,
         *((prev,) if has_prev else ()),
         *carriers,
+        *(in_hbm(base) if has_base else ()),
     )
 
 
-def carry_kernel(n_row, rows, owners_ref, base_hbm, came_ref, *refs):
-    out_ref, base, sems = refs[-3:]
-    (base_copy,) = fetch([base_hbm], [base], sems)
-    out_ref[:H, :] = jnp.zeros((H, NODES_DEV), F32)
+def carry_kernel(n_row, rows, owners_ref, base_ref, came_ref, *refs):
+    out_ref = refs[-1]
+    out_ref[:H, :] = base_ref[...]
     for q in range(n_row):
         here = pl.ds(pl.multiple_of(owners_ref[q] * TB, TB), TB)
-        out_ref[:H, here] += came_ref[q]
+        out_ref[:H, here] += 2.0 * came_ref[q]
     if rows:
         pieces_ref = refs[0]
         share = pieces_ref[0]
@@ -342,22 +424,19 @@
             share = share + pieces_ref[q]
         for j in range(NODES_DEV // LANES):
             out_ref[H:, j * LANES : (j + 1) * LANES] = share[j * rows : (j + 1) * rows, :]
-    base_copy.wait()
-    out_ref[:H, :] = base[...] + 2.0 * out_ref[:H, :]
 
 
 def carry(n_row, owners, base, came, *pieces):
     rows = pieces[0].shape[1] * LANES // NODES_DEV if pieces else 0
     return pl.pallas_call(
         functools.partial(carry_kernel, n_row, rows),
-        in_specs=[SMEM, HBM] + [VMEM] * (1 + len(pieces)),
+        in_specs=[SMEM] + [VMEM] * (2 + len(pieces)),
         out_specs=VMEM,
         out_shape=jax.ShapeDtypeStruct((H + rows, NODES_DEV), F32),
-        scratch_shapes=[pltpu.VMEM((H, NODES_DEV), F32), pltpu.SemaphoreType.DMA((1,))],
         compiler_params=params(24),
         cost_estimate=LIGHT,
         name="carry",
-    )(owners, *in_hbm(base), came, *pieces)
+    )(owners, base, came, *pieces)
 
 
 def finish_kernel(n_row, owners_ref, base_ref, left_ref, right_ref, out_ref, total):
@@ -450,18 +529,20 @@
     return steps
 
 
-def early(n_row, n_col, ids, operator, steps, total=None, done=0):
+def early(n_row, n_col, ids, operators, steps, total=None, done=0, base=None):
     pairs = [pair for step in steps[:-1] for pair in step][done:]
     for begin in range(0, len(pairs), 3):
         origins, fields = zip(*pairs[begin : begin + 3])
-        total = product(n_row, n_col, ids, origins, operator, fields, total, False)
+        origins = tuple(o if o < n_col // 2 else o - 1 for o in origins)
+        brought = base if begin + 3 >= len(pairs) else None
+        total = product(n_row, n_col, ids, origins, operators[0], fields, total, False, base=brought)
     return total
 
 
-def final(n_row, n_col, ids, operator, steps, total, carrying=False):
-    origins, fields = zip(*steps[-1])
+def final(n_row, n_col, ids, operators, steps, total, carrying=False):
+    ((_, field),) = steps[-1]
     carriers = [x for _, x in sorted((p for step in steps for p in step), key=lambda p: p[0])] if carrying else ()
-    return product(n_row, n_col, ids, origins, operator, fields, total, True, carriers)
+    return product(n_row, n_col, ids, (0,), operators[1], [field], total, True, carriers)
 
 
 def per_device(
@@ -487,21 +568,24 @@
     )
     steps = gather(n_col, left, 1)
     first = steps[0] + steps[1] if len(steps) > 2 else steps[0]
-    operator, left_early = build_operator(
+    operator, left_early, lists, counts = build_operator(
         n_row, n_col, ids, live_tiles, tile_rows, tile_slots, tile_values, first
     )
     pieces = exchange(pieces)
-    common = (n_row, n_col, ids, operator)
-
-    left_early = early(*common, steps, left_early, len(first))
+
+    left_early = early(n_row, n_col, ids, (operator,), steps, left_early, len(first))
     right_steps = gather(n_col, after(right, left_early, steps[-1][0][1]), -1)
-    left_came = exchange(final(*common, steps, after(left_early, pieces)))
-    right_early = early(*common, right_steps)
+    opposite_part, left_last = build_opposite(
+        n_row, n_col, lists, counts, tile_values, steps[-1][0][1], after(left_early, pieces)
+    )
+    left_came = exchange(left_last)
+    common = (n_row, n_col, ids, (operator, opposite_part))
+    right_early, one_left = early(*common, right_steps, base=one_left)
 
     left_carried = carry(n_row, owners, after(one_left, right_early, right_steps[-1][0][1]), left_came, pieces)
     steps = gather(n_col, left_carried, 1)
     right_came = exchange(final(*common, right_steps, right_early))
-    left_early = early(*common, steps)
+    left_early, one_right = early(*common, steps, base=one_right)
 
     right_carried = carry(n_row, owners, after(one_right, left_early, steps[-1][0][1]), right_came)
     right_steps = gather(n_col, right_carried, -1)

time: 127 us -> 130 us (1.024)
  local copies, waits for them, and re-layouts: 0.01 us -> 6.63 us
  waiting for transfers between devices: 27.6 us -> 25.7 us
    unnamed x2 -> x18, local copies, waits for them, and re-layouts: 0.01 us -> 6.63 us
    pallas_call x0 -> x1, Pallas kernels: none -> 5 us  [build_opposite(): pl.pallas_call(functools.partial(opposite_kernel, n_row, n_col // 2), in_...]
    pallas_call x7 -> x6, Pallas kernels: 30.9 us -> 28.9 us  [product(): pl.pallas_call(functools.partial(product_kernel, n_row, n_col, origins, h...]
    pallas_call x2, Pallas kernels: 3.06 us -> 1.34 us  [carry(): pl.pallas_call(functools.partial(carry_kernel, n_row, rows), in_specs=[SM...]
    ppermute x4, waiting for transfers between devices: 5.22 us -> 3.88 us  [opposite(): return lax.ppermute(sent, 'col', [(1, 0), (2, 3), (3, 1), (0, 2)])]
  transfers between devices with their start and end apart: 18 -> 18, of which waited for: 10 -> 8; matrix products, arithmetic and copies ran while one was open for 0% -> 0% of each run, Pallas kernels for 37% -> 38%
where the time goes in v13:
time: 130 us; the launch traced here: 129 us
  Pallas kernels  53.4 us (41%)
  starting transfers between devices  41.8 us (32%)
  waiting for transfers between devices  25.7 us (20%)
  local copies, waits for them, and re-layouts  6.63 us (5%)
  between operations  1.52 us (1%)
    pallas_call x6, Pallas kernels, product(): pl.pallas_call(functools.partial(product_kernel, n_row, n_col, origins, h...  28.9 us
    all_to_all x5, starting transfers between devices, exchange(): lax.all_to_all(pieces, 'row', split_axis=0, concat_axis=0, tiled=True)  19.1 us
    ppermute x8, starting transfers between devices, shift(): lax.ppermute(x, 'col', [(c, (c + step) % n_col) for c in range(n_col)])  16.7 us
    ppermute x8, waiting for transfers between devices, shift(): lax.ppermute(x, 'col', [(c, (c + step) % n_col) for c in range(n_col)])  13.2 us
    all_to_all x5, waiting for transfers between devices, exchange(): lax.all_to_all(pieces, 'row', split_axis=0, concat_axis=0, tiled=True)  8.6 us
    pallas_call x1, Pallas kernels, build_operator(): pl.pallas_call(functools.partial(operator_kernel, n_col, origins), grid=(...  8.5 us
    unnamed x18, local copies, waits for them, and re-layouts  6.63 us
    ppermute x4, starting transfers between devices, opposite(): return lax.ppermute(sent, 'col', [(1, 0), (2, 3), (3, 1), (0, 2)])  5.92 us
  transfers between devices with their start and end apart: 18, of which 8 were waited for; matrix products, arithmetic and copies ran while one was open for 0% of the time, Pallas kernels for 38%

profile of v13, /device:TPU:0, one launch (start us, length us, event | category | flops | bytes accessed | tf_op | source)
XLA Modules:
  0.0 129.3 jit_solution(8316132593286804496)
XLA Ops:
  0.6 1.7 %term_two.1 = (f32[128,512]{1,0:T(8,128)S(1)}, f32[128,512]{1,0:T(8,128)S(1)}) custom-call(f32[512,256]{1,0:T(8,128)} %grad_hbm.3, s32[512,256]{1,0:T(8,128)} %mask_hbm.3, f32[3,256,256]{2,1,0:T(8,128)} %weight_hbm.3), custom_call_target="tpu_custom_call" | custom-call | flops 1024 | bytes 1024 | tf_op jit(solution)/shard_map/term_two/pallas_call | solution.py:76
  2.4 5.1 %collective-permute-start.1 = (f32[128,512]{1,0:T(8,128)S(1)}, f32[128,512]{1,0:T(8,128)S(1)}, u32[]{:S(2)}, u32[]{:S(2)}) collective-permute-start(f32[128,512]{1,0:T(8,128)S(1)} %get-tuple-element.28.first_ref.refs_0_), channel_id=1, source_target_pairs={{0,3},{1,0},{2,1},{3,2},{4,7},{5,4},{6,5},{7,6},{8,11},{9,8},{10,9... | collective-permute-start | bytes 786440 | tf_op jit(solution)/shard_map/ppermute | solution.py:495
  7.5 0.0 collective-permute-start
  7.5 4.9 %local_terms.1 = (f32[128,512]{1,0:T(8,128)}, f32[128,512]{1,0:T(8,128)}, f32[256,512]{1,0:T(8,128)S(1)}, f32[8,192,128]{2,1,0:T(8,128)}) custom-call(f32[128,512]{1,0:T(8,128)S(1)} %get-tuple-element.28.first_ref.refs_0_, f32[512,256]{1,0:T(8,128)} %grad_hbm.3, s32[512,256]{1,0:T(8,128)} %mask_hbm.3, f32[3,256,256]{2,1,0:T(8,128)} %weight_hbm.3, ...), custom_call_target="tpu_custom_call" | custom-call | flops 1024 | bytes 1024 | tf_op jit(solution)/shard_map/local_terms/pallas_call | solution.py:123
  12.4 3.7 %all-to-all-start = ((f32[8,192,128]{2,1,0:T(8,128)}), f32[8,192,128]{2,1,0:T(8,128)S(1)}, u32[]{:S(2)}, u32[]{:S(2)}) async-start(f32[8,192,128]{2,1,0:T(8,128)} %get-tuple-element.34), calls=%async_computation | async-start | bytes 1572864 | tf_op jit(solution)/shard_map/all_to_all | solution.py:499
  16.8 0.0 collective-permute-done.1.refs_2_
  16.8 2.8 %collective-permute-done.refs_1_ = f32[128,512]{1,0:T(8,128)S(1)} collective-permute-done((f32[128,512]{1,0:T(8,128)S(1)}, f32[128,512]{1,0:T(8,128)S(1)}, u32[]{:S(2)}, u32[]{:S(2)}) %collective-permute-start) | collective-permute-done | bytes 262176 | tf_op jit(solution)/shard_map/ppermute | solution.py:495
  19.6 0.1 select_select_fusion.3
  19.6 0.8 collective-permute-start.2
  20.4 8.5 %operator.1 = (bf16[3,4,1024,256]{3,2,1,0:T(8,128)(2,1)}, f32[128,1024]{1,0:T(8,128)S(1)}, s32[4,128]{1,0:T(4,128)S(1)}, s32[4]{0:T(128)S(1)}) custom-call(s32[1]{0:T(128)} %bitcast.2.ids_ref.refs_0_, s32[1]{0:T(128)S(6)} %copy.13.live_ref, s32[1,128]{1,0:T(1,128)} %rows_hbm.1, s32[1,128]{1,0:T(1,128)} %slots_hbm.1, f32[1,128,128,128]{3,2,1,0:T(8,128)} %values_ref.3, ...), custom_call_target="tpu_custom_call" | custom-call | flops 17179869184 | bytes 67108864 | tf_op jit(solution)/shard_map/operator/pallas_call | solution.py:227
  28.9 0.0 collective-permute-done.2.field_ref
  28.9 0.0 copy-start.6
  29.0 0.7 copy-done.6
  29.6 1.3 %collective-permute-start.4 = (f32[128,512]{1,0:T(8,128)S(1)}, f32[128,512]{1,0:T(8,128)S(1)}, u32[]{:S(2)}, u32[]{:S(2)}) collective-permute-start(f32[128,512]{1,0:T(8,128)S(1)} %get-tuple-element.39.refs_2_), channel_id=1, source_target_pairs={{0,1},{1,2},{2,3},{3,0},{4,5},{5,6},{6,7},{7,4},{8,9},{9,10},{10,1... | collective-permute-start | bytes 786440 | tf_op jit(solution)/shard_map/ppermute | solution.py:495
  31.0 2.5 %collective-permute-start.3 = (f32[128,512]{1,0:T(8,128)S(1)}, f32[128,512]{1,0:T(8,128)S(1)}, u32[]{:S(2)}, u32[]{:S(2)}) collective-permute-start(f32[128,512]{1,0:T(8,128)S(1)} %get-tuple-element.39.refs_2_), channel_id=1, source_target_pairs={{0,3},{1,0},{2,1},{3,2},{4,7},{5,4},{6,5},{7,6},{8,11},{9,8},{10,9... | collective-permute-start | bytes 786440 | tf_op jit(solution)/shard_map/ppermute | solution.py:495
  33.5 0.0 all-to-all-done.refs_0_
  33.5 0.9 copy-done.7
  34.4 5.0 %opposite.1 = (bf16[1,4,1024,256]{3,2,1,0:T(8,128)(2,1)}, f32[8,128,128]{2,1,0:T(8,128)}) custom-call(s32[4,128]{1,0:T(4,128)S(1)} %get-tuple-element.30.lists, s32[4]{0:T(128)S(1)} %get-tuple-element.31.counts, f32[1,128,128,128]{3,2,1,0:T(8,128)} %values_ref.3, f32[128,512]{1,0:T(8,128)S(1)} %copy-done.7, f32[128,1024]{1,0:T(8,128)S(1)} %get-tuple-element.35.prev), custom_call_target="tpu_custom_call" | custom-call | flops 1024 | bytes 1024 | tf_op jit(solution)/shard_map/opposite/pallas_call | solution.py:298
  39.4 4.7 %all-to-all-start.1 = ((f32[8,128,128]{2,1,0:T(8,128)}), f32[8,128,128]{2,1,0:T(8,128)S(1)}, u32[]{:S(2)}, u32[]{:S(2)}) async-start(f32[8,128,128]{2,1,0:T(8,128)} %get-tuple-element.45), calls=%async_computation.1 | async-start | bytes 1048576 | tf_op jit(solution)/shard_map/all_to_all | solution.py:499
  44.1 0.0 collective-permute-done.4.refs_4_
  44.1 0.0 collective-permute-done.3.refs_3_
  44.1 0.1 select_select_fusion.2
  44.2 2.2 %collective-permute-start.5 = (f32[128,512]{1,0:T(8,128)S(1)}, f32[128,512]{1,0:T(8,128)S(1)}, u32[]{:S(2)}, u32[]{:S(2)}) collective-permute-start(f32[128,512]{1,0:T(8,128)S(1)} %select_select_fusion.2), channel_id=1, source_target_pairs={{1,0},{2,3},{3,1},{0,2},{5,4},{6,7},{7,5},{4,6},{9,8},{10,11},{11,... | collective-permute-start | bytes 786440 | tf_op jit(solution)/shard_map/ppermute | solution.py:509
  46.4 5.5 %product.6 = (f32[128,1024]{1,0:T(8,128)S(1)}, f32[128,512]{1,0:T(8,128)S(1)}) custom-call(s32[1]{0:T(128)} %bitcast.2.ids_ref.refs_0_, bf16[3,4,1024,256]{3,2,1,0:T(8,128)(2,1)} %get-tuple-element.37.refs_1_, f32[128,512]{1,0:T(8,128)S(1)} %get-tuple-element.39.refs_2_, f32[128,512]{1,0:T(8,128)S(1)} %collective-permute-done.3.refs_3_, ...), custom_call_target="tpu_custom_call" | custom-call | flops 17179869184 | bytes 67108864 | tf_op jit(solution)/shard_map/product/pallas_call | solution.py:395
  51.8 0.0 copy-start.2
  51.9 0.7 copy-done.2
  52.5 0.4 collective-permute-done.5.refs_2_
  52.9 0.7 copy-done
  53.7 0.2 all-to-all-done.1.came_ref
  53.8 0.9 copy-done.3
  54.8 0.7 carry.2.refs_2_.refs_4_
  55.5 2.4 %collective-permute-start.7 = (f32[176,512]{1,0:T(8,128)S(1)}, f32[176,512]{1,0:T(8,128)S(1)}, u32[]{:S(2)}, u32[]{:S(2)}) collective-permute-start(f32[176,512]{1,0:T(8,128)S(1)} %carry.2.refs_2_.refs_4_), channel_id=1, source_target_pairs={{0,1},{1,2},{2,3},{3,0},{4,5},{5,6},{6,7},{7,4},{8,9},{9,10},{10,1... | collective-permute-start | bytes 1081352 | tf_op jit(solution)/shard_map/ppermute | solution.py:495
  57.9 1.4 %collective-permute-start.6 = (f32[176,512]{1,0:T(8,128)S(1)}, f32[176,512]{1,0:T(8,128)S(1)}, u32[]{:S(2)}, u32[]{:S(2)}) collective-permute-start(f32[176,512]{1,0:T(8,128)S(1)} %carry.2.refs_2_.refs_4_), channel_id=1, source_target_pairs={{0,3},{1,0},{2,1},{3,2},{4,7},{5,4},{6,5},{7,6},{8,11},{9,8},{10,9... | collective-permute-start | bytes 1081352 | tf_op jit(solution)/shard_map/ppermute | solution.py:495
  59.4 0.9 copy-done.1
  60.3 3.6 %product.9 = f32[8,128,128]{2,1,0:T(8,128)} custom-call(s32[1]{0:T(128)} %bitcast.2.ids_ref.refs_0_, bf16[1,4,1024,256]{3,2,1,0:T(8,128)(2,1)} %get-tuple-element.36.refs_1_, f32[128,512]{1,0:T(8,128)S(1)} %copy-done.1, f32[128,1024]{1,0:T(8,128)S(1)} %get-tuple-element.42.refs_3_), custom_call_target="tpu_custom_call" | custom-call | flops 1024 | bytes 1024 | tf_op jit(solution)/shard_map/product/pallas_call | solution.py:395
  63.9 3.7 %all-to-all-start.3 = ((f32[8,128,128]{2,1,0:T(8,128)}), f32[8,128,128]{2,1,0:T(8,128)S(1)}, u32[]{:S(2)}, u32[]{:S(2)}) async-start(f32[8,128,128]{2,1,0:T(8,128)} %product.9), calls=%async_computation.3 | async-start | bytes 1048576 | tf_op jit(solution)/shard_map/all_to_all | solution.py:499
  67.6 1.1 collective-permute-done.7.refs_3_.refs_7_
  68.7 6.1 %collective-permute-done.6.refs_4_.refs_5_ = f32[176,512]{1,0:T(8,128)S(1)} collective-permute-done((f32[176,512]{1,0:T(8,128)S(1)}, f32[176,512]{1,0:T(8,128)S(1)}, u32[]{:S(2)}, u32[]{:S(2)}) %collective-permute-start.6) | collective-permute-done | bytes 360480 | tf_op jit(solution)/shard_map/ppermute | solution.py:495
  74.8 0.1 select_select_fusion
  74.9 0.8 collective-permute-start.8
  75.8 5.5 %product.7 = (f32[128,1024]{1,0:T(8,128)S(1)}, f32[128,512]{1,0:T(8,128)S(1)}) custom-call(s32[1]{0:T(128)} %bitcast.2.ids_ref.refs_0_, bf16[3,4,1024,256]{3,2,1,0:T(8,128)(2,1)} %get-tuple-element.37.refs_1_, f32[176,512]{1,0:T(8,128)S(1)} %carry.2.refs_2_.refs_4_, f32[176,512]{1,0:T(8,128)S(1)} %collective-permute-done.7.refs_3_.refs_7_, ...), custom_call_target="tpu_custom_call" | custom-call | flops 17179869184 | bytes 67108864 | tf_op jit(solution)/shard_map/product/pallas_call | solution.py:395
  81.3 0.0 copy-start.4
  81.3 0.7 copy-done.4
  82.0 3.5 %collective-permute-done.8.refs_2_.refs_6_ = f32[176,512]{1,0:T(8,128)S(1)} collective-permute-done((f32[176,512]{1,0:T(8,128)S(1)}, f32[176,512]{1,0:T(8,128)S(1)}, u32[]{:S(2)}, u32[]{:S(2)}) %collective-permute-start.8) | collective-permute-done | bytes 360480 | tf_op jit(solution)/shard_map/ppermute | solution.py:509
  85.4 0.0 all-to-all-done.3.came_ref
  85.5 0.9 copy-done.5
  86.4 0.7 carry.3.refs_2_
  87.1 1.6 %collective-permute-start.10 = (f32[128,512]{1,0:T(8,128)S(1)}, f32[128,512]{1,0:T(8,128)}, u32[]{:S(2)}, u32[]{:S(2)}) collective-permute-start(f32[128,512]{1,0:T(8,128)S(1)} %carry.3.refs_2_), channel_id=1, source_target_pairs={{0,1},{1,2},{2,3},{3,0},{4,5},{5,6},{6,7},{7,4},{8,9},{9,10},{10,1... | collective-permute-start | bytes 786440 | tf_op jit(solution)/shard_map/ppermute | solution.py:495
  88.6 2.3 %collective-permute-start.9 = (f32[128,512]{1,0:T(8,128)S(1)}, f32[128,512]{1,0:T(8,128)}, u32[]{:S(2)}, u32[]{:S(2)}) collective-permute-start(f32[128,512]{1,0:T(8,128)S(1)} %carry.3.refs_2_), channel_id=1, source_target_pairs={{0,3},{1,0},{2,1},{3,2},{4,7},{5,4},{6,5},{7,6},{8,11},{9,8},{10,9... | collective-permute-start | bytes 786440 | tf_op jit(solution)/shard_map/ppermute | solution.py:495
  90.9 3.8 %product.8 = f32[8,224,128]{2,1,0:T(8,128)} custom-call(s32[1]{0:T(128)} %bitcast.2.ids_ref.refs_0_, bf16[1,4,1024,256]{3,2,1,0:T(8,128)(2,1)} %get-tuple-element.36.refs_1_, f32[176,512]{1,0:T(8,128)S(1)} %collective-permute-done.8.refs_2_.refs_6_, f32[128,1024]{1,0:T(8,128)S(1)} %get-tuple-element.48.refs_3_, f32[176,512]{1,0:T(8,128)S(1)} %carry.2.refs_2_.refs_4_, ...), custom_call_target="tpu_custom_call" | custom-call | flops 1024 | bytes 1024 | tf_op jit(solution)/shard_map/product/pallas_call | solution.py:395
  94.7 3.6 %all-to-all-start.2 = ((f32[8,224,128]{2,1,0:T(8,128)}), f32[8,224,128]{2,1,0:T(8,128)S(1)}, u32[]{:S(2)}, u32[]{:S(2)}) async-start(f32[8,224,128]{2,1,0:T(8,128)} %product.8), calls=%async_computation.2 | async-start | bytes 1835008 | tf_op jit(solution)/shard_map/all_to_all | solution.py:499
  98.3 0.0 collective-permute-done.10.refs_4_
  98.3 3.2 %collective-permute-done.9.refs_3_ = f32[128,512]{1,0:T(8,128)} collective-permute-done((f32[128,512]{1,0:T(8,128)S(1)}, f32[128,512]{1,0:T(8,128)}, u32[]{:S(2)}, u32[]{:S(2)}) %collective-permute-start.9) | collective-permute-done | bytes 262176 | tf_op jit(solution)/shard_map/ppermute | solution.py:495
  101.5 0.1 select_select_fusion.1
  101.5 2.1 %collective-permute-start.11 = (f32[128,512]{1,0:T(8,128)S(1)}, f32[128,512]{1,0:T(8,128)S(1)}, u32[]{:S(2)}, u32[]{:S(2)}) collective-permute-start(f32[128,512]{1,0:T(8,128)S(1)} %select_select_fusion.1), channel_id=1, source_target_pairs={{1,0},{2,3},{3,1},{0,2},{5,4},{6,7},{7,5},{4,6},{9,8},{10,11},{11,... | collective-permute-start | bytes 786440 | tf_op jit(solution)/shard_map/ppermute | solution.py:509
  103.6 7.1 %product.10.refs_3_ = f32[128,1024]{1,0:T(8,128)S(1)} custom-call(s32[1]{0:T(128)} %bitcast.2.ids_ref.refs_0_, bf16[3,4,1024,256]{3,2,1,0:T(8,128)(2,1)} %get-tuple-element.37.refs_1_, f32[128,512]{1,0:T(8,128)S(1)} %carry.3.refs_2_, f32[128,512]{1,0:T(8,128)} %collective-permute-done.9.refs_3_, f32[128,512]{1,0:T(8,128)} %collective-permute-done.10.refs_4_), custom_call_target="tpu_custom_call" | custom-call | flops 17179869184 | bytes 67108864 | tf_op jit(solution)/shard_map/product/pallas_call | solution.py:395
  110.7 0.0 collective-permute-done.11.refs_2_
  110.7 3.6 %product.11 = f32[8,128,128]{2,1,0:T(8,128)} custom-call(s32[1]{0:T(128)} %bitcast.2.ids_ref.refs_0_, bf16[1,4,1024,256]{3,2,1,0:T(8,128)(2,1)} %get-tuple-element.36.refs_1_, f32[128,512]{1,0:T(8,128)S(1)} %collective-permute-done.11.refs_2_, f32[128,1024]{1,0:T(8,128)S(1)} %product.10.refs_3_), custom_call_target="tpu_custom_call" | custom-call | flops 1024 | bytes 1024 | tf_op jit(solution)/shard_map/product/pallas_call | solution.py:395
  114.3 0.1 collective-permute-start.12
  114.4 3.5 %all-to-all-start.4 = ((f32[8,128,128]{2,1,0:T(8,128)}), f32[8,128,128]{2,1,0:T(8,128)S(1)}, u32[]{:S(2)}, u32[]{:S(2)}) async-start(f32[8,128,128]{2,1,0:T(8,128)} %product.11), calls=%async_computation.4 | async-start | bytes 1048576 | tf_op jit(solution)/shard_map/all_to_all | solution.py:499
  117.9 0.0 collective-permute-done.12.other_ref
  117.9 1.2 assemble.1
  119.1 8.4 %all-to-all-done.4.right_ref = f32[8,128,128]{2,1,0:T(8,128)S(1)} async-done(((f32[8,128,128]{2,1,0:T(8,128)}), f32[8,128,128]{2,1,0:T(8,128)S(1)}, u32[]{:S(2)}, u32[]{:S(2)}) %all-to-all-start.4) | async-done | bytes 524320 | tf_op jit(solution)/shard_map/all_to_all | solution.py:499
  127.6 1.8 %finish.1 = f32[512,256]{1,0:T(8,128)} custom-call(s32[8]{0:T(128)S(1)} %bitcast.5, f32[256,512]{1,0:T(8,128)S(1)} %get-tuple-element.53.base_ref, f32[8,224,128]{2,1,0:T(8,128)S(1)} %all-to-all-done.2.own_ref.left_ref, f32[8,128,128]{2,1,0:T(8,128)S(1)} %all-to-all-done.4.right_ref), custom_call_target="tpu_custom_call" | custom-call | flops 1024 | bytes 1024 | tf_op jit(solution)/shard_map/finish/pallas_call | solution.py:452
  (8 shorter events, 0.0 us)
Async XLA Ops:
  2.4 14.4 %collective-permute-start.1 = (f32[128,512]{1,0:T(8,128)S(1)}, f32[128,512]{1,0:T(8,128)S(1)}, u32[]{:S(2)}, u32[]{:S(2)}) collective-permute-start(f32[128,512]{1,0:T(8,128)S(1)} %get-tuple-element.28.first_ref.refs_0_), channel_id=1, source_target_pairs={{0,3},{1,0},{2,1},{3,2},{4,7},{5,4},{6,5},{7,6},{8,11},{9,8},{10,9... | collective-permute-start | bytes 786440 | tf_op jit(solution)/shard_map/ppermute | solution.py:495
  7.5 12.1 %collective-permute-start = (f32[128,512]{1,0:T(8,128)S(1)}, f32[128,512]{1,0:T(8,128)S(1)}, u32[]{:S(2)}, u32[]{:S(2)}) collective-permute-start(f32[128,512]{1,0:T(8,128)S(1)} %get-tuple-element.28.first_ref.refs_0_), channel_id=1, source_target_pairs={{0,1},{1,2},{2,3},{3,0},{4,5},{5,6},{6,7},{7,4},{8,9},{9,10},{10,1... | collective-permute-start | bytes 786440 | tf_op jit(solution)/shard_map/ppermute | solution.py:495
  12.4 21.1 %all-to-all-start = ((f32[8,192,128]{2,1,0:T(8,128)}), f32[8,192,128]{2,1,0:T(8,128)S(1)}, u32[]{:S(2)}, u32[]{:S(2)}) async-start(f32[8,192,128]{2,1,0:T(8,128)} %get-tuple-element.34), calls=%async_computation | async-start | bytes 1572864 | tf_op jit(solution)/shard_map/all_to_all | solution.py:499
  19.6 9.3 %collective-permute-start.2 = (f32[128,512]{1,0:T(8,128)S(1)}, f32[128,512]{1,0:T(8,128)S(1)}, u32[]{:S(2)}, u32[]{:S(2)}) collective-permute-start(f32[128,512]{1,0:T(8,128)S(1)} %select_select_fusion.3), channel_id=1, source_target_pairs={{1,0},{2,3},{3,1},{0,2},{5,4},{6,7},{7,5},{4,6},{9,8},{10,11},{11,... | collective-permute-start | bytes 786440 | tf_op jit(solution)/shard_map/ppermute | solution.py:509
  28.9 0.7 copy-start.6
  29.6 14.4 %collective-permute-start.4 = (f32[128,512]{1,0:T(8,128)S(1)}, f32[128,512]{1,0:T(8,128)S(1)}, u32[]{:S(2)}, u32[]{:S(2)}) collective-permute-start(f32[128,512]{1,0:T(8,128)S(1)} %get-tuple-element.39.refs_2_), channel_id=1, source_target_pairs={{0,1},{1,2},{2,3},{3,0},{4,5},{5,6},{6,7},{7,4},{8,9},{9,10},{10,1... | collective-permute-start | bytes 786440 | tf_op jit(solution)/shard_map/ppermute | solution.py:495
  31.0 13.1 %collective-permute-start.3 = (f32[128,512]{1,0:T(8,128)S(1)}, f32[128,512]{1,0:T(8,128)S(1)}, u32[]{:S(2)}, u32[]{:S(2)}) collective-permute-start(f32[128,512]{1,0:T(8,128)S(1)} %get-tuple-element.39.refs_2_), channel_id=1, source_target_pairs={{0,3},{1,0},{2,1},{3,2},{4,7},{5,4},{6,5},{7,6},{8,11},{9,8},{10,9... | collective-permute-start | bytes 786440 | tf_op jit(solution)/shard_map/ppermute | solution.py:495
  33.5 1.0 copy-start.7
  39.4 14.4 %all-to-all-start.1 = ((f32[8,128,128]{2,1,0:T(8,128)}), f32[8,128,128]{2,1,0:T(8,128)S(1)}, u32[]{:S(2)}, u32[]{:S(2)}) async-start(f32[8,128,128]{2,1,0:T(8,128)} %get-tuple-element.45), calls=%async_computation.1 | async-start | bytes 1048576 | tf_op jit(solution)/shard_map/all_to_all | solution.py:499
  44.2 8.8 %collective-permute-start.5 = (f32[128,512]{1,0:T(8,128)S(1)}, f32[128,512]{1,0:T(8,128)S(1)}, u32[]{:S(2)}, u32[]{:S(2)}) collective-permute-start(f32[128,512]{1,0:T(8,128)S(1)} %select_select_fusion.2), channel_id=1, source_target_pairs={{1,0},{2,3},{3,1},{0,2},{5,4},{6,7},{7,5},{4,6},{9,8},{10,11},{11,... | collective-permute-start | bytes 786440 | tf_op jit(solution)/shard_map/ppermute | solution.py:509
  46.4 7.5 %copy-start.8 = (s32[1,8,1]{1,2,0:T(1,128)S(1)}, s32[1,8,1]{1,2,0:T(1,128)}, u32[]{:S(2)}) copy-start(s32[1,8,1]{1,2,0:T(1,128)} %param.20) | copy-start | bytes 100
  51.8 0.7 copy-start.2
  52.9 0.7 copy-start
  53.8 1.0 copy-start.3
  55.5 13.2 %collective-permute-start.7 = (f32[176,512]{1,0:T(8,128)S(1)}, f32[176,512]{1,0:T(8,128)S(1)}, u32[]{:S(2)}, u32[]{:S(2)}) collective-permute-start(f32[176,512]{1,0:T(8,128)S(1)} %carry.2.refs_2_.refs_4_), channel_id=1, source_target_pairs={{0,1},{1,2},{2,3},{3,0},{4,5},{5,6},{6,7},{7,4},{8,9},{9,10},{10,1... | collective-permute-start | bytes 1081352 | tf_op jit(solution)/shard_map/ppermute | solution.py:495
  57.9 16.9 %collective-permute-start.6 = (f32[176,512]{1,0:T(8,128)S(1)}, f32[176,512]{1,0:T(8,128)S(1)}, u32[]{:S(2)}, u32[]{:S(2)}) collective-permute-start(f32[176,512]{1,0:T(8,128)S(1)} %carry.2.refs_2_.refs_4_), channel_id=1, source_target_pairs={{0,3},{1,0},{2,1},{3,2},{4,7},{5,4},{6,5},{7,6},{8,11},{9,8},{10,9... | collective-permute-start | bytes 1081352 | tf_op jit(solution)/shard_map/ppermute | solution.py:495
  59.4 0.9 copy-start.1
  63.9 21.6 %all-to-all-start.3 = ((f32[8,128,128]{2,1,0:T(8,128)}), f32[8,128,128]{2,1,0:T(8,128)S(1)}, u32[]{:S(2)}, u32[]{:S(2)}) async-start(f32[8,128,128]{2,1,0:T(8,128)} %product.9), calls=%async_computation.3 | async-start | bytes 1048576 | tf_op jit(solution)/shard_map/all_to_all | solution.py:499
  74.9 10.5 %collective-permute-start.8 = (f32[176,512]{1,0:T(8,128)S(1)}, f32[176,512]{1,0:T(8,128)S(1)}, u32[]{:S(2)}, u32[]{:S(2)}) collective-permute-start(f32[176,512]{1,0:T(8,128)S(1)} %select_select_fusion), channel_id=1, source_target_pairs={{1,0},{2,3},{3,1},{0,2},{5,4},{6,7},{7,5},{4,6},{9,8},{10,11},{11,... | collective-permute-start | bytes 1081352 | tf_op jit(solution)/shard_map/ppermute | solution.py:509
  81.3 0.7 copy-start.4
  85.5 1.0 copy-start.5
  87.1 11.2 %collective-permute-start.10 = (f32[128,512]{1,0:T(8,128)S(1)}, f32[128,512]{1,0:T(8,128)}, u32[]{:S(2)}, u32[]{:S(2)}) collective-permute-start(f32[128,512]{1,0:T(8,128)S(1)} %carry.3.refs_2_), channel_id=1, source_target_pairs={{0,1},{1,2},{2,3},{3,0},{4,5},{5,6},{6,7},{7,4},{8,9},{9,10},{10,1... | collective-permute-start | bytes 786440 | tf_op jit(solution)/shard_map/ppermute | solution.py:495
  88.6 12.8 %collective-permute-start.9 = (f32[128,512]{1,0:T(8,128)S(1)}, f32[128,512]{1,0:T(8,128)}, u32[]{:S(2)}, u32[]{:S(2)}) collective-permute-start(f32[128,512]{1,0:T(8,128)S(1)} %carry.3.refs_2_), channel_id=1, source_target_pairs={{0,3},{1,0},{2,1},{3,2},{4,7},{5,4},{6,5},{7,6},{8,11},{9,8},{10,9... | collective-permute-start | bytes 786440 | tf_op jit(solution)/shard_map/ppermute | solution.py:495
  94.7 19.6 %all-to-all-start.2 = ((f32[8,224,128]{2,1,0:T(8,128)}), f32[8,224,128]{2,1,0:T(8,128)S(1)}, u32[]{:S(2)}, u32[]{:S(2)}) async-start(f32[8,224,128]{2,1,0:T(8,128)} %product.8), calls=%async_computation.2 | async-start | bytes 1835008 | tf_op jit(solution)/shard_map/all_to_all | solution.py:499
  101.5 9.2 %collective-permute-start.11 = (f32[128,512]{1,0:T(8,128)S(1)}, f32[128,512]{1,0:T(8,128)S(1)}, u32[]{:S(2)}, u32[]{:S(2)}) collective-permute-start(f32[128,512]{1,0:T(8,128)S(1)} %select_select_fusion.1), channel_id=1, source_target_pairs={{1,0},{2,3},{3,1},{0,2},{5,4},{6,7},{7,5},{4,6},{9,8},{10,11},{11,... | collective-permute-start | bytes 786440 | tf_op jit(solution)/shard_map/ppermute | solution.py:509
  114.3 3.6 %collective-permute-start.12 = (f32[8,224,128]{2,1,0:T(8,128)S(1)}, f32[8,224,128]{2,1,0:T(8,128)S(1)}, u32[]{:S(2)}, u32[]{:S(2)}) collective-permute-start(f32[8,224,128]{2,1,0:T(8,128)S(1)} %all-to-all-done.2.own_ref.left_ref), channel_id=1, source_target_pairs={{0,4},{4,0},{8,12},{12,8},{16,20},{20,16},{24,28},{28,24},{1,5},{5... | collective-permute-start | bytes 2752520 | tf_op jit(solution)/shard_map/ppermute | solution.py:597
  114.4 13.2 %all-to-all-start.4 = ((f32[8,128,128]{2,1,0:T(8,128)}), f32[8,128,128]{2,1,0:T(8,128)S(1)}, u32[]{:S(2)}, u32[]{:S(2)}) async-start(f32[8,128,128]{2,1,0:T(8,128)} %product.11), calls=%async_computation.4 | async-start | bytes 1048576 | tf_op jit(solution)/shard_map/all_to_all | solution.py:499

commit v14 on v12

--- a/solution.py
+++ b/solution.py
@@ -150,95 +150,98 @@
     return jnp.concatenate([jnp.concatenate([x, x], axis=1) for x in (high, low)], axis=0)
 
 
-def operator_kernel(n_col, origins, ids_ref, live_ref, rows_hbm, slots_hbm, values_ref, *refs):
+def operator_kernel(n_row, n_col, origins, ids_ref, live_ref, rows_hbm, slots_hbm, values_ref, *refs):
     fields, refs = refs[: len(origins)], refs[len(origins) :]
-    out_ref, total_ref, tiles, acc, lists, counts, rows, slots, sems, small_sems = refs
-    origin = pl.program_id(0)
+    out_hbm, total_ref, tiles, acc, buf, held, lists, counts, rows, slots, sems, small_sems, field_sems, out_sems = refs
     size = TILES_DEV // GROUPS
-
-    def copy(g):
-        part = pl.ds(g * size, size)
-        return pltpu.make_async_copy(values_ref.at[0, part], tiles.at[part], sems.at[g])
-
-    @pl.when(origin == 0)
-    def _():
-        small = fetch((rows_hbm, slots_hbm), (rows, slots), small_sems)
-        for g in range(GROUPS):
-            copy(g).start()
-        for s in range(n_col):
-            counts[s] = 0
-        for item in small:
-            item.wait()
-
-        def place(t, carry):
-            row = rows[0, t]
-            s = lax.rem(row // CHB - ids_ref[0] + n_col, n_col)
-            position = slots[0, t] * CHB + lax.rem(row, CHB)
-            n = counts[s]
-            lists[s, n] = position * TILES_DEV + t
-            counts[s] = n + 1
+    pairs = n_row // 2
+    small = fetch((rows_hbm, slots_hbm), (rows, slots), small_sems)
+    parts = [pl.ds(g * size, size) for g in range(GROUPS)]
+    tile_copies = fetch([values_ref.at[0, part] for part in parts], [tiles.at[part] for part in parts], sems)
+    field_copies = fetch(fields, [held.at[k] for k in range(len(fields))], field_sems)
+    for item in small:
+        item.wait()
+
+    def place(t, counted):
+        row = rows[0, t]
+        s = lax.rem(row // CHB - ids_ref[0] + n_col, n_col)
+        if n_col & (n_col - 1) == 0:
+            s = (lax.shift_right_logical(row, CHB.bit_length() - 1) - ids_ref[0]) & (n_col - 1)
+        position = slots[0, t] * CHB + (row & (CHB - 1))
+        n = counted[0]
+        for k in range(1, n_col):
+            n = jnp.where(s == k, counted[k], n)
+        lists[s, n] = position * TILES_DEV + t
+        return tuple(c + (s == k).astype(jnp.int32) for k, c in enumerate(counted))
+
+    counted = lax.fori_loop(0, live_ref[0], place, (jnp.int32(0),) * n_col)
+    for s in range(n_col):
+        counts[s] = counted[s]
+
+    def out_copy(origin, p):
+        return pltpu.make_async_copy(buf.at[origin % 2, p], out_hbm.at[origin, p], out_sems.at[origin % 2, p])
+
+    for origin in range(n_col):
+        acc[...] = jnp.zeros_like(acc)
+        if origin == 0:
+            for item in tile_copies:
+                item.wait()
+
+        def add(n, carry):
+            entry = lists[origin, n]
+            tile = entry & (TILES_DEV - 1)
+            position = lax.shift_right_logical(entry, TILES_DEV.bit_length() - 1)
+            slot = lax.shift_right_logical(position, CHB.bit_length() - 1)
+            at_row = pl.ds(pl.multiple_of((position & (CHB - 1)) * TB, TB), TB)
+            at_lane = pl.ds(pl.multiple_of((slot & 1) * TB, TB), TB)
+            acc[lax.shift_right_logical(slot, 1), at_row, at_lane] += tiles[tile]
             return carry
 
-        lax.fori_loop(0, live_ref[0], place, 0)
-
-    acc[...] = jnp.zeros_like(acc)
-
-    @pl.when(origin == 0)
-    def _():
-        for g in range(GROUPS):
-            copy(g).wait()
-
-    def add(n, carry):
-        entry = lists[origin, n]
-        position = entry // TILES_DEV
-        slot = position // CHB
-        at_row = pl.ds(pl.multiple_of(lax.rem(position, CHB) * TB, TB), TB)
-        at_lane = pl.ds(pl.multiple_of(lax.rem(slot, 2) * TB, TB), TB)
-        acc[slot // 2, at_row, at_lane] += tiles[lax.rem(entry, TILES_DEV)]
-        return carry
-
-    lax.fori_loop(0, counts[origin], add, 0)
-    pairs = acc.shape[0]
-    for p in range(pairs):
-        high, low = split(acc[p])
-        out_ref[0, p, :NODES_DEV, :] = high
-        out_ref[0, p, NODES_DEV:, :] = low
-
-    for k, field in zip(origins, fields):
-
-        @pl.when(origin == k)
-        def _():
-            left = stacked(field[...])
+        lax.fori_loop(0, counts[origin], add, 0)
+        for p in range(pairs):
+            if origin >= 2:
+                out_copy(origin - 2, p).wait()
+            high, low = split(acc[p])
+            buf[origin % 2, p, :NODES_DEV, :] = high
+            buf[origin % 2, p, NODES_DEV:, :] = low
+            out_copy(origin, p).start()
+        if origin in origins:
+            k = origins.index(origin)
+            field_copies[k].wait()
+            left = stacked(held[k])
             for p in range(pairs):
-                part = jnp.dot(left, out_ref[0, p], preferred_element_type=F32)
+                part = jnp.dot(left, buf[origin % 2, p], preferred_element_type=F32)
                 summed = part[:H] + part[H:]
                 here = slice(p * WIDE, (p + 1) * WIDE)
-                total_ref[:, here] = summed if k == 0 else total_ref[:, here] + summed
+                total_ref[:, here] = summed if origin == 0 else total_ref[:, here] + summed
+    for origin in range(n_col - 2, n_col):
+        for p in range(pairs):
+            out_copy(origin, p).wait()
 
 
 def build_operator(n_row, n_col, ids, live, rows, slots, values, pairs):
     part = (n_row // 2, 2 * NODES_DEV, WIDE)
     origins, fields = zip(*pairs)
     return pl.pallas_call(
-        functools.partial(operator_kernel, n_col, origins),
-        grid=(n_col,),
-        in_specs=[SMEM] * 2 + [HBM] * 3 + [pl.BlockSpec((H, NODES_DEV), lambda s: (0, 0))] * len(fields),
-        out_specs=[
-            pl.BlockSpec((1,) + part, lambda s: (s, 0, 0, 0)),
-            pl.BlockSpec((H, n_row * TB), lambda s: (0, 0)),
-        ],
+        functools.partial(operator_kernel, n_row, n_col, origins),
+        in_specs=[SMEM] * 2 + [HBM] * 3 + [ANY] * len(fields),
+        out_specs=[HBM, VMEM],
         out_shape=[pltpu.HBM((n_col,) + part, BF16), jax.ShapeDtypeStruct((H, n_row * TB), F32)],
         scratch_shapes=[
             pltpu.VMEM((TILES_DEV, TB, TB), F32),
             pltpu.VMEM((n_row // 2, NODES_DEV, WIDE), F32),
+            pltpu.VMEM((2,) + part, BF16),
+            pltpu.VMEM((len(fields), H, NODES_DEV), F32),
             pltpu.SMEM((n_col, TILES_DEV), jnp.int32),
             pltpu.SMEM((n_col,), jnp.int32),
             pltpu.SMEM((1, TILES_DEV), jnp.int32),
             pltpu.SMEM((1, TILES_DEV), jnp.int32),
             pltpu.SemaphoreType.DMA((GROUPS,)),
             pltpu.SemaphoreType.DMA((2,)),
+            pltpu.SemaphoreType.DMA((len(fields),)),
+            pltpu.SemaphoreType.DMA((2, n_row // 2)),
         ],
-        compiler_params=params(40),
+        compiler_params=params(48),
         cost_estimate=HEAVY,
         name="operator",
     )(ids, live, *in_hbm(rows, slots, values), *fields)

time: 127 us -> 125 us (0.984); the launches traced: 125 us -> 126 us
  waiting for transfers between devices: 27.6 us -> 29.3 us
  transfers between devices with their start and end apart: 18 -> 18, of which waited for: 10 -> 11; matrix products, arithmetic and copies ran while one was open for 0% -> 0% of each run, Pallas kernels for 37% -> 37%
where the time goes in v14:
time: 125 us; the launch traced here: 126 us
  Pallas kernels  52.5 us (42%)
  starting transfers between devices  42.1 us (34%)
  waiting for transfers between devices  29.3 us (23%)
  between operations  1.45 us (1%)
    pallas_call x7, Pallas kernels, product(): pl.pallas_call(functools.partial(product_kernel, n_row, n_col, origins, h...  30.9 us
    all_to_all x5, starting transfers between devices, exchange(): lax.all_to_all(pieces, 'row', split_axis=0, concat_axis=0, tiled=True)  20.7 us
    ppermute x8, starting transfers between devices, shift(): lax.ppermute(x, 'col', [(c, (c + step) % n_col) for c in range(n_col)])  16.7 us
    ppermute x8, waiting for transfers between devices, shift(): lax.ppermute(x, 'col', [(c, (c + step) % n_col) for c in range(n_col)])  14 us
    all_to_all x5, waiting for transfers between devices, exchange(): lax.all_to_all(pieces, 'row', split_axis=0, concat_axis=0, tiled=True)  9.15 us
    pallas_call x1, Pallas kernels, build_operator(): pl.pallas_call(functools.partial(operator_kernel, n_row, n_col, origins),...  8.83 us
    ppermute x4, waiting for transfers between devices, opposite(): return lax.ppermute(sent, 'col', [(1, 0), (2, 3), (3, 1), (0, 2)])  6.1 us
    pallas_call x1, Pallas kernels, local_terms(): pl.pallas_call(functools.partial(local_kernel, n_row), in_specs=[ANY] + [...  4.88 us
  transfers between devices with their start and end apart: 18, of which 11 were waited for; matrix products, arithmetic and copies ran while one was open for 0% of the time, Pallas kernels for 37%

profile of v14, /device:TPU:0, one launch (start us, length us, event | category | flops | bytes accessed | tf_op | source)
XLA Modules:
  0.0 125.5 jit_solution(17720737625629374134)
XLA Ops:
  0.6 1.7 %term_two.1 = (f32[128,512]{1,0:T(8,128)S(1)}, f32[128,512]{1,0:T(8,128)S(1)}) custom-call(f32[512,256]{1,0:T(8,128)} %grad_hbm.3, s32[512,256]{1,0:T(8,128)} %mask_hbm.3, f32[3,256,256]{2,1,0:T(8,128)} %weight_hbm.3), custom_call_target="tpu_custom_call" | custom-call | flops 1024 | bytes 1024 | tf_op jit(solution)/shard_map/term_two/pallas_call | solution.py:76
  2.4 5.1 %collective-permute-start.1 = (f32[128,512]{1,0:T(8,128)S(1)}, f32[128,512]{1,0:T(8,128)S(1)}, u32[]{:S(2)}, u32[]{:S(2)}) collective-permute-start(f32[128,512]{1,0:T(8,128)S(1)} %get-tuple-element.20.first_ref.refs_0_), channel_id=1, source_target_pairs={{0,3},{1,0},{2,1},{3,2},{4,7},{5,4},{6,5},{7,6},{8,11},{9,8},{10,9... | collective-permute-start | bytes 786440 | tf_op jit(solution)/shard_map/ppermute | solution.py:419
  7.5 0.0 collective-permute-start
  7.5 4.9 %local_terms.1 = (f32[128,512]{1,0:T(8,128)}, f32[128,512]{1,0:T(8,128)}, f32[256,512]{1,0:T(8,128)S(1)}, f32[8,192,128]{2,1,0:T(8,128)}) custom-call(f32[128,512]{1,0:T(8,128)S(1)} %get-tuple-element.20.first_ref.refs_0_, f32[512,256]{1,0:T(8,128)} %grad_hbm.3, s32[512,256]{1,0:T(8,128)} %mask_hbm.3, f32[3,256,256]{2,1,0:T(8,128)} %weight_hbm.3, ...), custom_call_target="tpu_custom_call" | custom-call | flops 1024 | bytes 1024 | tf_op jit(solution)/shard_map/local_terms/pallas_call | solution.py:123
  12.4 3.7 %all-to-all-start = ((f32[8,192,128]{2,1,0:T(8,128)}), f32[8,192,128]{2,1,0:T(8,128)S(1)}, u32[]{:S(2)}, u32[]{:S(2)}) async-start(f32[8,192,128]{2,1,0:T(8,128)} %get-tuple-element.30), calls=%async_computation | async-start | bytes 1572864 | tf_op jit(solution)/shard_map/all_to_all | solution.py:423
  16.8 0.0 collective-permute-done.1.refs_2_
  16.8 2.8 %collective-permute-done.refs_1_ = f32[128,512]{1,0:T(8,128)S(1)} collective-permute-done((f32[128,512]{1,0:T(8,128)S(1)}, f32[128,512]{1,0:T(8,128)S(1)}, u32[]{:S(2)}, u32[]{:S(2)}) %collective-permute-start) | collective-permute-done | bytes 262176 | tf_op jit(solution)/shard_map/ppermute | solution.py:419
  19.6 0.1 select_select_fusion.3
  19.6 0.8 collective-permute-start.2
  20.4 8.8 %operator.1 = (bf16[4,4,1024,256]{3,2,1,0:T(8,128)(2,1)}, f32[128,1024]{1,0:T(8,128)S(1)}) custom-call(s32[1]{0:T(128)} %bitcast.2.ids_ref.refs_0_, s32[1]{0:T(128)S(6)} %copy.13.live_ref, s32[1,128]{1,0:T(1,128)} %rows_hbm.1, s32[1,128]{1,0:T(1,128)} %slots_hbm.1, f32[1,128,128,128]{3,2,1,0:T(8,128)} %values_ref.1, ...), custom_call_target="tpu_custom_call" | custom-call | flops 17179869184 | bytes 67108864 | tf_op jit(solution)/shard_map/operator/pallas_call | solution.py:225
  29.3 0.0 collective-permute-done.2.refs_2_
  29.3 0.3 collective-permute-start.4
  29.6 3.5 %collective-permute-start.3 = (f32[128,512]{1,0:T(8,128)S(1)}, f32[128,512]{1,0:T(8,128)S(1)}, u32[]{:S(2)}, u32[]{:S(2)}) collective-permute-start(f32[128,512]{1,0:T(8,128)S(1)} %get-tuple-element.27.refs_2_), channel_id=1, source_target_pairs={{0,3},{1,0},{2,1},{3,2},{4,7},{5,4},{6,5},{7,6},{8,11},{9,8},{10,9... | collective-permute-start | bytes 786440 | tf_op jit(solution)/shard_map/ppermute | solution.py:419
  33.1 0.0 all-to-all-done.refs_0_
  33.1 3.6 %product.8 = f32[8,128,128]{2,1,0:T(8,128)} custom-call(s32[1]{0:T(128)} %bitcast.2.ids_ref.refs_0_, bf16[4,4,1024,256]{3,2,1,0:T(8,128)(2,1)} %get-tuple-element.22.refs_1_, f32[128,512]{1,0:T(8,128)S(1)} %collective-permute-done.2.refs_2_, f32[128,1024]{1,0:T(8,128)S(1)} %get-tuple-element.31.refs_3_), custom_call_target="tpu_custom_call" | custom-call | flops 1024 | bytes 1024 | tf_op jit(solution)/shard_map/product/pallas_call | solution.py:316
  36.7 3.5 %all-to-all-start.1 = ((f32[8,128,128]{2,1,0:T(8,128)}), f32[8,128,128]{2,1,0:T(8,128)S(1)}, u32[]{:S(2)}, u32[]{:S(2)}) async-start(f32[8,128,128]{2,1,0:T(8,128)} %product.8), calls=%async_computation.1 | async-start | bytes 1048576 | tf_op jit(solution)/shard_map/all_to_all | solution.py:423
  40.2 0.1 collective-permute-done.4.refs_4_
  40.4 1.8 %collective-permute-done.3.refs_3_ = f32[128,512]{1,0:T(8,128)S(1)} collective-permute-done((f32[128,512]{1,0:T(8,128)S(1)}, f32[128,512]{1,0:T(8,128)S(1)}, u32[]{:S(2)}, u32[]{:S(2)}) %collective-permute-start.3) | collective-permute-done | bytes 262176 | tf_op jit(solution)/shard_map/ppermute | solution.py:419
  42.1 0.1 select_select_fusion.2
  42.2 0.0 copy-start
  42.2 1.8 %collective-permute-start.5 = (f32[128,512]{1,0:T(8,128)S(1)}, f32[128,512]{1,0:T(8,128)S(1)}, u32[]{:S(2)}, u32[]{:S(2)}) collective-permute-start(f32[128,512]{1,0:T(8,128)S(1)} %select_select_fusion.2), channel_id=1, source_target_pairs={{1,0},{2,3},{3,1},{0,2},{5,4},{6,7},{7,5},{4,6},{9,8},{10,11},{11,... | collective-permute-start | bytes 786440 | tf_op jit(solution)/shard_map/ppermute | solution.py:433
  44.0 5.5 %product.7.refs_3_ = f32[128,1024]{1,0:T(8,128)S(1)} custom-call(s32[1]{0:T(128)} %bitcast.2.ids_ref.refs_0_, bf16[4,4,1024,256]{3,2,1,0:T(8,128)(2,1)} %get-tuple-element.22.refs_1_, f32[128,512]{1,0:T(8,128)S(1)} %get-tuple-element.27.refs_2_, f32[128,512]{1,0:T(8,128)S(1)} %collective-permute-done.3.refs_3_, f32[128,512]{1,0:T(8,128)S(1)} %collective-permute-done.4.refs_4_), custom_call_target="tpu_custom_call" | custom-call | flops 17179869184 | bytes 67108864 | tf_op jit(solution)/shard_map/product/pallas_call | solution.py:316
  49.5 1.0 collective-permute-done.5.refs_2_
  50.5 0.0 all-to-all-done.1.came_ref
  50.5 0.0 copy-done
  50.5 1.5 %carry.2.refs_2_.refs_4_ = f32[176,512]{1,0:T(8,128)S(1)} custom-call(s32[8]{0:T(128)S(1)} %bitcast.3, f32[128,512]{1,0:T(8,128)} %get-tuple-element.29.base_hbm, f32[8,128,128]{2,1,0:T(8,128)S(1)} %all-to-all-done.1.came_ref, f32[8,192,128]{2,1,0:T(8,128)S(1)} %all-to-all-done.refs_0_), custom_call_target="tpu_custom_call" | custom-call | flops 1024 | bytes 1024 | tf_op jit(solution)/shard_map/carry/pallas_call | solution.py:354
  52.0 2.7 %collective-permute-start.7 = (f32[176,512]{1,0:T(8,128)S(1)}, f32[176,512]{1,0:T(8,128)S(1)}, u32[]{:S(2)}, u32[]{:S(2)}) collective-permute-start(f32[176,512]{1,0:T(8,128)S(1)} %carry.2.refs_2_.refs_4_), channel_id=1, source_target_pairs={{0,1},{1,2},{2,3},{3,0},{4,5},{5,6},{6,7},{7,4},{8,9},{9,10},{10,1... | collective-permute-start | bytes 1081352 | tf_op jit(solution)/shard_map/ppermute | solution.py:419
  54.7 1.2 collective-permute-start.6
  55.9 3.6 %product.11 = f32[8,128,128]{2,1,0:T(8,128)} custom-call(s32[1]{0:T(128)} %bitcast.2.ids_ref.refs_0_, bf16[4,4,1024,256]{3,2,1,0:T(8,128)(2,1)} %get-tuple-element.22.refs_1_, f32[128,512]{1,0:T(8,128)S(1)} %collective-permute-done.5.refs_2_, f32[128,1024]{1,0:T(8,128)S(1)} %product.7.refs_3_), custom_call_target="tpu_custom_call" | custom-call | flops 1024 | bytes 1024 | tf_op jit(solution)/shard_map/product/pallas_call | solution.py:316
  59.5 4.4 %all-to-all-start.3 = ((f32[8,128,128]{2,1,0:T(8,128)}), f32[8,128,128]{2,1,0:T(8,128)S(1)}, u32[]{:S(2)}, u32[]{:S(2)}) async-start(f32[8,128,128]{2,1,0:T(8,128)} %product.11), calls=%async_computation.3 | async-start | bytes 1048576 | tf_op jit(solution)/shard_map/all_to_all | solution.py:423
  63.8 1.4 %collective-permute-done.7.refs_3_.refs_7_ = f32[176,512]{1,0:T(8,128)S(1)} collective-permute-done((f32[176,512]{1,0:T(8,128)S(1)}, f32[176,512]{1,0:T(8,128)S(1)}, u32[]{:S(2)}, u32[]{:S(2)}) %collective-permute-start.7) | collective-permute-done | bytes 360480 | tf_op jit(solution)/shard_map/ppermute | solution.py:419
  65.3 5.8 %collective-permute-done.6.refs_4_.refs_5_ = f32[176,512]{1,0:T(8,128)S(1)} collective-permute-done((f32[176,512]{1,0:T(8,128)S(1)}, f32[176,512]{1,0:T(8,128)S(1)}, u32[]{:S(2)}, u32[]{:S(2)}) %collective-permute-start.6) | collective-permute-done | bytes 360480 | tf_op jit(solution)/shard_map/ppermute | solution.py:419
  71.1 0.1 select_select_fusion
  71.1 0.8 collective-permute-start.8
  72.0 5.5 %product.9.refs_3_ = f32[128,1024]{1,0:T(8,128)S(1)} custom-call(s32[1]{0:T(128)} %bitcast.2.ids_ref.refs_0_, bf16[4,4,1024,256]{3,2,1,0:T(8,128)(2,1)} %get-tuple-element.22.refs_1_, f32[176,512]{1,0:T(8,128)S(1)} %carry.2.refs_2_.refs_4_, f32[176,512]{1,0:T(8,128)S(1)} %collective-permute-done.7.refs_3_.refs_7_, ...), custom_call_target="tpu_custom_call" | custom-call | flops 17179869184 | bytes 67108864 | tf_op jit(solution)/shard_map/product/pallas_call | solution.py:316
  77.4 4.2 %collective-permute-done.8.refs_2_.refs_6_ = f32[176,512]{1,0:T(8,128)S(1)} collective-permute-done((f32[176,512]{1,0:T(8,128)S(1)}, f32[176,512]{1,0:T(8,128)S(1)}, u32[]{:S(2)}, u32[]{:S(2)}) %collective-permute-start.8) | collective-permute-done | bytes 360480 | tf_op jit(solution)/shard_map/ppermute | solution.py:433
  81.7 0.0 all-to-all-done.3.came_ref
  81.7 1.5 %carry.3.refs_2_ = f32[128,512]{1,0:T(8,128)S(1)} custom-call(s32[8]{0:T(128)S(1)} %bitcast.4, f32[128,512]{1,0:T(8,128)} %get-tuple-element.34.base_hbm, f32[8,128,128]{2,1,0:T(8,128)S(1)} %all-to-all-done.3.came_ref), custom_call_target="tpu_custom_call" | custom-call | flops 1024 | bytes 1024 | tf_op jit(solution)/shard_map/carry/pallas_call | solution.py:354
  83.2 1.5 %collective-permute-start.10 = (f32[128,512]{1,0:T(8,128)S(1)}, f32[128,512]{1,0:T(8,128)S(1)}, u32[]{:S(2)}, u32[]{:S(2)}) collective-permute-start(f32[128,512]{1,0:T(8,128)S(1)} %carry.3.refs_2_), channel_id=1, source_target_pairs={{0,1},{1,2},{2,3},{3,0},{4,5},{5,6},{6,7},{7,4},{8,9},{9,10},{10,1... | collective-permute-start | bytes 786440 | tf_op jit(solution)/shard_map/ppermute | solution.py:419
  84.8 2.3 %collective-permute-start.9 = (f32[128,512]{1,0:T(8,128)S(1)}, f32[128,512]{1,0:T(8,128)}, u32[]{:S(2)}, u32[]{:S(2)}) collective-permute-start(f32[128,512]{1,0:T(8,128)S(1)} %carry.3.refs_2_), channel_id=1, source_target_pairs={{0,3},{1,0},{2,1},{3,2},{4,7},{5,4},{6,5},{7,6},{8,11},{9,8},{10,9... | collective-permute-start | bytes 786440 | tf_op jit(solution)/shard_map/ppermute | solution.py:419
  87.1 3.8 %product.10 = f32[8,224,128]{2,1,0:T(8,128)} custom-call(s32[1]{0:T(128)} %bitcast.2.ids_ref.refs_0_, bf16[4,4,1024,256]{3,2,1,0:T(8,128)(2,1)} %get-tuple-element.22.refs_1_, f32[176,512]{1,0:T(8,128)S(1)} %collective-permute-done.8.refs_2_.refs_6_, f32[128,1024]{1,0:T(8,128)S(1)} %product.9.refs_3_, f32[176,512]{1,0:T(8,128)S(1)} %carry.2.refs_2_.refs_4_, ...), custom_call_target="tpu_custom_call" | custom-call | flops 1024 | bytes 1024 | tf_op jit(solution)/shard_map/product/pallas_call | solution.py:316
  90.9 4.6 %all-to-all-start.2 = ((f32[8,224,128]{2,1,0:T(8,128)}), f32[8,224,128]{2,1,0:T(8,128)S(1)}, u32[]{:S(2)}, u32[]{:S(2)}) async-start(f32[8,224,128]{2,1,0:T(8,128)} %product.10), calls=%async_computation.2 | async-start | bytes 1835008 | tf_op jit(solution)/shard_map/all_to_all | solution.py:423
  95.5 0.0 collective-permute-done.10.refs_4_
  95.5 2.1 %collective-permute-done.9.refs_3_ = f32[128,512]{1,0:T(8,128)} collective-permute-done((f32[128,512]{1,0:T(8,128)S(1)}, f32[128,512]{1,0:T(8,128)}, u32[]{:S(2)}, u32[]{:S(2)}) %collective-permute-start.9) | collective-permute-done | bytes 262176 | tf_op jit(solution)/shard_map/ppermute | solution.py:419
  97.6 0.1 select_select_fusion.1
  97.6 1.2 collective-permute-start.11
  98.9 5.5 %product.12.refs_3_ = f32[128,1024]{1,0:T(8,128)S(1)} custom-call(s32[1]{0:T(128)} %bitcast.2.ids_ref.refs_0_, bf16[4,4,1024,256]{3,2,1,0:T(8,128)(2,1)} %get-tuple-element.22.refs_1_, f32[128,512]{1,0:T(8,128)S(1)} %carry.3.refs_2_, f32[128,512]{1,0:T(8,128)} %collective-permute-done.9.refs_3_, f32[128,512]{1,0:T(8,128)S(1)} %collective-permute-done.10.refs_4_), custom_call_target="tpu_custom_call" | custom-call | flops 17179869184 | bytes 67108864 | tf_op jit(solution)/shard_map/product/pallas_call | solution.py:316
  104.4 0.9 collective-permute-done.11.refs_2_
  105.3 3.6 %product.13 = f32[8,128,128]{2,1,0:T(8,128)} custom-call(s32[1]{0:T(128)} %bitcast.2.ids_ref.refs_0_, bf16[4,4,1024,256]{3,2,1,0:T(8,128)(2,1)} %get-tuple-element.22.refs_1_, f32[128,512]{1,0:T(8,128)S(1)} %collective-permute-done.11.refs_2_, f32[128,1024]{1,0:T(8,128)S(1)} %product.12.refs_3_), custom_call_target="tpu_custom_call" | custom-call | flops 1024 | bytes 1024 | tf_op jit(solution)/shard_map/product/pallas_call | solution.py:316
  108.8 0.6 all-to-all-done.2.own_ref.left_ref
  109.5 0.0 collective-permute-start.12
  109.5 4.5 %all-to-all-start.4 = ((f32[8,128,128]{2,1,0:T(8,128)}), f32[8,128,128]{2,1,0:T(8,128)S(1)}, u32[]{:S(2)}, u32[]{:S(2)}) async-start(f32[8,128,128]{2,1,0:T(8,128)} %product.13), calls=%async_computation.4 | async-start | bytes 1048576 | tf_op jit(solution)/shard_map/all_to_all | solution.py:423
  114.0 0.0 collective-permute-done.12.other_ref
  114.0 1.2 assemble.1
  115.3 8.5 %all-to-all-done.4.right_ref = f32[8,128,128]{2,1,0:T(8,128)S(1)} async-done(((f32[8,128,128]{2,1,0:T(8,128)}), f32[8,128,128]{2,1,0:T(8,128)S(1)}, u32[]{:S(2)}, u32[]{:S(2)}) %all-to-all-start.4) | async-done | bytes 524320 | tf_op jit(solution)/shard_map/all_to_all | solution.py:423
  123.8 1.8 %finish.1 = f32[512,256]{1,0:T(8,128)} custom-call(s32[8]{0:T(128)S(1)} %bitcast.5, f32[256,512]{1,0:T(8,128)S(1)} %get-tuple-element.37.base_ref, f32[8,224,128]{2,1,0:T(8,128)S(1)} %all-to-all-done.2.own_ref.left_ref, f32[8,128,128]{2,1,0:T(8,128)S(1)} %all-to-all-done.4.right_ref), custom_call_target="tpu_custom_call" | custom-call | flops 1024 | bytes 1024 | tf_op jit(solution)/shard_map/finish/pallas_call | solution.py:376
Async XLA Ops:
  2.4 14.4 %collective-permute-start.1 = (f32[128,512]{1,0:T(8,128)S(1)}, f32[128,512]{1,0:T(8,128)S(1)}, u32[]{:S(2)}, u32[]{:S(2)}) collective-permute-start(f32[128,512]{1,0:T(8,128)S(1)} %get-tuple-element.20.first_ref.refs_0_), channel_id=1, source_target_pairs={{0,3},{1,0},{2,1},{3,2},{4,7},{5,4},{6,5},{7,6},{8,11},{9,8},{10,9... | collective-permute-start | bytes 786440 | tf_op jit(solution)/shard_map/ppermute | solution.py:419
  7.5 12.1 %collective-permute-start = (f32[128,512]{1,0:T(8,128)S(1)}, f32[128,512]{1,0:T(8,128)S(1)}, u32[]{:S(2)}, u32[]{:S(2)}) collective-permute-start(f32[128,512]{1,0:T(8,128)S(1)} %get-tuple-element.20.first_ref.refs_0_), channel_id=1, source_target_pairs={{0,1},{1,2},{2,3},{3,0},{4,5},{5,6},{6,7},{7,4},{8,9},{9,10},{10,1... | collective-permute-start | bytes 786440 | tf_op jit(solution)/shard_map/ppermute | solution.py:419
  12.4 20.8 %all-to-all-start = ((f32[8,192,128]{2,1,0:T(8,128)}), f32[8,192,128]{2,1,0:T(8,128)S(1)}, u32[]{:S(2)}, u32[]{:S(2)}) async-start(f32[8,192,128]{2,1,0:T(8,128)} %get-tuple-element.30), calls=%async_computation | async-start | bytes 1572864 | tf_op jit(solution)/shard_map/all_to_all | solution.py:423
  19.6 9.6 %collective-permute-start.2 = (f32[128,512]{1,0:T(8,128)S(1)}, f32[128,512]{1,0:T(8,128)S(1)}, u32[]{:S(2)}, u32[]{:S(2)}) collective-permute-start(f32[128,512]{1,0:T(8,128)S(1)} %select_select_fusion.3), channel_id=1, source_target_pairs={{1,0},{2,3},{3,1},{0,2},{5,4},{6,7},{7,5},{4,6},{9,8},{10,11},{11,... | collective-permute-start | bytes 786440 | tf_op jit(solution)/shard_map/ppermute | solution.py:433
  29.3 11.1 %collective-permute-start.4 = (f32[128,512]{1,0:T(8,128)S(1)}, f32[128,512]{1,0:T(8,128)S(1)}, u32[]{:S(2)}, u32[]{:S(2)}) collective-permute-start(f32[128,512]{1,0:T(8,128)S(1)} %get-tuple-element.27.refs_2_), channel_id=1, source_target_pairs={{0,1},{1,2},{2,3},{3,0},{4,5},{5,6},{6,7},{7,4},{8,9},{9,10},{10,1... | collective-permute-start | bytes 786440 | tf_op jit(solution)/shard_map/ppermute | solution.py:419
  29.6 12.5 %collective-permute-start.3 = (f32[128,512]{1,0:T(8,128)S(1)}, f32[128,512]{1,0:T(8,128)S(1)}, u32[]{:S(2)}, u32[]{:S(2)}) collective-permute-start(f32[128,512]{1,0:T(8,128)S(1)} %get-tuple-element.27.refs_2_), channel_id=1, source_target_pairs={{0,3},{1,0},{2,1},{3,2},{4,7},{5,4},{6,5},{7,6},{8,11},{9,8},{10,9... | collective-permute-start | bytes 786440 | tf_op jit(solution)/shard_map/ppermute | solution.py:419
  36.7 13.7 %all-to-all-start.1 = ((f32[8,128,128]{2,1,0:T(8,128)}), f32[8,128,128]{2,1,0:T(8,128)S(1)}, u32[]{:S(2)}, u32[]{:S(2)}) async-start(f32[8,128,128]{2,1,0:T(8,128)} %product.8), calls=%async_computation.1 | async-start | bytes 1048576 | tf_op jit(solution)/shard_map/all_to_all | solution.py:423
  42.2 8.3 %copy-start = (s32[1,8,1]{1,2,0:T(1,128)S(1)}, s32[1,8,1]{1,2,0:T(1,128)}, u32[]{:S(2)}) copy-start(s32[1,8,1]{1,2,0:T(1,128)} %param.20) | copy-start | bytes 100
  42.2 8.3 %collective-permute-start.5 = (f32[128,512]{1,0:T(8,128)S(1)}, f32[128,512]{1,0:T(8,128)S(1)}, u32[]{:S(2)}, u32[]{:S(2)}) collective-permute-start(f32[128,512]{1,0:T(8,128)S(1)} %select_select_fusion.2), channel_id=1, source_target_pairs={{1,0},{2,3},{3,1},{0,2},{5,4},{6,7},{7,5},{4,6},{9,8},{10,11},{11,... | collective-permute-start | bytes 786440 | tf_op jit(solution)/shard_map/ppermute | solution.py:433
  52.0 13.2 %collective-permute-start.7 = (f32[176,512]{1,0:T(8,128)S(1)}, f32[176,512]{1,0:T(8,128)S(1)}, u32[]{:S(2)}, u32[]{:S(2)}) collective-permute-start(f32[176,512]{1,0:T(8,128)S(1)} %carry.2.refs_2_.refs_4_), channel_id=1, source_target_pairs={{0,1},{1,2},{2,3},{3,0},{4,5},{5,6},{6,7},{7,4},{8,9},{9,10},{10,1... | collective-permute-start | bytes 1081352 | tf_op jit(solution)/shard_map/ppermute | solution.py:419
  54.7 16.4 %collective-permute-start.6 = (f32[176,512]{1,0:T(8,128)S(1)}, f32[176,512]{1,0:T(8,128)S(1)}, u32[]{:S(2)}, u32[]{:S(2)}) collective-permute-start(f32[176,512]{1,0:T(8,128)S(1)} %carry.2.refs_2_.refs_4_), channel_id=1, source_target_pairs={{0,3},{1,0},{2,1},{3,2},{4,7},{5,4},{6,5},{7,6},{8,11},{9,8},{10,9... | collective-permute-start | bytes 1081352 | tf_op jit(solution)/shard_map/ppermute | solution.py:419
  59.5 22.2 %all-to-all-start.3 = ((f32[8,128,128]{2,1,0:T(8,128)}), f32[8,128,128]{2,1,0:T(8,128)S(1)}, u32[]{:S(2)}, u32[]{:S(2)}) async-start(f32[8,128,128]{2,1,0:T(8,128)} %product.11), calls=%async_computation.3 | async-start | bytes 1048576 | tf_op jit(solution)/shard_map/all_to_all | solution.py:423
  71.1 10.5 %collective-permute-start.8 = (f32[176,512]{1,0:T(8,128)S(1)}, f32[176,512]{1,0:T(8,128)S(1)}, u32[]{:S(2)}, u32[]{:S(2)}) collective-permute-start(f32[176,512]{1,0:T(8,128)S(1)} %select_select_fusion), channel_id=1, source_target_pairs={{1,0},{2,3},{3,1},{0,2},{5,4},{6,7},{7,5},{4,6},{9,8},{10,11},{11,... | collective-permute-start | bytes 1081352 | tf_op jit(solution)/shard_map/ppermute | solution.py:433
  83.2 12.3 %collective-permute-start.10 = (f32[128,512]{1,0:T(8,128)S(1)}, f32[128,512]{1,0:T(8,128)S(1)}, u32[]{:S(2)}, u32[]{:S(2)}) collective-permute-start(f32[128,512]{1,0:T(8,128)S(1)} %carry.3.refs_2_), channel_id=1, source_target_pairs={{0,1},{1,2},{2,3},{3,0},{4,5},{5,6},{6,7},{7,4},{8,9},{9,10},{10,1... | collective-permute-start | bytes 786440 | tf_op jit(solution)/shard_map/ppermute | solution.py:419
  84.8 12.8 %collective-permute-start.9 = (f32[128,512]{1,0:T(8,128)S(1)}, f32[128,512]{1,0:T(8,128)}, u32[]{:S(2)}, u32[]{:S(2)}) collective-permute-start(f32[128,512]{1,0:T(8,128)S(1)} %carry.3.refs_2_), channel_id=1, source_target_pairs={{0,3},{1,0},{2,1},{3,2},{4,7},{5,4},{6,5},{7,6},{8,11},{9,8},{10,9... | collective-permute-start | bytes 786440 | tf_op jit(solution)/shard_map/ppermute | solution.py:419
  90.9 18.6 %all-to-all-start.2 = ((f32[8,224,128]{2,1,0:T(8,128)}), f32[8,224,128]{2,1,0:T(8,128)S(1)}, u32[]{:S(2)}, u32[]{:S(2)}) async-start(f32[8,224,128]{2,1,0:T(8,128)} %product.10), calls=%async_computation.2 | async-start | bytes 1835008 | tf_op jit(solution)/shard_map/all_to_all | solution.py:423
  97.6 7.6 %collective-permute-start.11 = (f32[128,512]{1,0:T(8,128)S(1)}, f32[128,512]{1,0:T(8,128)S(1)}, u32[]{:S(2)}, u32[]{:S(2)}) collective-permute-start(f32[128,512]{1,0:T(8,128)S(1)} %select_select_fusion.1), channel_id=1, source_target_pairs={{1,0},{2,3},{3,1},{0,2},{5,4},{6,7},{7,5},{4,6},{9,8},{10,11},{11,... | collective-permute-start | bytes 786440 | tf_op jit(solution)/shard_map/ppermute | solution.py:433
  109.5 4.5 %collective-permute-start.12 = (f32[8,224,128]{2,1,0:T(8,128)S(1)}, f32[8,224,128]{2,1,0:T(8,128)S(1)}, u32[]{:S(2)}, u32[]{:S(2)}) collective-permute-start(f32[8,224,128]{2,1,0:T(8,128)S(1)} %all-to-all-done.2.own_ref.left_ref), channel_id=1, source_target_pairs={{0,4},{4,0},{8,12},{12,8},{16,20},{20,16},{24,28},{28,24},{1,5},{5... | collective-permute-start | bytes 2752520 | tf_op jit(solution)/shard_map/ppermute | solution.py:516
  109.5 14.3 %all-to-all-start.4 = ((f32[8,128,128]{2,1,0:T(8,128)}), f32[8,128,128]{2,1,0:T(8,128)S(1)}, u32[]{:S(2)}, u32[]{:S(2)}) async-start(f32[8,128,128]{2,1,0:T(8,128)} %product.13), calls=%async_computation.4 | async-start | bytes 1048576 | tf_op jit(solution)/shard_map/all_to_all | solution.py:423

commit v15 on v14

--- a/solution.py
+++ b/solution.py
@@ -17,6 +17,8 @@
 TILES_DEV = 128
 GROUPS = 8
 MIB = 1 << 20
+WHOLE_BYTES = 12 * MIB
+DEPTH = 4
 HEAVY = pl.CostEstimate(flops=1 << 34, bytes_accessed=64 * MIB, transcendentals=0)
 LIGHT = pl.CostEstimate(flops=1024, bytes_accessed=1024, transcendentals=0)
 BF16 = jnp.bfloat16
@@ -155,6 +157,7 @@
     out_hbm, total_ref, tiles, acc, buf, held, lists, counts, rows, slots, sems, small_sems, field_sems, out_sems = refs
     size = TILES_DEV // GROUPS
     pairs = n_row // 2
+    whole = acc.shape[0] == n_col
     small = fetch((rows_hbm, slots_hbm), (rows, slots), small_sems)
     parts = [pl.ds(g * size, size) for g in range(GROUPS)]
     tile_copies = fetch([values_ref.at[0, part] for part in parts], [tiles.at[part] for part in parts], sems)
@@ -162,46 +165,74 @@
     for item in small:
         item.wait()
 
-    def place(t, counted):
+    def place_of(t):
         row = rows[0, t]
-        s = lax.rem(row // CHB - ids_ref[0] + n_col, n_col)
         if n_col & (n_col - 1) == 0:
             s = (lax.shift_right_logical(row, CHB.bit_length() - 1) - ids_ref[0]) & (n_col - 1)
-        position = slots[0, t] * CHB + (row & (CHB - 1))
-        n = counted[0]
-        for k in range(1, n_col):
-            n = jnp.where(s == k, counted[k], n)
-        lists[s, n] = position * TILES_DEV + t
-        return tuple(c + (s == k).astype(jnp.int32) for k, c in enumerate(counted))
-
-    counted = lax.fori_loop(0, live_ref[0], place, (jnp.int32(0),) * n_col)
-    for s in range(n_col):
-        counts[s] = counted[s]
+        else:
+            s = lax.rem(row // CHB - ids_ref[0] + n_col, n_col)
+        return s, slots[0, t] * CHB + (row & (CHB - 1))
+
+    def add_block(into, position, tile):
+        slot = lax.shift_right_logical(position, CHB.bit_length() - 1)
+        at_row = pl.ds(pl.multiple_of((position & (CHB - 1)) * TB, TB), TB)
+        at_lane = pl.ds(pl.multiple_of((slot & 1) * TB, TB), TB)
+        acc[into, lax.shift_right_logical(slot, 1), at_row, at_lane] += tiles[tile]
+
+    if whole:
+
+        def add_now(t, carry):
+            s, position = place_of(t)
+            add_block(s, position, t)
+            return carry
+
+        acc[...] = jnp.zeros_like(acc)
+        for g, item in enumerate(tile_copies):
+            item.wait()
+            end = (g + 1) * size
+
+            @pl.when(live_ref[0] >= end)
+            def _():
+                lax.fori_loop(end - size, end, add_now, 0, unroll=4)
+
+            @pl.when(live_ref[0] < end)
+            def _():
+                lax.fori_loop(end - size, live_ref[0], add_now, 0)
+
+    else:
+
+        def place(t, counted):
+            s, position = place_of(t)
+            n = counted[0]
+            for k in range(1, n_col):
+                n = jnp.where(s == k, counted[k], n)
+            lists[s, n] = position * TILES_DEV + t
+            return tuple(c + (s == k).astype(jnp.int32) for k, c in enumerate(counted))
+
+        counted = lax.fori_loop(0, live_ref[0], place, (jnp.int32(0),) * n_col)
+        for s in range(n_col):
+            counts[s] = counted[s]
+        for item in tile_copies:
+            item.wait()
 
     def out_copy(origin, p):
         return pltpu.make_async_copy(buf.at[origin % 2, p], out_hbm.at[origin, p], out_sems.at[origin % 2, p])
 
     for origin in range(n_col):
-        acc[...] = jnp.zeros_like(acc)
-        if origin == 0:
-            for item in tile_copies:
-                item.wait()
-
-        def add(n, carry):
-            entry = lists[origin, n]
-            tile = entry & (TILES_DEV - 1)
-            position = lax.shift_right_logical(entry, TILES_DEV.bit_length() - 1)
-            slot = lax.shift_right_logical(position, CHB.bit_length() - 1)
-            at_row = pl.ds(pl.multiple_of((position & (CHB - 1)) * TB, TB), TB)
-            at_lane = pl.ds(pl.multiple_of((slot & 1) * TB, TB), TB)
-            acc[lax.shift_right_logical(slot, 1), at_row, at_lane] += tiles[tile]
-            return carry
-
-        lax.fori_loop(0, counts[origin], add, 0)
+        if not whole:
+
+            def add(n, carry):
+                entry = lists[origin, n]
+                add_block(0, lax.shift_right_logical(entry, TILES_DEV.bit_length() - 1), entry & (TILES_DEV - 1))
+                return carry
+
+            acc[...] = jnp.zeros_like(acc)
+            lax.fori_loop(0, counts[origin], add, 0)
+        summed_blocks = acc.at[origin if whole else 0]
         for p in range(pairs):
             if origin >= 2:
                 out_copy(origin - 2, p).wait()
-            high, low = split(acc[p])
+            high, low = split(summed_blocks[p])
             buf[origin % 2, p, :NODES_DEV, :] = high
             buf[origin % 2, p, NODES_DEV:, :] = low
             out_copy(origin, p).start()
@@ -221,6 +252,8 @@
 
 def build_operator(n_row, n_col, ids, live, rows, slots, values, pairs):
     part = (n_row // 2, 2 * NODES_DEV, WIDE)
+    sums = (n_row // 2, NODES_DEV, WIDE)
+    held_origins = n_col if 4 * n_col * n_row * TB * NODES_DEV <= WHOLE_BYTES else 1
     origins, fields = zip(*pairs)
     return pl.pallas_call(
         functools.partial(operator_kernel, n_row, n_col, origins),
@@ -229,7 +262,7 @@
         out_shape=[pltpu.HBM((n_col,) + part, BF16), jax.ShapeDtypeStruct((H, n_row * TB), F32)],
         scratch_shapes=[
             pltpu.VMEM((TILES_DEV, TB, TB), F32),
-            pltpu.VMEM((n_row // 2, NODES_DEV, WIDE), F32),
+            pltpu.VMEM((held_origins,) + sums, F32),
             pltpu.VMEM((2,) + part, BF16),
             pltpu.VMEM((len(fields), H, NODES_DEV), F32),
             pltpu.SMEM((n_col, TILES_DEV), jnp.int32),
@@ -254,21 +287,21 @@
     if has_prev:
         prev, refs = refs[0], refs[1:]
     carriers, refs = refs[:n_carriers], refs[n_carriers:]
-    out_ref, held, buf, field_sems, sems = refs[:5]
+    out_ref, held, buf, field_sems, sems, out, out_sems = refs[:7]
+    order = [(k, p) for p in range(n_row // 2) for k in range(n)]
 
     def copy(k, p):
         return pltpu.make_async_copy(op_ref.at[origins[k], p], buf.at[k, p], sems.at[k, p])
 
     field_copies = fetch([x.at[pl.ds(0, H)] for x in fields], [held.at[k] for k in range(n)], field_sems)
-    for p in range(n_row // 2):
-        for k in range(n):
-            copy(k, p).start()
+    for k, p in order[:DEPTH]:
+        copy(k, p).start()
     left = []
     for k in range(n):
         field_copies[k].wait()
         left.append(stacked(held[k]))
     if n_carriers:
-        ordered = refs[5]
+        ordered = refs[7]
         for k in range(n_col):
             ordered[lax.rem(ids_ref[0] + k, n_col)] = carriers[k][H:, :]
         share = ordered[0]
@@ -279,22 +312,31 @@
         for j in range(groups):
             for q in range(n_row):
                 from_lane = (q % 2 * groups + j) * LANES
-                out_ref[q, H + j * rows : H + (j + 1) * rows, :] = share[:, from_lane : from_lane + LANES]
+                out[q, H + j * rows : H + (j + 1) * rows, :] = share[:, from_lane : from_lane + LANES]
+    sent = []
     for p in range(n_row // 2):
         here = slice(p * WIDE, (p + 1) * WIDE)
         total = None
         for k in range(n):
             copy(k, p).wait()
+            ahead = p * n + k + DEPTH
+            if ahead < len(order):
+                copy(*order[ahead]).start()
             part = jnp.dot(left[k], buf[k, p], preferred_element_type=F32)
             total = part if total is None else total + part
         summed = total[:H] + total[H:]
         if has_prev:
             summed = summed + prev[:, here]
         if last:
-            out_ref[2 * p, :H, :] = summed[:, :TB]
-            out_ref[2 * p + 1, :H, :] = summed[:, TB:]
+            out[2 * p, :H, :] = summed[:, :TB]
+            out[2 * p + 1, :H, :] = summed[:, TB:]
+            both = pl.ds(2 * p, 2)
+            sent.append(pltpu.make_async_copy(out.at[both], out_ref.at[both], out_sems.at[p]))
+            sent[-1].start()
         else:
             out_ref[:, here] = summed
+    for item in sent:
+        item.wait()
 
 
 def product(n_row, n_col, ids, origins, operator, fields, prev, last, carriers=()):
@@ -310,14 +352,16 @@
     if carriers:
         rows = carriers[0].shape[0] - H
         share = rows * NODES_DEV // LANES // 2
+    scratch += [pltpu.VMEM((n_row, H + share, TB) if last else (8, LANES), F32), pltpu.SemaphoreType.DMA((n_row // 2,))]
+    if carriers:
         scratch.append(pltpu.VMEM((n_col, rows, NODES_DEV), F32))
     shape = (n_row, H + share, TB) if last else (H, n_row * TB)
     count = has_prev + len(carriers)
     return pl.pallas_call(
         functools.partial(product_kernel, n_row, n_col, origins, has_prev, last, len(carriers)),
         in_specs=[SMEM, HBM] + [ANY] * n + [VMEM] * count,
-        out_specs=VMEM,
-        out_shape=jax.ShapeDtypeStruct(shape, F32),
+        out_specs=HBM if last else VMEM,
+        out_shape=(pltpu.HBM if last else jax.ShapeDtypeStruct)(shape, F32),
         scratch_shapes=scratch,
         compiler_params=params(48),
         cost_estimate=LIGHT if last else HEAVY,

time: 125 us -> 123 us (0.984); the launches traced: 126 us -> 122 us
  starting transfers between devices: 42.1 us -> 40.2 us
  Pallas kernels: 52.5 us -> 51 us
    all_to_all x5, starting transfers between devices: 20.7 us -> 18.7 us  [exchange(): lax.all_to_all(pieces, 'row', split_axis=0, concat_axis=0, tiled=True)]
    ppermute x4, waiting for transfers between devices: 6.1 us -> 4.71 us  [opposite(): return lax.ppermute(sent, 'col', [(1, 0), (2, 3), (3, 1), (0, 2)])]
    pallas_call x1, Pallas kernels: 8.83 us -> 7.55 us  [build_operator(): pl.pallas_call(functools.partial(operator_kernel, n_row, n_col, origins),...]
  transfers between devices with their start and end apart: 18 -> 18, of which waited for: 11 -> 9; matrix products, arithmetic and copies ran while one was open for 0% -> 0% of each run, Pallas kernels for 37% -> 37%
where the time goes in v15:
time: 123 us; the launch traced here: 122 us
  Pallas kernels  51 us (41%)
  starting transfers between devices  40.2 us (33%)
  waiting for transfers between devices  28.7 us (23%)
  between operations  1.45 us (1%)
    pallas_call x7, Pallas kernels, product(): pl.pallas_call(functools.partial(product_kernel, n_row, n_col, origins, h...  30.7 us
    all_to_all x5, starting transfers between devices, exchange(): lax.all_to_all(pieces, 'row', split_axis=0, concat_axis=0, tiled=True)  18.7 us
    ppermute x8, starting transfers between devices, shift(): lax.ppermute(x, 'col', [(c, (c + step) % n_col) for c in range(n_col)])  16.7 us
    ppermute x8, waiting for transfers between devices, shift(): lax.ppermute(x, 'col', [(c, (c + step) % n_col) for c in range(n_col)])  15 us
    all_to_all x5, waiting for transfers between devices, exchange(): lax.all_to_all(pieces, 'row', split_axis=0, concat_axis=0, tiled=True)  8.99 us
    pallas_call x1, Pallas kernels, build_operator(): pl.pallas_call(functools.partial(operator_kernel, n_row, n_col, origins),...  7.55 us
    pallas_call x1, Pallas kernels, local_terms(): pl.pallas_call(functools.partial(local_kernel, n_row), in_specs=[ANY] + [...  4.88 us
    ppermute x4, starting transfers between devices, opposite(): return lax.ppermute(sent, 'col', [(1, 0), (2, 3), (3, 1), (0, 2)])  4.8 us
  transfers between devices with their start and end apart: 18, of which 9 were waited for; matrix products, arithmetic and copies ran while one was open for 0% of the time, Pallas kernels for 37%

profile of v15, /device:TPU:0, one launch (start us, length us, event | category | flops | bytes accessed | tf_op | source)
XLA Modules:
  0.0 121.6 jit_solution(17182763107488927316)
XLA Ops:
  0.6 1.7 %term_two.1 = (f32[128,512]{1,0:T(8,128)S(1)}, f32[128,512]{1,0:T(8,128)S(1)}) custom-call(f32[512,256]{1,0:T(8,128)} %grad_hbm.3, s32[512,256]{1,0:T(8,128)} %mask_hbm.3, f32[3,256,256]{2,1,0:T(8,128)} %weight_hbm.3), custom_call_target="tpu_custom_call" | custom-call | flops 1024 | bytes 1024 | tf_op jit(solution)/shard_map/term_two/pallas_call | solution.py:78
  2.4 5.1 %collective-permute-start.1 = (f32[128,512]{1,0:T(8,128)S(1)}, f32[128,512]{1,0:T(8,128)S(1)}, u32[]{:S(2)}, u32[]{:S(2)}) collective-permute-start(f32[128,512]{1,0:T(8,128)S(1)} %get-tuple-element.20.first_ref.refs_0_), channel_id=1, source_target_pairs={{0,3},{1,0},{2,1},{3,2},{4,7},{5,4},{6,5},{7,6},{8,11},{9,8},{10,9... | collective-permute-start | bytes 786440 | tf_op jit(solution)/shard_map/ppermute | solution.py:463
  7.5 0.0 collective-permute-start
  7.5 4.9 %local_terms.1 = (f32[128,512]{1,0:T(8,128)}, f32[128,512]{1,0:T(8,128)}, f32[256,512]{1,0:T(8,128)S(1)}, f32[8,192,128]{2,1,0:T(8,128)}) custom-call(f32[128,512]{1,0:T(8,128)S(1)} %get-tuple-element.20.first_ref.refs_0_, f32[512,256]{1,0:T(8,128)} %grad_hbm.3, s32[512,256]{1,0:T(8,128)} %mask_hbm.3, f32[3,256,256]{2,1,0:T(8,128)} %weight_hbm.3, ...), custom_call_target="tpu_custom_call" | custom-call | flops 1024 | bytes 1024 | tf_op jit(solution)/shard_map/local_terms/pallas_call | solution.py:125
  12.4 3.7 %all-to-all-start = ((f32[8,192,128]{2,1,0:T(8,128)}), f32[8,192,128]{2,1,0:T(8,128)S(1)}, u32[]{:S(2)}, u32[]{:S(2)}) async-start(f32[8,192,128]{2,1,0:T(8,128)} %get-tuple-element.30), calls=%async_computation | async-start | bytes 1572864 | tf_op jit(solution)/shard_map/all_to_all | solution.py:467
  16.8 0.0 collective-permute-done.1.refs_2_
  16.8 2.8 %collective-permute-done.refs_1_ = f32[128,512]{1,0:T(8,128)S(1)} collective-permute-done((f32[128,512]{1,0:T(8,128)S(1)}, f32[128,512]{1,0:T(8,128)S(1)}, u32[]{:S(2)}, u32[]{:S(2)}) %collective-permute-start) | collective-permute-done | bytes 262176 | tf_op jit(solution)/shard_map/ppermute | solution.py:463
  19.6 0.1 select_select_fusion.3
  19.6 0.8 collective-permute-start.2
  20.4 7.6 %operator.1 = (bf16[4,4,1024,256]{3,2,1,0:T(8,128)(2,1)}, f32[128,1024]{1,0:T(8,128)S(1)}) custom-call(s32[1]{0:T(128)} %bitcast.2.ids_ref.refs_0_, s32[1]{0:T(128)S(6)} %copy.13.live_ref, s32[1,128]{1,0:T(1,128)} %rows_hbm.1, s32[1,128]{1,0:T(1,128)} %slots_hbm.1, f32[1,128,128,128]{3,2,1,0:T(8,128)} %values_ref.1, ...), custom_call_target="tpu_custom_call" | custom-call | flops 17179869184 | bytes 67108864 | tf_op jit(solution)/shard_map/operator/pallas_call | solution.py:258
  28.0 0.0 collective-permute-done.2.refs_2_
  28.0 1.4 %collective-permute-start.4 = (f32[128,512]{1,0:T(8,128)S(1)}, f32[128,512]{1,0:T(8,128)S(1)}, u32[]{:S(2)}, u32[]{:S(2)}) collective-permute-start(f32[128,512]{1,0:T(8,128)S(1)} %get-tuple-element.27.refs_2_), channel_id=1, source_target_pairs={{0,1},{1,2},{2,3},{3,0},{4,5},{5,6},{6,7},{7,4},{8,9},{9,10},{10,1... | collective-permute-start | bytes 786440 | tf_op jit(solution)/shard_map/ppermute | solution.py:463
  29.4 2.5 %collective-permute-start.3 = (f32[128,512]{1,0:T(8,128)S(1)}, f32[128,512]{1,0:T(8,128)S(1)}, u32[]{:S(2)}, u32[]{:S(2)}) collective-permute-start(f32[128,512]{1,0:T(8,128)S(1)} %get-tuple-element.27.refs_2_), channel_id=1, source_target_pairs={{0,3},{1,0},{2,1},{3,2},{4,7},{5,4},{6,5},{7,6},{8,11},{9,8},{10,9... | collective-permute-start | bytes 786440 | tf_op jit(solution)/shard_map/ppermute | solution.py:463
  31.9 0.0 all-to-all-done.refs_0_
  31.9 3.5 %product.8 = f32[8,128,128]{2,1,0:T(8,128)} custom-call(s32[1]{0:T(128)} %bitcast.2.ids_ref.refs_0_, bf16[4,4,1024,256]{3,2,1,0:T(8,128)(2,1)} %get-tuple-element.22.refs_1_, f32[128,512]{1,0:T(8,128)S(1)} %collective-permute-done.2.refs_2_, f32[128,1024]{1,0:T(8,128)S(1)} %get-tuple-element.31.refs_3_), custom_call_target="tpu_custom_call" | custom-call | flops 1024 | bytes 1024 | tf_op jit(solution)/shard_map/product/pallas_call | solution.py:360
  35.4 3.7 %all-to-all-start.1 = ((f32[8,128,128]{2,1,0:T(8,128)}), f32[8,128,128]{2,1,0:T(8,128)S(1)}, u32[]{:S(2)}, u32[]{:S(2)}) async-start(f32[8,128,128]{2,1,0:T(8,128)} %product.8), calls=%async_computation.1 | async-start | bytes 1048576 | tf_op jit(solution)/shard_map/all_to_all | solution.py:467
  39.1 0.0 collective-permute-done.4.refs_4_
  39.1 2.5 %collective-permute-done.3.refs_3_ = f32[128,512]{1,0:T(8,128)S(1)} collective-permute-done((f32[128,512]{1,0:T(8,128)S(1)}, f32[128,512]{1,0:T(8,128)S(1)}, u32[]{:S(2)}, u32[]{:S(2)}) %collective-permute-start.3) | collective-permute-done | bytes 262176 | tf_op jit(solution)/shard_map/ppermute | solution.py:463
  41.6 0.1 select_select_fusion.2
  41.6 0.0 copy-start
  41.6 1.5 %collective-permute-start.5 = (f32[128,512]{1,0:T(8,128)S(1)}, f32[128,512]{1,0:T(8,128)S(1)}, u32[]{:S(2)}, u32[]{:S(2)}) collective-permute-start(f32[128,512]{1,0:T(8,128)S(1)} %select_select_fusion.2), channel_id=1, source_target_pairs={{1,0},{2,3},{3,1},{0,2},{5,4},{6,7},{7,5},{4,6},{9,8},{10,11},{11,... | collective-permute-start | bytes 786440 | tf_op jit(solution)/shard_map/ppermute | solution.py:477
  43.1 5.6 %product.7.refs_3_ = f32[128,1024]{1,0:T(8,128)S(1)} custom-call(s32[1]{0:T(128)} %bitcast.2.ids_ref.refs_0_, bf16[4,4,1024,256]{3,2,1,0:T(8,128)(2,1)} %get-tuple-element.22.refs_1_, f32[128,512]{1,0:T(8,128)S(1)} %get-tuple-element.27.refs_2_, f32[128,512]{1,0:T(8,128)S(1)} %collective-permute-done.3.refs_3_, f32[128,512]{1,0:T(8,128)S(1)} %collective-permute-done.4.refs_4_), custom_call_target="tpu_custom_call" | custom-call | flops 17179869184 | bytes 67108864 | tf_op jit(solution)/shard_map/product/pallas_call | solution.py:360
  48.7 0.6 collective-permute-done.5.refs_2_
  49.3 0.0 all-to-all-done.1.came_ref
  49.3 0.0 copy-done
  49.3 1.5 %carry.2.refs_2_.refs_4_ = f32[176,512]{1,0:T(8,128)S(1)} custom-call(s32[8]{0:T(128)S(1)} %bitcast.3, f32[128,512]{1,0:T(8,128)} %get-tuple-element.29.base_hbm, f32[8,128,128]{2,1,0:T(8,128)S(1)} %all-to-all-done.1.came_ref, f32[8,192,128]{2,1,0:T(8,128)S(1)} %all-to-all-done.refs_0_), custom_call_target="tpu_custom_call" | custom-call | flops 1024 | bytes 1024 | tf_op jit(solution)/shard_map/carry/pallas_call | solution.py:398
  50.8 2.7 %collective-permute-start.7 = (f32[176,512]{1,0:T(8,128)S(1)}, f32[176,512]{1,0:T(8,128)S(1)}, u32[]{:S(2)}, u32[]{:S(2)}) collective-permute-start(f32[176,512]{1,0:T(8,128)S(1)} %carry.2.refs_2_.refs_4_), channel_id=1, source_target_pairs={{0,1},{1,2},{2,3},{3,0},{4,5},{5,6},{6,7},{7,4},{8,9},{9,10},{10,1... | collective-permute-start | bytes 1081352 | tf_op jit(solution)/shard_map/ppermute | solution.py:463
  53.5 1.2 collective-permute-start.6
  54.7 3.5 %product.11 = f32[8,128,128]{2,1,0:T(8,128)} custom-call(s32[1]{0:T(128)} %bitcast.2.ids_ref.refs_0_, bf16[4,4,1024,256]{3,2,1,0:T(8,128)(2,1)} %get-tuple-element.22.refs_1_, f32[128,512]{1,0:T(8,128)S(1)} %collective-permute-done.5.refs_2_, f32[128,1024]{1,0:T(8,128)S(1)} %product.7.refs_3_), custom_call_target="tpu_custom_call" | custom-call | flops 1024 | bytes 1024 | tf_op jit(solution)/shard_map/product/pallas_call | solution.py:360
  58.2 3.8 %all-to-all-start.3 = ((f32[8,128,128]{2,1,0:T(8,128)}), f32[8,128,128]{2,1,0:T(8,128)S(1)}, u32[]{:S(2)}, u32[]{:S(2)}) async-start(f32[8,128,128]{2,1,0:T(8,128)} %product.11), calls=%async_computation.3 | async-start | bytes 1048576 | tf_op jit(solution)/shard_map/all_to_all | solution.py:467
  62.0 2.1 %collective-permute-done.7.refs_3_.refs_7_ = f32[176,512]{1,0:T(8,128)S(1)} collective-permute-done((f32[176,512]{1,0:T(8,128)S(1)}, f32[176,512]{1,0:T(8,128)S(1)}, u32[]{:S(2)}, u32[]{:S(2)}) %collective-permute-start.7) | collective-permute-done | bytes 360480 | tf_op jit(solution)/shard_map/ppermute | solution.py:463
  64.0 5.1 %collective-permute-done.6.refs_4_.refs_5_ = f32[176,512]{1,0:T(8,128)S(1)} collective-permute-done((f32[176,512]{1,0:T(8,128)S(1)}, f32[176,512]{1,0:T(8,128)S(1)}, u32[]{:S(2)}, u32[]{:S(2)}) %collective-permute-start.6) | collective-permute-done | bytes 360480 | tf_op jit(solution)/shard_map/ppermute | solution.py:463
  69.2 0.1 select_select_fusion
  69.2 0.8 collective-permute-start.8
  70.1 5.6 %product.9.refs_3_ = f32[128,1024]{1,0:T(8,128)S(1)} custom-call(s32[1]{0:T(128)} %bitcast.2.ids_ref.refs_0_, bf16[4,4,1024,256]{3,2,1,0:T(8,128)(2,1)} %get-tuple-element.22.refs_1_, f32[176,512]{1,0:T(8,128)S(1)} %carry.2.refs_2_.refs_4_, f32[176,512]{1,0:T(8,128)S(1)} %collective-permute-done.7.refs_3_.refs_7_, ...), custom_call_target="tpu_custom_call" | custom-call | flops 17179869184 | bytes 67108864 | tf_op jit(solution)/shard_map/product/pallas_call | solution.py:360
  75.7 4.1 %collective-permute-done.8.refs_2_.refs_6_ = f32[176,512]{1,0:T(8,128)S(1)} collective-permute-done((f32[176,512]{1,0:T(8,128)S(1)}, f32[176,512]{1,0:T(8,128)S(1)}, u32[]{:S(2)}, u32[]{:S(2)}) %collective-permute-start.8) | collective-permute-done | bytes 360480 | tf_op jit(solution)/shard_map/ppermute | solution.py:477
  79.8 0.0 all-to-all-done.3.came_ref
  79.8 1.5 %carry.3.refs_2_ = f32[128,512]{1,0:T(8,128)S(1)} custom-call(s32[8]{0:T(128)S(1)} %bitcast.4, f32[128,512]{1,0:T(8,128)} %get-tuple-element.34.base_hbm, f32[8,128,128]{2,1,0:T(8,128)S(1)} %all-to-all-done.3.came_ref), custom_call_target="tpu_custom_call" | custom-call | flops 1024 | bytes 1024 | tf_op jit(solution)/shard_map/carry/pallas_call | solution.py:398
  81.3 1.5 %collective-permute-start.10 = (f32[128,512]{1,0:T(8,128)S(1)}, f32[128,512]{1,0:T(8,128)S(1)}, u32[]{:S(2)}, u32[]{:S(2)}) collective-permute-start(f32[128,512]{1,0:T(8,128)S(1)} %carry.3.refs_2_), channel_id=1, source_target_pairs={{0,1},{1,2},{2,3},{3,0},{4,5},{5,6},{6,7},{7,4},{8,9},{9,10},{10,1... | collective-permute-start | bytes 786440 | tf_op jit(solution)/shard_map/ppermute | solution.py:463
  82.9 2.3 %collective-permute-start.9 = (f32[128,512]{1,0:T(8,128)S(1)}, f32[128,512]{1,0:T(8,128)}, u32[]{:S(2)}, u32[]{:S(2)}) collective-permute-start(f32[128,512]{1,0:T(8,128)S(1)} %carry.3.refs_2_), channel_id=1, source_target_pairs={{0,3},{1,0},{2,1},{3,2},{4,7},{5,4},{6,5},{7,6},{8,11},{9,8},{10,9... | collective-permute-start | bytes 786440 | tf_op jit(solution)/shard_map/ppermute | solution.py:463
  85.2 3.5 %product.10 = f32[8,224,128]{2,1,0:T(8,128)} custom-call(s32[1]{0:T(128)} %bitcast.2.ids_ref.refs_0_, bf16[4,4,1024,256]{3,2,1,0:T(8,128)(2,1)} %get-tuple-element.22.refs_1_, f32[176,512]{1,0:T(8,128)S(1)} %collective-permute-done.8.refs_2_.refs_6_, f32[128,1024]{1,0:T(8,128)S(1)} %product.9.refs_3_, f32[176,512]{1,0:T(8,128)S(1)} %carry.2.refs_2_.refs_4_, ...), custom_call_target="tpu_custom_call" | custom-call | flops 1024 | bytes 1024 | tf_op jit(solution)/shard_map/product/pallas_call | solution.py:360
  88.7 3.9 %all-to-all-start.2 = ((f32[8,224,128]{2,1,0:T(8,128)}), f32[8,224,128]{2,1,0:T(8,128)S(1)}, u32[]{:S(2)}, u32[]{:S(2)}) async-start(f32[8,224,128]{2,1,0:T(8,128)} %product.10), calls=%async_computation.2 | async-start | bytes 1835008 | tf_op jit(solution)/shard_map/all_to_all | solution.py:467
  92.6 0.0 collective-permute-done.10.refs_4_
  92.6 2.6 %collective-permute-done.9.refs_3_ = f32[128,512]{1,0:T(8,128)} collective-permute-done((f32[128,512]{1,0:T(8,128)S(1)}, f32[128,512]{1,0:T(8,128)}, u32[]{:S(2)}, u32[]{:S(2)}) %collective-permute-start.9) | collective-permute-done | bytes 262176 | tf_op jit(solution)/shard_map/ppermute | solution.py:463
  95.2 0.1 select_select_fusion.1
  95.2 1.7 %collective-permute-start.11 = (f32[128,512]{1,0:T(8,128)S(1)}, f32[128,512]{1,0:T(8,128)S(1)}, u32[]{:S(2)}, u32[]{:S(2)}) collective-permute-start(f32[128,512]{1,0:T(8,128)S(1)} %select_select_fusion.1), channel_id=1, source_target_pairs={{1,0},{2,3},{3,1},{0,2},{5,4},{6,7},{7,5},{4,6},{9,8},{10,11},{11,... | collective-permute-start | bytes 786440 | tf_op jit(solution)/shard_map/ppermute | solution.py:477
  97.0 5.6 %product.12.refs_3_ = f32[128,1024]{1,0:T(8,128)S(1)} custom-call(s32[1]{0:T(128)} %bitcast.2.ids_ref.refs_0_, bf16[4,4,1024,256]{3,2,1,0:T(8,128)(2,1)} %get-tuple-element.22.refs_1_, f32[128,512]{1,0:T(8,128)S(1)} %carry.3.refs_2_, f32[128,512]{1,0:T(8,128)} %collective-permute-done.9.refs_3_, f32[128,512]{1,0:T(8,128)S(1)} %collective-permute-done.10.refs_4_), custom_call_target="tpu_custom_call" | custom-call | flops 17179869184 | bytes 67108864 | tf_op jit(solution)/shard_map/product/pallas_call | solution.py:360
  102.6 0.0 collective-permute-done.11.refs_2_
  102.6 3.5 %product.13 = f32[8,128,128]{2,1,0:T(8,128)} custom-call(s32[1]{0:T(128)} %bitcast.2.ids_ref.refs_0_, bf16[4,4,1024,256]{3,2,1,0:T(8,128)(2,1)} %get-tuple-element.22.refs_1_, f32[128,512]{1,0:T(8,128)S(1)} %collective-permute-done.11.refs_2_, f32[128,1024]{1,0:T(8,128)S(1)} %product.12.refs_3_), custom_call_target="tpu_custom_call" | custom-call | flops 1024 | bytes 1024 | tf_op jit(solution)/shard_map/product/pallas_call | solution.py:360
  106.1 0.5 all-to-all-done.2.own_ref.left_ref
  106.6 0.0 collective-permute-start.12
  106.6 3.6 %all-to-all-start.4 = ((f32[8,128,128]{2,1,0:T(8,128)}), f32[8,128,128]{2,1,0:T(8,128)S(1)}, u32[]{:S(2)}, u32[]{:S(2)}) async-start(f32[8,128,128]{2,1,0:T(8,128)} %product.13), calls=%async_computation.4 | async-start | bytes 1048576 | tf_op jit(solution)/shard_map/all_to_all | solution.py:467
  110.1 0.0 collective-permute-done.12.other_ref
  110.1 1.2 %assemble.1 = f32[3,256,256]{2,1,0:T(8,128)} custom-call(s32[1]{0:T(128)} %bitcast.1.row_ref, f32[8,224,128]{2,1,0:T(8,128)S(1)} %all-to-all-done.2.own_ref.left_ref, f32[8,224,128]{2,1,0:T(8,128)S(1)} %collective-permute-done.12.other_ref), custom_call_target="tpu_custom_call" | custom-call | flops 1024 | bytes 1024 | tf_op jit(solution)/shard_map/assemble/pallas_call | solution.py:447
  111.4 8.5 %all-to-all-done.4.right_ref = f32[8,128,128]{2,1,0:T(8,128)S(1)} async-done(((f32[8,128,128]{2,1,0:T(8,128)}), f32[8,128,128]{2,1,0:T(8,128)S(1)}, u32[]{:S(2)}, u32[]{:S(2)}) %all-to-all-start.4) | async-done | bytes 524320 | tf_op jit(solution)/shard_map/all_to_all | solution.py:467
  119.9 1.8 %finish.1 = f32[512,256]{1,0:T(8,128)} custom-call(s32[8]{0:T(128)S(1)} %bitcast.5, f32[256,512]{1,0:T(8,128)S(1)} %get-tuple-element.37.base_ref, f32[8,224,128]{2,1,0:T(8,128)S(1)} %all-to-all-done.2.own_ref.left_ref, f32[8,128,128]{2,1,0:T(8,128)S(1)} %all-to-all-done.4.right_ref), custom_call_target="tpu_custom_call" | custom-call | flops 1024 | bytes 1024 | tf_op jit(solution)/shard_map/finish/pallas_call | solution.py:420
Async XLA Ops:
  2.4 14.4 %collective-permute-start.1 = (f32[128,512]{1,0:T(8,128)S(1)}, f32[128,512]{1,0:T(8,128)S(1)}, u32[]{:S(2)}, u32[]{:S(2)}) collective-permute-start(f32[128,512]{1,0:T(8,128)S(1)} %get-tuple-element.20.first_ref.refs_0_), channel_id=1, source_target_pairs={{0,3},{1,0},{2,1},{3,2},{4,7},{5,4},{6,5},{7,6},{8,11},{9,8},{10,9... | collective-permute-start | bytes 786440 | tf_op jit(solution)/shard_map/ppermute | solution.py:463
  7.5 12.1 %collective-permute-start = (f32[128,512]{1,0:T(8,128)S(1)}, f32[128,512]{1,0:T(8,128)S(1)}, u32[]{:S(2)}, u32[]{:S(2)}) collective-permute-start(f32[128,512]{1,0:T(8,128)S(1)} %get-tuple-element.20.first_ref.refs_0_), channel_id=1, source_target_pairs={{0,1},{1,2},{2,3},{3,0},{4,5},{5,6},{6,7},{7,4},{8,9},{9,10},{10,1... | collective-permute-start | bytes 786440 | tf_op jit(solution)/shard_map/ppermute | solution.py:463
  12.4 19.5 %all-to-all-start = ((f32[8,192,128]{2,1,0:T(8,128)}), f32[8,192,128]{2,1,0:T(8,128)S(1)}, u32[]{:S(2)}, u32[]{:S(2)}) async-start(f32[8,192,128]{2,1,0:T(8,128)} %get-tuple-element.30), calls=%async_computation | async-start | bytes 1572864 | tf_op jit(solution)/shard_map/all_to_all | solution.py:467
  19.6 8.4 %collective-permute-start.2 = (f32[128,512]{1,0:T(8,128)S(1)}, f32[128,512]{1,0:T(8,128)S(1)}, u32[]{:S(2)}, u32[]{:S(2)}) collective-permute-start(f32[128,512]{1,0:T(8,128)S(1)} %select_select_fusion.3), channel_id=1, source_target_pairs={{1,0},{2,3},{3,1},{0,2},{5,4},{6,7},{7,5},{4,6},{9,8},{10,11},{11,... | collective-permute-start | bytes 786440 | tf_op jit(solution)/shard_map/ppermute | solution.py:477
  28.0 11.1 %collective-permute-start.4 = (f32[128,512]{1,0:T(8,128)S(1)}, f32[128,512]{1,0:T(8,128)S(1)}, u32[]{:S(2)}, u32[]{:S(2)}) collective-permute-start(f32[128,512]{1,0:T(8,128)S(1)} %get-tuple-element.27.refs_2_), channel_id=1, source_target_pairs={{0,1},{1,2},{2,3},{3,0},{4,5},{5,6},{6,7},{7,4},{8,9},{9,10},{10,1... | collective-permute-start | bytes 786440 | tf_op jit(solution)/shard_map/ppermute | solution.py:463
  29.4 12.2 %collective-permute-start.3 = (f32[128,512]{1,0:T(8,128)S(1)}, f32[128,512]{1,0:T(8,128)S(1)}, u32[]{:S(2)}, u32[]{:S(2)}) collective-permute-start(f32[128,512]{1,0:T(8,128)S(1)} %get-tuple-element.27.refs_2_), channel_id=1, source_target_pairs={{0,3},{1,0},{2,1},{3,2},{4,7},{5,4},{6,5},{7,6},{8,11},{9,8},{10,9... | collective-permute-start | bytes 786440 | tf_op jit(solution)/shard_map/ppermute | solution.py:463
  35.4 13.9 %all-to-all-start.1 = ((f32[8,128,128]{2,1,0:T(8,128)}), f32[8,128,128]{2,1,0:T(8,128)S(1)}, u32[]{:S(2)}, u32[]{:S(2)}) async-start(f32[8,128,128]{2,1,0:T(8,128)} %product.8), calls=%async_computation.1 | async-start | bytes 1048576 | tf_op jit(solution)/shard_map/all_to_all | solution.py:467
  41.6 7.7 %copy-start = (s32[1,8,1]{1,2,0:T(1,128)S(1)}, s32[1,8,1]{1,2,0:T(1,128)}, u32[]{:S(2)}) copy-start(s32[1,8,1]{1,2,0:T(1,128)} %param.20) | copy-start | bytes 100
  41.6 7.6 %collective-permute-start.5 = (f32[128,512]{1,0:T(8,128)S(1)}, f32[128,512]{1,0:T(8,128)S(1)}, u32[]{:S(2)}, u32[]{:S(2)}) collective-permute-start(f32[128,512]{1,0:T(8,128)S(1)} %select_select_fusion.2), channel_id=1, source_target_pairs={{1,0},{2,3},{3,1},{0,2},{5,4},{6,7},{7,5},{4,6},{9,8},{10,11},{11,... | collective-permute-start | bytes 786440 | tf_op jit(solution)/shard_map/ppermute | solution.py:477
  50.8 13.2 %collective-permute-start.7 = (f32[176,512]{1,0:T(8,128)S(1)}, f32[176,512]{1,0:T(8,128)S(1)}, u32[]{:S(2)}, u32[]{:S(2)}) collective-permute-start(f32[176,512]{1,0:T(8,128)S(1)} %carry.2.refs_2_.refs_4_), channel_id=1, source_target_pairs={{0,1},{1,2},{2,3},{3,0},{4,5},{5,6},{6,7},{7,4},{8,9},{9,10},{10,1... | collective-permute-start | bytes 1081352 | tf_op jit(solution)/shard_map/ppermute | solution.py:463
  53.5 15.7 %collective-permute-start.6 = (f32[176,512]{1,0:T(8,128)S(1)}, f32[176,512]{1,0:T(8,128)S(1)}, u32[]{:S(2)}, u32[]{:S(2)}) collective-permute-start(f32[176,512]{1,0:T(8,128)S(1)} %carry.2.refs_2_.refs_4_), channel_id=1, source_target_pairs={{0,3},{1,0},{2,1},{3,2},{4,7},{5,4},{6,5},{7,6},{8,11},{9,8},{10,9... | collective-permute-start | bytes 1081352 | tf_op jit(solution)/shard_map/ppermute | solution.py:463
  58.2 21.6 %all-to-all-start.3 = ((f32[8,128,128]{2,1,0:T(8,128)}), f32[8,128,128]{2,1,0:T(8,128)S(1)}, u32[]{:S(2)}, u32[]{:S(2)}) async-start(f32[8,128,128]{2,1,0:T(8,128)} %product.11), calls=%async_computation.3 | async-start | bytes 1048576 | tf_op jit(solution)/shard_map/all_to_all | solution.py:467
  69.2 10.5 %collective-permute-start.8 = (f32[176,512]{1,0:T(8,128)S(1)}, f32[176,512]{1,0:T(8,128)S(1)}, u32[]{:S(2)}, u32[]{:S(2)}) collective-permute-start(f32[176,512]{1,0:T(8,128)S(1)} %select_select_fusion), channel_id=1, source_target_pairs={{1,0},{2,3},{3,1},{0,2},{5,4},{6,7},{7,5},{4,6},{9,8},{10,11},{11,... | collective-permute-start | bytes 1081352 | tf_op jit(solution)/shard_map/ppermute | solution.py:477
  81.3 11.2 %collective-permute-start.10 = (f32[128,512]{1,0:T(8,128)S(1)}, f32[128,512]{1,0:T(8,128)S(1)}, u32[]{:S(2)}, u32[]{:S(2)}) collective-permute-start(f32[128,512]{1,0:T(8,128)S(1)} %carry.3.refs_2_), channel_id=1, source_target_pairs={{0,1},{1,2},{2,3},{3,0},{4,5},{5,6},{6,7},{7,4},{8,9},{9,10},{10,1... | collective-permute-start | bytes 786440 | tf_op jit(solution)/shard_map/ppermute | solution.py:463
  82.9 12.3 %collective-permute-start.9 = (f32[128,512]{1,0:T(8,128)S(1)}, f32[128,512]{1,0:T(8,128)}, u32[]{:S(2)}, u32[]{:S(2)}) collective-permute-start(f32[128,512]{1,0:T(8,128)S(1)} %carry.3.refs_2_), channel_id=1, source_target_pairs={{0,3},{1,0},{2,1},{3,2},{4,7},{5,4},{6,5},{7,6},{8,11},{9,8},{10,9... | collective-permute-start | bytes 786440 | tf_op jit(solution)/shard_map/ppermute | solution.py:463
  88.7 17.9 %all-to-all-start.2 = ((f32[8,224,128]{2,1,0:T(8,128)}), f32[8,224,128]{2,1,0:T(8,128)S(1)}, u32[]{:S(2)}, u32[]{:S(2)}) async-start(f32[8,224,128]{2,1,0:T(8,128)} %product.10), calls=%async_computation.2 | async-start | bytes 1835008 | tf_op jit(solution)/shard_map/all_to_all | solution.py:467
  95.2 7.4 %collective-permute-start.11 = (f32[128,512]{1,0:T(8,128)S(1)}, f32[128,512]{1,0:T(8,128)S(1)}, u32[]{:S(2)}, u32[]{:S(2)}) collective-permute-start(f32[128,512]{1,0:T(8,128)S(1)} %select_select_fusion.1), channel_id=1, source_target_pairs={{1,0},{2,3},{3,1},{0,2},{5,4},{6,7},{7,5},{4,6},{9,8},{10,11},{11,... | collective-permute-start | bytes 786440 | tf_op jit(solution)/shard_map/ppermute | solution.py:477
  106.6 3.6 %collective-permute-start.12 = (f32[8,224,128]{2,1,0:T(8,128)S(1)}, f32[8,224,128]{2,1,0:T(8,128)S(1)}, u32[]{:S(2)}, u32[]{:S(2)}) collective-permute-start(f32[8,224,128]{2,1,0:T(8,128)S(1)} %all-to-all-done.2.own_ref.left_ref), channel_id=1, source_target_pairs={{0,4},{4,0},{8,12},{12,8},{16,20},{20,16},{24,28},{28,24},{1,5},{5... | collective-permute-start | bytes 2752520 | tf_op jit(solution)/shard_map/ppermute | solution.py:560
  106.6 13.3 %all-to-all-start.4 = ((f32[8,128,128]{2,1,0:T(8,128)}), f32[8,128,128]{2,1,0:T(8,128)S(1)}, u32[]{:S(2)}, u32[]{:S(2)}) async-start(f32[8,128,128]{2,1,0:T(8,128)} %product.13), calls=%async_computation.4 | async-start | bytes 1048576 | tf_op jit(solution)/shard_map/all_to_all | solution.py:467

commit v16 on v15

--- a/solution.py
+++ b/solution.py
@@ -148,8 +148,13 @@
 
 
 def stacked(field):
-    high, low = split(field)
-    return jnp.concatenate([jnp.concatenate([x, x], axis=1) for x in (high, low)], axis=0)
+    return jnp.concatenate(split(field), axis=0)
+
+
+def times(left, part):
+    by_high = jnp.dot(left, part[:NODES_DEV, :], preferred_element_type=F32)
+    by_low = jnp.dot(left[:H], part[NODES_DEV:, :], preferred_element_type=F32)
+    return by_high[:H] + (by_high[H:] + by_low)
 
 
 def operator_kernel(n_row, n_col, origins, ids_ref, live_ref, rows_hbm, slots_hbm, values_ref, *refs):
@@ -241,8 +246,7 @@
             field_copies[k].wait()
             left = stacked(held[k])
             for p in range(pairs):
-                part = jnp.dot(left, buf[origin % 2, p], preferred_element_type=F32)
-                summed = part[:H] + part[H:]
+                summed = times(left, buf.at[origin % 2, p])
                 here = slice(p * WIDE, (p + 1) * WIDE)
                 total_ref[:, here] = summed if origin == 0 else total_ref[:, here] + summed
     for origin in range(n_col - 2, n_col):
@@ -280,14 +284,18 @@
     )(ids, live, *in_hbm(rows, slots, values), *fields)
 
 
-def product_kernel(n_row, n_col, origins, has_prev, last, n_carriers, *refs):
+def product_kernel(n_row, n_col, origins, has_prev, last, n_carriers, has_base, *refs):
     n = len(origins)
     ids_ref, op_ref, refs = refs[0], refs[1], refs[2:]
     fields, refs = refs[:n], refs[n:]
     if has_prev:
-        prev, refs = refs[0], refs[1:]
+        prev_hbm, refs = refs[0], refs[1:]
     carriers, refs = refs[:n_carriers], refs[n_carriers:]
-    out_ref, held, buf, field_sems, sems, out, out_sems = refs[:7]
+    if has_base:
+        base_hbm, out_ref, base_ref, refs = refs[0], refs[1], refs[2], refs[3:]
+    else:
+        out_ref, refs = refs[0], refs[1:]
+    held, buf, field_sems, sems, out, out_sems, prev, other_sems = refs[:8]
     order = [(k, p) for p in range(n_row // 2) for k in range(n)]
 
     def copy(k, p):
@@ -296,12 +304,16 @@
     field_copies = fetch([x.at[pl.ds(0, H)] for x in fields], [held.at[k] for k in range(n)], field_sems)
     for k, p in order[:DEPTH]:
         copy(k, p).start()
+    if has_prev:
+        (prev_copy,) = fetch([prev_hbm], [prev], other_sems.at[pl.ds(0, 1)])
+    if has_base:
+        (base_copy,) = fetch([base_hbm], [base_ref], other_sems.at[pl.ds(1, 1)])
     left = []
     for k in range(n):
         field_copies[k].wait()
         left.append(stacked(held[k]))
     if n_carriers:
-        ordered = refs[7]
+        ordered = refs[8]
         for k in range(n_col):
             ordered[lax.rem(ids_ref[0] + k, n_col)] = carriers[k][H:, :]
         share = ordered[0]
@@ -322,46 +334,53 @@
             ahead = p * n + k + DEPTH
             if ahead < len(order):
                 copy(*order[ahead]).start()
-            part = jnp.dot(left[k], buf[k, p], preferred_element_type=F32)
+            part = times(left[k], buf.at[k, p])
             total = part if total is None else total + part
-        summed = total[:H] + total[H:]
         if has_prev:
-            summed = summed + prev[:, here]
+            if p == 0:
+                prev_copy.wait()
+            total = total + prev[:, here]
         if last:
-            out[2 * p, :H, :] = summed[:, :TB]
-            out[2 * p + 1, :H, :] = summed[:, TB:]
-            both = pl.ds(2 * p, 2)
-            sent.append(pltpu.make_async_copy(out.at[both], out_ref.at[both], out_sems.at[p]))
-            sent[-1].start()
+            out[2 * p, :H, :] = total[:, :TB]
+            out[2 * p + 1, :H, :] = total[:, TB:]
+            place = pl.ds(2 * p, 2)
+            sent.append(pltpu.make_async_copy(out.at[place], out_ref.at[place], out_sems.at[p]))
         else:
-            out_ref[:, here] = summed
+            out[:, here] = total
+            place = (pl.ds(0, H), pl.ds(p * WIDE, WIDE))
+            sent.append(pltpu.make_async_copy(out.at[place], out_ref.at[place], out_sems.at[p]))
+        sent[-1].start()
+    if has_base:
+        base_copy.wait()
     for item in sent:
         item.wait()
 
 
-def product(n_row, n_col, ids, origins, operator, fields, prev, last, carriers=()):
+def product(n_row, n_col, ids, origins, operator, fields, prev, last, carriers=(), base=None, prev_near=False):
     n = len(origins)
     has_prev = prev is not None
-    share = 0
+    has_base = base is not None
+    rows = carriers[0].shape[0] - H if carriers else 0
+    under = rows * NODES_DEV // LANES // 2
+    shape = (n_row, H + under, TB) if last else (H, n_row * TB)
     scratch = [
         pltpu.VMEM((n, H, NODES_DEV), F32),
         pltpu.VMEM((n, n_row // 2, 2 * NODES_DEV, WIDE), BF16),
         pltpu.SemaphoreType.DMA((n,)),
         pltpu.SemaphoreType.DMA((n, n_row // 2)),
+        pltpu.VMEM(shape, F32),
+        pltpu.SemaphoreType.DMA((n_row // 2,)),
+        pltpu.VMEM((H, n_row * TB) if has_prev else (8, LANES), F32),
+        pltpu.SemaphoreType.DMA((2,)),
     ]
     if carriers:
-        rows = carriers[0].shape[0] - H
-        share = rows * NODES_DEV // LANES // 2
-    scratch += [pltpu.VMEM((n_row, H + share, TB) if last else (8, LANES), F32), pltpu.SemaphoreType.DMA((n_row // 2,))]
-    if carriers:
         scratch.append(pltpu.VMEM((n_col, rows, NODES_DEV), F32))
-    shape = (n_row, H + share, TB) if last else (H, n_row * TB)
-    count = has_prev + len(carriers)
+    out = pltpu.HBM(shape, F32)
     return pl.pallas_call(
-        functools.partial(product_kernel, n_row, n_col, origins, has_prev, last, len(carriers)),
-        in_specs=[SMEM, HBM] + [ANY] * n + [VMEM] * count,
-        out_specs=HBM if last else VMEM,
-        out_shape=(pltpu.HBM if last else jax.ShapeDtypeStruct)(shape, F32),
+        functools.partial(product_kernel, n_row, n_col, origins, has_prev, last, len(carriers), has_base),
+        in_specs=[SMEM, HBM] + [ANY] * (n + has_prev) + [VMEM] * len(carriers) + [HBM] * has_base,
+        out_specs=[HBM, VMEM] if has_base else HBM,
+        out_shape=[out, jax.ShapeDtypeStruct(base.shape, F32)] if has_base else out,
         scratch_shapes=scratch,
         compiler_params=params(48),
         cost_estimate=LIGHT if last else HEAVY,
@@ -370,18 +389,18 @@
         ids,
         *in_hbm(operator),
         *fields,
-        *((prev,) if has_prev else ()),
+        *((prev,) if prev_near else in_hbm(prev) if has_prev else ()),
         *carriers,
+        *(in_hbm(base) if has_base else ()),
     )
 
 
-def carry_kernel(n_row, rows, owners_ref, base_hbm, came_ref, *refs):
-    out_ref, base, sems = refs[-3:]
-    (base_copy,) = fetch([base_hbm], [base], sems)
-    out_ref[:H, :] = jnp.zeros((H, NODES_DEV), F32)
+def carry_kernel(n_row, rows, owners_ref, base_ref, came_ref, *refs):
+    out_ref = refs[-1]
+    out_ref[:H, :] = base_ref[...]
     for q in range(n_row):
         here = pl.ds(pl.multiple_of(owners_ref[q] * TB, TB), TB)
-        out_ref[:H, here] += came_ref[q]
+        out_ref[:H, here] += 2.0 * came_ref[q]
     if rows:
         pieces_ref = refs[0]
         share = pieces_ref[0]
@@ -389,22 +408,19 @@
             share = share + pieces_ref[q]
         for j in range(NODES_DEV // LANES):
             out_ref[H:, j * LANES : (j + 1) * LANES] = share[j * rows : (j + 1) * rows, :]
-    base_copy.wait()
-    out_ref[:H, :] = base[...] + 2.0 * out_ref[:H, :]
 
 
 def carry(n_row, owners, base, came, *pieces):
     rows = pieces[0].shape[1] * LANES // NODES_DEV if pieces else 0
     return pl.pallas_call(
         functools.partial(carry_kernel, n_row, rows),
-        in_specs=[SMEM, HBM] + [VMEM] * (1 + len(pieces)),
+        in_specs=[SMEM] + [VMEM] * (2 + len(pieces)),
         out_specs=VMEM,
         out_shape=jax.ShapeDtypeStruct((H + rows, NODES_DEV), F32),
-        scratch_shapes=[pltpu.VMEM((H, NODES_DEV), F32), pltpu.SemaphoreType.DMA((1,))],
         compiler_params=params(24),
         cost_estimate=LIGHT,
         name="carry",
-    )(owners, *in_hbm(base), came, *pieces)
+    )(owners, base, came, *pieces)
 
 
 def finish_kernel(n_row, owners_ref, base_ref, left_ref, right_ref, out_ref, total):
@@ -497,18 +513,19 @@
     return steps
 
 
-def early(n_row, n_col, ids, operator, steps, total=None, done=0):
+def early(n_row, n_col, ids, operator, steps, total=None, done=0, base=None):
     pairs = [pair for step in steps[:-1] for pair in step][done:]
     for begin in range(0, len(pairs), 3):
         origins, fields = zip(*pairs[begin : begin + 3])
-        total = product(n_row, n_col, ids, origins, operator, fields, total, False)
+        brought = base if begin + 3 >= len(pairs) else None
+        total = product(n_row, n_col, ids, origins, operator, fields, total, False, base=brought)
     return total
 
 
-def final(n_row, n_col, ids, operator, steps, total, carrying=False):
+def final(n_row, n_col, ids, operator, steps, total, carrying=False, near=False):
     origins, fields = zip(*steps[-1])
     carriers = [x for _, x in sorted((p for step in steps for p in step), key=lambda p: p[0])] if carrying else ()
-    return product(n_row, n_col, ids, origins, operator, fields, total, True, carriers)
+    return product(n_row, n_col, ids, origins, operator, fields, total, True, carriers, prev_near=near)
 
 
 def per_device(
@@ -542,13 +559,13 @@
 
     left_early = early(*common, steps, left_early, len(first))
     right_steps = gather(n_col, after(right, left_early, steps[-1][0][1]), -1)
-    left_came = exchange(final(*common, steps, after(left_early, pieces)))
-    right_early = early(*common, right_steps)
+    left_came = exchange(final(*common, steps, after(left_early, pieces), near=len(steps) == 3))
+    right_early, one_left = early(*common, right_steps, base=one_left)
 
     left_carried = carry(n_row, owners, after(one_left, right_early, right_steps[-1][0][1]), left_came, pieces)
     steps = gather(n_col, left_carried, 1)
     right_came = exchange(final(*common, right_steps, right_early))
-    left_early = early(*common, steps)
+    left_early, one_right = early(*common, steps, base=one_right)
 
     right_carried = carry(n_row, owners, after(one_right, left_early, steps[-1][0][1]), right_came)
     right_steps = gather(n_col, right_carried, -1)

time: 123 us -> 121 us (0.984)
  Pallas kernels: 51 us -> 48.5 us
    pallas_call x2, Pallas kernels: 3.06 us -> 1.35 us  [carry(): pl.pallas_call(functools.partial(carry_kernel, n_row, rows), in_specs=[SM...]
  transfers between devices with their start and end apart: 18 -> 18, of which waited for: 9 -> 10; matrix products, arithmetic and copies ran while one was open for 0% -> 0% of each run, Pallas kernels for 37% -> 37%
where the time goes in v16:
time: 121 us; the launch traced here: 120 us
  Pallas kernels  48.5 us (40%)
  starting transfers between devices  40.2 us (33%)
  waiting for transfers between devices  29.1 us (24%)
  between operations  1.45 us (1%)
    pallas_call x7, Pallas kernels, product(): pl.pallas_call(functools.partial(product_kernel, n_row, n_col, origins, h...  30.3 us
    all_to_all x5, starting transfers between devices, exchange(): lax.all_to_all(pieces, 'row', split_axis=0, concat_axis=0, tiled=True)  18.7 us
    ppermute x8, starting transfers between devices, shift(): lax.ppermute(x, 'col', [(c, (c + step) % n_col) for c in range(n_col)])  16.7 us
    ppermute x8, waiting for transfers between devices, shift(): lax.ppermute(x, 'col', [(c, (c + step) % n_col) for c in range(n_col)])  15.1 us
    all_to_all x5, waiting for transfers between devices, exchange(): lax.all_to_all(pieces, 'row', split_axis=0, concat_axis=0, tiled=True)  9.19 us
    pallas_call x1, Pallas kernels, build_operator(): pl.pallas_call(functools.partial(operator_kernel, n_row, n_col, origins),...  7.29 us
    pallas_call x1, Pallas kernels, local_terms(): pl.pallas_call(functools.partial(local_kernel, n_row), in_specs=[ANY] + [...  4.88 us
    ppermute x4, waiting for transfers between devices, opposite(): return lax.ppermute(sent, 'col', [(1, 0), (2, 3), (3, 1), (0, 2)])  4.88 us
  transfers between devices with their start and end apart: 18, of which 10 were waited for; matrix products, arithmetic and copies ran while one was open for 0% of the time, Pallas kernels for 37%

profile of v16, /device:TPU:0, one launch (start us, length us, event | category | flops | bytes accessed | tf_op | source)
XLA Modules:
  0.0 119.6 jit_solution(18051461361219572298)
XLA Ops:
  0.6 1.7 %term_two.1 = (f32[128,512]{1,0:T(8,128)S(1)}, f32[128,512]{1,0:T(8,128)S(1)}) custom-call(f32[512,256]{1,0:T(8,128)} %grad_hbm.3, s32[512,256]{1,0:T(8,128)} %mask_hbm.3, f32[3,256,256]{2,1,0:T(8,128)} %weight_hbm.3), custom_call_target="tpu_custom_call" | custom-call | flops 1024 | bytes 1024 | tf_op jit(solution)/shard_map/term_two/pallas_call | solution.py:78
  2.4 5.1 %collective-permute-start.1 = (f32[128,512]{1,0:T(8,128)S(1)}, f32[128,512]{1,0:T(8,128)S(1)}, u32[]{:S(2)}, u32[]{:S(2)}) collective-permute-start(f32[128,512]{1,0:T(8,128)S(1)} %get-tuple-element.24.first_ref.refs_0_), channel_id=1, source_target_pairs={{0,3},{1,0},{2,1},{3,2},{4,7},{5,4},{6,5},{7,6},{8,11},{9,8},{10,9... | collective-permute-start | bytes 786440 | tf_op jit(solution)/shard_map/ppermute | solution.py:479
  7.5 0.0 collective-permute-start
  7.5 4.9 %local_terms.1 = (f32[128,512]{1,0:T(8,128)}, f32[128,512]{1,0:T(8,128)}, f32[256,512]{1,0:T(8,128)S(1)}, f32[8,192,128]{2,1,0:T(8,128)}) custom-call(f32[128,512]{1,0:T(8,128)S(1)} %get-tuple-element.24.first_ref.refs_0_, f32[512,256]{1,0:T(8,128)} %grad_hbm.3, s32[512,256]{1,0:T(8,128)} %mask_hbm.3, f32[3,256,256]{2,1,0:T(8,128)} %weight_hbm.3, ...), custom_call_target="tpu_custom_call" | custom-call | flops 1024 | bytes 1024 | tf_op jit(solution)/shard_map/local_terms/pallas_call | solution.py:125
  12.4 3.7 %all-to-all-start = ((f32[8,192,128]{2,1,0:T(8,128)}), f32[8,192,128]{2,1,0:T(8,128)S(1)}, u32[]{:S(2)}, u32[]{:S(2)}) async-start(f32[8,192,128]{2,1,0:T(8,128)} %get-tuple-element.36), calls=%async_computation | async-start | bytes 1572864 | tf_op jit(solution)/shard_map/all_to_all | solution.py:483
  16.8 0.0 collective-permute-done.1.refs_2_
  16.8 2.8 %collective-permute-done.refs_1_ = f32[128,512]{1,0:T(8,128)S(1)} collective-permute-done((f32[128,512]{1,0:T(8,128)S(1)}, f32[128,512]{1,0:T(8,128)S(1)}, u32[]{:S(2)}, u32[]{:S(2)}) %collective-permute-start) | collective-permute-done | bytes 262176 | tf_op jit(solution)/shard_map/ppermute | solution.py:479
  19.6 0.1 select_select_fusion.3
  19.6 0.8 collective-permute-start.2
  20.4 7.3 %operator.1 = (bf16[4,4,1024,256]{3,2,1,0:T(8,128)(2,1)}, f32[128,1024]{1,0:T(8,128)S(1)}) custom-call(s32[1]{0:T(128)} %bitcast.2.ids_ref.refs_0_, s32[1]{0:T(128)S(6)} %copy.13.live_ref, s32[1,128]{1,0:T(1,128)} %rows_hbm.1, s32[1,128]{1,0:T(1,128)} %slots_hbm.1, f32[1,128,128,128]{3,2,1,0:T(8,128)} %values_ref.1, ...), custom_call_target="tpu_custom_call" | custom-call | flops 17179869184 | bytes 67108864 | tf_op jit(solution)/shard_map/operator/pallas_call | solution.py:262
  27.7 0.0 collective-permute-done.2.refs_2_
  27.7 1.7 %collective-permute-start.4 = (f32[128,512]{1,0:T(8,128)S(1)}, f32[128,512]{1,0:T(8,128)S(1)}, u32[]{:S(2)}, u32[]{:S(2)}) collective-permute-start(f32[128,512]{1,0:T(8,128)S(1)} %get-tuple-element.30.refs_2_), channel_id=1, source_target_pairs={{0,1},{1,2},{2,3},{3,0},{4,5},{5,6},{6,7},{7,4},{8,9},{9,10},{10,1... | collective-permute-start | bytes 786440 | tf_op jit(solution)/shard_map/ppermute | solution.py:479
  29.4 2.2 %collective-permute-start.3 = (f32[128,512]{1,0:T(8,128)S(1)}, f32[128,512]{1,0:T(8,128)S(1)}, u32[]{:S(2)}, u32[]{:S(2)}) collective-permute-start(f32[128,512]{1,0:T(8,128)S(1)} %get-tuple-element.30.refs_2_), channel_id=1, source_target_pairs={{0,3},{1,0},{2,1},{3,2},{4,7},{5,4},{6,5},{7,6},{8,11},{9,8},{10,9... | collective-permute-start | bytes 786440 | tf_op jit(solution)/shard_map/ppermute | solution.py:479
  31.6 0.0 all-to-all-done.refs_0_
  31.6 3.2 %product.8 = f32[8,128,128]{2,1,0:T(8,128)} custom-call(s32[1]{0:T(128)} %bitcast.2.ids_ref.refs_0_, bf16[4,4,1024,256]{3,2,1,0:T(8,128)(2,1)} %get-tuple-element.26.refs_1_, f32[128,512]{1,0:T(8,128)S(1)} %collective-permute-done.2.refs_2_, f32[128,1024]{1,0:T(8,128)S(1)} %get-tuple-element.37.refs_3_), custom_call_target="tpu_custom_call" | custom-call | flops 1024 | bytes 1024 | tf_op jit(solution)/shard_map/product/pallas_call | solution.py:379
  34.9 3.7 %all-to-all-start.1 = ((f32[8,128,128]{2,1,0:T(8,128)}), f32[8,128,128]{2,1,0:T(8,128)S(1)}, u32[]{:S(2)}, u32[]{:S(2)}) async-start(f32[8,128,128]{2,1,0:T(8,128)} %product.8), calls=%async_computation.1 | async-start | bytes 1048576 | tf_op jit(solution)/shard_map/all_to_all | solution.py:483
  38.6 0.2 collective-permute-done.4.refs_4_
  38.8 2.5 %collective-permute-done.3.refs_3_ = f32[128,512]{1,0:T(8,128)S(1)} collective-permute-done((f32[128,512]{1,0:T(8,128)S(1)}, f32[128,512]{1,0:T(8,128)S(1)}, u32[]{:S(2)}, u32[]{:S(2)}) %collective-permute-start.3) | collective-permute-done | bytes 262176 | tf_op jit(solution)/shard_map/ppermute | solution.py:479
  41.3 0.1 select_select_fusion.2
  41.4 1.5 %collective-permute-start.5 = (f32[128,512]{1,0:T(8,128)S(1)}, f32[128,512]{1,0:T(8,128)S(1)}, u32[]{:S(2)}, u32[]{:S(2)}) collective-permute-start(f32[128,512]{1,0:T(8,128)S(1)} %select_select_fusion.2), channel_id=1, source_target_pairs={{1,0},{2,3},{3,1},{0,2},{5,4},{6,7},{7,5},{4,6},{9,8},{10,11},{11,... | collective-permute-start | bytes 786440 | tf_op jit(solution)/shard_map/ppermute | solution.py:493
  42.8 0.0 copy-start
  42.8 5.5 %product.7 = (f32[128,1024]{1,0:T(8,128)}, f32[128,512]{1,0:T(8,128)S(1)}) custom-call(s32[1]{0:T(128)} %bitcast.2.ids_ref.refs_0_, bf16[4,4,1024,256]{3,2,1,0:T(8,128)(2,1)} %get-tuple-element.26.refs_1_, f32[128,512]{1,0:T(8,128)S(1)} %get-tuple-element.30.refs_2_, f32[128,512]{1,0:T(8,128)S(1)} %collective-permute-done.3.refs_3_, ...), custom_call_target="tpu_custom_call" | custom-call | flops 17179869184 | bytes 67108864 | tf_op jit(solution)/shard_map/product/pallas_call | solution.py:379
  48.3 0.7 collective-permute-done.5.refs_2_
  49.0 0.0 all-to-all-done.1.came_ref
  49.0 0.0 copy-done
  49.0 0.7 carry.2.refs_2_.refs_4_
  49.7 2.7 %collective-permute-start.7 = (f32[176,512]{1,0:T(8,128)S(1)}, f32[176,512]{1,0:T(8,128)S(1)}, u32[]{:S(2)}, u32[]{:S(2)}) collective-permute-start(f32[176,512]{1,0:T(8,128)S(1)} %carry.2.refs_2_.refs_4_), channel_id=1, source_target_pairs={{0,1},{1,2},{2,3},{3,0},{4,5},{5,6},{6,7},{7,4},{8,9},{9,10},{10,1... | collective-permute-start | bytes 1081352 | tf_op jit(solution)/shard_map/ppermute | solution.py:479
  52.4 1.2 collective-permute-start.6
  53.6 3.5 %product.11 = f32[8,128,128]{2,1,0:T(8,128)} custom-call(s32[1]{0:T(128)} %bitcast.2.ids_ref.refs_0_, bf16[4,4,1024,256]{3,2,1,0:T(8,128)(2,1)} %get-tuple-element.26.refs_1_, f32[128,512]{1,0:T(8,128)S(1)} %collective-permute-done.5.refs_2_, f32[128,1024]{1,0:T(8,128)} %get-tuple-element.33.refs_3_), custom_call_target="tpu_custom_call" | custom-call | flops 1024 | bytes 1024 | tf_op jit(solution)/shard_map/product/pallas_call | solution.py:379
  57.1 3.8 %all-to-all-start.3 = ((f32[8,128,128]{2,1,0:T(8,128)}), f32[8,128,128]{2,1,0:T(8,128)S(1)}, u32[]{:S(2)}, u32[]{:S(2)}) async-start(f32[8,128,128]{2,1,0:T(8,128)} %product.11), calls=%async_computation.3 | async-start | bytes 1048576 | tf_op jit(solution)/shard_map/all_to_all | solution.py:483
  60.9 2.0 %collective-permute-done.7.refs_3_.refs_7_ = f32[176,512]{1,0:T(8,128)S(1)} collective-permute-done((f32[176,512]{1,0:T(8,128)S(1)}, f32[176,512]{1,0:T(8,128)S(1)}, u32[]{:S(2)}, u32[]{:S(2)}) %collective-permute-start.7) | collective-permute-done | bytes 360480 | tf_op jit(solution)/shard_map/ppermute | solution.py:479
  62.9 5.1 %collective-permute-done.6.refs_4_.refs_5_ = f32[176,512]{1,0:T(8,128)S(1)} collective-permute-done((f32[176,512]{1,0:T(8,128)S(1)}, f32[176,512]{1,0:T(8,128)S(1)}, u32[]{:S(2)}, u32[]{:S(2)}) %collective-permute-start.6) | collective-permute-done | bytes 360480 | tf_op jit(solution)/shard_map/ppermute | solution.py:479
  68.1 0.1 select_select_fusion
  68.1 0.8 collective-permute-start.8
  69.0 5.5 %product.9 = (f32[128,1024]{1,0:T(8,128)}, f32[128,512]{1,0:T(8,128)S(1)}) custom-call(s32[1]{0:T(128)} %bitcast.2.ids_ref.refs_0_, bf16[4,4,1024,256]{3,2,1,0:T(8,128)(2,1)} %get-tuple-element.26.refs_1_, f32[176,512]{1,0:T(8,128)S(1)} %carry.2.refs_2_.refs_4_, f32[176,512]{1,0:T(8,128)S(1)} %collective-permute-done.7.refs_3_.refs_7_, ...), custom_call_target="tpu_custom_call" | custom-call | flops 17179869184 | bytes 67108864 | tf_op jit(solution)/shard_map/product/pallas_call | solution.py:379
  74.5 4.2 %collective-permute-done.8.refs_2_.refs_6_ = f32[176,512]{1,0:T(8,128)S(1)} collective-permute-done((f32[176,512]{1,0:T(8,128)S(1)}, f32[176,512]{1,0:T(8,128)S(1)}, u32[]{:S(2)}, u32[]{:S(2)}) %collective-permute-start.8) | collective-permute-done | bytes 360480 | tf_op jit(solution)/shard_map/ppermute | solution.py:493
  78.7 0.0 all-to-all-done.3.came_ref
  78.7 0.7 carry.3.refs_2_
  79.3 1.5 %collective-permute-start.10 = (f32[128,512]{1,0:T(8,128)S(1)}, f32[128,512]{1,0:T(8,128)S(1)}, u32[]{:S(2)}, u32[]{:S(2)}) collective-permute-start(f32[128,512]{1,0:T(8,128)S(1)} %carry.3.refs_2_), channel_id=1, source_target_pairs={{0,1},{1,2},{2,3},{3,0},{4,5},{5,6},{6,7},{7,4},{8,9},{9,10},{10,1... | collective-permute-start | bytes 786440 | tf_op jit(solution)/shard_map/ppermute | solution.py:479
  80.9 2.3 %collective-permute-start.9 = (f32[128,512]{1,0:T(8,128)S(1)}, f32[128,512]{1,0:T(8,128)S(1)}, u32[]{:S(2)}, u32[]{:S(2)}) collective-permute-start(f32[128,512]{1,0:T(8,128)S(1)} %carry.3.refs_2_), channel_id=1, source_target_pairs={{0,3},{1,0},{2,1},{3,2},{4,7},{5,4},{6,5},{7,6},{8,11},{9,8},{10,9... | collective-permute-start | bytes 786440 | tf_op jit(solution)/shard_map/ppermute | solution.py:479
  83.2 3.5 %product.10 = f32[8,224,128]{2,1,0:T(8,128)} custom-call(s32[1]{0:T(128)} %bitcast.2.ids_ref.refs_0_, bf16[4,4,1024,256]{3,2,1,0:T(8,128)(2,1)} %get-tuple-element.26.refs_1_, f32[176,512]{1,0:T(8,128)S(1)} %collective-permute-done.8.refs_2_.refs_6_, f32[128,1024]{1,0:T(8,128)} %get-tuple-element.40.refs_3_, f32[176,512]{1,0:T(8,128)S(1)} %carry.2.refs_2_.refs_4_, ...), custom_call_target="tpu_custom_call" | custom-call | flops 1024 | bytes 1024 | tf_op jit(solution)/shard_map/product/pallas_call | solution.py:379
  86.8 3.9 %all-to-all-start.2 = ((f32[8,224,128]{2,1,0:T(8,128)}), f32[8,224,128]{2,1,0:T(8,128)S(1)}, u32[]{:S(2)}, u32[]{:S(2)}) async-start(f32[8,224,128]{2,1,0:T(8,128)} %product.10), calls=%async_computation.2 | async-start | bytes 1835008 | tf_op jit(solution)/shard_map/all_to_all | solution.py:483
  90.6 0.0 collective-permute-done.10.refs_4_
  90.6 2.4 %collective-permute-done.9.refs_3_ = f32[128,512]{1,0:T(8,128)S(1)} collective-permute-done((f32[128,512]{1,0:T(8,128)S(1)}, f32[128,512]{1,0:T(8,128)S(1)}, u32[]{:S(2)}, u32[]{:S(2)}) %collective-permute-start.9) | collective-permute-done | bytes 262176 | tf_op jit(solution)/shard_map/ppermute | solution.py:479
  93.1 0.1 select_select_fusion.1
  93.1 1.7 %collective-permute-start.11 = (f32[128,512]{1,0:T(8,128)S(1)}, f32[128,512]{1,0:T(8,128)S(1)}, u32[]{:S(2)}, u32[]{:S(2)}) collective-permute-start(f32[128,512]{1,0:T(8,128)S(1)} %select_select_fusion.1), channel_id=1, source_target_pairs={{1,0},{2,3},{3,1},{0,2},{5,4},{6,7},{7,5},{4,6},{9,8},{10,11},{11,... | collective-permute-start | bytes 786440 | tf_op jit(solution)/shard_map/ppermute | solution.py:493
  94.9 5.5 %product.12.refs_3_ = f32[128,1024]{1,0:T(8,128)} custom-call(s32[1]{0:T(128)} %bitcast.2.ids_ref.refs_0_, bf16[4,4,1024,256]{3,2,1,0:T(8,128)(2,1)} %get-tuple-element.26.refs_1_, f32[128,512]{1,0:T(8,128)S(1)} %carry.3.refs_2_, f32[128,512]{1,0:T(8,128)S(1)} %collective-permute-done.9.refs_3_, f32[128,512]{1,0:T(8,128)S(1)} %collective-permute-done.10.refs_4_), custom_call_target="tpu_custom_call" | custom-call | flops 17179869184 | bytes 67108864 | tf_op jit(solution)/shard_map/product/pallas_call | solution.py:379
  100.3 0.0 collective-permute-done.11.refs_2_
  100.4 3.5 %product.13 = f32[8,128,128]{2,1,0:T(8,128)} custom-call(s32[1]{0:T(128)} %bitcast.2.ids_ref.refs_0_, bf16[4,4,1024,256]{3,2,1,0:T(8,128)(2,1)} %get-tuple-element.26.refs_1_, f32[128,512]{1,0:T(8,128)S(1)} %collective-permute-done.11.refs_2_, f32[128,1024]{1,0:T(8,128)} %product.12.refs_3_), custom_call_target="tpu_custom_call" | custom-call | flops 1024 | bytes 1024 | tf_op jit(solution)/shard_map/product/pallas_call | solution.py:379
  103.9 0.8 all-to-all-done.2.own_ref.left_ref
  104.6 0.0 collective-permute-start.12
  104.6 3.5 %all-to-all-start.4 = ((f32[8,128,128]{2,1,0:T(8,128)}), f32[8,128,128]{2,1,0:T(8,128)S(1)}, u32[]{:S(2)}, u32[]{:S(2)}) async-start(f32[8,128,128]{2,1,0:T(8,128)} %product.13), calls=%async_computation.4 | async-start | bytes 1048576 | tf_op jit(solution)/shard_map/all_to_all | solution.py:483
  108.1 0.0 collective-permute-done.12.other_ref
  108.2 1.2 %assemble.1 = f32[3,256,256]{2,1,0:T(8,128)} custom-call(s32[1]{0:T(128)} %bitcast.1.row_ref, f32[8,224,128]{2,1,0:T(8,128)S(1)} %all-to-all-done.2.own_ref.left_ref, f32[8,224,128]{2,1,0:T(8,128)S(1)} %collective-permute-done.12.other_ref), custom_call_target="tpu_custom_call" | custom-call | flops 1024 | bytes 1024 | tf_op jit(solution)/shard_map/assemble/pallas_call | solution.py:463
  109.4 8.4 %all-to-all-done.4.right_ref = f32[8,128,128]{2,1,0:T(8,128)S(1)} async-done(((f32[8,128,128]{2,1,0:T(8,128)}), f32[8,128,128]{2,1,0:T(8,128)S(1)}, u32[]{:S(2)}, u32[]{:S(2)}) %all-to-all-start.4) | async-done | bytes 524320 | tf_op jit(solution)/shard_map/all_to_all | solution.py:483
  117.8 1.8 %finish.1 = f32[512,256]{1,0:T(8,128)} custom-call(s32[8]{0:T(128)S(1)} %bitcast.5, f32[256,512]{1,0:T(8,128)S(1)} %get-tuple-element.45.base_ref, f32[8,224,128]{2,1,0:T(8,128)S(1)} %all-to-all-done.2.own_ref.left_ref, f32[8,128,128]{2,1,0:T(8,128)S(1)} %all-to-all-done.4.right_ref), custom_call_target="tpu_custom_call" | custom-call | flops 1024 | bytes 1024 | tf_op jit(solution)/shard_map/finish/pallas_call | solution.py:436
Async XLA Ops:
  2.4 14.4 %collective-permute-start.1 = (f32[128,512]{1,0:T(8,128)S(1)}, f32[128,512]{1,0:T(8,128)S(1)}, u32[]{:S(2)}, u32[]{:S(2)}) collective-permute-start(f32[128,512]{1,0:T(8,128)S(1)} %get-tuple-element.24.first_ref.refs_0_), channel_id=1, source_target_pairs={{0,3},{1,0},{2,1},{3,2},{4,7},{5,4},{6,5},{7,6},{8,11},{9,8},{10,9... | collective-permute-start | bytes 786440 | tf_op jit(solution)/shard_map/ppermute | solution.py:479
  7.5 12.1 %collective-permute-start = (f32[128,512]{1,0:T(8,128)S(1)}, f32[128,512]{1,0:T(8,128)S(1)}, u32[]{:S(2)}, u32[]{:S(2)}) collective-permute-start(f32[128,512]{1,0:T(8,128)S(1)} %get-tuple-element.24.first_ref.refs_0_), channel_id=1, source_target_pairs={{0,1},{1,2},{2,3},{3,0},{4,5},{5,6},{6,7},{7,4},{8,9},{9,10},{10,1... | collective-permute-start | bytes 786440 | tf_op jit(solution)/shard_map/ppermute | solution.py:479
  12.4 19.2 %all-to-all-start = ((f32[8,192,128]{2,1,0:T(8,128)}), f32[8,192,128]{2,1,0:T(8,128)S(1)}, u32[]{:S(2)}, u32[]{:S(2)}) async-start(f32[8,192,128]{2,1,0:T(8,128)} %get-tuple-element.36), calls=%async_computation | async-start | bytes 1572864 | tf_op jit(solution)/shard_map/all_to_all | solution.py:483
  19.6 8.1 %collective-permute-start.2 = (f32[128,512]{1,0:T(8,128)S(1)}, f32[128,512]{1,0:T(8,128)S(1)}, u32[]{:S(2)}, u32[]{:S(2)}) collective-permute-start(f32[128,512]{1,0:T(8,128)S(1)} %select_select_fusion.3), channel_id=1, source_target_pairs={{1,0},{2,3},{3,1},{0,2},{5,4},{6,7},{7,5},{4,6},{9,8},{10,11},{11,... | collective-permute-start | bytes 786440 | tf_op jit(solution)/shard_map/ppermute | solution.py:493
  27.7 11.1 %collective-permute-start.4 = (f32[128,512]{1,0:T(8,128)S(1)}, f32[128,512]{1,0:T(8,128)S(1)}, u32[]{:S(2)}, u32[]{:S(2)}) collective-permute-start(f32[128,512]{1,0:T(8,128)S(1)} %get-tuple-element.30.refs_2_), channel_id=1, source_target_pairs={{0,1},{1,2},{2,3},{3,0},{4,5},{5,6},{6,7},{7,4},{8,9},{9,10},{10,1... | collective-permute-start | bytes 786440 | tf_op jit(solution)/shard_map/ppermute | solution.py:479
  29.4 11.9 %collective-permute-start.3 = (f32[128,512]{1,0:T(8,128)S(1)}, f32[128,512]{1,0:T(8,128)S(1)}, u32[]{:S(2)}, u32[]{:S(2)}) collective-permute-start(f32[128,512]{1,0:T(8,128)S(1)} %get-tuple-element.30.refs_2_), channel_id=1, source_target_pairs={{0,3},{1,0},{2,1},{3,2},{4,7},{5,4},{6,5},{7,6},{8,11},{9,8},{10,9... | collective-permute-start | bytes 786440 | tf_op jit(solution)/shard_map/ppermute | solution.py:479
  34.9 14.1 %all-to-all-start.1 = ((f32[8,128,128]{2,1,0:T(8,128)}), f32[8,128,128]{2,1,0:T(8,128)S(1)}, u32[]{:S(2)}, u32[]{:S(2)}) async-start(f32[8,128,128]{2,1,0:T(8,128)} %product.8), calls=%async_computation.1 | async-start | bytes 1048576 | tf_op jit(solution)/shard_map/all_to_all | solution.py:483
  41.4 7.6 %collective-permute-start.5 = (f32[128,512]{1,0:T(8,128)S(1)}, f32[128,512]{1,0:T(8,128)S(1)}, u32[]{:S(2)}, u32[]{:S(2)}) collective-permute-start(f32[128,512]{1,0:T(8,128)S(1)} %select_select_fusion.2), channel_id=1, source_target_pairs={{1,0},{2,3},{3,1},{0,2},{5,4},{6,7},{7,5},{4,6},{9,8},{10,11},{11,... | collective-permute-start | bytes 786440 | tf_op jit(solution)/shard_map/ppermute | solution.py:493
  42.8 6.2 %copy-start = (s32[1,8,1]{1,2,0:T(1,128)S(1)}, s32[1,8,1]{1,2,0:T(1,128)}, u32[]{:S(2)}) copy-start(s32[1,8,1]{1,2,0:T(1,128)} %param.20) | copy-start | bytes 100
  49.7 13.2 %collective-permute-start.7 = (f32[176,512]{1,0:T(8,128)S(1)}, f32[176,512]{1,0:T(8,128)S(1)}, u32[]{:S(2)}, u32[]{:S(2)}) collective-permute-start(f32[176,512]{1,0:T(8,128)S(1)} %carry.2.refs_2_.refs_4_), channel_id=1, source_target_pairs={{0,1},{1,2},{2,3},{3,0},{4,5},{5,6},{6,7},{7,4},{8,9},{9,10},{10,1... | collective-permute-start | bytes 1081352 | tf_op jit(solution)/shard_map/ppermute | solution.py:479
  52.4 15.7 %collective-permute-start.6 = (f32[176,512]{1,0:T(8,128)S(1)}, f32[176,512]{1,0:T(8,128)S(1)}, u32[]{:S(2)}, u32[]{:S(2)}) collective-permute-start(f32[176,512]{1,0:T(8,128)S(1)} %carry.2.refs_2_.refs_4_), channel_id=1, source_target_pairs={{0,3},{1,0},{2,1},{3,2},{4,7},{5,4},{6,5},{7,6},{8,11},{9,8},{10,9... | collective-permute-start | bytes 1081352 | tf_op jit(solution)/shard_map/ppermute | solution.py:479
  57.1 21.6 %all-to-all-start.3 = ((f32[8,128,128]{2,1,0:T(8,128)}), f32[8,128,128]{2,1,0:T(8,128)S(1)}, u32[]{:S(2)}, u32[]{:S(2)}) async-start(f32[8,128,128]{2,1,0:T(8,128)} %product.11), calls=%async_computation.3 | async-start | bytes 1048576 | tf_op jit(solution)/shard_map/all_to_all | solution.py:483
  68.1 10.5 %collective-permute-start.8 = (f32[176,512]{1,0:T(8,128)S(1)}, f32[176,512]{1,0:T(8,128)S(1)}, u32[]{:S(2)}, u32[]{:S(2)}) collective-permute-start(f32[176,512]{1,0:T(8,128)S(1)} %select_select_fusion), channel_id=1, source_target_pairs={{1,0},{2,3},{3,1},{0,2},{5,4},{6,7},{7,5},{4,6},{9,8},{10,11},{11,... | collective-permute-start | bytes 1081352 | tf_op jit(solution)/shard_map/ppermute | solution.py:493
  79.3 11.3 %collective-permute-start.10 = (f32[128,512]{1,0:T(8,128)S(1)}, f32[128,512]{1,0:T(8,128)S(1)}, u32[]{:S(2)}, u32[]{:S(2)}) collective-permute-start(f32[128,512]{1,0:T(8,128)S(1)} %carry.3.refs_2_), channel_id=1, source_target_pairs={{0,1},{1,2},{2,3},{3,0},{4,5},{5,6},{6,7},{7,4},{8,9},{9,10},{10,1... | collective-permute-start | bytes 786440 | tf_op jit(solution)/shard_map/ppermute | solution.py:479
  80.9 12.2 %collective-permute-start.9 = (f32[128,512]{1,0:T(8,128)S(1)}, f32[128,512]{1,0:T(8,128)S(1)}, u32[]{:S(2)}, u32[]{:S(2)}) collective-permute-start(f32[128,512]{1,0:T(8,128)S(1)} %carry.3.refs_2_), channel_id=1, source_target_pairs={{0,3},{1,0},{2,1},{3,2},{4,7},{5,4},{6,5},{7,6},{8,11},{9,8},{10,9... | collective-permute-start | bytes 786440 | tf_op jit(solution)/shard_map/ppermute | solution.py:479
  86.8 17.9 %all-to-all-start.2 = ((f32[8,224,128]{2,1,0:T(8,128)}), f32[8,224,128]{2,1,0:T(8,128)S(1)}, u32[]{:S(2)}, u32[]{:S(2)}) async-start(f32[8,224,128]{2,1,0:T(8,128)} %product.10), calls=%async_computation.2 | async-start | bytes 1835008 | tf_op jit(solution)/shard_map/all_to_all | solution.py:483
  93.1 7.2 %collective-permute-start.11 = (f32[128,512]{1,0:T(8,128)S(1)}, f32[128,512]{1,0:T(8,128)S(1)}, u32[]{:S(2)}, u32[]{:S(2)}) collective-permute-start(f32[128,512]{1,0:T(8,128)S(1)} %select_select_fusion.1), channel_id=1, source_target_pairs={{1,0},{2,3},{3,1},{0,2},{5,4},{6,7},{7,5},{4,6},{9,8},{10,11},{11,... | collective-permute-start | bytes 786440 | tf_op jit(solution)/shard_map/ppermute | solution.py:493
  104.6 3.5 %collective-permute-start.12 = (f32[8,224,128]{2,1,0:T(8,128)S(1)}, f32[8,224,128]{2,1,0:T(8,128)S(1)}, u32[]{:S(2)}, u32[]{:S(2)}) collective-permute-start(f32[8,224,128]{2,1,0:T(8,128)S(1)} %all-to-all-done.2.own_ref.left_ref), channel_id=1, source_target_pairs={{0,4},{4,0},{8,12},{12,8},{16,20},{20,16},{24,28},{28,24},{1,5},{5... | collective-permute-start | bytes 2752520 | tf_op jit(solution)/shard_map/ppermute | solution.py:577
  104.6 13.2 %all-to-all-start.4 = ((f32[8,128,128]{2,1,0:T(8,128)}), f32[8,128,128]{2,1,0:T(8,128)S(1)}, u32[]{:S(2)}, u32[]{:S(2)}) async-start(f32[8,128,128]{2,1,0:T(8,128)} %product.13), calls=%async_computation.4 | async-start | bytes 1048576 | tf_op jit(solution)/shard_map/all_to_all | solution.py:483

commit v17 on v16

--- a/solution.py
+++ b/solution.py
@@ -284,7 +284,7 @@
     )(ids, live, *in_hbm(rows, slots, values), *fields)
 
 
-def product_kernel(n_row, n_col, origins, has_prev, last, n_carriers, has_base, *refs):
+def product_kernel(n_row, n_col, origins, has_prev, last, n_carriers, has_base, apart, *refs):
     n = len(origins)
     ids_ref, op_ref, refs = refs[0], refs[1], refs[2:]
     fields, refs = refs[:n], refs[n:]
@@ -293,6 +293,8 @@
     carriers, refs = refs[:n_carriers], refs[n_carriers:]
     if has_base:
         base_hbm, out_ref, base_ref, refs = refs[0], refs[1], refs[2], refs[3:]
+    elif apart:
+        slot_refs, refs = refs[:n_row], refs[n_row:]
     else:
         out_ref, refs = refs[0], refs[1:]
     held, buf, field_sems, sems, out, out_sems, prev, other_sems = refs[:8]
@@ -344,6 +346,8 @@
             out[2 * p, :H, :] = total[:, :TB]
             out[2 * p + 1, :H, :] = total[:, TB:]
             place = pl.ds(2 * p, 2)
+            if apart:
+                continue
             sent.append(pltpu.make_async_copy(out.at[place], out_ref.at[place], out_sems.at[p]))
         else:
             out[:, here] = total
@@ -352,11 +356,14 @@
         sent[-1].start()
     if has_base:
         base_copy.wait()
+    if apart:
+        for j, slot_ref in enumerate(slot_refs):
+            slot_ref[...] = out[ids_ref[1] ^ j]
     for item in sent:
         item.wait()
 
 
-def product(n_row, n_col, ids, origins, operator, fields, prev, last, carriers=(), base=None, prev_near=False):
+def product(n_row, n_col, ids, origins, operator, fields, prev, last, carriers=(), base=None, prev_near=False, apart=False):
     n = len(origins)
     has_prev = prev is not None
     has_base = base is not None
@@ -376,11 +383,16 @@
     if carriers:
         scratch.append(pltpu.VMEM((n_col, rows, NODES_DEV), F32))
     out = pltpu.HBM(shape, F32)
+    out_specs, out_shape = HBM, out
+    if has_base:
+        out_specs, out_shape = [HBM, VMEM], [out, jax.ShapeDtypeStruct(base.shape, F32)]
+    elif apart:
+        out_specs, out_shape = [VMEM] * n_row, [jax.ShapeDtypeStruct((H, TB), F32)] * n_row
     return pl.pallas_call(
-        functools.partial(product_kernel, n_row, n_col, origins, has_prev, last, len(carriers), has_base),
+        functools.partial(product_kernel, n_row, n_col, origins, has_prev, last, len(carriers), has_base, apart),
         in_specs=[SMEM, HBM] + [ANY] * (n + has_prev) + [VMEM] * len(carriers) + [HBM] * has_base,
-        out_specs=[HBM, VMEM] if has_base else HBM,
-        out_shape=[out, jax.ShapeDtypeStruct(base.shape, F32)] if has_base else out,
+        out_specs=out_specs,
+        out_shape=out_shape,
         scratch_shapes=scratch,
         compiler_params=params(48),
         cost_estimate=LIGHT if last else HEAVY,
@@ -423,31 +435,34 @@
     )(owners, base, came, *pieces)
 
 
-def finish_kernel(n_row, owners_ref, base_ref, left_ref, right_ref, out_ref, total):
+def finish_kernel(n_row, ids_ref, owners_ref, base_ref, left_ref, *refs):
+    right_refs, out_ref, total = refs[:n_row], refs[n_row], refs[n_row + 1]
     total[...] = base_ref[...]
-    for h, came in enumerate((left_ref, right_ref)):
-        for q in range(n_row):
-            here = pl.ds(pl.multiple_of(owners_ref[q] * TB, TB), TB)
-            total[h * H : (h + 1) * H, here] += came[q, :H, :]
+    for q in range(n_row):
+        here = pl.ds(pl.multiple_of(owners_ref[q] * TB, TB), TB)
+        total[:H, here] += left_ref[q, :H, :]
+    for j in range(n_row):
+        here = pl.ds(pl.multiple_of(owners_ref[ids_ref[1] ^ j] * TB, TB), TB)
+        total[H:, here] += right_refs[j][...]
     out_ref[...] = total[...].T
 
 
-def finish(n_row, owners, base, left, right):
+def finish(n_row, ids, owners, base, left, right):
     return pl.pallas_call(
         functools.partial(finish_kernel, n_row),
-        in_specs=[SMEM] + [VMEM] * 3,
+        in_specs=[SMEM] * 2 + [VMEM] * (2 + n_row),
         out_specs=VMEM,
         out_shape=jax.ShapeDtypeStruct((NODES_DEV, F), F32),
         scratch_shapes=[pltpu.VMEM((F, NODES_DEV), F32)],
         compiler_params=params(24),
         cost_estimate=LIGHT,
         name="finish",
-    )(owners, base, left, right)
+    )(ids, owners, base, left, *right)
 
 
 def assemble_kernel(n_row, row_ref, own_ref, other_ref, out_ref, halves, turned):
     rows = F // n_row
-    half = lax.rem(row_ref[0], 2)
+    half = lax.rem(row_ref[1], 2)
     halves[half] = own_ref[:, H:, :]
     halves[1 - half] = other_ref[:, H:, :]
     groups = 3 * F // LANES // 2
@@ -522,10 +537,10 @@
     return total
 
 
-def final(n_row, n_col, ids, operator, steps, total, carrying=False, near=False):
+def final(n_row, n_col, ids, operator, steps, total, carrying=False, near=False, apart=False):
     origins, fields = zip(*steps[-1])
     carriers = [x for _, x in sorted((p for step in steps for p in step), key=lambda p: p[0])] if carrying else ()
-    return product(n_row, n_col, ids, origins, operator, fields, total, True, carriers, prev_near=near)
+    return product(n_row, n_col, ids, origins, operator, fields, total, True, carriers, prev_near=near, apart=apart)
 
 
 def per_device(
@@ -543,7 +558,7 @@
 ):
     n_row = lax.axis_size("row")
     n_col = lax.axis_size("col")
-    ids = lax.axis_index("col").astype(jnp.int32).reshape(1)
+    ids = jnp.stack([lax.axis_index("col"), lax.axis_index("row")]).astype(jnp.int32)
     owners = send_blocks.reshape(n_row)
     left, right = term_two(grad_out, relu_mask, cheb_weight)
     one_left, one_right, diff, pieces = local_terms(
@@ -572,12 +587,13 @@
     left_came = exchange(final(*common, steps, left_early, carrying=True))
     right_early = early(*common, right_steps)
 
-    right_last = final(*common, right_steps, right_early)
-    right_came = exchange(right_last)
-    other = lax.ppermute(after(left_came, right_last), "row", [(r, r ^ 1) for r in range(n_row)])
-    row = lax.axis_index("row").astype(jnp.int32).reshape(1)
-    weight_grad = assemble(n_row, row, left_came, other)
-    return finish(n_row, owners, after(diff, weight_grad), left_came, right_came), weight_grad
+    right_last = final(*common, right_steps, right_early, apart=True)
+    right_came = [right_last[0]] * n_row
+    for j in range(n_row - 1, 0, -1):
+        right_came[j] = lax.ppermute(right_last[j], "row", [(r, r ^ j) for r in range(n_row)])
+    other = lax.ppermute(after(left_came, right_last[0]), "row", [(r, r ^ 1) for r in range(n_row)])
+    weight_grad = assemble(n_row, ids, left_came, other)
+    return finish(n_row, ids, owners, after(diff, weight_grad), left_came, right_came), weight_grad
 
 
 def solution(mesh):

time: 121 us -> 121 us (level)
  waiting for transfers between devices: 29.1 us -> 21.4 us
  Pallas kernels: 48.5 us -> 52.8 us
  starting transfers between devices: 40.2 us -> 43.4 us
    all_to_all x5 -> x4, waiting for transfers between devices: 9.19 us -> 1.02 us  [exchange(): lax.all_to_all(pieces, 'row', split_axis=0, concat_axis=0, tiled=True)]
    ppermute x1 -> x8, starting transfers between devices: 0.01 us -> 6.36 us  [the longest x7 6.36 us: per_device(): lax.ppermute(right_last[j], 'row', [(r, r ^ j) for r in range(n_row)])]
    ppermute x1 -> x8, waiting for transfers between devices: 0.01 us -> 3.57 us  [the longest x7 3.57 us: per_device(): lax.ppermute(right_last[j], 'row', [(r, r ^ j) for r in range(n_row)])]
    all_to_all x5 -> x4, starting transfers between devices: 18.7 us -> 15.4 us  [exchange(): lax.all_to_all(pieces, 'row', split_axis=0, concat_axis=0, tiled=True)]
    pallas_call x7, Pallas kernels: 30.3 us -> 33.5 us  [product(): pl.pallas_call(functools.partial(product_kernel, n_row, n_col, origins, h...]
    ppermute x8, waiting for transfers between devices: 15.1 us -> 13.1 us  [shift(): lax.ppermute(x, 'col', [(c, (c + step) % n_col) for c in range(n_col)])]
  transfers between devices with their start and end apart: 18 -> 24, of which waited for: 10 -> 11; matrix products, arithmetic and copies ran while one was open for 0% -> 0% of each run, Pallas kernels for 37% -> 40%
where the time goes in v17:
time: 121 us; the launch traced here: 119 us
  Pallas kernels  52.8 us (44%)
  starting transfers between devices  43.4 us (36%)
  waiting for transfers between devices  21.4 us (18%)
  between operations  1.43 us (1%)
    pallas_call x7, Pallas kernels, product(): pl.pallas_call(functools.partial(product_kernel, n_row, n_col, origins, h...  33.5 us
    ppermute x8, starting transfers between devices, shift(): lax.ppermute(x, 'col', [(c, (c + step) % n_col) for c in range(n_col)])  16.7 us
    all_to_all x4, starting transfers between devices, exchange(): lax.all_to_all(pieces, 'row', split_axis=0, concat_axis=0, tiled=True)  15.4 us
    ppermute x8, waiting for transfers between devices, shift(): lax.ppermute(x, 'col', [(c, (c + step) % n_col) for c in range(n_col)])  13.1 us
    pallas_call x1, Pallas kernels, build_operator(): pl.pallas_call(functools.partial(operator_kernel, n_row, n_col, origins),...  7.82 us
    ppermute x7, starting transfers between devices, per_device(): lax.ppermute(right_last[j], 'row', [(r, r ^ j) for r in range(n_row)])  6.36 us
    pallas_call x1, Pallas kernels, local_terms(): pl.pallas_call(functools.partial(local_kernel, n_row), in_specs=[ANY] + [...  4.88 us
    ppermute x4, starting transfers between devices, opposite(): return lax.ppermute(sent, 'col', [(1, 0), (2, 3), (3, 1), (0, 2)])  4.86 us
  transfers between devices with their start and end apart: 24, of which 11 were waited for; matrix products, arithmetic and copies ran while one was open for 0% of the time, Pallas kernels for 40%

profile of v17, /device:TPU:0, one launch (start us, length us, event | category | flops | bytes accessed | tf_op | source)
XLA Modules:
  0.0 119.4 jit_solution(17849520409076460376)
XLA Ops:
  0.6 1.7 %term_two.1 = (f32[128,512]{1,0:T(8,128)S(1)}, f32[128,512]{1,0:T(8,128)S(1)}) custom-call(f32[512,256]{1,0:T(8,128)} %grad_hbm.3, s32[512,256]{1,0:T(8,128)} %mask_hbm.3, f32[3,256,256]{2,1,0:T(8,128)} %weight_hbm.3), custom_call_target="tpu_custom_call" | custom-call | flops 1024 | bytes 1024 | tf_op jit(solution)/shard_map/term_two/pallas_call | solution.py:78
  2.4 5.1 %collective-permute-start.1 = (f32[128,512]{1,0:T(8,128)S(1)}, f32[128,512]{1,0:T(8,128)S(1)}, u32[]{:S(2)}, u32[]{:S(2)}) collective-permute-start(f32[128,512]{1,0:T(8,128)S(1)} %get-tuple-element.32.first_ref.refs_0_), channel_id=1, source_target_pairs={{0,3},{1,0},{2,1},{3,2},{4,7},{5,4},{6,5},{7,6},{8,11},{9,8},{10,9... | collective-permute-start | bytes 786440 | tf_op jit(solution)/shard_map/ppermute | solution.py:494
  7.5 0.0 collective-permute-start
  7.5 4.9 %local_terms.1 = (f32[128,512]{1,0:T(8,128)}, f32[128,512]{1,0:T(8,128)}, f32[256,512]{1,0:T(8,128)S(1)}, f32[8,192,128]{2,1,0:T(8,128)}) custom-call(f32[128,512]{1,0:T(8,128)S(1)} %get-tuple-element.32.first_ref.refs_0_, f32[512,256]{1,0:T(8,128)} %grad_hbm.3, s32[512,256]{1,0:T(8,128)} %mask_hbm.3, f32[3,256,256]{2,1,0:T(8,128)} %weight_hbm.3, ...), custom_call_target="tpu_custom_call" | custom-call | flops 1024 | bytes 1024 | tf_op jit(solution)/shard_map/local_terms/pallas_call | solution.py:125
  12.4 3.7 %all-to-all-start = ((f32[8,192,128]{2,1,0:T(8,128)}), f32[8,192,128]{2,1,0:T(8,128)S(1)}, u32[]{:S(2)}, u32[]{:S(2)}) async-start(f32[8,192,128]{2,1,0:T(8,128)} %get-tuple-element.44), calls=%async_computation | async-start | bytes 1572864 | tf_op jit(solution)/shard_map/all_to_all | solution.py:498
  16.8 0.1 pad_add_fusion.ids_ref.refs_0_.row_ref
  16.8 0.0 collective-permute-done.1.refs_2_
  16.8 2.7 %collective-permute-done.refs_1_ = f32[128,512]{1,0:T(8,128)S(1)} collective-permute-done((f32[128,512]{1,0:T(8,128)S(1)}, f32[128,512]{1,0:T(8,128)S(1)}, u32[]{:S(2)}, u32[]{:S(2)}) %collective-permute-start) | collective-permute-done | bytes 262176 | tf_op jit(solution)/shard_map/ppermute | solution.py:494
  19.6 0.1 select_select_fusion.3
  19.6 0.8 collective-permute-start.2
  20.4 7.8 %operator.1 = (bf16[4,4,1024,256]{3,2,1,0:T(8,128)(2,1)}, f32[128,1024]{1,0:T(8,128)S(1)}) custom-call(s32[2]{0:T(128)S(1)} %pad_add_fusion.ids_ref.refs_0_.row_ref, s32[1]{0:T(128)S(6)} %copy.13.live_ref, s32[1,128]{1,0:T(1,128)} %rows_hbm.1, s32[1,128]{1,0:T(1,128)} %slots_hbm.1, f32[1,128,128,128]{3,2,1,0:T(8,128)} %values_ref.1, ...), custom_call_target="tpu_custom_call" | custom-call | flops 17179869184 | bytes 67108864 | tf_op jit(solution)/shard_map/operator/pallas_call | solution.py:262
  28.3 0.0 collective-permute-done.2.refs_2_
  28.3 1.3 %collective-permute-start.4 = (f32[128,512]{1,0:T(8,128)S(1)}, f32[128,512]{1,0:T(8,128)S(1)}, u32[]{:S(2)}, u32[]{:S(2)}) collective-permute-start(f32[128,512]{1,0:T(8,128)S(1)} %get-tuple-element.38.refs_2_), channel_id=1, source_target_pairs={{0,1},{1,2},{2,3},{3,0},{4,5},{5,6},{6,7},{7,4},{8,9},{9,10},{10,1... | collective-permute-start | bytes 786440 | tf_op jit(solution)/shard_map/ppermute | solution.py:494
  29.6 2.5 %collective-permute-start.3 = (f32[128,512]{1,0:T(8,128)S(1)}, f32[128,512]{1,0:T(8,128)S(1)}, u32[]{:S(2)}, u32[]{:S(2)}) collective-permute-start(f32[128,512]{1,0:T(8,128)S(1)} %get-tuple-element.38.refs_2_), channel_id=1, source_target_pairs={{0,3},{1,0},{2,1},{3,2},{4,7},{5,4},{6,5},{7,6},{8,11},{9,8},{10,9... | collective-permute-start | bytes 786440 | tf_op jit(solution)/shard_map/ppermute | solution.py:494
  32.1 0.0 all-to-all-done.refs_0_
  32.1 3.8 %product.8 = f32[8,128,128]{2,1,0:T(8,128)} custom-call(s32[2]{0:T(128)S(1)} %pad_add_fusion.ids_ref.refs_0_.row_ref, bf16[4,4,1024,256]{3,2,1,0:T(8,128)(2,1)} %get-tuple-element.34.refs_1_, f32[128,512]{1,0:T(8,128)S(1)} %collective-permute-done.2.refs_2_, f32[128,1024]{1,0:T(8,128)S(1)} %get-tuple-element.45.refs_3_), custom_call_target="tpu_custom_call" | custom-call | flops 1024 | bytes 1024 | tf_op jit(solution)/shard_map/product/pallas_call | solution.py:391
  35.9 3.7 %all-to-all-start.1 = ((f32[8,128,128]{2,1,0:T(8,128)}), f32[8,128,128]{2,1,0:T(8,128)S(1)}, u32[]{:S(2)}, u32[]{:S(2)}) async-start(f32[8,128,128]{2,1,0:T(8,128)} %product.8), calls=%async_computation.1 | async-start | bytes 1048576 | tf_op jit(solution)/shard_map/all_to_all | solution.py:498
  39.7 0.0 collective-permute-done.4.refs_4_
  39.7 2.2 %collective-permute-done.3.refs_3_ = f32[128,512]{1,0:T(8,128)S(1)} collective-permute-done((f32[128,512]{1,0:T(8,128)S(1)}, f32[128,512]{1,0:T(8,128)S(1)}, u32[]{:S(2)}, u32[]{:S(2)}) %collective-permute-start.3) | collective-permute-done | bytes 262176 | tf_op jit(solution)/shard_map/ppermute | solution.py:494
  41.8 0.1 select_select_fusion.2
  41.9 1.5 %collective-permute-start.5 = (f32[128,512]{1,0:T(8,128)S(1)}, f32[128,512]{1,0:T(8,128)S(1)}, u32[]{:S(2)}, u32[]{:S(2)}) collective-permute-start(f32[128,512]{1,0:T(8,128)S(1)} %select_select_fusion.2), channel_id=1, source_target_pairs={{1,0},{2,3},{3,1},{0,2},{5,4},{6,7},{7,5},{4,6},{9,8},{10,11},{11,... | collective-permute-start | bytes 786440 | tf_op jit(solution)/shard_map/ppermute | solution.py:508
  43.4 6.0 %product.7 = (f32[128,1024]{1,0:T(8,128)}, f32[128,512]{1,0:T(8,128)S(1)}) custom-call(s32[2]{0:T(128)S(1)} %pad_add_fusion.ids_ref.refs_0_.row_ref, bf16[4,4,1024,256]{3,2,1,0:T(8,128)(2,1)} %get-tuple-element.34.refs_1_, f32[128,512]{1,0:T(8,128)S(1)} %get-tuple-element.38.refs_2_, f32[128,512]{1,0:T(8,128)S(1)} %collective-permute-done.3.refs_3_, ...), custom_call_target="tpu_custom_call" | custom-call | flops 17179869184 | bytes 67108864 | tf_op jit(solution)/shard_map/product/pallas_call | solution.py:391
  49.5 0.1 collective-permute-done.5.refs_2_
  49.5 0.0 all-to-all-done.1.came_ref
  49.5 0.7 carry.2.refs_2_.refs_4_
  50.2 2.7 %collective-permute-start.7 = (f32[176,512]{1,0:T(8,128)S(1)}, f32[176,512]{1,0:T(8,128)S(1)}, u32[]{:S(2)}, u32[]{:S(2)}) collective-permute-start(f32[176,512]{1,0:T(8,128)S(1)} %carry.2.refs_2_.refs_4_), channel_id=1, source_target_pairs={{0,1},{1,2},{2,3},{3,0},{4,5},{5,6},{6,7},{7,4},{8,9},{9,10},{10,1... | collective-permute-start | bytes 1081352 | tf_op jit(solution)/shard_map/ppermute | solution.py:494
  52.9 1.2 collective-permute-start.6
  54.1 4.1 %product.11 = f32[8,128,128]{2,1,0:T(8,128)} custom-call(s32[2]{0:T(128)S(1)} %pad_add_fusion.ids_ref.refs_0_.row_ref, bf16[4,4,1024,256]{3,2,1,0:T(8,128)(2,1)} %get-tuple-element.34.refs_1_, f32[128,512]{1,0:T(8,128)S(1)} %collective-permute-done.5.refs_2_, f32[128,1024]{1,0:T(8,128)} %get-tuple-element.41.refs_3_), custom_call_target="tpu_custom_call" | custom-call | flops 1024 | bytes 1024 | tf_op jit(solution)/shard_map/product/pallas_call | solution.py:391
  58.2 3.9 %all-to-all-start.3 = ((f32[8,128,128]{2,1,0:T(8,128)}), f32[8,128,128]{2,1,0:T(8,128)S(1)}, u32[]{:S(2)}, u32[]{:S(2)}) async-start(f32[8,128,128]{2,1,0:T(8,128)} %product.11), calls=%async_computation.3 | async-start | bytes 1048576 | tf_op jit(solution)/shard_map/all_to_all | solution.py:498
  62.1 1.4 %collective-permute-done.7.refs_3_.refs_7_ = f32[176,512]{1,0:T(8,128)S(1)} collective-permute-done((f32[176,512]{1,0:T(8,128)S(1)}, f32[176,512]{1,0:T(8,128)S(1)}, u32[]{:S(2)}, u32[]{:S(2)}) %collective-permute-start.7) | collective-permute-done | bytes 360480 | tf_op jit(solution)/shard_map/ppermute | solution.py:494
  63.5 5.1 %collective-permute-done.6.refs_4_.refs_5_ = f32[176,512]{1,0:T(8,128)S(1)} collective-permute-done((f32[176,512]{1,0:T(8,128)S(1)}, f32[176,512]{1,0:T(8,128)S(1)}, u32[]{:S(2)}, u32[]{:S(2)}) %collective-permute-start.6) | collective-permute-done | bytes 360480 | tf_op jit(solution)/shard_map/ppermute | solution.py:494
  68.6 0.1 select_select_fusion
  68.7 0.8 collective-permute-start.8
  69.5 6.0 %product.9 = (f32[128,1024]{1,0:T(8,128)}, f32[128,512]{1,0:T(8,128)S(1)}) custom-call(s32[2]{0:T(128)S(1)} %pad_add_fusion.ids_ref.refs_0_.row_ref, bf16[4,4,1024,256]{3,2,1,0:T(8,128)(2,1)} %get-tuple-element.34.refs_1_, f32[176,512]{1,0:T(8,128)S(1)} %carry.2.refs_2_.refs_4_, f32[176,512]{1,0:T(8,128)S(1)} %collective-permute-done.7.refs_3_.refs_7_, ...), custom_call_target="tpu_custom_call" | custom-call | flops 17179869184 | bytes 67108864 | tf_op jit(solution)/shard_map/product/pallas_call | solution.py:391
  75.5 3.7 %collective-permute-done.8.refs_2_.refs_6_ = f32[176,512]{1,0:T(8,128)S(1)} collective-permute-done((f32[176,512]{1,0:T(8,128)S(1)}, f32[176,512]{1,0:T(8,128)S(1)}, u32[]{:S(2)}, u32[]{:S(2)}) %collective-permute-start.8) | collective-permute-done | bytes 360480 | tf_op jit(solution)/shard_map/ppermute | solution.py:508
  79.2 0.0 all-to-all-done.3.came_ref
  79.2 0.7 carry.3.refs_2_
  79.9 1.5 %collective-permute-start.10 = (f32[128,512]{1,0:T(8,128)S(1)}, f32[128,512]{1,0:T(8,128)S(1)}, u32[]{:S(2)}, u32[]{:S(2)}) collective-permute-start(f32[128,512]{1,0:T(8,128)S(1)} %carry.3.refs_2_), channel_id=1, source_target_pairs={{0,1},{1,2},{2,3},{3,0},{4,5},{5,6},{6,7},{7,4},{8,9},{9,10},{10,1... | collective-permute-start | bytes 786440 | tf_op jit(solution)/shard_map/ppermute | solution.py:494
  81.4 2.3 %collective-permute-start.9 = (f32[128,512]{1,0:T(8,128)S(1)}, f32[128,512]{1,0:T(8,128)S(1)}, u32[]{:S(2)}, u32[]{:S(2)}) collective-permute-start(f32[128,512]{1,0:T(8,128)S(1)} %carry.3.refs_2_), channel_id=1, source_target_pairs={{0,3},{1,0},{2,1},{3,2},{4,7},{5,4},{6,5},{7,6},{8,11},{9,8},{10,9... | collective-permute-start | bytes 786440 | tf_op jit(solution)/shard_map/ppermute | solution.py:494
  83.7 4.1 %product.10 = f32[8,224,128]{2,1,0:T(8,128)} custom-call(s32[2]{0:T(128)S(1)} %pad_add_fusion.ids_ref.refs_0_.row_ref, bf16[4,4,1024,256]{3,2,1,0:T(8,128)(2,1)} %get-tuple-element.34.refs_1_, f32[176,512]{1,0:T(8,128)S(1)} %collective-permute-done.8.refs_2_.refs_6_, f32[128,1024]{1,0:T(8,128)} %get-tuple-element.48.refs_3_, ...), custom_call_target="tpu_custom_call" | custom-call | flops 1024 | bytes 1024 | tf_op jit(solution)/shard_map/product/pallas_call | solution.py:391
  87.8 4.0 %all-to-all-start.2 = ((f32[8,224,128]{2,1,0:T(8,128)}), f32[8,224,128]{2,1,0:T(8,128)S(1)}, u32[]{:S(2)}, u32[]{:S(2)}) async-start(f32[8,224,128]{2,1,0:T(8,128)} %product.10), calls=%async_computation.2 | async-start | bytes 1835008 | tf_op jit(solution)/shard_map/all_to_all | solution.py:498
  91.9 0.0 collective-permute-done.10.refs_4_
  91.9 1.7 %collective-permute-done.9.refs_3_ = f32[128,512]{1,0:T(8,128)S(1)} collective-permute-done((f32[128,512]{1,0:T(8,128)S(1)}, f32[128,512]{1,0:T(8,128)S(1)}, u32[]{:S(2)}, u32[]{:S(2)}) %collective-permute-start.9) | collective-permute-done | bytes 262176 | tf_op jit(solution)/shard_map/ppermute | solution.py:494
  93.6 0.1 select_select_fusion.1
  93.7 1.7 %collective-permute-start.11 = (f32[128,512]{1,0:T(8,128)S(1)}, f32[128,512]{1,0:T(8,128)S(1)}, u32[]{:S(2)}, u32[]{:S(2)}) collective-permute-start(f32[128,512]{1,0:T(8,128)S(1)} %select_select_fusion.1), channel_id=1, source_target_pairs={{1,0},{2,3},{3,1},{0,2},{5,4},{6,7},{7,5},{4,6},{9,8},{10,11},{11,... | collective-permute-start | bytes 786440 | tf_op jit(solution)/shard_map/ppermute | solution.py:508
  95.4 6.0 %product.12.refs_3_ = f32[128,1024]{1,0:T(8,128)} custom-call(s32[2]{0:T(128)S(1)} %pad_add_fusion.ids_ref.refs_0_.row_ref, bf16[4,4,1024,256]{3,2,1,0:T(8,128)(2,1)} %get-tuple-element.34.refs_1_, f32[128,512]{1,0:T(8,128)S(1)} %carry.3.refs_2_, f32[128,512]{1,0:T(8,128)S(1)} %collective-permute-done.9.refs_3_, f32[128,512]{1,0:T(8,128)S(1)} %collective-permute-done.10.refs_4_), custom_call_target="tpu_custom_call" | custom-call | flops 17179869184 | bytes 67108864 | tf_op jit(solution)/shard_map/product/pallas_call | solution.py:391
  101.4 0.0 collective-permute-done.11.refs_2_
  101.4 3.4 %product.13 = (f32[128,128]{1,0:T(8,128)S(1)}, f32[128,128]{1,0:T(8,128)S(1)}, f32[128,128]{1,0:T(8,128)S(1)}, f32[128,128]{1,0:T(8,128)S(1)}, f32[128,128]{1,0:...) custom-call(s32[2]{0:T(128)S(1)} %pad_add_fusion.ids_ref.refs_0_.row_ref, ...), custom_call_target="tpu_custom_call" | custom-call | flops 1024 | bytes 1024 | tf_op jit(solution)/shard_map/product/pallas_call | solution.py:391
  104.9 1.0 all-to-all-done.2.own_ref.left_ref
  105.9 0.5 collective-permute-start.13
  106.4 1.5 %collective-permute-start.14 = (f32[128,128]{1,0:T(8,128)S(1)}, f32[128,128]{1,0:T(8,128)S(1)}, u32[]{:S(2)}, u32[]{:S(2)}) collective-permute-start(f32[128,128]{1,0:T(8,128)S(1)} %get-tuple-element.56), channel_id=1, source_target_pairs={{0,8},{4,12},{8,0},{12,4},{16,24},{20,28},{24,16},{28,20},{1,9},{5... | collective-permute-start | bytes 196616 | tf_op jit(solution)/shard_map/ppermute | solution.py:593
  107.9 0.9 collective-permute-start.16
  108.8 1.1 collective-permute-start.17
  109.9 0.8 collective-permute-done.14.refs_2_
  110.7 2.4 %collective-permute-start.18 = (f32[128,128]{1,0:T(8,128)S(1)}, f32[128,128]{1,0:T(8,128)S(1)}, u32[]{:S(2)}, u32[]{:S(2)}) collective-permute-start(f32[128,128]{1,0:T(8,128)S(1)} %get-tuple-element.60), channel_id=1, source_target_pairs={{0,24},{4,28},{8,16},{12,20},{16,8},{20,12},{24,0},{28,4},{1,25},{... | collective-permute-start | bytes 196616 | tf_op jit(solution)/shard_map/ppermute | solution.py:593
  113.0 0.0 collective-permute-done.12.other_ref
  113.0 0.0 collective-permute-start.19
  113.0 1.8 %assemble.1 = f32[3,256,256]{2,1,0:T(8,128)} custom-call(s32[2]{0:T(128)S(1)} %pad_add_fusion.ids_ref.refs_0_.row_ref, f32[8,224,128]{2,1,0:T(8,128)S(1)} %all-to-all-done.2.own_ref.left_ref, f32[8,224,128]{2,1,0:T(8,128)S(1)} %collective-permute-done.12.other_ref), custom_call_target="tpu_custom_call" | custom-call | flops 1024 | bytes 1024 | tf_op jit(solution)/shard_map/assemble/pallas_call | solution.py:478
  114.8 0.0 collective-permute-done.15.refs_3_
  114.8 0.0 collective-permute-done.16.refs_4_
  114.8 0.0 collective-permute-done.17.refs_5_
  114.8 1.0 collective-permute-done.18.refs_6_
  115.8 1.8 %collective-permute-done.19.refs_7_ = f32[128,128]{1,0:T(8,128)S(1)} collective-permute-done((f32[128,128]{1,0:T(8,128)S(1)}, f32[128,128]{1,0:T(8,128)S(1)}, u32[]{:S(2)}, u32[]{:S(2)}) %collective-permute-start.19) | collective-permute-done | bytes 65568 | tf_op jit(solution)/shard_map/ppermute | solution.py:593
  117.6 1.8 %finish.1 = f32[512,256]{1,0:T(8,128)} custom-call(s32[2]{0:T(128)S(1)} %pad_add_fusion.ids_ref.refs_0_.row_ref, s32[8]{0:T(128)S(1)} %bitcast.5, f32[256,512]{1,0:T(8,128)S(1)} %get-tuple-element.54.base_ref, f32[8,224,128]{2,1,0:T(8,128)S(1)} %all-to-all-done.2.own_ref.left_ref, f32[128,128]{1,0:T(8,128)S(1)} %get-tuple-element.52.refs_0_, ...), custom_call_target="tpu_custom_call" | custom-call | flops 1024 | bytes 1024 | tf_op jit(solution)/shard_map/finish/pallas_call | solution.py:451
  (5 shorter events, 0.0 us)
Async XLA Ops:
  2.4 14.5 %collective-permute-start.1 = (f32[128,512]{1,0:T(8,128)S(1)}, f32[128,512]{1,0:T(8,128)S(1)}, u32[]{:S(2)}, u32[]{:S(2)}) collective-permute-start(f32[128,512]{1,0:T(8,128)S(1)} %get-tuple-element.32.first_ref.refs_0_), channel_id=1, source_target_pairs={{0,3},{1,0},{2,1},{3,2},{4,7},{5,4},{6,5},{7,6},{8,11},{9,8},{10,9... | collective-permute-start | bytes 786440 | tf_op jit(solution)/shard_map/ppermute | solution.py:494
  7.5 12.1 %collective-permute-start = (f32[128,512]{1,0:T(8,128)S(1)}, f32[128,512]{1,0:T(8,128)S(1)}, u32[]{:S(2)}, u32[]{:S(2)}) collective-permute-start(f32[128,512]{1,0:T(8,128)S(1)} %get-tuple-element.32.first_ref.refs_0_), channel_id=1, source_target_pairs={{0,1},{1,2},{2,3},{3,0},{4,5},{5,6},{6,7},{7,4},{8,9},{9,10},{10,1... | collective-permute-start | bytes 786440 | tf_op jit(solution)/shard_map/ppermute | solution.py:494
  12.4 19.8 %all-to-all-start = ((f32[8,192,128]{2,1,0:T(8,128)}), f32[8,192,128]{2,1,0:T(8,128)S(1)}, u32[]{:S(2)}, u32[]{:S(2)}) async-start(f32[8,192,128]{2,1,0:T(8,128)} %get-tuple-element.44), calls=%async_computation | async-start | bytes 1572864 | tf_op jit(solution)/shard_map/all_to_all | solution.py:498
  19.6 8.6 %collective-permute-start.2 = (f32[128,512]{1,0:T(8,128)S(1)}, f32[128,512]{1,0:T(8,128)S(1)}, u32[]{:S(2)}, u32[]{:S(2)}) collective-permute-start(f32[128,512]{1,0:T(8,128)S(1)} %select_select_fusion.3), channel_id=1, source_target_pairs={{1,0},{2,3},{3,1},{0,2},{5,4},{6,7},{7,5},{4,6},{9,8},{10,11},{11,... | collective-permute-start | bytes 786440 | tf_op jit(solution)/shard_map/ppermute | solution.py:508
  28.3 11.4 %collective-permute-start.4 = (f32[128,512]{1,0:T(8,128)S(1)}, f32[128,512]{1,0:T(8,128)S(1)}, u32[]{:S(2)}, u32[]{:S(2)}) collective-permute-start(f32[128,512]{1,0:T(8,128)S(1)} %get-tuple-element.38.refs_2_), channel_id=1, source_target_pairs={{0,1},{1,2},{2,3},{3,0},{4,5},{5,6},{6,7},{7,4},{8,9},{9,10},{10,1... | collective-permute-start | bytes 786440 | tf_op jit(solution)/shard_map/ppermute | solution.py:494
  29.6 12.2 %collective-permute-start.3 = (f32[128,512]{1,0:T(8,128)S(1)}, f32[128,512]{1,0:T(8,128)S(1)}, u32[]{:S(2)}, u32[]{:S(2)}) collective-permute-start(f32[128,512]{1,0:T(8,128)S(1)} %get-tuple-element.38.refs_2_), channel_id=1, source_target_pairs={{0,3},{1,0},{2,1},{3,2},{4,7},{5,4},{6,5},{7,6},{8,11},{9,8},{10,9... | collective-permute-start | bytes 786440 | tf_op jit(solution)/shard_map/ppermute | solution.py:494
  35.9 13.6 %all-to-all-start.1 = ((f32[8,128,128]{2,1,0:T(8,128)}), f32[8,128,128]{2,1,0:T(8,128)S(1)}, u32[]{:S(2)}, u32[]{:S(2)}) async-start(f32[8,128,128]{2,1,0:T(8,128)} %product.8), calls=%async_computation.1 | async-start | bytes 1048576 | tf_op jit(solution)/shard_map/all_to_all | solution.py:498
  41.9 7.6 %collective-permute-start.5 = (f32[128,512]{1,0:T(8,128)S(1)}, f32[128,512]{1,0:T(8,128)S(1)}, u32[]{:S(2)}, u32[]{:S(2)}) collective-permute-start(f32[128,512]{1,0:T(8,128)S(1)} %select_select_fusion.2), channel_id=1, source_target_pairs={{1,0},{2,3},{3,1},{0,2},{5,4},{6,7},{7,5},{4,6},{9,8},{10,11},{11,... | collective-permute-start | bytes 786440 | tf_op jit(solution)/shard_map/ppermute | solution.py:508
  43.4 6.1 %copy-start = (s32[1,8,1]{1,2,0:T(1,128)S(1)}, s32[1,8,1]{1,2,0:T(1,128)}, u32[]{:S(2)}) copy-start(s32[1,8,1]{1,2,0:T(1,128)} %param.20) | copy-start | bytes 100
  50.2 13.2 %collective-permute-start.7 = (f32[176,512]{1,0:T(8,128)S(1)}, f32[176,512]{1,0:T(8,128)S(1)}, u32[]{:S(2)}, u32[]{:S(2)}) collective-permute-start(f32[176,512]{1,0:T(8,128)S(1)} %carry.2.refs_2_.refs_4_), channel_id=1, source_target_pairs={{0,1},{1,2},{2,3},{3,0},{4,5},{5,6},{6,7},{7,4},{8,9},{9,10},{10,1... | collective-permute-start | bytes 1081352 | tf_op jit(solution)/shard_map/ppermute | solution.py:494
  52.9 15.7 %collective-permute-start.6 = (f32[176,512]{1,0:T(8,128)S(1)}, f32[176,512]{1,0:T(8,128)S(1)}, u32[]{:S(2)}, u32[]{:S(2)}) collective-permute-start(f32[176,512]{1,0:T(8,128)S(1)} %carry.2.refs_2_.refs_4_), channel_id=1, source_target_pairs={{0,3},{1,0},{2,1},{3,2},{4,7},{5,4},{6,5},{7,6},{8,11},{9,8},{10,9... | collective-permute-start | bytes 1081352 | tf_op jit(solution)/shard_map/ppermute | solution.py:494
  58.2 21.0 %all-to-all-start.3 = ((f32[8,128,128]{2,1,0:T(8,128)}), f32[8,128,128]{2,1,0:T(8,128)S(1)}, u32[]{:S(2)}, u32[]{:S(2)}) async-start(f32[8,128,128]{2,1,0:T(8,128)} %product.11), calls=%async_computation.3 | async-start | bytes 1048576 | tf_op jit(solution)/shard_map/all_to_all | solution.py:498
  68.7 10.5 %collective-permute-start.8 = (f32[176,512]{1,0:T(8,128)S(1)}, f32[176,512]{1,0:T(8,128)S(1)}, u32[]{:S(2)}, u32[]{:S(2)}) collective-permute-start(f32[176,512]{1,0:T(8,128)S(1)} %select_select_fusion), channel_id=1, source_target_pairs={{1,0},{2,3},{3,1},{0,2},{5,4},{6,7},{7,5},{4,6},{9,8},{10,11},{11,... | collective-permute-start | bytes 1081352 | tf_op jit(solution)/shard_map/ppermute | solution.py:508
  79.9 12.0 %collective-permute-start.10 = (f32[128,512]{1,0:T(8,128)S(1)}, f32[128,512]{1,0:T(8,128)S(1)}, u32[]{:S(2)}, u32[]{:S(2)}) collective-permute-start(f32[128,512]{1,0:T(8,128)S(1)} %carry.3.refs_2_), channel_id=1, source_target_pairs={{0,1},{1,2},{2,3},{3,0},{4,5},{5,6},{6,7},{7,4},{8,9},{9,10},{10,1... | collective-permute-start | bytes 786440 | tf_op jit(solution)/shard_map/ppermute | solution.py:494
  81.4 12.2 %collective-permute-start.9 = (f32[128,512]{1,0:T(8,128)S(1)}, f32[128,512]{1,0:T(8,128)S(1)}, u32[]{:S(2)}, u32[]{:S(2)}) collective-permute-start(f32[128,512]{1,0:T(8,128)S(1)} %carry.3.refs_2_), channel_id=1, source_target_pairs={{0,3},{1,0},{2,1},{3,2},{4,7},{5,4},{6,5},{7,6},{8,11},{9,8},{10,9... | collective-permute-start | bytes 786440 | tf_op jit(solution)/shard_map/ppermute | solution.py:494
  87.8 18.1 %all-to-all-start.2 = ((f32[8,224,128]{2,1,0:T(8,128)}), f32[8,224,128]{2,1,0:T(8,128)S(1)}, u32[]{:S(2)}, u32[]{:S(2)}) async-start(f32[8,224,128]{2,1,0:T(8,128)} %product.10), calls=%async_computation.2 | async-start | bytes 1835008 | tf_op jit(solution)/shard_map/all_to_all | solution.py:498
  93.7 7.8 %collective-permute-start.11 = (f32[128,512]{1,0:T(8,128)S(1)}, f32[128,512]{1,0:T(8,128)S(1)}, u32[]{:S(2)}, u32[]{:S(2)}) collective-permute-start(f32[128,512]{1,0:T(8,128)S(1)} %select_select_fusion.1), channel_id=1, source_target_pairs={{1,0},{2,3},{3,1},{0,2},{5,4},{6,7},{7,5},{4,6},{9,8},{10,11},{11,... | collective-permute-start | bytes 786440 | tf_op jit(solution)/shard_map/ppermute | solution.py:508
  105.9 7.1 %collective-permute-start.12 = (f32[8,224,128]{2,1,0:T(8,128)S(1)}, f32[8,224,128]{2,1,0:T(8,128)S(1)}, u32[]{:S(2)}, u32[]{:S(2)}) collective-permute-start(f32[8,224,128]{2,1,0:T(8,128)S(1)} %all-to-all-done.2.own_ref.left_ref), channel_id=1, source_target_pairs={{0,4},{4,0},{8,12},{12,8},{16,20},{20,16},{24,28},{28,24},{1,5},{5... | collective-permute-start | bytes 2752520 | tf_op jit(solution)/shard_map/ppermute | solution.py:594
  105.9 2.9 %collective-permute-start.13 = (f32[128,128]{1,0:T(8,128)S(1)}, f32[128,128]{1,0:T(8,128)S(1)}, u32[]{:S(2)}, u32[]{:S(2)}) collective-permute-start(f32[128,128]{1,0:T(8,128)S(1)} %get-tuple-element.55), channel_id=1, source_target_pairs={{0,4},{4,0},{8,12},{12,8},{16,20},{20,16},{24,28},{28,24},{1,5},{5... | collective-permute-start | bytes 196616 | tf_op jit(solution)/shard_map/ppermute | solution.py:593
  106.4 4.3 %collective-permute-start.14 = (f32[128,128]{1,0:T(8,128)S(1)}, f32[128,128]{1,0:T(8,128)S(1)}, u32[]{:S(2)}, u32[]{:S(2)}) collective-permute-start(f32[128,128]{1,0:T(8,128)S(1)} %get-tuple-element.56), channel_id=1, source_target_pairs={{0,8},{4,12},{8,0},{12,4},{16,24},{20,28},{24,16},{28,20},{1,9},{5... | collective-permute-start | bytes 196616 | tf_op jit(solution)/shard_map/ppermute | solution.py:593
  107.9 6.9 %collective-permute-start.15 = (f32[128,128]{1,0:T(8,128)S(1)}, f32[128,128]{1,0:T(8,128)S(1)}, u32[]{:S(2)}, u32[]{:S(2)}) collective-permute-start(f32[128,128]{1,0:T(8,128)S(1)} %get-tuple-element.57), channel_id=1, source_target_pairs={{0,12},{4,8},{8,4},{12,0},{16,28},{20,24},{24,20},{28,16},{1,13},{... | collective-permute-start | bytes 196616 | tf_op jit(solution)/shard_map/ppermute | solution.py:593
  107.9 6.9 %collective-permute-start.16 = (f32[128,128]{1,0:T(8,128)S(1)}, f32[128,128]{1,0:T(8,128)S(1)}, u32[]{:S(2)}, u32[]{:S(2)}) collective-permute-start(f32[128,128]{1,0:T(8,128)S(1)} %get-tuple-element.58), channel_id=1, source_target_pairs={{0,16},{4,20},{8,24},{12,28},{16,0},{20,4},{24,8},{28,12},{1,17},{... | collective-permute-start | bytes 196616 | tf_op jit(solution)/shard_map/ppermute | solution.py:593
  108.8 6.0 %collective-permute-start.17 = (f32[128,128]{1,0:T(8,128)S(1)}, f32[128,128]{1,0:T(8,128)S(1)}, u32[]{:S(2)}, u32[]{:S(2)}) collective-permute-start(f32[128,128]{1,0:T(8,128)S(1)} %get-tuple-element.59), channel_id=1, source_target_pairs={{0,20},{4,16},{8,28},{12,24},{16,4},{20,0},{24,12},{28,8},{1,21},{... | collective-permute-start | bytes 196616 | tf_op jit(solution)/shard_map/ppermute | solution.py:593
  110.7 5.2 %collective-permute-start.18 = (f32[128,128]{1,0:T(8,128)S(1)}, f32[128,128]{1,0:T(8,128)S(1)}, u32[]{:S(2)}, u32[]{:S(2)}) collective-permute-start(f32[128,128]{1,0:T(8,128)S(1)} %get-tuple-element.60), channel_id=1, source_target_pairs={{0,24},{4,28},{8,16},{12,20},{16,8},{20,12},{24,0},{28,4},{1,25},{... | collective-permute-start | bytes 196616 | tf_op jit(solution)/shard_map/ppermute | solution.py:593
  113.0 4.6 %collective-permute-start.19 = (f32[128,128]{1,0:T(8,128)S(1)}, f32[128,128]{1,0:T(8,128)S(1)}, u32[]{:S(2)}, u32[]{:S(2)}) collective-permute-start(f32[128,128]{1,0:T(8,128)S(1)} %get-tuple-element.61), channel_id=1, source_target_pairs={{0,28},{4,24},{8,20},{12,16},{16,12},{20,8},{24,4},{28,0},{1,29},{... | collective-permute-start | bytes 196616 | tf_op jit(solution)/shard_map/ppermute | solution.py:593

commit v18 on v17

--- a/solution.py
+++ b/solution.py
@@ -286,7 +286,9 @@
 
 def product_kernel(n_row, n_col, origins, has_prev, last, n_carriers, has_base, apart, *refs):
     n = len(origins)
-    ids_ref, op_ref, refs = refs[0], refs[1], refs[2:]
+    if n_carriers or apart:
+        index_ref, refs = refs[0], refs[1:]
+    op_ref, refs = refs[0], refs[1:]
     fields, refs = refs[:n], refs[n:]
     if has_prev:
         prev_hbm, refs = refs[0], refs[1:]
@@ -317,7 +319,7 @@
     if n_carriers:
         ordered = refs[8]
         for k in range(n_col):
-            ordered[lax.rem(ids_ref[0] + k, n_col)] = carriers[k][H:, :]
+            ordered[lax.rem(index_ref[0] + k, n_col)] = carriers[k][H:, :]
         share = ordered[0]
         for k in range(1, n_col):
             share = share + ordered[k]
@@ -358,12 +360,12 @@
         base_copy.wait()
     if apart:
         for j, slot_ref in enumerate(slot_refs):
-            slot_ref[...] = out[ids_ref[1] ^ j]
+            slot_ref[...] = out[index_ref[0] ^ j]
     for item in sent:
         item.wait()
 
 
-def product(n_row, n_col, ids, origins, operator, fields, prev, last, carriers=(), base=None, prev_near=False, apart=False):
+def product(n_row, n_col, ids, row, origins, operator, fields, prev, last, carriers=(), base=None, prev_near=False, apart=False):
     n = len(origins)
     has_prev = prev is not None
     has_base = base is not None
@@ -382,6 +384,7 @@
     ]
     if carriers:
         scratch.append(pltpu.VMEM((n_col, rows, NODES_DEV), F32))
+    index = (ids,) if carriers else (row,) if apart else ()
     out = pltpu.HBM(shape, F32)
     out_specs, out_shape = HBM, out
     if has_base:
@@ -390,7 +393,7 @@
         out_specs, out_shape = [VMEM] * n_row, [jax.ShapeDtypeStruct((H, TB), F32)] * n_row
     return pl.pallas_call(
         functools.partial(product_kernel, n_row, n_col, origins, has_prev, last, len(carriers), has_base, apart),
-        in_specs=[SMEM, HBM] + [ANY] * (n + has_prev) + [VMEM] * len(carriers) + [HBM] * has_base,
+        in_specs=[SMEM] * len(index) + [HBM] + [ANY] * (n + has_prev) + [VMEM] * len(carriers) + [HBM] * has_base,
         out_specs=out_specs,
         out_shape=out_shape,
         scratch_shapes=scratch,
@@ -398,7 +401,7 @@
         cost_estimate=LIGHT if last else HEAVY,
         name="product",
     )(
-        ids,
+        *index,
         *in_hbm(operator),
         *fields,
         *((prev,) if prev_near else in_hbm(prev) if has_prev else ()),
@@ -435,19 +438,19 @@
     )(owners, base, came, *pieces)
 
 
-def finish_kernel(n_row, ids_ref, owners_ref, base_ref, left_ref, *refs):
+def finish_kernel(n_row, row_ref, owners_ref, base_ref, left_ref, *refs):
     right_refs, out_ref, total = refs[:n_row], refs[n_row], refs[n_row + 1]
     total[...] = base_ref[...]
     for q in range(n_row):
         here = pl.ds(pl.multiple_of(owners_ref[q] * TB, TB), TB)
         total[:H, here] += left_ref[q, :H, :]
     for j in range(n_row):
-        here = pl.ds(pl.multiple_of(owners_ref[ids_ref[1] ^ j] * TB, TB), TB)
+        here = pl.ds(pl.multiple_of(owners_ref[row_ref[0] ^ j] * TB, TB), TB)
         total[H:, here] += right_refs[j][...]
     out_ref[...] = total[...].T
 
 
-def finish(n_row, ids, owners, base, left, right):
+def finish(n_row, row, owners, base, left, right):
     return pl.pallas_call(
         functools.partial(finish_kernel, n_row),
         in_specs=[SMEM] * 2 + [VMEM] * (2 + n_row),
@@ -457,12 +460,12 @@
         compiler_params=params(24),
         cost_estimate=LIGHT,
         name="finish",
-    )(ids, owners, base, left, *right)
+    )(row, owners, base, left, *right)
 
 
 def assemble_kernel(n_row, row_ref, own_ref, other_ref, out_ref, halves, turned):
     rows = F // n_row
-    half = lax.rem(row_ref[1], 2)
+    half = lax.rem(row_ref[0], 2)
     halves[half] = own_ref[:, H:, :]
     halves[1 - half] = other_ref[:, H:, :]
     groups = 3 * F // LANES // 2
@@ -528,19 +531,19 @@
     return steps
 
 
-def early(n_row, n_col, ids, operator, steps, total=None, done=0, base=None):
+def early(n_row, n_col, ids, row, operator, steps, total=None, done=0, base=None):
     pairs = [pair for step in steps[:-1] for pair in step][done:]
     for begin in range(0, len(pairs), 3):
         origins, fields = zip(*pairs[begin : begin + 3])
         brought = base if begin + 3 >= len(pairs) else None
-        total = product(n_row, n_col, ids, origins, operator, fields, total, False, base=brought)
+        total = product(n_row, n_col, ids, row, origins, operator, fields, total, False, base=brought)
     return total
 
 
-def final(n_row, n_col, ids, operator, steps, total, carrying=False, near=False, apart=False):
+def final(n_row, n_col, ids, row, operator, steps, total, carrying=False, near=False, apart=False):
     origins, fields = zip(*steps[-1])
     carriers = [x for _, x in sorted((p for step in steps for p in step), key=lambda p: p[0])] if carrying else ()
-    return product(n_row, n_col, ids, origins, operator, fields, total, True, carriers, prev_near=near, apart=apart)
+    return product(n_row, n_col, ids, row, origins, operator, fields, total, True, carriers, prev_near=near, apart=apart)
 
 
 def per_device(
@@ -558,7 +561,8 @@
 ):
     n_row = lax.axis_size("row")
     n_col = lax.axis_size("col")
-    ids = jnp.stack([lax.axis_index("col"), lax.axis_index("row")]).astype(jnp.int32)
+    ids = lax.axis_index("col").astype(jnp.int32).reshape(1)
+    row = lax.axis_index("row").astype(jnp.int32).reshape(1)
     owners = send_blocks.reshape(n_row)
     left, right = term_two(grad_out, relu_mask, cheb_weight)
     one_left, one_right, diff, pieces = local_terms(
@@ -570,7 +574,7 @@
         n_row, n_col, ids, live_tiles, tile_rows, tile_slots, tile_values, first
     )
     pieces = exchange(pieces)
-    common = (n_row, n_col, ids, operator)
+    common = (n_row, n_col, ids, row, operator)
 
     left_early = early(*common, steps, left_early, len(first))
     right_steps = gather(n_col, after(right, left_early, steps[-1][0][1]), -1)
@@ -592,8 +596,8 @@
     for j in range(n_row - 1, 0, -1):
         right_came[j] = lax.ppermute(right_last[j], "row", [(r, r ^ j) for r in range(n_row)])
     other = lax.ppermute(after(left_came, right_last[0]), "row", [(r, r ^ 1) for r in range(n_row)])
-    weight_grad = assemble(n_row, ids, left_came, other)
-    return finish(n_row, ids, owners, after(diff, weight_grad), left_came, right_came), weight_grad
+    weight_grad = assemble(n_row, row, left_came, other)
+    return finish(n_row, row, owners, after(diff, weight_grad), left_came, right_came), weight_grad
 
 
 def solution(mesh):

time: 121 us -> 119 us (0.983)
  waiting for transfers between devices: 21.4 us -> 27 us
  Pallas kernels: 52.8 us -> 47.9 us
  starting transfers between devices: 43.4 us -> 41.4 us
    pallas_call x7, Pallas kernels: 33.5 us -> 29.7 us  [product(): pl.pallas_call(functools.partial(product_kernel, n_row, n_col, origins, h...]
    ppermute x8, waiting for transfers between devices: 13.1 us -> 16.2 us  [shift(): lax.ppermute(x, 'col', [(c, (c + step) % n_col) for c in range(n_col)])]
    ppermute x4, waiting for transfers between devices: 3.73 us -> 5.53 us  [opposite(): return lax.ppermute(sent, 'col', [(1, 0), (2, 3), (3, 1), (0, 2)])]
    ppermute x7, waiting for transfers between devices: 3.57 us -> 4.87 us  [per_device(): lax.ppermute(right_last[j], 'row', [(r, r ^ j) for r in range(n_row)])]
  transfers between devices with their start and end apart: 24 -> 24, of which waited for: 11 -> 15; matrix products, arithmetic and copies ran while one was open for 0% -> 0% of each run, Pallas kernels for 40% -> 36%
where the time goes in v18:
time: 119 us; the launch traced here: 118 us
  Pallas kernels  47.9 us (40%)
  starting transfers between devices  41.4 us (35%)
  waiting for transfers between devices  27 us (23%)
  between operations  1.43 us (1%)
    pallas_call x7, Pallas kernels, product(): pl.pallas_call(functools.partial(product_kernel, n_row, n_col, origins, h...  29.7 us
    ppermute x8, starting transfers between devices, shift(): lax.ppermute(x, 'col', [(c, (c + step) % n_col) for c in range(n_col)])  16.7 us
    ppermute x8, waiting for transfers between devices, shift(): lax.ppermute(x, 'col', [(c, (c + step) % n_col) for c in range(n_col)])  16.2 us
    all_to_all x4, starting transfers between devices, exchange(): lax.all_to_all(pieces, 'row', split_axis=0, concat_axis=0, tiled=True)  14.7 us
    pallas_call x1, Pallas kernels, build_operator(): pl.pallas_call(functools.partial(operator_kernel, n_row, n_col, origins),...  7.28 us
    ppermute x7, starting transfers between devices, per_device(): lax.ppermute(right_last[j], 'row', [(r, r ^ j) for r in range(n_row)])  5.53 us
    ppermute x4, waiting for transfers between devices, opposite(): return lax.ppermute(sent, 'col', [(1, 0), (2, 3), (3, 1), (0, 2)])  5.53 us
    pallas_call x1, Pallas kernels, local_terms(): pl.pallas_call(functools.partial(local_kernel, n_row), in_specs=[ANY] + [...  4.88 us
  transfers between devices with their start and end apart: 24, of which 15 were waited for; matrix products, arithmetic and copies ran while one was open for 0% of the time, Pallas kernels for 36%

profile of v18, /device:TPU:0, one launch (start us, length us, event | category | flops | bytes accessed | tf_op | source)
XLA Modules:
  0.0 118.0 jit_solution(4871191716139836240)
XLA Ops:
  0.6 1.7 %term_two.1 = (f32[128,512]{1,0:T(8,128)S(1)}, f32[128,512]{1,0:T(8,128)S(1)}) custom-call(f32[512,256]{1,0:T(8,128)} %grad_hbm.3, s32[512,256]{1,0:T(8,128)} %mask_hbm.3, f32[3,256,256]{2,1,0:T(8,128)} %weight_hbm.3), custom_call_target="tpu_custom_call" | custom-call | flops 1024 | bytes 1024 | tf_op jit(solution)/shard_map/term_two/pallas_call | solution.py:78
  2.4 5.1 %collective-permute-start.1 = (f32[128,512]{1,0:T(8,128)S(1)}, f32[128,512]{1,0:T(8,128)S(1)}, u32[]{:S(2)}, u32[]{:S(2)}) collective-permute-start(f32[128,512]{1,0:T(8,128)S(1)} %get-tuple-element.32.first_ref.refs_0_), channel_id=1, source_target_pairs={{0,3},{1,0},{2,1},{3,2},{4,7},{5,4},{6,5},{7,6},{8,11},{9,8},{10,9... | collective-permute-start | bytes 786440 | tf_op jit(solution)/shard_map/ppermute | solution.py:497
  7.5 0.0 collective-permute-start
  7.5 4.9 %local_terms.1 = (f32[128,512]{1,0:T(8,128)}, f32[128,512]{1,0:T(8,128)}, f32[256,512]{1,0:T(8,128)S(1)}, f32[8,192,128]{2,1,0:T(8,128)}) custom-call(f32[128,512]{1,0:T(8,128)S(1)} %get-tuple-element.32.first_ref.refs_0_, f32[512,256]{1,0:T(8,128)} %grad_hbm.3, s32[512,256]{1,0:T(8,128)} %mask_hbm.3, f32[3,256,256]{2,1,0:T(8,128)} %weight_hbm.3, ...), custom_call_target="tpu_custom_call" | custom-call | flops 1024 | bytes 1024 | tf_op jit(solution)/shard_map/local_terms/pallas_call | solution.py:125
  12.4 3.7 %all-to-all-start = ((f32[8,192,128]{2,1,0:T(8,128)}), f32[8,192,128]{2,1,0:T(8,128)S(1)}, u32[]{:S(2)}, u32[]{:S(2)}) async-start(f32[8,192,128]{2,1,0:T(8,128)} %get-tuple-element.44), calls=%async_computation | async-start | bytes 1572864 | tf_op jit(solution)/shard_map/all_to_all | solution.py:501
  16.8 0.0 collective-permute-done.1.refs_2_
  16.8 2.8 %collective-permute-done.refs_1_ = f32[128,512]{1,0:T(8,128)S(1)} collective-permute-done((f32[128,512]{1,0:T(8,128)S(1)}, f32[128,512]{1,0:T(8,128)S(1)}, u32[]{:S(2)}, u32[]{:S(2)}) %collective-permute-start) | collective-permute-done | bytes 262176 | tf_op jit(solution)/shard_map/ppermute | solution.py:497
  19.6 0.1 select_select_fusion.3
  19.6 0.8 collective-permute-start.2
  20.4 7.3 %operator.1 = (bf16[4,4,1024,256]{3,2,1,0:T(8,128)(2,1)}, f32[128,1024]{1,0:T(8,128)S(1)}) custom-call(s32[1]{0:T(128)} %bitcast.2.ids_ref.refs_0_, s32[1]{0:T(128)S(6)} %copy.13.live_ref, s32[1,128]{1,0:T(1,128)} %rows_hbm.1, s32[1,128]{1,0:T(1,128)} %slots_hbm.1, f32[1,128,128,128]{3,2,1,0:T(8,128)} %values_ref.1, ...), custom_call_target="tpu_custom_call" | custom-call | flops 17179869184 | bytes 67108864 | tf_op jit(solution)/shard_map/operator/pallas_call | solution.py:262
  27.7 1.7 %collective-permute-start.4 = (f32[128,512]{1,0:T(8,128)S(1)}, f32[128,512]{1,0:T(8,128)S(1)}, u32[]{:S(2)}, u32[]{:S(2)}) collective-permute-start(f32[128,512]{1,0:T(8,128)S(1)} %get-tuple-element.38.refs_1_), channel_id=1, source_target_pairs={{0,1},{1,2},{2,3},{3,0},{4,5},{5,6},{6,7},{7,4},{8,9},{9,10},{10,1... | collective-permute-start | bytes 786440 | tf_op jit(solution)/shard_map/ppermute | solution.py:497
  29.4 2.2 %collective-permute-start.3 = (f32[128,512]{1,0:T(8,128)S(1)}, f32[128,512]{1,0:T(8,128)S(1)}, u32[]{:S(2)}, u32[]{:S(2)}) collective-permute-start(f32[128,512]{1,0:T(8,128)S(1)} %get-tuple-element.38.refs_1_), channel_id=1, source_target_pairs={{0,3},{1,0},{2,1},{3,2},{4,7},{5,4},{6,5},{7,6},{8,11},{9,8},{10,9... | collective-permute-start | bytes 786440 | tf_op jit(solution)/shard_map/ppermute | solution.py:497
  31.6 3.2 %product.8 = f32[8,128,128]{2,1,0:T(8,128)} custom-call(bf16[4,4,1024,256]{3,2,1,0:T(8,128)(2,1)} %get-tuple-element.34.refs_0_.refs_1_, f32[128,512]{1,0:T(8,128)S(1)} %collective-permute-done.2.refs_1_, f32[128,1024]{1,0:T(8,128)S(1)} %get-tuple-element.45.refs_2_), custom_call_target="tpu_custom_call" | custom-call | flops 1024 | bytes 1024 | tf_op jit(solution)/shard_map/product/pallas_call | solution.py:394
  34.8 3.7 %all-to-all-start.1 = ((f32[8,128,128]{2,1,0:T(8,128)}), f32[8,128,128]{2,1,0:T(8,128)S(1)}, u32[]{:S(2)}, u32[]{:S(2)}) async-start(f32[8,128,128]{2,1,0:T(8,128)} %product.8), calls=%async_computation.1 | async-start | bytes 1048576 | tf_op jit(solution)/shard_map/all_to_all | solution.py:501
  38.6 0.2 collective-permute-done.4.refs_3_
  38.8 2.6 %collective-permute-done.3.refs_2_ = f32[128,512]{1,0:T(8,128)S(1)} collective-permute-done((f32[128,512]{1,0:T(8,128)S(1)}, f32[128,512]{1,0:T(8,128)S(1)}, u32[]{:S(2)}, u32[]{:S(2)}) %collective-permute-start.3) | collective-permute-done | bytes 262176 | tf_op jit(solution)/shard_map/ppermute | solution.py:497
  41.4 0.1 select_select_fusion.2
  41.5 1.5 %collective-permute-start.5 = (f32[128,512]{1,0:T(8,128)S(1)}, f32[128,512]{1,0:T(8,128)S(1)}, u32[]{:S(2)}, u32[]{:S(2)}) collective-permute-start(f32[128,512]{1,0:T(8,128)S(1)} %select_select_fusion.2), channel_id=1, source_target_pairs={{1,0},{2,3},{3,1},{0,2},{5,4},{6,7},{7,5},{4,6},{9,8},{10,11},{11,... | collective-permute-start | bytes 786440 | tf_op jit(solution)/shard_map/ppermute | solution.py:511
  43.0 5.5 %product.7 = (f32[128,1024]{1,0:T(8,128)}, f32[128,512]{1,0:T(8,128)S(1)}) custom-call(bf16[4,4,1024,256]{3,2,1,0:T(8,128)(2,1)} %get-tuple-element.34.refs_0_.refs_1_, f32[128,512]{1,0:T(8,128)S(1)} %get-tuple-element.38.refs_1_, f32[128,512]{1,0:T(8,128)S(1)} %collective-permute-done.3.refs_2_, f32[128,512]{1,0:T(8,128)S(1)} %collective-permute-done.4.refs_3_, ...), custom_call_target="tpu_custom_call" | custom-call | flops 17179869184 | bytes 67108864 | tf_op jit(solution)/shard_map/product/pallas_call | solution.py:394
  48.5 0.7 collective-permute-done.5.refs_1_
  49.2 0.0 all-to-all-done.1.came_ref
  49.2 0.7 carry.2.refs_1_.refs_4_
  49.9 2.5 %collective-permute-start.7 = (f32[176,512]{1,0:T(8,128)S(1)}, f32[176,512]{1,0:T(8,128)S(1)}, u32[]{:S(2)}, u32[]{:S(2)}) collective-permute-start(f32[176,512]{1,0:T(8,128)S(1)} %carry.2.refs_1_.refs_4_), channel_id=1, source_target_pairs={{0,1},{1,2},{2,3},{3,0},{4,5},{5,6},{6,7},{7,4},{8,9},{9,10},{10,1... | collective-permute-start | bytes 1081352 | tf_op jit(solution)/shard_map/ppermute | solution.py:497
  52.4 1.4 %collective-permute-start.6 = (f32[176,512]{1,0:T(8,128)S(1)}, f32[176,512]{1,0:T(8,128)S(1)}, u32[]{:S(2)}, u32[]{:S(2)}) collective-permute-start(f32[176,512]{1,0:T(8,128)S(1)} %carry.2.refs_1_.refs_4_), channel_id=1, source_target_pairs={{0,3},{1,0},{2,1},{3,2},{4,7},{5,4},{6,5},{7,6},{8,11},{9,8},{10,9... | collective-permute-start | bytes 1081352 | tf_op jit(solution)/shard_map/ppermute | solution.py:497
  53.8 3.5 %product.11 = f32[8,128,128]{2,1,0:T(8,128)} custom-call(bf16[4,4,1024,256]{3,2,1,0:T(8,128)(2,1)} %get-tuple-element.34.refs_0_.refs_1_, f32[128,512]{1,0:T(8,128)S(1)} %collective-permute-done.5.refs_1_, f32[128,1024]{1,0:T(8,128)} %get-tuple-element.41.refs_2_), custom_call_target="tpu_custom_call" | custom-call | flops 1024 | bytes 1024 | tf_op jit(solution)/shard_map/product/pallas_call | solution.py:394
  57.3 3.6 %all-to-all-start.3 = ((f32[8,128,128]{2,1,0:T(8,128)}), f32[8,128,128]{2,1,0:T(8,128)S(1)}, u32[]{:S(2)}, u32[]{:S(2)}) async-start(f32[8,128,128]{2,1,0:T(8,128)} %product.11), calls=%async_computation.3 | async-start | bytes 1048576 | tf_op jit(solution)/shard_map/all_to_all | solution.py:501
  60.9 2.2 %collective-permute-done.7.refs_2_.refs_7_ = f32[176,512]{1,0:T(8,128)S(1)} collective-permute-done((f32[176,512]{1,0:T(8,128)S(1)}, f32[176,512]{1,0:T(8,128)S(1)}, u32[]{:S(2)}, u32[]{:S(2)}) %collective-permute-start.7) | collective-permute-done | bytes 360480 | tf_op jit(solution)/shard_map/ppermute | solution.py:497
  63.1 5.2 %collective-permute-done.6.refs_3_.refs_5_ = f32[176,512]{1,0:T(8,128)S(1)} collective-permute-done((f32[176,512]{1,0:T(8,128)S(1)}, f32[176,512]{1,0:T(8,128)S(1)}, u32[]{:S(2)}, u32[]{:S(2)}) %collective-permute-start.6) | collective-permute-done | bytes 360480 | tf_op jit(solution)/shard_map/ppermute | solution.py:497
  68.3 0.1 select_select_fusion
  68.4 0.8 collective-permute-start.8
  69.3 5.5 %product.9 = (f32[128,1024]{1,0:T(8,128)}, f32[128,512]{1,0:T(8,128)S(1)}) custom-call(bf16[4,4,1024,256]{3,2,1,0:T(8,128)(2,1)} %get-tuple-element.34.refs_0_.refs_1_, f32[176,512]{1,0:T(8,128)S(1)} %carry.2.refs_1_.refs_4_, f32[176,512]{1,0:T(8,128)S(1)} %collective-permute-done.7.refs_2_.refs_7_, f32[176,512]{1,0:T(8,128)S(1)} %collective-permute-done.6.refs_3_.refs_5_, ...), custom_call_target="tpu_custom_call" | custom-call | flops 17179869184 | bytes 67108864 | tf_op jit(solution)/shard_map/product/pallas_call | solution.py:394
  74.8 4.2 %collective-permute-done.8.refs_2_.refs_6_ = f32[176,512]{1,0:T(8,128)S(1)} collective-permute-done((f32[176,512]{1,0:T(8,128)S(1)}, f32[176,512]{1,0:T(8,128)S(1)}, u32[]{:S(2)}, u32[]{:S(2)}) %collective-permute-start.8) | collective-permute-done | bytes 360480 | tf_op jit(solution)/shard_map/ppermute | solution.py:511
  79.0 0.0 all-to-all-done.3.came_ref
  79.0 0.7 carry.3.refs_1_
  79.6 1.5 %collective-permute-start.10 = (f32[128,512]{1,0:T(8,128)S(1)}, f32[128,512]{1,0:T(8,128)S(1)}, u32[]{:S(2)}, u32[]{:S(2)}) collective-permute-start(f32[128,512]{1,0:T(8,128)S(1)} %carry.3.refs_1_), channel_id=1, source_target_pairs={{0,1},{1,2},{2,3},{3,0},{4,5},{5,6},{6,7},{7,4},{8,9},{9,10},{10,1... | collective-permute-start | bytes 786440 | tf_op jit(solution)/shard_map/ppermute | solution.py:497
  81.2 2.3 %collective-permute-start.9 = (f32[128,512]{1,0:T(8,128)S(1)}, f32[128,512]{1,0:T(8,128)S(1)}, u32[]{:S(2)}, u32[]{:S(2)}) collective-permute-start(f32[128,512]{1,0:T(8,128)S(1)} %carry.3.refs_1_), channel_id=1, source_target_pairs={{0,3},{1,0},{2,1},{3,2},{4,7},{5,4},{6,5},{7,6},{8,11},{9,8},{10,9... | collective-permute-start | bytes 786440 | tf_op jit(solution)/shard_map/ppermute | solution.py:497
  83.5 3.5 %product.10 = f32[8,224,128]{2,1,0:T(8,128)} custom-call(s32[1]{0:T(128)} %bitcast.2.ids_ref.refs_0_, bf16[4,4,1024,256]{3,2,1,0:T(8,128)(2,1)} %get-tuple-element.34.refs_0_.refs_1_, f32[176,512]{1,0:T(8,128)S(1)} %collective-permute-done.8.refs_2_.refs_6_, f32[128,1024]{1,0:T(8,128)} %get-tuple-element.48.refs_3_, f32[176,512]{1,0:T(8,128)S(1)} %carry.2.refs_1_.refs_4_, ...), custom_call_target="tpu_custom_call" | custom-call | flops 1024 | bytes 1024 | tf_op jit(solution)/shard_map/product/pallas_call | solution.py:394
  87.1 3.6 %all-to-all-start.2 = ((f32[8,224,128]{2,1,0:T(8,128)}), f32[8,224,128]{2,1,0:T(8,128)S(1)}, u32[]{:S(2)}, u32[]{:S(2)}) async-start(f32[8,224,128]{2,1,0:T(8,128)} %product.10), calls=%async_computation.2 | async-start | bytes 1835008 | tf_op jit(solution)/shard_map/all_to_all | solution.py:501
  90.6 0.1 collective-permute-done.10.refs_3_
  90.7 3.0 %collective-permute-done.9.refs_2_ = f32[128,512]{1,0:T(8,128)S(1)} collective-permute-done((f32[128,512]{1,0:T(8,128)S(1)}, f32[128,512]{1,0:T(8,128)S(1)}, u32[]{:S(2)}, u32[]{:S(2)}) %collective-permute-start.9) | collective-permute-done | bytes 262176 | tf_op jit(solution)/shard_map/ppermute | solution.py:497
  93.7 0.1 select_select_fusion.1
  93.8 1.4 %collective-permute-start.11 = (f32[128,512]{1,0:T(8,128)S(1)}, f32[128,512]{1,0:T(8,128)S(1)}, u32[]{:S(2)}, u32[]{:S(2)}) collective-permute-start(f32[128,512]{1,0:T(8,128)S(1)} %select_select_fusion.1), channel_id=1, source_target_pairs={{1,0},{2,3},{3,1},{0,2},{5,4},{6,7},{7,5},{4,6},{9,8},{10,11},{11,... | collective-permute-start | bytes 786440 | tf_op jit(solution)/shard_map/ppermute | solution.py:511
  95.1 5.5 %product.12.refs_3_ = f32[128,1024]{1,0:T(8,128)} custom-call(bf16[4,4,1024,256]{3,2,1,0:T(8,128)(2,1)} %get-tuple-element.34.refs_0_.refs_1_, f32[128,512]{1,0:T(8,128)S(1)} %carry.3.refs_1_, f32[128,512]{1,0:T(8,128)S(1)} %collective-permute-done.9.refs_2_, f32[128,512]{1,0:T(8,128)S(1)} %collective-permute-done.10.refs_3_), custom_call_target="tpu_custom_call" | custom-call | flops 17179869184 | bytes 67108864 | tf_op jit(solution)/shard_map/product/pallas_call | solution.py:394
  100.6 0.6 collective-permute-done.11.refs_2_
  101.2 2.9 %product.13 = (f32[128,128]{1,0:T(8,128)S(1)}, f32[128,128]{1,0:T(8,128)S(1)}, f32[128,128]{1,0:T(8,128)S(1)}, f32[128,128]{1,0:T(8,128)S(1)}, f32[128,128]{1,0:...) custom-call(s32[1]{0:T(128)} %bitcast.refs_0_.row_ref, ...), custom_call_target="tpu_custom_call" | custom-call | flops 1024 | bytes 1024 | tf_op jit(solution)/shard_map/product/pallas_call | solution.py:394
  104.1 0.5 all-to-all-done.2.own_ref.left_ref
  104.6 0.0 collective-permute-start.12
  104.6 0.5 collective-permute-start.13
  105.1 1.0 collective-permute-start.14
  106.2 0.3 collective-permute-start.15
  106.5 1.0 collective-permute-start.16
  107.5 0.0 collective-permute-done.13.refs_1_
  107.5 1.2 collective-permute-start.17
  108.6 1.1 collective-permute-done.14.refs_2_
  109.7 1.5 %collective-permute-start.18 = (f32[128,128]{1,0:T(8,128)S(1)}, f32[128,128]{1,0:T(8,128)S(1)}, u32[]{:S(2)}, u32[]{:S(2)}) collective-permute-start(f32[128,128]{1,0:T(8,128)S(1)} %get-tuple-element.60), channel_id=1, source_target_pairs={{0,24},{4,28},{8,16},{12,20},{16,8},{20,12},{24,0},{28,4},{1,25},{... | collective-permute-start | bytes 196616 | tf_op jit(solution)/shard_map/ppermute | solution.py:597
  111.3 0.0 collective-permute-done.12.other_ref
  111.3 0.0 collective-permute-start.19
  111.3 1.2 %assemble.1 = f32[3,256,256]{2,1,0:T(8,128)} custom-call(s32[1]{0:T(128)} %bitcast.refs_0_.row_ref, f32[8,224,128]{2,1,0:T(8,128)S(1)} %all-to-all-done.2.own_ref.left_ref, f32[8,224,128]{2,1,0:T(8,128)S(1)} %collective-permute-done.12.other_ref), custom_call_target="tpu_custom_call" | custom-call | flops 1024 | bytes 1024 | tf_op jit(solution)/shard_map/assemble/pallas_call | solution.py:481
  112.5 0.0 collective-permute-done.15.refs_3_
  112.5 0.0 collective-permute-done.16.refs_4_
  112.5 0.7 collective-permute-done.17.refs_5_
  113.2 1.7 %collective-permute-done.18.refs_6_ = f32[128,128]{1,0:T(8,128)S(1)} collective-permute-done((f32[128,128]{1,0:T(8,128)S(1)}, f32[128,128]{1,0:T(8,128)S(1)}, u32[]{:S(2)}, u32[]{:S(2)}) %collective-permute-start.18) | collective-permute-done | bytes 65568 | tf_op jit(solution)/shard_map/ppermute | solution.py:597
  114.9 1.4 %collective-permute-done.19.refs_7_ = f32[128,128]{1,0:T(8,128)S(1)} collective-permute-done((f32[128,128]{1,0:T(8,128)S(1)}, f32[128,128]{1,0:T(8,128)S(1)}, u32[]{:S(2)}, u32[]{:S(2)}) %collective-permute-start.19) | collective-permute-done | bytes 65568 | tf_op jit(solution)/shard_map/ppermute | solution.py:597
  116.3 1.8 %finish.1 = f32[512,256]{1,0:T(8,128)} custom-call(s32[1]{0:T(128)} %bitcast.refs_0_.row_ref, s32[8]{0:T(128)S(1)} %bitcast.5, f32[256,512]{1,0:T(8,128)S(1)} %get-tuple-element.54.base_ref, f32[8,224,128]{2,1,0:T(8,128)S(1)} %all-to-all-done.2.own_ref.left_ref, f32[128,128]{1,0:T(8,128)S(1)} %get-tuple-element.52.refs_0_, ...), custom_call_target="tpu_custom_call" | custom-call | flops 1024 | bytes 1024 | tf_op jit(solution)/shard_map/finish/pallas_call | solution.py:454
  (4 shorter events, 0.0 us)
Async XLA Ops:
  2.4 14.4 %collective-permute-start.1 = (f32[128,512]{1,0:T(8,128)S(1)}, f32[128,512]{1,0:T(8,128)S(1)}, u32[]{:S(2)}, u32[]{:S(2)}) collective-permute-start(f32[128,512]{1,0:T(8,128)S(1)} %get-tuple-element.32.first_ref.refs_0_), channel_id=1, source_target_pairs={{0,3},{1,0},{2,1},{3,2},{4,7},{5,4},{6,5},{7,6},{8,11},{9,8},{10,9... | collective-permute-start | bytes 786440 | tf_op jit(solution)/shard_map/ppermute | solution.py:497
  7.5 12.1 %collective-permute-start = (f32[128,512]{1,0:T(8,128)S(1)}, f32[128,512]{1,0:T(8,128)S(1)}, u32[]{:S(2)}, u32[]{:S(2)}) collective-permute-start(f32[128,512]{1,0:T(8,128)S(1)} %get-tuple-element.32.first_ref.refs_0_), channel_id=1, source_target_pairs={{0,1},{1,2},{2,3},{3,0},{4,5},{5,6},{6,7},{7,4},{8,9},{9,10},{10,1... | collective-permute-start | bytes 786440 | tf_op jit(solution)/shard_map/ppermute | solution.py:497
  12.4 19.2 %all-to-all-start = ((f32[8,192,128]{2,1,0:T(8,128)}), f32[8,192,128]{2,1,0:T(8,128)S(1)}, u32[]{:S(2)}, u32[]{:S(2)}) async-start(f32[8,192,128]{2,1,0:T(8,128)} %get-tuple-element.44), calls=%async_computation | async-start | bytes 1572864 | tf_op jit(solution)/shard_map/all_to_all | solution.py:501
  19.6 8.1 %collective-permute-start.2 = (f32[128,512]{1,0:T(8,128)S(1)}, f32[128,512]{1,0:T(8,128)S(1)}, u32[]{:S(2)}, u32[]{:S(2)}) collective-permute-start(f32[128,512]{1,0:T(8,128)S(1)} %select_select_fusion.3), channel_id=1, source_target_pairs={{1,0},{2,3},{3,1},{0,2},{5,4},{6,7},{7,5},{4,6},{9,8},{10,11},{11,... | collective-permute-start | bytes 786440 | tf_op jit(solution)/shard_map/ppermute | solution.py:511
  27.7 11.1 %collective-permute-start.4 = (f32[128,512]{1,0:T(8,128)S(1)}, f32[128,512]{1,0:T(8,128)S(1)}, u32[]{:S(2)}, u32[]{:S(2)}) collective-permute-start(f32[128,512]{1,0:T(8,128)S(1)} %get-tuple-element.38.refs_1_), channel_id=1, source_target_pairs={{0,1},{1,2},{2,3},{3,0},{4,5},{5,6},{6,7},{7,4},{8,9},{9,10},{10,1... | collective-permute-start | bytes 786440 | tf_op jit(solution)/shard_map/ppermute | solution.py:497
  29.4 12.0 %collective-permute-start.3 = (f32[128,512]{1,0:T(8,128)S(1)}, f32[128,512]{1,0:T(8,128)S(1)}, u32[]{:S(2)}, u32[]{:S(2)}) collective-permute-start(f32[128,512]{1,0:T(8,128)S(1)} %get-tuple-element.38.refs_1_), channel_id=1, source_target_pairs={{0,3},{1,0},{2,1},{3,2},{4,7},{5,4},{6,5},{7,6},{8,11},{9,8},{10,9... | collective-permute-start | bytes 786440 | tf_op jit(solution)/shard_map/ppermute | solution.py:497
  34.8 14.3 %all-to-all-start.1 = ((f32[8,128,128]{2,1,0:T(8,128)}), f32[8,128,128]{2,1,0:T(8,128)S(1)}, u32[]{:S(2)}, u32[]{:S(2)}) async-start(f32[8,128,128]{2,1,0:T(8,128)} %product.8), calls=%async_computation.1 | async-start | bytes 1048576 | tf_op jit(solution)/shard_map/all_to_all | solution.py:501
  41.5 7.7 %collective-permute-start.5 = (f32[128,512]{1,0:T(8,128)S(1)}, f32[128,512]{1,0:T(8,128)S(1)}, u32[]{:S(2)}, u32[]{:S(2)}) collective-permute-start(f32[128,512]{1,0:T(8,128)S(1)} %select_select_fusion.2), channel_id=1, source_target_pairs={{1,0},{2,3},{3,1},{0,2},{5,4},{6,7},{7,5},{4,6},{9,8},{10,11},{11,... | collective-permute-start | bytes 786440 | tf_op jit(solution)/shard_map/ppermute | solution.py:511
  43.0 6.2 %copy-start = (s32[1,8,1]{1,2,0:T(1,128)S(1)}, s32[1,8,1]{1,2,0:T(1,128)}, u32[]{:S(2)}) copy-start(s32[1,8,1]{1,2,0:T(1,128)} %param.20) | copy-start | bytes 100
  49.9 13.2 %collective-permute-start.7 = (f32[176,512]{1,0:T(8,128)S(1)}, f32[176,512]{1,0:T(8,128)S(1)}, u32[]{:S(2)}, u32[]{:S(2)}) collective-permute-start(f32[176,512]{1,0:T(8,128)S(1)} %carry.2.refs_1_.refs_4_), channel_id=1, source_target_pairs={{0,1},{1,2},{2,3},{3,0},{4,5},{5,6},{6,7},{7,4},{8,9},{9,10},{10,1... | collective-permute-start | bytes 1081352 | tf_op jit(solution)/shard_map/ppermute | solution.py:497
  52.4 16.0 %collective-permute-start.6 = (f32[176,512]{1,0:T(8,128)S(1)}, f32[176,512]{1,0:T(8,128)S(1)}, u32[]{:S(2)}, u32[]{:S(2)}) collective-permute-start(f32[176,512]{1,0:T(8,128)S(1)} %carry.2.refs_1_.refs_4_), channel_id=1, source_target_pairs={{0,3},{1,0},{2,1},{3,2},{4,7},{5,4},{6,5},{7,6},{8,11},{9,8},{10,9... | collective-permute-start | bytes 1081352 | tf_op jit(solution)/shard_map/ppermute | solution.py:497
  57.3 21.7 %all-to-all-start.3 = ((f32[8,128,128]{2,1,0:T(8,128)}), f32[8,128,128]{2,1,0:T(8,128)S(1)}, u32[]{:S(2)}, u32[]{:S(2)}) async-start(f32[8,128,128]{2,1,0:T(8,128)} %product.11), calls=%async_computation.3 | async-start | bytes 1048576 | tf_op jit(solution)/shard_map/all_to_all | solution.py:501
  68.4 10.5 %collective-permute-start.8 = (f32[176,512]{1,0:T(8,128)S(1)}, f32[176,512]{1,0:T(8,128)S(1)}, u32[]{:S(2)}, u32[]{:S(2)}) collective-permute-start(f32[176,512]{1,0:T(8,128)S(1)} %select_select_fusion), channel_id=1, source_target_pairs={{1,0},{2,3},{3,1},{0,2},{5,4},{6,7},{7,5},{4,6},{9,8},{10,11},{11,... | collective-permute-start | bytes 1081352 | tf_op jit(solution)/shard_map/ppermute | solution.py:511
  79.6 11.1 %collective-permute-start.10 = (f32[128,512]{1,0:T(8,128)S(1)}, f32[128,512]{1,0:T(8,128)S(1)}, u32[]{:S(2)}, u32[]{:S(2)}) collective-permute-start(f32[128,512]{1,0:T(8,128)S(1)} %carry.3.refs_1_), channel_id=1, source_target_pairs={{0,1},{1,2},{2,3},{3,0},{4,5},{5,6},{6,7},{7,4},{8,9},{9,10},{10,1... | collective-permute-start | bytes 786440 | tf_op jit(solution)/shard_map/ppermute | solution.py:497
  81.2 12.6 %collective-permute-start.9 = (f32[128,512]{1,0:T(8,128)S(1)}, f32[128,512]{1,0:T(8,128)S(1)}, u32[]{:S(2)}, u32[]{:S(2)}) collective-permute-start(f32[128,512]{1,0:T(8,128)S(1)} %carry.3.refs_1_), channel_id=1, source_target_pairs={{0,3},{1,0},{2,1},{3,2},{4,7},{5,4},{6,5},{7,6},{8,11},{9,8},{10,9... | collective-permute-start | bytes 786440 | tf_op jit(solution)/shard_map/ppermute | solution.py:497
  87.1 17.6 %all-to-all-start.2 = ((f32[8,224,128]{2,1,0:T(8,128)}), f32[8,224,128]{2,1,0:T(8,128)S(1)}, u32[]{:S(2)}, u32[]{:S(2)}) async-start(f32[8,224,128]{2,1,0:T(8,128)} %product.10), calls=%async_computation.2 | async-start | bytes 1835008 | tf_op jit(solution)/shard_map/all_to_all | solution.py:501
  93.8 7.5 %collective-permute-start.11 = (f32[128,512]{1,0:T(8,128)S(1)}, f32[128,512]{1,0:T(8,128)S(1)}, u32[]{:S(2)}, u32[]{:S(2)}) collective-permute-start(f32[128,512]{1,0:T(8,128)S(1)} %select_select_fusion.1), channel_id=1, source_target_pairs={{1,0},{2,3},{3,1},{0,2},{5,4},{6,7},{7,5},{4,6},{9,8},{10,11},{11,... | collective-permute-start | bytes 786440 | tf_op jit(solution)/shard_map/ppermute | solution.py:511
  104.6 6.6 %collective-permute-start.12 = (f32[8,224,128]{2,1,0:T(8,128)S(1)}, f32[8,224,128]{2,1,0:T(8,128)S(1)}, u32[]{:S(2)}, u32[]{:S(2)}) collective-permute-start(f32[8,224,128]{2,1,0:T(8,128)S(1)} %all-to-all-done.2.own_ref.left_ref), channel_id=1, source_target_pairs={{0,4},{4,0},{8,12},{12,8},{16,20},{20,16},{24,28},{28,24},{1,5},{5... | collective-permute-start | bytes 2752520 | tf_op jit(solution)/shard_map/ppermute | solution.py:598
  104.6 2.8 %collective-permute-start.13 = (f32[128,128]{1,0:T(8,128)S(1)}, f32[128,128]{1,0:T(8,128)S(1)}, u32[]{:S(2)}, u32[]{:S(2)}) collective-permute-start(f32[128,128]{1,0:T(8,128)S(1)} %get-tuple-element.55), channel_id=1, source_target_pairs={{0,4},{4,0},{8,12},{12,8},{16,20},{20,16},{24,28},{28,24},{1,5},{5... | collective-permute-start | bytes 196616 | tf_op jit(solution)/shard_map/ppermute | solution.py:597
  105.1 4.6 %collective-permute-start.14 = (f32[128,128]{1,0:T(8,128)S(1)}, f32[128,128]{1,0:T(8,128)S(1)}, u32[]{:S(2)}, u32[]{:S(2)}) collective-permute-start(f32[128,128]{1,0:T(8,128)S(1)} %get-tuple-element.56), channel_id=1, source_target_pairs={{0,8},{4,12},{8,0},{12,4},{16,24},{20,28},{24,16},{28,20},{1,9},{5... | collective-permute-start | bytes 196616 | tf_op jit(solution)/shard_map/ppermute | solution.py:597
  106.2 6.3 %collective-permute-start.15 = (f32[128,128]{1,0:T(8,128)S(1)}, f32[128,128]{1,0:T(8,128)S(1)}, u32[]{:S(2)}, u32[]{:S(2)}) collective-permute-start(f32[128,128]{1,0:T(8,128)S(1)} %get-tuple-element.57), channel_id=1, source_target_pairs={{0,12},{4,8},{8,4},{12,0},{16,28},{20,24},{24,20},{28,16},{1,13},{... | collective-permute-start | bytes 196616 | tf_op jit(solution)/shard_map/ppermute | solution.py:597
  106.5 6.0 %collective-permute-start.16 = (f32[128,128]{1,0:T(8,128)S(1)}, f32[128,128]{1,0:T(8,128)S(1)}, u32[]{:S(2)}, u32[]{:S(2)}) collective-permute-start(f32[128,128]{1,0:T(8,128)S(1)} %get-tuple-element.58), channel_id=1, source_target_pairs={{0,16},{4,20},{8,24},{12,28},{16,0},{20,4},{24,8},{28,12},{1,17},{... | collective-permute-start | bytes 196616 | tf_op jit(solution)/shard_map/ppermute | solution.py:597
  107.5 5.7 %collective-permute-start.17 = (f32[128,128]{1,0:T(8,128)S(1)}, f32[128,128]{1,0:T(8,128)S(1)}, u32[]{:S(2)}, u32[]{:S(2)}) collective-permute-start(f32[128,128]{1,0:T(8,128)S(1)} %get-tuple-element.59), channel_id=1, source_target_pairs={{0,20},{4,16},{8,28},{12,24},{16,4},{20,0},{24,12},{28,8},{1,21},{... | collective-permute-start | bytes 196616 | tf_op jit(solution)/shard_map/ppermute | solution.py:597
  109.7 5.2 %collective-permute-start.18 = (f32[128,128]{1,0:T(8,128)S(1)}, f32[128,128]{1,0:T(8,128)S(1)}, u32[]{:S(2)}, u32[]{:S(2)}) collective-permute-start(f32[128,128]{1,0:T(8,128)S(1)} %get-tuple-element.60), channel_id=1, source_target_pairs={{0,24},{4,28},{8,16},{12,20},{16,8},{20,12},{24,0},{28,4},{1,25},{... | collective-permute-start | bytes 196616 | tf_op jit(solution)/shard_map/ppermute | solution.py:597
  111.3 5.0 %collective-permute-start.19 = (f32[128,128]{1,0:T(8,128)S(1)}, f32[128,128]{1,0:T(8,128)S(1)}, u32[]{:S(2)}, u32[]{:S(2)}) collective-permute-start(f32[128,128]{1,0:T(8,128)S(1)} %get-tuple-element.61), channel_id=1, source_target_pairs={{0,28},{4,24},{8,20},{12,16},{16,12},{20,8},{24,4},{28,0},{1,29},{... | collective-permute-start | bytes 196616 | tf_op jit(solution)/shard_map/ppermute | solution.py:597

commit v19 on v18

--- a/solution.py
+++ b/solution.py
@@ -595,7 +595,7 @@
     right_came = [right_last[0]] * n_row
     for j in range(n_row - 1, 0, -1):
         right_came[j] = lax.ppermute(right_last[j], "row", [(r, r ^ j) for r in range(n_row)])
-    other = lax.ppermute(after(left_came, right_last[0]), "row", [(r, r ^ 1) for r in range(n_row)])
+    other = lax.ppermute(after(left_came, right_came[-1]), "row", [(r, r ^ 1) for r in range(n_row)])
     weight_grad = assemble(n_row, row, left_came, other)
     return finish(n_row, row, owners, after(diff, weight_grad), left_came, right_came), weight_grad
 

time: 119 us -> 120 us (level)
  starting transfers between devices: 41.4 us -> 43.4 us
    ppermute x7, waiting for transfers between devices: 4.87 us -> 6.6 us  [per_device(): lax.ppermute(right_last[j], 'row', [(r, r ^ j) for r in range(n_row)])]
  transfers between devices with their start and end apart: 24 -> 24, of which waited for: 15 -> 11; matrix products, arithmetic and copies ran while one was open for 0% -> 0% of each run, Pallas kernels for 36% -> 36%
where the time goes in v19:
time: 120 us
  Pallas kernels  47.9 us (40%)
  starting transfers between devices  43.4 us (36%)
  waiting for transfers between devices  26.6 us (22%)
  between operations  1.44 us (1%)
    pallas_call x7, Pallas kernels, product(): pl.pallas_call(functools.partial(product_kernel, n_row, n_col, origins, h...  29.7 us
    ppermute x8, starting transfers between devices, shift(): lax.ppermute(x, 'col', [(c, (c + step) % n_col) for c in range(n_col)])  16.7 us
    all_to_all x4, starting transfers between devices, exchange(): lax.all_to_all(pieces, 'row', split_axis=0, concat_axis=0, tiled=True)  15.2 us
    ppermute x8, waiting for transfers between devices, shift(): lax.ppermute(x, 'col', [(c, (c + step) % n_col) for c in range(n_col)])  15.1 us
    pallas_call x1, Pallas kernels, build_operator(): pl.pallas_call(functools.partial(operator_kernel, n_row, n_col, origins),...  7.28 us
    ppermute x7, waiting for transfers between devices, per_device(): lax.ppermute(right_last[j], 'row', [(r, r ^ j) for r in range(n_row)])  6.6 us
    ppermute x7, starting transfers between devices, per_device(): lax.ppermute(right_last[j], 'row', [(r, r ^ j) for r in range(n_row)])  6.58 us
    pallas_call x1, Pallas kernels, local_terms(): pl.pallas_call(functools.partial(local_kernel, n_row), in_specs=[ANY] + [...  4.88 us
  transfers between devices with their start and end apart: 24, of which 11 were waited for; matrix products, arithmetic and copies ran while one was open for 0% of the time, Pallas kernels for 36%

profile of v19, /device:TPU:0, one launch (start us, length us, event | category | flops | bytes accessed | tf_op | source)
XLA Modules:
  0.0 119.6 jit_solution(18223698249780158718)
XLA Ops:
  0.6 1.7 %term_two.1 = (f32[128,512]{1,0:T(8,128)S(1)}, f32[128,512]{1,0:T(8,128)S(1)}) custom-call(f32[512,256]{1,0:T(8,128)} %grad_hbm.3, s32[512,256]{1,0:T(8,128)} %mask_hbm.3, f32[3,256,256]{2,1,0:T(8,128)} %weight_hbm.3), custom_call_target="tpu_custom_call" | custom-call | flops 1024 | bytes 1024 | tf_op jit(solution)/shard_map/term_two/pallas_call | solution.py:78
  2.4 5.1 %collective-permute-start.1 = (f32[128,512]{1,0:T(8,128)S(1)}, f32[128,512]{1,0:T(8,128)S(1)}, u32[]{:S(2)}, u32[]{:S(2)}) collective-permute-start(f32[128,512]{1,0:T(8,128)S(1)} %get-tuple-element.32.first_ref.refs_0_), channel_id=1, source_target_pairs={{0,3},{1,0},{2,1},{3,2},{4,7},{5,4},{6,5},{7,6},{8,11},{9,8},{10,9... | collective-permute-start | bytes 786440 | tf_op jit(solution)/shard_map/ppermute | solution.py:497
  7.5 0.0 collective-permute-start
  7.5 4.9 %local_terms.1 = (f32[128,512]{1,0:T(8,128)}, f32[128,512]{1,0:T(8,128)}, f32[256,512]{1,0:T(8,128)S(1)}, f32[8,192,128]{2,1,0:T(8,128)}) custom-call(f32[128,512]{1,0:T(8,128)S(1)} %get-tuple-element.32.first_ref.refs_0_, f32[512,256]{1,0:T(8,128)} %grad_hbm.3, s32[512,256]{1,0:T(8,128)} %mask_hbm.3, f32[3,256,256]{2,1,0:T(8,128)} %weight_hbm.3, ...), custom_call_target="tpu_custom_call" | custom-call | flops 1024 | bytes 1024 | tf_op jit(solution)/shard_map/local_terms/pallas_call | solution.py:125
  12.4 3.7 %all-to-all-start = ((f32[8,192,128]{2,1,0:T(8,128)}), f32[8,192,128]{2,1,0:T(8,128)S(1)}, u32[]{:S(2)}, u32[]{:S(2)}) async-start(f32[8,192,128]{2,1,0:T(8,128)} %get-tuple-element.44), calls=%async_computation | async-start | bytes 1572864 | tf_op jit(solution)/shard_map/all_to_all | solution.py:501
  16.8 0.0 collective-permute-done.1.refs_2_
  16.8 2.8 %collective-permute-done.refs_1_ = f32[128,512]{1,0:T(8,128)S(1)} collective-permute-done((f32[128,512]{1,0:T(8,128)S(1)}, f32[128,512]{1,0:T(8,128)S(1)}, u32[]{:S(2)}, u32[]{:S(2)}) %collective-permute-start) | collective-permute-done | bytes 262176 | tf_op jit(solution)/shard_map/ppermute | solution.py:497
  19.6 0.1 select_select_fusion.3
  19.6 0.8 collective-permute-start.2
  20.4 7.3 %operator.1 = (bf16[4,4,1024,256]{3,2,1,0:T(8,128)(2,1)}, f32[128,1024]{1,0:T(8,128)S(1)}) custom-call(s32[1]{0:T(128)} %bitcast.2.ids_ref.refs_0_, s32[1]{0:T(128)S(6)} %copy.13.live_ref, s32[1,128]{1,0:T(1,128)} %rows_hbm.1, s32[1,128]{1,0:T(1,128)} %slots_hbm.1, f32[1,128,128,128]{3,2,1,0:T(8,128)} %values_ref.1, ...), custom_call_target="tpu_custom_call" | custom-call | flops 17179869184 | bytes 67108864 | tf_op jit(solution)/shard_map/operator/pallas_call | solution.py:262
  27.7 0.0 collective-permute-done.2.refs_1_
  27.7 1.7 %collective-permute-start.4 = (f32[128,512]{1,0:T(8,128)S(1)}, f32[128,512]{1,0:T(8,128)S(1)}, u32[]{:S(2)}, u32[]{:S(2)}) collective-permute-start(f32[128,512]{1,0:T(8,128)S(1)} %get-tuple-element.38.refs_1_), channel_id=1, source_target_pairs={{0,1},{1,2},{2,3},{3,0},{4,5},{5,6},{6,7},{7,4},{8,9},{9,10},{10,1... | collective-permute-start | bytes 786440 | tf_op jit(solution)/shard_map/ppermute | solution.py:497
  29.4 2.2 %collective-permute-start.3 = (f32[128,512]{1,0:T(8,128)S(1)}, f32[128,512]{1,0:T(8,128)S(1)}, u32[]{:S(2)}, u32[]{:S(2)}) collective-permute-start(f32[128,512]{1,0:T(8,128)S(1)} %get-tuple-element.38.refs_1_), channel_id=1, source_target_pairs={{0,3},{1,0},{2,1},{3,2},{4,7},{5,4},{6,5},{7,6},{8,11},{9,8},{10,9... | collective-permute-start | bytes 786440 | tf_op jit(solution)/shard_map/ppermute | solution.py:497
  31.6 0.0 all-to-all-done.refs_0_
  31.6 3.2 %product.8 = f32[8,128,128]{2,1,0:T(8,128)} custom-call(bf16[4,4,1024,256]{3,2,1,0:T(8,128)(2,1)} %get-tuple-element.34.refs_0_.refs_1_, f32[128,512]{1,0:T(8,128)S(1)} %collective-permute-done.2.refs_1_, f32[128,1024]{1,0:T(8,128)S(1)} %get-tuple-element.45.refs_2_), custom_call_target="tpu_custom_call" | custom-call | flops 1024 | bytes 1024 | tf_op jit(solution)/shard_map/product/pallas_call | solution.py:394
  34.8 3.7 %all-to-all-start.1 = ((f32[8,128,128]{2,1,0:T(8,128)}), f32[8,128,128]{2,1,0:T(8,128)S(1)}, u32[]{:S(2)}, u32[]{:S(2)}) async-start(f32[8,128,128]{2,1,0:T(8,128)} %product.8), calls=%async_computation.1 | async-start | bytes 1048576 | tf_op jit(solution)/shard_map/all_to_all | solution.py:501
  38.6 0.2 collective-permute-done.4.refs_3_
  38.8 2.5 %collective-permute-done.3.refs_2_ = f32[128,512]{1,0:T(8,128)S(1)} collective-permute-done((f32[128,512]{1,0:T(8,128)S(1)}, f32[128,512]{1,0:T(8,128)S(1)}, u32[]{:S(2)}, u32[]{:S(2)}) %collective-permute-start.3) | collective-permute-done | bytes 262176 | tf_op jit(solution)/shard_map/ppermute | solution.py:497
  41.3 0.1 select_select_fusion.2
  41.3 1.5 %collective-permute-start.5 = (f32[128,512]{1,0:T(8,128)S(1)}, f32[128,512]{1,0:T(8,128)S(1)}, u32[]{:S(2)}, u32[]{:S(2)}) collective-permute-start(f32[128,512]{1,0:T(8,128)S(1)} %select_select_fusion.2), channel_id=1, source_target_pairs={{1,0},{2,3},{3,1},{0,2},{5,4},{6,7},{7,5},{4,6},{9,8},{10,11},{11,... | collective-permute-start | bytes 786440 | tf_op jit(solution)/shard_map/ppermute | solution.py:511
  42.8 5.5 %product.7 = (f32[128,1024]{1,0:T(8,128)}, f32[128,512]{1,0:T(8,128)S(1)}) custom-call(bf16[4,4,1024,256]{3,2,1,0:T(8,128)(2,1)} %get-tuple-element.34.refs_0_.refs_1_, f32[128,512]{1,0:T(8,128)S(1)} %get-tuple-element.38.refs_1_, f32[128,512]{1,0:T(8,128)S(1)} %collective-permute-done.3.refs_2_, f32[128,512]{1,0:T(8,128)S(1)} %collective-permute-done.4.refs_3_, ...), custom_call_target="tpu_custom_call" | custom-call | flops 17179869184 | bytes 67108864 | tf_op jit(solution)/shard_map/product/pallas_call | solution.py:394
  48.3 0.7 collective-permute-done.5.refs_1_
  49.0 0.0 all-to-all-done.1.came_ref
  49.0 0.7 carry.2.refs_1_.refs_4_
  49.7 2.7 %collective-permute-start.7 = (f32[176,512]{1,0:T(8,128)S(1)}, f32[176,512]{1,0:T(8,128)S(1)}, u32[]{:S(2)}, u32[]{:S(2)}) collective-permute-start(f32[176,512]{1,0:T(8,128)S(1)} %carry.2.refs_1_.refs_4_), channel_id=1, source_target_pairs={{0,1},{1,2},{2,3},{3,0},{4,5},{5,6},{6,7},{7,4},{8,9},{9,10},{10,1... | collective-permute-start | bytes 1081352 | tf_op jit(solution)/shard_map/ppermute | solution.py:497
  52.4 1.2 collective-permute-start.6
  53.6 3.5 %product.11 = f32[8,128,128]{2,1,0:T(8,128)} custom-call(bf16[4,4,1024,256]{3,2,1,0:T(8,128)(2,1)} %get-tuple-element.34.refs_0_.refs_1_, f32[128,512]{1,0:T(8,128)S(1)} %collective-permute-done.5.refs_1_, f32[128,1024]{1,0:T(8,128)} %get-tuple-element.41.refs_2_), custom_call_target="tpu_custom_call" | custom-call | flops 1024 | bytes 1024 | tf_op jit(solution)/shard_map/product/pallas_call | solution.py:394
  57.1 3.8 %all-to-all-start.3 = ((f32[8,128,128]{2,1,0:T(8,128)}), f32[8,128,128]{2,1,0:T(8,128)S(1)}, u32[]{:S(2)}, u32[]{:S(2)}) async-start(f32[8,128,128]{2,1,0:T(8,128)} %product.11), calls=%async_computation.3 | async-start | bytes 1048576 | tf_op jit(solution)/shard_map/all_to_all | solution.py:501
  60.9 2.0 %collective-permute-done.7.refs_2_.refs_7_ = f32[176,512]{1,0:T(8,128)S(1)} collective-permute-done((f32[176,512]{1,0:T(8,128)S(1)}, f32[176,512]{1,0:T(8,128)S(1)}, u32[]{:S(2)}, u32[]{:S(2)}) %collective-permute-start.7) | collective-permute-done | bytes 360480 | tf_op jit(solution)/shard_map/ppermute | solution.py:497
  62.9 5.1 %collective-permute-done.6.refs_3_.refs_5_ = f32[176,512]{1,0:T(8,128)S(1)} collective-permute-done((f32[176,512]{1,0:T(8,128)S(1)}, f32[176,512]{1,0:T(8,128)S(1)}, u32[]{:S(2)}, u32[]{:S(2)}) %collective-permute-start.6) | collective-permute-done | bytes 360480 | tf_op jit(solution)/shard_map/ppermute | solution.py:497
  68.0 0.1 select_select_fusion
  68.1 0.8 collective-permute-start.8
  69.0 5.5 %product.9 = (f32[128,1024]{1,0:T(8,128)}, f32[128,512]{1,0:T(8,128)S(1)}) custom-call(bf16[4,4,1024,256]{3,2,1,0:T(8,128)(2,1)} %get-tuple-element.34.refs_0_.refs_1_, f32[176,512]{1,0:T(8,128)S(1)} %carry.2.refs_1_.refs_4_, f32[176,512]{1,0:T(8,128)S(1)} %collective-permute-done.7.refs_2_.refs_7_, f32[176,512]{1,0:T(8,128)S(1)} %collective-permute-done.6.refs_3_.refs_5_, ...), custom_call_target="tpu_custom_call" | custom-call | flops 17179869184 | bytes 67108864 | tf_op jit(solution)/shard_map/product/pallas_call | solution.py:394
  74.5 4.2 %collective-permute-done.8.refs_2_.refs_6_ = f32[176,512]{1,0:T(8,128)S(1)} collective-permute-done((f32[176,512]{1,0:T(8,128)S(1)}, f32[176,512]{1,0:T(8,128)S(1)}, u32[]{:S(2)}, u32[]{:S(2)}) %collective-permute-start.8) | collective-permute-done | bytes 360480 | tf_op jit(solution)/shard_map/ppermute | solution.py:511
  78.7 0.0 all-to-all-done.3.came_ref
  78.7 0.7 carry.3.refs_1_
  79.3 1.5 %collective-permute-start.10 = (f32[128,512]{1,0:T(8,128)S(1)}, f32[128,512]{1,0:T(8,128)S(1)}, u32[]{:S(2)}, u32[]{:S(2)}) collective-permute-start(f32[128,512]{1,0:T(8,128)S(1)} %carry.3.refs_1_), channel_id=1, source_target_pairs={{0,1},{1,2},{2,3},{3,0},{4,5},{5,6},{6,7},{7,4},{8,9},{9,10},{10,1... | collective-permute-start | bytes 786440 | tf_op jit(solution)/shard_map/ppermute | solution.py:497
  80.9 2.3 %collective-permute-start.9 = (f32[128,512]{1,0:T(8,128)S(1)}, f32[128,512]{1,0:T(8,128)S(1)}, u32[]{:S(2)}, u32[]{:S(2)}) collective-permute-start(f32[128,512]{1,0:T(8,128)S(1)} %carry.3.refs_1_), channel_id=1, source_target_pairs={{0,3},{1,0},{2,1},{3,2},{4,7},{5,4},{6,5},{7,6},{8,11},{9,8},{10,9... | collective-permute-start | bytes 786440 | tf_op jit(solution)/shard_map/ppermute | solution.py:497
  83.2 3.5 %product.10 = f32[8,224,128]{2,1,0:T(8,128)} custom-call(s32[1]{0:T(128)} %bitcast.2.ids_ref.refs_0_, bf16[4,4,1024,256]{3,2,1,0:T(8,128)(2,1)} %get-tuple-element.34.refs_0_.refs_1_, f32[176,512]{1,0:T(8,128)S(1)} %collective-permute-done.8.refs_2_.refs_6_, f32[128,1024]{1,0:T(8,128)} %get-tuple-element.48.refs_3_, f32[176,512]{1,0:T(8,128)S(1)} %carry.2.refs_1_.refs_4_, ...), custom_call_target="tpu_custom_call" | custom-call | flops 1024 | bytes 1024 | tf_op jit(solution)/shard_map/product/pallas_call | solution.py:394
  86.7 3.9 %all-to-all-start.2 = ((f32[8,224,128]{2,1,0:T(8,128)}), f32[8,224,128]{2,1,0:T(8,128)S(1)}, u32[]{:S(2)}, u32[]{:S(2)}) async-start(f32[8,224,128]{2,1,0:T(8,128)} %product.10), calls=%async_computation.2 | async-start | bytes 1835008 | tf_op jit(solution)/shard_map/all_to_all | solution.py:501
  90.6 0.0 collective-permute-done.10.refs_3_
  90.6 2.4 %collective-permute-done.9.refs_2_ = f32[128,512]{1,0:T(8,128)S(1)} collective-permute-done((f32[128,512]{1,0:T(8,128)S(1)}, f32[128,512]{1,0:T(8,128)S(1)}, u32[]{:S(2)}, u32[]{:S(2)}) %collective-permute-start.9) | collective-permute-done | bytes 262176 | tf_op jit(solution)/shard_map/ppermute | solution.py:497
  93.1 0.1 select_select_fusion.1
  93.1 1.7 %collective-permute-start.11 = (f32[128,512]{1,0:T(8,128)S(1)}, f32[128,512]{1,0:T(8,128)S(1)}, u32[]{:S(2)}, u32[]{:S(2)}) collective-permute-start(f32[128,512]{1,0:T(8,128)S(1)} %select_select_fusion.1), channel_id=1, source_target_pairs={{1,0},{2,3},{3,1},{0,2},{5,4},{6,7},{7,5},{4,6},{9,8},{10,11},{11,... | collective-permute-start | bytes 786440 | tf_op jit(solution)/shard_map/ppermute | solution.py:511
  94.8 5.5 %product.12.refs_3_ = f32[128,1024]{1,0:T(8,128)} custom-call(bf16[4,4,1024,256]{3,2,1,0:T(8,128)(2,1)} %get-tuple-element.34.refs_0_.refs_1_, f32[128,512]{1,0:T(8,128)S(1)} %carry.3.refs_1_, f32[128,512]{1,0:T(8,128)S(1)} %collective-permute-done.9.refs_2_, f32[128,512]{1,0:T(8,128)S(1)} %collective-permute-done.10.refs_3_), custom_call_target="tpu_custom_call" | custom-call | flops 17179869184 | bytes 67108864 | tf_op jit(solution)/shard_map/product/pallas_call | solution.py:394
  100.3 0.0 collective-permute-done.11.refs_2_
  100.3 2.9 %product.13 = (f32[128,128]{1,0:T(8,128)S(1)}, f32[128,128]{1,0:T(8,128)S(1)}, f32[128,128]{1,0:T(8,128)S(1)}, f32[128,128]{1,0:T(8,128)S(1)}, f32[128,128]{1,0:...) custom-call(s32[1]{0:T(128)} %bitcast.refs_0_.row_ref, ...), custom_call_target="tpu_custom_call" | custom-call | flops 1024 | bytes 1024 | tf_op jit(solution)/shard_map/product/pallas_call | solution.py:394
  103.2 0.4 collective-permute-start.12
  103.7 4.7 %collective-permute-done.12.refs_7_ = f32[128,128]{1,0:T(8,128)S(1)} collective-permute-done((f32[128,128]{1,0:T(8,128)S(1)}, f32[128,128]{1,0:T(8,128)S(1)}, u32[]{:S(2)}, u32[]{:S(2)}) %collective-permute-start.12) | collective-permute-done | bytes 65568 | tf_op jit(solution)/shard_map/ppermute | solution.py:597
  108.3 0.0 all-to-all-done.2.own_ref.left_ref
  108.3 0.1 collective-permute-start.13
  108.5 0.4 collective-permute-start.14
  108.8 1.6 %collective-permute-start.15 = (f32[128,128]{1,0:T(8,128)S(1)}, f32[128,128]{1,0:T(8,128)S(1)}, u32[]{:S(2)}, u32[]{:S(2)}) collective-permute-start(f32[128,128]{1,0:T(8,128)S(1)} %get-tuple-element.57), channel_id=1, source_target_pairs={{0,8},{4,12},{8,0},{12,4},{16,24},{20,28},{24,16},{28,20},{1,9},{5... | collective-permute-start | bytes 196616 | tf_op jit(solution)/shard_map/ppermute | solution.py:597
  110.4 1.5 %collective-permute-start.17 = (f32[128,128]{1,0:T(8,128)S(1)}, f32[128,128]{1,0:T(8,128)S(1)}, u32[]{:S(2)}, u32[]{:S(2)}) collective-permute-start(f32[128,128]{1,0:T(8,128)S(1)} %get-tuple-element.59), channel_id=1, source_target_pairs={{0,16},{4,20},{8,24},{12,28},{16,0},{20,4},{24,8},{28,12},{1,17},{... | collective-permute-start | bytes 196616 | tf_op jit(solution)/shard_map/ppermute | solution.py:597
  112.0 0.0 collective-permute-done.14.refs_1_
  112.0 0.4 collective-permute-start.18
  112.4 0.0 collective-permute-done.13.other_ref
  112.4 2.2 %collective-permute-start.19 = (f32[128,128]{1,0:T(8,128)S(1)}, f32[128,128]{1,0:T(8,128)S(1)}, u32[]{:S(2)}, u32[]{:S(2)}) collective-permute-start(f32[128,128]{1,0:T(8,128)S(1)} %get-tuple-element.61), channel_id=1, source_target_pairs={{0,24},{4,28},{8,16},{12,20},{16,8},{20,12},{24,0},{28,4},{1,25},{... | collective-permute-start | bytes 196616 | tf_op jit(solution)/shard_map/ppermute | solution.py:597
  114.6 1.2 %assemble.1 = f32[3,256,256]{2,1,0:T(8,128)} custom-call(s32[1]{0:T(128)} %bitcast.refs_0_.row_ref, f32[8,224,128]{2,1,0:T(8,128)S(1)} %all-to-all-done.2.own_ref.left_ref, f32[8,224,128]{2,1,0:T(8,128)S(1)} %collective-permute-done.13.other_ref), custom_call_target="tpu_custom_call" | custom-call | flops 1024 | bytes 1024 | tf_op jit(solution)/shard_map/assemble/pallas_call | solution.py:481
  115.9 0.0 collective-permute-done.15.refs_2_
  115.9 0.0 collective-permute-done.16.refs_3_
  115.9 1.2 %collective-permute-done.18.refs_5_ = f32[128,128]{1,0:T(8,128)S(1)} collective-permute-done((f32[128,128]{1,0:T(8,128)S(1)}, f32[128,128]{1,0:T(8,128)S(1)}, u32[]{:S(2)}, u32[]{:S(2)}) %collective-permute-start.18) | collective-permute-done | bytes 65568 | tf_op jit(solution)/shard_map/ppermute | solution.py:597
  117.1 0.7 collective-permute-done.19.refs_6_
  117.8 1.8 %finish.1 = f32[512,256]{1,0:T(8,128)} custom-call(s32[1]{0:T(128)} %bitcast.refs_0_.row_ref, s32[8]{0:T(128)S(1)} %bitcast.5, f32[256,512]{1,0:T(8,128)S(1)} %get-tuple-element.54.base_ref, f32[8,224,128]{2,1,0:T(8,128)S(1)} %all-to-all-done.2.own_ref.left_ref, f32[128,128]{1,0:T(8,128)S(1)} %get-tuple-element.55.refs_0_, ...), custom_call_target="tpu_custom_call" | custom-call | flops 1024 | bytes 1024 | tf_op jit(solution)/shard_map/finish/pallas_call | solution.py:454
  (4 shorter events, 0.0 us)
Async XLA Ops:
  2.4 14.4 %collective-permute-start.1 = (f32[128,512]{1,0:T(8,128)S(1)}, f32[128,512]{1,0:T(8,128)S(1)}, u32[]{:S(2)}, u32[]{:S(2)}) collective-permute-start(f32[128,512]{1,0:T(8,128)S(1)} %get-tuple-element.32.first_ref.refs_0_), channel_id=1, source_target_pairs={{0,3},{1,0},{2,1},{3,2},{4,7},{5,4},{6,5},{7,6},{8,11},{9,8},{10,9... | collective-permute-start | bytes 786440 | tf_op jit(solution)/shard_map/ppermute | solution.py:497
  7.5 12.1 %collective-permute-start = (f32[128,512]{1,0:T(8,128)S(1)}, f32[128,512]{1,0:T(8,128)S(1)}, u32[]{:S(2)}, u32[]{:S(2)}) collective-permute-start(f32[128,512]{1,0:T(8,128)S(1)} %get-tuple-element.32.first_ref.refs_0_), channel_id=1, source_target_pairs={{0,1},{1,2},{2,3},{3,0},{4,5},{5,6},{6,7},{7,4},{8,9},{9,10},{10,1... | collective-permute-start | bytes 786440 | tf_op jit(solution)/shard_map/ppermute | solution.py:497
  12.4 19.2 %all-to-all-start = ((f32[8,192,128]{2,1,0:T(8,128)}), f32[8,192,128]{2,1,0:T(8,128)S(1)}, u32[]{:S(2)}, u32[]{:S(2)}) async-start(f32[8,192,128]{2,1,0:T(8,128)} %get-tuple-element.44), calls=%async_computation | async-start | bytes 1572864 | tf_op jit(solution)/shard_map/all_to_all | solution.py:501
  19.6 8.1 %collective-permute-start.2 = (f32[128,512]{1,0:T(8,128)S(1)}, f32[128,512]{1,0:T(8,128)S(1)}, u32[]{:S(2)}, u32[]{:S(2)}) collective-permute-start(f32[128,512]{1,0:T(8,128)S(1)} %select_select_fusion.3), channel_id=1, source_target_pairs={{1,0},{2,3},{3,1},{0,2},{5,4},{6,7},{7,5},{4,6},{9,8},{10,11},{11,... | collective-permute-start | bytes 786440 | tf_op jit(solution)/shard_map/ppermute | solution.py:511
  27.7 11.1 %collective-permute-start.4 = (f32[128,512]{1,0:T(8,128)S(1)}, f32[128,512]{1,0:T(8,128)S(1)}, u32[]{:S(2)}, u32[]{:S(2)}) collective-permute-start(f32[128,512]{1,0:T(8,128)S(1)} %get-tuple-element.38.refs_1_), channel_id=1, source_target_pairs={{0,1},{1,2},{2,3},{3,0},{4,5},{5,6},{6,7},{7,4},{8,9},{9,10},{10,1... | collective-permute-start | bytes 786440 | tf_op jit(solution)/shard_map/ppermute | solution.py:497
  29.4 11.9 %collective-permute-start.3 = (f32[128,512]{1,0:T(8,128)S(1)}, f32[128,512]{1,0:T(8,128)S(1)}, u32[]{:S(2)}, u32[]{:S(2)}) collective-permute-start(f32[128,512]{1,0:T(8,128)S(1)} %get-tuple-element.38.refs_1_), channel_id=1, source_target_pairs={{0,3},{1,0},{2,1},{3,2},{4,7},{5,4},{6,5},{7,6},{8,11},{9,8},{10,9... | collective-permute-start | bytes 786440 | tf_op jit(solution)/shard_map/ppermute | solution.py:497
  34.8 14.1 %all-to-all-start.1 = ((f32[8,128,128]{2,1,0:T(8,128)}), f32[8,128,128]{2,1,0:T(8,128)S(1)}, u32[]{:S(2)}, u32[]{:S(2)}) async-start(f32[8,128,128]{2,1,0:T(8,128)} %product.8), calls=%async_computation.1 | async-start | bytes 1048576 | tf_op jit(solution)/shard_map/all_to_all | solution.py:501
  41.3 7.6 %collective-permute-start.5 = (f32[128,512]{1,0:T(8,128)S(1)}, f32[128,512]{1,0:T(8,128)S(1)}, u32[]{:S(2)}, u32[]{:S(2)}) collective-permute-start(f32[128,512]{1,0:T(8,128)S(1)} %select_select_fusion.2), channel_id=1, source_target_pairs={{1,0},{2,3},{3,1},{0,2},{5,4},{6,7},{7,5},{4,6},{9,8},{10,11},{11,... | collective-permute-start | bytes 786440 | tf_op jit(solution)/shard_map/ppermute | solution.py:511
  42.8 6.2 %copy-start = (s32[1,8,1]{1,2,0:T(1,128)S(1)}, s32[1,8,1]{1,2,0:T(1,128)}, u32[]{:S(2)}) copy-start(s32[1,8,1]{1,2,0:T(1,128)} %param.20) | copy-start | bytes 100
  49.7 13.2 %collective-permute-start.7 = (f32[176,512]{1,0:T(8,128)S(1)}, f32[176,512]{1,0:T(8,128)S(1)}, u32[]{:S(2)}, u32[]{:S(2)}) collective-permute-start(f32[176,512]{1,0:T(8,128)S(1)} %carry.2.refs_1_.refs_4_), channel_id=1, source_target_pairs={{0,1},{1,2},{2,3},{3,0},{4,5},{5,6},{6,7},{7,4},{8,9},{9,10},{10,1... | collective-permute-start | bytes 1081352 | tf_op jit(solution)/shard_map/ppermute | solution.py:497
  52.4 15.7 %collective-permute-start.6 = (f32[176,512]{1,0:T(8,128)S(1)}, f32[176,512]{1,0:T(8,128)S(1)}, u32[]{:S(2)}, u32[]{:S(2)}) collective-permute-start(f32[176,512]{1,0:T(8,128)S(1)} %carry.2.refs_1_.refs_4_), channel_id=1, source_target_pairs={{0,3},{1,0},{2,1},{3,2},{4,7},{5,4},{6,5},{7,6},{8,11},{9,8},{10,9... | collective-permute-start | bytes 1081352 | tf_op jit(solution)/shard_map/ppermute | solution.py:497
  57.1 21.6 %all-to-all-start.3 = ((f32[8,128,128]{2,1,0:T(8,128)}), f32[8,128,128]{2,1,0:T(8,128)S(1)}, u32[]{:S(2)}, u32[]{:S(2)}) async-start(f32[8,128,128]{2,1,0:T(8,128)} %product.11), calls=%async_computation.3 | async-start | bytes 1048576 | tf_op jit(solution)/shard_map/all_to_all | solution.py:501
  68.1 10.5 %collective-permute-start.8 = (f32[176,512]{1,0:T(8,128)S(1)}, f32[176,512]{1,0:T(8,128)S(1)}, u32[]{:S(2)}, u32[]{:S(2)}) collective-permute-start(f32[176,512]{1,0:T(8,128)S(1)} %select_select_fusion), channel_id=1, source_target_pairs={{1,0},{2,3},{3,1},{0,2},{5,4},{6,7},{7,5},{4,6},{9,8},{10,11},{11,... | collective-permute-start | bytes 1081352 | tf_op jit(solution)/shard_map/ppermute | solution.py:511
  79.3 11.3 %collective-permute-start.10 = (f32[128,512]{1,0:T(8,128)S(1)}, f32[128,512]{1,0:T(8,128)S(1)}, u32[]{:S(2)}, u32[]{:S(2)}) collective-permute-start(f32[128,512]{1,0:T(8,128)S(1)} %carry.3.refs_1_), channel_id=1, source_target_pairs={{0,1},{1,2},{2,3},{3,0},{4,5},{5,6},{6,7},{7,4},{8,9},{9,10},{10,1... | collective-permute-start | bytes 786440 | tf_op jit(solution)/shard_map/ppermute | solution.py:497
  80.9 12.2 %collective-permute-start.9 = (f32[128,512]{1,0:T(8,128)S(1)}, f32[128,512]{1,0:T(8,128)S(1)}, u32[]{:S(2)}, u32[]{:S(2)}) collective-permute-start(f32[128,512]{1,0:T(8,128)S(1)} %carry.3.refs_1_), channel_id=1, source_target_pairs={{0,3},{1,0},{2,1},{3,2},{4,7},{5,4},{6,5},{7,6},{8,11},{9,8},{10,9... | collective-permute-start | bytes 786440 | tf_op jit(solution)/shard_map/ppermute | solution.py:497
  86.7 21.6 %all-to-all-start.2 = ((f32[8,224,128]{2,1,0:T(8,128)}), f32[8,224,128]{2,1,0:T(8,128)S(1)}, u32[]{:S(2)}, u32[]{:S(2)}) async-start(f32[8,224,128]{2,1,0:T(8,128)} %product.10), calls=%async_computation.2 | async-start | bytes 1835008 | tf_op jit(solution)/shard_map/all_to_all | solution.py:501
  93.1 7.2 %collective-permute-start.11 = (f32[128,512]{1,0:T(8,128)S(1)}, f32[128,512]{1,0:T(8,128)S(1)}, u32[]{:S(2)}, u32[]{:S(2)}) collective-permute-start(f32[128,512]{1,0:T(8,128)S(1)} %select_select_fusion.1), channel_id=1, source_target_pairs={{1,0},{2,3},{3,1},{0,2},{5,4},{6,7},{7,5},{4,6},{9,8},{10,11},{11,... | collective-permute-start | bytes 786440 | tf_op jit(solution)/shard_map/ppermute | solution.py:511
  103.2 5.1 %collective-permute-start.12 = (f32[128,128]{1,0:T(8,128)S(1)}, f32[128,128]{1,0:T(8,128)S(1)}, u32[]{:S(2)}, u32[]{:S(2)}) collective-permute-start(f32[128,128]{1,0:T(8,128)S(1)} %get-tuple-element.52), channel_id=1, source_target_pairs={{0,28},{4,24},{8,20},{12,16},{16,12},{20,8},{24,4},{28,0},{1,29},{... | collective-permute-start | bytes 196616 | tf_op jit(solution)/shard_map/ppermute | solution.py:597
  108.3 4.1 %collective-permute-start.13 = (f32[8,224,128]{2,1,0:T(8,128)S(1)}, f32[8,224,128]{2,1,0:T(8,128)S(1)}, u32[]{:S(2)}, u32[]{:S(2)}) collective-permute-start(f32[8,224,128]{2,1,0:T(8,128)S(1)} %all-to-all-done.2.own_ref.left_ref), channel_id=1, source_target_pairs={{0,4},{4,0},{8,12},{12,8},{16,20},{20,16},{24,28},{28,24},{1,5},{5... | collective-permute-start | bytes 2752520 | tf_op jit(solution)/shard_map/ppermute | solution.py:598
  108.5 3.5 %collective-permute-start.14 = (f32[128,128]{1,0:T(8,128)S(1)}, f32[128,128]{1,0:T(8,128)S(1)}, u32[]{:S(2)}, u32[]{:S(2)}) collective-permute-start(f32[128,128]{1,0:T(8,128)S(1)} %get-tuple-element.56), channel_id=1, source_target_pairs={{0,4},{4,0},{8,12},{12,8},{16,20},{20,16},{24,28},{28,24},{1,5},{5... | collective-permute-start | bytes 196616 | tf_op jit(solution)/shard_map/ppermute | solution.py:597
  108.8 7.0 %collective-permute-start.15 = (f32[128,128]{1,0:T(8,128)S(1)}, f32[128,128]{1,0:T(8,128)S(1)}, u32[]{:S(2)}, u32[]{:S(2)}) collective-permute-start(f32[128,128]{1,0:T(8,128)S(1)} %get-tuple-element.57), channel_id=1, source_target_pairs={{0,8},{4,12},{8,0},{12,4},{16,24},{20,28},{24,16},{28,20},{1,9},{5... | collective-permute-start | bytes 196616 | tf_op jit(solution)/shard_map/ppermute | solution.py:597
  110.4 5.4 %collective-permute-start.16 = (f32[128,128]{1,0:T(8,128)S(1)}, f32[128,128]{1,0:T(8,128)S(1)}, u32[]{:S(2)}, u32[]{:S(2)}) collective-permute-start(f32[128,128]{1,0:T(8,128)S(1)} %get-tuple-element.58), channel_id=1, source_target_pairs={{0,12},{4,8},{8,4},{12,0},{16,28},{20,24},{24,20},{28,16},{1,13},{... | collective-permute-start | bytes 196616 | tf_op jit(solution)/shard_map/ppermute | solution.py:597
  110.4 5.4 %collective-permute-start.17 = (f32[128,128]{1,0:T(8,128)S(1)}, f32[128,128]{1,0:T(8,128)S(1)}, u32[]{:S(2)}, u32[]{:S(2)}) collective-permute-start(f32[128,128]{1,0:T(8,128)S(1)} %get-tuple-element.59), channel_id=1, source_target_pairs={{0,16},{4,20},{8,24},{12,28},{16,0},{20,4},{24,8},{28,12},{1,17},{... | collective-permute-start | bytes 196616 | tf_op jit(solution)/shard_map/ppermute | solution.py:597
  112.0 5.1 %collective-permute-start.18 = (f32[128,128]{1,0:T(8,128)S(1)}, f32[128,128]{1,0:T(8,128)S(1)}, u32[]{:S(2)}, u32[]{:S(2)}) collective-permute-start(f32[128,128]{1,0:T(8,128)S(1)} %get-tuple-element.60), channel_id=1, source_target_pairs={{0,20},{4,16},{8,28},{12,24},{16,4},{20,0},{24,12},{28,8},{1,21},{... | collective-permute-start | bytes 196616 | tf_op jit(solution)/shard_map/ppermute | solution.py:597
  112.4 5.4 %collective-permute-start.19 = (f32[128,128]{1,0:T(8,128)S(1)}, f32[128,128]{1,0:T(8,128)S(1)}, u32[]{:S(2)}, u32[]{:S(2)}) collective-permute-start(f32[128,128]{1,0:T(8,128)S(1)} %get-tuple-element.61), channel_id=1, source_target_pairs={{0,24},{4,28},{8,16},{12,20},{16,8},{20,12},{24,0},{28,4},{1,25},{... | collective-permute-start | bytes 196616 | tf_op jit(solution)/shard_map/ppermute | solution.py:597

commit v20 on v19

--- a/solution.py
+++ b/solution.py
@@ -595,7 +595,7 @@
     right_came = [right_last[0]] * n_row
     for j in range(n_row - 1, 0, -1):
         right_came[j] = lax.ppermute(right_last[j], "row", [(r, r ^ j) for r in range(n_row)])
-    other = lax.ppermute(after(left_came, right_came[-1]), "row", [(r, r ^ 1) for r in range(n_row)])
+    other = lax.ppermute(after(left_came, *right_came[n_row // 2 :]), "row", [(r, r ^ 1) for r in range(n_row)])
     weight_grad = assemble(n_row, row, left_came, other)
     return finish(n_row, row, owners, after(diff, weight_grad), left_came, right_came), weight_grad
 

time: 120 us -> 121 us (level)
  transfers between devices with their start and end apart: 24 -> 24, of which waited for: 11 -> 14; matrix products, arithmetic and copies ran while one was open for 0% -> 0% of each run, Pallas kernels for 36% -> 36%
where the time goes in v20:
time: 121 us; the launch traced here: 120 us
  Pallas kernels  47.9 us (40%)
  starting transfers between devices  44.1 us (36%)
  waiting for transfers between devices  26.2 us (22%)
  between operations  1.43 us (1%)
    pallas_call x7, Pallas kernels, product(): pl.pallas_call(functools.partial(product_kernel, n_row, n_col, origins, h...  29.7 us
    ppermute x8, starting transfers between devices, shift(): lax.ppermute(x, 'col', [(c, (c + step) % n_col) for c in range(n_col)])  16.7 us
    all_to_all x4, starting transfers between devices, exchange(): lax.all_to_all(pieces, 'row', split_axis=0, concat_axis=0, tiled=True)  15.2 us
    ppermute x8, waiting for transfers between devices, shift(): lax.ppermute(x, 'col', [(c, (c + step) % n_col) for c in range(n_col)])  15.1 us
    pallas_call x1, Pallas kernels, build_operator(): pl.pallas_call(functools.partial(operator_kernel, n_row, n_col, origins),...  7.28 us
    ppermute x7, starting transfers between devices, per_device(): lax.ppermute(right_last[j], 'row', [(r, r ^ j) for r in range(n_row)])  6.59 us
    ppermute x7, waiting for transfers between devices, per_device(): lax.ppermute(right_last[j], 'row', [(r, r ^ j) for r in range(n_row)])  6.07 us
    pallas_call x1, Pallas kernels, local_terms(): pl.pallas_call(functools.partial(local_kernel, n_row), in_specs=[ANY] + [...  4.88 us
  transfers between devices with their start and end apart: 24, of which 14 were waited for; matrix products, arithmetic and copies ran while one was open for 0% of the time, Pallas kernels for 36%

profile of v20, /device:TPU:0, one launch (start us, length us, event | category | flops | bytes accessed | tf_op | source)
XLA Modules:
  0.0 119.9 jit_solution(13816068661115552433)
XLA Ops:
  0.6 1.7 %term_two.1 = (f32[128,512]{1,0:T(8,128)S(1)}, f32[128,512]{1,0:T(8,128)S(1)}) custom-call(f32[512,256]{1,0:T(8,128)} %grad_hbm.3, s32[512,256]{1,0:T(8,128)} %mask_hbm.3, f32[3,256,256]{2,1,0:T(8,128)} %weight_hbm.3), custom_call_target="tpu_custom_call" | custom-call | flops 1024 | bytes 1024 | tf_op jit(solution)/shard_map/term_two/pallas_call | solution.py:78
  2.4 5.1 %collective-permute-start.1 = (f32[128,512]{1,0:T(8,128)S(1)}, f32[128,512]{1,0:T(8,128)S(1)}, u32[]{:S(2)}, u32[]{:S(2)}) collective-permute-start(f32[128,512]{1,0:T(8,128)S(1)} %get-tuple-element.32.first_ref.refs_0_), channel_id=1, source_target_pairs={{0,3},{1,0},{2,1},{3,2},{4,7},{5,4},{6,5},{7,6},{8,11},{9,8},{10,9... | collective-permute-start | bytes 786440 | tf_op jit(solution)/shard_map/ppermute | solution.py:497
  7.5 0.0 collective-permute-start
  7.5 4.9 %local_terms.1 = (f32[128,512]{1,0:T(8,128)}, f32[128,512]{1,0:T(8,128)}, f32[256,512]{1,0:T(8,128)S(1)}, f32[8,192,128]{2,1,0:T(8,128)}) custom-call(f32[128,512]{1,0:T(8,128)S(1)} %get-tuple-element.32.first_ref.refs_0_, f32[512,256]{1,0:T(8,128)} %grad_hbm.3, s32[512,256]{1,0:T(8,128)} %mask_hbm.3, f32[3,256,256]{2,1,0:T(8,128)} %weight_hbm.3, ...), custom_call_target="tpu_custom_call" | custom-call | flops 1024 | bytes 1024 | tf_op jit(solution)/shard_map/local_terms/pallas_call | solution.py:125
  12.4 3.7 %all-to-all-start = ((f32[8,192,128]{2,1,0:T(8,128)}), f32[8,192,128]{2,1,0:T(8,128)S(1)}, u32[]{:S(2)}, u32[]{:S(2)}) async-start(f32[8,192,128]{2,1,0:T(8,128)} %get-tuple-element.44), calls=%async_computation | async-start | bytes 1572864 | tf_op jit(solution)/shard_map/all_to_all | solution.py:501
  16.8 0.0 collective-permute-done.1.refs_2_
  16.8 2.8 %collective-permute-done.refs_1_ = f32[128,512]{1,0:T(8,128)S(1)} collective-permute-done((f32[128,512]{1,0:T(8,128)S(1)}, f32[128,512]{1,0:T(8,128)S(1)}, u32[]{:S(2)}, u32[]{:S(2)}) %collective-permute-start) | collective-permute-done | bytes 262176 | tf_op jit(solution)/shard_map/ppermute | solution.py:497
  19.6 0.1 select_select_fusion.3
  19.6 0.8 collective-permute-start.2
  20.4 7.3 %operator.1 = (bf16[4,4,1024,256]{3,2,1,0:T(8,128)(2,1)}, f32[128,1024]{1,0:T(8,128)S(1)}) custom-call(s32[1]{0:T(128)} %bitcast.2.ids_ref.refs_0_, s32[1]{0:T(128)S(6)} %copy.13.live_ref, s32[1,128]{1,0:T(1,128)} %rows_hbm.1, s32[1,128]{1,0:T(1,128)} %slots_hbm.1, f32[1,128,128,128]{3,2,1,0:T(8,128)} %values_ref.1, ...), custom_call_target="tpu_custom_call" | custom-call | flops 17179869184 | bytes 67108864 | tf_op jit(solution)/shard_map/operator/pallas_call | solution.py:262
  27.7 0.0 collective-permute-done.2.refs_1_
  27.7 1.7 %collective-permute-start.4 = (f32[128,512]{1,0:T(8,128)S(1)}, f32[128,512]{1,0:T(8,128)S(1)}, u32[]{:S(2)}, u32[]{:S(2)}) collective-permute-start(f32[128,512]{1,0:T(8,128)S(1)} %get-tuple-element.38.refs_1_), channel_id=1, source_target_pairs={{0,1},{1,2},{2,3},{3,0},{4,5},{5,6},{6,7},{7,4},{8,9},{9,10},{10,1... | collective-permute-start | bytes 786440 | tf_op jit(solution)/shard_map/ppermute | solution.py:497
  29.4 2.2 %collective-permute-start.3 = (f32[128,512]{1,0:T(8,128)S(1)}, f32[128,512]{1,0:T(8,128)S(1)}, u32[]{:S(2)}, u32[]{:S(2)}) collective-permute-start(f32[128,512]{1,0:T(8,128)S(1)} %get-tuple-element.38.refs_1_), channel_id=1, source_target_pairs={{0,3},{1,0},{2,1},{3,2},{4,7},{5,4},{6,5},{7,6},{8,11},{9,8},{10,9... | collective-permute-start | bytes 786440 | tf_op jit(solution)/shard_map/ppermute | solution.py:497
  31.6 0.0 all-to-all-done.refs_0_
  31.6 3.2 %product.8 = f32[8,128,128]{2,1,0:T(8,128)} custom-call(bf16[4,4,1024,256]{3,2,1,0:T(8,128)(2,1)} %get-tuple-element.34.refs_0_.refs_1_, f32[128,512]{1,0:T(8,128)S(1)} %collective-permute-done.2.refs_1_, f32[128,1024]{1,0:T(8,128)S(1)} %get-tuple-element.45.refs_2_), custom_call_target="tpu_custom_call" | custom-call | flops 1024 | bytes 1024 | tf_op jit(solution)/shard_map/product/pallas_call | solution.py:394
  34.8 3.7 %all-to-all-start.1 = ((f32[8,128,128]{2,1,0:T(8,128)}), f32[8,128,128]{2,1,0:T(8,128)S(1)}, u32[]{:S(2)}, u32[]{:S(2)}) async-start(f32[8,128,128]{2,1,0:T(8,128)} %product.8), calls=%async_computation.1 | async-start | bytes 1048576 | tf_op jit(solution)/shard_map/all_to_all | solution.py:501
  38.6 0.2 collective-permute-done.4.refs_3_
  38.8 2.5 %collective-permute-done.3.refs_2_ = f32[128,512]{1,0:T(8,128)S(1)} collective-permute-done((f32[128,512]{1,0:T(8,128)S(1)}, f32[128,512]{1,0:T(8,128)S(1)}, u32[]{:S(2)}, u32[]{:S(2)}) %collective-permute-start.3) | collective-permute-done | bytes 262176 | tf_op jit(solution)/shard_map/ppermute | solution.py:497
  41.3 0.1 select_select_fusion.2
  41.3 1.5 %collective-permute-start.5 = (f32[128,512]{1,0:T(8,128)S(1)}, f32[128,512]{1,0:T(8,128)S(1)}, u32[]{:S(2)}, u32[]{:S(2)}) collective-permute-start(f32[128,512]{1,0:T(8,128)S(1)} %select_select_fusion.2), channel_id=1, source_target_pairs={{1,0},{2,3},{3,1},{0,2},{5,4},{6,7},{7,5},{4,6},{9,8},{10,11},{11,... | collective-permute-start | bytes 786440 | tf_op jit(solution)/shard_map/ppermute | solution.py:511
  42.9 5.5 %product.7 = (f32[128,1024]{1,0:T(8,128)}, f32[128,512]{1,0:T(8,128)S(1)}) custom-call(bf16[4,4,1024,256]{3,2,1,0:T(8,128)(2,1)} %get-tuple-element.34.refs_0_.refs_1_, f32[128,512]{1,0:T(8,128)S(1)} %get-tuple-element.38.refs_1_, f32[128,512]{1,0:T(8,128)S(1)} %collective-permute-done.3.refs_2_, f32[128,512]{1,0:T(8,128)S(1)} %collective-permute-done.4.refs_3_, ...), custom_call_target="tpu_custom_call" | custom-call | flops 17179869184 | bytes 67108864 | tf_op jit(solution)/shard_map/product/pallas_call | solution.py:394
  48.4 0.6 collective-permute-done.5.refs_1_
  49.0 0.0 all-to-all-done.1.came_ref
  49.0 0.7 carry.2.refs_1_.refs_4_
  49.7 2.7 %collective-permute-start.7 = (f32[176,512]{1,0:T(8,128)S(1)}, f32[176,512]{1,0:T(8,128)S(1)}, u32[]{:S(2)}, u32[]{:S(2)}) collective-permute-start(f32[176,512]{1,0:T(8,128)S(1)} %carry.2.refs_1_.refs_4_), channel_id=1, source_target_pairs={{0,1},{1,2},{2,3},{3,0},{4,5},{5,6},{6,7},{7,4},{8,9},{9,10},{10,1... | collective-permute-start | bytes 1081352 | tf_op jit(solution)/shard_map/ppermute | solution.py:497
  52.4 1.2 collective-permute-start.6
  53.6 3.5 %product.11 = f32[8,128,128]{2,1,0:T(8,128)} custom-call(bf16[4,4,1024,256]{3,2,1,0:T(8,128)(2,1)} %get-tuple-element.34.refs_0_.refs_1_, f32[128,512]{1,0:T(8,128)S(1)} %collective-permute-done.5.refs_1_, f32[128,1024]{1,0:T(8,128)} %get-tuple-element.41.refs_2_), custom_call_target="tpu_custom_call" | custom-call | flops 1024 | bytes 1024 | tf_op jit(solution)/shard_map/product/pallas_call | solution.py:394
  57.1 3.8 %all-to-all-start.3 = ((f32[8,128,128]{2,1,0:T(8,128)}), f32[8,128,128]{2,1,0:T(8,128)S(1)}, u32[]{:S(2)}, u32[]{:S(2)}) async-start(f32[8,128,128]{2,1,0:T(8,128)} %product.11), calls=%async_computation.3 | async-start | bytes 1048576 | tf_op jit(solution)/shard_map/all_to_all | solution.py:501
  60.9 2.0 %collective-permute-done.7.refs_2_.refs_7_ = f32[176,512]{1,0:T(8,128)S(1)} collective-permute-done((f32[176,512]{1,0:T(8,128)S(1)}, f32[176,512]{1,0:T(8,128)S(1)}, u32[]{:S(2)}, u32[]{:S(2)}) %collective-permute-start.7) | collective-permute-done | bytes 360480 | tf_op jit(solution)/shard_map/ppermute | solution.py:497
  62.9 5.1 %collective-permute-done.6.refs_3_.refs_5_ = f32[176,512]{1,0:T(8,128)S(1)} collective-permute-done((f32[176,512]{1,0:T(8,128)S(1)}, f32[176,512]{1,0:T(8,128)S(1)}, u32[]{:S(2)}, u32[]{:S(2)}) %collective-permute-start.6) | collective-permute-done | bytes 360480 | tf_op jit(solution)/shard_map/ppermute | solution.py:497
  68.0 0.1 select_select_fusion
  68.1 0.8 collective-permute-start.8
  69.0 5.5 %product.9 = (f32[128,1024]{1,0:T(8,128)}, f32[128,512]{1,0:T(8,128)S(1)}) custom-call(bf16[4,4,1024,256]{3,2,1,0:T(8,128)(2,1)} %get-tuple-element.34.refs_0_.refs_1_, f32[176,512]{1,0:T(8,128)S(1)} %carry.2.refs_1_.refs_4_, f32[176,512]{1,0:T(8,128)S(1)} %collective-permute-done.7.refs_2_.refs_7_, f32[176,512]{1,0:T(8,128)S(1)} %collective-permute-done.6.refs_3_.refs_5_, ...), custom_call_target="tpu_custom_call" | custom-call | flops 17179869184 | bytes 67108864 | tf_op jit(solution)/shard_map/product/pallas_call | solution.py:394
  74.5 4.2 %collective-permute-done.8.refs_2_.refs_6_ = f32[176,512]{1,0:T(8,128)S(1)} collective-permute-done((f32[176,512]{1,0:T(8,128)S(1)}, f32[176,512]{1,0:T(8,128)S(1)}, u32[]{:S(2)}, u32[]{:S(2)}) %collective-permute-start.8) | collective-permute-done | bytes 360480 | tf_op jit(solution)/shard_map/ppermute | solution.py:511
  78.7 0.0 all-to-all-done.3.came_ref
  78.7 0.7 carry.3.refs_1_
  79.3 1.5 %collective-permute-start.10 = (f32[128,512]{1,0:T(8,128)S(1)}, f32[128,512]{1,0:T(8,128)S(1)}, u32[]{:S(2)}, u32[]{:S(2)}) collective-permute-start(f32[128,512]{1,0:T(8,128)S(1)} %carry.3.refs_1_), channel_id=1, source_target_pairs={{0,1},{1,2},{2,3},{3,0},{4,5},{5,6},{6,7},{7,4},{8,9},{9,10},{10,1... | collective-permute-start | bytes 786440 | tf_op jit(solution)/shard_map/ppermute | solution.py:497
  80.9 2.3 %collective-permute-start.9 = (f32[128,512]{1,0:T(8,128)S(1)}, f32[128,512]{1,0:T(8,128)S(1)}, u32[]{:S(2)}, u32[]{:S(2)}) collective-permute-start(f32[128,512]{1,0:T(8,128)S(1)} %carry.3.refs_1_), channel_id=1, source_target_pairs={{0,3},{1,0},{2,1},{3,2},{4,7},{5,4},{6,5},{7,6},{8,11},{9,8},{10,9... | collective-permute-start | bytes 786440 | tf_op jit(solution)/shard_map/ppermute | solution.py:497
  83.2 3.5 %product.10 = f32[8,224,128]{2,1,0:T(8,128)} custom-call(s32[1]{0:T(128)} %bitcast.2.ids_ref.refs_0_, bf16[4,4,1024,256]{3,2,1,0:T(8,128)(2,1)} %get-tuple-element.34.refs_0_.refs_1_, f32[176,512]{1,0:T(8,128)S(1)} %collective-permute-done.8.refs_2_.refs_6_, f32[128,1024]{1,0:T(8,128)} %get-tuple-element.48.refs_3_, f32[176,512]{1,0:T(8,128)S(1)} %carry.2.refs_1_.refs_4_, ...), custom_call_target="tpu_custom_call" | custom-call | flops 1024 | bytes 1024 | tf_op jit(solution)/shard_map/product/pallas_call | solution.py:394
  86.8 3.9 %all-to-all-start.2 = ((f32[8,224,128]{2,1,0:T(8,128)}), f32[8,224,128]{2,1,0:T(8,128)S(1)}, u32[]{:S(2)}, u32[]{:S(2)}) async-start(f32[8,224,128]{2,1,0:T(8,128)} %product.10), calls=%async_computation.2 | async-start | bytes 1835008 | tf_op jit(solution)/shard_map/all_to_all | solution.py:501
  90.6 0.0 collective-permute-done.10.refs_3_
  90.6 2.4 %collective-permute-done.9.refs_2_ = f32[128,512]{1,0:T(8,128)S(1)} collective-permute-done((f32[128,512]{1,0:T(8,128)S(1)}, f32[128,512]{1,0:T(8,128)S(1)}, u32[]{:S(2)}, u32[]{:S(2)}) %collective-permute-start.9) | collective-permute-done | bytes 262176 | tf_op jit(solution)/shard_map/ppermute | solution.py:497
  93.1 0.1 select_select_fusion.1
  93.1 1.7 %collective-permute-start.11 = (f32[128,512]{1,0:T(8,128)S(1)}, f32[128,512]{1,0:T(8,128)S(1)}, u32[]{:S(2)}, u32[]{:S(2)}) collective-permute-start(f32[128,512]{1,0:T(8,128)S(1)} %select_select_fusion.1), channel_id=1, source_target_pairs={{1,0},{2,3},{3,1},{0,2},{5,4},{6,7},{7,5},{4,6},{9,8},{10,11},{11,... | collective-permute-start | bytes 786440 | tf_op jit(solution)/shard_map/ppermute | solution.py:511
  94.8 5.5 %product.12.refs_3_ = f32[128,1024]{1,0:T(8,128)} custom-call(bf16[4,4,1024,256]{3,2,1,0:T(8,128)(2,1)} %get-tuple-element.34.refs_0_.refs_1_, f32[128,512]{1,0:T(8,128)S(1)} %carry.3.refs_1_, f32[128,512]{1,0:T(8,128)S(1)} %collective-permute-done.9.refs_2_, f32[128,512]{1,0:T(8,128)S(1)} %collective-permute-done.10.refs_3_), custom_call_target="tpu_custom_call" | custom-call | flops 17179869184 | bytes 67108864 | tf_op jit(solution)/shard_map/product/pallas_call | solution.py:394
  100.3 0.0 collective-permute-done.11.refs_2_
  100.3 2.9 %product.13 = (f32[128,128]{1,0:T(8,128)S(1)}, f32[128,128]{1,0:T(8,128)S(1)}, f32[128,128]{1,0:T(8,128)S(1)}, f32[128,128]{1,0:T(8,128)S(1)}, f32[128,128]{1,0:...) custom-call(s32[1]{0:T(128)} %bitcast.refs_0_.row_ref, ...), custom_call_target="tpu_custom_call" | custom-call | flops 1024 | bytes 1024 | tf_op jit(solution)/shard_map/product/pallas_call | solution.py:394
  103.3 2.3 %collective-permute-start.12 = (f32[128,128]{1,0:T(8,128)S(1)}, f32[128,128]{1,0:T(8,128)S(1)}, u32[]{:S(2)}, u32[]{:S(2)}) collective-permute-start(f32[128,128]{1,0:T(8,128)S(1)} %get-tuple-element.52), channel_id=1, source_target_pairs={{0,16},{4,20},{8,24},{12,28},{16,0},{20,4},{24,8},{28,12},{1,17},{... | collective-permute-start | bytes 196616 | tf_op jit(solution)/shard_map/ppermute | solution.py:597
  105.5 0.0 collective-permute-start.13
  105.5 1.6 %collective-permute-start.14 = (f32[128,128]{1,0:T(8,128)S(1)}, f32[128,128]{1,0:T(8,128)S(1)}, u32[]{:S(2)}, u32[]{:S(2)}) collective-permute-start(f32[128,128]{1,0:T(8,128)S(1)} %get-tuple-element.54), channel_id=1, source_target_pairs={{0,24},{4,28},{8,16},{12,20},{16,8},{20,12},{24,0},{28,4},{1,25},{... | collective-permute-start | bytes 196616 | tf_op jit(solution)/shard_map/ppermute | solution.py:597
  107.1 0.9 collective-permute-start.15
  108.0 1.7 %collective-permute-done.13.refs_5_ = f32[128,128]{1,0:T(8,128)S(1)} collective-permute-done((f32[128,128]{1,0:T(8,128)S(1)}, f32[128,128]{1,0:T(8,128)S(1)}, u32[]{:S(2)}, u32[]{:S(2)}) %collective-permute-start.13) | collective-permute-done | bytes 65568 | tf_op jit(solution)/shard_map/ppermute | solution.py:597
  109.7 1.0 collective-permute-done.14.refs_6_
  110.7 1.0 collective-permute-done.15.refs_7_
  111.7 0.0 all-to-all-done.2.own_ref.left_ref
  111.7 0.8 collective-permute-start.16
  112.5 0.0 collective-permute-start.17
  112.5 1.6 %collective-permute-start.18 = (f32[128,128]{1,0:T(8,128)S(1)}, f32[128,128]{1,0:T(8,128)S(1)}, u32[]{:S(2)}, u32[]{:S(2)}) collective-permute-start(f32[128,128]{1,0:T(8,128)S(1)} %get-tuple-element.60), channel_id=1, source_target_pairs={{0,8},{4,12},{8,0},{12,4},{16,24},{20,28},{24,16},{28,20},{1,9},{5... | collective-permute-start | bytes 196616 | tf_op jit(solution)/shard_map/ppermute | solution.py:597
  114.1 0.2 collective-permute-start.19
  114.4 0.2 collective-permute-done.16.other_ref
  114.6 1.2 %assemble.1 = f32[3,256,256]{2,1,0:T(8,128)} custom-call(s32[1]{0:T(128)} %bitcast.refs_0_.row_ref, f32[8,224,128]{2,1,0:T(8,128)S(1)} %all-to-all-done.2.own_ref.left_ref, f32[8,224,128]{2,1,0:T(8,128)S(1)} %collective-permute-done.16.other_ref), custom_call_target="tpu_custom_call" | custom-call | flops 1024 | bytes 1024 | tf_op jit(solution)/shard_map/assemble/pallas_call | solution.py:481
  115.8 1.2 collective-permute-done.18.refs_2_
  117.0 1.2 collective-permute-done.19.refs_3_
  118.2 1.8 %finish.1 = f32[512,256]{1,0:T(8,128)} custom-call(s32[1]{0:T(128)} %bitcast.refs_0_.row_ref, s32[8]{0:T(128)S(1)} %bitcast.5, f32[256,512]{1,0:T(8,128)S(1)} %get-tuple-element.57.base_ref, f32[8,224,128]{2,1,0:T(8,128)S(1)} %all-to-all-done.2.own_ref.left_ref, f32[128,128]{1,0:T(8,128)S(1)} %get-tuple-element.58.refs_0_, ...), custom_call_target="tpu_custom_call" | custom-call | flops 1024 | bytes 1024 | tf_op jit(solution)/shard_map/finish/pallas_call | solution.py:454
  (4 shorter events, 0.0 us)
Async XLA Ops:
  2.4 14.4 %collective-permute-start.1 = (f32[128,512]{1,0:T(8,128)S(1)}, f32[128,512]{1,0:T(8,128)S(1)}, u32[]{:S(2)}, u32[]{:S(2)}) collective-permute-start(f32[128,512]{1,0:T(8,128)S(1)} %get-tuple-element.32.first_ref.refs_0_), channel_id=1, source_target_pairs={{0,3},{1,0},{2,1},{3,2},{4,7},{5,4},{6,5},{7,6},{8,11},{9,8},{10,9... | collective-permute-start | bytes 786440 | tf_op jit(solution)/shard_map/ppermute | solution.py:497
  7.5 12.1 %collective-permute-start = (f32[128,512]{1,0:T(8,128)S(1)}, f32[128,512]{1,0:T(8,128)S(1)}, u32[]{:S(2)}, u32[]{:S(2)}) collective-permute-start(f32[128,512]{1,0:T(8,128)S(1)} %get-tuple-element.32.first_ref.refs_0_), channel_id=1, source_target_pairs={{0,1},{1,2},{2,3},{3,0},{4,5},{5,6},{6,7},{7,4},{8,9},{9,10},{10,1... | collective-permute-start | bytes 786440 | tf_op jit(solution)/shard_map/ppermute | solution.py:497
  12.4 19.2 %all-to-all-start = ((f32[8,192,128]{2,1,0:T(8,128)}), f32[8,192,128]{2,1,0:T(8,128)S(1)}, u32[]{:S(2)}, u32[]{:S(2)}) async-start(f32[8,192,128]{2,1,0:T(8,128)} %get-tuple-element.44), calls=%async_computation | async-start | bytes 1572864 | tf_op jit(solution)/shard_map/all_to_all | solution.py:501
  19.6 8.1 %collective-permute-start.2 = (f32[128,512]{1,0:T(8,128)S(1)}, f32[128,512]{1,0:T(8,128)S(1)}, u32[]{:S(2)}, u32[]{:S(2)}) collective-permute-start(f32[128,512]{1,0:T(8,128)S(1)} %select_select_fusion.3), channel_id=1, source_target_pairs={{1,0},{2,3},{3,1},{0,2},{5,4},{6,7},{7,5},{4,6},{9,8},{10,11},{11,... | collective-permute-start | bytes 786440 | tf_op jit(solution)/shard_map/ppermute | solution.py:511
  27.7 11.1 %collective-permute-start.4 = (f32[128,512]{1,0:T(8,128)S(1)}, f32[128,512]{1,0:T(8,128)S(1)}, u32[]{:S(2)}, u32[]{:S(2)}) collective-permute-start(f32[128,512]{1,0:T(8,128)S(1)} %get-tuple-element.38.refs_1_), channel_id=1, source_target_pairs={{0,1},{1,2},{2,3},{3,0},{4,5},{5,6},{6,7},{7,4},{8,9},{9,10},{10,1... | collective-permute-start | bytes 786440 | tf_op jit(solution)/shard_map/ppermute | solution.py:497
  29.4 11.9 %collective-permute-start.3 = (f32[128,512]{1,0:T(8,128)S(1)}, f32[128,512]{1,0:T(8,128)S(1)}, u32[]{:S(2)}, u32[]{:S(2)}) collective-permute-start(f32[128,512]{1,0:T(8,128)S(1)} %get-tuple-element.38.refs_1_), channel_id=1, source_target_pairs={{0,3},{1,0},{2,1},{3,2},{4,7},{5,4},{6,5},{7,6},{8,11},{9,8},{10,9... | collective-permute-start | bytes 786440 | tf_op jit(solution)/shard_map/ppermute | solution.py:497
  34.8 14.1 %all-to-all-start.1 = ((f32[8,128,128]{2,1,0:T(8,128)}), f32[8,128,128]{2,1,0:T(8,128)S(1)}, u32[]{:S(2)}, u32[]{:S(2)}) async-start(f32[8,128,128]{2,1,0:T(8,128)} %product.8), calls=%async_computation.1 | async-start | bytes 1048576 | tf_op jit(solution)/shard_map/all_to_all | solution.py:501
  41.3 7.6 %collective-permute-start.5 = (f32[128,512]{1,0:T(8,128)S(1)}, f32[128,512]{1,0:T(8,128)S(1)}, u32[]{:S(2)}, u32[]{:S(2)}) collective-permute-start(f32[128,512]{1,0:T(8,128)S(1)} %select_select_fusion.2), channel_id=1, source_target_pairs={{1,0},{2,3},{3,1},{0,2},{5,4},{6,7},{7,5},{4,6},{9,8},{10,11},{11,... | collective-permute-start | bytes 786440 | tf_op jit(solution)/shard_map/ppermute | solution.py:511
  42.9 6.1 %copy-start = (s32[1,8,1]{1,2,0:T(1,128)S(1)}, s32[1,8,1]{1,2,0:T(1,128)}, u32[]{:S(2)}) copy-start(s32[1,8,1]{1,2,0:T(1,128)} %param.20) | copy-start | bytes 100
  49.7 13.2 %collective-permute-start.7 = (f32[176,512]{1,0:T(8,128)S(1)}, f32[176,512]{1,0:T(8,128)S(1)}, u32[]{:S(2)}, u32[]{:S(2)}) collective-permute-start(f32[176,512]{1,0:T(8,128)S(1)} %carry.2.refs_1_.refs_4_), channel_id=1, source_target_pairs={{0,1},{1,2},{2,3},{3,0},{4,5},{5,6},{6,7},{7,4},{8,9},{9,10},{10,1... | collective-permute-start | bytes 1081352 | tf_op jit(solution)/shard_map/ppermute | solution.py:497
  52.4 15.7 %collective-permute-start.6 = (f32[176,512]{1,0:T(8,128)S(1)}, f32[176,512]{1,0:T(8,128)S(1)}, u32[]{:S(2)}, u32[]{:S(2)}) collective-permute-start(f32[176,512]{1,0:T(8,128)S(1)} %carry.2.refs_1_.refs_4_), channel_id=1, source_target_pairs={{0,3},{1,0},{2,1},{3,2},{4,7},{5,4},{6,5},{7,6},{8,11},{9,8},{10,9... | collective-permute-start | bytes 1081352 | tf_op jit(solution)/shard_map/ppermute | solution.py:497
  57.1 21.6 %all-to-all-start.3 = ((f32[8,128,128]{2,1,0:T(8,128)}), f32[8,128,128]{2,1,0:T(8,128)S(1)}, u32[]{:S(2)}, u32[]{:S(2)}) async-start(f32[8,128,128]{2,1,0:T(8,128)} %product.11), calls=%async_computation.3 | async-start | bytes 1048576 | tf_op jit(solution)/shard_map/all_to_all | solution.py:501
  68.1 10.5 %collective-permute-start.8 = (f32[176,512]{1,0:T(8,128)S(1)}, f32[176,512]{1,0:T(8,128)S(1)}, u32[]{:S(2)}, u32[]{:S(2)}) collective-permute-start(f32[176,512]{1,0:T(8,128)S(1)} %select_select_fusion), channel_id=1, source_target_pairs={{1,0},{2,3},{3,1},{0,2},{5,4},{6,7},{7,5},{4,6},{9,8},{10,11},{11,... | collective-permute-start | bytes 1081352 | tf_op jit(solution)/shard_map/ppermute | solution.py:511
  79.3 11.3 %collective-permute-start.10 = (f32[128,512]{1,0:T(8,128)S(1)}, f32[128,512]{1,0:T(8,128)S(1)}, u32[]{:S(2)}, u32[]{:S(2)}) collective-permute-start(f32[128,512]{1,0:T(8,128)S(1)} %carry.3.refs_1_), channel_id=1, source_target_pairs={{0,1},{1,2},{2,3},{3,0},{4,5},{5,6},{6,7},{7,4},{8,9},{9,10},{10,1... | collective-permute-start | bytes 786440 | tf_op jit(solution)/shard_map/ppermute | solution.py:497
  80.9 12.2 %collective-permute-start.9 = (f32[128,512]{1,0:T(8,128)S(1)}, f32[128,512]{1,0:T(8,128)S(1)}, u32[]{:S(2)}, u32[]{:S(2)}) collective-permute-start(f32[128,512]{1,0:T(8,128)S(1)} %carry.3.refs_1_), channel_id=1, source_target_pairs={{0,3},{1,0},{2,1},{3,2},{4,7},{5,4},{6,5},{7,6},{8,11},{9,8},{10,9... | collective-permute-start | bytes 786440 | tf_op jit(solution)/shard_map/ppermute | solution.py:497
  86.8 25.0 %all-to-all-start.2 = ((f32[8,224,128]{2,1,0:T(8,128)}), f32[8,224,128]{2,1,0:T(8,128)S(1)}, u32[]{:S(2)}, u32[]{:S(2)}) async-start(f32[8,224,128]{2,1,0:T(8,128)} %product.10), calls=%async_computation.2 | async-start | bytes 1835008 | tf_op jit(solution)/shard_map/all_to_all | solution.py:501
  93.1 7.2 %collective-permute-start.11 = (f32[128,512]{1,0:T(8,128)S(1)}, f32[128,512]{1,0:T(8,128)S(1)}, u32[]{:S(2)}, u32[]{:S(2)}) collective-permute-start(f32[128,512]{1,0:T(8,128)S(1)} %select_select_fusion.1), channel_id=1, source_target_pairs={{1,0},{2,3},{3,1},{0,2},{5,4},{6,7},{7,5},{4,6},{9,8},{10,11},{11,... | collective-permute-start | bytes 786440 | tf_op jit(solution)/shard_map/ppermute | solution.py:511
  103.3 4.7 %collective-permute-start.12 = (f32[128,128]{1,0:T(8,128)S(1)}, f32[128,128]{1,0:T(8,128)S(1)}, u32[]{:S(2)}, u32[]{:S(2)}) collective-permute-start(f32[128,128]{1,0:T(8,128)S(1)} %get-tuple-element.52), channel_id=1, source_target_pairs={{0,16},{4,20},{8,24},{12,28},{16,0},{20,4},{24,8},{28,12},{1,17},{... | collective-permute-start | bytes 196616 | tf_op jit(solution)/shard_map/ppermute | solution.py:597
  105.5 4.1 %collective-permute-start.13 = (f32[128,128]{1,0:T(8,128)S(1)}, f32[128,128]{1,0:T(8,128)S(1)}, u32[]{:S(2)}, u32[]{:S(2)}) collective-permute-start(f32[128,128]{1,0:T(8,128)S(1)} %get-tuple-element.53), channel_id=1, source_target_pairs={{0,20},{4,16},{8,28},{12,24},{16,4},{20,0},{24,12},{28,8},{1,21},{... | collective-permute-start | bytes 196616 | tf_op jit(solution)/shard_map/ppermute | solution.py:597
  105.5 5.2 %collective-permute-start.14 = (f32[128,128]{1,0:T(8,128)S(1)}, f32[128,128]{1,0:T(8,128)S(1)}, u32[]{:S(2)}, u32[]{:S(2)}) collective-permute-start(f32[128,128]{1,0:T(8,128)S(1)} %get-tuple-element.54), channel_id=1, source_target_pairs={{0,24},{4,28},{8,16},{12,20},{16,8},{20,12},{24,0},{28,4},{1,25},{... | collective-permute-start | bytes 196616 | tf_op jit(solution)/shard_map/ppermute | solution.py:597
  107.1 4.6 %collective-permute-start.15 = (f32[128,128]{1,0:T(8,128)S(1)}, f32[128,128]{1,0:T(8,128)S(1)}, u32[]{:S(2)}, u32[]{:S(2)}) collective-permute-start(f32[128,128]{1,0:T(8,128)S(1)} %get-tuple-element.55), channel_id=1, source_target_pairs={{0,28},{4,24},{8,20},{12,16},{16,12},{20,8},{24,4},{28,0},{1,29},{... | collective-permute-start | bytes 196616 | tf_op jit(solution)/shard_map/ppermute | solution.py:597
  111.7 2.9 %collective-permute-start.16 = (f32[8,224,128]{2,1,0:T(8,128)S(1)}, f32[8,224,128]{2,1,0:T(8,128)S(1)}, u32[]{:S(2)}, u32[]{:S(2)}) collective-permute-start(f32[8,224,128]{2,1,0:T(8,128)S(1)} %all-to-all-done.2.own_ref.left_ref), channel_id=1, source_target_pairs={{0,4},{4,0},{8,12},{12,8},{16,20},{20,16},{24,28},{28,24},{1,5},{5... | collective-permute-start | bytes 2752520 | tf_op jit(solution)/shard_map/ppermute | solution.py:598
  112.5 3.3 %collective-permute-start.17 = (f32[128,128]{1,0:T(8,128)S(1)}, f32[128,128]{1,0:T(8,128)S(1)}, u32[]{:S(2)}, u32[]{:S(2)}) collective-permute-start(f32[128,128]{1,0:T(8,128)S(1)} %get-tuple-element.59), channel_id=1, source_target_pairs={{0,4},{4,0},{8,12},{12,8},{16,20},{20,16},{24,28},{28,24},{1,5},{5... | collective-permute-start | bytes 196616 | tf_op jit(solution)/shard_map/ppermute | solution.py:597
  112.5 4.5 %collective-permute-start.18 = (f32[128,128]{1,0:T(8,128)S(1)}, f32[128,128]{1,0:T(8,128)S(1)}, u32[]{:S(2)}, u32[]{:S(2)}) collective-permute-start(f32[128,128]{1,0:T(8,128)S(1)} %get-tuple-element.60), channel_id=1, source_target_pairs={{0,8},{4,12},{8,0},{12,4},{16,24},{20,28},{24,16},{28,20},{1,9},{5... | collective-permute-start | bytes 196616 | tf_op jit(solution)/shard_map/ppermute | solution.py:597
  114.1 4.0 %collective-permute-start.19 = (f32[128,128]{1,0:T(8,128)S(1)}, f32[128,128]{1,0:T(8,128)S(1)}, u32[]{:S(2)}, u32[]{:S(2)}) collective-permute-start(f32[128,128]{1,0:T(8,128)S(1)} %get-tuple-element.61), channel_id=1, source_target_pairs={{0,12},{4,8},{8,4},{12,0},{16,28},{20,24},{24,20},{28,16},{1,13},{... | collective-permute-start | bytes 196616 | tf_op jit(solution)/shard_map/ppermute | solution.py:597

commit v21 on v20

--- a/solution.py
+++ b/solution.py
@@ -324,11 +324,9 @@
         for k in range(1, n_col):
             share = share + ordered[k]
         rows = share.shape[0]
-        groups = NODES_DEV // LANES // 2
-        for j in range(groups):
+        for j in range(NODES_DEV // LANES):
             for q in range(n_row):
-                from_lane = (q % 2 * groups + j) * LANES
-                out[q, H + j * rows : H + (j + 1) * rows, :] = share[:, from_lane : from_lane + LANES]
+                out[q, H + j * rows : H + (j + 1) * rows, :] = share[:, j * LANES : (j + 1) * LANES]
     sent = []
     for p in range(n_row // 2):
         here = slice(p * WIDE, (p + 1) * WIDE)
@@ -370,7 +368,7 @@
     has_prev = prev is not None
     has_base = base is not None
     rows = carriers[0].shape[0] - H if carriers else 0
-    under = rows * NODES_DEV // LANES // 2
+    under = rows * NODES_DEV // LANES
     shape = (n_row, H + under, TB) if last else (H, n_row * TB)
     scratch = [
         pltpu.VMEM((n, H, NODES_DEV), F32),
@@ -463,34 +461,28 @@
     )(row, owners, base, left, *right)
 
 
-def assemble_kernel(n_row, row_ref, own_ref, other_ref, out_ref, halves, turned):
+def assemble_kernel(n_row, came_ref, out_ref, turned):
     rows = F // n_row
-    half = lax.rem(row_ref[0], 2)
-    halves[half] = own_ref[:, H:, :]
-    halves[1 - half] = other_ref[:, H:, :]
-    groups = 3 * F // LANES // 2
+    per = F // LANES
     for q in range(n_row):
-        for j in range(2 * groups):
-            here = slice(j % groups * rows, (j % groups + 1) * rows)
-            turned[q * rows : (q + 1) * rows, j * LANES : (j + 1) * LANES] = halves[j // groups, q, here, :]
+        for j in range(3 * per):
+            here = slice(H + j * rows, H + (j + 1) * rows)
+            turned[q * rows : (q + 1) * rows, j * LANES : (j + 1) * LANES] = came_ref[q, here, :]
     for k in range(3):
         out_ref[k] = turned[:, k * F : (k + 1) * F].T
 
 
-def assemble(n_row, row, own, other):
+def assemble(n_row, came):
     return pl.pallas_call(
         functools.partial(assemble_kernel, n_row),
-        in_specs=[SMEM, VMEM, VMEM],
+        in_specs=[VMEM],
         out_specs=VMEM,
         out_shape=jax.ShapeDtypeStruct((3, F, F), F32),
-        scratch_shapes=[
-            pltpu.VMEM((2, n_row, own.shape[1] - H, LANES), F32),
-            pltpu.VMEM((F, 3 * F), F32),
-        ],
+        scratch_shapes=[pltpu.VMEM((F, 3 * F), F32)],
         compiler_params=params(16),
         cost_estimate=LIGHT,
         name="assemble",
-    )(row, own, other)
+    )(came)
 
 
 def shift(n_col, x, step):
@@ -588,15 +580,16 @@
 
     right_carried = carry(n_row, owners, after(one_right, left_early, steps[-1][0][1]), right_came)
     right_steps = gather(n_col, right_carried, -1)
-    left_came = exchange(final(*common, steps, left_early, carrying=True))
+    left_last = final(*common, steps, left_early, carrying=True)
+    left_came = exchange(left_last)
+    right_steps[0] = [(0, after(right_carried, left_last))]
     right_early = early(*common, right_steps)
 
     right_last = final(*common, right_steps, right_early, apart=True)
     right_came = [right_last[0]] * n_row
     for j in range(n_row - 1, 0, -1):
         right_came[j] = lax.ppermute(right_last[j], "row", [(r, r ^ j) for r in range(n_row)])
-    other = lax.ppermute(after(left_came, *right_came[n_row // 2 :]), "row", [(r, r ^ 1) for r in range(n_row)])
-    weight_grad = assemble(n_row, row, left_came, other)
+    weight_grad = assemble(n_row, left_came)
     return finish(n_row, row, owners, after(diff, weight_grad), left_came, right_came), weight_grad
 
 

time: 121 us -> 118 us (0.975)
  waiting for transfers between devices: 26.2 us -> 23.7 us
    ppermute x7, waiting for transfers between devices: 6.07 us -> 3.84 us  [per_device(): lax.ppermute(right_last[j], 'row', [(r, r ^ j) for r in range(n_row)])]
  transfers between devices with their start and end apart: 24 -> 23, of which waited for: 14 -> 12; matrix products, arithmetic and copies ran while one was open for 0% -> 0% of each run, Pallas kernels for 36% -> 37%
where the time goes in v21:
time: 118 us; the launch traced here: 117 us
  Pallas kernels  47.9 us (41%)
  starting transfers between devices  43.5 us (37%)
  waiting for transfers between devices  23.7 us (20%)
  between operations  1.44 us (1%)
    pallas_call x7, Pallas kernels, product(): pl.pallas_call(functools.partial(product_kernel, n_row, n_col, origins, h...  29.7 us
    ppermute x8, starting transfers between devices, shift(): lax.ppermute(x, 'col', [(c, (c + step) % n_col) for c in range(n_col)])  16.7 us
    all_to_all x4, starting transfers between devices, exchange(): lax.all_to_all(pieces, 'row', split_axis=0, concat_axis=0, tiled=True)  15.2 us
    ppermute x8, waiting for transfers between devices, shift(): lax.ppermute(x, 'col', [(c, (c + step) % n_col) for c in range(n_col)])  15 us
    pallas_call x1, Pallas kernels, build_operator(): pl.pallas_call(functools.partial(operator_kernel, n_row, n_col, origins),...  7.29 us
    ppermute x7, starting transfers between devices, per_device(): lax.ppermute(right_last[j], 'row', [(r, r ^ j) for r in range(n_row)])  6.81 us
    pallas_call x1, Pallas kernels, local_terms(): pl.pallas_call(functools.partial(local_kernel, n_row), in_specs=[ANY] + [...  4.88 us
    ppermute x4, waiting for transfers between devices, opposite(): return lax.ppermute(sent, 'col', [(1, 0), (2, 3), (3, 1), (0, 2)])  4.87 us
  transfers between devices with their start and end apart: 23, of which 12 were waited for; matrix products, arithmetic and copies ran while one was open for 0% of the time, Pallas kernels for 37%

profile of v21, /device:TPU:0, one launch (start us, length us, event | category | flops | bytes accessed | tf_op | source)
XLA Modules:
  0.0 116.8 jit_solution(11344901714179151033)
XLA Ops:
  0.6 1.7 %term_two.1 = (f32[128,512]{1,0:T(8,128)S(1)}, f32[128,512]{1,0:T(8,128)S(1)}) custom-call(f32[512,256]{1,0:T(8,128)} %grad_hbm.3, s32[512,256]{1,0:T(8,128)} %mask_hbm.3, f32[3,256,256]{2,1,0:T(8,128)} %weight_hbm.3), custom_call_target="tpu_custom_call" | custom-call | flops 1024 | bytes 1024 | tf_op jit(solution)/shard_map/term_two/pallas_call | solution.py:78
  2.4 5.1 %collective-permute-start.1 = (f32[128,512]{1,0:T(8,128)S(1)}, f32[128,512]{1,0:T(8,128)S(1)}, u32[]{:S(2)}, u32[]{:S(2)}) collective-permute-start(f32[128,512]{1,0:T(8,128)S(1)} %get-tuple-element.32.first_ref.refs_0_), channel_id=1, source_target_pairs={{0,3},{1,0},{2,1},{3,2},{4,7},{5,4},{6,5},{7,6},{8,11},{9,8},{10,9... | collective-permute-start | bytes 786440 | tf_op jit(solution)/shard_map/ppermute | solution.py:489
  7.5 0.0 collective-permute-start
  7.5 4.9 %local_terms.1 = (f32[128,512]{1,0:T(8,128)}, f32[128,512]{1,0:T(8,128)}, f32[256,512]{1,0:T(8,128)S(1)}, f32[8,192,128]{2,1,0:T(8,128)}) custom-call(f32[128,512]{1,0:T(8,128)S(1)} %get-tuple-element.32.first_ref.refs_0_, f32[512,256]{1,0:T(8,128)} %grad_hbm.3, s32[512,256]{1,0:T(8,128)} %mask_hbm.3, f32[3,256,256]{2,1,0:T(8,128)} %weight_hbm.3, ...), custom_call_target="tpu_custom_call" | custom-call | flops 1024 | bytes 1024 | tf_op jit(solution)/shard_map/local_terms/pallas_call | solution.py:125
  12.4 3.7 %all-to-all-start = ((f32[8,192,128]{2,1,0:T(8,128)}), f32[8,192,128]{2,1,0:T(8,128)S(1)}, u32[]{:S(2)}, u32[]{:S(2)}) async-start(f32[8,192,128]{2,1,0:T(8,128)} %get-tuple-element.44), calls=%async_computation | async-start | bytes 1572864 | tf_op jit(solution)/shard_map/all_to_all | solution.py:493
  16.8 0.0 collective-permute-done.1.refs_2_
  16.8 2.8 %collective-permute-done.refs_1_ = f32[128,512]{1,0:T(8,128)S(1)} collective-permute-done((f32[128,512]{1,0:T(8,128)S(1)}, f32[128,512]{1,0:T(8,128)S(1)}, u32[]{:S(2)}, u32[]{:S(2)}) %collective-permute-start) | collective-permute-done | bytes 262176 | tf_op jit(solution)/shard_map/ppermute | solution.py:489
  19.6 0.1 select_select_fusion.3
  19.6 0.8 collective-permute-start.2
  20.4 7.3 %operator.1 = (bf16[4,4,1024,256]{3,2,1,0:T(8,128)(2,1)}, f32[128,1024]{1,0:T(8,128)S(1)}) custom-call(s32[1]{0:T(128)} %bitcast.2.ids_ref.refs_0_, s32[1]{0:T(128)S(6)} %copy.13.live_ref, s32[1,128]{1,0:T(1,128)} %rows_hbm.1, s32[1,128]{1,0:T(1,128)} %slots_hbm.1, f32[1,128,128,128]{3,2,1,0:T(8,128)} %values_ref.1, ...), custom_call_target="tpu_custom_call" | custom-call | flops 17179869184 | bytes 67108864 | tf_op jit(solution)/shard_map/operator/pallas_call | solution.py:262
  27.7 0.0 collective-permute-done.2.refs_1_
  27.7 1.7 %collective-permute-start.4 = (f32[128,512]{1,0:T(8,128)S(1)}, f32[128,512]{1,0:T(8,128)S(1)}, u32[]{:S(2)}, u32[]{:S(2)}) collective-permute-start(f32[128,512]{1,0:T(8,128)S(1)} %get-tuple-element.38.refs_1_), channel_id=1, source_target_pairs={{0,1},{1,2},{2,3},{3,0},{4,5},{5,6},{6,7},{7,4},{8,9},{9,10},{10,1... | collective-permute-start | bytes 786440 | tf_op jit(solution)/shard_map/ppermute | solution.py:489
  29.4 2.2 %collective-permute-start.3 = (f32[128,512]{1,0:T(8,128)S(1)}, f32[128,512]{1,0:T(8,128)S(1)}, u32[]{:S(2)}, u32[]{:S(2)}) collective-permute-start(f32[128,512]{1,0:T(8,128)S(1)} %get-tuple-element.38.refs_1_), channel_id=1, source_target_pairs={{0,3},{1,0},{2,1},{3,2},{4,7},{5,4},{6,5},{7,6},{8,11},{9,8},{10,9... | collective-permute-start | bytes 786440 | tf_op jit(solution)/shard_map/ppermute | solution.py:489
  31.6 0.0 all-to-all-done.refs_0_
  31.6 3.2 %product.8 = f32[8,128,128]{2,1,0:T(8,128)} custom-call(bf16[4,4,1024,256]{3,2,1,0:T(8,128)(2,1)} %get-tuple-element.34.refs_0_.refs_1_, f32[128,512]{1,0:T(8,128)S(1)} %collective-permute-done.2.refs_1_, f32[128,1024]{1,0:T(8,128)S(1)} %get-tuple-element.45.refs_2_), custom_call_target="tpu_custom_call" | custom-call | flops 1024 | bytes 1024 | tf_op jit(solution)/shard_map/product/pallas_call | solution.py:392
  34.8 3.7 %all-to-all-start.1 = ((f32[8,128,128]{2,1,0:T(8,128)}), f32[8,128,128]{2,1,0:T(8,128)S(1)}, u32[]{:S(2)}, u32[]{:S(2)}) async-start(f32[8,128,128]{2,1,0:T(8,128)} %product.8), calls=%async_computation.1 | async-start | bytes 1048576 | tf_op jit(solution)/shard_map/all_to_all | solution.py:493
  38.6 0.2 collective-permute-done.4.refs_3_
  38.8 2.5 %collective-permute-done.3.refs_2_ = f32[128,512]{1,0:T(8,128)S(1)} collective-permute-done((f32[128,512]{1,0:T(8,128)S(1)}, f32[128,512]{1,0:T(8,128)S(1)}, u32[]{:S(2)}, u32[]{:S(2)}) %collective-permute-start.3) | collective-permute-done | bytes 262176 | tf_op jit(solution)/shard_map/ppermute | solution.py:489
  41.3 0.1 select_select_fusion.2
  41.3 1.5 %collective-permute-start.5 = (f32[128,512]{1,0:T(8,128)S(1)}, f32[128,512]{1,0:T(8,128)S(1)}, u32[]{:S(2)}, u32[]{:S(2)}) collective-permute-start(f32[128,512]{1,0:T(8,128)S(1)} %select_select_fusion.2), channel_id=1, source_target_pairs={{1,0},{2,3},{3,1},{0,2},{5,4},{6,7},{7,5},{4,6},{9,8},{10,11},{11,... | collective-permute-start | bytes 786440 | tf_op jit(solution)/shard_map/ppermute | solution.py:503
  42.8 5.5 %product.7 = (f32[128,1024]{1,0:T(8,128)}, f32[128,512]{1,0:T(8,128)S(1)}) custom-call(bf16[4,4,1024,256]{3,2,1,0:T(8,128)(2,1)} %get-tuple-element.34.refs_0_.refs_1_, f32[128,512]{1,0:T(8,128)S(1)} %get-tuple-element.38.refs_1_, f32[128,512]{1,0:T(8,128)S(1)} %collective-permute-done.3.refs_2_, f32[128,512]{1,0:T(8,128)S(1)} %collective-permute-done.4.refs_3_, ...), custom_call_target="tpu_custom_call" | custom-call | flops 17179869184 | bytes 67108864 | tf_op jit(solution)/shard_map/product/pallas_call | solution.py:392
  48.3 0.7 collective-permute-done.5.refs_1_
  49.0 0.0 all-to-all-done.1.came_ref
  49.0 0.7 carry.2.refs_1_.refs_4_
  49.7 2.7 %collective-permute-start.7 = (f32[176,512]{1,0:T(8,128)S(1)}, f32[176,512]{1,0:T(8,128)S(1)}, u32[]{:S(2)}, u32[]{:S(2)}) collective-permute-start(f32[176,512]{1,0:T(8,128)S(1)} %carry.2.refs_1_.refs_4_), channel_id=1, source_target_pairs={{0,1},{1,2},{2,3},{3,0},{4,5},{5,6},{6,7},{7,4},{8,9},{9,10},{10,1... | collective-permute-start | bytes 1081352 | tf_op jit(solution)/shard_map/ppermute | solution.py:489
  52.4 1.2 %collective-permute-start.6 = (f32[176,512]{1,0:T(8,128)S(1)}, f32[176,512]{1,0:T(8,128)S(1)}, u32[]{:S(2)}, u32[]{:S(2)}) collective-permute-start(f32[176,512]{1,0:T(8,128)S(1)} %carry.2.refs_1_.refs_4_), channel_id=1, source_target_pairs={{0,3},{1,0},{2,1},{3,2},{4,7},{5,4},{6,5},{7,6},{8,11},{9,8},{10,9... | collective-permute-start | bytes 1081352 | tf_op jit(solution)/shard_map/ppermute | solution.py:489
  53.6 3.5 %product.11 = f32[8,128,128]{2,1,0:T(8,128)} custom-call(bf16[4,4,1024,256]{3,2,1,0:T(8,128)(2,1)} %get-tuple-element.34.refs_0_.refs_1_, f32[128,512]{1,0:T(8,128)S(1)} %collective-permute-done.5.refs_1_, f32[128,1024]{1,0:T(8,128)} %get-tuple-element.41.refs_2_), custom_call_target="tpu_custom_call" | custom-call | flops 1024 | bytes 1024 | tf_op jit(solution)/shard_map/product/pallas_call | solution.py:392
  57.1 3.8 %all-to-all-start.3 = ((f32[8,128,128]{2,1,0:T(8,128)}), f32[8,128,128]{2,1,0:T(8,128)S(1)}, u32[]{:S(2)}, u32[]{:S(2)}) async-start(f32[8,128,128]{2,1,0:T(8,128)} %product.11), calls=%async_computation.3 | async-start | bytes 1048576 | tf_op jit(solution)/shard_map/all_to_all | solution.py:493
  60.9 2.0 %collective-permute-done.7.refs_2_.refs_7_ = f32[176,512]{1,0:T(8,128)S(1)} collective-permute-done((f32[176,512]{1,0:T(8,128)S(1)}, f32[176,512]{1,0:T(8,128)S(1)}, u32[]{:S(2)}, u32[]{:S(2)}) %collective-permute-start.7) | collective-permute-done | bytes 360480 | tf_op jit(solution)/shard_map/ppermute | solution.py:489
  62.9 5.1 %collective-permute-done.6.refs_3_.refs_5_ = f32[176,512]{1,0:T(8,128)S(1)} collective-permute-done((f32[176,512]{1,0:T(8,128)S(1)}, f32[176,512]{1,0:T(8,128)S(1)}, u32[]{:S(2)}, u32[]{:S(2)}) %collective-permute-start.6) | collective-permute-done | bytes 360480 | tf_op jit(solution)/shard_map/ppermute | solution.py:489
  68.0 0.1 select_select_fusion
  68.1 0.8 collective-permute-start.8
  69.0 5.5 %product.9 = (f32[128,1024]{1,0:T(8,128)}, f32[128,512]{1,0:T(8,128)S(1)}) custom-call(bf16[4,4,1024,256]{3,2,1,0:T(8,128)(2,1)} %get-tuple-element.34.refs_0_.refs_1_, f32[176,512]{1,0:T(8,128)S(1)} %carry.2.refs_1_.refs_4_, f32[176,512]{1,0:T(8,128)S(1)} %collective-permute-done.7.refs_2_.refs_7_, f32[176,512]{1,0:T(8,128)S(1)} %collective-permute-done.6.refs_3_.refs_5_, ...), custom_call_target="tpu_custom_call" | custom-call | flops 17179869184 | bytes 67108864 | tf_op jit(solution)/shard_map/product/pallas_call | solution.py:392
  74.5 4.2 %collective-permute-done.8.refs_2_.refs_6_ = f32[176,512]{1,0:T(8,128)S(1)} collective-permute-done((f32[176,512]{1,0:T(8,128)S(1)}, f32[176,512]{1,0:T(8,128)S(1)}, u32[]{:S(2)}, u32[]{:S(2)}) %collective-permute-start.8) | collective-permute-done | bytes 360480 | tf_op jit(solution)/shard_map/ppermute | solution.py:503
  78.7 0.0 all-to-all-done.3.came_ref
  78.7 0.7 carry.3.refs_1_
  79.3 1.5 %collective-permute-start.10 = (f32[128,512]{1,0:T(8,128)S(1)}, f32[128,512]{1,0:T(8,128)S(1)}, u32[]{:S(2)}, u32[]{:S(2)}) collective-permute-start(f32[128,512]{1,0:T(8,128)S(1)} %carry.3.refs_1_), channel_id=1, source_target_pairs={{0,1},{1,2},{2,3},{3,0},{4,5},{5,6},{6,7},{7,4},{8,9},{9,10},{10,1... | collective-permute-start | bytes 786440 | tf_op jit(solution)/shard_map/ppermute | solution.py:489
  80.9 2.3 %collective-permute-start.9 = (f32[128,512]{1,0:T(8,128)S(1)}, f32[128,512]{1,0:T(8,128)S(1)}, u32[]{:S(2)}, u32[]{:S(2)}) collective-permute-start(f32[128,512]{1,0:T(8,128)S(1)} %carry.3.refs_1_), channel_id=1, source_target_pairs={{0,3},{1,0},{2,1},{3,2},{4,7},{5,4},{6,5},{7,6},{8,11},{9,8},{10,9... | collective-permute-start | bytes 786440 | tf_op jit(solution)/shard_map/ppermute | solution.py:489
  83.2 3.6 %product.10 = f32[8,320,128]{2,1,0:T(8,128)} custom-call(s32[1]{0:T(128)} %bitcast.2.ids_ref.refs_0_, bf16[4,4,1024,256]{3,2,1,0:T(8,128)(2,1)} %get-tuple-element.34.refs_0_.refs_1_, f32[176,512]{1,0:T(8,128)S(1)} %collective-permute-done.8.refs_2_.refs_6_, f32[128,1024]{1,0:T(8,128)} %get-tuple-element.48.refs_3_, f32[176,512]{1,0:T(8,128)S(1)} %carry.2.refs_1_.refs_4_, ...), custom_call_target="tpu_custom_call" | custom-call | flops 1024 | bytes 1024 | tf_op jit(solution)/shard_map/product/pallas_call | solution.py:392
  86.8 3.9 %all-to-all-start.2 = ((f32[8,320,128]{2,1,0:T(8,128)}), f32[8,320,128]{2,1,0:T(8,128)S(1)}, u32[]{:S(2)}, u32[]{:S(2)}) async-start(f32[8,320,128]{2,1,0:T(8,128)} %product.10), calls=%async_computation.2 | async-start | bytes 2621440 | tf_op jit(solution)/shard_map/all_to_all | solution.py:493
  90.7 0.0 collective-permute-done.10.refs_3_
  90.7 2.4 %collective-permute-done.9.refs_2_ = f32[128,512]{1,0:T(8,128)S(1)} collective-permute-done((f32[128,512]{1,0:T(8,128)S(1)}, f32[128,512]{1,0:T(8,128)S(1)}, u32[]{:S(2)}, u32[]{:S(2)}) %collective-permute-start.9) | collective-permute-done | bytes 262176 | tf_op jit(solution)/shard_map/ppermute | solution.py:489
  93.1 0.1 select_select_fusion.1
  93.1 1.7 %collective-permute-start.11 = (f32[128,512]{1,0:T(8,128)S(1)}, f32[128,512]{1,0:T(8,128)S(1)}, u32[]{:S(2)}, u32[]{:S(2)}) collective-permute-start(f32[128,512]{1,0:T(8,128)S(1)} %select_select_fusion.1), channel_id=1, source_target_pairs={{1,0},{2,3},{3,1},{0,2},{5,4},{6,7},{7,5},{4,6},{9,8},{10,11},{11,... | collective-permute-start | bytes 786440 | tf_op jit(solution)/shard_map/ppermute | solution.py:503
  94.9 5.5 %product.12.refs_3_ = f32[128,1024]{1,0:T(8,128)} custom-call(bf16[4,4,1024,256]{3,2,1,0:T(8,128)(2,1)} %get-tuple-element.34.refs_0_.refs_1_, f32[128,512]{1,0:T(8,128)S(1)} %carry.3.refs_1_, f32[128,512]{1,0:T(8,128)S(1)} %collective-permute-done.9.refs_2_, f32[128,512]{1,0:T(8,128)S(1)} %collective-permute-done.10.refs_3_), custom_call_target="tpu_custom_call" | custom-call | flops 17179869184 | bytes 67108864 | tf_op jit(solution)/shard_map/product/pallas_call | solution.py:392
  100.3 0.0 collective-permute-done.11.refs_2_
  100.4 2.9 %product.13 = (f32[128,128]{1,0:T(8,128)S(1)}, f32[128,128]{1,0:T(8,128)S(1)}, f32[128,128]{1,0:T(8,128)S(1)}, f32[128,128]{1,0:T(8,128)S(1)}, f32[128,128]{1,0:...) custom-call(s32[1]{0:T(128)} %bitcast.refs_0_.row_ref, ...), custom_call_target="tpu_custom_call" | custom-call | flops 1024 | bytes 1024 | tf_op jit(solution)/shard_map/product/pallas_call | solution.py:392
  103.3 0.1 collective-permute-start.12
  103.3 2.4 %collective-permute-start.13 = (f32[128,128]{1,0:T(8,128)S(1)}, f32[128,128]{1,0:T(8,128)S(1)}, u32[]{:S(2)}, u32[]{:S(2)}) collective-permute-start(f32[128,128]{1,0:T(8,128)S(1)} %get-tuple-element.56), channel_id=1, source_target_pairs={{0,8},{4,12},{8,0},{12,4},{16,24},{20,28},{24,16},{28,20},{1,9},{5... | collective-permute-start | bytes 196616 | tf_op jit(solution)/shard_map/ppermute | solution.py:591
  105.7 0.1 collective-permute-start.14
  105.8 1.6 %collective-permute-start.15 = (f32[128,128]{1,0:T(8,128)S(1)}, f32[128,128]{1,0:T(8,128)S(1)}, u32[]{:S(2)}, u32[]{:S(2)}) collective-permute-start(f32[128,128]{1,0:T(8,128)S(1)} %get-tuple-element.58), channel_id=1, source_target_pairs={{0,16},{4,20},{8,24},{12,28},{16,0},{20,4},{24,8},{28,12},{1,17},{... | collective-permute-start | bytes 196616 | tf_op jit(solution)/shard_map/ppermute | solution.py:591
  107.4 0.0 collective-permute-start.16
  107.4 0.0 collective-permute-done.12.refs_1_
  107.4 2.2 %collective-permute-start.17 = (f32[128,128]{1,0:T(8,128)S(1)}, f32[128,128]{1,0:T(8,128)S(1)}, u32[]{:S(2)}, u32[]{:S(2)}) collective-permute-start(f32[128,128]{1,0:T(8,128)S(1)} %get-tuple-element.60), channel_id=1, source_target_pairs={{0,24},{4,28},{8,16},{12,20},{16,8},{20,12},{24,0},{28,4},{1,25},{... | collective-permute-start | bytes 196616 | tf_op jit(solution)/shard_map/ppermute | solution.py:591
  109.6 0.3 collective-permute-done.13.refs_2_
  109.9 0.5 collective-permute-start.18
  110.3 0.0 all-to-all-done.2.came_ref.left_ref
  110.3 1.1 assemble.1
  111.5 0.0 collective-permute-done.14.refs_3_
  111.5 0.0 collective-permute-done.15.refs_4_
  111.5 0.1 collective-permute-done.16.refs_5_
  111.6 1.6 %collective-permute-done.17.refs_6_ = f32[128,128]{1,0:T(8,128)S(1)} collective-permute-done((f32[128,128]{1,0:T(8,128)S(1)}, f32[128,128]{1,0:T(8,128)S(1)}, u32[]{:S(2)}, u32[]{:S(2)}) %collective-permute-start.17) | collective-permute-done | bytes 65568 | tf_op jit(solution)/shard_map/ppermute | solution.py:591
  113.2 1.9 %collective-permute-done.18.refs_7_ = f32[128,128]{1,0:T(8,128)S(1)} collective-permute-done((f32[128,128]{1,0:T(8,128)S(1)}, f32[128,128]{1,0:T(8,128)S(1)}, u32[]{:S(2)}, u32[]{:S(2)}) %collective-permute-start.18) | collective-permute-done | bytes 65568 | tf_op jit(solution)/shard_map/ppermute | solution.py:591
  115.1 1.8 %finish.1 = f32[512,256]{1,0:T(8,128)} custom-call(s32[1]{0:T(128)} %bitcast.refs_0_.row_ref, s32[8]{0:T(128)S(1)} %bitcast.5, f32[256,512]{1,0:T(8,128)S(1)} %get-tuple-element.49.base_ref, f32[8,320,128]{2,1,0:T(8,128)S(1)} %all-to-all-done.2.came_ref.left_ref, f32[128,128]{1,0:T(8,128)S(1)} %get-tuple-element.54.refs_0_, ...), custom_call_target="tpu_custom_call" | custom-call | flops 1024 | bytes 1024 | tf_op jit(solution)/shard_map/finish/pallas_call | solution.py:452
  (2 shorter events, 0.0 us)
Async XLA Ops:
  2.4 14.4 %collective-permute-start.1 = (f32[128,512]{1,0:T(8,128)S(1)}, f32[128,512]{1,0:T(8,128)S(1)}, u32[]{:S(2)}, u32[]{:S(2)}) collective-permute-start(f32[128,512]{1,0:T(8,128)S(1)} %get-tuple-element.32.first_ref.refs_0_), channel_id=1, source_target_pairs={{0,3},{1,0},{2,1},{3,2},{4,7},{5,4},{6,5},{7,6},{8,11},{9,8},{10,9... | collective-permute-start | bytes 786440 | tf_op jit(solution)/shard_map/ppermute | solution.py:489
  7.5 12.1 %collective-permute-start = (f32[128,512]{1,0:T(8,128)S(1)}, f32[128,512]{1,0:T(8,128)S(1)}, u32[]{:S(2)}, u32[]{:S(2)}) collective-permute-start(f32[128,512]{1,0:T(8,128)S(1)} %get-tuple-element.32.first_ref.refs_0_), channel_id=1, source_target_pairs={{0,1},{1,2},{2,3},{3,0},{4,5},{5,6},{6,7},{7,4},{8,9},{9,10},{10,1... | collective-permute-start | bytes 786440 | tf_op jit(solution)/shard_map/ppermute | solution.py:489
  12.4 19.2 %all-to-all-start = ((f32[8,192,128]{2,1,0:T(8,128)}), f32[8,192,128]{2,1,0:T(8,128)S(1)}, u32[]{:S(2)}, u32[]{:S(2)}) async-start(f32[8,192,128]{2,1,0:T(8,128)} %get-tuple-element.44), calls=%async_computation | async-start | bytes 1572864 | tf_op jit(solution)/shard_map/all_to_all | solution.py:493
  19.6 8.1 %collective-permute-start.2 = (f32[128,512]{1,0:T(8,128)S(1)}, f32[128,512]{1,0:T(8,128)S(1)}, u32[]{:S(2)}, u32[]{:S(2)}) collective-permute-start(f32[128,512]{1,0:T(8,128)S(1)} %select_select_fusion.3), channel_id=1, source_target_pairs={{1,0},{2,3},{3,1},{0,2},{5,4},{6,7},{7,5},{4,6},{9,8},{10,11},{11,... | collective-permute-start | bytes 786440 | tf_op jit(solution)/shard_map/ppermute | solution.py:503
  27.7 11.1 %collective-permute-start.4 = (f32[128,512]{1,0:T(8,128)S(1)}, f32[128,512]{1,0:T(8,128)S(1)}, u32[]{:S(2)}, u32[]{:S(2)}) collective-permute-start(f32[128,512]{1,0:T(8,128)S(1)} %get-tuple-element.38.refs_1_), channel_id=1, source_target_pairs={{0,1},{1,2},{2,3},{3,0},{4,5},{5,6},{6,7},{7,4},{8,9},{9,10},{10,1... | collective-permute-start | bytes 786440 | tf_op jit(solution)/shard_map/ppermute | solution.py:489
  29.4 11.9 %collective-permute-start.3 = (f32[128,512]{1,0:T(8,128)S(1)}, f32[128,512]{1,0:T(8,128)S(1)}, u32[]{:S(2)}, u32[]{:S(2)}) collective-permute-start(f32[128,512]{1,0:T(8,128)S(1)} %get-tuple-element.38.refs_1_), channel_id=1, source_target_pairs={{0,3},{1,0},{2,1},{3,2},{4,7},{5,4},{6,5},{7,6},{8,11},{9,8},{10,9... | collective-permute-start | bytes 786440 | tf_op jit(solution)/shard_map/ppermute | solution.py:489
  34.8 14.1 %all-to-all-start.1 = ((f32[8,128,128]{2,1,0:T(8,128)}), f32[8,128,128]{2,1,0:T(8,128)S(1)}, u32[]{:S(2)}, u32[]{:S(2)}) async-start(f32[8,128,128]{2,1,0:T(8,128)} %product.8), calls=%async_computation.1 | async-start | bytes 1048576 | tf_op jit(solution)/shard_map/all_to_all | solution.py:493
  41.3 7.6 %collective-permute-start.5 = (f32[128,512]{1,0:T(8,128)S(1)}, f32[128,512]{1,0:T(8,128)S(1)}, u32[]{:S(2)}, u32[]{:S(2)}) collective-permute-start(f32[128,512]{1,0:T(8,128)S(1)} %select_select_fusion.2), channel_id=1, source_target_pairs={{1,0},{2,3},{3,1},{0,2},{5,4},{6,7},{7,5},{4,6},{9,8},{10,11},{11,... | collective-permute-start | bytes 786440 | tf_op jit(solution)/shard_map/ppermute | solution.py:503
  42.8 6.2 %copy-start = (s32[1,8,1]{1,2,0:T(1,128)S(1)}, s32[1,8,1]{1,2,0:T(1,128)}, u32[]{:S(2)}) copy-start(s32[1,8,1]{1,2,0:T(1,128)} %param.20) | copy-start | bytes 100
  49.7 13.2 %collective-permute-start.7 = (f32[176,512]{1,0:T(8,128)S(1)}, f32[176,512]{1,0:T(8,128)S(1)}, u32[]{:S(2)}, u32[]{:S(2)}) collective-permute-start(f32[176,512]{1,0:T(8,128)S(1)} %carry.2.refs_1_.refs_4_), channel_id=1, source_target_pairs={{0,1},{1,2},{2,3},{3,0},{4,5},{5,6},{6,7},{7,4},{8,9},{9,10},{10,1... | collective-permute-start | bytes 1081352 | tf_op jit(solution)/shard_map/ppermute | solution.py:489
  52.4 15.7 %collective-permute-start.6 = (f32[176,512]{1,0:T(8,128)S(1)}, f32[176,512]{1,0:T(8,128)S(1)}, u32[]{:S(2)}, u32[]{:S(2)}) collective-permute-start(f32[176,512]{1,0:T(8,128)S(1)} %carry.2.refs_1_.refs_4_), channel_id=1, source_target_pairs={{0,3},{1,0},{2,1},{3,2},{4,7},{5,4},{6,5},{7,6},{8,11},{9,8},{10,9... | collective-permute-start | bytes 1081352 | tf_op jit(solution)/shard_map/ppermute | solution.py:489
  57.1 21.6 %all-to-all-start.3 = ((f32[8,128,128]{2,1,0:T(8,128)}), f32[8,128,128]{2,1,0:T(8,128)S(1)}, u32[]{:S(2)}, u32[]{:S(2)}) async-start(f32[8,128,128]{2,1,0:T(8,128)} %product.11), calls=%async_computation.3 | async-start | bytes 1048576 | tf_op jit(solution)/shard_map/all_to_all | solution.py:493
  68.1 10.5 %collective-permute-start.8 = (f32[176,512]{1,0:T(8,128)S(1)}, f32[176,512]{1,0:T(8,128)S(1)}, u32[]{:S(2)}, u32[]{:S(2)}) collective-permute-start(f32[176,512]{1,0:T(8,128)S(1)} %select_select_fusion), channel_id=1, source_target_pairs={{1,0},{2,3},{3,1},{0,2},{5,4},{6,7},{7,5},{4,6},{9,8},{10,11},{11,... | collective-permute-start | bytes 1081352 | tf_op jit(solution)/shard_map/ppermute | solution.py:503
  79.3 11.4 %collective-permute-start.10 = (f32[128,512]{1,0:T(8,128)S(1)}, f32[128,512]{1,0:T(8,128)S(1)}, u32[]{:S(2)}, u32[]{:S(2)}) collective-permute-start(f32[128,512]{1,0:T(8,128)S(1)} %carry.3.refs_1_), channel_id=1, source_target_pairs={{0,1},{1,2},{2,3},{3,0},{4,5},{5,6},{6,7},{7,4},{8,9},{9,10},{10,1... | collective-permute-start | bytes 786440 | tf_op jit(solution)/shard_map/ppermute | solution.py:489
  80.9 12.2 %collective-permute-start.9 = (f32[128,512]{1,0:T(8,128)S(1)}, f32[128,512]{1,0:T(8,128)S(1)}, u32[]{:S(2)}, u32[]{:S(2)}) collective-permute-start(f32[128,512]{1,0:T(8,128)S(1)} %carry.3.refs_1_), channel_id=1, source_target_pairs={{0,3},{1,0},{2,1},{3,2},{4,7},{5,4},{6,5},{7,6},{8,11},{9,8},{10,9... | collective-permute-start | bytes 786440 | tf_op jit(solution)/shard_map/ppermute | solution.py:489
  86.8 23.5 %all-to-all-start.2 = ((f32[8,320,128]{2,1,0:T(8,128)}), f32[8,320,128]{2,1,0:T(8,128)S(1)}, u32[]{:S(2)}, u32[]{:S(2)}) async-start(f32[8,320,128]{2,1,0:T(8,128)} %product.10), calls=%async_computation.2 | async-start | bytes 2621440 | tf_op jit(solution)/shard_map/all_to_all | solution.py:493
  93.1 7.2 %collective-permute-start.11 = (f32[128,512]{1,0:T(8,128)S(1)}, f32[128,512]{1,0:T(8,128)S(1)}, u32[]{:S(2)}, u32[]{:S(2)}) collective-permute-start(f32[128,512]{1,0:T(8,128)S(1)} %select_select_fusion.1), channel_id=1, source_target_pairs={{1,0},{2,3},{3,1},{0,2},{5,4},{6,7},{7,5},{4,6},{9,8},{10,11},{11,... | collective-permute-start | bytes 786440 | tf_op jit(solution)/shard_map/ppermute | solution.py:503
  103.3 4.2 %collective-permute-start.12 = (f32[128,128]{1,0:T(8,128)S(1)}, f32[128,128]{1,0:T(8,128)S(1)}, u32[]{:S(2)}, u32[]{:S(2)}) collective-permute-start(f32[128,128]{1,0:T(8,128)S(1)} %get-tuple-element.55), channel_id=1, source_target_pairs={{0,4},{4,0},{8,12},{12,8},{16,20},{20,16},{24,28},{28,24},{1,5},{5... | collective-permute-start | bytes 196616 | tf_op jit(solution)/shard_map/ppermute | solution.py:591
  103.3 6.5 %collective-permute-start.13 = (f32[128,128]{1,0:T(8,128)S(1)}, f32[128,128]{1,0:T(8,128)S(1)}, u32[]{:S(2)}, u32[]{:S(2)}) collective-permute-start(f32[128,128]{1,0:T(8,128)S(1)} %get-tuple-element.56), channel_id=1, source_target_pairs={{0,8},{4,12},{8,0},{12,4},{16,24},{20,28},{24,16},{28,20},{1,9},{5... | collective-permute-start | bytes 196616 | tf_op jit(solution)/shard_map/ppermute | solution.py:591
  105.7 5.7 %collective-permute-start.14 = (f32[128,128]{1,0:T(8,128)S(1)}, f32[128,128]{1,0:T(8,128)S(1)}, u32[]{:S(2)}, u32[]{:S(2)}) collective-permute-start(f32[128,128]{1,0:T(8,128)S(1)} %get-tuple-element.57), channel_id=1, source_target_pairs={{0,12},{4,8},{8,4},{12,0},{16,28},{20,24},{24,20},{28,16},{1,13},{... | collective-permute-start | bytes 196616 | tf_op jit(solution)/shard_map/ppermute | solution.py:591
  105.8 5.7 %collective-permute-start.15 = (f32[128,128]{1,0:T(8,128)S(1)}, f32[128,128]{1,0:T(8,128)S(1)}, u32[]{:S(2)}, u32[]{:S(2)}) collective-permute-start(f32[128,128]{1,0:T(8,128)S(1)} %get-tuple-element.58), channel_id=1, source_target_pairs={{0,16},{4,20},{8,24},{12,28},{16,0},{20,4},{24,8},{28,12},{1,17},{... | collective-permute-start | bytes 196616 | tf_op jit(solution)/shard_map/ppermute | solution.py:591
  107.4 4.2 %collective-permute-start.16 = (f32[128,128]{1,0:T(8,128)S(1)}, f32[128,128]{1,0:T(8,128)S(1)}, u32[]{:S(2)}, u32[]{:S(2)}) collective-permute-start(f32[128,128]{1,0:T(8,128)S(1)} %get-tuple-element.59), channel_id=1, source_target_pairs={{0,20},{4,16},{8,28},{12,24},{16,4},{20,0},{24,12},{28,8},{1,21},{... | collective-permute-start | bytes 196616 | tf_op jit(solution)/shard_map/ppermute | solution.py:591
  107.4 5.8 %collective-permute-start.17 = (f32[128,128]{1,0:T(8,128)S(1)}, f32[128,128]{1,0:T(8,128)S(1)}, u32[]{:S(2)}, u32[]{:S(2)}) collective-permute-start(f32[128,128]{1,0:T(8,128)S(1)} %get-tuple-element.60), channel_id=1, source_target_pairs={{0,24},{4,28},{8,16},{12,20},{16,8},{20,12},{24,0},{28,4},{1,25},{... | collective-permute-start | bytes 196616 | tf_op jit(solution)/shard_map/ppermute | solution.py:591
  109.9 5.2 %collective-permute-start.18 = (f32[128,128]{1,0:T(8,128)S(1)}, f32[128,128]{1,0:T(8,128)S(1)}, u32[]{:S(2)}, u32[]{:S(2)}) collective-permute-start(f32[128,128]{1,0:T(8,128)S(1)} %get-tuple-element.61), channel_id=1, source_target_pairs={{0,28},{4,24},{8,20},{12,16},{16,12},{20,8},{24,4},{28,0},{1,29},{... | collective-permute-start | bytes 196616 | tf_op jit(solution)/shard_map/ppermute | solution.py:591

commit v22 on v21

--- a/solution.py
+++ b/solution.py
@@ -588,7 +588,8 @@
     right_last = final(*common, right_steps, right_early, apart=True)
     right_came = [right_last[0]] * n_row
     for j in range(n_row - 1, 0, -1):
-        right_came[j] = lax.ppermute(right_last[j], "row", [(r, r ^ j) for r in range(n_row)])
+        sent = right_last[j] if j > 1 else after(right_last[j], right_came[-1])
+        right_came[j] = lax.ppermute(sent, "row", [(r, r ^ j) for r in range(n_row)])
     weight_grad = assemble(n_row, left_came)
     return finish(n_row, row, owners, after(diff, weight_grad), left_came, right_came), weight_grad
 

time: 118 us -> 118 us (level)
  transfers between devices with their start and end apart: 23 -> 23, of which waited for: 12 -> 11; matrix products, arithmetic and copies ran while one was open for 0% -> 0% of each run, Pallas kernels for 37% -> 37%
where the time goes in v22:
time: 118 us; the launch traced here: 117 us
  Pallas kernels  47.9 us (41%)
  starting transfers between devices  43.4 us (37%)
  waiting for transfers between devices  24.3 us (21%)
  between operations  1.44 us (1%)
    pallas_call x7, Pallas kernels, product(): pl.pallas_call(functools.partial(product_kernel, n_row, n_col, origins, h...  29.7 us
    ppermute x8, starting transfers between devices, shift(): lax.ppermute(x, 'col', [(c, (c + step) % n_col) for c in range(n_col)])  16.7 us
    all_to_all x4, starting transfers between devices, exchange(): lax.all_to_all(pieces, 'row', split_axis=0, concat_axis=0, tiled=True)  15.2 us
    ppermute x8, waiting for transfers between devices, shift(): lax.ppermute(x, 'col', [(c, (c + step) % n_col) for c in range(n_col)])  15 us
    pallas_call x1, Pallas kernels, build_operator(): pl.pallas_call(functools.partial(operator_kernel, n_row, n_col, origins),...  7.29 us
    ppermute x7, starting transfers between devices, per_device(): lax.ppermute(sent, 'row', [(r, r ^ j) for r in range(n_row)])  6.68 us
    pallas_call x1, Pallas kernels, local_terms(): pl.pallas_call(functools.partial(local_kernel, n_row), in_specs=[ANY] + [...  4.88 us
    ppermute x4, waiting for transfers between devices, opposite(): return lax.ppermute(sent, 'col', [(1, 0), (2, 3), (3, 1), (0, 2)])  4.88 us
  transfers between devices with their start and end apart: 23, of which 11 were waited for; matrix products, arithmetic and copies ran while one was open for 0% of the time, Pallas kernels for 37%

profile of v22, /device:TPU:0, one launch (start us, length us, event | category | flops | bytes accessed | tf_op | source)
XLA Modules:
  0.0 117.3 jit_solution(3453197631729758193)
XLA Ops:
  0.6 1.7 %term_two.1 = (f32[128,512]{1,0:T(8,128)S(1)}, f32[128,512]{1,0:T(8,128)S(1)}) custom-call(f32[512,256]{1,0:T(8,128)} %grad_hbm.3, s32[512,256]{1,0:T(8,128)} %mask_hbm.3, f32[3,256,256]{2,1,0:T(8,128)} %weight_hbm.3), custom_call_target="tpu_custom_call" | custom-call | flops 1024 | bytes 1024 | tf_op jit(solution)/shard_map/term_two/pallas_call | solution.py:78
  2.4 5.1 %collective-permute-start.1 = (f32[128,512]{1,0:T(8,128)S(1)}, f32[128,512]{1,0:T(8,128)S(1)}, u32[]{:S(2)}, u32[]{:S(2)}) collective-permute-start(f32[128,512]{1,0:T(8,128)S(1)} %get-tuple-element.33.first_ref.refs_0_), channel_id=1, source_target_pairs={{0,3},{1,0},{2,1},{3,2},{4,7},{5,4},{6,5},{7,6},{8,11},{9,8},{10,9... | collective-permute-start | bytes 786440 | tf_op jit(solution)/shard_map/ppermute | solution.py:489
  7.5 0.0 collective-permute-start
  7.5 4.9 %local_terms.1 = (f32[128,512]{1,0:T(8,128)}, f32[128,512]{1,0:T(8,128)}, f32[256,512]{1,0:T(8,128)S(1)}, f32[8,192,128]{2,1,0:T(8,128)}) custom-call(f32[128,512]{1,0:T(8,128)S(1)} %get-tuple-element.33.first_ref.refs_0_, f32[512,256]{1,0:T(8,128)} %grad_hbm.3, s32[512,256]{1,0:T(8,128)} %mask_hbm.3, f32[3,256,256]{2,1,0:T(8,128)} %weight_hbm.3, ...), custom_call_target="tpu_custom_call" | custom-call | flops 1024 | bytes 1024 | tf_op jit(solution)/shard_map/local_terms/pallas_call | solution.py:125
  12.4 3.7 %all-to-all-start = ((f32[8,192,128]{2,1,0:T(8,128)}), f32[8,192,128]{2,1,0:T(8,128)S(1)}, u32[]{:S(2)}, u32[]{:S(2)}) async-start(f32[8,192,128]{2,1,0:T(8,128)} %get-tuple-element.45), calls=%async_computation | async-start | bytes 1572864 | tf_op jit(solution)/shard_map/all_to_all | solution.py:493
  16.8 0.0 collective-permute-done.1.refs_2_
  16.8 2.8 %collective-permute-done.refs_1_ = f32[128,512]{1,0:T(8,128)S(1)} collective-permute-done((f32[128,512]{1,0:T(8,128)S(1)}, f32[128,512]{1,0:T(8,128)S(1)}, u32[]{:S(2)}, u32[]{:S(2)}) %collective-permute-start) | collective-permute-done | bytes 262176 | tf_op jit(solution)/shard_map/ppermute | solution.py:489
  19.6 0.1 select_select_fusion.3
  19.6 0.8 collective-permute-start.2
  20.4 7.3 %operator.1 = (bf16[4,4,1024,256]{3,2,1,0:T(8,128)(2,1)}, f32[128,1024]{1,0:T(8,128)S(1)}) custom-call(s32[1]{0:T(128)} %bitcast.2.ids_ref.refs_0_, s32[1]{0:T(128)S(6)} %copy.13.live_ref, s32[1,128]{1,0:T(1,128)} %rows_hbm.1, s32[1,128]{1,0:T(1,128)} %slots_hbm.1, f32[1,128,128,128]{3,2,1,0:T(8,128)} %values_ref.1, ...), custom_call_target="tpu_custom_call" | custom-call | flops 17179869184 | bytes 67108864 | tf_op jit(solution)/shard_map/operator/pallas_call | solution.py:262
  27.7 0.0 collective-permute-done.2.refs_1_
  27.7 1.7 %collective-permute-start.4 = (f32[128,512]{1,0:T(8,128)S(1)}, f32[128,512]{1,0:T(8,128)S(1)}, u32[]{:S(2)}, u32[]{:S(2)}) collective-permute-start(f32[128,512]{1,0:T(8,128)S(1)} %get-tuple-element.39.refs_1_), channel_id=1, source_target_pairs={{0,1},{1,2},{2,3},{3,0},{4,5},{5,6},{6,7},{7,4},{8,9},{9,10},{10,1... | collective-permute-start | bytes 786440 | tf_op jit(solution)/shard_map/ppermute | solution.py:489
  29.4 2.2 %collective-permute-start.3 = (f32[128,512]{1,0:T(8,128)S(1)}, f32[128,512]{1,0:T(8,128)S(1)}, u32[]{:S(2)}, u32[]{:S(2)}) collective-permute-start(f32[128,512]{1,0:T(8,128)S(1)} %get-tuple-element.39.refs_1_), channel_id=1, source_target_pairs={{0,3},{1,0},{2,1},{3,2},{4,7},{5,4},{6,5},{7,6},{8,11},{9,8},{10,9... | collective-permute-start | bytes 786440 | tf_op jit(solution)/shard_map/ppermute | solution.py:489
  31.6 0.0 all-to-all-done.refs_0_
  31.6 3.2 %product.8 = f32[8,128,128]{2,1,0:T(8,128)} custom-call(bf16[4,4,1024,256]{3,2,1,0:T(8,128)(2,1)} %get-tuple-element.35.refs_0_.refs_1_, f32[128,512]{1,0:T(8,128)S(1)} %collective-permute-done.2.refs_1_, f32[128,1024]{1,0:T(8,128)S(1)} %get-tuple-element.46.refs_2_), custom_call_target="tpu_custom_call" | custom-call | flops 1024 | bytes 1024 | tf_op jit(solution)/shard_map/product/pallas_call | solution.py:392
  34.8 3.7 %all-to-all-start.1 = ((f32[8,128,128]{2,1,0:T(8,128)}), f32[8,128,128]{2,1,0:T(8,128)S(1)}, u32[]{:S(2)}, u32[]{:S(2)}) async-start(f32[8,128,128]{2,1,0:T(8,128)} %product.8), calls=%async_computation.1 | async-start | bytes 1048576 | tf_op jit(solution)/shard_map/all_to_all | solution.py:493
  38.6 0.2 collective-permute-done.4.refs_3_
  38.8 2.5 %collective-permute-done.3.refs_2_ = f32[128,512]{1,0:T(8,128)S(1)} collective-permute-done((f32[128,512]{1,0:T(8,128)S(1)}, f32[128,512]{1,0:T(8,128)S(1)}, u32[]{:S(2)}, u32[]{:S(2)}) %collective-permute-start.3) | collective-permute-done | bytes 262176 | tf_op jit(solution)/shard_map/ppermute | solution.py:489
  41.3 0.1 select_select_fusion.2
  41.3 1.5 %collective-permute-start.5 = (f32[128,512]{1,0:T(8,128)S(1)}, f32[128,512]{1,0:T(8,128)S(1)}, u32[]{:S(2)}, u32[]{:S(2)}) collective-permute-start(f32[128,512]{1,0:T(8,128)S(1)} %select_select_fusion.2), channel_id=1, source_target_pairs={{1,0},{2,3},{3,1},{0,2},{5,4},{6,7},{7,5},{4,6},{9,8},{10,11},{11,... | collective-permute-start | bytes 786440 | tf_op jit(solution)/shard_map/ppermute | solution.py:503
  42.8 5.5 %product.7 = (f32[128,1024]{1,0:T(8,128)}, f32[128,512]{1,0:T(8,128)S(1)}) custom-call(bf16[4,4,1024,256]{3,2,1,0:T(8,128)(2,1)} %get-tuple-element.35.refs_0_.refs_1_, f32[128,512]{1,0:T(8,128)S(1)} %get-tuple-element.39.refs_1_, f32[128,512]{1,0:T(8,128)S(1)} %collective-permute-done.3.refs_2_, f32[128,512]{1,0:T(8,128)S(1)} %collective-permute-done.4.refs_3_, ...), custom_call_target="tpu_custom_call" | custom-call | flops 17179869184 | bytes 67108864 | tf_op jit(solution)/shard_map/product/pallas_call | solution.py:392
  48.3 0.7 collective-permute-done.5.refs_1_
  49.0 0.0 all-to-all-done.1.came_ref
  49.0 0.7 carry.2.refs_1_.refs_4_
  49.7 2.7 %collective-permute-start.7 = (f32[176,512]{1,0:T(8,128)S(1)}, f32[176,512]{1,0:T(8,128)S(1)}, u32[]{:S(2)}, u32[]{:S(2)}) collective-permute-start(f32[176,512]{1,0:T(8,128)S(1)} %carry.2.refs_1_.refs_4_), channel_id=1, source_target_pairs={{0,1},{1,2},{2,3},{3,0},{4,5},{5,6},{6,7},{7,4},{8,9},{9,10},{10,1... | collective-permute-start | bytes 1081352 | tf_op jit(solution)/shard_map/ppermute | solution.py:489
  52.4 1.2 %collective-permute-start.6 = (f32[176,512]{1,0:T(8,128)S(1)}, f32[176,512]{1,0:T(8,128)S(1)}, u32[]{:S(2)}, u32[]{:S(2)}) collective-permute-start(f32[176,512]{1,0:T(8,128)S(1)} %carry.2.refs_1_.refs_4_), channel_id=1, source_target_pairs={{0,3},{1,0},{2,1},{3,2},{4,7},{5,4},{6,5},{7,6},{8,11},{9,8},{10,9... | collective-permute-start | bytes 1081352 | tf_op jit(solution)/shard_map/ppermute | solution.py:489
  53.6 3.5 %product.11 = f32[8,128,128]{2,1,0:T(8,128)} custom-call(bf16[4,4,1024,256]{3,2,1,0:T(8,128)(2,1)} %get-tuple-element.35.refs_0_.refs_1_, f32[128,512]{1,0:T(8,128)S(1)} %collective-permute-done.5.refs_1_, f32[128,1024]{1,0:T(8,128)} %get-tuple-element.42.refs_2_), custom_call_target="tpu_custom_call" | custom-call | flops 1024 | bytes 1024 | tf_op jit(solution)/shard_map/product/pallas_call | solution.py:392
  57.1 3.8 %all-to-all-start.3 = ((f32[8,128,128]{2,1,0:T(8,128)}), f32[8,128,128]{2,1,0:T(8,128)S(1)}, u32[]{:S(2)}, u32[]{:S(2)}) async-start(f32[8,128,128]{2,1,0:T(8,128)} %product.11), calls=%async_computation.3 | async-start | bytes 1048576 | tf_op jit(solution)/shard_map/all_to_all | solution.py:493
  60.9 2.0 %collective-permute-done.7.refs_2_.refs_7_ = f32[176,512]{1,0:T(8,128)S(1)} collective-permute-done((f32[176,512]{1,0:T(8,128)S(1)}, f32[176,512]{1,0:T(8,128)S(1)}, u32[]{:S(2)}, u32[]{:S(2)}) %collective-permute-start.7) | collective-permute-done | bytes 360480 | tf_op jit(solution)/shard_map/ppermute | solution.py:489
  62.9 5.1 %collective-permute-done.6.refs_3_.refs_5_ = f32[176,512]{1,0:T(8,128)S(1)} collective-permute-done((f32[176,512]{1,0:T(8,128)S(1)}, f32[176,512]{1,0:T(8,128)S(1)}, u32[]{:S(2)}, u32[]{:S(2)}) %collective-permute-start.6) | collective-permute-done | bytes 360480 | tf_op jit(solution)/shard_map/ppermute | solution.py:489
  68.0 0.1 select_select_fusion
  68.1 0.8 collective-permute-start.8
  69.0 5.5 %product.9 = (f32[128,1024]{1,0:T(8,128)}, f32[128,512]{1,0:T(8,128)S(1)}) custom-call(bf16[4,4,1024,256]{3,2,1,0:T(8,128)(2,1)} %get-tuple-element.35.refs_0_.refs_1_, f32[176,512]{1,0:T(8,128)S(1)} %carry.2.refs_1_.refs_4_, f32[176,512]{1,0:T(8,128)S(1)} %collective-permute-done.7.refs_2_.refs_7_, f32[176,512]{1,0:T(8,128)S(1)} %collective-permute-done.6.refs_3_.refs_5_, ...), custom_call_target="tpu_custom_call" | custom-call | flops 17179869184 | bytes 67108864 | tf_op jit(solution)/shard_map/product/pallas_call | solution.py:392
  74.5 4.2 %collective-permute-done.8.refs_2_.refs_6_ = f32[176,512]{1,0:T(8,128)S(1)} collective-permute-done((f32[176,512]{1,0:T(8,128)S(1)}, f32[176,512]{1,0:T(8,128)S(1)}, u32[]{:S(2)}, u32[]{:S(2)}) %collective-permute-start.8) | collective-permute-done | bytes 360480 | tf_op jit(solution)/shard_map/ppermute | solution.py:503
  78.7 0.0 all-to-all-done.3.came_ref
  78.7 0.7 carry.3.refs_1_
  79.3 1.5 %collective-permute-start.10 = (f32[128,512]{1,0:T(8,128)S(1)}, f32[128,512]{1,0:T(8,128)S(1)}, u32[]{:S(2)}, u32[]{:S(2)}) collective-permute-start(f32[128,512]{1,0:T(8,128)S(1)} %carry.3.refs_1_), channel_id=1, source_target_pairs={{0,1},{1,2},{2,3},{3,0},{4,5},{5,6},{6,7},{7,4},{8,9},{9,10},{10,1... | collective-permute-start | bytes 786440 | tf_op jit(solution)/shard_map/ppermute | solution.py:489
  80.9 2.3 %collective-permute-start.9 = (f32[128,512]{1,0:T(8,128)S(1)}, f32[128,512]{1,0:T(8,128)S(1)}, u32[]{:S(2)}, u32[]{:S(2)}) collective-permute-start(f32[128,512]{1,0:T(8,128)S(1)} %carry.3.refs_1_), channel_id=1, source_target_pairs={{0,3},{1,0},{2,1},{3,2},{4,7},{5,4},{6,5},{7,6},{8,11},{9,8},{10,9... | collective-permute-start | bytes 786440 | tf_op jit(solution)/shard_map/ppermute | solution.py:489
  83.2 3.6 %product.10 = f32[8,320,128]{2,1,0:T(8,128)} custom-call(s32[1]{0:T(128)} %bitcast.2.ids_ref.refs_0_, bf16[4,4,1024,256]{3,2,1,0:T(8,128)(2,1)} %get-tuple-element.35.refs_0_.refs_1_, f32[176,512]{1,0:T(8,128)S(1)} %collective-permute-done.8.refs_2_.refs_6_, f32[128,1024]{1,0:T(8,128)} %get-tuple-element.49.refs_3_, f32[176,512]{1,0:T(8,128)S(1)} %carry.2.refs_1_.refs_4_, ...), custom_call_target="tpu_custom_call" | custom-call | flops 1024 | bytes 1024 | tf_op jit(solution)/shard_map/product/pallas_call | solution.py:392
  86.8 3.9 %all-to-all-start.2 = ((f32[8,320,128]{2,1,0:T(8,128)}), f32[8,320,128]{2,1,0:T(8,128)S(1)}, u32[]{:S(2)}, u32[]{:S(2)}) async-start(f32[8,320,128]{2,1,0:T(8,128)} %product.10), calls=%async_computation.2 | async-start | bytes 2621440 | tf_op jit(solution)/shard_map/all_to_all | solution.py:493
  90.7 0.0 collective-permute-done.10.refs_3_
  90.7 2.4 %collective-permute-done.9.refs_2_ = f32[128,512]{1,0:T(8,128)S(1)} collective-permute-done((f32[128,512]{1,0:T(8,128)S(1)}, f32[128,512]{1,0:T(8,128)S(1)}, u32[]{:S(2)}, u32[]{:S(2)}) %collective-permute-start.9) | collective-permute-done | bytes 262176 | tf_op jit(solution)/shard_map/ppermute | solution.py:489
  93.1 0.1 select_select_fusion.1
  93.1 1.7 %collective-permute-start.11 = (f32[128,512]{1,0:T(8,128)S(1)}, f32[128,512]{1,0:T(8,128)S(1)}, u32[]{:S(2)}, u32[]{:S(2)}) collective-permute-start(f32[128,512]{1,0:T(8,128)S(1)} %select_select_fusion.1), channel_id=1, source_target_pairs={{1,0},{2,3},{3,1},{0,2},{5,4},{6,7},{7,5},{4,6},{9,8},{10,11},{11,... | collective-permute-start | bytes 786440 | tf_op jit(solution)/shard_map/ppermute | solution.py:503
  94.8 5.5 %product.12.refs_3_ = f32[128,1024]{1,0:T(8,128)} custom-call(bf16[4,4,1024,256]{3,2,1,0:T(8,128)(2,1)} %get-tuple-element.35.refs_0_.refs_1_, f32[128,512]{1,0:T(8,128)S(1)} %carry.3.refs_1_, f32[128,512]{1,0:T(8,128)S(1)} %collective-permute-done.9.refs_2_, f32[128,512]{1,0:T(8,128)S(1)} %collective-permute-done.10.refs_3_), custom_call_target="tpu_custom_call" | custom-call | flops 17179869184 | bytes 67108864 | tf_op jit(solution)/shard_map/product/pallas_call | solution.py:392
  100.3 0.0 collective-permute-done.11.refs_2_
  100.3 2.9 %product.13 = (f32[128,128]{1,0:T(8,128)S(1)}, f32[128,128]{1,0:T(8,128)S(1)}, f32[128,128]{1,0:T(8,128)S(1)}, f32[128,128]{1,0:T(8,128)S(1)}, f32[128,128]{1,0:...) custom-call(s32[1]{0:T(128)} %bitcast.refs_0_.row_ref, ...), custom_call_target="tpu_custom_call" | custom-call | flops 1024 | bytes 1024 | tf_op jit(solution)/shard_map/product/pallas_call | solution.py:392
  103.3 0.4 collective-permute-start.12
  103.7 2.1 %collective-permute-start.14 = (f32[128,128]{1,0:T(8,128)S(1)}, f32[128,128]{1,0:T(8,128)S(1)}, u32[]{:S(2)}, u32[]{:S(2)}) collective-permute-start(f32[128,128]{1,0:T(8,128)S(1)} %get-tuple-element.59), channel_id=1, source_target_pairs={{0,8},{4,12},{8,0},{12,4},{16,24},{20,28},{24,16},{28,20},{1,9},{5... | collective-permute-start | bytes 196616 | tf_op jit(solution)/shard_map/ppermute | solution.py:592
  105.8 1.7 %collective-permute-start.15 = (f32[128,128]{1,0:T(8,128)S(1)}, f32[128,128]{1,0:T(8,128)S(1)}, u32[]{:S(2)}, u32[]{:S(2)}) collective-permute-start(f32[128,128]{1,0:T(8,128)S(1)} %get-tuple-element.60), channel_id=1, source_target_pairs={{0,12},{4,8},{8,4},{12,0},{16,28},{20,24},{24,20},{28,16},{1,13},{... | collective-permute-start | bytes 196616 | tf_op jit(solution)/shard_map/ppermute | solution.py:592
  107.5 1.1 collective-permute-start.16
  108.6 0.0 collective-permute-start.17
  108.6 1.3 %collective-permute-done.12.refs_7_ = f32[128,128]{1,0:T(8,128)S(1)} collective-permute-done((f32[128,128]{1,0:T(8,128)S(1)}, f32[128,128]{1,0:T(8,128)S(1)}, u32[]{:S(2)}, u32[]{:S(2)}) %collective-permute-start.12) | collective-permute-done | bytes 65568 | tf_op jit(solution)/shard_map/ppermute | solution.py:592
  109.9 1.3 %collective-permute-start.18 = (f32[128,128]{1,0:T(8,128)S(1)}, f32[128,128]{1,0:T(8,128)S(1)}, u32[]{:S(2)}, u32[]{:S(2)}) collective-permute-start(f32[128,128]{1,0:T(8,128)S(1)} %get-tuple-element.63), channel_id=1, source_target_pairs={{0,24},{4,28},{8,16},{12,20},{16,8},{20,12},{24,0},{28,4},{1,25},{... | collective-permute-start | bytes 196616 | tf_op jit(solution)/shard_map/ppermute | solution.py:592
  111.2 0.0 collective-permute-done.14.refs_2_
  111.2 0.0 collective-permute-start.13
  111.2 0.0 all-to-all-done.2.came_ref.left_ref
  111.2 1.1 assemble.1
  112.4 0.0 collective-permute-done.15.refs_3_
  112.4 0.0 collective-permute-done.16.refs_4_
  112.4 0.6 collective-permute-done.17.refs_5_
  112.9 2.6 %collective-permute-done.18.refs_6_ = f32[128,128]{1,0:T(8,128)S(1)} collective-permute-done((f32[128,128]{1,0:T(8,128)S(1)}, f32[128,128]{1,0:T(8,128)S(1)}, u32[]{:S(2)}, u32[]{:S(2)}) %collective-permute-start.18) | collective-permute-done | bytes 65568 | tf_op jit(solution)/shard_map/ppermute | solution.py:592
  115.5 0.0 collective-permute-done.13.refs_1_
  115.5 1.8 %finish.1 = f32[512,256]{1,0:T(8,128)} custom-call(s32[1]{0:T(128)} %bitcast.refs_0_.row_ref, s32[8]{0:T(128)S(1)} %bitcast.5, f32[256,512]{1,0:T(8,128)S(1)} %get-tuple-element.50.base_ref, f32[8,320,128]{2,1,0:T(8,128)S(1)} %all-to-all-done.2.came_ref.left_ref, f32[128,128]{1,0:T(8,128)S(1)} %get-tuple-element.55.refs_0_, ...), custom_call_target="tpu_custom_call" | custom-call | flops 1024 | bytes 1024 | tf_op jit(solution)/shard_map/finish/pallas_call | solution.py:452
  (2 shorter events, 0.0 us)
Async XLA Ops:
  2.4 14.4 %collective-permute-start.1 = (f32[128,512]{1,0:T(8,128)S(1)}, f32[128,512]{1,0:T(8,128)S(1)}, u32[]{:S(2)}, u32[]{:S(2)}) collective-permute-start(f32[128,512]{1,0:T(8,128)S(1)} %get-tuple-element.33.first_ref.refs_0_), channel_id=1, source_target_pairs={{0,3},{1,0},{2,1},{3,2},{4,7},{5,4},{6,5},{7,6},{8,11},{9,8},{10,9... | collective-permute-start | bytes 786440 | tf_op jit(solution)/shard_map/ppermute | solution.py:489
  7.5 12.1 %collective-permute-start = (f32[128,512]{1,0:T(8,128)S(1)}, f32[128,512]{1,0:T(8,128)S(1)}, u32[]{:S(2)}, u32[]{:S(2)}) collective-permute-start(f32[128,512]{1,0:T(8,128)S(1)} %get-tuple-element.33.first_ref.refs_0_), channel_id=1, source_target_pairs={{0,1},{1,2},{2,3},{3,0},{4,5},{5,6},{6,7},{7,4},{8,9},{9,10},{10,1... | collective-permute-start | bytes 786440 | tf_op jit(solution)/shard_map/ppermute | solution.py:489
  12.4 19.2 %all-to-all-start = ((f32[8,192,128]{2,1,0:T(8,128)}), f32[8,192,128]{2,1,0:T(8,128)S(1)}, u32[]{:S(2)}, u32[]{:S(2)}) async-start(f32[8,192,128]{2,1,0:T(8,128)} %get-tuple-element.45), calls=%async_computation | async-start | bytes 1572864 | tf_op jit(solution)/shard_map/all_to_all | solution.py:493
  19.6 8.1 %collective-permute-start.2 = (f32[128,512]{1,0:T(8,128)S(1)}, f32[128,512]{1,0:T(8,128)S(1)}, u32[]{:S(2)}, u32[]{:S(2)}) collective-permute-start(f32[128,512]{1,0:T(8,128)S(1)} %select_select_fusion.3), channel_id=1, source_target_pairs={{1,0},{2,3},{3,1},{0,2},{5,4},{6,7},{7,5},{4,6},{9,8},{10,11},{11,... | collective-permute-start | bytes 786440 | tf_op jit(solution)/shard_map/ppermute | solution.py:503
  27.7 11.1 %collective-permute-start.4 = (f32[128,512]{1,0:T(8,128)S(1)}, f32[128,512]{1,0:T(8,128)S(1)}, u32[]{:S(2)}, u32[]{:S(2)}) collective-permute-start(f32[128,512]{1,0:T(8,128)S(1)} %get-tuple-element.39.refs_1_), channel_id=1, source_target_pairs={{0,1},{1,2},{2,3},{3,0},{4,5},{5,6},{6,7},{7,4},{8,9},{9,10},{10,1... | collective-permute-start | bytes 786440 | tf_op jit(solution)/shard_map/ppermute | solution.py:489
  29.4 11.9 %collective-permute-start.3 = (f32[128,512]{1,0:T(8,128)S(1)}, f32[128,512]{1,0:T(8,128)S(1)}, u32[]{:S(2)}, u32[]{:S(2)}) collective-permute-start(f32[128,512]{1,0:T(8,128)S(1)} %get-tuple-element.39.refs_1_), channel_id=1, source_target_pairs={{0,3},{1,0},{2,1},{3,2},{4,7},{5,4},{6,5},{7,6},{8,11},{9,8},{10,9... | collective-permute-start | bytes 786440 | tf_op jit(solution)/shard_map/ppermute | solution.py:489
  34.8 14.1 %all-to-all-start.1 = ((f32[8,128,128]{2,1,0:T(8,128)}), f32[8,128,128]{2,1,0:T(8,128)S(1)}, u32[]{:S(2)}, u32[]{:S(2)}) async-start(f32[8,128,128]{2,1,0:T(8,128)} %product.8), calls=%async_computation.1 | async-start | bytes 1048576 | tf_op jit(solution)/shard_map/all_to_all | solution.py:493
  41.3 7.6 %collective-permute-start.5 = (f32[128,512]{1,0:T(8,128)S(1)}, f32[128,512]{1,0:T(8,128)S(1)}, u32[]{:S(2)}, u32[]{:S(2)}) collective-permute-start(f32[128,512]{1,0:T(8,128)S(1)} %select_select_fusion.2), channel_id=1, source_target_pairs={{1,0},{2,3},{3,1},{0,2},{5,4},{6,7},{7,5},{4,6},{9,8},{10,11},{11,... | collective-permute-start | bytes 786440 | tf_op jit(solution)/shard_map/ppermute | solution.py:503
  42.8 6.2 %copy-start = (s32[1,8,1]{1,2,0:T(1,128)S(1)}, s32[1,8,1]{1,2,0:T(1,128)}, u32[]{:S(2)}) copy-start(s32[1,8,1]{1,2,0:T(1,128)} %param.20) | copy-start | bytes 100
  49.7 13.2 %collective-permute-start.7 = (f32[176,512]{1,0:T(8,128)S(1)}, f32[176,512]{1,0:T(8,128)S(1)}, u32[]{:S(2)}, u32[]{:S(2)}) collective-permute-start(f32[176,512]{1,0:T(8,128)S(1)} %carry.2.refs_1_.refs_4_), channel_id=1, source_target_pairs={{0,1},{1,2},{2,3},{3,0},{4,5},{5,6},{6,7},{7,4},{8,9},{9,10},{10,1... | collective-permute-start | bytes 1081352 | tf_op jit(solution)/shard_map/ppermute | solution.py:489
  52.4 15.7 %collective-permute-start.6 = (f32[176,512]{1,0:T(8,128)S(1)}, f32[176,512]{1,0:T(8,128)S(1)}, u32[]{:S(2)}, u32[]{:S(2)}) collective-permute-start(f32[176,512]{1,0:T(8,128)S(1)} %carry.2.refs_1_.refs_4_), channel_id=1, source_target_pairs={{0,3},{1,0},{2,1},{3,2},{4,7},{5,4},{6,5},{7,6},{8,11},{9,8},{10,9... | collective-permute-start | bytes 1081352 | tf_op jit(solution)/shard_map/ppermute | solution.py:489
  57.1 21.6 %all-to-all-start.3 = ((f32[8,128,128]{2,1,0:T(8,128)}), f32[8,128,128]{2,1,0:T(8,128)S(1)}, u32[]{:S(2)}, u32[]{:S(2)}) async-start(f32[8,128,128]{2,1,0:T(8,128)} %product.11), calls=%async_computation.3 | async-start | bytes 1048576 | tf_op jit(solution)/shard_map/all_to_all | solution.py:493
  68.1 10.5 %collective-permute-start.8 = (f32[176,512]{1,0:T(8,128)S(1)}, f32[176,512]{1,0:T(8,128)S(1)}, u32[]{:S(2)}, u32[]{:S(2)}) collective-permute-start(f32[176,512]{1,0:T(8,128)S(1)} %select_select_fusion), channel_id=1, source_target_pairs={{1,0},{2,3},{3,1},{0,2},{5,4},{6,7},{7,5},{4,6},{9,8},{10,11},{11,... | collective-permute-start | bytes 1081352 | tf_op jit(solution)/shard_map/ppermute | solution.py:503
  79.3 11.4 %collective-permute-start.10 = (f32[128,512]{1,0:T(8,128)S(1)}, f32[128,512]{1,0:T(8,128)S(1)}, u32[]{:S(2)}, u32[]{:S(2)}) collective-permute-start(f32[128,512]{1,0:T(8,128)S(1)} %carry.3.refs_1_), channel_id=1, source_target_pairs={{0,1},{1,2},{2,3},{3,0},{4,5},{5,6},{6,7},{7,4},{8,9},{9,10},{10,1... | collective-permute-start | bytes 786440 | tf_op jit(solution)/shard_map/ppermute | solution.py:489
  80.9 12.2 %collective-permute-start.9 = (f32[128,512]{1,0:T(8,128)S(1)}, f32[128,512]{1,0:T(8,128)S(1)}, u32[]{:S(2)}, u32[]{:S(2)}) collective-permute-start(f32[128,512]{1,0:T(8,128)S(1)} %carry.3.refs_1_), channel_id=1, source_target_pairs={{0,3},{1,0},{2,1},{3,2},{4,7},{5,4},{6,5},{7,6},{8,11},{9,8},{10,9... | collective-permute-start | bytes 786440 | tf_op jit(solution)/shard_map/ppermute | solution.py:489
  86.8 24.4 %all-to-all-start.2 = ((f32[8,320,128]{2,1,0:T(8,128)}), f32[8,320,128]{2,1,0:T(8,128)S(1)}, u32[]{:S(2)}, u32[]{:S(2)}) async-start(f32[8,320,128]{2,1,0:T(8,128)} %product.10), calls=%async_computation.2 | async-start | bytes 2621440 | tf_op jit(solution)/shard_map/all_to_all | solution.py:493
  93.1 7.2 %collective-permute-start.11 = (f32[128,512]{1,0:T(8,128)S(1)}, f32[128,512]{1,0:T(8,128)S(1)}, u32[]{:S(2)}, u32[]{:S(2)}) collective-permute-start(f32[128,512]{1,0:T(8,128)S(1)} %select_select_fusion.1), channel_id=1, source_target_pairs={{1,0},{2,3},{3,1},{0,2},{5,4},{6,7},{7,5},{4,6},{9,8},{10,11},{11,... | collective-permute-start | bytes 786440 | tf_op jit(solution)/shard_map/ppermute | solution.py:503
  103.3 6.6 %collective-permute-start.12 = (f32[128,128]{1,0:T(8,128)S(1)}, f32[128,128]{1,0:T(8,128)S(1)}, u32[]{:S(2)}, u32[]{:S(2)}) collective-permute-start(f32[128,128]{1,0:T(8,128)S(1)} %get-tuple-element.57), channel_id=1, source_target_pairs={{0,28},{4,24},{8,20},{12,16},{16,12},{20,8},{24,4},{28,0},{1,29},{... | collective-permute-start | bytes 196616 | tf_op jit(solution)/shard_map/ppermute | solution.py:592
  103.7 7.5 %collective-permute-start.14 = (f32[128,128]{1,0:T(8,128)S(1)}, f32[128,128]{1,0:T(8,128)S(1)}, u32[]{:S(2)}, u32[]{:S(2)}) collective-permute-start(f32[128,128]{1,0:T(8,128)S(1)} %get-tuple-element.59), channel_id=1, source_target_pairs={{0,8},{4,12},{8,0},{12,4},{16,24},{20,28},{24,16},{28,20},{1,9},{5... | collective-permute-start | bytes 196616 | tf_op jit(solution)/shard_map/ppermute | solution.py:592
  105.8 6.6 %collective-permute-start.15 = (f32[128,128]{1,0:T(8,128)S(1)}, f32[128,128]{1,0:T(8,128)S(1)}, u32[]{:S(2)}, u32[]{:S(2)}) collective-permute-start(f32[128,128]{1,0:T(8,128)S(1)} %get-tuple-element.60), channel_id=1, source_target_pairs={{0,12},{4,8},{8,4},{12,0},{16,28},{20,24},{24,20},{28,16},{1,13},{... | collective-permute-start | bytes 196616 | tf_op jit(solution)/shard_map/ppermute | solution.py:592
  107.5 4.9 %collective-permute-start.16 = (f32[128,128]{1,0:T(8,128)S(1)}, f32[128,128]{1,0:T(8,128)S(1)}, u32[]{:S(2)}, u32[]{:S(2)}) collective-permute-start(f32[128,128]{1,0:T(8,128)S(1)} %get-tuple-element.61), channel_id=1, source_target_pairs={{0,16},{4,20},{8,24},{12,28},{16,0},{20,4},{24,8},{28,12},{1,17},{... | collective-permute-start | bytes 196616 | tf_op jit(solution)/shard_map/ppermute | solution.py:592
  108.6 4.3 %collective-permute-start.17 = (f32[128,128]{1,0:T(8,128)S(1)}, f32[128,128]{1,0:T(8,128)S(1)}, u32[]{:S(2)}, u32[]{:S(2)}) collective-permute-start(f32[128,128]{1,0:T(8,128)S(1)} %get-tuple-element.62), channel_id=1, source_target_pairs={{0,20},{4,16},{8,28},{12,24},{16,4},{20,0},{24,12},{28,8},{1,21},{... | collective-permute-start | bytes 196616 | tf_op jit(solution)/shard_map/ppermute | solution.py:592
  109.9 5.6 %collective-permute-start.18 = (f32[128,128]{1,0:T(8,128)S(1)}, f32[128,128]{1,0:T(8,128)S(1)}, u32[]{:S(2)}, u32[]{:S(2)}) collective-permute-start(f32[128,128]{1,0:T(8,128)S(1)} %get-tuple-element.63), channel_id=1, source_target_pairs={{0,24},{4,28},{8,16},{12,20},{16,8},{20,12},{24,0},{28,4},{1,25},{... | collective-permute-start | bytes 196616 | tf_op jit(solution)/shard_map/ppermute | solution.py:592
  111.2 4.3 %collective-permute-start.13 = (f32[128,128]{1,0:T(8,128)S(1)}, f32[128,128]{1,0:T(8,128)S(1)}, u32[]{:S(2)}, u32[]{:S(2)}) collective-permute-start(f32[128,128]{1,0:T(8,128)S(1)} %get-tuple-element.58), channel_id=1, source_target_pairs={{0,4},{4,0},{8,12},{12,8},{16,20},{20,16},{24,28},{28,24},{1,5},{5... | collective-permute-start | bytes 196616 | tf_op jit(solution)/shard_map/ppermute | solution.py:592
